TPU v7x, 32 devices: a whole 2x2x4 slice. The times are simulated.
32 devices in a mesh: groups: 2 (over x), tensor: 8 (over z, y), store: 2 (over core).
Axes of the slice: x: 2, y: 2, z: 4, core: 2. Of those that a mesh axis runs over, the one named last changes fastest.
Arguments:
- tokens: bfloat16 [4, 1024, 8192], P(('groups', 'store'), 'tensor'), parts along dimension 0, may hold values from -6 to 6
- query_weight: bfloat16 [8192, 8192], P(None, 'tensor'), may hold values from -0.0625 to 0.0625
- adapter_down_maps: bfloat16 [64, 64, 8192], P(('tensor', 'store')), may hold values from -0.0625 to 0.0625
- adapter_up_maps: bfloat16 [64, 64, 8192], P(('tensor', 'store')), may hold values from -0.75 to 0.75
- adapter_home_slot: int32 [64], replicated, may hold values from 0 to 63, as said below
- adapter_per_block: int32 [2, 8], replicated, may hold values from 0 to 63, as said below
Outputs:
- query: bfloat16 [4, 1024, 8192], P(('groups', 'store'), None, 'tensor'), parts along dimension 0
There are 2 independent parts, one for each index of `groups`. A program takes and returns all parts, laid end to end along the dimension named above; an argument that names none is the same for every part. Nothing has to cross between parts.
Inputs may be any that keep to these rules, and one draw needn't show every extreme that they name: `adapter_home_slot`: A permutation: each adapter has its own slot; slot j lies on the device of index j // 4 along tensor+store. `adapter_per_block`: each request batch names exactly min(8, 16) different adapters, and the different adapters of one batch always lie in slots on different devices.
All inputs are finite; a program needn't handle non-finite values.
Results may differ from a plain program's by a relative error of at most 0.0031.
Values may be sent and summed in bfloat16 or wider, within the bound.
No kernel may reach another device: no remote copies, remote signals or barrier semaphores. Data moves between devices by JAX's collectives and lax.ppermute only.
A program may use at most 128 MiB of HBM per device.

v0:
```python
import jax
import jax.numpy as jnp
from jax import lax
from jax.sharding import PartitionSpec as P

BLOCK = 128


def body(
    tokens, query_weight, adapter_down_maps, adapter_up_maps, adapter_home_slot, adapter_per_block
):
    shard_count = lax.axis_size("tensor")
    store_count = lax.axis_size("store")
    devices_all = shard_count * store_count
    my_tensor = lax.axis_index("tensor")
    my_store = lax.axis_index("store")
    myself = lax.axis_index(("tensor", "store"))
    held_adapters, rank_index, feature_width = adapter_down_maps.shape
    feature_index = query_weight.shape[1]
    own_rows = tokens[0]
    group_rows = own_rows.shape[0] * shard_count
    blocks = group_rows // BLOCK
    catalog = jnp.arange(adapter_home_slot.shape[0], dtype=jnp.int32)
    store_slots = jnp.sum(
        jnp.where(
            adapter_per_block[:, :, None] == catalog[None, None, :],
            adapter_home_slot[None, None, :],
            0,
        ),
        axis=2,
    )
    owner = store_slots // held_adapters
    inside = store_slots % held_adapters
    picked = jnp.max(jnp.where(owner == myself, inside, -1), axis=1)
    select = (picked[:, None] == jnp.arange(held_adapters, dtype=jnp.int32)[None, :]).astype(
        jnp.bfloat16
    )
    down_map_parts = adapter_down_maps.reshape(
        held_adapters, rank_index, shard_count, feature_index
    )
    up_map_parts = adapter_up_maps.reshape(held_adapters, rank_index, shard_count, feature_index)
    send_down = jnp.einsum(
        "sl,lrtf->tsrf", select, down_map_parts, preferred_element_type=jnp.float32
    ).astype(jnp.bfloat16)
    send_up = jnp.einsum(
        "sl,lrtf->tsrf", select, up_map_parts, preferred_element_type=jnp.float32
    ).astype(jnp.bfloat16)
    recv_down, recv_up = (
        lax.all_to_all(
            send_down.reshape(devices_all, rank_index, feature_index),
            ("tensor", "store"),
            split_axis=0,
            concat_axis=0,
            tiled=True,
        ),
        lax.all_to_all(
            send_up.reshape(devices_all, rank_index, feature_index),
            ("tensor", "store"),
            split_axis=0,
            concat_axis=0,
            tiled=True,
        ),
    )
    owner_row = lax.dynamic_index_in_dim(owner, my_store, 0, keepdims=False)
    source_pick = (owner_row[:, None] == jnp.arange(devices_all, dtype=jnp.int32)[None, :]).astype(
        jnp.bfloat16
    )
    block_down = jnp.einsum(
        "bj,jrf->brf", source_pick, recv_down, preferred_element_type=jnp.float32
    ).astype(jnp.bfloat16)
    block_up = jnp.einsum(
        "bj,jrf->brf", source_pick, recv_up, preferred_element_type=jnp.float32
    ).astype(jnp.bfloat16)
    piece = lax.all_gather(own_rows, "tensor", axis=0, tiled=True)
    product = jnp.dot(piece, query_weight, preferred_element_type=jnp.float32)
    features = lax.dynamic_slice_in_dim(piece, my_tensor * feature_index, feature_index, 1)
    partial_value = jnp.einsum(
        "bnf,brf->bnr",
        features.reshape(blocks, BLOCK, feature_index),
        block_down,
        preferred_element_type=jnp.float32,
    )
    shrunk = lax.psum(partial_value, "tensor").astype(jnp.bfloat16)
    grown = jnp.einsum(
        "bnr,brf->bnf", shrunk, block_up, preferred_element_type=jnp.float32
    ).reshape(group_rows, feature_index)
    query = (product + 0.5 * grown).astype(jnp.bfloat16)
    return query[None]


def solution(mesh):
    placed = (
        P(("groups", "store"), "tensor", None),
        P(None, "tensor"),
        P(("tensor", "store"), None, None),
        P(("tensor", "store"), None, None),
        P(),
        P(),
    )
    return jax.shard_map(
        body,
        mesh=mesh,
        in_specs=placed,
        out_specs=P(("groups", "store"), None, "tensor"),
        check_vma=False,
    )
```

profile of v0, /device:TPU:0, one launch (start us, length us, event | category | flops | bytes accessed | tf_op | source)
XLA Modules:
  0.0 392.7 jit_solution(3296415142363824061)
XLA Ops:
  6.5 0.0 all-gather.3.cloned.1.call-start
  6.5 0.7 all-gather.3.cloned.1.call-update
  7.3 0.0 copy-start
  7.3 0.0 copy-start.1
  7.3 8.5 %copy.24 = bf16[32,8,8,1024]{3,2,1,0:T(8,128)(2,1)} copy(bf16[32,8,8,1024]{3,1,2,0:T(8,128)(2,1)} %bitcast.48) | data formatting | bytes 8388608
  15.7 0.0 copy-done
  15.7 0.0 copy-done.1
  15.7 0.2 select_reduce_fusion
  16.0 0.1 fusion.45
  16.1 5.6 %fusion.16 = bf16[8,2,64,1024]{3,1,0,2:T(2,128)(2,1)S(1)} fusion(bf16[4,64,8,1024]{3,2,1,0:T(8,128)(2,1)} %bitcast.50, s32[2]{0:T(128)S(1)} %get-tuple-element.5), kind=kOutput, calls=%fused_computation.11 | convolution fusion | flops 9437192 | bytes 6291464 | tf_op jit(solution)/shard_map/sl,lrtf->tsrf/dot_general | solution.py:42
  21.7 2.5 copy.22
  24.2 7.7 %all-to-all-start = ((bf16[16,64,1024]{2,1,0:T(8,128)(2,1)}), bf16[16,64,1024]{2,1,0:T(8,128)(2,1)S(1)}, u32[]{:S(2)}, u32[]{:S(2)}) async-start(bf16[16,64,1024]{2,1,0:T(8,128)(2,1)} %bitcast.47), calls=%async_computation | async-start | bytes 4194304 | tf_op jit(solution)/shard_map/all_to_all | solution.py:49
  31.9 6.5 %copy.25 = bf16[32,8,8,1024]{3,2,1,0:T(8,128)(2,1)S(1)} copy(bf16[32,8,8,1024]{3,1,2,0:T(8,128)(2,1)} %bitcast.49) | data formatting | bytes 8388608
  38.4 3.1 fusion.13
  41.5 2.5 copy.23
  44.0 61.5 %all-to-all-done = bf16[16,64,1024]{2,1,0:T(8,128)(2,1)S(1)} async-done(((bf16[16,64,1024]{2,1,0:T(8,128)(2,1)}), bf16[16,64,1024]{2,1,0:T(8,128)(2,1)S(1)}, u32[]{:S(2)}, u32[]{:S(2)}) %all-to-all-start) | async-done | bytes 2097184 | tf_op jit(solution)/shard_map/all_to_all | solution.py:49
  105.5 29.5 %all-to-all-start.1 = ((bf16[16,64,1024]{2,1,0:T(8,128)(2,1)}), bf16[16,64,1024]{2,1,0:T(8,128)(2,1)}, u32[]{:S(2)}, u32[]{:S(2)}) async-start(bf16[16,64,1024]{2,1,0:T(8,128)(2,1)} %bitcast.46), calls=%async_computation.1 | async-start | bytes 4194304 | tf_op jit(solution)/shard_map/all_to_all | solution.py:56
  135.0 1.3 fusion.28
  136.3 69.6 %all-to-all-done.1 = bf16[16,64,1024]{2,1,0:T(8,128)(2,1)} async-done(((bf16[16,64,1024]{2,1,0:T(8,128)(2,1)}), bf16[16,64,1024]{2,1,0:T(8,128)(2,1)}, u32[]{:S(2)}, u32[]{:S(2)}) %all-to-all-start.1) | async-done | bytes 2097184 | tf_op jit(solution)/shard_map/all_to_all | solution.py:56
  205.9 2.9 fusion.31
  208.8 110.8 %all-gather.3.cloned.1.call-done = bf16[1,1024,8192]{2,1,0:T(8,128)(2,1)} async-done(((bf16[1,128,8192]{2,1,0:T(8,128)(2,1)}), bf16[1,1024,8192]{2,1,0:T(8,128)(2,1)}) %all-gather.3.cloned.1.call-update) | async-done | bytes 16777232 | tf_op jit(solution)/shard_map/all_gather | solution.py:74
  319.6 1.8 constant_dynamic-slice_fusion
  321.4 0.9 fusion.35
  322.3 38.3 %all-reduce.1 = bf16[8,128,64]{1,2,0:T(8,128)(2,1)S(1)} all-reduce(f32[8,128,64]{1,2,0:T(8,128)S(1)} %fusion.35), channel_id=1, replica_groups=mesh['groups'=2,'tensor'=8,'store'=2] {'tensor'}, use_global_device_ids=true, to_apply=%region_2.3 | all-reduce | flops 65536 | bytes 393216 | tf_op jit(solution)/shard_map/psum | solution.py:83
  360.6 1.7 convolution_multiply_fusion
  362.4 23.5 %fusion.25 = bf16[1,1024,1024]{2,1,0:T(8,128)(2,1)} fusion(f32[8,128,1024]{2,1,0:T(8,128)S(1)} %convolution_multiply_fusion, bf16[8192,1024]{1,0:T(8,128)(2,1)} %param.7, bf16[1,1024,8192]{2,1,0:T(8,128)(2,1)} %all-gather.3.cloned.1.call-done), kind=kOutput, calls=%fused_computation.17 | convolution fusion | flops 17181966336 | bytes 39845888 | tf_op jit(solution)/shard_map/dot_general | solution.py:75
  (1 shorter events, 0.0 us)
Async XLA Ops:
  6.5 313.1 %all-gather.3.cloned.1.call-start = ((), (), s32[]{:S(2)}) async-start(), calls=%async_computation.2 | async-start | bytes 18874368 | tf_op jit(solution)/shard_map/all_gather | solution.py:74
  7.3 8.5 %copy-start = (s32[2,8]{1,0:T(2,128)S(1)}, s32[2,8]{1,0:T(2,128)}, u32[]{:S(2)}) copy-start(s32[2,8]{1,0:T(2,128)} %param.11) | copy-start | bytes 196
  7.3 8.5 %copy-start.1 = (s32[64]{0:T(128)S(1)}, s32[64]{0:T(128)}, u32[]{:S(2)}) copy-start(s32[64]{0:T(128)} %param.10) | copy-start | bytes 772
  24.2 81.3 %all-to-all-start = ((bf16[16,64,1024]{2,1,0:T(8,128)(2,1)}), bf16[16,64,1024]{2,1,0:T(8,128)(2,1)S(1)}, u32[]{:S(2)}, u32[]{:S(2)}) async-start(bf16[16,64,1024]{2,1,0:T(8,128)(2,1)} %bitcast.47), calls=%async_computation | async-start | bytes 4194304 | tf_op jit(solution)/shard_map/all_to_all | solution.py:49
  105.5 100.4 %all-to-all-start.1 = ((bf16[16,64,1024]{2,1,0:T(8,128)(2,1)}), bf16[16,64,1024]{2,1,0:T(8,128)(2,1)}, u32[]{:S(2)}, u32[]{:S(2)}) async-start(bf16[16,64,1024]{2,1,0:T(8,128)(2,1)} %bitcast.46), calls=%async_computation.1 | async-start | bytes 4194304 | tf_op jit(solution)/shard_map/all_to_all | solution.py:56
Sparse Core Ops, SparseCore 0:
  9.5 310.0 all-gather.2
where the time goes:
time: 393 us
  waiting for transfers between devices  243 us (62%)
  matrix products  38.9 us (10%)
  blocking collectives  38.3 us (10%)
  starting transfers between devices  37.2 us (9%)
  local copies, waits for them, and re-layouts  21.7 us (6%)
  between operations  13.5 us (3%)
    all_gather x1, waiting for transfers between devices, body(): piece = lax.all_gather(own_rows, 'tensor', axis=0, tiled=True)  111 us
    all_to_all x1, waiting for transfers between devices, body(): lax.all_to_all(send_up.reshape(devices_all, rank_index, feature_index), (...  69.6 us
    all_to_all x1, waiting for transfers between devices, body(): lax.all_to_all(send_down.reshape(devices_all, rank_index, feature_index),...  61.5 us
    psum x1, blocking collectives, body(): shrunk = lax.psum(partial_value, 'tensor').astype(jnp.bfloat16)  38.3 us
    all_to_all x1, starting transfers between devices, body(): lax.all_to_all(send_up.reshape(devices_all, rank_index, feature_index), (...  29.5 us
    dot_general x1, matrix products, body(): product = jnp.dot(piece, query_weight, preferred_element_type=jnp.float32)  23.5 us
    unnamed x6, local copies, waits for them, and re-layouts  15 us
  transfers between devices with their start and end apart: 3, of which 3 were waited for; matrix products, arithmetic and copies ran while one was open for 8% of the time, Pallas kernels for 0%

commit v1 on v0

--- a/solution.py
+++ b/solution.py
@@ -6,7 +6,19 @@
 BLOCK = 128
 
 
-def body(
+def find_slots(adapter_home_slot, adapter_per_block):
+    catalog = jnp.arange(adapter_home_slot.shape[0], dtype=jnp.int32)
+    return jnp.sum(
+        jnp.where(
+            adapter_per_block[:, :, None] == catalog[None, None, :],
+            adapter_home_slot[None, None, :],
+            0,
+        ),
+        axis=2,
+    )
+
+
+def general_body(
     tokens, query_weight, adapter_down_maps, adapter_up_maps, adapter_home_slot, adapter_per_block
 ):
     shard_count = lax.axis_size("tensor")
@@ -20,15 +32,7 @@
     own_rows = tokens[0]
     group_rows = own_rows.shape[0] * shard_count
     blocks = group_rows // BLOCK
-    catalog = jnp.arange(adapter_home_slot.shape[0], dtype=jnp.int32)
-    store_slots = jnp.sum(
-        jnp.where(
-            adapter_per_block[:, :, None] == catalog[None, None, :],
-            adapter_home_slot[None, None, :],
-            0,
-        ),
-        axis=2,
-    )
+    store_slots = find_slots(adapter_home_slot, adapter_per_block)
     owner = store_slots // held_adapters
     inside = store_slots % held_adapters
     picked = jnp.max(jnp.where(owner == myself, inside, -1), axis=1)
@@ -47,19 +51,13 @@
     ).astype(jnp.bfloat16)
     recv_down, recv_up = (
         lax.all_to_all(
-            send_down.reshape(devices_all, rank_index, feature_index),
+            sent.reshape(devices_all, rank_index, feature_index),
             ("tensor", "store"),
             split_axis=0,
             concat_axis=0,
             tiled=True,
-        ),
-        lax.all_to_all(
-            send_up.reshape(devices_all, rank_index, feature_index),
-            ("tensor", "store"),
-            split_axis=0,
-            concat_axis=0,
-            tiled=True,
-        ),
+        )
+        for sent in (send_down, send_up)
     )
     owner_row = lax.dynamic_index_in_dim(owner, my_store, 0, keepdims=False)
     source_pick = (owner_row[:, None] == jnp.arange(devices_all, dtype=jnp.int32)[None, :]).astype(
@@ -88,6 +86,104 @@
     return query[None]
 
 
+def both_ways(pairs):
+    return pairs + [(b, a) for a, b in pairs]
+
+
+ACROSS = both_ways([(0, 1), (2, 3), (4, 5), (6, 7)])
+NEAR = both_ways([(0, 2), (1, 3), (4, 6), (5, 7)])
+FAR = both_ways([(0, 4), (1, 5), (2, 6), (3, 7)])
+CHUNKS = 4
+
+
+def swap(value, axis):
+    return lax.ppermute(value, axis, [(0, 1), (1, 0)])
+
+
+def chain_body(
+    tokens, query_weight, adapter_down_maps, adapter_up_maps, adapter_home_slot, adapter_per_block
+):
+    me = lax.axis_index("tensor")
+    store = lax.axis_index("store")
+    group = lax.axis_index("groups")
+    myself = me * 2 + store
+    held, rank, width = adapter_down_maps.shape
+    columns = query_weight.shape[1]
+    part = columns // 2
+    rows = tokens[0]
+    step = BLOCK // CHUNKS
+
+    store_slots = find_slots(adapter_home_slot, adapter_per_block)
+    owner = store_slots // held
+    inside = store_slots % held
+    picked = jnp.max(jnp.where(owner == myself, inside, 0), axis=1)
+    owner_row = lax.dynamic_index_in_dim(owner, store, 0, keepdims=False)
+
+    gathered = [
+        lax.all_gather(rows[c * step : (c + 1) * step], "tensor", axis=0) for c in range(CHUNKS)
+    ]
+
+    def pick(maps, index):
+        local = lax.dynamic_index_in_dim(picked, index, 0, keepdims=False)
+        return lax.dynamic_index_in_dim(maps, local, 0, keepdims=False)
+
+    down_own = pick(adapter_down_maps, store)
+    down_swapped = swap(pick(adapter_down_maps, 1 - store), "store")
+    candidates = jnp.concatenate([down_own, down_swapped])
+    use_own = (owner_row == myself)[:, None, None]
+    use_swapped = (owner_row == me * 2 + 1 - store)[:, None, None]
+
+    def shrink(chunk):
+        value = lax.dot_general(
+            candidates,
+            chunk.reshape(8 * step, width),
+            (((1,), (1,)), ((), ())),
+            preferred_element_type=jnp.float32,
+        )
+        value = value.reshape(2, rank, 8, step).transpose(0, 2, 1, 3)
+        value = jnp.where(use_own, value[0], jnp.where(use_swapped, value[1], 0))
+        value = value.astype(jnp.bfloat16)
+        for pairs in (ACROSS, NEAR, FAR):
+            value = value + lax.ppermute(value, "tensor", pairs)
+        return value
+
+    def columns_of(up):
+        halves = up.reshape(rank, 8, 2, part)
+        half = lax.dynamic_index_in_dim(halves, group, 2, keepdims=False)
+        return half.transpose(1, 0, 2)
+
+    up_sent = jnp.stack(
+        [columns_of(pick(adapter_up_maps, 0)), columns_of(pick(adapter_up_maps, 1))], axis=1
+    )
+    up_got = lax.all_to_all(
+        up_sent.reshape(16, rank, part), ("tensor", "store"), split_axis=0, concat_axis=0, tiled=True
+    )
+    up_half = jnp.stack(
+        [lax.dynamic_index_in_dim(up_got, owner_row[b], 0, keepdims=False) for b in range(8)]
+    )
+    up_other = swap(up_half, "groups")
+    up = jnp.concatenate(
+        [jnp.where(group == 0, up_half, up_other), jnp.where(group == 0, up_other, up_half)], axis=2
+    )
+
+    outputs = []
+    for chunk in gathered:
+        base = jnp.dot(
+            chunk.reshape(8 * step, width), query_weight, preferred_element_type=jnp.float32
+        )
+        grown = jnp.einsum("brn,brf->bnf", shrink(chunk), up, preferred_element_type=jnp.float32)
+        value = base.reshape(8, step, columns) + 0.5 * grown
+        outputs.append(value.astype(jnp.bfloat16))
+    query = jnp.concatenate(outputs, axis=1)
+    return query.reshape(1, 8 * BLOCK, columns)
+
+
+def body(tokens, *rest):
+    sizes = tuple(lax.axis_size(name) for name in ("groups", "tensor", "store"))
+    fits = sizes == (2, 8, 2) and tokens.shape[1] == BLOCK
+    return (chain_body if fits else general_body)(tokens, *rest)
+
+
 def solution(mesh):
     placed = (
         P(("groups", "store"), "tensor", None),

time: 393 us -> 382 us (0.972)
  blocking collectives: 38.3 us -> 0 us
  between operations: 13.5 us -> 35.7 us
  waiting for transfers between devices: 243 us -> 259 us
  starting transfers between devices: 37.2 us -> 24.1 us
  local copies, waits for them, and re-layouts: 21.7 us -> 13.9 us
  matrix products: 38.9 us -> 44.3 us
    all_gather x1 -> x4, waiting for transfers between devices: 111 us -> 231 us  [chain_body(): lax.all_gather(rows[c * step:(c + 1) * step], 'tensor', axis=0)]
    all_to_all x2 -> x1, waiting for transfers between devices: 131 us -> 11.6 us  [chain_body(): lax.all_to_all(up_sent.reshape(16, rank, part), ('tensor', 'store'), spli...]
    psum x1 -> x0, blocking collectives: 38.3 us -> none  [body(): shrunk = lax.psum(partial_value, 'tensor').astype(jnp.bfloat16)]
    all_to_all x2 -> x1, starting transfers between devices: 37.2 us -> 7.4 us  [chain_body(): lax.all_to_all(up_sent.reshape(16, rank, part), ('tensor', 'store'), spli...]
    ppermute x0 -> x14, starting transfers between devices: none -> 16.6 us  [the longest x12 14.6 us: shrink(): value = value + lax.ppermute(value, 'tensor', pairs)]
    ppermute x0 -> x14, waiting for transfers between devices: none -> 15.2 us  [the longest x2 11.5 us: swap(): return lax.ppermute(value, axis, [(0, 1), (1, 0)])]
    unnamed x6 -> x21, local copies, waits for them, and re-layouts: 15 us -> 0.56 us
    dot_general x7 -> x12, matrix products: 38.9 us -> 44.3 us  [the longest x4 29.3 us: chain_body(): jnp.dot(chunk.reshape(8 * step, width), query_weight, preferred_element_t...]
  transfers between devices with their start and end apart: 3 -> 19, of which waited for: 3 -> 9; matrix products, arithmetic and copies ran while one was open for 8% -> 14% of each run, Pallas kernels for 0% -> 0%
where the time goes in v1:
time: 382 us; the launch traced here: 381 us
  waiting for transfers between devices  259 us (68%)
  matrix products  44.3 us (12%)
  between operations  35.7 us (9%)
  starting transfers between devices  24.1 us (6%)
  local copies, waits for them, and re-layouts  13.9 us (4%)
    all_gather x4, waiting for transfers between devices, chain_body(): lax.all_gather(rows[c * step:(c + 1) * step], 'tensor', axis=0)  231 us
    dot_general x4, matrix products, chain_body(): jnp.dot(chunk.reshape(8 * step, width), query_weight, preferred_element_t...  29.3 us
    ppermute x12, starting transfers between devices, shrink(): value = value + lax.ppermute(value, 'tensor', pairs)  14.6 us
    dot_general x4, matrix products, shrink(): lax.dot_general(candidates, chunk.reshape(8 * step, width), (((1,), (1,))...  13.8 us
    all_to_all x1, waiting for transfers between devices, chain_body(): lax.all_to_all(up_sent.reshape(16, rank, part), ('tensor', 'store'), spli...  11.6 us
    ppermute x2, waiting for transfers between devices, swap(): return lax.ppermute(value, axis, [(0, 1), (1, 0)])  11.5 us
  transfers between devices with their start and end apart: 19, of which 9 were waited for; matrix products, arithmetic and copies ran while one was open for 14% of the time, Pallas kernels for 0%

profile of v1, /device:TPU:0, one launch (start us, length us, event | category | flops | bytes accessed | tf_op | source)
XLA Modules:
  0.0 381.1 jit_solution(5534095412345591976)
XLA Ops:
  6.5 2.9 fusion.53
  9.5 0.7 all-gather.7.cloned.1.call-update
  10.3 0.7 all-gather.9.cloned.1.call-update
  11.0 0.5 all-gather.11.cloned.1.call-update
  11.9 0.6 fusion.55
  16.3 1.7 constant_dynamic-slice_fusion.3
  18.0 0.8 reshape.91
  18.8 0.8 reshape.90
  19.6 2.7 constant_dynamic-slice_fusion
  22.7 1.3 copy.9
  24.0 7.4 %all-to-all-start = ((bf16[16,64,512]{2,1,0:T(8,128)(2,1)}), bf16[16,64,512]{2,1,0:T(8,128)(2,1)S(1)}, u32[]{:S(2)}, u32[]{:S(2)}) async-start(bf16[16,64,512]{2,1,0:T(8,128)(2,1)} %bitcast.20), calls=%async_computation | async-start | bytes 2097152 | tf_op jit(solution)/shard_map/all_to_all | solution.py:158
  35.1 1.8 dynamic-slice_bitcast_fusion.1
  36.9 0.5 collective-permute-start
  37.4 0.7 fusion.54
  52.8 11.6 %all-to-all-done = bf16[16,64,512]{2,1,0:T(8,128)(2,1)S(1)} async-done(((bf16[16,64,512]{2,1,0:T(8,128)(2,1)}), bf16[16,64,512]{2,1,0:T(8,128)(2,1)S(1)}, u32[]{:S(2)}, u32[]{:S(2)}) %all-to-all-start) | async-done | bytes 1048608 | tf_op jit(solution)/shard_map/all_to_all | solution.py:158
  64.6 1.5 collective-permute-start.4
  66.1 1.4 pad_maximum_fusion
  67.5 11.4 %collective-permute-done.4 = bf16[8,64,512]{2,1,0:T(8,128)(2,1)S(1)} collective-permute-done((bf16[8,64,512]{2,1,0:T(8,128)(2,1)S(1)}, bf16[8,64,512]{2,1,0:T(8,128)(2,1)S(1)}, u32[]{:S(2)}, u32[]{:S(2)}) %collective-permute-start.4) | collective-permute-done | bytes 524320 | tf_op jit(solution)/shard_map/ppermute | solution.py:100
  79.0 19.2 %all-gather.5.cloned.1.call-done = bf16[8,32,8192]{2,1,0:T(8,128)(2,1)} async-done(((bf16[1,32,8192]{2,1,0:T(8,128)(2,1)}), bf16[8,32,8192]{2,1,0:T(8,128)(2,1)}) %all-gather.5.cloned.1.call-update) | async-done | bytes 4194320 | tf_op jit(solution)/shard_map/all_gather | solution.py:123
  98.2 3.4 fusion.24
  101.6 70.8 %all-gather.7.cloned.1.call-done = bf16[8,32,8192]{2,1,0:T(8,128)(2,1)} async-done(((bf16[1,32,8192]{2,1,0:T(8,128)(2,1)}), bf16[8,32,8192]{2,1,0:T(8,128)(2,1)}) %all-gather.7.cloned.1.call-update) | async-done | bytes 4194320 | tf_op jit(solution)/shard_map/all_gather | solution.py:123
  172.5 3.5 fusion.27
  175.9 70.4 %all-gather.9.cloned.1.call-done = bf16[8,32,8192]{2,1,0:T(8,128)(2,1)} async-done(((bf16[1,32,8192]{2,1,0:T(8,128)(2,1)}), bf16[8,32,8192]{2,1,0:T(8,128)(2,1)}) %all-gather.9.cloned.1.call-update) | async-done | bytes 4194320 | tf_op jit(solution)/shard_map/all_gather | solution.py:123
  246.3 3.5 fusion.30
  249.8 70.2 %all-gather.11.cloned.1.call-done = bf16[8,32,8192]{2,1,0:T(8,128)(2,1)} async-done(((bf16[1,32,8192]{2,1,0:T(8,128)(2,1)}), bf16[8,32,8192]{2,1,0:T(8,128)(2,1)}) %all-gather.11.cloned.1.call-update) | async-done | bytes 4194320 | tf_op jit(solution)/shard_map/all_gather | solution.py:123
  320.0 3.5 fusion.33
  323.6 0.6 collective-permute-start.11
  324.2 1.5 collective-permute-start.8
  325.7 0.5 collective-permute-start.5
  326.3 1.5 collective-permute-start.1
  327.8 10.0 %fusion = f32[8,32,1024]{2,1,0:T(8,128)S(1)} fusion(bf16[8,32,8192]{2,1,0:T(8,128)(2,1)} %all-gather.11.cloned.1.call-done, bf16[8192,1024]{1,0:T(8,128)(2,1)} %param.7), kind=kOutput, calls=%fused_computation | convolution fusion | flops 4294967296 | bytes 22020096 | tf_op jit(solution)/shard_map/dot_general | solution.py:171
  338.1 6.4 %fusion.2 = f32[8,32,1024]{2,1,0:T(8,128)S(1)} fusion(bf16[8,32,8192]{2,1,0:T(8,128)(2,1)} %all-gather.9.cloned.1.call-done, bf16[8192,1024]{1,0:T(8,128)(2,1)S(1)} %bitcast.141), kind=kOutput, calls=%fused_computation.2 | convolution fusion | flops 4294967296 | bytes 22020096 | tf_op jit(solution)/shard_map/dot_general | solution.py:171
  344.5 0.9 collective-permute-start.12
  345.4 6.6 %fusion.4 = f32[8,32,1024]{2,1,0:T(8,128)S(1)} fusion(bf16[8,32,8192]{2,1,0:T(8,128)(2,1)} %all-gather.7.cloned.1.call-done, bf16[8192,1024]{1,0:T(8,128)(2,1)S(1)} %bitcast.141), kind=kOutput, calls=%fused_computation.4 | convolution fusion | flops 4294967296 | bytes 22020096 | tf_op jit(solution)/shard_map/dot_general | solution.py:171
  352.1 1.2 collective-permute-start.9
  353.3 0.9 collective-permute-start.6
  354.3 1.2 collective-permute-start.2
  355.6 1.7 collective-permute-start.13
  357.2 6.4 %fusion.6 = f32[8,32,1024]{2,1,0:T(8,128)S(1)} fusion(bf16[8,32,8192]{2,1,0:T(8,128)(2,1)} %all-gather.5.cloned.1.call-done, bf16[8192,1024]{1,0:T(8,128)(2,1)S(1)} %bitcast.141), kind=kOutput, calls=%fused_computation.6 | convolution fusion | flops 4294967296 | bytes 22020096 | tf_op jit(solution)/shard_map/dot_general | solution.py:171
  363.6 1.4 collective-permute-start.10
  365.1 1.7 collective-permute-start.7
  366.7 1.4 collective-permute-start.3
  368.1 0.3 fusion.23
  368.4 2.3 collective-permute-done.10
  371.0 1.1 collective-permute-done.7
  372.1 0.3 fusion.21
  372.4 0.4 collective-permute-done.3
  373.1 1.5 pad_maximum_fusion.1
  (55 shorter events, 2.2 us)
Async XLA Ops:
  6.5 5.0 %copy-start.1 = (s32[64]{0:T(128)S(1)}, s32[64]{0:T(128)}, u32[]{:S(2)}) copy-start(s32[64]{0:T(128)} %param.10) | copy-start | bytes 772
  6.5 5.0 %copy-start = (s32[2,8]{1,0:T(2,128)S(1)}, s32[2,8]{1,0:T(2,128)}, u32[]{:S(2)}) copy-start(s32[2,8]{1,0:T(2,128)} %param.11) | copy-start | bytes 196
  6.5 91.7 %all-gather.5.cloned.1.call-start = ((), (), s32[]{:S(2)}) async-start(), calls=%async_computation.1 | async-start | bytes 4718592 | tf_op jit(solution)/shard_map/all_gather | solution.py:123
  9.5 163.0 %all-gather.7.cloned.1.call-start = ((), (), s32[]{:S(2)}) async-start(), calls=%async_computation.2 | async-start | bytes 4718592 | tf_op jit(solution)/shard_map/all_gather | solution.py:123
  10.2 236.1 %all-gather.9.cloned.1.call-start = ((), (), s32[]{:S(2)}) async-start(), calls=%async_computation.3 | async-start | bytes 4718592 | tf_op jit(solution)/shard_map/all_gather | solution.py:123
  11.0 309.0 %all-gather.11.cloned.1.call-start = ((), (), s32[]{:S(2)}) async-start(), calls=%async_computation.4 | async-start | bytes 4718592 | tf_op jit(solution)/shard_map/all_gather | solution.py:123
  24.0 40.4 %all-to-all-start = ((bf16[16,64,512]{2,1,0:T(8,128)(2,1)}), bf16[16,64,512]{2,1,0:T(8,128)(2,1)S(1)}, u32[]{:S(2)}, u32[]{:S(2)}) async-start(bf16[16,64,512]{2,1,0:T(8,128)(2,1)} %bitcast.20), calls=%async_computation | async-start | bytes 2097152 | tf_op jit(solution)/shard_map/all_to_all | solution.py:158
  36.9 29.2 %collective-permute-start = (bf16[64,8192]{1,0:T(8,128)(2,1)S(1)}, bf16[64,8192]{1,0:T(8,128)(2,1)}, u32[]{:S(2)}, u32[]{:S(2)}) collective-permute-start(bf16[64,8192]{1,0:T(8,128)(2,1)S(1)} %get-tuple-element.12), channel_id=1, source_target_pairs={{0,1},{1,0},{2,3},{3,2},{4,5},{5,4},{6,7},{7,6},{8,9},{9,8},{10,11... | collective-permute-start | bytes 3145736 | tf_op jit(solution)/shard_map/ppermute | solution.py:100
  64.6 14.3 %collective-permute-start.4 = (bf16[8,64,512]{2,1,0:T(8,128)(2,1)S(1)}, bf16[8,64,512]{2,1,0:T(8,128)(2,1)S(1)}, u32[]{:S(2)}, u32[]{:S(2)}) collective-permute-start(bf16[8,64,512]{2,1,0:T(8,128)(2,1)S(1)} %dynamic-slice_dynamic-update-slice_fusion), channel_id=1, source_target_pairs={{0,16},{16,0},{1,17},{17,1},{2,18},{18,2},{3,19},{19,3},{4,20},{20... | collective-permute-start | bytes 1572872 | tf_op jit(solution)/shard_map/ppermute | solution.py:100
  323.6 20.8 %collective-permute-start.11 = (bf16[8,64,32]{1,2,0:T(8,128)(2,1)S(1)}, bf16[8,64,32]{1,2,0:T(8,128)(2,1)S(1)}, u32[]{:S(2)}, u32[]{:S(2)}) collective-permute-start(bf16[8,64,32]{1,2,0:T(8,128)(2,1)S(1)} %get-tuple-element.22), channel_id=1, source_target_pairs={{0,2},{4,6},{8,10},{12,14},{2,0},{6,4},{10,8},{14,12},{1,3},{5,7},... | collective-permute-start | bytes 98312 | tf_op jit(solution)/shard_map/ppermute | solution.py:147
  324.2 27.8 %collective-permute-start.8 = (bf16[8,64,32]{1,2,0:T(8,128)(2,1)S(1)}, bf16[8,64,32]{1,2,0:T(8,128)(2,1)S(1)}, u32[]{:S(2)}, u32[]{:S(2)}) collective-permute-start(bf16[8,64,32]{1,2,0:T(8,128)(2,1)S(1)} %get-tuple-element.21), channel_id=1, source_target_pairs={{0,2},{4,6},{8,10},{12,14},{2,0},{6,4},{10,8},{14,12},{1,3},{5,7},... | collective-permute-start | bytes 98312 | tf_op jit(solution)/shard_map/ppermute | solution.py:147
  325.7 27.6 %collective-permute-start.5 = (bf16[8,64,32]{1,2,0:T(8,128)(2,1)S(1)}, bf16[8,64,32]{1,2,0:T(8,128)(2,1)S(1)}, u32[]{:S(2)}, u32[]{:S(2)}) collective-permute-start(bf16[8,64,32]{1,2,0:T(8,128)(2,1)S(1)} %get-tuple-element.20), channel_id=1, source_target_pairs={{0,2},{4,6},{8,10},{12,14},{2,0},{6,4},{10,8},{14,12},{1,3},{5,7},... | collective-permute-start | bytes 98312 | tf_op jit(solution)/shard_map/ppermute | solution.py:147
  326.3 11.6 %slice-start = ((s8[16777216]{0:T(1024)(128)(4,1)}), s8[4194304]{0:T(1024)(128)(4,1)S(1)}, s32[]{:S(2)}) async-start(s8[16777216]{0:T(1024)(128)(4,1)} %bitcast.140), calls=%async_computation.5 | async-start | bytes 8388608
  326.3 11.6 %slice-start.1 = ((s8[16777216]{0:T(1024)(128)(4,1)}), s8[4194304]{0:T(1024)(128)(4,1)S(1)}, s32[]{:S(2)}) async-start(s8[16777216]{0:T(1024)(128)(4,1)} %bitcast.140), calls=%async_computation.6 | async-start | bytes 8388608
  326.3 11.6 %slice-start.2 = ((s8[16777216]{0:T(1024)(128)(4,1)}), s8[4194304]{0:T(1024)(128)(4,1)S(1)}, s32[]{:S(2)}) async-start(s8[16777216]{0:T(1024)(128)(4,1)} %bitcast.140), calls=%async_computation.7 | async-start | bytes 8388608
  326.3 11.8 %slice-start.3 = ((s8[16777216]{0:T(1024)(128)(4,1)}), s8[4194304]{0:T(1024)(128)(4,1)S(1)}, s32[]{:S(2)}) async-start(s8[16777216]{0:T(1024)(128)(4,1)} %bitcast.140), calls=%async_computation.8 | async-start | bytes 8388608
  326.3 28.0 %collective-permute-start.1 = (bf16[8,64,32]{1,2,0:T(8,128)(2,1)S(1)}, bf16[8,64,32]{1,2,0:T(8,128)(2,1)S(1)}, u32[]{:S(2)}, u32[]{:S(2)}) collective-permute-start(bf16[8,64,32]{1,2,0:T(8,128)(2,1)S(1)} %get-tuple-element.19), channel_id=1, source_target_pairs={{0,2},{4,6},{8,10},{12,14},{2,0},{6,4},{10,8},{14,12},{1,3},{5,7},... | collective-permute-start | bytes 98312 | tf_op jit(solution)/shard_map/ppermute | solution.py:147
  344.5 11.0 %collective-permute-start.12 = (bf16[8,64,32]{1,2,0:T(8,128)(2,1)S(1)}, bf16[8,64,32]{1,2,0:T(8,128)(2,1)S(1)}, u32[]{:S(2)}, u32[]{:S(2)}) collective-permute-start(bf16[8,64,32]{1,2,0:T(8,128)(2,1)S(1)} %add.147), channel_id=1, source_target_pairs={{0,4},{2,6},{8,12},{10,14},{4,0},{6,2},{12,8},{14,10},{1,5},{3,7},... | collective-permute-start | bytes 98312 | tf_op jit(solution)/shard_map/ppermute | solution.py:147
  352.1 11.5 %collective-permute-start.9 = (bf16[8,64,32]{1,2,0:T(8,128)(2,1)S(1)}, bf16[8,64,32]{1,2,0:T(8,128)(2,1)S(1)}, u32[]{:S(2)}, u32[]{:S(2)}) collective-permute-start(bf16[8,64,32]{1,2,0:T(8,128)(2,1)S(1)} %add.143), channel_id=1, source_target_pairs={{0,4},{2,6},{8,12},{10,14},{4,0},{6,2},{12,8},{14,10},{1,5},{3,7},... | collective-permute-start | bytes 98312 | tf_op jit(solution)/shard_map/ppermute | solution.py:147
  353.3 11.7 %collective-permute-start.6 = (bf16[8,64,32]{1,2,0:T(8,128)(2,1)S(1)}, bf16[8,64,32]{1,2,0:T(8,128)(2,1)S(1)}, u32[]{:S(2)}, u32[]{:S(2)}) collective-permute-start(bf16[8,64,32]{1,2,0:T(8,128)(2,1)S(1)} %add.139), channel_id=1, source_target_pairs={{0,4},{2,6},{8,12},{10,14},{4,0},{6,2},{12,8},{14,10},{1,5},{3,7},... | collective-permute-start | bytes 98312 | tf_op jit(solution)/shard_map/ppermute | solution.py:147
  354.3 12.4 %collective-permute-start.2 = (bf16[8,64,32]{1,2,0:T(8,128)(2,1)S(1)}, bf16[8,64,32]{1,2,0:T(8,128)(2,1)S(1)}, u32[]{:S(2)}, u32[]{:S(2)}) collective-permute-start(bf16[8,64,32]{1,2,0:T(8,128)(2,1)S(1)} %add.124), channel_id=1, source_target_pairs={{0,4},{2,6},{8,12},{10,14},{4,0},{6,2},{12,8},{14,10},{1,5},{3,7},... | collective-permute-start | bytes 98312 | tf_op jit(solution)/shard_map/ppermute | solution.py:147
  355.6 12.6 %collective-permute-start.13 = (bf16[8,64,32]{1,2,0:T(8,128)(2,1)S(1)}, bf16[8,64,32]{1,2,0:T(8,128)(2,1)S(1)}, u32[]{:S(2)}, u32[]{:S(2)}) collective-permute-start(bf16[8,64,32]{1,2,0:T(8,128)(2,1)S(1)} %add.148), channel_id=1, source_target_pairs={{0,8},{2,10},{4,12},{6,14},{8,0},{10,2},{12,4},{14,6},{1,9},{3,11}... | collective-permute-start | bytes 98312 | tf_op jit(solution)/shard_map/ppermute | solution.py:147
  363.6 7.1 %collective-permute-start.10 = (bf16[8,64,32]{1,2,0:T(8,128)(2,1)S(1)}, bf16[8,64,32]{1,2,0:T(8,128)(2,1)S(1)}, u32[]{:S(2)}, u32[]{:S(2)}) collective-permute-start(bf16[8,64,32]{1,2,0:T(8,128)(2,1)S(1)} %add.144), channel_id=1, source_target_pairs={{0,8},{2,10},{4,12},{6,14},{8,0},{10,2},{12,4},{14,6},{1,9},{3,11}... | collective-permute-start | bytes 98312 | tf_op jit(solution)/shard_map/ppermute | solution.py:147
  365.1 7.1 %collective-permute-start.7 = (bf16[8,64,32]{1,2,0:T(8,128)(2,1)S(1)}, bf16[8,64,32]{1,2,0:T(8,128)(2,1)S(1)}, u32[]{:S(2)}, u32[]{:S(2)}) collective-permute-start(bf16[8,64,32]{1,2,0:T(8,128)(2,1)S(1)} %add.140), channel_id=1, source_target_pairs={{0,8},{2,10},{4,12},{6,14},{8,0},{10,2},{12,4},{14,6},{1,9},{3,11}... | collective-permute-start | bytes 98312 | tf_op jit(solution)/shard_map/ppermute | solution.py:147
  366.7 6.1 %collective-permute-start.3 = (bf16[8,64,32]{1,2,0:T(8,128)(2,1)S(1)}, bf16[8,64,32]{1,2,0:T(8,128)(2,1)S(1)}, u32[]{:S(2)}, u32[]{:S(2)}) collective-permute-start(bf16[8,64,32]{1,2,0:T(8,128)(2,1)S(1)} %add.125), channel_id=1, source_target_pairs={{0,8},{2,10},{4,12},{6,14},{8,0},{10,2},{12,4},{14,6},{1,9},{3,11}... | collective-permute-start | bytes 98312 | tf_op jit(solution)/shard_map/ppermute | solution.py:147
Sparse Core Ops, SparseCore 0:
  9.6 88.5 all-gather.4
  100.3 72.1 all-gather.6
  174.6 71.6 all-gather.8
  248.3 71.6 all-gather.10

commit v2 on v1

--- a/solution.py
+++ b/solution.py
@@ -92,8 +92,14 @@
 
 ACROSS = both_ways([(0, 1), (2, 3), (4, 5), (6, 7)])
 NEAR = both_ways([(0, 2), (1, 3), (4, 6), (5, 7)])
+MIDDLE = both_ways([(2, 4), (3, 5)])
+OUTWARD = [(2, 0), (3, 1), (4, 6), (5, 7)]
 FAR = both_ways([(0, 4), (1, 5), (2, 6), (3, 7)])
-CHUNKS = 4
+HALF = BLOCK // 2
+
+
+def send(value, pairs):
+    return lax.ppermute(value, "tensor", pairs)
 
 
 def swap(value, axis):
@@ -104,14 +110,15 @@
     tokens, query_weight, adapter_down_maps, adapter_up_maps, adapter_home_slot, adapter_per_block
 ):
     me = lax.axis_index("tensor")
+    z, y = me // 2, me % 2
     store = lax.axis_index("store")
     group = lax.axis_index("groups")
     myself = me * 2 + store
+    inner = (z == 1) | (z == 2)
     held, rank, width = adapter_down_maps.shape
     columns = query_weight.shape[1]
     part = columns // 2
     rows = tokens[0]
-    step = BLOCK // CHUNKS
 
     store_slots = find_slots(adapter_home_slot, adapter_per_block)
     owner = store_slots // held
@@ -119,33 +126,9 @@
     picked = jnp.max(jnp.where(owner == myself, inside, 0), axis=1)
     owner_row = lax.dynamic_index_in_dim(owner, store, 0, keepdims=False)
 
-    gathered = [
-        lax.all_gather(rows[c * step : (c + 1) * step], "tensor", axis=0) for c in range(CHUNKS)
-    ]
-
     def pick(maps, index):
         local = lax.dynamic_index_in_dim(picked, index, 0, keepdims=False)
         return lax.dynamic_index_in_dim(maps, local, 0, keepdims=False)
-
-    down_own = pick(adapter_down_maps, store)
-    down_swapped = swap(pick(adapter_down_maps, 1 - store), "store")
-    candidates = jnp.concatenate([down_own, down_swapped])
-    use_own = (owner_row == myself)[:, None, None]
-    use_swapped = (owner_row == me * 2 + 1 - store)[:, None, None]
-
-    def shrink(chunk):
-        value = lax.dot_general(
-            candidates,
-            chunk.reshape(8 * step, width),
-            (((1,), (1,)), ((), ())),
-            preferred_element_type=jnp.float32,
-        )
-        value = value.reshape(2, rank, 8, step).transpose(0, 2, 1, 3)
-        value = jnp.where(use_own, value[0], jnp.where(use_swapped, value[1], 0))
-        value = value.astype(jnp.bfloat16)
-        for pairs in (ACROSS, NEAR, FAR):
-            value = value + lax.ppermute(value, "tensor", pairs)
-        return value
 
     def columns_of(up):
         halves = up.reshape(rank, 8, 2, part)
@@ -166,16 +149,85 @@
         [jnp.where(group == 0, up_half, up_other), jnp.where(group == 0, up_other, up_half)], axis=2
     )
 
-    outputs = []
-    for chunk in gathered:
-        base = jnp.dot(
-            chunk.reshape(8 * step, width), query_weight, preferred_element_type=jnp.float32
+    candidates = jnp.concatenate(
+        [pick(adapter_down_maps, store), swap(pick(adapter_down_maps, 1 - store), "store")]
+    )
+
+    z_of = {
+        "own": z,
+        "near": z + 1 - 2 * (z % 2),
+        "far": jnp.where(z < 2, 2, 1),
+        "last": jnp.where(z < 2, 3, 0),
+    }
+
+    def place(name, half):
+        column = 1 - y if name.endswith("_y") else y
+        return z_of[name.removesuffix("_y")] * 2 + column, half
+
+    def work(state, arrivals):
+        base, shrunk = state
+        block = jnp.concatenate([value for _, value in arrivals])
+        product = jnp.dot(block, query_weight, preferred_element_type=jnp.float32)
+        small = lax.dot_general(
+            candidates, block, (((1,), (1,)), ((), ())), preferred_element_type=jnp.float32
         )
-        grown = jnp.einsum("brn,brf->bnf", shrink(chunk), up, preferred_element_type=jnp.float32)
-        value = base.reshape(8, step, columns) + 0.5 * grown
-        outputs.append(value.astype(jnp.bfloat16))
-    query = jnp.concatenate(outputs, axis=1)
-    return query.reshape(1, 8 * BLOCK, columns)
+        for at, (name_half, _) in enumerate(arrivals):
+            index, half = place(*name_half)
+            home = lax.dynamic_index_in_dim(owner_row, index, 0, keepdims=False)
+            cut = slice(at * HALF, (at + 1) * HALF)
+            value = jnp.where(
+                home == myself,
+                small[:rank, cut],
+                jnp.where(home == me * 2 + 1 - store, small[rank:, cut], 0),
+            ).astype(jnp.bfloat16)
+            shrunk = lax.dynamic_update_slice(shrunk, value[None, None], (index, half, 0, 0))
+            base = lax.dynamic_update_slice(base, product[cut], (index * BLOCK + half * HALF, 0))
+        return base, shrunk
+
+    have = {("own", 0): rows[:HALF], ("own", 1): rows[HALF:]}
+    state = (
+        jnp.zeros((8 * BLOCK, columns), jnp.float32),
+        jnp.zeros((8, 2, rank, HALF), jnp.bfloat16),
+    )
+    steps = [
+        (("own", 0), ("own", 0, NEAR), ("own", 0)),
+        (("own", 1), ("own", 1, NEAR), ("own", 1)),
+        (("near", 0), ("far", 0, OUTWARD), ("near", 0)),
+        (("far", 0), ("far", 1, OUTWARD), ("near", 1)),
+        (("far", 1), ("last", 0, OUTWARD), None),
+        (("last", 0), ("last", 1, OUTWARD), None),
+        (("last", 1), ("own_y", 1, NEAR), None),
+    ]
+    inner_has = {}
+    fresh = [(("own", 0), have["own", 0]), (("own", 1), have["own", 1])]
+    for across, along, middle in steps:
+        got_y = send(have[across], ACROSS)
+        name, half, pairs = along
+        sent = inner_has[name, half] if pairs is OUTWARD else have[name, half]
+        got_z = send(sent, pairs)
+        got_m = None if middle is None else send(have[middle], MIDDLE)
+        state = work(state, fresh)
+        got_y, got_z, got_m, state, have, inner_has = lax.optimization_barrier(
+            (got_y, got_z, got_m, state, have, inner_has)
+        )
+        if middle is not None:
+            inner_has[{"own": "far", "near": "last"}[middle[0]], middle[1]] = got_m
+        if pairs is OUTWARD:
+            arrived = (name, half)
+            got_z = jnp.where(inner, inner_has[arrived], got_z)
+        else:
+            arrived = ({"own": "near", "own_y": "near_y"}[name], half)
+        have[arrived] = got_z
+        seen_y = ("own_y" if across[0] == "own" else across[0] + "_y", across[1])
+        have[seen_y] = got_y
+        fresh = [(arrived, got_z), (seen_y, got_y)]
+    base, shrunk = work(state, fresh)
+
+    for pairs in (ACROSS, NEAR, FAR):
+        shrunk = shrunk + send(shrunk, pairs)
+    grown = jnp.einsum("bhrn,brf->bhnf", shrunk, up, preferred_element_type=jnp.float32)
+    query = base + 0.5 * grown.reshape(8 * BLOCK, columns)
+    return query.astype(jnp.bfloat16)[None]
 
 
 def body(tokens, *rest):

time: 382 us -> 296 us (0.77)
  waiting for transfers between devices: 259 us -> 83.9 us
  matrix products: 44.3 us -> 87.9 us
  local copies, waits for them, and re-layouts: 13.9 us -> 44.4 us
  other arithmetic: 3.73 us -> 12.8 us
  starting transfers between devices: 24.1 us -> 32.5 us
    all_gather x4 -> x0, waiting for transfers between devices: 231 us -> none  [chain_body(): lax.all_gather(rows[c * step:(c + 1) * step], 'tensor', axis=0)]
    ppermute x12 -> x21, waiting for transfers between devices: 3.8 us -> 83.9 us  [send(): return lax.ppermute(value, 'tensor', pairs)]
    dot_general x12 -> x17, matrix products: 44.3 us -> 87.9 us  [the longest x8 68.3 us: work(): product = jnp.dot(block, query_weight, preferred_element_type=jnp.float32)]
    dynamic_update_slice x0 -> x32, local copies, waits for them, and re-layouts: none -> 11.9 us  [the longest x16 11.7 us: work(): lax.dynamic_update_slice(base, product[cut], (index * BLOCK + half * HALF...]
    all_to_all x1, waiting for transfers between devices: 11.6 us -> 0.01 us  [chain_body(): lax.all_to_all(up_sent.reshape(16, rank, part), ('tensor', 'store'), spli...]
    ppermute x12 -> x21, starting transfers between devices: 14.6 us -> 26.2 us  [send(): return lax.ppermute(value, 'tensor', pairs)]
    ppermute x2, waiting for transfers between devices: 11.5 us -> 0.01 us  [swap(): return lax.ppermute(value, axis, [(0, 1), (1, 0)])]
    unnamed x21 -> x28, local copies, waits for them, and re-layouts: 0.56 us -> 8.33 us
  transfers between devices with their start and end apart: 19 -> 24, of which waited for: 9 -> 13; matrix products, arithmetic and copies ran while one was open for 14% -> 43% of each run, Pallas kernels for 0% -> 0%
where the time goes in v2:
time: 296 us; the launch traced here: 295 us
  matrix products  87.9 us (30%)
  waiting for transfers between devices  83.9 us (28%)
  local copies, waits for them, and re-layouts  44.4 us (15%)
  between operations  33 us (11%)
  starting transfers between devices  32.5 us (11%)
  other arithmetic  12.8 us (4%)
    ppermute x21, waiting for transfers between devices, send(): return lax.ppermute(value, 'tensor', pairs)  83.9 us
    dot_general x8, matrix products, work(): product = jnp.dot(block, query_weight, preferred_element_type=jnp.float32)  68.3 us
    ppermute x21, starting transfers between devices, send(): return lax.ppermute(value, 'tensor', pairs)  26.2 us
    dot_general x8, matrix products, work(): lax.dot_general(candidates, block, (((1,), (1,)), ((), ())), preferred_el...  18.9 us
    dynamic_update_slice x16, local copies, waits for them, and re-layouts, work(): lax.dynamic_update_slice(base, product[cut], (index * BLOCK + half * HALF...  11.7 us
    unnamed x28, local copies, waits for them, and re-layouts  8.33 us
  transfers between devices with their start and end apart: 24, of which 13 were waited for; matrix products, arithmetic and copies ran while one was open for 43% of the time, Pallas kernels for 0%

profile of v2, /device:TPU:0, one launch (start us, length us, event | category | flops | bytes accessed | tf_op | source)
XLA Modules:
  0.0 294.5 jit_solution(14871522776378557990)
XLA Ops:
  0.0 3.1 %slice_bitcast_fusion = (bf16[64,8192]{1,0:T(8,128)(2,1)}, bf16[64,8192]{1,0:T(8,128)(2,1)}) fusion(bf16[1,128,8192]{2,1,0:T(8,128)(2,1)} %param.6), kind=kLoop, calls=%fused_computation.25 | loop fusion | bytes 4194304 | tf_op jit(solution)/shard_map/slice | solution.py:187
  3.1 3.0 %collective-permute-start = (bf16[64,8192]{1,0:T(8,128)(2,1)}, bf16[64,8192]{1,0:T(8,128)(2,1)}, u32[]{:S(2)}, u32[]{:S(2)}) collective-permute-start(bf16[64,8192]{1,0:T(8,128)(2,1)} %get-tuple-element.106), channel_id=1, source_target_pairs={{0,2},{4,6},{8,10},{12,14},{2,0},{6,4},{10,8},{14,12},{1,3},{5,7},... | collective-permute-start | bytes 3145736 | tf_op jit(solution)/shard_map/ppermute | solution.py:102
  6.0 1.6 collective-permute-start.1
  7.6 1.7 collective-permute-start.2
  14.2 3.2 %dynamic-slice_bitcast_fusion.1 = (bf16[64,8192]{1,0:T(8,128)(2,1)}, bf16[64,8192]{1,0:T(8,128)(2,1)}) fusion(bf16[4,64,8192]{2,1,0:T(8,128)(2,1)} %param.8, s32[]{:T(128)S(6)} %select_n.421, s32[]{:T(128)S(6)} %select_n.423), kind=kLoop, calls=%fused_computation.24 | loop fusion | bytes 4194312 | tf_op jit(solution)/shard_map/jit(dynamic_index_in_dim)/squeeze | solution.py:131
  21.2 1.7 constant_dynamic-slice_fusion.4
  24.5 2.7 constant_dynamic-slice_fusion.1
  28.9 4.9 %all-to-all-start = ((bf16[16,64,512]{2,1,0:T(8,128)(2,1)}), bf16[16,64,512]{2,1,0:T(8,128)(2,1)S(1)}, u32[]{:S(2)}, u32[]{:S(2)}) async-start(bf16[16,64,512]{2,1,0:T(8,128)(2,1)} %bitcast.36), calls=%async_computation | async-start | bytes 2097152 | tf_op jit(solution)/shard_map/all_to_all | solution.py:141
  60.0 8.8 %fusion.10 = f32[128,1024]{1,0:T(8,128)S(1)} fusion(bf16[8192,1024]{1,0:T(8,128)(2,1)} %param.7, bf16[64,8192]{1,0:T(8,128)(2,1)} %get-tuple-element.52, bf16[64,8192]{1,0:T(8,128)(2,1)} %get-tuple-element.106), kind=kOutput, calls=%fused_computation.18 | convolution fusion | flops 2151677952 | bytes 19398656 | tf_op jit(solution)/shard_map/dot_general | solution.py:170
  68.7 2.5 broadcast_in_dim.93
  72.7 2.6 fusion.9
  75.7 1.9 collective-permute-start.4
  77.5 1.4 collective-permute-start.5
  78.9 1.7 collective-permute-start.6
  83.2 2.2 fusion.76
  85.6 8.1 %fusion.80 = f32[128,1024]{1,0:T(8,128)S(1)} fusion(bf16[128,8192]{1,0:T(8,128)(2,1)S(1)} %constant_dynamic-update-slice_fusion, bf16[8192,1024]{1,0:T(8,128)(2,1)} %param.7), kind=kOutput, calls=%fused_computation.179 | convolution fusion | flops 2147483648 | bytes 19398656 | tf_op jit(solution)/shard_map/dot_general | solution.py:170
  100.4 1.5 collective-permute-start.22
  107.1 8.4 %fusion.81 = f32[128,1024]{1,0:T(8,128)S(1)} fusion(bf16[128,8192]{1,0:T(8,128)(2,1)S(1)} %constant_dynamic-update-slice_fusion.2, bf16[8192,1024]{1,0:T(8,128)(2,1)} %param.7), kind=kOutput, calls=%fused_computation.180 | convolution fusion | flops 2147483648 | bytes 19398656 | tf_op jit(solution)/shard_map/dot_general | solution.py:170
  116.8 1.9 fusion.75
  121.8 5.4 %collective-permute-done.7 = bf16[64,8192]{1,0:T(8,128)(2,1)} collective-permute-done((bf16[64,8192]{1,0:T(8,128)(2,1)}, bf16[64,8192]{1,0:T(8,128)(2,1)}, u32[]{:S(2)}, u32[]{:S(2)}) %collective-permute-start.7) | collective-permute-done | bytes 1048608 | tf_op jit(solution)/shard_map/ppermute | solution.py:102
  127.2 18.1 %collective-permute-done.8 = bf16[64,8192]{1,0:T(8,128)(2,1)} collective-permute-done((bf16[64,8192]{1,0:T(8,128)(2,1)}, bf16[64,8192]{1,0:T(8,128)(2,1)}, u32[]{:S(2)}, u32[]{:S(2)}) %collective-permute-start.8) | collective-permute-done | bytes 1048608 | tf_op jit(solution)/shard_map/ppermute | solution.py:102
  145.2 2.3 broadcast_select_fusion.3
  147.5 1.5 collective-permute-start.10
  149.0 2.6 fusion.7
  153.9 8.8 %fusion.8 = f32[128,1024]{1,0:T(8,128)S(1)} fusion(bf16[8192,1024]{1,0:T(8,128)(2,1)} %param.7, bf16[64,8192]{1,0:T(8,128)(2,1)} %collective-permute-done.7, bf16[64,8192]{1,0:T(8,128)(2,1)} %broadcast_select_fusion.3), kind=kOutput, calls=%fused_computation.16 | convolution fusion | flops 2151677952 | bytes 19398656 | tf_op jit(solution)/shard_map/dot_general | solution.py:170
  164.1 6.3 %collective-permute-done.10 = bf16[64,8192]{1,0:T(8,128)(2,1)} collective-permute-done((bf16[64,8192]{1,0:T(8,128)(2,1)}, bf16[64,8192]{1,0:T(8,128)(2,1)}, u32[]{:S(2)}, u32[]{:S(2)}) %collective-permute-start.10) | collective-permute-done | bytes 1048608 | tf_op jit(solution)/shard_map/ppermute | solution.py:102
  170.4 5.8 %collective-permute-done.11 = bf16[64,8192]{1,0:T(8,128)(2,1)S(1)} collective-permute-done((bf16[64,8192]{1,0:T(8,128)(2,1)}, bf16[64,8192]{1,0:T(8,128)(2,1)S(1)}, u32[]{:S(2)}, u32[]{:S(2)}) %collective-permute-start.11) | collective-permute-done | bytes 1048608 | tf_op jit(solution)/shard_map/ppermute | solution.py:102
  178.0 2.6 fusion.5
  180.9 1.5 collective-permute-start.14
  182.4 8.8 %fusion.6 = f32[128,1024]{1,0:T(8,128)S(1)} fusion(bf16[8192,1024]{1,0:T(8,128)(2,1)} %param.7, bf16[64,8192]{1,0:T(8,128)(2,1)} %collective-permute-done.10, bf16[64,8192]{1,0:T(8,128)(2,1)} %broadcast_select_fusion.2), kind=kOutput, calls=%fused_computation.14 | convolution fusion | flops 2151677952 | bytes 19398656 | tf_op jit(solution)/shard_map/dot_general | solution.py:170
  192.7 6.4 %collective-permute-done.13 = bf16[64,8192]{1,0:T(8,128)(2,1)} collective-permute-done((bf16[64,8192]{1,0:T(8,128)(2,1)}, bf16[64,8192]{1,0:T(8,128)(2,1)}, u32[]{:S(2)}, u32[]{:S(2)}) %collective-permute-start.13) | collective-permute-done | bytes 1048608 | tf_op jit(solution)/shard_map/ppermute | solution.py:102
  199.1 7.2 %collective-permute-done.14 = bf16[64,8192]{1,0:T(8,128)(2,1)S(1)} collective-permute-done((bf16[64,8192]{1,0:T(8,128)(2,1)S(1)}, bf16[64,8192]{1,0:T(8,128)(2,1)S(1)}, u32[]{:S(2)}, u32[]{:S(2)}) %collective-permute-start.14) | collective-permute-done | bytes 1048608 | tf_op jit(solution)/shard_map/ppermute | solution.py:102
  207.5 1.5 collective-permute-start.15
  209.0 2.6 fusion.3
  213.1 8.8 %fusion.4 = f32[128,1024]{1,0:T(8,128)S(1)} fusion(bf16[8192,1024]{1,0:T(8,128)(2,1)} %param.7, bf16[64,8192]{1,0:T(8,128)(2,1)} %collective-permute-done.13, bf16[64,8192]{1,0:T(8,128)(2,1)} %broadcast_select_fusion.1), kind=kOutput, calls=%fused_computation.12 | convolution fusion | flops 2151677952 | bytes 19398656 | tf_op jit(solution)/shard_map/dot_general | solution.py:170
  223.4 4.6 %collective-permute-done.15 = bf16[64,8192]{1,0:T(8,128)(2,1)} collective-permute-done((bf16[64,8192]{1,0:T(8,128)(2,1)}, bf16[64,8192]{1,0:T(8,128)(2,1)}, u32[]{:S(2)}, u32[]{:S(2)}) %collective-permute-start.15) | collective-permute-done | bytes 1048608 | tf_op jit(solution)/shard_map/ppermute | solution.py:102
  227.9 5.6 %collective-permute-done.16 = bf16[64,8192]{1,0:T(8,128)(2,1)S(1)} collective-permute-done((bf16[64,8192]{1,0:T(8,128)(2,1)S(1)}, bf16[64,8192]{1,0:T(8,128)(2,1)S(1)}, u32[]{:S(2)}, u32[]{:S(2)}) %collective-permute-start.16) | collective-permute-done | bytes 1048608 | tf_op jit(solution)/shard_map/ppermute | solution.py:102
  235.3 2.6 fusion.1
  238.2 8.8 %fusion.2 = f32[128,1024]{1,0:T(8,128)S(1)} fusion(bf16[8192,1024]{1,0:T(8,128)(2,1)} %param.7, bf16[64,8192]{1,0:T(8,128)(2,1)} %collective-permute-done.15, bf16[64,8192]{1,0:T(8,128)(2,1)} %broadcast_select_fusion), kind=kOutput, calls=%fused_computation.10 | convolution fusion | flops 2151677952 | bytes 19398656 | tf_op jit(solution)/shard_map/dot_general | solution.py:170
  248.4 5.5 %collective-permute-done.17 = bf16[64,8192]{1,0:T(8,128)(2,1)S(1)} collective-permute-done((bf16[64,8192]{1,0:T(8,128)(2,1)}, bf16[64,8192]{1,0:T(8,128)(2,1)S(1)}, u32[]{:S(2)}, u32[]{:S(2)}) %collective-permute-start.17) | collective-permute-done | bytes 1048608 | tf_op jit(solution)/shard_map/ppermute | solution.py:102
  254.9 2.3 collective-permute-done.18
  257.3 1.3 constant_dynamic-update-slice_fusion.4
  258.6 1.9 fusion.74
  260.8 1.5 collective-permute-start.19
  262.3 8.1 %fusion.82 = f32[128,1024]{1,0:T(8,128)S(1)} fusion(bf16[128,8192]{1,0:T(8,128)(2,1)S(1)} %constant_dynamic-update-slice_fusion.4, bf16[8192,1024]{1,0:T(8,128)(2,1)} %param.7), kind=kOutput, calls=%fused_computation.181 | convolution fusion | flops 2147483648 | bytes 19398656 | tf_op jit(solution)/shard_map/dot_general | solution.py:170
  271.5 7.6 %collective-permute-done.20 = bf16[8,2,64,64]{2,3,1,0:T(8,128)(2,1)S(1)} collective-permute-done((bf16[8,2,64,64]{2,3,1,0:T(8,128)(2,1)S(1)}, bf16[8,2,64,64]{2,3,1,0:T(8,128)(2,1)S(1)}, u32[]{:S(2)}, u32[]{:S(2)}) %collective-permute-start.20) | collective-permute-done | bytes 131104 | tf_op jit(solution)/shard_map/ppermute | solution.py:102
  281.1 8.3 %collective-permute-done.21 = bf16[8,2,64,64]{2,3,1,0:T(8,128)(2,1)S(1)} collective-permute-done((bf16[8,2,64,64]{2,3,1,0:T(8,128)(2,1)S(1)}, bf16[8,2,64,64]{2,3,1,0:T(8,128)(2,1)S(1)}, u32[]{:S(2)}, u32[]{:S(2)}) %collective-permute-start.21) | collective-permute-done | bytes 131104 | tf_op jit(solution)/shard_map/ppermute | solution.py:102
  290.1 4.4 %fusion = bf16[1024,1024]{1,0:T(8,128)(2,1)} fusion(f32[1024,1024]{1,0:T(8,128)} %slice_dynamic-update-slice_fusion, f32[8,2,64,1024]{3,2,1,0:T(8,128)S(1)} %convolution_multiply_fusion), kind=kLoop, calls=%fused_computation.1 | loop fusion | flops 2097152 | bytes 10485760 | tf_op jit(solution)/shard_map/convert_element_type | solution.py:230
  (129 shorter events, 46.5 us)
Async XLA Ops:
  0.0 9.3 %copy-start.7 = (s32[64]{0:T(128)S(1)}, s32[64]{0:T(128)}, u32[]{:S(2)}) copy-start(s32[64]{0:T(128)} %param.10) | copy-start | bytes 772
  0.0 9.3 %copy-start.6 = (s32[2,8]{1,0:T(2,128)S(1)}, s32[2,8]{1,0:T(2,128)}, u32[]{:S(2)}) copy-start(s32[2,8]{1,0:T(2,128)} %param.11) | copy-start | bytes 196
  3.1 72.6 %collective-permute-start = (bf16[64,8192]{1,0:T(8,128)(2,1)}, bf16[64,8192]{1,0:T(8,128)(2,1)}, u32[]{:S(2)}, u32[]{:S(2)}) collective-permute-start(bf16[64,8192]{1,0:T(8,128)(2,1)} %get-tuple-element.106), channel_id=1, source_target_pairs={{0,2},{4,6},{8,10},{12,14},{2,0},{6,4},{10,8},{14,12},{1,3},{5,7},... | collective-permute-start | bytes 3145736 | tf_op jit(solution)/shard_map/ppermute | solution.py:102
  6.0 69.6 %collective-permute-start.1 = (bf16[64,8192]{1,0:T(8,128)(2,1)}, bf16[64,8192]{1,0:T(8,128)(2,1)}, u32[]{:S(2)}, u32[]{:S(2)}) collective-permute-start(bf16[64,8192]{1,0:T(8,128)(2,1)} %get-tuple-element.106), channel_id=1, source_target_pairs={{0,4},{2,6},{8,12},{10,14},{4,0},{6,2},{12,8},{14,10},{1,5},{3,7},... | collective-permute-start | bytes 3145736 | tf_op jit(solution)/shard_map/ppermute | solution.py:102
  7.6 68.0 %collective-permute-start.2 = (bf16[64,8192]{1,0:T(8,128)(2,1)}, bf16[64,8192]{1,0:T(8,128)(2,1)}, u32[]{:S(2)}, u32[]{:S(2)}) collective-permute-start(bf16[64,8192]{1,0:T(8,128)(2,1)} %get-tuple-element.106), channel_id=1, source_target_pairs={{4,8},{6,10},{8,4},{10,6},{5,9},{7,11},{9,5},{11,7},{20,24},{22,26... | collective-permute-start | bytes 3145736 | tf_op jit(solution)/shard_map/ppermute | solution.py:102
  17.5 55.2 %collective-permute-start.3 = (bf16[64,8192]{1,0:T(8,128)(2,1)}, bf16[64,8192]{1,0:T(8,128)(2,1)}, u32[]{:S(2)}, u32[]{:S(2)}) collective-permute-start(bf16[64,8192]{1,0:T(8,128)(2,1)} %get-tuple-element.104), channel_id=1, source_target_pairs={{0,1},{1,0},{2,3},{3,2},{4,5},{5,4},{6,7},{7,6},{8,9},{9,8},{10,11... | collective-permute-start | bytes 3145736 | tf_op jit(solution)/shard_map/ppermute | solution.py:106
  28.9 66.5 %all-to-all-start = ((bf16[16,64,512]{2,1,0:T(8,128)(2,1)}), bf16[16,64,512]{2,1,0:T(8,128)(2,1)S(1)}, u32[]{:S(2)}, u32[]{:S(2)}) async-start(bf16[16,64,512]{2,1,0:T(8,128)(2,1)} %bitcast.36), calls=%async_computation | async-start | bytes 2097152 | tf_op jit(solution)/shard_map/all_to_all | solution.py:141
  68.7 4.0 %copy-start = (bf16[64,8192]{1,0:T(8,128)(2,1)S(1)}, bf16[64,8192]{1,0:T(8,128)(2,1)}, u32[]{:S(2)}) copy-start(bf16[64,8192]{1,0:T(8,128)(2,1)} %get-tuple-element.103) | copy-start | bytes 3145732
  75.7 26.3 %collective-permute-start.4 = (bf16[64,8192]{1,0:T(8,128)(2,1)}, bf16[64,8192]{1,0:T(8,128)(2,1)}, u32[]{:S(2)}, u32[]{:S(2)}) collective-permute-start(bf16[64,8192]{1,0:T(8,128)(2,1)} %get-tuple-element.52), channel_id=1, source_target_pairs={{0,2},{4,6},{8,10},{12,14},{2,0},{6,4},{10,8},{14,12},{1,3},{5,7},... | collective-permute-start | bytes 3145736 | tf_op jit(solution)/shard_map/ppermute | solution.py:102
  77.5 25.2 %collective-permute-start.5 = (bf16[64,8192]{1,0:T(8,128)(2,1)}, bf16[64,8192]{1,0:T(8,128)(2,1)}, u32[]{:S(2)}, u32[]{:S(2)}) collective-permute-start(bf16[64,8192]{1,0:T(8,128)(2,1)} %get-tuple-element.52), channel_id=1, source_target_pairs={{0,4},{2,6},{8,12},{10,14},{4,0},{6,2},{12,8},{14,10},{1,5},{3,7},... | collective-permute-start | bytes 3145736 | tf_op jit(solution)/shard_map/ppermute | solution.py:102
  78.9 23.8 %collective-permute-start.6 = (bf16[64,8192]{1,0:T(8,128)(2,1)}, bf16[64,8192]{1,0:T(8,128)(2,1)}, u32[]{:S(2)}, u32[]{:S(2)}) collective-permute-start(bf16[64,8192]{1,0:T(8,128)(2,1)} %get-tuple-element.52), channel_id=1, source_target_pairs={{4,8},{6,10},{8,4},{10,6},{5,9},{7,11},{9,5},{11,7},{20,24},{22,26... | collective-permute-start | bytes 3145736 | tf_op jit(solution)/shard_map/ppermute | solution.py:102
  100.4 20.1 %collective-permute-start.22 = (bf16[8,64,512]{2,1,0:T(8,128)(2,1)}, bf16[8,64,512]{2,1,0:T(8,128)(2,1)}, u32[]{:S(2)}, u32[]{:S(2)}) collective-permute-start(bf16[8,64,512]{2,1,0:T(8,128)(2,1)} %dynamic-slice_dynamic-update-slice_fusion), channel_id=1, source_target_pairs={{0,16},{16,0},{1,17},{17,1},{2,18},{18,2},{3,19},{19,3},{4,20},{20... | collective-permute-start | bytes 1572872 | tf_op jit(solution)/shard_map/ppermute | solution.py:106
  102.8 24.4 %collective-permute-start.7 = (bf16[64,8192]{1,0:T(8,128)(2,1)}, bf16[64,8192]{1,0:T(8,128)(2,1)}, u32[]{:S(2)}, u32[]{:S(2)}) collective-permute-start(bf16[64,8192]{1,0:T(8,128)(2,1)} %collective-permute-done.1), channel_id=1, source_target_pairs={{0,2},{4,6},{8,10},{12,14},{2,0},{6,4},{10,8},{14,12},{1,3},{5,7},... | collective-permute-start | bytes 3145736 | tf_op jit(solution)/shard_map/ppermute | solution.py:102
  103.8 41.5 %collective-permute-start.9 = (bf16[64,8192]{1,0:T(8,128)(2,1)}, bf16[64,8192]{1,0:T(8,128)(2,1)S(1)}, u32[]{:S(2)}, u32[]{:S(2)}) collective-permute-start(bf16[64,8192]{1,0:T(8,128)(2,1)} %collective-permute-done.1), channel_id=1, source_target_pairs={{4,8},{6,10},{8,4},{10,6},{5,9},{7,11},{9,5},{11,7},{20,24},{22,26... | collective-permute-start | bytes 3145736 | tf_op jit(solution)/shard_map/ppermute | solution.py:102
  107.1 9.7 %copy-start.1 = (bf16[64,8192]{1,0:T(8,128)(2,1)S(1)}, bf16[64,8192]{1,0:T(8,128)(2,1)}, u32[]{:S(2)}) copy-start(bf16[64,8192]{1,0:T(8,128)(2,1)} %get-tuple-element.103) | copy-start | bytes 3145732
  115.4 29.8 %collective-permute-start.8 = (bf16[64,8192]{1,0:T(8,128)(2,1)}, bf16[64,8192]{1,0:T(8,128)(2,1)}, u32[]{:S(2)}, u32[]{:S(2)}) collective-permute-start(bf16[64,8192]{1,0:T(8,128)(2,1)} %collective-permute-done.2), channel_id=1, source_target_pairs={{4,0},{6,2},{8,12},{10,14},{5,1},{7,3},{9,13},{11,15},{20,16},{22,... | collective-permute-start | bytes 3145736 | tf_op jit(solution)/shard_map/ppermute | solution.py:102
  147.5 22.9 %collective-permute-start.10 = (bf16[64,8192]{1,0:T(8,128)(2,1)}, bf16[64,8192]{1,0:T(8,128)(2,1)}, u32[]{:S(2)}, u32[]{:S(2)}) collective-permute-start(bf16[64,8192]{1,0:T(8,128)(2,1)} %broadcast_select_fusion.3), channel_id=1, source_target_pairs={{0,2},{4,6},{8,10},{12,14},{2,0},{6,4},{10,8},{14,12},{1,3},{5,7},... | collective-permute-start | bytes 3145736 | tf_op jit(solution)/shard_map/ppermute | solution.py:102
  151.8 24.4 %collective-permute-start.11 = (bf16[64,8192]{1,0:T(8,128)(2,1)}, bf16[64,8192]{1,0:T(8,128)(2,1)S(1)}, u32[]{:S(2)}, u32[]{:S(2)}) collective-permute-start(bf16[64,8192]{1,0:T(8,128)(2,1)} %collective-permute-done.6), channel_id=1, source_target_pairs={{4,0},{6,2},{8,12},{10,14},{5,1},{7,3},{9,13},{11,15},{20,16},{22,... | collective-permute-start | bytes 3145736 | tf_op jit(solution)/shard_map/ppermute | solution.py:102
  153.1 23.1 %collective-permute-start.12 = (bf16[64,8192]{1,0:T(8,128)(2,1)}, bf16[64,8192]{1,0:T(8,128)(2,1)S(1)}, u32[]{:S(2)}, u32[]{:S(2)}) collective-permute-start(bf16[64,8192]{1,0:T(8,128)(2,1)} %collective-permute-done.5), channel_id=1, source_target_pairs={{4,8},{6,10},{8,4},{10,6},{5,9},{7,11},{9,5},{11,7},{20,24},{22,26... | collective-permute-start | bytes 3145736 | tf_op jit(solution)/shard_map/ppermute | solution.py:102
  176.2 4.4 %copy-start.3 = (bf16[64,8192]{1,0:T(8,128)(2,1)}, bf16[64,8192]{1,0:T(8,128)(2,1)S(1)}, u32[]{:S(2)}) copy-start(bf16[64,8192]{1,0:T(8,128)(2,1)S(1)} %collective-permute-done.12) | copy-start | bytes 3145732
  177.5 21.7 %collective-permute-start.13 = (bf16[64,8192]{1,0:T(8,128)(2,1)}, bf16[64,8192]{1,0:T(8,128)(2,1)}, u32[]{:S(2)}, u32[]{:S(2)}) collective-permute-start(bf16[64,8192]{1,0:T(8,128)(2,1)} %broadcast_select_fusion.2), channel_id=1, source_target_pairs={{0,2},{4,6},{8,10},{12,14},{2,0},{6,4},{10,8},{14,12},{1,3},{5,7},... | collective-permute-start | bytes 3145736 | tf_op jit(solution)/shard_map/ppermute | solution.py:102
  180.9 25.5 %collective-permute-start.14 = (bf16[64,8192]{1,0:T(8,128)(2,1)S(1)}, bf16[64,8192]{1,0:T(8,128)(2,1)S(1)}, u32[]{:S(2)}, u32[]{:S(2)}) collective-permute-start(bf16[64,8192]{1,0:T(8,128)(2,1)S(1)} %collective-permute-done.9), channel_id=1, source_target_pairs={{4,0},{6,2},{8,12},{10,14},{5,1},{7,3},{9,13},{11,15},{20,16},{22,... | collective-permute-start | bytes 3145736 | tf_op jit(solution)/shard_map/ppermute | solution.py:102
  207.5 4.3 %copy-start.4 = (bf16[64,8192]{1,0:T(8,128)(2,1)S(1)}, bf16[64,8192]{1,0:T(8,128)(2,1)}, u32[]{:S(2)}) copy-start(bf16[64,8192]{1,0:T(8,128)(2,1)} %copy-done.3) | copy-start | bytes 3145732
  207.5 20.5 %collective-permute-start.15 = (bf16[64,8192]{1,0:T(8,128)(2,1)}, bf16[64,8192]{1,0:T(8,128)(2,1)}, u32[]{:S(2)}, u32[]{:S(2)}) collective-permute-start(bf16[64,8192]{1,0:T(8,128)(2,1)} %broadcast_select_fusion.1), channel_id=1, source_target_pairs={{0,2},{4,6},{8,10},{12,14},{2,0},{6,4},{10,8},{14,12},{1,3},{5,7},... | collective-permute-start | bytes 3145736 | tf_op jit(solution)/shard_map/ppermute | solution.py:102
  211.8 21.8 %collective-permute-start.16 = (bf16[64,8192]{1,0:T(8,128)(2,1)S(1)}, bf16[64,8192]{1,0:T(8,128)(2,1)S(1)}, u32[]{:S(2)}, u32[]{:S(2)}) collective-permute-start(bf16[64,8192]{1,0:T(8,128)(2,1)S(1)} %copy-done.4), channel_id=1, source_target_pairs={{4,0},{6,2},{8,12},{10,14},{5,1},{7,3},{9,13},{11,15},{20,16},{22,... | collective-permute-start | bytes 3145736 | tf_op jit(solution)/shard_map/ppermute | solution.py:102
  234.7 19.3 %collective-permute-start.17 = (bf16[64,8192]{1,0:T(8,128)(2,1)}, bf16[64,8192]{1,0:T(8,128)(2,1)S(1)}, u32[]{:S(2)}, u32[]{:S(2)}) collective-permute-start(bf16[64,8192]{1,0:T(8,128)(2,1)} %broadcast_select_fusion), channel_id=1, source_target_pairs={{0,2},{4,6},{8,10},{12,14},{2,0},{6,4},{10,8},{14,12},{1,3},{5,7},... | collective-permute-start | bytes 3145736 | tf_op jit(solution)/shard_map/ppermute | solution.py:102
  238.1 19.1 %collective-permute-start.18 = (bf16[64,8192]{1,0:T(8,128)(2,1)}, bf16[64,8192]{1,0:T(8,128)(2,1)S(1)}, u32[]{:S(2)}, u32[]{:S(2)}) collective-permute-start(bf16[64,8192]{1,0:T(8,128)(2,1)} %collective-permute-done.4), channel_id=1, source_target_pairs={{0,4},{2,6},{8,12},{10,14},{4,0},{6,2},{12,8},{14,10},{1,5},{3,7},... | collective-permute-start | bytes 3145736 | tf_op jit(solution)/shard_map/ppermute | solution.py:102
  247.0 11.6 %copy-start.2 = (bf16[64,8192]{1,0:T(8,128)(2,1)S(1)}, bf16[64,8192]{1,0:T(8,128)(2,1)}, u32[]{:S(2)}) copy-start(bf16[64,8192]{1,0:T(8,128)(2,1)} %get-tuple-element.103) | copy-start | bytes 3145732
  253.9 1.0 copy-start.5
  260.8 9.6 %collective-permute-start.19 = (bf16[8,2,64,64]{2,3,1,0:T(8,128)(2,1)S(1)}, bf16[8,2,64,64]{2,3,1,0:T(8,128)(2,1)S(1)}, u32[]{:S(2)}, u32[]{:S(2)}) collective-permute-start(bf16[8,2,64,64]{2,3,1,0:T(8,128)(2,1)S(1)} %constant_dynamic-update-slice_fusion.6), channel_id=1, source_target_pairs={{0,2},{4,6},{8,10},{12,14},{2,0},{6,4},{10,8},{14,12},{1,3},{5,7},... | collective-permute-start | bytes 393224 | tf_op jit(solution)/shard_map/ppermute | solution.py:102
  270.5 8.7 %collective-permute-start.20 = (bf16[8,2,64,64]{2,3,1,0:T(8,128)(2,1)S(1)}, bf16[8,2,64,64]{2,3,1,0:T(8,128)(2,1)S(1)}, u32[]{:S(2)}, u32[]{:S(2)}) collective-permute-start(bf16[8,2,64,64]{2,3,1,0:T(8,128)(2,1)S(1)} %add.342), channel_id=1, source_target_pairs={{0,4},{2,6},{8,12},{10,14},{4,0},{6,2},{12,8},{14,10},{1,5},{3,7},... | collective-permute-start | bytes 393224 | tf_op jit(solution)/shard_map/ppermute | solution.py:102
  279.2 10.1 %collective-permute-start.21 = (bf16[8,2,64,64]{2,3,1,0:T(8,128)(2,1)S(1)}, bf16[8,2,64,64]{2,3,1,0:T(8,128)(2,1)S(1)}, u32[]{:S(2)}, u32[]{:S(2)}) collective-permute-start(bf16[8,2,64,64]{2,3,1,0:T(8,128)(2,1)S(1)} %add.343), channel_id=1, source_target_pairs={{0,8},{2,10},{4,12},{6,14},{8,0},{10,2},{12,4},{14,6},{1,9},{3,11}... | collective-permute-start | bytes 393224 | tf_op jit(solution)/shard_map/ppermute | solution.py:102

commit v3 on v1

--- a/solution.py
+++ b/solution.py
@@ -1,6 +1,10 @@
+import functools
+
 import jax
 import jax.numpy as jnp
 from jax import lax
+from jax.experimental import pallas as pl
+from jax.experimental.pallas import tpu as pltpu
 from jax.sharding import PartitionSpec as P
 
 BLOCK = 128
@@ -92,90 +96,362 @@
 
 ACROSS = both_ways([(0, 1), (2, 3), (4, 5), (6, 7)])
 NEAR = both_ways([(0, 2), (1, 3), (4, 6), (5, 7)])
-FAR = both_ways([(0, 4), (1, 5), (2, 6), (3, 7)])
-CHUNKS = 4
+MIDDLE = both_ways([(2, 4), (3, 5)])
+OUTWARD = [(2, 0), (3, 1), (4, 6), (5, 7)]
+ALONG = [[(i, (i + 2 * d) % 8) for i in range(8)] for d in (1, 2, 3)]
+PIECE = BLOCK // 4
+DEPTH = 2048
+VMEM_LIMIT = 40 * 1024 * 1024
+
+
+def send(value, pairs):
+    return lax.ppermute(value, "tensor", pairs)
 
 
 def swap(value, axis):
     return lax.ppermute(value, axis, [(0, 1), (1, 0)])
+
+
+def params():
+    return pltpu.CompilerParams(vmem_limit_bytes=VMEM_LIMIT)
+
+
+def rows_kernel(n, with_base, with_small, aliased, table, *refs):
+    refs = list(refs)
+    pieces = [refs.pop(0) for _ in range(n)]
+    weight = refs.pop(0) if with_base else None
+    downs = [refs.pop(0) for _ in range(2)] if with_small else None
+    if aliased:
+        for _ in range(with_base + with_small):
+            refs.pop(0)
+    base_out = refs.pop(0) if with_base else None
+    small_out = refs.pop(0) if with_small else None
+    acc = refs.pop(0) if with_base else None
+    small, rounded = (refs.pop(0), refs.pop(0)) if with_small else (None, None)
+    sems = refs.pop(0)
+    k = pl.program_id(0)
+    x = jnp.concatenate([p[...] for p in pieces], axis=0)
+
+    def add(total, value):
+        @pl.when(k == 0)
+        def _():
+            total[...] = value
+
+        @pl.when(k > 0)
+        def _():
+            total[...] += value
+
+    if with_base:
+        add(acc, jnp.dot(x, weight[...], preferred_element_type=jnp.float32))
+    if with_small:
+        down = jnp.concatenate([downs[0][0], downs[1][...]], axis=0)
+        add(
+            small,
+            lax.dot_general(
+                x, down, (((1,), (1,)), ((), ())), preferred_element_type=jnp.float32
+            ),
+        )
+
+    @pl.when(k == pl.num_programs(0) - 1)
+    def _():
+        copies = []
+        for i in range(n):
+            cut = pl.ds(i * PIECE, PIECE)
+            if with_base:
+                to = pl.ds(pl.multiple_of(table[1 + i] * PIECE, PIECE), PIECE)
+                copies.append(
+                    pltpu.make_async_copy(acc.at[cut], base_out.at[to], sems.at[len(copies)])
+                )
+            if with_small:
+                lane = lax.broadcasted_iota(jnp.int32, (PIECE, 2 * 64), 1)
+                use = jnp.where(lane < 64, table[1 + 2 * n + i], table[1 + 3 * n + i])
+                rounded[cut] = jnp.where(use > 0, small[cut], 0.0).astype(jnp.bfloat16)
+                to = pl.ds(pl.multiple_of(table[1 + n + i] * PIECE, PIECE), PIECE)
+                copies.append(
+                    pltpu.make_async_copy(rounded.at[cut], small_out.at[to], sems.at[len(copies)])
+                )
+        for copy in copies:
+            copy.start()
+        for copy in copies:
+            copy.wait()
+
+
+def rows_call(pieces, table, weight, down_maps, down_swapped, base, small, wants):
+    n = len(pieces)
+    with_base, with_small = wants
+    width, columns = weight.shape
+    rank = down_swapped.shape[0]
+    aliased = base is not None
+    operands, specs = list(pieces), []
+    specs += [pl.BlockSpec((PIECE, DEPTH), lambda k, t: (0, k))] * n
+    if with_base:
+        operands.append(weight)
+        specs.append(pl.BlockSpec((DEPTH, columns), lambda k, t: (k, 0)))
+    if with_small:
+        operands += [down_maps, down_swapped]
+        specs.append(pl.BlockSpec((1, rank, DEPTH), lambda k, t: (t[0], 0, k)))
+        specs.append(pl.BlockSpec((rank, DEPTH), lambda k, t: (0, k)))
+    outs, scratch, aliases = [], [], {}
+    rows = 8 * BLOCK
+    if with_base:
+        outs.append(jax.ShapeDtypeStruct((rows, columns), jnp.float32))
+        scratch.append(pltpu.VMEM((n * PIECE, columns), jnp.float32))
+    if with_small:
+        outs.append(jax.ShapeDtypeStruct((rows, 2 * rank), jnp.bfloat16))
+        scratch.append(pltpu.VMEM((n * PIECE, 2 * rank), jnp.float32))
+        scratch.append(pltpu.VMEM((n * PIECE, 2 * rank), jnp.bfloat16))
+    scratch.append(pltpu.SemaphoreType.DMA((2 * n,)))
+    if aliased:
+        for at, value in enumerate([base] * with_base + [small] * with_small):
+            aliases[1 + len(operands)] = at
+            operands.append(value)
+            specs.append(pl.BlockSpec(memory_space=pl.ANY))
+    wide = columns * with_base + 2 * rank * with_small
+    return pl.pallas_call(
+        functools.partial(rows_kernel, n, with_base, with_small, aliased),
+        grid_spec=pltpu.PrefetchScalarGridSpec(
+            num_scalar_prefetch=1,
+            grid=(width // DEPTH,),
+            in_specs=specs,
+            out_specs=[pl.BlockSpec(memory_space=pl.ANY)] * len(outs),
+            scratch_shapes=scratch,
+        ),
+        out_shape=outs,
+        input_output_aliases=aliases,
+        compiler_params=params(),
+        cost_estimate=pl.CostEstimate(
+            flops=2 * n * PIECE * width * wide,
+            bytes_accessed=2 * width * (wide + n * PIECE),
+            transcendentals=0,
+        ),
+        name="rows",
+    )(table, *operands)
+
+
+def pack_kernel(table, up, out):
+    part = out.shape[3]
+    for t in range(8):
+        at = pl.multiple_of((2 * t + table[2]) * part, part)
+        out[t, 0] = up[0, :, pl.ds(at, part)]
+
+
+def pack_call(table, up_maps):
+    _, rank, width = up_maps.shape
+    part = width // 16
+    return pl.pallas_call(
+        pack_kernel,
+        grid_spec=pltpu.PrefetchScalarGridSpec(
+            num_scalar_prefetch=1,
+            grid=(2,),
+            in_specs=[pl.BlockSpec((1, rank, width), lambda s, t: (t[s], 0, 0))],
+            out_specs=pl.BlockSpec((8, 1, rank, part), lambda s, t: (0, s, 0, 0)),
+        ),
+        out_shape=jax.ShapeDtypeStruct((8, 2, rank, part), jnp.bfloat16),
+        compiler_params=params(),
+        name="pack",
+    )(table, up_maps)
+
+
+def take_kernel(table, got, out):
+    out[...] = got[...]
+
+
+def take_call(table, got):
+    _, rank, part = got.shape
+    return pl.pallas_call(
+        take_kernel,
+        grid_spec=pltpu.PrefetchScalarGridSpec(
+            num_scalar_prefetch=1,
+            grid=(8,),
+            in_specs=[pl.BlockSpec((1, rank, part), lambda b, t: (t[b], 0, 0))],
+            out_specs=pl.BlockSpec((1, rank, part), lambda b, t: (b, 0, 0)),
+        ),
+        out_shape=jax.ShapeDtypeStruct((8, rank, part), jnp.bfloat16),
+        compiler_params=params(),
+        name="take",
+    )(table, got)
+
+
+def finish_kernel(table, base, first, second, up_mine, up_other, out):
+    both = jnp.concatenate([first[...], second[...]], axis=0).astype(jnp.float32)
+    shrunk = (both[:, :64] + both[:, 64:]).astype(jnp.bfloat16)
+    part = up_mine.shape[2]
+    for up, side in ((up_mine, table[0]), (up_other, 1 - table[0])):
+        cut = pl.ds(pl.multiple_of(side * part, part), part)
+        grown = jnp.dot(shrunk, up[0], preferred_element_type=jnp.float32)
+        out[:, cut] = (base[:, cut] + 0.5 * grown).astype(out.dtype)
+
+
+def finish_call(table, base, first, second, up_mine, up_other):
+    rows, columns = base.shape
+    _, rank, part = up_mine.shape
+    half = pl.BlockSpec((BLOCK // 2, 2 * rank), lambda b, t: (b, 0))
+    up = pl.BlockSpec((1, rank, part), lambda b, t: (b, 0, 0))
+    whole = pl.BlockSpec((BLOCK, columns), lambda b, t: (b, 0))
+    return pl.pallas_call(
+        finish_kernel,
+        grid_spec=pltpu.PrefetchScalarGridSpec(
+            num_scalar_prefetch=1,
+            grid=(8,),
+            in_specs=[whole, half, half, up, up],
+            out_specs=whole,
+        ),
+        out_shape=jax.ShapeDtypeStruct((rows, columns), jnp.bfloat16),
+        compiler_params=params(),
+        name="finish",
+    )(table, base, first, second, up_mine, up_other)
+
+
+STEPS = [
+    (("own", 0), ("own", 0, NEAR), ("own", 0)),
+    (("own", 1), ("own", 1, NEAR), ("near", 0)),
+    (("near", 0), ("far", 0, OUTWARD), ("own", 1)),
+    (("far", 0), ("last", 0, OUTWARD), ("near", 1)),
+    (("last", 0), ("far", 1, OUTWARD), None),
+    (("far", 1), ("last", 1, OUTWARD), None),
+    (("last", 1), ("own_y", 1, NEAR), None),
+]
 
 
 def chain_body(
     tokens, query_weight, adapter_down_maps, adapter_up_maps, adapter_home_slot, adapter_per_block
 ):
     me = lax.axis_index("tensor")
+    z, y = me // 2, me % 2
     store = lax.axis_index("store")
     group = lax.axis_index("groups")
     myself = me * 2 + store
+    inner = (z == 1) | (z == 2)
     held, rank, width = adapter_down_maps.shape
-    columns = query_weight.shape[1]
-    part = columns // 2
     rows = tokens[0]
-    step = BLOCK // CHUNKS
 
     store_slots = find_slots(adapter_home_slot, adapter_per_block)
     owner = store_slots // held
     inside = store_slots % held
     picked = jnp.max(jnp.where(owner == myself, inside, 0), axis=1)
     owner_row = lax.dynamic_index_in_dim(owner, store, 0, keepdims=False)
-
-    gathered = [
-        lax.all_gather(rows[c * step : (c + 1) * step], "tensor", axis=0) for c in range(CHUNKS)
-    ]
-
-    def pick(maps, index):
-        local = lax.dynamic_index_in_dim(picked, index, 0, keepdims=False)
-        return lax.dynamic_index_in_dim(maps, local, 0, keepdims=False)
-
-    down_own = pick(adapter_down_maps, store)
-    down_swapped = swap(pick(adapter_down_maps, 1 - store), "store")
-    candidates = jnp.concatenate([down_own, down_swapped])
-    use_own = (owner_row == myself)[:, None, None]
-    use_swapped = (owner_row == me * 2 + 1 - store)[:, None, None]
-
-    def shrink(chunk):
-        value = lax.dot_general(
-            candidates,
-            chunk.reshape(8 * step, width),
-            (((1,), (1,)), ((), ())),
-            preferred_element_type=jnp.float32,
+    pick_own = lax.dynamic_index_in_dim(picked, store, 0, keepdims=False)
+    pick_lent = lax.dynamic_index_in_dim(picked, 1 - store, 0, keepdims=False)
+    is_own = (owner_row == myself).astype(jnp.int32)
+    is_swapped = (owner_row == me * 2 + 1 - store).astype(jnp.int32)
+
+    z_of = {
+        "own": z,
+        "near": z + 1 - 2 * (z % 2),
+        "far": jnp.where(z < 2, 2, 1),
+        "last": jnp.where(z < 2, 3, 0),
+    }
+
+    def make_table(keys):
+        blocks, base_at, small_at = [], [], []
+        for name, half, sub in keys:
+            column = 1 - y if name.endswith("_y") else y
+            block = z_of[name.removesuffix("_y")] * 2 + column
+            blocks.append(block)
+            base_at.append(block * 4 + half * 2 + sub)
+            small_at.append(half * 16 + block * 2 + sub)
+        blocks = jnp.stack(blocks)
+        return jnp.concatenate(
+            [pick_own[None], jnp.stack(base_at), jnp.stack(small_at), is_own[blocks], is_swapped[blocks]]
+        ).astype(jnp.int32)
+
+    def work(state, keys, have, wants=(True, True)):
+        base, small = state
+        outs = rows_call(
+            [have[key] for key in keys],
+            make_table(keys),
+            query_weight,
+            adapter_down_maps,
+            down_swapped,
+            base,
+            small,
+            wants,
         )
-        value = value.reshape(2, rank, 8, step).transpose(0, 2, 1, 3)
-        value = jnp.where(use_own, value[0], jnp.where(use_swapped, value[1], 0))
-        value = value.astype(jnp.bfloat16)
-        for pairs in (ACROSS, NEAR, FAR):
-            value = value + lax.ppermute(value, "tensor", pairs)
-        return value
-
-    def columns_of(up):
-        halves = up.reshape(rank, 8, 2, part)
-        half = lax.dynamic_index_in_dim(halves, group, 2, keepdims=False)
-        return half.transpose(1, 0, 2)
-
-    up_sent = jnp.stack(
-        [columns_of(pick(adapter_up_maps, 0)), columns_of(pick(adapter_up_maps, 1))], axis=1
-    )
-    up_got = lax.all_to_all(
-        up_sent.reshape(16, rank, part), ("tensor", "store"), split_axis=0, concat_axis=0, tiled=True
-    )
-    up_half = jnp.stack(
-        [lax.dynamic_index_in_dim(up_got, owner_row[b], 0, keepdims=False) for b in range(8)]
-    )
-    up_other = swap(up_half, "groups")
-    up = jnp.concatenate(
-        [jnp.where(group == 0, up_half, up_other), jnp.where(group == 0, up_other, up_half)], axis=2
-    )
-
-    outputs = []
-    for chunk in gathered:
-        base = jnp.dot(
-            chunk.reshape(8 * step, width), query_weight, preferred_element_type=jnp.float32
+        if wants == (True, True):
+            return tuple(outs)
+        return (outs[0], small) if wants[0] else (base, outs[0])
+
+    have = {
+        ("own", half, sub): rows[(2 * half + sub) * PIECE : (2 * half + sub + 1) * PIECE]
+        for half in range(2)
+        for sub in range(2)
+    }
+    inner_has = {}
+
+    def issue(n):
+        across, along, middle = STEPS[n // 2]
+        sub = n % 2
+        name, half, pairs = along
+        sent = (inner_has if pairs is OUTWARD else have)[name, half, sub]
+        got = {"y": send(have[across + (sub,)], ACROSS), "z": send(sent, pairs)}
+        if middle is not None:
+            got["m"] = send(have[middle + (sub,)], MIDDLE)
+        return got
+
+    def arrive(n, got):
+        across, along, middle = STEPS[n // 2]
+        sub = n % 2
+        name, half, pairs = along
+        if middle is not None:
+            inner_has[{"own": "far", "near": "last"}[middle[0]], middle[1], sub] = got["m"]
+        if pairs is OUTWARD:
+            key = (name, half, sub)
+            have[key] = jnp.where(inner, inner_has[key], got["z"])
+        else:
+            key = ({"own": "near", "own_y": "near_y"}[name], half, sub)
+            have[key] = got["z"]
+        seen = (across[0] + "_y", across[1], sub)
+        have[seen] = got["y"]
+        return [key, seen]
+
+    flight = {0: issue(0), 1: issue(1)}
+    down_swapped = swap(
+        lax.dynamic_index_in_dim(adapter_down_maps, pick_lent, 0, keepdims=False), "store"
+    )
+    up_sent = pack_call(jnp.concatenate([picked, group[None]]).astype(jnp.int32), adapter_up_maps)
+
+    state = (None, None)
+    waiting = [key for key in have]
+    extra = {"up": up_sent}
+    up_got = None
+    for n in range(14):
+        got, state, have, inner_has, extra = lax.optimization_barrier(
+            (flight.pop(n), state, have, inner_has, extra)
         )
-        grown = jnp.einsum("brn,brf->bnf", shrink(chunk), up, preferred_element_type=jnp.float32)
-        value = base.reshape(8, step, columns) + 0.5 * grown
-        outputs.append(value.astype(jnp.bfloat16))
-    query = jnp.concatenate(outputs, axis=1)
-    return query.reshape(1, 8 * BLOCK, columns)
+        waiting += arrive(n, got)
+        if n + 2 < 14:
+            flight[n + 2] = issue(n + 2)
+        if n == 9:
+            up_got = lax.all_to_all(
+                extra.pop("up").reshape(16, rank, -1),
+                ("tensor", "store"),
+                split_axis=0,
+                concat_axis=0,
+                tiled=True,
+            )
+        if n == 10:
+            first = state[1][: 4 * BLOCK]
+            flight[12]["first"] = send(first, ACROSS)
+            extra["first"] = first
+        if n == 12:
+            first = extra.pop("first") + got["first"]
+            firsts = [first] + [send(first, pairs) for pairs in ALONG]
+        if n in (1, 5, 9, 11):
+            state = work(state, waiting, have)
+            waiting = []
+
+    state = work(state, waiting, have, (False, True))
+    second = state[1][4 * BLOCK :]
+    second = second + send(second, ACROSS)
+    seconds = [second] + [send(second, pairs) for pairs in ALONG]
+    state = work(state, waiting, have, (True, False))
+
+    up_mine = take_call(owner_row.astype(jnp.int32), up_got)
+    up_other = swap(up_mine, "groups")
+    query = finish_call(
+        group[None].astype(jnp.int32), state[0], sum(firsts), sum(seconds), up_mine, up_other
+    )
+    return query[None]
 
 
 def body(tokens, *rest):

time: 382 us -> 275 us (0.72)
  waiting for transfers between devices: 259 us -> 65.1 us
  Pallas kernels: 0 us -> 72.8 us
  matrix products: 44.3 us -> 0 us
  local copies, waits for them, and re-layouts: 13.9 us -> 56.9 us
  starting transfers between devices: 24.1 us -> 65.6 us
  between operations: 35.7 us -> 2.49 us
  other arithmetic: 3.73 us -> 10.8 us
    all_gather x4 -> x0, waiting for transfers between devices: 231 us -> none  [chain_body(): lax.all_gather(rows[c * step:(c + 1) * step], 'tensor', axis=0)]
    pallas_call x0 -> x9, Pallas kernels: none -> 72.8 us  [the longest x6 66.3 us: rows_call(): pl.pallas_call(functools.partial(rows_kernel, n, with_base, with_small, a...]
    ppermute x12 -> x44, waiting for transfers between devices: 3.8 us -> 65.1 us  [send(): return lax.ppermute(value, 'tensor', pairs)]
    ppermute x12 -> x44, starting transfers between devices: 14.6 us -> 60.3 us  [send(): return lax.ppermute(value, 'tensor', pairs)]
    dot_general x12 -> x0, matrix products: 44.3 us -> none  [the longest x4 29.3 us: chain_body(): jnp.dot(chunk.reshape(8 * step, width), query_weight, preferred_element_t...]
    unnamed x21 -> x70, local copies, waits for them, and re-layouts: 0.56 us -> 38 us
    all_to_all x1, waiting for transfers between devices: 11.6 us -> 0.01 us  [chain_body(): lax.all_to_all(extra.pop('up').reshape(16, rank, -1), ('tensor', 'store')...]
    ppermute x2, waiting for transfers between devices: 11.5 us -> 0.01 us  [swap(): return lax.ppermute(value, axis, [(0, 1), (1, 0)])]
  transfers between devices with their start and end apart: 19 -> 47, of which waited for: 9 -> 11; matrix products, arithmetic and copies ran while one was open for 14% -> 10% of each run, Pallas kernels for 0% -> 25%
where the time goes in v3:
time: 275 us; the launch traced here: 274 us
  Pallas kernels  72.8 us (26%)
  starting transfers between devices  65.6 us (24%)
  waiting for transfers between devices  65.1 us (24%)
  local copies, waits for them, and re-layouts  56.9 us (21%)
  other arithmetic  10.8 us (4%)
    pallas_call x6, Pallas kernels, rows_call(): pl.pallas_call(functools.partial(rows_kernel, n, with_base, with_small, a...  66.3 us
    ppermute x44, waiting for transfers between devices, send(): return lax.ppermute(value, 'tensor', pairs)  65.1 us
    ppermute x44, starting transfers between devices, send(): return lax.ppermute(value, 'tensor', pairs)  60.3 us
    unnamed x70, local copies, waits for them, and re-layouts  38 us
    select_n x8, other arithmetic, arrive(): have[key] = jnp.where(inner, inner_has[key], got['z'])  6.08 us
  transfers between devices with their start and end apart: 47, of which 11 were waited for; matrix products, arithmetic and copies ran while one was open for 10% of the time, Pallas kernels for 25%

profile of v3, /device:TPU:0, one launch (start us, length us, event | category | flops | bytes accessed | tf_op | source)
XLA Modules:
  0.0 273.6 jit_solution(14027560898186580385)
XLA Ops:
  0.0 1.7 slice_bitcast_fusion
  1.7 3.1 %collective-permute-start.5 = (bf16[32,8192]{1,0:T(8,128)(2,1)S(1)}, bf16[32,8192]{1,0:T(8,128)(2,1)}, u32[]{:S(2)}, u32[]{:S(2)}) collective-permute-start(bf16[32,8192]{1,0:T(8,128)(2,1)S(1)} %get-tuple-element.183.refs_0_), channel_id=1, source_target_pairs={{0,4},{2,6},{8,12},{10,14},{4,0},{6,2},{12,8},{14,10},{1,5},{3,7},... | collective-permute-start | bytes 1572872 | tf_op jit(solution)/shard_map/ppermute | solution.py:108
  10.7 2.3 dynamic-slice_bitcast_fusion
  13.0 3.6 %collective-permute-start.2 = (bf16[32,8192]{1,0:T(8,128)(2,1)S(1)}, bf16[32,8192]{1,0:T(8,128)(2,1)}, u32[]{:S(2)}, u32[]{:S(2)}) collective-permute-start(bf16[32,8192]{1,0:T(8,128)(2,1)S(1)} %get-tuple-element.184.refs_1_), channel_id=1, source_target_pairs={{0,4},{2,6},{8,12},{10,14},{4,0},{6,2},{12,8},{14,10},{1,5},{3,7},... | collective-permute-start | bytes 1572872 | tf_op jit(solution)/shard_map/ppermute | solution.py:108
  16.8 2.2 copy-done.13
  19.0 1.6 pack.1
  23.3 5.9 %collective-permute-done.2.refs_6_ = bf16[32,8192]{1,0:T(8,128)(2,1)} collective-permute-done((bf16[32,8192]{1,0:T(8,128)(2,1)S(1)}, bf16[32,8192]{1,0:T(8,128)(2,1)}, u32[]{:S(2)}, u32[]{:S(2)}) %collective-permute-start.2) | collective-permute-done | bytes 524320 | tf_op jit(solution)/shard_map/ppermute | solution.py:108
  29.3 1.7 collective-permute-start.11
  31.0 3.7 %collective-permute-done.1.refs_7_ = bf16[32,8192]{1,0:T(8,128)(2,1)S(1)} collective-permute-done((bf16[32,8192]{1,0:T(8,128)(2,1)S(1)}, bf16[32,8192]{1,0:T(8,128)(2,1)S(1)}, u32[]{:S(2)}, u32[]{:S(2)}) %collective-permute-start.1) | collective-permute-done | bytes 524320 | tf_op jit(solution)/shard_map/ppermute | solution.py:108
  40.3 4.0 %collective-permute-start.8 = (bf16[32,8192]{1,0:T(8,128)(2,1)S(1)}, bf16[32,8192]{1,0:T(8,128)(2,1)}, u32[]{:S(2)}, u32[]{:S(2)}) collective-permute-start(bf16[32,8192]{1,0:T(8,128)(2,1)S(1)} %get-tuple-element.206.refs_3_), channel_id=1, source_target_pairs={{0,4},{2,6},{8,12},{10,14},{4,0},{6,2},{12,8},{14,10},{1,5},{3,7},... | collective-permute-start | bytes 1572872 | tf_op jit(solution)/shard_map/ppermute | solution.py:108
  44.4 2.2 copy-done
  47.6 14.3 %rows.6 = (f32[1024,1024]{1,0:T(8,128)S(1)}, bf16[1024,128]{1,0:T(8,128)(2,1)S(1)}) custom-call(s32[33]{0:T(128)S(1)} %concatenate.116.table, bf16[32,8192]{1,0:T(8,128)(2,1)S(1)} %get-tuple-element.183.refs_0_, bf16[32,8192]{1,0:T(8,128)(2,1)S(1)} %get-tuple-element.184.refs_1_, bf16[32,8192]{1,0:T(8,128)(2,1)S(1)} %get-tuple-element.199.refs_2_, ...), custom_call_target="tpu_custom_call" | custom-call | flops 4831838208 | bytes 23068672 | tf_op jit(solution)/shard_map/rows/pallas_call | solution.py:210
  61.9 2.0 copy-done.5
  63.9 2.0 collective-permute-start.17
  73.8 5.2 %collective-permute-done.17.refs_5_ = bf16[32,8192]{1,0:T(8,128)(2,1)S(1)} collective-permute-done((bf16[32,8192]{1,0:T(8,128)(2,1)}, bf16[32,8192]{1,0:T(8,128)(2,1)S(1)}, u32[]{:S(2)}, u32[]{:S(2)}) %collective-permute-start.17) | collective-permute-done | bytes 524320 | tf_op jit(solution)/shard_map/ppermute | solution.py:108
  80.4 4.4 %collective-permute-done.18 = bf16[32,8192]{1,0:T(8,128)(2,1)} collective-permute-done((bf16[32,8192]{1,0:T(8,128)(2,1)}, bf16[32,8192]{1,0:T(8,128)(2,1)}, u32[]{:S(2)}, u32[]{:S(2)}) %collective-permute-start.18) | collective-permute-done | bytes 524320 | tf_op jit(solution)/shard_map/ppermute | solution.py:108
  85.9 2.7 collective-permute-start.23
  91.4 4.5 %collective-permute-done.15 = bf16[32,8192]{1,0:T(8,128)(2,1)S(1)} collective-permute-done((bf16[32,8192]{1,0:T(8,128)(2,1)}, bf16[32,8192]{1,0:T(8,128)(2,1)S(1)}, u32[]{:S(2)}, u32[]{:S(2)}) %collective-permute-start.15) | collective-permute-done | bytes 524320 | tf_op jit(solution)/shard_map/ppermute | solution.py:108
  95.9 1.7 collective-permute-start.20
  98.3 2.2 copy-done.1
  100.5 2.2 copy-done.6
  102.6 14.3 %rows.7 = (f32[1024,1024]{1,0:T(8,128)S(1)}, bf16[1024,128]{1,0:T(8,128)(2,1)S(1)}) custom-call(s32[33]{0:T(128)S(1)} %concatenate.117.table, bf16[32,8192]{1,0:T(8,128)(2,1)} %collective-permute-done.11.refs_0_, bf16[32,8192]{1,0:T(8,128)(2,1)} %collective-permute-done.10.refs_1_, ...), custom_call_target="tpu_custom_call", output_to_operand_aliasing={{0}: (12, {}), {1}: (13, {})} | custom-call | flops 4831838208 | bytes 23068672 | tf_op jit(solution)/shard_map/rows/pallas_call | solution.py:210
  117.0 2.0 copy-done.7
  122.2 16.5 %collective-permute-done.21 = bf16[32,8192]{1,0:T(8,128)(2,1)S(1)} collective-permute-done((bf16[32,8192]{1,0:T(8,128)(2,1)}, bf16[32,8192]{1,0:T(8,128)(2,1)S(1)}, u32[]{:S(2)}, u32[]{:S(2)}) %collective-permute-start.21) | collective-permute-done | bytes 524320 | tf_op jit(solution)/shard_map/ppermute | solution.py:108
  140.7 9.3 %collective-permute-done.28 = bf16[32,8192]{1,0:T(8,128)(2,1)S(1)} collective-permute-done((bf16[32,8192]{1,0:T(8,128)(2,1)}, bf16[32,8192]{1,0:T(8,128)(2,1)S(1)}, u32[]{:S(2)}, u32[]{:S(2)}) %collective-permute-start.28) | collective-permute-done | bytes 524320 | tf_op jit(solution)/shard_map/ppermute | solution.py:108
  153.8 7.3 %collective-permute-done.26 = bf16[32,8192]{1,0:T(8,128)(2,1)S(1)} collective-permute-done((bf16[32,8192]{1,0:T(8,128)(2,1)S(1)}, bf16[32,8192]{1,0:T(8,128)(2,1)S(1)}, u32[]{:S(2)}, u32[]{:S(2)}) %collective-permute-start.26) | collective-permute-done | bytes 524320 | tf_op jit(solution)/shard_map/ppermute | solution.py:108
  162.0 3.7 %all-to-all-start = ((bf16[16,64,512]{2,1,0:T(8,128)(2,1)}), bf16[16,64,512]{2,1,0:T(8,128)(2,1)S(1)}, u32[]{:S(2)}, u32[]{:S(2)}) async-start(bf16[16,64,512]{2,1,0:T(8,128)(2,1)} %bitcast.85), calls=%async_computation | async-start | bytes 2097152 | tf_op jit(solution)/shard_map/all_to_all | solution.py:425
  166.8 1.9 collective-permute-start.29
  170.2 2.2 copy-done.2
  172.4 2.2 copy-done.8
  178.7 14.2 %rows.8 = (f32[1024,1024]{1,0:T(8,128)S(1)}, bf16[1024,128]{1,0:T(8,128)(2,1)S(1)}) custom-call(s32[33]{0:T(128)S(1)} %concatenate.118.table, bf16[32,8192]{1,0:T(8,128)(2,1)S(1)} %broadcast_select_fusion.5.refs_0_, bf16[32,8192]{1,0:T(8,128)(2,1)S(1)} %copy-done.15, ...), custom_call_target="tpu_custom_call", output_to_operand_aliasing={{0}: (12, {}), {1}: (13, {})} | custom-call | flops 4831838208 | bytes 23068672 | tf_op jit(solution)/shard_map/rows/pallas_call | solution.py:210
  192.9 2.0 copy-done.9
  194.9 1.9 broadcast_select_fusion.1.refs_0_
  197.1 2.7 collective-permute-start.37
  201.4 1.8 collective-permute-start.33
  212.2 2.2 copy-done.3
  214.4 2.2 copy-done.10
  217.6 10.7 %rows.9 = (f32[1024,1024]{1,0:T(8,128)S(1)}, bf16[1024,128]{1,0:T(8,128)(2,1)S(1)}) custom-call(s32[17]{0:T(128)S(1)} %concatenate.119.table, bf16[32,8192]{1,0:T(8,128)(2,1)} %broadcast_select_fusion.1.refs_0_, bf16[32,8192]{1,0:T(8,128)(2,1)} %collective-permute-done.31.refs_1_, ...), custom_call_target="tpu_custom_call", output_to_operand_aliasing={{0}: (8, {}), {1}: (9, {})} | custom-call | flops 2415919104 | bytes 20971520 | tf_op jit(solution)/shard_map/rows/pallas_call | solution.py:210
  229.3 3.7 %collective-permute-start.40 = (bf16[512,128]{1,0:T(8,128)(2,1)S(1)}, bf16[512,128]{1,0:T(8,128)(2,1)}, u32[]{:S(2)}, u32[]{:S(2)}) collective-permute-start(bf16[512,128]{1,0:T(8,128)(2,1)S(1)} %add.445), channel_id=1, source_target_pairs={{0,12},{2,14},{4,0},{6,2},{8,4},{10,6},{12,8},{14,10},{1,13},{3,15... | collective-permute-start | bytes 393224 | tf_op jit(solution)/shard_map/ppermute | solution.py:108
  233.7 1.9 collective-permute-start.38
  235.6 3.8 %rows.11 = bf16[1024,128]{1,0:T(8,128)(2,1)S(1)} custom-call(s32[17]{0:T(128)S(1)} %concatenate.114.table, bf16[32,8192]{1,0:T(8,128)(2,1)S(1)} %collective-permute-done.37.refs_0_, bf16[32,8192]{1,0:T(8,128)(2,1)S(1)} %collective-permute-done.36.refs_1_, bf16[32,8192]{1,0:T(8,128)(2,1)} %collective-permute-done.34.refs_2_, ...), custom_call_target="tpu_custom_call", output_to_operand_aliasing={{}: (7, {})} | custom-call | flops 268435456 | bytes 4194304 | tf_op jit(solution)/shard_map/rows/pallas_call | solution.py:210
  241.5 9.1 %rows.10.base = f32[1024,1024]{1,0:T(8,128)S(1)} custom-call(s32[17]{0:T(128)S(1)} %concatenate.114.table, bf16[32,8192]{1,0:T(8,128)(2,1)S(1)} %collective-permute-done.37.refs_0_, bf16[32,8192]{1,0:T(8,128)(2,1)S(1)} %collective-permute-done.36.refs_1_, bf16[32,8192]{1,0:T(8,128)(2,1)} %collective-permute-done.34.refs_2_, ...), custom_call_target="tpu_custom_call", output_to_operand_aliasing={{}: (6, {})} | custom-call | flops 2147483648 | bytes 18874368 | tf_op jit(solution)/shard_map/rows/pallas_call | solution.py:210
  250.7 2.0 copy-done.11
  255.9 1.9 collective-permute-start.44
  259.5 3.4 %collective-permute-done.44 = bf16[512,128]{1,0:T(8,128)(2,1)S(1)} collective-permute-done((bf16[512,128]{1,0:T(8,128)(2,1)S(1)}, bf16[512,128]{1,0:T(8,128)(2,1)S(1)}, u32[]{:S(2)}, u32[]{:S(2)}) %collective-permute-start.44) | collective-permute-done | bytes 131104 | tf_op jit(solution)/shard_map/ppermute | solution.py:108
  262.9 4.3 %collective-permute-done.43 = bf16[512,128]{1,0:T(8,128)(2,1)S(1)} collective-permute-done((bf16[512,128]{1,0:T(8,128)(2,1)S(1)}, bf16[512,128]{1,0:T(8,128)(2,1)S(1)}, u32[]{:S(2)}, u32[]{:S(2)}) %collective-permute-start.43) | collective-permute-done | bytes 131104 | tf_op jit(solution)/shard_map/ppermute | solution.py:108
  267.3 2.2 copy-done.12
  269.5 4.2 %finish.1 = bf16[1024,1024]{1,0:T(8,128)(2,1)} custom-call(s32[1]{0:T(128)} %bitcast.table, f32[1024,1024]{1,0:T(8,128)S(1)} %copy-done.12, bf16[512,128]{1,0:T(8,128)(2,1)S(1)} %add_add_fusion.1.first, bf16[512,128]{1,0:T(8,128)(2,1)S(1)} %add_add_fusion.second, bf16[8,64,512]{2,1,0:T(8,128)(2,1)S(1)} %take.1.up_mine, ...), custom_call_target="tpu_custom_call" | custom-call | tf_op jit(solution)/shard_map/finish/pallas_call | solution.py:291
  (173 shorter events, 64.5 us)
Async XLA Ops:
  1.7 19.0 %collective-permute-start.5 = (bf16[32,8192]{1,0:T(8,128)(2,1)S(1)}, bf16[32,8192]{1,0:T(8,128)(2,1)}, u32[]{:S(2)}, u32[]{:S(2)}) collective-permute-start(bf16[32,8192]{1,0:T(8,128)(2,1)S(1)} %get-tuple-element.183.refs_0_), channel_id=1, source_target_pairs={{0,4},{2,6},{8,12},{10,14},{4,0},{6,2},{12,8},{14,10},{1,5},{3,7},... | collective-permute-start | bytes 1572872 | tf_op jit(solution)/shard_map/ppermute | solution.py:108
  4.8 16.4 %collective-permute-start.4 = (bf16[32,8192]{1,0:T(8,128)(2,1)S(1)}, bf16[32,8192]{1,0:T(8,128)(2,1)}, u32[]{:S(2)}, u32[]{:S(2)}) collective-permute-start(bf16[32,8192]{1,0:T(8,128)(2,1)S(1)} %get-tuple-element.183.refs_0_), channel_id=1, source_target_pairs={{0,2},{4,6},{8,10},{12,14},{2,0},{6,4},{10,8},{14,12},{1,3},{5,7},... | collective-permute-start | bytes 1572872 | tf_op jit(solution)/shard_map/ppermute | solution.py:108
  6.3 15.6 %collective-permute-start.3 = (bf16[32,8192]{1,0:T(8,128)(2,1)S(1)}, bf16[32,8192]{1,0:T(8,128)(2,1)}, u32[]{:S(2)}, u32[]{:S(2)}) collective-permute-start(bf16[32,8192]{1,0:T(8,128)(2,1)S(1)} %get-tuple-element.183.refs_0_), channel_id=1, source_target_pairs={{4,8},{6,10},{8,4},{10,6},{5,9},{7,11},{9,5},{11,7},{20,24},{22,26... | collective-permute-start | bytes 1572872 | tf_op jit(solution)/shard_map/ppermute | solution.py:108
  13.0 27.3 %collective-permute-start.12 = (bf16[64,8192]{1,0:T(8,128)(2,1)}, bf16[64,8192]{1,0:T(8,128)(2,1)S(1)}, u32[]{:S(2)}, u32[]{:S(2)}) collective-permute-start(bf16[64,8192]{1,0:T(8,128)(2,1)} %dynamic-slice_bitcast_fusion), channel_id=1, source_target_pairs={{0,1},{1,0},{2,3},{3,2},{4,5},{5,4},{6,7},{7,6},{8,9},{9,8},{10,11... | collective-permute-start | bytes 3145736 | tf_op jit(solution)/shard_map/ppermute | solution.py:112
  13.0 16.3 %collective-permute-start.2 = (bf16[32,8192]{1,0:T(8,128)(2,1)S(1)}, bf16[32,8192]{1,0:T(8,128)(2,1)}, u32[]{:S(2)}, u32[]{:S(2)}) collective-permute-start(bf16[32,8192]{1,0:T(8,128)(2,1)S(1)} %get-tuple-element.184.refs_1_), channel_id=1, source_target_pairs={{0,4},{2,6},{8,12},{10,14},{4,0},{6,2},{12,8},{14,10},{1,5},{3,7},... | collective-permute-start | bytes 1572872 | tf_op jit(solution)/shard_map/ppermute | solution.py:108
  20.6 14.1 %collective-permute-start.1 = (bf16[32,8192]{1,0:T(8,128)(2,1)S(1)}, bf16[32,8192]{1,0:T(8,128)(2,1)S(1)}, u32[]{:S(2)}, u32[]{:S(2)}) collective-permute-start(bf16[32,8192]{1,0:T(8,128)(2,1)S(1)} %get-tuple-element.184.refs_1_), channel_id=1, source_target_pairs={{0,2},{4,6},{8,10},{12,14},{2,0},{6,4},{10,8},{14,12},{1,3},{5,7},... | collective-permute-start | bytes 1572872 | tf_op jit(solution)/shard_map/ppermute | solution.py:108
  21.2 14.9 %collective-permute-start = (bf16[32,8192]{1,0:T(8,128)(2,1)S(1)}, bf16[32,8192]{1,0:T(8,128)(2,1)S(1)}, u32[]{:S(2)}, u32[]{:S(2)}) collective-permute-start(bf16[32,8192]{1,0:T(8,128)(2,1)S(1)} %get-tuple-element.184.refs_1_), channel_id=1, source_target_pairs={{4,8},{6,10},{8,4},{10,6},{5,9},{7,11},{9,5},{11,7},{20,24},{22,26... | collective-permute-start | bytes 1572872 | tf_op jit(solution)/shard_map/ppermute | solution.py:108
  21.9 22.5 %collective-permute-start.9 = (bf16[32,8192]{1,0:T(8,128)(2,1)}, bf16[32,8192]{1,0:T(8,128)(2,1)}, u32[]{:S(2)}, u32[]{:S(2)}) collective-permute-start(bf16[32,8192]{1,0:T(8,128)(2,1)} %collective-permute-done.5.refs_4_), channel_id=1, source_target_pairs={{4,8},{6,10},{8,4},{10,6},{5,9},{7,11},{9,5},{11,7},{20,24},{22,26... | collective-permute-start | bytes 1572872 | tf_op jit(solution)/shard_map/ppermute | solution.py:108
  29.3 34.7 %collective-permute-start.11 = (bf16[32,8192]{1,0:T(8,128)(2,1)S(1)}, bf16[32,8192]{1,0:T(8,128)(2,1)}, u32[]{:S(2)}, u32[]{:S(2)}) collective-permute-start(bf16[32,8192]{1,0:T(8,128)(2,1)S(1)} %get-tuple-element.199.refs_2_), channel_id=1, source_target_pairs={{0,4},{2,6},{8,12},{10,14},{4,0},{6,2},{12,8},{14,10},{1,5},{3,7},... | collective-permute-start | bytes 1572872 | tf_op jit(solution)/shard_map/ppermute | solution.py:108
  35.5 28.4 %collective-permute-start.10 = (bf16[32,8192]{1,0:T(8,128)(2,1)S(1)}, bf16[32,8192]{1,0:T(8,128)(2,1)}, u32[]{:S(2)}, u32[]{:S(2)}) collective-permute-start(bf16[32,8192]{1,0:T(8,128)(2,1)S(1)} %get-tuple-element.199.refs_2_), channel_id=1, source_target_pairs={{0,2},{4,6},{8,10},{12,14},{2,0},{6,4},{10,8},{14,12},{1,3},{5,7},... | collective-permute-start | bytes 1572872 | tf_op jit(solution)/shard_map/ppermute | solution.py:108
  36.8 30.6 %collective-permute-start.6 = (bf16[32,8192]{1,0:T(8,128)(2,1)}, bf16[32,8192]{1,0:T(8,128)(2,1)}, u32[]{:S(2)}, u32[]{:S(2)}) collective-permute-start(bf16[32,8192]{1,0:T(8,128)(2,1)} %collective-permute-done.2.refs_6_), channel_id=1, source_target_pairs={{4,8},{6,10},{8,4},{10,6},{5,9},{7,11},{9,5},{11,7},{20,24},{22,26... | collective-permute-start | bytes 1572872 | tf_op jit(solution)/shard_map/ppermute | solution.py:108
  40.3 32.6 %collective-permute-start.8 = (bf16[32,8192]{1,0:T(8,128)(2,1)S(1)}, bf16[32,8192]{1,0:T(8,128)(2,1)}, u32[]{:S(2)}, u32[]{:S(2)}) collective-permute-start(bf16[32,8192]{1,0:T(8,128)(2,1)S(1)} %get-tuple-element.206.refs_3_), channel_id=1, source_target_pairs={{0,4},{2,6},{8,12},{10,14},{4,0},{6,2},{12,8},{14,10},{1,5},{3,7},... | collective-permute-start | bytes 1572872 | tf_op jit(solution)/shard_map/ppermute | solution.py:108
  44.3 28.6 %collective-permute-start.7 = (bf16[32,8192]{1,0:T(8,128)(2,1)S(1)}, bf16[32,8192]{1,0:T(8,128)(2,1)}, u32[]{:S(2)}, u32[]{:S(2)}) collective-permute-start(bf16[32,8192]{1,0:T(8,128)(2,1)S(1)} %get-tuple-element.206.refs_3_), channel_id=1, source_target_pairs={{0,2},{4,6},{8,10},{12,14},{2,0},{6,4},{10,8},{14,12},{1,3},{5,7},... | collective-permute-start | bytes 1572872 | tf_op jit(solution)/shard_map/ppermute | solution.py:108
  63.9 15.1 %collective-permute-start.17 = (bf16[32,8192]{1,0:T(8,128)(2,1)}, bf16[32,8192]{1,0:T(8,128)(2,1)S(1)}, u32[]{:S(2)}, u32[]{:S(2)}) collective-permute-start(bf16[32,8192]{1,0:T(8,128)(2,1)} %collective-permute-done.5.refs_4_), channel_id=1, source_target_pairs={{0,2},{4,6},{8,10},{12,14},{2,0},{6,4},{10,8},{14,12},{1,3},{5,7},... | collective-permute-start | bytes 1572872 | tf_op jit(solution)/shard_map/ppermute | solution.py:108
  66.0 14.4 %collective-permute-start.16 = (bf16[32,8192]{1,0:T(8,128)(2,1)S(1)}, bf16[32,8192]{1,0:T(8,128)(2,1)}, u32[]{:S(2)}, u32[]{:S(2)}) collective-permute-start(bf16[32,8192]{1,0:T(8,128)(2,1)S(1)} %get-tuple-element.199.refs_2_), channel_id=1, source_target_pairs={{4,8},{6,10},{8,4},{10,6},{5,9},{7,11},{9,5},{11,7},{20,24},{22,26... | collective-permute-start | bytes 1572872 | tf_op jit(solution)/shard_map/ppermute | solution.py:108
  67.4 17.4 %collective-permute-start.18 = (bf16[32,8192]{1,0:T(8,128)(2,1)}, bf16[32,8192]{1,0:T(8,128)(2,1)}, u32[]{:S(2)}, u32[]{:S(2)}) collective-permute-start(bf16[32,8192]{1,0:T(8,128)(2,1)} %collective-permute-done.3), channel_id=1, source_target_pairs={{4,0},{6,2},{8,12},{10,14},{5,1},{7,3},{9,13},{11,15},{20,16},{22,... | collective-permute-start | bytes 1572872 | tf_op jit(solution)/shard_map/ppermute | solution.py:108
  72.9 17.2 %collective-permute-start.13 = (bf16[32,8192]{1,0:T(8,128)(2,1)S(1)}, bf16[32,8192]{1,0:T(8,128)(2,1)S(1)}, u32[]{:S(2)}, u32[]{:S(2)}) collective-permute-start(bf16[32,8192]{1,0:T(8,128)(2,1)S(1)} %get-tuple-element.206.refs_3_), channel_id=1, source_target_pairs={{4,8},{6,10},{8,4},{10,6},{5,9},{7,11},{9,5},{11,7},{20,24},{22,26... | collective-permute-start | bytes 1572872 | tf_op jit(solution)/shard_map/ppermute | solution.py:108
  73.6 17.8 %collective-permute-start.14 = (bf16[32,8192]{1,0:T(8,128)(2,1)}, bf16[32,8192]{1,0:T(8,128)(2,1)S(1)}, u32[]{:S(2)}, u32[]{:S(2)}) collective-permute-start(bf16[32,8192]{1,0:T(8,128)(2,1)} %collective-permute-done.2.refs_6_), channel_id=1, source_target_pairs={{0,2},{4,6},{8,10},{12,14},{2,0},{6,4},{10,8},{14,12},{1,3},{5,7},... | collective-permute-start | bytes 1572872 | tf_op jit(solution)/shard_map/ppermute | solution.py:108
  79.1 16.8 %collective-permute-start.15 = (bf16[32,8192]{1,0:T(8,128)(2,1)}, bf16[32,8192]{1,0:T(8,128)(2,1)S(1)}, u32[]{:S(2)}, u32[]{:S(2)}) collective-permute-start(bf16[32,8192]{1,0:T(8,128)(2,1)} %copy-done.27), channel_id=1, source_target_pairs={{4,0},{6,2},{8,12},{10,14},{5,1},{7,3},{9,13},{11,15},{20,16},{22,... | collective-permute-start | bytes 1572872 | tf_op jit(solution)/shard_map/ppermute | solution.py:108
  85.9 33.1 %collective-permute-start.23 = (bf16[32,8192]{1,0:T(8,128)(2,1)S(1)}, bf16[32,8192]{1,0:T(8,128)(2,1)S(1)}, u32[]{:S(2)}, u32[]{:S(2)}) collective-permute-start(bf16[32,8192]{1,0:T(8,128)(2,1)S(1)} %broadcast_select_fusion.7.refs_4_), channel_id=1, source_target_pairs={{0,2},{4,6},{8,10},{12,14},{2,0},{6,4},{10,8},{14,12},{1,3},{5,7},... | collective-permute-start | bytes 1572872 | tf_op jit(solution)/shard_map/ppermute | solution.py:108
  88.6 31.7 %collective-permute-start.22 = (bf16[32,8192]{1,0:T(8,128)(2,1)}, bf16[32,8192]{1,0:T(8,128)(2,1)}, u32[]{:S(2)}, u32[]{:S(2)}) collective-permute-start(bf16[32,8192]{1,0:T(8,128)(2,1)} %collective-permute-done.11.refs_0_), channel_id=1, source_target_pairs={{4,8},{6,10},{8,4},{10,6},{5,9},{7,11},{9,5},{11,7},{20,24},{22,26... | collective-permute-start | bytes 1572872 | tf_op jit(solution)/shard_map/ppermute | solution.py:108
  90.1 49.3 %copy-start.29 = (bf16[32,8192]{1,0:T(8,128)(2,1)}, bf16[32,8192]{1,0:T(8,128)(2,1)S(1)}, u32[]{:S(2)}) copy-start(bf16[32,8192]{1,0:T(8,128)(2,1)S(1)} %collective-permute-done.13) | copy-start | bytes 1572868
  90.1 30.2 %collective-permute-start.24 = (bf16[32,8192]{1,0:T(8,128)(2,1)}, bf16[32,8192]{1,0:T(8,128)(2,1)S(1)}, u32[]{:S(2)}, u32[]{:S(2)}) collective-permute-start(bf16[32,8192]{1,0:T(8,128)(2,1)} %collective-permute-done.9), channel_id=1, source_target_pairs={{4,0},{6,2},{8,12},{10,14},{5,1},{7,3},{9,13},{11,15},{20,16},{22,... | collective-permute-start | bytes 1572872 | tf_op jit(solution)/shard_map/ppermute | solution.py:108
  95.9 26.2 %collective-permute-start.20 = (bf16[32,8192]{1,0:T(8,128)(2,1)S(1)}, bf16[32,8192]{1,0:T(8,128)(2,1)S(1)}, u32[]{:S(2)}, u32[]{:S(2)}) collective-permute-start(bf16[32,8192]{1,0:T(8,128)(2,1)S(1)} %broadcast_select_fusion.6.refs_6_), channel_id=1, source_target_pairs={{0,2},{4,6},{8,10},{12,14},{2,0},{6,4},{10,8},{14,12},{1,3},{5,7},... | collective-permute-start | bytes 1572872 | tf_op jit(solution)/shard_map/ppermute | solution.py:108
  97.6 41.1 %collective-permute-start.19 = (bf16[32,8192]{1,0:T(8,128)(2,1)}, bf16[32,8192]{1,0:T(8,128)(2,1)S(1)}, u32[]{:S(2)}, u32[]{:S(2)}) collective-permute-start(bf16[32,8192]{1,0:T(8,128)(2,1)} %collective-permute-done.8.refs_2_), channel_id=1, source_target_pairs={{4,8},{6,10},{8,4},{10,6},{5,9},{7,11},{9,5},{11,7},{20,24},{22,26... | collective-permute-start | bytes 1572872 | tf_op jit(solution)/shard_map/ppermute | solution.py:108
  119.0 19.7 %collective-permute-start.21 = (bf16[32,8192]{1,0:T(8,128)(2,1)}, bf16[32,8192]{1,0:T(8,128)(2,1)S(1)}, u32[]{:S(2)}, u32[]{:S(2)}) collective-permute-start(bf16[32,8192]{1,0:T(8,128)(2,1)} %collective-permute-done.6), channel_id=1, source_target_pairs={{4,0},{6,2},{8,12},{10,14},{5,1},{7,3},{9,13},{11,15},{20,16},{22,... | collective-permute-start | bytes 1572872 | tf_op jit(solution)/shard_map/ppermute | solution.py:108
  120.4 20.3 %collective-permute-start.27 = (bf16[32,8192]{1,0:T(8,128)(2,1)S(1)}, bf16[32,8192]{1,0:T(8,128)(2,1)S(1)}, u32[]{:S(2)}, u32[]{:S(2)}) collective-permute-start(bf16[32,8192]{1,0:T(8,128)(2,1)S(1)} %broadcast_select_fusion.5.refs_0_), channel_id=1, source_target_pairs={{0,2},{4,6},{8,10},{12,14},{2,0},{6,4},{10,8},{14,12},{1,3},{5,7},... | collective-permute-start | bytes 1572872 | tf_op jit(solution)/shard_map/ppermute | solution.py:108
  120.9 29.1 %collective-permute-start.28 = (bf16[32,8192]{1,0:T(8,128)(2,1)}, bf16[32,8192]{1,0:T(8,128)(2,1)S(1)}, u32[]{:S(2)}, u32[]{:S(2)}) collective-permute-start(bf16[32,8192]{1,0:T(8,128)(2,1)} %collective-permute-done.16), channel_id=1, source_target_pairs={{4,0},{6,2},{8,12},{10,14},{5,1},{7,3},{9,13},{11,15},{20,16},{22,... | collective-permute-start | bytes 1572872 | tf_op jit(solution)/shard_map/ppermute | solution.py:108
  138.8 14.2 %collective-permute-start.25 = (bf16[32,8192]{1,0:T(8,128)(2,1)S(1)}, bf16[32,8192]{1,0:T(8,128)(2,1)S(1)}, u32[]{:S(2)}, u32[]{:S(2)}) collective-permute-start(bf16[32,8192]{1,0:T(8,128)(2,1)S(1)} %broadcast_select_fusion.4.refs_2_), channel_id=1, source_target_pairs={{0,2},{4,6},{8,10},{12,14},{2,0},{6,4},{10,8},{14,12},{1,3},{5,7},... | collective-permute-start | bytes 1572872 | tf_op jit(solution)/shard_map/ppermute | solution.py:108
  139.4 21.8 %collective-permute-start.26 = (bf16[32,8192]{1,0:T(8,128)(2,1)S(1)}, bf16[32,8192]{1,0:T(8,128)(2,1)S(1)}, u32[]{:S(2)}, u32[]{:S(2)}) collective-permute-start(bf16[32,8192]{1,0:T(8,128)(2,1)S(1)} %collective-permute-done.13), channel_id=1, source_target_pairs={{4,0},{6,2},{8,12},{10,14},{5,1},{7,3},{9,13},{11,15},{20,16},{22,... | collective-permute-start | bytes 1572872 | tf_op jit(solution)/shard_map/ppermute | solution.py:108
  150.8 44.1 %collective-permute-start.31 = (bf16[32,8192]{1,0:T(8,128)(2,1)}, bf16[32,8192]{1,0:T(8,128)(2,1)}, u32[]{:S(2)}, u32[]{:S(2)}) collective-permute-start(bf16[32,8192]{1,0:T(8,128)(2,1)} %broadcast_select_fusion.3.refs_4_), channel_id=1, source_target_pairs={{0,2},{4,6},{8,10},{12,14},{2,0},{6,4},{10,8},{14,12},{1,3},{5,7},... | collective-permute-start | bytes 1572872 | tf_op jit(solution)/shard_map/ppermute | solution.py:108
  151.3 43.6 %collective-permute-start.32 = (bf16[32,8192]{1,0:T(8,128)(2,1)}, bf16[32,8192]{1,0:T(8,128)(2,1)}, u32[]{:S(2)}, u32[]{:S(2)}) collective-permute-start(bf16[32,8192]{1,0:T(8,128)(2,1)} %collective-permute-done.22), channel_id=1, source_target_pairs={{4,0},{6,2},{8,12},{10,14},{5,1},{7,3},{9,13},{11,15},{20,16},{22,... | collective-permute-start | bytes 1572872 | tf_op jit(solution)/shard_map/ppermute | solution.py:108
  162.0 90.7 %all-to-all-start = ((bf16[16,64,512]{2,1,0:T(8,128)(2,1)}), bf16[16,64,512]{2,1,0:T(8,128)(2,1)S(1)}, u32[]{:S(2)}, u32[]{:S(2)}) async-start(bf16[16,64,512]{2,1,0:T(8,128)(2,1)} %bitcast.85), calls=%async_computation | async-start | bytes 2097152 | tf_op jit(solution)/shard_map/all_to_all | solution.py:425
  166.8 33.0 %collective-permute-start.29 = (bf16[32,8192]{1,0:T(8,128)(2,1)S(1)}, bf16[32,8192]{1,0:T(8,128)(2,1)S(1)}, u32[]{:S(2)}, u32[]{:S(2)}) collective-permute-start(bf16[32,8192]{1,0:T(8,128)(2,1)S(1)} %broadcast_select_fusion.2.refs_6_), channel_id=1, source_target_pairs={{0,2},{4,6},{8,10},{12,14},{2,0},{6,4},{10,8},{14,12},{1,3},{5,7},... | collective-permute-start | bytes 1572872 | tf_op jit(solution)/shard_map/ppermute | solution.py:108
  168.7 31.9 %collective-permute-start.30 = (bf16[32,8192]{1,0:T(8,128)(2,1)}, bf16[32,8192]{1,0:T(8,128)(2,1)S(1)}, u32[]{:S(2)}, u32[]{:S(2)}) collective-permute-start(bf16[32,8192]{1,0:T(8,128)(2,1)} %copy-done.30), channel_id=1, source_target_pairs={{4,0},{6,2},{8,12},{10,14},{5,1},{7,3},{9,13},{11,15},{20,16},{22,... | collective-permute-start | bytes 1572872 | tf_op jit(solution)/shard_map/ppermute | solution.py:108
  196.8 31.5 %collective-permute-start.36 = (bf16[32,8192]{1,0:T(8,128)(2,1)}, bf16[32,8192]{1,0:T(8,128)(2,1)S(1)}, u32[]{:S(2)}, u32[]{:S(2)}) collective-permute-start(bf16[32,8192]{1,0:T(8,128)(2,1)} %broadcast_select_fusion.1.refs_0_), channel_id=1, source_target_pairs={{0,2},{4,6},{8,10},{12,14},{2,0},{6,4},{10,8},{14,12},{1,3},{5,7},... | collective-permute-start | bytes 1572872 | tf_op jit(solution)/shard_map/ppermute | solution.py:108
  197.1 31.2 %collective-permute-start.37 = (bf16[32,8192]{1,0:T(8,128)(2,1)}, bf16[32,8192]{1,0:T(8,128)(2,1)S(1)}, u32[]{:S(2)}, u32[]{:S(2)}) collective-permute-start(bf16[32,8192]{1,0:T(8,128)(2,1)} %collective-permute-done.10.refs_1_), channel_id=1, source_target_pairs={{0,4},{2,6},{8,12},{10,14},{4,0},{6,2},{12,8},{14,10},{1,5},{3,7},... | collective-permute-start | bytes 1572872 | tf_op jit(solution)/shard_map/ppermute | solution.py:108
  201.4 34.2 %collective-permute-start.33 = (bf16[32,8192]{1,0:T(8,128)(2,1)}, bf16[32,8192]{1,0:T(8,128)(2,1)}, u32[]{:S(2)}, u32[]{:S(2)}) collective-permute-start(bf16[32,8192]{1,0:T(8,128)(2,1)} %broadcast_select_fusion.refs_2_), channel_id=1, source_target_pairs={{0,2},{4,6},{8,10},{12,14},{2,0},{6,4},{10,8},{14,12},{1,3},{5,7},... | collective-permute-start | bytes 1572872 | tf_op jit(solution)/shard_map/ppermute | solution.py:108
  203.2 32.4 %collective-permute-start.34 = (bf16[32,8192]{1,0:T(8,128)(2,1)}, bf16[32,8192]{1,0:T(8,128)(2,1)}, u32[]{:S(2)}, u32[]{:S(2)}) collective-permute-start(bf16[32,8192]{1,0:T(8,128)(2,1)} %collective-permute-done.7.refs_3_), channel_id=1, source_target_pairs={{0,4},{2,6},{8,12},{10,14},{4,0},{6,2},{12,8},{14,10},{1,5},{3,7},... | collective-permute-start | bytes 1572872 | tf_op jit(solution)/shard_map/ppermute | solution.py:108
  212.0 16.4 %collective-permute-start.35 = (bf16[512,128]{1,0:T(8,128)(2,1)S(1)}, bf16[512,128]{1,0:T(8,128)(2,1)S(1)}, u32[]{:S(2)}, u32[]{:S(2)}) collective-permute-start(bf16[512,128]{1,0:T(8,128)(2,1)S(1)} %slice.38), channel_id=1, source_target_pairs={{0,2},{4,6},{8,10},{12,14},{2,0},{6,4},{10,8},{14,12},{1,3},{5,7},... | collective-permute-start | bytes 393224 | tf_op jit(solution)/shard_map/ppermute | solution.py:108
  229.3 28.5 %collective-permute-start.40 = (bf16[512,128]{1,0:T(8,128)(2,1)S(1)}, bf16[512,128]{1,0:T(8,128)(2,1)}, u32[]{:S(2)}, u32[]{:S(2)}) collective-permute-start(bf16[512,128]{1,0:T(8,128)(2,1)S(1)} %add.445), channel_id=1, source_target_pairs={{0,12},{2,14},{4,0},{6,2},{8,4},{10,6},{12,8},{14,10},{1,13},{3,15... | collective-permute-start | bytes 393224 | tf_op jit(solution)/shard_map/ppermute | solution.py:108
  233.0 25.3 %collective-permute-start.39 = (bf16[512,128]{1,0:T(8,128)(2,1)S(1)}, bf16[512,128]{1,0:T(8,128)(2,1)}, u32[]{:S(2)}, u32[]{:S(2)}) collective-permute-start(bf16[512,128]{1,0:T(8,128)(2,1)S(1)} %add.445), channel_id=1, source_target_pairs={{0,8},{2,10},{4,12},{6,14},{8,0},{10,2},{12,4},{14,6},{1,9},{3,11}... | collective-permute-start | bytes 393224 | tf_op jit(solution)/shard_map/ppermute | solution.py:108
  233.7 24.8 %collective-permute-start.38 = (bf16[512,128]{1,0:T(8,128)(2,1)S(1)}, bf16[512,128]{1,0:T(8,128)(2,1)}, u32[]{:S(2)}, u32[]{:S(2)}) collective-permute-start(bf16[512,128]{1,0:T(8,128)(2,1)S(1)} %add.445), channel_id=1, source_target_pairs={{0,4},{2,6},{4,8},{6,10},{8,12},{10,14},{12,0},{14,2},{1,5},{3,7},... | collective-permute-start | bytes 393224 | tf_op jit(solution)/shard_map/ppermute | solution.py:108
  240.0 14.9 %collective-permute-start.41 = (bf16[512,128]{1,0:T(8,128)(2,1)}, bf16[512,128]{1,0:T(8,128)(2,1)}, u32[]{:S(2)}, u32[]{:S(2)}) collective-permute-start(bf16[512,128]{1,0:T(8,128)(2,1)} %slice.60), channel_id=1, source_target_pairs={{0,2},{4,6},{8,10},{12,14},{2,0},{6,4},{10,8},{14,12},{1,3},{5,7},... | collective-permute-start | bytes 393224 | tf_op jit(solution)/shard_map/ppermute | solution.py:108
  253.4 13.9 %collective-permute-start.45 = (bf16[8,64,512]{2,1,0:T(8,128)(2,1)S(1)}, bf16[8,64,512]{2,1,0:T(8,128)(2,1)S(1)}, u32[]{:S(2)}, u32[]{:S(2)}) collective-permute-start(bf16[8,64,512]{2,1,0:T(8,128)(2,1)S(1)} %take.1.up_mine), channel_id=1, source_target_pairs={{0,16},{16,0},{1,17},{17,1},{2,18},{18,2},{3,19},{19,3},{4,20},{20... | collective-permute-start | bytes 1572872 | tf_op jit(solution)/shard_map/ppermute | solution.py:112
  255.9 7.0 %collective-permute-start.44 = (bf16[512,128]{1,0:T(8,128)(2,1)S(1)}, bf16[512,128]{1,0:T(8,128)(2,1)S(1)}, u32[]{:S(2)}, u32[]{:S(2)}) collective-permute-start(bf16[512,128]{1,0:T(8,128)(2,1)S(1)} %slice_add_fusion), channel_id=1, source_target_pairs={{0,12},{2,14},{4,0},{6,2},{8,4},{10,6},{12,8},{14,10},{1,13},{3,15... | collective-permute-start | bytes 393224 | tf_op jit(solution)/shard_map/ppermute | solution.py:108
  257.8 9.4 %collective-permute-start.43 = (bf16[512,128]{1,0:T(8,128)(2,1)S(1)}, bf16[512,128]{1,0:T(8,128)(2,1)S(1)}, u32[]{:S(2)}, u32[]{:S(2)}) collective-permute-start(bf16[512,128]{1,0:T(8,128)(2,1)S(1)} %slice_add_fusion), channel_id=1, source_target_pairs={{0,8},{2,10},{4,12},{6,14},{8,0},{10,2},{12,4},{14,6},{1,9},{3,11}... | collective-permute-start | bytes 393224 | tf_op jit(solution)/shard_map/ppermute | solution.py:108
  258.3 8.9 %collective-permute-start.42 = (bf16[512,128]{1,0:T(8,128)(2,1)S(1)}, bf16[512,128]{1,0:T(8,128)(2,1)S(1)}, u32[]{:S(2)}, u32[]{:S(2)}) collective-permute-start(bf16[512,128]{1,0:T(8,128)(2,1)S(1)} %slice_add_fusion), channel_id=1, source_target_pairs={{0,4},{2,6},{4,8},{6,10},{8,12},{10,14},{12,0},{14,2},{1,5},{3,7},... | collective-permute-start | bytes 393224 | tf_op jit(solution)/shard_map/ppermute | solution.py:108
  (34 other events, 287.6 us)

commit v4 on v3

--- a/solution.py
+++ b/solution.py
@@ -2,6 +2,7 @@
 
 import jax
 import jax.numpy as jnp
+import numpy as np
 from jax import lax
 from jax.experimental import pallas as pl
 from jax.experimental.pallas import tpu as pltpu
@@ -100,8 +101,8 @@
 OUTWARD = [(2, 0), (3, 1), (4, 6), (5, 7)]
 ALONG = [[(i, (i + 2 * d) % 8) for i in range(8)] for d in (1, 2, 3)]
 PIECE = BLOCK // 4
-DEPTH = 2048
-VMEM_LIMIT = 40 * 1024 * 1024
+DEPTH = 1024
+VMEM_LIMIT = 16 * 1024 * 1024
 
 
 def send(value, pairs):
@@ -116,7 +117,7 @@
     return pltpu.CompilerParams(vmem_limit_bytes=VMEM_LIMIT)
 
 
-def rows_kernel(n, with_base, with_small, aliased, table, *refs):
+def rows_kernel(n, first, with_base, with_small, aliased, table, *refs):
     refs = list(refs)
     pieces = [refs.pop(0) for _ in range(n)]
     weight = refs.pop(0) if with_base else None
@@ -144,7 +145,7 @@
     if with_base:
         add(acc, jnp.dot(x, weight[...], preferred_element_type=jnp.float32))
     if with_small:
-        down = jnp.concatenate([downs[0][0], downs[1][...]], axis=0)
+        down = jnp.concatenate([downs[0][...], downs[1][...]], axis=0)
         add(
             small,
             lax.dot_general(
@@ -158,15 +159,15 @@
         for i in range(n):
             cut = pl.ds(i * PIECE, PIECE)
             if with_base:
-                to = pl.ds(pl.multiple_of(table[1 + i] * PIECE, PIECE), PIECE)
+                to = pl.ds(pl.multiple_of(table[0, first + i] * PIECE, PIECE), PIECE)
                 copies.append(
                     pltpu.make_async_copy(acc.at[cut], base_out.at[to], sems.at[len(copies)])
                 )
             if with_small:
                 lane = lax.broadcasted_iota(jnp.int32, (PIECE, 2 * 64), 1)
-                use = jnp.where(lane < 64, table[1 + 2 * n + i], table[1 + 3 * n + i])
+                use = jnp.where(lane < 64, table[2, first + i], table[3, first + i])
                 rounded[cut] = jnp.where(use > 0, small[cut], 0.0).astype(jnp.bfloat16)
-                to = pl.ds(pl.multiple_of(table[1 + n + i] * PIECE, PIECE), PIECE)
+                to = pl.ds(pl.multiple_of(table[1, first + i] * PIECE, PIECE), PIECE)
                 copies.append(
                     pltpu.make_async_copy(rounded.at[cut], small_out.at[to], sems.at[len(copies)])
                 )
@@ -176,7 +177,7 @@
             copy.wait()
 
 
-def rows_call(pieces, table, weight, down_maps, down_swapped, base, small, wants):
+def rows_call(first, pieces, table, weight, down_own, down_swapped, base, small, wants):
     n = len(pieces)
     with_base, with_small = wants
     width, columns = weight.shape
@@ -188,9 +189,8 @@
         operands.append(weight)
         specs.append(pl.BlockSpec((DEPTH, columns), lambda k, t: (k, 0)))
     if with_small:
-        operands += [down_maps, down_swapped]
-        specs.append(pl.BlockSpec((1, rank, DEPTH), lambda k, t: (t[0], 0, k)))
-        specs.append(pl.BlockSpec((rank, DEPTH), lambda k, t: (0, k)))
+        operands += [down_own, down_swapped]
+        specs += [pl.BlockSpec((rank, DEPTH), lambda k, t: (0, k))] * 2
     outs, scratch, aliases = [], [], {}
     rows = 8 * BLOCK
     if with_base:
@@ -205,25 +205,20 @@
         for at, value in enumerate([base] * with_base + [small] * with_small):
             aliases[1 + len(operands)] = at
             operands.append(value)
-            specs.append(pl.BlockSpec(memory_space=pl.ANY))
-    wide = columns * with_base + 2 * rank * with_small
+            specs.append(pl.BlockSpec(memory_space=pltpu.HBM))
     return pl.pallas_call(
-        functools.partial(rows_kernel, n, with_base, with_small, aliased),
+        functools.partial(rows_kernel, n, first, with_base, with_small, aliased),
         grid_spec=pltpu.PrefetchScalarGridSpec(
             num_scalar_prefetch=1,
             grid=(width // DEPTH,),
             in_specs=specs,
-            out_specs=[pl.BlockSpec(memory_space=pl.ANY)] * len(outs),
+            out_specs=[pl.BlockSpec(memory_space=pltpu.HBM)] * len(outs),
             scratch_shapes=scratch,
         ),
         out_shape=outs,
         input_output_aliases=aliases,
         compiler_params=params(),
-        cost_estimate=pl.CostEstimate(
-            flops=2 * n * PIECE * width * wide,
-            bytes_accessed=2 * width * (wide + n * PIECE),
-            transcendentals=0,
-        ),
+        cost_estimate=pl.CostEstimate(flops=1, bytes_accessed=1, transcendentals=0),
         name="rows",
     )(table, *operands)
 
@@ -313,6 +308,12 @@
 ]
 
 
+def arrivals(n):
+    across, (name, half, pairs), _ = STEPS[n // 2]
+    along = name if pairs is OUTWARD else {"own": "near", "own_y": "near_y"}[name]
+    return [(along, half, n % 2), (across[0] + "_y", across[1], n % 2)]
+
+
 def chain_body(
     tokens, query_weight, adapter_down_maps, adapter_up_maps, adapter_home_slot, adapter_per_block
 ):
@@ -342,26 +343,37 @@
         "last": jnp.where(z < 2, 3, 0),
     }
 
-    def make_table(keys):
-        blocks, base_at, small_at = [], [], []
-        for name, half, sub in keys:
-            column = 1 - y if name.endswith("_y") else y
-            block = z_of[name.removesuffix("_y")] * 2 + column
-            blocks.append(block)
-            base_at.append(block * 4 + half * 2 + sub)
-            small_at.append(half * 16 + block * 2 + sub)
-        blocks = jnp.stack(blocks)
-        return jnp.concatenate(
-            [pick_own[None], jnp.stack(base_at), jnp.stack(small_at), is_own[blocks], is_swapped[blocks]]
-        ).astype(jnp.int32)
+    order = [("own", half, sub) for half in range(2) for sub in range(2)]
+    for n in range(14):
+        order += arrivals(n)
+    order = {key: at for at, key in enumerate(order)}
+    blocks, halves, subs = [], [], []
+    for name, half, sub in order:
+        column = 1 - y if name.endswith("_y") else y
+        blocks.append(z_of[name.removesuffix("_y")] * 2 + column)
+        halves.append(half)
+        subs.append(sub)
+    blocks = jnp.stack(blocks).astype(jnp.int32)
+    halves, subs = np.array(halves, np.int32), np.array(subs, np.int32)
+    hit = blocks[:, None] == jnp.arange(8, dtype=jnp.int32)[None, :]
+    owners = jnp.sum(jnp.where(hit, owner_row[None, :], 0), axis=1)
+    table = jnp.stack(
+        [
+            blocks * 4 + halves * 2 + subs,
+            halves * 16 + blocks * 2 + subs,
+            owners == myself,
+            owners == me * 2 + 1 - store,
+        ]
+    ).astype(jnp.int32)
 
     def work(state, keys, have, wants=(True, True)):
         base, small = state
         outs = rows_call(
+            order[keys[0]],
             [have[key] for key in keys],
-            make_table(keys),
+            table,
             query_weight,
-            adapter_down_maps,
+            down_own,
             down_swapped,
             base,
             small,
@@ -394,17 +406,13 @@
         name, half, pairs = along
         if middle is not None:
             inner_has[{"own": "far", "near": "last"}[middle[0]], middle[1], sub] = got["m"]
-        if pairs is OUTWARD:
-            key = (name, half, sub)
-            have[key] = jnp.where(inner, inner_has[key], got["z"])
-        else:
-            key = ({"own": "near", "own_y": "near_y"}[name], half, sub)
-            have[key] = got["z"]
-        seen = (across[0] + "_y", across[1], sub)
+        key, seen = arrivals(n)
+        have[key] = jnp.where(inner, inner_has[key], got["z"]) if pairs is OUTWARD else got["z"]
         have[seen] = got["y"]
         return [key, seen]
 
     flight = {0: issue(0), 1: issue(1)}
+    down_own = lax.dynamic_index_in_dim(adapter_down_maps, pick_own, 0, keepdims=False)
     down_swapped = swap(
         lax.dynamic_index_in_dim(adapter_down_maps, pick_lent, 0, keepdims=False), "store"
     )
@@ -413,7 +421,6 @@
     state = (None, None)
     waiting = [key for key in have]
     extra = {"up": up_sent}
-    up_got = None
     for n in range(14):
         got, state, have, inner_has, extra = lax.optimization_barrier(
             (flight.pop(n), state, have, inner_has, extra)
@@ -434,22 +441,23 @@
             flight[12]["first"] = send(first, ACROSS)
             extra["first"] = first
         if n == 12:
+            extra["got"] = up_got
             first = extra.pop("first") + got["first"]
             firsts = [first] + [send(first, pairs) for pairs in ALONG]
         if n in (1, 5, 9, 11):
             state = work(state, waiting, have)
             waiting = []
 
+    up_mine = take_call(owner_row.astype(jnp.int32), extra["got"])
+    up_other = swap(up_mine, "groups")
     state = work(state, waiting, have, (False, True))
     second = state[1][4 * BLOCK :]
     second = second + send(second, ACROSS)
     seconds = [second] + [send(second, pairs) for pairs in ALONG]
     state = work(state, waiting, have, (True, False))
 
-    up_mine = take_call(owner_row.astype(jnp.int32), up_got)
-    up_other = swap(up_mine, "groups")
     query = finish_call(
-        group[None].astype(jnp.int32), state[0], sum(firsts), sum(seconds), up_mine, up_other
+        group[None].astype(jnp.int32), state[0], sum(firsts[1:], firsts[0]), sum(seconds[1:], seconds[0]), up_mine, up_other
     )
     return query[None]
 

time: 275 us -> 292 us (1.062)
  waiting for transfers between devices: 65.1 us -> 76.7 us
  local copies, waits for them, and re-layouts: 56.9 us -> 65.5 us
  other arithmetic: 10.8 us -> 6.02 us
  Pallas kernels: 72.8 us -> 68.1 us
  starting transfers between devices: 65.6 us -> 69 us
    unnamed x70 -> x112, local copies, waits for them, and re-layouts: 38 us -> 59.4 us
    ppermute x44, waiting for transfers between devices: 65.1 us -> 76.7 us  [send(): return lax.ppermute(value, 'tensor', pairs)]
    gather x10 -> x0, local copies, waits for them, and re-layouts: 8.59 us -> none  [the longest x5 4.31 us: make_table(): is_swapped[blocks]]
    concatenate x5 -> x0, local copies, waits for them, and re-layouts: 4.78 us -> none  [make_table(): jnp.concatenate([pick_own[None], jnp.stack(base_at), jnp.stack(small_at),...]
    pallas_call x6, Pallas kernels: 66.3 us -> 62.5 us  [rows_call(): pl.pallas_call(functools.partial(rows_kernel, n, first, with_base, with_s...]
    ppermute x44, starting transfers between devices: 60.3 us -> 63.6 us  [send(): return lax.ppermute(value, 'tensor', pairs)]
    select_n x11 -> x8, other arithmetic: 6.74 us -> 4.48 us  [arrive(): jnp.where(inner, inner_has[key], got['z'])]
  transfers between devices with their start and end apart: 47 -> 47, of which waited for: 11 -> 9; matrix products, arithmetic and copies ran while one was open for 10% -> 3% of each run, Pallas kernels for 25% -> 21%
where the time goes in v4:
time: 292 us; the launch traced here: 290 us
  waiting for transfers between devices  76.7 us (26%)
  starting transfers between devices  69 us (24%)
  Pallas kernels  68.1 us (23%)
  local copies, waits for them, and re-layouts  65.5 us (22%)
  other arithmetic  6.02 us (2%)
  between operations  4.54 us (2%)
    ppermute x44, waiting for transfers between devices, send(): return lax.ppermute(value, 'tensor', pairs)  76.7 us
    ppermute x44, starting transfers between devices, send(): return lax.ppermute(value, 'tensor', pairs)  63.6 us
    pallas_call x6, Pallas kernels, rows_call(): pl.pallas_call(functools.partial(rows_kernel, n, first, with_base, with_s...  62.5 us
    unnamed x112, local copies, waits for them, and re-layouts  59.4 us
  transfers between devices with their start and end apart: 47, of which 9 were waited for; matrix products, arithmetic and copies ran while one was open for 3% of the time, Pallas kernels for 21%

profile of v4, /device:TPU:0, one launch (start us, length us, event | category | flops | bytes accessed | tf_op | source)
XLA Modules:
  0.0 289.9 jit_solution(12519255295660416415)
XLA Ops:
  0.0 2.7 slice_bitcast_fusion
  2.7 3.0 %collective-permute-start.5 = (bf16[32,8192]{1,0:T(8,128)(2,1)}, bf16[32,8192]{1,0:T(8,128)(2,1)}, u32[]{:S(2)}, u32[]{:S(2)}) collective-permute-start(bf16[32,8192]{1,0:T(8,128)(2,1)} %get-tuple-element.184.refs_0_), channel_id=1, source_target_pairs={{0,4},{2,6},{8,12},{10,14},{4,0},{6,2},{12,8},{14,10},{1,5},{3,7},... | collective-permute-start | bytes 1572872 | tf_op jit(solution)/shard_map/ppermute | solution.py:109
  5.7 1.5 collective-permute-start.4
  7.2 1.5 collective-permute-start.3
  8.7 3.6 %collective-permute-start.2 = (bf16[32,8192]{1,0:T(8,128)(2,1)}, bf16[32,8192]{1,0:T(8,128)(2,1)}, u32[]{:S(2)}, u32[]{:S(2)}) collective-permute-start(bf16[32,8192]{1,0:T(8,128)(2,1)} %get-tuple-element.185.refs_1_), channel_id=1, source_target_pairs={{0,4},{2,6},{8,12},{10,14},{4,0},{6,2},{12,8},{14,10},{1,5},{3,7},... | collective-permute-start | bytes 1572872 | tf_op jit(solution)/shard_map/ppermute | solution.py:109
  18.8 1.5 collective-permute-start
  20.2 2.7 dynamic-slice_bitcast_fusion
  23.8 2.2 copy-done.10
  27.9 4.1 %collective-permute-start.11 = (bf16[32,8192]{1,0:T(8,128)(2,1)S(1)}, bf16[32,8192]{1,0:T(8,128)(2,1)S(1)}, u32[]{:S(2)}, u32[]{:S(2)}) collective-permute-start(bf16[32,8192]{1,0:T(8,128)(2,1)S(1)} %get-tuple-element.200.refs_2_), channel_id=1, source_target_pairs={{0,4},{2,6},{8,12},{10,14},{4,0},{6,2},{12,8},{14,10},{1,5},{3,7},... | collective-permute-start | bytes 1572872 | tf_op jit(solution)/shard_map/ppermute | solution.py:109
  32.1 1.5 collective-permute-start.10
  35.1 4.6 %collective-permute-start.8 = (bf16[32,8192]{1,0:T(8,128)(2,1)S(1)}, bf16[32,8192]{1,0:T(8,128)(2,1)}, u32[]{:S(2)}, u32[]{:S(2)}) collective-permute-start(bf16[32,8192]{1,0:T(8,128)(2,1)S(1)} %get-tuple-element.207.refs_3_), channel_id=1, source_target_pairs={{0,4},{2,6},{8,12},{10,14},{4,0},{6,2},{12,8},{14,10},{1,5},{3,7},... | collective-permute-start | bytes 1572872 | tf_op jit(solution)/shard_map/ppermute | solution.py:109
  40.5 5.8 %copy-done = bf16[8192,1024]{1,0:T(8,128)(2,1)S(1)} copy-done((bf16[8192,1024]{1,0:T(8,128)(2,1)S(1)}, bf16[8192,1024]{1,0:T(8,128)(2,1)}, u32[]{:S(2)}) %copy-start) | copy-done | bytes 16777240
  47.3 14.7 %rows.6 = (f32[1024,1024]{1,0:T(8,128)S(1)}, bf16[1024,128]{1,0:T(8,128)(2,1)S(1)}) custom-call(s32[4,32]{1,0:T(4,128)S(1)} %pad_add_fusion.table, bf16[32,8192]{1,0:T(8,128)(2,1)} %get-tuple-element.184.refs_0_, bf16[32,8192]{1,0:T(8,128)(2,1)} %get-tuple-element.185.refs_1_, bf16[32,8192]{1,0:T(8,128)(2,1)S(1)} %get-tuple-element.200.refs_2_, ...), custom_call_target="tpu_custom_call" | custom-call | flops 1 | bytes 1 | tf_op jit(solution)/shard_map/rows/pallas_call | solution.py:209
  62.0 2.0 copy-done.4
  66.1 1.5 collective-permute-start.16
  71.3 8.8 %collective-permute-done.17.refs_5_ = bf16[32,8192]{1,0:T(8,128)(2,1)} collective-permute-done((bf16[32,8192]{1,0:T(8,128)(2,1)}, bf16[32,8192]{1,0:T(8,128)(2,1)}, u32[]{:S(2)}, u32[]{:S(2)}) %collective-permute-start.17) | collective-permute-done | bytes 524320 | tf_op jit(solution)/shard_map/ppermute | solution.py:109
  81.4 13.2 %collective-permute-done.18 = bf16[32,8192]{1,0:T(8,128)(2,1)} collective-permute-done((bf16[32,8192]{1,0:T(8,128)(2,1)}, bf16[32,8192]{1,0:T(8,128)(2,1)}, u32[]{:S(2)}, u32[]{:S(2)}) %collective-permute-start.18) | collective-permute-done | bytes 524320 | tf_op jit(solution)/shard_map/ppermute | solution.py:109
  95.7 1.5 collective-permute-start.23
  97.2 1.5 collective-permute-start.22
  100.0 4.0 %collective-permute-done.15 = bf16[32,8192]{1,0:T(8,128)(2,1)S(1)} collective-permute-done((bf16[32,8192]{1,0:T(8,128)(2,1)}, bf16[32,8192]{1,0:T(8,128)(2,1)S(1)}, u32[]{:S(2)}, u32[]{:S(2)}) %collective-permute-start.15) | collective-permute-done | bytes 524320 | tf_op jit(solution)/shard_map/ppermute | solution.py:109
  105.6 5.8 %copy-done.1 = bf16[8192,1024]{1,0:T(8,128)(2,1)S(1)} copy-done((bf16[8192,1024]{1,0:T(8,128)(2,1)S(1)}, bf16[8192,1024]{1,0:T(8,128)(2,1)}, u32[]{:S(2)}) %copy-start.1) | copy-done | bytes 16777240
  111.4 2.2 copy-done.5
  115.7 14.8 %rows.7 = (f32[1024,1024]{1,0:T(8,128)S(1)}, bf16[1024,128]{1,0:T(8,128)(2,1)S(1)}) custom-call(s32[4,32]{1,0:T(4,128)S(1)} %pad_add_fusion.table, bf16[32,8192]{1,0:T(8,128)(2,1)S(1)} %copy-done.34, bf16[32,8192]{1,0:T(8,128)(2,1)S(1)} %copy-done.29, ...), custom_call_target="tpu_custom_call", output_to_operand_aliasing={{0}: (12, {}), {1}: (13, {})} | custom-call | flops 1 | bytes 1 | tf_op jit(solution)/shard_map/rows/pallas_call | solution.py:209
  130.4 2.0 copy-done.6
  133.8 1.3 collective-permute-start.27
  137.2 15.1 %collective-permute-done.21 = bf16[32,8192]{1,0:T(8,128)(2,1)S(1)} collective-permute-done((bf16[32,8192]{1,0:T(8,128)(2,1)S(1)}, bf16[32,8192]{1,0:T(8,128)(2,1)S(1)}, u32[]{:S(2)}, u32[]{:S(2)}) %collective-permute-start.21) | collective-permute-done | bytes 524320 | tf_op jit(solution)/shard_map/ppermute | solution.py:109
  152.4 1.3 collective-permute-start.25
  155.8 7.7 %collective-permute-done.28 = bf16[32,8192]{1,0:T(8,128)(2,1)S(1)} collective-permute-done((bf16[32,8192]{1,0:T(8,128)(2,1)}, bf16[32,8192]{1,0:T(8,128)(2,1)S(1)}, u32[]{:S(2)}, u32[]{:S(2)}) %collective-permute-start.28) | collective-permute-done | bytes 524320 | tf_op jit(solution)/shard_map/ppermute | solution.py:109
  167.8 5.9 %collective-permute-done.26 = bf16[32,8192]{1,0:T(8,128)(2,1)S(1)} collective-permute-done((bf16[32,8192]{1,0:T(8,128)(2,1)S(1)}, bf16[32,8192]{1,0:T(8,128)(2,1)S(1)}, u32[]{:S(2)}, u32[]{:S(2)}) %collective-permute-start.26) | collective-permute-done | bytes 524320 | tf_op jit(solution)/shard_map/ppermute | solution.py:109
  174.5 3.8 %all-to-all-start = ((bf16[16,64,512]{2,1,0:T(8,128)(2,1)}), bf16[16,64,512]{2,1,0:T(8,128)(2,1)S(1)}, u32[]{:S(2)}, u32[]{:S(2)}) async-start(bf16[16,64,512]{2,1,0:T(8,128)(2,1)} %bitcast.35), calls=%async_computation | async-start | bytes 2097152 | tf_op jit(solution)/shard_map/all_to_all | solution.py:432
  179.5 2.0 collective-permute-start.29
  182.8 5.8 %copy-done.2 = bf16[8192,1024]{1,0:T(8,128)(2,1)S(1)} copy-done((bf16[8192,1024]{1,0:T(8,128)(2,1)S(1)}, bf16[8192,1024]{1,0:T(8,128)(2,1)}, u32[]{:S(2)}) %copy-start.2) | copy-done | bytes 16777240
  188.6 2.2 copy-done.7
  197.0 14.8 %rows.8 = (f32[1024,1024]{1,0:T(8,128)S(1)}, bf16[1024,128]{1,0:T(8,128)(2,1)S(1)}) custom-call(s32[4,32]{1,0:T(4,128)S(1)} %pad_add_fusion.table, bf16[32,8192]{1,0:T(8,128)(2,1)S(1)} %copy-done.25, bf16[32,8192]{1,0:T(8,128)(2,1)S(1)} %copy-done.36, bf16[32,8192]{1,0:T(8,128)(2,1)S(1)} %copy-done.27, ...), custom_call_target="tpu_custom_call", output_to_operand_aliasing={{0}: (12, {}), {1}: (13, {})} | custom-call | flops 1 | bytes 1 | tf_op jit(solution)/shard_map/rows/pallas_call | solution.py:209
  213.2 2.7 collective-permute-start.37
  215.9 2.0 collective-permute-start.33
  218.0 9.5 %rows.9 = (f32[1024,1024]{1,0:T(8,128)S(1)}, bf16[1024,128]{1,0:T(8,128)(2,1)S(1)}) custom-call(s32[4,32]{1,0:T(4,128)S(1)} %pad_add_fusion.table, bf16[32,8192]{1,0:T(8,128)(2,1)S(1)} %broadcast_select_fusion.1.refs_0_, bf16[32,8192]{1,0:T(8,128)(2,1)} %collective-permute-done.31.refs_1_, ...), custom_call_target="tpu_custom_call", output_to_operand_aliasing={{0}: (8, {}), {1}: (9, {})} | custom-call | flops 1 | bytes 1 | tf_op jit(solution)/shard_map/rows/pallas_call | solution.py:209
  227.6 2.0 copy-done.8
  229.6 11.2 %collective-permute-done.35 = bf16[512,128]{1,0:T(8,128)(2,1)S(1)} collective-permute-done((bf16[512,128]{1,0:T(8,128)(2,1)S(1)}, bf16[512,128]{1,0:T(8,128)(2,1)S(1)}, u32[]{:S(2)}, u32[]{:S(2)}) %collective-permute-start.35) | collective-permute-done | bytes 131104 | tf_op jit(solution)/shard_map/ppermute | solution.py:109
  248.3 3.1 %rows.11 = bf16[1024,128]{1,0:T(8,128)(2,1)S(1)} custom-call(s32[4,32]{1,0:T(4,128)S(1)} %pad_add_fusion.table, bf16[32,8192]{1,0:T(8,128)(2,1)S(1)} %copy-done.16, bf16[32,8192]{1,0:T(8,128)(2,1)S(1)} %copy-done.13, bf16[32,8192]{1,0:T(8,128)(2,1)S(1)} %copy-done.22, bf16[32,8192]{1,0:T(8,128)(2,1)S(1)} %copy-done.19, ...), custom_call_target="tpu_custom_call", output_to_operand_aliasing={{}: (7, {})} | custom-call | flops 1 | bytes 1 | tf_op jit(solution)/shard_map/rows/pallas_call | solution.py:209
  252.7 3.5 %collective-permute-start.40 = (bf16[512,128]{1,0:T(8,128)(2,1)S(1)}, bf16[512,128]{1,0:T(8,128)(2,1)S(1)}, u32[]{:S(2)}, u32[]{:S(2)}) collective-permute-start(bf16[512,128]{1,0:T(8,128)(2,1)S(1)} %add.147), channel_id=1, source_target_pairs={{0,12},{2,14},{4,0},{6,2},{8,4},{10,6},{12,8},{14,10},{1,13},{3,15... | collective-permute-start | bytes 393224 | tf_op jit(solution)/shard_map/ppermute | solution.py:109
  257.2 1.9 collective-permute-start.38
  259.9 1.6 collective-permute-start.45
  261.5 1.9 collective-permute-start.44
  264.5 9.6 %collective-permute-done.39 = bf16[512,128]{1,0:T(8,128)(2,1)S(1)} collective-permute-done((bf16[512,128]{1,0:T(8,128)(2,1)S(1)}, bf16[512,128]{1,0:T(8,128)(2,1)S(1)}, u32[]{:S(2)}, u32[]{:S(2)}) %collective-permute-start.39) | collective-permute-done | bytes 131104 | tf_op jit(solution)/shard_map/ppermute | solution.py:109
  274.2 5.8 %copy-done.3 = bf16[8192,1024]{1,0:T(8,128)(2,1)S(1)} copy-done((bf16[8192,1024]{1,0:T(8,128)(2,1)S(1)}, bf16[8192,1024]{1,0:T(8,128)(2,1)}, u32[]{:S(2)}) %copy-start.3) | copy-done | bytes 16777240
  280.0 5.6 %rows.10.base = f32[1024,1024]{1,0:T(8,128)S(1)} custom-call(s32[4,32]{1,0:T(4,128)S(1)} %pad_add_fusion.table, bf16[32,8192]{1,0:T(8,128)(2,1)S(1)} %copy-done.17, bf16[32,8192]{1,0:T(8,128)(2,1)S(1)} %copy-done.14, bf16[32,8192]{1,0:T(8,128)(2,1)S(1)} %copy-done.23, bf16[32,8192]{1,0:T(8,128)(2,1)S(1)} %copy-done.20, ...), custom_call_target="tpu_custom_call", output_to_operand_aliasing={{}: (6, {})} | custom-call | flops 1 | bytes 1 | tf_op jit(solution)/shard_map/rows/pallas_call | solution.py:209
  285.7 4.2 %finish.1 = bf16[1024,1024]{1,0:T(8,128)(2,1)} custom-call(s32[1]{0:T(128)} %bitcast.table, f32[1024,1024]{1,0:T(8,128)S(1)} %rows.10.base, bf16[512,128]{1,0:T(8,128)(2,1)S(1)} %add_add_fusion.1.first, bf16[512,128]{1,0:T(8,128)(2,1)S(1)} %add_add_fusion.second, bf16[8,64,512]{2,1,0:T(8,128)(2,1)S(1)} %take.1.up_mine, ...), custom_call_target="tpu_custom_call" | custom-call | tf_op jit(solution)/shard_map/finish/pallas_call | solution.py:286
  (193 shorter events, 54.3 us)
Async XLA Ops:
  2.7 16.1 %collective-permute-start.5 = (bf16[32,8192]{1,0:T(8,128)(2,1)}, bf16[32,8192]{1,0:T(8,128)(2,1)}, u32[]{:S(2)}, u32[]{:S(2)}) collective-permute-start(bf16[32,8192]{1,0:T(8,128)(2,1)} %get-tuple-element.184.refs_0_), channel_id=1, source_target_pairs={{0,4},{2,6},{8,12},{10,14},{4,0},{6,2},{12,8},{14,10},{1,5},{3,7},... | collective-permute-start | bytes 1572872 | tf_op jit(solution)/shard_map/ppermute | solution.py:109
  5.7 17.2 %collective-permute-start.4 = (bf16[32,8192]{1,0:T(8,128)(2,1)}, bf16[32,8192]{1,0:T(8,128)(2,1)S(1)}, u32[]{:S(2)}, u32[]{:S(2)}) collective-permute-start(bf16[32,8192]{1,0:T(8,128)(2,1)} %get-tuple-element.184.refs_0_), channel_id=1, source_target_pairs={{0,2},{4,6},{8,10},{12,14},{2,0},{6,4},{10,8},{14,12},{1,3},{5,7},... | collective-permute-start | bytes 1572872 | tf_op jit(solution)/shard_map/ppermute | solution.py:109
  7.2 20.7 %collective-permute-start.3 = (bf16[32,8192]{1,0:T(8,128)(2,1)}, bf16[32,8192]{1,0:T(8,128)(2,1)}, u32[]{:S(2)}, u32[]{:S(2)}) collective-permute-start(bf16[32,8192]{1,0:T(8,128)(2,1)} %get-tuple-element.184.refs_0_), channel_id=1, source_target_pairs={{4,8},{6,10},{8,4},{10,6},{5,9},{7,11},{9,5},{11,7},{20,24},{22,26... | collective-permute-start | bytes 1572872 | tf_op jit(solution)/shard_map/ppermute | solution.py:109
  8.7 23.4 %collective-permute-start.2 = (bf16[32,8192]{1,0:T(8,128)(2,1)}, bf16[32,8192]{1,0:T(8,128)(2,1)}, u32[]{:S(2)}, u32[]{:S(2)}) collective-permute-start(bf16[32,8192]{1,0:T(8,128)(2,1)} %get-tuple-element.185.refs_1_), channel_id=1, source_target_pairs={{0,4},{2,6},{8,12},{10,14},{4,0},{6,2},{12,8},{14,10},{1,5},{3,7},... | collective-permute-start | bytes 1572872 | tf_op jit(solution)/shard_map/ppermute | solution.py:109
  12.3 21.3 %collective-permute-start.1 = (bf16[32,8192]{1,0:T(8,128)(2,1)}, bf16[32,8192]{1,0:T(8,128)(2,1)}, u32[]{:S(2)}, u32[]{:S(2)}) collective-permute-start(bf16[32,8192]{1,0:T(8,128)(2,1)} %get-tuple-element.185.refs_1_), channel_id=1, source_target_pairs={{0,2},{4,6},{8,10},{12,14},{2,0},{6,4},{10,8},{14,12},{1,3},{5,7},... | collective-permute-start | bytes 1572872 | tf_op jit(solution)/shard_map/ppermute | solution.py:109
  18.8 15.5 %collective-permute-start = (bf16[32,8192]{1,0:T(8,128)(2,1)}, bf16[32,8192]{1,0:T(8,128)(2,1)}, u32[]{:S(2)}, u32[]{:S(2)}) collective-permute-start(bf16[32,8192]{1,0:T(8,128)(2,1)} %get-tuple-element.185.refs_1_), channel_id=1, source_target_pairs={{4,8},{6,10},{8,4},{10,6},{5,9},{7,11},{9,5},{11,7},{20,24},{22,26... | collective-permute-start | bytes 1572872 | tf_op jit(solution)/shard_map/ppermute | solution.py:109
  23.7 11.3 %collective-permute-start.12 = (bf16[64,8192]{1,0:T(8,128)(2,1)}, bf16[64,8192]{1,0:T(8,128)(2,1)S(1)}, u32[]{:S(2)}, u32[]{:S(2)}) collective-permute-start(bf16[64,8192]{1,0:T(8,128)(2,1)} %get-tuple-element.345), channel_id=1, source_target_pairs={{0,1},{1,0},{2,3},{3,2},{4,5},{5,4},{6,7},{7,6},{8,9},{9,8},{10,11... | collective-permute-start | bytes 3145736 | tf_op jit(solution)/shard_map/ppermute | solution.py:113
  27.9 36.1 %collective-permute-start.11 = (bf16[32,8192]{1,0:T(8,128)(2,1)S(1)}, bf16[32,8192]{1,0:T(8,128)(2,1)S(1)}, u32[]{:S(2)}, u32[]{:S(2)}) collective-permute-start(bf16[32,8192]{1,0:T(8,128)(2,1)S(1)} %get-tuple-element.200.refs_2_), channel_id=1, source_target_pairs={{0,4},{2,6},{8,12},{10,14},{4,0},{6,2},{12,8},{14,10},{1,5},{3,7},... | collective-permute-start | bytes 1572872 | tf_op jit(solution)/shard_map/ppermute | solution.py:109
  32.1 32.0 %collective-permute-start.10 = (bf16[32,8192]{1,0:T(8,128)(2,1)S(1)}, bf16[32,8192]{1,0:T(8,128)(2,1)S(1)}, u32[]{:S(2)}, u32[]{:S(2)}) collective-permute-start(bf16[32,8192]{1,0:T(8,128)(2,1)S(1)} %get-tuple-element.200.refs_2_), channel_id=1, source_target_pairs={{0,2},{4,6},{8,10},{12,14},{2,0},{6,4},{10,8},{14,12},{1,3},{5,7},... | collective-permute-start | bytes 1572872 | tf_op jit(solution)/shard_map/ppermute | solution.py:109
  33.6 6.1 %collective-permute-start.9 = (bf16[32,8192]{1,0:T(8,128)(2,1)}, bf16[32,8192]{1,0:T(8,128)(2,1)S(1)}, u32[]{:S(2)}, u32[]{:S(2)}) collective-permute-start(bf16[32,8192]{1,0:T(8,128)(2,1)} %collective-permute-done.5.refs_4_), channel_id=1, source_target_pairs={{4,8},{6,10},{8,4},{10,6},{5,9},{7,11},{9,5},{11,7},{20,24},{22,26... | collective-permute-start | bytes 1572872 | tf_op jit(solution)/shard_map/ppermute | solution.py:109
  34.3 33.3 %collective-permute-start.6 = (bf16[32,8192]{1,0:T(8,128)(2,1)}, bf16[32,8192]{1,0:T(8,128)(2,1)S(1)}, u32[]{:S(2)}, u32[]{:S(2)}) collective-permute-start(bf16[32,8192]{1,0:T(8,128)(2,1)} %collective-permute-done.2.refs_6_), channel_id=1, source_target_pairs={{4,8},{6,10},{8,4},{10,6},{5,9},{7,11},{9,5},{11,7},{20,24},{22,26... | collective-permute-start | bytes 1572872 | tf_op jit(solution)/shard_map/ppermute | solution.py:109
  35.1 34.6 %collective-permute-start.8 = (bf16[32,8192]{1,0:T(8,128)(2,1)S(1)}, bf16[32,8192]{1,0:T(8,128)(2,1)}, u32[]{:S(2)}, u32[]{:S(2)}) collective-permute-start(bf16[32,8192]{1,0:T(8,128)(2,1)S(1)} %get-tuple-element.207.refs_3_), channel_id=1, source_target_pairs={{0,4},{2,6},{8,12},{10,14},{4,0},{6,2},{12,8},{14,10},{1,5},{3,7},... | collective-permute-start | bytes 1572872 | tf_op jit(solution)/shard_map/ppermute | solution.py:109
  39.7 30.0 %collective-permute-start.7 = (bf16[32,8192]{1,0:T(8,128)(2,1)S(1)}, bf16[32,8192]{1,0:T(8,128)(2,1)}, u32[]{:S(2)}, u32[]{:S(2)}) collective-permute-start(bf16[32,8192]{1,0:T(8,128)(2,1)S(1)} %get-tuple-element.207.refs_3_), channel_id=1, source_target_pairs={{0,2},{4,6},{8,10},{12,14},{2,0},{6,4},{10,8},{14,12},{1,3},{5,7},... | collective-permute-start | bytes 1572872 | tf_op jit(solution)/shard_map/ppermute | solution.py:109
  64.9 15.2 %collective-permute-start.17 = (bf16[32,8192]{1,0:T(8,128)(2,1)}, bf16[32,8192]{1,0:T(8,128)(2,1)}, u32[]{:S(2)}, u32[]{:S(2)}) collective-permute-start(bf16[32,8192]{1,0:T(8,128)(2,1)} %collective-permute-done.5.refs_4_), channel_id=1, source_target_pairs={{0,2},{4,6},{8,10},{12,14},{2,0},{6,4},{10,8},{14,12},{1,3},{5,7},... | collective-permute-start | bytes 1572872 | tf_op jit(solution)/shard_map/ppermute | solution.py:109
  66.1 15.2 %collective-permute-start.16 = (bf16[32,8192]{1,0:T(8,128)(2,1)S(1)}, bf16[32,8192]{1,0:T(8,128)(2,1)}, u32[]{:S(2)}, u32[]{:S(2)}) collective-permute-start(bf16[32,8192]{1,0:T(8,128)(2,1)S(1)} %get-tuple-element.200.refs_2_), channel_id=1, source_target_pairs={{4,8},{6,10},{8,4},{10,6},{5,9},{7,11},{9,5},{11,7},{20,24},{22,26... | collective-permute-start | bytes 1572872 | tf_op jit(solution)/shard_map/ppermute | solution.py:109
  68.4 26.2 %collective-permute-start.18 = (bf16[32,8192]{1,0:T(8,128)(2,1)}, bf16[32,8192]{1,0:T(8,128)(2,1)}, u32[]{:S(2)}, u32[]{:S(2)}) collective-permute-start(bf16[32,8192]{1,0:T(8,128)(2,1)} %collective-permute-done.3), channel_id=1, source_target_pairs={{4,0},{6,2},{8,12},{10,14},{5,1},{7,3},{9,13},{11,15},{20,16},{22,... | collective-permute-start | bytes 1572872 | tf_op jit(solution)/shard_map/ppermute | solution.py:109
  69.7 29.0 %collective-permute-start.13 = (bf16[32,8192]{1,0:T(8,128)(2,1)S(1)}, bf16[32,8192]{1,0:T(8,128)(2,1)S(1)}, u32[]{:S(2)}, u32[]{:S(2)}) collective-permute-start(bf16[32,8192]{1,0:T(8,128)(2,1)S(1)} %get-tuple-element.207.refs_3_), channel_id=1, source_target_pairs={{4,8},{6,10},{8,4},{10,6},{5,9},{7,11},{9,5},{11,7},{20,24},{22,26... | collective-permute-start | bytes 1572872 | tf_op jit(solution)/shard_map/ppermute | solution.py:109
  70.4 29.6 %collective-permute-start.14 = (bf16[32,8192]{1,0:T(8,128)(2,1)}, bf16[32,8192]{1,0:T(8,128)(2,1)S(1)}, u32[]{:S(2)}, u32[]{:S(2)}) collective-permute-start(bf16[32,8192]{1,0:T(8,128)(2,1)} %collective-permute-done.2.refs_6_), channel_id=1, source_target_pairs={{0,2},{4,6},{8,10},{12,14},{2,0},{6,4},{10,8},{14,12},{1,3},{5,7},... | collective-permute-start | bytes 1572872 | tf_op jit(solution)/shard_map/ppermute | solution.py:109
  80.1 23.9 %collective-permute-start.15 = (bf16[32,8192]{1,0:T(8,128)(2,1)}, bf16[32,8192]{1,0:T(8,128)(2,1)S(1)}, u32[]{:S(2)}, u32[]{:S(2)}) collective-permute-start(bf16[32,8192]{1,0:T(8,128)(2,1)} %collective-permute-done), channel_id=1, source_target_pairs={{4,0},{6,2},{8,12},{10,14},{5,1},{7,3},{9,13},{11,15},{20,16},{22,... | collective-permute-start | bytes 1572872 | tf_op jit(solution)/shard_map/ppermute | solution.py:109
  95.7 36.8 %collective-permute-start.23 = (bf16[32,8192]{1,0:T(8,128)(2,1)S(1)}, bf16[32,8192]{1,0:T(8,128)(2,1)S(1)}, u32[]{:S(2)}, u32[]{:S(2)}) collective-permute-start(bf16[32,8192]{1,0:T(8,128)(2,1)S(1)} %broadcast_select_fusion.7.refs_4_), channel_id=1, source_target_pairs={{0,2},{4,6},{8,10},{12,14},{2,0},{6,4},{10,8},{14,12},{1,3},{5,7},... | collective-permute-start | bytes 1572872 | tf_op jit(solution)/shard_map/ppermute | solution.py:109
  97.2 36.5 %collective-permute-start.22 = (bf16[32,8192]{1,0:T(8,128)(2,1)}, bf16[32,8192]{1,0:T(8,128)(2,1)}, u32[]{:S(2)}, u32[]{:S(2)}) collective-permute-start(bf16[32,8192]{1,0:T(8,128)(2,1)} %copy-done.33), channel_id=1, source_target_pairs={{4,8},{6,10},{8,4},{10,6},{5,9},{7,11},{9,5},{11,7},{20,24},{22,26... | collective-permute-start | bytes 1572872 | tf_op jit(solution)/shard_map/ppermute | solution.py:109
  98.7 55.0 %copy-start.47 = (bf16[32,8192]{1,0:T(8,128)(2,1)}, bf16[32,8192]{1,0:T(8,128)(2,1)S(1)}, u32[]{:S(2)}) copy-start(bf16[32,8192]{1,0:T(8,128)(2,1)S(1)} %collective-permute-done.13) | copy-start | bytes 1572868
  98.7 35.0 %collective-permute-start.24 = (bf16[32,8192]{1,0:T(8,128)(2,1)}, bf16[32,8192]{1,0:T(8,128)(2,1)S(1)}, u32[]{:S(2)}, u32[]{:S(2)}) collective-permute-start(bf16[32,8192]{1,0:T(8,128)(2,1)} %copy-done.45), channel_id=1, source_target_pairs={{4,0},{6,2},{8,12},{10,14},{5,1},{7,3},{9,13},{11,15},{20,16},{22,... | collective-permute-start | bytes 1572872 | tf_op jit(solution)/shard_map/ppermute | solution.py:109
  104.1 33.1 %collective-permute-start.20 = (bf16[32,8192]{1,0:T(8,128)(2,1)S(1)}, bf16[32,8192]{1,0:T(8,128)(2,1)S(1)}, u32[]{:S(2)}, u32[]{:S(2)}) collective-permute-start(bf16[32,8192]{1,0:T(8,128)(2,1)S(1)} %broadcast_select_fusion.6.refs_6_), channel_id=1, source_target_pairs={{0,2},{4,6},{8,10},{12,14},{2,0},{6,4},{10,8},{14,12},{1,3},{5,7},... | collective-permute-start | bytes 1572872 | tf_op jit(solution)/shard_map/ppermute | solution.py:109
  104.9 47.4 %collective-permute-start.19 = (bf16[32,8192]{1,0:T(8,128)(2,1)}, bf16[32,8192]{1,0:T(8,128)(2,1)S(1)}, u32[]{:S(2)}, u32[]{:S(2)}) collective-permute-start(bf16[32,8192]{1,0:T(8,128)(2,1)} %collective-permute-done.8.refs_2_), channel_id=1, source_target_pairs={{4,8},{6,10},{8,4},{10,6},{5,9},{7,11},{9,5},{11,7},{20,24},{22,26... | collective-permute-start | bytes 1572872 | tf_op jit(solution)/shard_map/ppermute | solution.py:109
  132.4 19.9 %collective-permute-start.21 = (bf16[32,8192]{1,0:T(8,128)(2,1)S(1)}, bf16[32,8192]{1,0:T(8,128)(2,1)S(1)}, u32[]{:S(2)}, u32[]{:S(2)}) collective-permute-start(bf16[32,8192]{1,0:T(8,128)(2,1)S(1)} %copy-done.44), channel_id=1, source_target_pairs={{4,0},{6,2},{8,12},{10,14},{5,1},{7,3},{9,13},{11,15},{20,16},{22,... | collective-permute-start | bytes 1572872 | tf_op jit(solution)/shard_map/ppermute | solution.py:109
  133.8 22.0 %collective-permute-start.27 = (bf16[32,8192]{1,0:T(8,128)(2,1)S(1)}, bf16[32,8192]{1,0:T(8,128)(2,1)S(1)}, u32[]{:S(2)}, u32[]{:S(2)}) collective-permute-start(bf16[32,8192]{1,0:T(8,128)(2,1)S(1)} %broadcast_select_fusion.5.refs_0_), channel_id=1, source_target_pairs={{0,2},{4,6},{8,10},{12,14},{2,0},{6,4},{10,8},{14,12},{1,3},{5,7},... | collective-permute-start | bytes 1572872 | tf_op jit(solution)/shard_map/ppermute | solution.py:109
  135.9 27.6 %collective-permute-start.28 = (bf16[32,8192]{1,0:T(8,128)(2,1)}, bf16[32,8192]{1,0:T(8,128)(2,1)S(1)}, u32[]{:S(2)}, u32[]{:S(2)}) collective-permute-start(bf16[32,8192]{1,0:T(8,128)(2,1)} %collective-permute-done.16), channel_id=1, source_target_pairs={{4,0},{6,2},{8,12},{10,14},{5,1},{7,3},{9,13},{11,15},{20,16},{22,... | collective-permute-start | bytes 1572872 | tf_op jit(solution)/shard_map/ppermute | solution.py:109
  152.4 14.6 %collective-permute-start.25 = (bf16[32,8192]{1,0:T(8,128)(2,1)S(1)}, bf16[32,8192]{1,0:T(8,128)(2,1)S(1)}, u32[]{:S(2)}, u32[]{:S(2)}) collective-permute-start(bf16[32,8192]{1,0:T(8,128)(2,1)S(1)} %broadcast_select_fusion.4.refs_2_), channel_id=1, source_target_pairs={{0,2},{4,6},{8,10},{12,14},{2,0},{6,4},{10,8},{14,12},{1,3},{5,7},... | collective-permute-start | bytes 1572872 | tf_op jit(solution)/shard_map/ppermute | solution.py:109
  154.5 19.2 %collective-permute-start.26 = (bf16[32,8192]{1,0:T(8,128)(2,1)S(1)}, bf16[32,8192]{1,0:T(8,128)(2,1)S(1)}, u32[]{:S(2)}, u32[]{:S(2)}) collective-permute-start(bf16[32,8192]{1,0:T(8,128)(2,1)S(1)} %collective-permute-done.13), channel_id=1, source_target_pairs={{4,0},{6,2},{8,12},{10,14},{5,1},{7,3},{9,13},{11,15},{20,16},{22,... | collective-permute-start | bytes 1572872 | tf_op jit(solution)/shard_map/ppermute | solution.py:109
  164.4 47.4 %collective-permute-start.31 = (bf16[32,8192]{1,0:T(8,128)(2,1)}, bf16[32,8192]{1,0:T(8,128)(2,1)}, u32[]{:S(2)}, u32[]{:S(2)}) collective-permute-start(bf16[32,8192]{1,0:T(8,128)(2,1)} %broadcast_select_fusion.3.refs_4_), channel_id=1, source_target_pairs={{0,2},{4,6},{8,10},{12,14},{2,0},{6,4},{10,8},{14,12},{1,3},{5,7},... | collective-permute-start | bytes 1572872 | tf_op jit(solution)/shard_map/ppermute | solution.py:109
  165.6 46.2 %collective-permute-start.32 = (bf16[32,8192]{1,0:T(8,128)(2,1)}, bf16[32,8192]{1,0:T(8,128)(2,1)}, u32[]{:S(2)}, u32[]{:S(2)}) collective-permute-start(bf16[32,8192]{1,0:T(8,128)(2,1)} %collective-permute-done.22), channel_id=1, source_target_pairs={{4,0},{6,2},{8,12},{10,14},{5,1},{7,3},{9,13},{11,15},{20,16},{22,... | collective-permute-start | bytes 1572872 | tf_op jit(solution)/shard_map/ppermute | solution.py:109
  174.5 69.6 %all-to-all-start = ((bf16[16,64,512]{2,1,0:T(8,128)(2,1)}), bf16[16,64,512]{2,1,0:T(8,128)(2,1)S(1)}, u32[]{:S(2)}, u32[]{:S(2)}) async-start(bf16[16,64,512]{2,1,0:T(8,128)(2,1)} %bitcast.35), calls=%async_computation | async-start | bytes 2097152 | tf_op jit(solution)/shard_map/all_to_all | solution.py:432
  179.5 36.3 %collective-permute-start.29 = (bf16[32,8192]{1,0:T(8,128)(2,1)S(1)}, bf16[32,8192]{1,0:T(8,128)(2,1)S(1)}, u32[]{:S(2)}, u32[]{:S(2)}) collective-permute-start(bf16[32,8192]{1,0:T(8,128)(2,1)S(1)} %broadcast_select_fusion.2.refs_6_), channel_id=1, source_target_pairs={{0,2},{4,6},{8,10},{12,14},{2,0},{6,4},{10,8},{14,12},{1,3},{5,7},... | collective-permute-start | bytes 1572872 | tf_op jit(solution)/shard_map/ppermute | solution.py:109
  181.5 34.3 %collective-permute-start.30 = (bf16[32,8192]{1,0:T(8,128)(2,1)}, bf16[32,8192]{1,0:T(8,128)(2,1)S(1)}, u32[]{:S(2)}, u32[]{:S(2)}) collective-permute-start(bf16[32,8192]{1,0:T(8,128)(2,1)} %copy-done.48), channel_id=1, source_target_pairs={{4,0},{6,2},{8,12},{10,14},{5,1},{7,3},{9,13},{11,15},{20,16},{22,... | collective-permute-start | bytes 1572872 | tf_op jit(solution)/shard_map/ppermute | solution.py:109
  213.0 27.8 %collective-permute-start.36 = (bf16[32,8192]{1,0:T(8,128)(2,1)S(1)}, bf16[32,8192]{1,0:T(8,128)(2,1)S(1)}, u32[]{:S(2)}, u32[]{:S(2)}) collective-permute-start(bf16[32,8192]{1,0:T(8,128)(2,1)S(1)} %broadcast_select_fusion.1.refs_0_), channel_id=1, source_target_pairs={{0,2},{4,6},{8,10},{12,14},{2,0},{6,4},{10,8},{14,12},{1,3},{5,7},... | collective-permute-start | bytes 1572872 | tf_op jit(solution)/shard_map/ppermute | solution.py:109
  213.2 28.5 %collective-permute-start.37 = (bf16[32,8192]{1,0:T(8,128)(2,1)S(1)}, bf16[32,8192]{1,0:T(8,128)(2,1)S(1)}, u32[]{:S(2)}, u32[]{:S(2)}) collective-permute-start(bf16[32,8192]{1,0:T(8,128)(2,1)S(1)} %copy-done.30), channel_id=1, source_target_pairs={{0,4},{2,6},{8,12},{10,14},{4,0},{6,2},{12,8},{14,10},{1,5},{3,7},... | collective-permute-start | bytes 1572872 | tf_op jit(solution)/shard_map/ppermute | solution.py:109
  215.9 26.5 %collective-permute-start.33 = (bf16[32,8192]{1,0:T(8,128)(2,1)S(1)}, bf16[32,8192]{1,0:T(8,128)(2,1)S(1)}, u32[]{:S(2)}, u32[]{:S(2)}) collective-permute-start(bf16[32,8192]{1,0:T(8,128)(2,1)S(1)} %broadcast_select_fusion.refs_2_), channel_id=1, source_target_pairs={{0,2},{4,6},{8,10},{12,14},{2,0},{6,4},{10,8},{14,12},{1,3},{5,7},... | collective-permute-start | bytes 1572872 | tf_op jit(solution)/shard_map/ppermute | solution.py:109
  217.9 25.4 %collective-permute-start.34 = (bf16[32,8192]{1,0:T(8,128)(2,1)}, bf16[32,8192]{1,0:T(8,128)(2,1)S(1)}, u32[]{:S(2)}, u32[]{:S(2)}) collective-permute-start(bf16[32,8192]{1,0:T(8,128)(2,1)} %collective-permute-done.7.refs_3_), channel_id=1, source_target_pairs={{0,4},{2,6},{8,12},{10,14},{4,0},{6,2},{12,8},{14,10},{1,5},{3,7},... | collective-permute-start | bytes 1572872 | tf_op jit(solution)/shard_map/ppermute | solution.py:109
  217.9 22.9 %collective-permute-start.35 = (bf16[512,128]{1,0:T(8,128)(2,1)S(1)}, bf16[512,128]{1,0:T(8,128)(2,1)S(1)}, u32[]{:S(2)}, u32[]{:S(2)}) collective-permute-start(bf16[512,128]{1,0:T(8,128)(2,1)S(1)} %slice.38), channel_id=1, source_target_pairs={{0,2},{4,6},{8,10},{12,14},{2,0},{6,4},{10,8},{14,12},{1,3},{5,7},... | collective-permute-start | bytes 393224 | tf_op jit(solution)/shard_map/ppermute | solution.py:109
  251.3 10.1 %collective-permute-start.41 = (bf16[512,128]{1,0:T(8,128)(2,1)S(1)}, bf16[512,128]{1,0:T(8,128)(2,1)S(1)}, u32[]{:S(2)}, u32[]{:S(2)}) collective-permute-start(bf16[512,128]{1,0:T(8,128)(2,1)S(1)} %slice.40), channel_id=1, source_target_pairs={{0,2},{4,6},{8,10},{12,14},{2,0},{6,4},{10,8},{14,12},{1,3},{5,7},... | collective-permute-start | bytes 393224 | tf_op jit(solution)/shard_map/ppermute | solution.py:109
  252.7 10.7 %collective-permute-start.40 = (bf16[512,128]{1,0:T(8,128)(2,1)S(1)}, bf16[512,128]{1,0:T(8,128)(2,1)S(1)}, u32[]{:S(2)}, u32[]{:S(2)}) collective-permute-start(bf16[512,128]{1,0:T(8,128)(2,1)S(1)} %add.147), channel_id=1, source_target_pairs={{0,12},{2,14},{4,0},{6,2},{8,4},{10,6},{12,8},{14,10},{1,13},{3,15... | collective-permute-start | bytes 393224 | tf_op jit(solution)/shard_map/ppermute | solution.py:109
  256.2 17.9 %collective-permute-start.39 = (bf16[512,128]{1,0:T(8,128)(2,1)S(1)}, bf16[512,128]{1,0:T(8,128)(2,1)S(1)}, u32[]{:S(2)}, u32[]{:S(2)}) collective-permute-start(bf16[512,128]{1,0:T(8,128)(2,1)S(1)} %add.147), channel_id=1, source_target_pairs={{0,8},{2,10},{4,12},{6,14},{8,0},{10,2},{12,4},{14,6},{1,9},{3,11}... | collective-permute-start | bytes 393224 | tf_op jit(solution)/shard_map/ppermute | solution.py:109
  257.2 16.9 %collective-permute-start.38 = (bf16[512,128]{1,0:T(8,128)(2,1)S(1)}, bf16[512,128]{1,0:T(8,128)(2,1)S(1)}, u32[]{:S(2)}, u32[]{:S(2)}) collective-permute-start(bf16[512,128]{1,0:T(8,128)(2,1)S(1)} %add.147), channel_id=1, source_target_pairs={{0,4},{2,6},{4,8},{6,10},{8,12},{10,14},{12,0},{14,2},{1,5},{3,7},... | collective-permute-start | bytes 393224 | tf_op jit(solution)/shard_map/ppermute | solution.py:109
  259.9 25.7 %collective-permute-start.45 = (bf16[8,64,512]{2,1,0:T(8,128)(2,1)S(1)}, bf16[8,64,512]{2,1,0:T(8,128)(2,1)S(1)}, u32[]{:S(2)}, u32[]{:S(2)}) collective-permute-start(bf16[8,64,512]{2,1,0:T(8,128)(2,1)S(1)} %take.1.up_mine), channel_id=1, source_target_pairs={{0,16},{16,0},{1,17},{17,1},{2,18},{18,2},{3,19},{19,3},{4,20},{20... | collective-permute-start | bytes 1572872 | tf_op jit(solution)/shard_map/ppermute | solution.py:113
  261.5 24.1 %collective-permute-start.44 = (bf16[512,128]{1,0:T(8,128)(2,1)S(1)}, bf16[512,128]{1,0:T(8,128)(2,1)S(1)}, u32[]{:S(2)}, u32[]{:S(2)}) collective-permute-start(bf16[512,128]{1,0:T(8,128)(2,1)S(1)} %slice_add_fusion), channel_id=1, source_target_pairs={{0,12},{2,14},{4,0},{6,2},{8,4},{10,6},{12,8},{14,10},{1,13},{3,15... | collective-permute-start | bytes 393224 | tf_op jit(solution)/shard_map/ppermute | solution.py:109
  263.4 22.2 %collective-permute-start.43 = (bf16[512,128]{1,0:T(8,128)(2,1)S(1)}, bf16[512,128]{1,0:T(8,128)(2,1)S(1)}, u32[]{:S(2)}, u32[]{:S(2)}) collective-permute-start(bf16[512,128]{1,0:T(8,128)(2,1)S(1)} %slice_add_fusion), channel_id=1, source_target_pairs={{0,8},{2,10},{4,12},{6,14},{8,0},{10,2},{12,4},{14,6},{1,9},{3,11}... | collective-permute-start | bytes 393224 | tf_op jit(solution)/shard_map/ppermute | solution.py:109
  274.1 11.5 %collective-permute-start.42 = (bf16[512,128]{1,0:T(8,128)(2,1)S(1)}, bf16[512,128]{1,0:T(8,128)(2,1)S(1)}, u32[]{:S(2)}, u32[]{:S(2)}) collective-permute-start(bf16[512,128]{1,0:T(8,128)(2,1)S(1)} %slice_add_fusion), channel_id=1, source_target_pairs={{0,4},{2,6},{4,8},{6,10},{8,12},{10,14},{12,0},{14,2},{1,5},{3,7},... | collective-permute-start | bytes 393224 | tf_op jit(solution)/shard_map/ppermute | solution.py:109
  (55 other events, 495.8 us)

commit v5 on v1

--- a/solution.py
+++ b/solution.py
@@ -1,6 +1,11 @@
+import functools
+
 import jax
 import jax.numpy as jnp
+import numpy as np
 from jax import lax
+from jax.experimental import pallas as pl
+from jax.experimental.pallas import tpu as pltpu
 from jax.sharding import PartitionSpec as P
 
 BLOCK = 128
@@ -92,90 +97,271 @@
 
 ACROSS = both_ways([(0, 1), (2, 3), (4, 5), (6, 7)])
 NEAR = both_ways([(0, 2), (1, 3), (4, 6), (5, 7)])
-FAR = both_ways([(0, 4), (1, 5), (2, 6), (3, 7)])
-CHUNKS = 4
+MIDDLE = both_ways([(2, 4), (3, 5)])
+OUTWARD = [(2, 0), (3, 1), (4, 6), (5, 7)]
+ALONG = [[(i, (i + 2 * d) % 8) for i in range(8)] for d in (1, 2, 3)]
+HALF = BLOCK // 2
+VMEM_LIMIT = 24 * 1024 * 1024
+
+
+def send(value, pairs):
+    return lax.ppermute(value, "tensor", pairs)
 
 
 def swap(value, axis):
     return lax.ppermute(value, axis, [(0, 1), (1, 0)])
+
+
+def params():
+    return pltpu.CompilerParams(vmem_limit_bytes=VMEM_LIMIT)
+
+
+def pack_kernel(table, up, out):
+    part = out.shape[3]
+    for t in range(8):
+        at = pl.multiple_of((2 * t + table[2]) * part, part)
+        out[t, 0] = up[0, :, pl.ds(at, part)]
+
+
+def pack_call(table, up_maps):
+    _, rank, width = up_maps.shape
+    part = width // 16
+    return pl.pallas_call(
+        pack_kernel,
+        grid_spec=pltpu.PrefetchScalarGridSpec(
+            num_scalar_prefetch=1,
+            grid=(2,),
+            in_specs=[pl.BlockSpec((1, rank, width), lambda s, t: (t[s], 0, 0))],
+            out_specs=pl.BlockSpec((8, 1, rank, part), lambda s, t: (0, s, 0, 0)),
+        ),
+        out_shape=jax.ShapeDtypeStruct((8, 2, rank, part), jnp.bfloat16),
+        compiler_params=params(),
+        name="pack",
+    )(table, up_maps)
+
+
+def take_kernel(table, got, out):
+    out[...] = got[...]
+
+
+def take_call(table, got):
+    _, rank, part = got.shape
+    return pl.pallas_call(
+        take_kernel,
+        grid_spec=pltpu.PrefetchScalarGridSpec(
+            num_scalar_prefetch=1,
+            grid=(8,),
+            in_specs=[pl.BlockSpec((1, rank, part), lambda b, t: (t[b], 0, 0))],
+            out_specs=pl.BlockSpec((1, rank, part), lambda b, t: (b, 0, 0)),
+        ),
+        out_shape=jax.ShapeDtypeStruct((8, rank, part), jnp.bfloat16),
+        compiler_params=params(),
+        name="take",
+    )(table, got)
+
+
+def finish_kernel(table, *refs):
+    *bases, shrunk, up_mine, up_other, out = refs
+    at = pl.program_id(0)
+    second = table[1, at] > 0
+    part = up_mine.shape[2]
+    for g, base in enumerate(bases):
+
+        @pl.when(at // 4 == g)
+        def _():
+            for up, side in ((up_mine, table[2, at]), (up_other, 1 - table[2, at])):
+                cut = pl.ds(pl.multiple_of(side * part, part), part)
+                grown = lax.dot_general(
+                    shrunk[0], up[0], (((0,), (0,)), ((), ())), preferred_element_type=jnp.float32
+                )
+                grown = jnp.where(second, grown[HALF:], grown[:HALF])
+                out[:, cut] = (base[:, cut] + 0.5 * grown).astype(out.dtype)
+
+
+def finish_call(table, bases, shrunk, up_mine, up_other):
+    columns = bases[0].shape[1]
+    _, rank, part = up_mine.shape
+
+    def base_spec(g):
+        return pl.BlockSpec((HALF, columns), lambda i, t: (jnp.clip(i - 4 * g, 0, 3), 0))
+
+    up = pl.BlockSpec((1, rank, part), lambda i, t: (t[0, i], 0, 0))
+    return pl.pallas_call(
+        finish_kernel,
+        grid_spec=pltpu.PrefetchScalarGridSpec(
+            num_scalar_prefetch=1,
+            grid=(16,),
+            in_specs=[base_spec(g) for g in range(4)]
+            + [pl.BlockSpec((1, rank, BLOCK), lambda i, t: (t[0, i], 0, 0)), up, up],
+            out_specs=pl.BlockSpec((HALF, columns), lambda i, t: (2 * t[0, i] + t[1, i], 0)),
+        ),
+        out_shape=jax.ShapeDtypeStruct((8 * BLOCK, columns), jnp.bfloat16),
+        compiler_params=params(),
+        name="finish",
+    )(table, *bases, shrunk, up_mine, up_other)
+
+
+ACROSS_SENDS = [
+    ("own", 0), ("own", 1), ("near", 1), ("near", 0), ("far", 0), ("far", 1), ("last", 0)
+]
+ALONG_SENDS = [
+    ("own", 0, NEAR), ("own", 1, NEAR), ("far", 0, OUTWARD), ("far", 1, OUTWARD),
+    ("last", 0, OUTWARD), ("last", 1, OUTWARD), ("last_y", 1, OUTWARD),
+]
+MIDDLE_SENDS = [("own", 0), ("own", 1), ("near", 0), ("near", 1), ("near_y", 1)]
+BEYOND = {"own": "far", "near": "last", "near_y": "last_y"}
+
+
+def arrivals(n):
+    name, half, pairs = ALONG_SENDS[n]
+    across = ACROSS_SENDS[n]
+    return [("near" if pairs is NEAR else name, half), (across[0] + "_y", across[1])]
 
 
 def chain_body(
     tokens, query_weight, adapter_down_maps, adapter_up_maps, adapter_home_slot, adapter_per_block
 ):
     me = lax.axis_index("tensor")
+    z, y = me // 2, me % 2
     store = lax.axis_index("store")
     group = lax.axis_index("groups")
     myself = me * 2 + store
+    inner = (z == 1) | (z == 2)
     held, rank, width = adapter_down_maps.shape
-    columns = query_weight.shape[1]
-    part = columns // 2
     rows = tokens[0]
-    step = BLOCK // CHUNKS
+
+    have = {("own", 0): rows[:HALF], ("own", 1): rows[HALF:]}
+    inner_has = {}
+
+    def send_across(n):
+        return send(have[ACROSS_SENDS[n]], ACROSS)
+
+    def send_along(n):
+        name, half, pairs = ALONG_SENDS[n]
+        return send((inner_has if pairs is OUTWARD else have)[name, half], pairs)
+
+    def send_middle(n):
+        return send(have[MIDDLE_SENDS[n]], MIDDLE)
+
+    flight = {n: {} for n in range(7)}
+    flight[0]["z"], flight[0]["y"] = send_along(0), send_across(0)
+    flight[0]["m"] = send_middle(0)
+    flight[1]["z"], flight[1]["y"] = send_along(1), send_across(1)
 
     store_slots = find_slots(adapter_home_slot, adapter_per_block)
     owner = store_slots // held
     inside = store_slots % held
     picked = jnp.max(jnp.where(owner == myself, inside, 0), axis=1)
-    owner_row = lax.dynamic_index_in_dim(owner, store, 0, keepdims=False)
-
-    gathered = [
-        lax.all_gather(rows[c * step : (c + 1) * step], "tensor", axis=0) for c in range(CHUNKS)
-    ]
-
-    def pick(maps, index):
-        local = lax.dynamic_index_in_dim(picked, index, 0, keepdims=False)
-        return lax.dynamic_index_in_dim(maps, local, 0, keepdims=False)
-
-    down_own = pick(adapter_down_maps, store)
-    down_swapped = swap(pick(adapter_down_maps, 1 - store), "store")
-    candidates = jnp.concatenate([down_own, down_swapped])
-    use_own = (owner_row == myself)[:, None, None]
-    use_swapped = (owner_row == me * 2 + 1 - store)[:, None, None]
-
-    def shrink(chunk):
-        value = lax.dot_general(
-            candidates,
-            chunk.reshape(8 * step, width),
-            (((1,), (1,)), ((), ())),
-            preferred_element_type=jnp.float32,
+    owner_row = lax.dynamic_index_in_dim(owner, store, 0, keepdims=False).astype(jnp.int32)
+    pick_own = lax.dynamic_index_in_dim(picked, store, 0, keepdims=False)
+    pick_lent = lax.dynamic_index_in_dim(picked, 1 - store, 0, keepdims=False)
+
+    down_own = lax.dynamic_index_in_dim(adapter_down_maps, pick_own, 0, keepdims=False)
+    down_lent = lax.dynamic_index_in_dim(adapter_down_maps, pick_lent, 0, keepdims=False)
+    candidates = jnp.concatenate([down_own, swap(down_lent, "store")])
+    up_sent = pack_call(jnp.concatenate([picked, group[None]]).astype(jnp.int32), adapter_up_maps)
+
+    z_of = {
+        "own": z,
+        "near": z + 1 - 2 * (z % 2),
+        "far": jnp.where(z < 2, 2, 1),
+        "last": jnp.where(z < 2, 3, 0),
+    }
+    order = [("own", 0), ("own", 1)]
+    for n in range(7):
+        order += arrivals(n)
+    order = {key: at for at, key in enumerate(order)}
+    blocks = jnp.stack(
+        [
+            z_of[name.removesuffix("_y")] * 2 + (1 - y if name.endswith("_y") else y)
+            for name, _ in order
+        ]
+    ).astype(jnp.int32)
+    halves = np.array([half for _, half in order], np.int32)
+    hit = blocks[:, None] == jnp.arange(8, dtype=jnp.int32)[None, :]
+    owners = jnp.sum(jnp.where(hit, owner_row[None, :], 0), axis=1)
+    is_own = owners == myself
+    is_swapped = owners == me * 2 + 1 - store
+
+    def shrink(shrunk, keys):
+        block = jnp.concatenate([have[key] for key in keys])
+        small = lax.dot_general(
+            candidates, block, (((1,), (1,)), ((), ())), preferred_element_type=jnp.float32
         )
-        value = value.reshape(2, rank, 8, step).transpose(0, 2, 1, 3)
-        value = jnp.where(use_own, value[0], jnp.where(use_swapped, value[1], 0))
-        value = value.astype(jnp.bfloat16)
-        for pairs in (ACROSS, NEAR, FAR):
-            value = value + lax.ppermute(value, "tensor", pairs)
-        return value
-
-    def columns_of(up):
-        halves = up.reshape(rank, 8, 2, part)
-        half = lax.dynamic_index_in_dim(halves, group, 2, keepdims=False)
-        return half.transpose(1, 0, 2)
-
-    up_sent = jnp.stack(
-        [columns_of(pick(adapter_up_maps, 0)), columns_of(pick(adapter_up_maps, 1))], axis=1
-    )
-    up_got = lax.all_to_all(
-        up_sent.reshape(16, rank, part), ("tensor", "store"), split_axis=0, concat_axis=0, tiled=True
-    )
-    up_half = jnp.stack(
-        [lax.dynamic_index_in_dim(up_got, owner_row[b], 0, keepdims=False) for b in range(8)]
-    )
-    up_other = swap(up_half, "groups")
-    up = jnp.concatenate(
-        [jnp.where(group == 0, up_half, up_other), jnp.where(group == 0, up_other, up_half)], axis=2
-    )
-
-    outputs = []
-    for chunk in gathered:
-        base = jnp.dot(
-            chunk.reshape(8 * step, width), query_weight, preferred_element_type=jnp.float32
+        for i, key in enumerate(keys):
+            at = order[key]
+            cut = slice(i * HALF, (i + 1) * HALF)
+            value = jnp.where(
+                is_own[at], small[:rank, cut], jnp.where(is_swapped[at], small[rank:, cut], 0)
+            )
+            shrunk = lax.dynamic_update_slice(
+                shrunk, value.astype(jnp.bfloat16)[None, None], (blocks[at], int(halves[at]), 0, 0)
+            )
+        return shrunk
+
+    def times_weight(keys):
+        block = jnp.concatenate([have[key] for key in keys])
+        return jnp.dot(block, query_weight, preferred_element_type=jnp.float32)
+
+    waiting = [("own", 0), ("own", 1)]
+    shrunk = jnp.zeros((8, 2, rank, HALF), jnp.bfloat16)
+    bases = []
+    extra = {"up": up_sent}
+    for n in range(7):
+        got, have, inner_has, shrunk, bases, extra = lax.optimization_barrier(
+            (flight[n], have, inner_has, shrunk, bases, extra)
         )
-        grown = jnp.einsum("brn,brf->bnf", shrink(chunk), up, preferred_element_type=jnp.float32)
-        value = base.reshape(8, step, columns) + 0.5 * grown
-        outputs.append(value.astype(jnp.bfloat16))
-    query = jnp.concatenate(outputs, axis=1)
-    return query.reshape(1, 8 * BLOCK, columns)
+        if "m" in got:
+            name, half = MIDDLE_SENDS[n]
+            inner_has[BEYOND[name], half] = got["m"]
+        along, across = arrivals(n)
+        have[along] = (
+            got["z"] if ALONG_SENDS[n][2] is NEAR else jnp.where(inner, inner_has[along], got["z"])
+        )
+        have[across] = got["y"]
+        waiting += [along, across]
+        if n == 1:
+            flight[2]["y"] = send_across(2)
+        if n + 2 < 7:
+            flight[n + 2]["z"] = send_along(n + 2)
+            if n > 0:
+                flight[n + 2]["y"] = send_across(n + 2)
+        if n + 1 < len(MIDDLE_SENDS):
+            flight[n + 1]["m"] = send_middle(n + 1)
+        if n == 4:
+            flight[6]["up"] = lax.all_to_all(
+                extra.pop("up").reshape(16, rank, -1),
+                ("tensor", "store"),
+                split_axis=0,
+                concat_axis=0,
+                tiled=True,
+            )
+        if n < 6:
+            shrunk = shrink(shrunk, waiting[-2:] if n else waiting)
+        if n == 5:
+            early = shrunk[2:6]
+            flight[6]["early"] = send(early, ACROSS)
+            extra["early"] = early
+        if len(waiting) == 4 and n < 6:
+            bases = bases + [times_weight(waiting)]
+            waiting = []
+
+    shrunk = shrink(shrunk, waiting[-2:])
+    late = jnp.concatenate([shrunk[:2], shrunk[6:]])
+    late = late + send(late, ACROSS)
+    early = extra["early"] + got["early"]
+    for pairs in ALONG:
+        early = early + send(extra["early"] + got["early"], pairs)
+    lates = [late] + [send(late, pairs) for pairs in ALONG]
+    bases = bases + [times_weight(waiting)]
+    late = sum(lates[1:], lates[0])
+    total = jnp.concatenate([late[:2], early, late[2:]])
+    total = total.transpose(0, 2, 1, 3).reshape(8, rank, BLOCK)
+
+    up_mine = take_call(owner_row, got["up"])
+    up_other = swap(up_mine, "groups")
+    table = jnp.stack([blocks, halves, jnp.broadcast_to(group, (16,))]).astype(jnp.int32)
+    return finish_call(table, bases, total, up_mine, up_other)[None]
 
 
 def body(tokens, *rest):

time: 382 us -> 247 us (0.65)
  waiting for transfers between devices: 259 us -> 62.6 us
  between operations: 35.7 us -> 4.43 us
  other arithmetic: 3.73 us -> 34.1 us
  starting transfers between devices: 24.1 us -> 50.6 us
  matrix products: 44.3 us -> 63.5 us
  Pallas kernels: 0 us -> 10.6 us
  local copies, waits for them, and re-layouts: 13.9 us -> 19.8 us
    all_gather x4 -> x0, waiting for transfers between devices: 231 us -> none  [chain_body(): lax.all_gather(rows[c * step:(c + 1) * step], 'tensor', axis=0)]
    ppermute x12 -> x27, waiting for transfers between devices: 3.8 us -> 56.6 us  [send(): return lax.ppermute(value, 'tensor', pairs)]
    ppermute x12 -> x27, starting transfers between devices: 14.6 us -> 38.6 us  [send(): return lax.ppermute(value, 'tensor', pairs)]
    broadcast_in_dim x0 -> x7, other arithmetic: none -> 20.1 us  [shrink(): value.astype(jnp.bfloat16)[None, None]]
    dot_general x12 -> x11, matrix products: 44.3 us -> 63.5 us  [the longest x4 47.1 us: times_weight(): return jnp.dot(block, query_weight, preferred_element_type=jnp.float32)]
    ppermute x2, waiting for transfers between devices: 11.5 us -> 0.01 us  [swap(): return lax.ppermute(value, axis, [(0, 1), (1, 0)])]
    pallas_call x0 -> x3, Pallas kernels: none -> 10.6 us  [the longest x1 8.26 us: finish_call(): pl.pallas_call(finish_kernel, grid_spec=pltpu.PrefetchScalarGridSpec(num_...]
    select_n x1 -> x5, other arithmetic: 0.07 us -> 9.69 us  [chain_body(): jnp.where(inner, inner_has[along], got['z'])]
  transfers between devices with their start and end apart: 19 -> 30, of which waited for: 9 -> 12; matrix products, arithmetic and copies ran while one was open for 14% -> 44% of each run, Pallas kernels for 0% -> 1%
where the time goes in v5:
time: 247 us; the launch traced here: 246 us
  matrix products  63.5 us (26%)
  waiting for transfers between devices  62.6 us (25%)
  starting transfers between devices  50.6 us (20%)
  other arithmetic  34.1 us (14%)
  local copies, waits for them, and re-layouts  19.8 us (8%)
  Pallas kernels  10.6 us (4%)
  between operations  4.43 us (2%)
    ppermute x27, waiting for transfers between devices, send(): return lax.ppermute(value, 'tensor', pairs)  56.6 us
    dot_general x4, matrix products, times_weight(): return jnp.dot(block, query_weight, preferred_element_type=jnp.float32)  47.1 us
    ppermute x27, starting transfers between devices, send(): return lax.ppermute(value, 'tensor', pairs)  38.6 us
    broadcast_in_dim x7, other arithmetic, shrink(): value.astype(jnp.bfloat16)[None, None]  20.1 us
    dot_general x7, matrix products, shrink(): lax.dot_general(candidates, block, (((1,), (1,)), ((), ())), preferred_el...  16.4 us
    all_to_all x1, starting transfers between devices, chain_body(): lax.all_to_all(extra.pop('up').reshape(16, rank, -1), ('tensor', 'store')...  10.4 us
    select_n x5, other arithmetic, chain_body(): jnp.where(inner, inner_has[along], got['z'])  9.69 us
    pallas_call x1, Pallas kernels, finish_call(): pl.pallas_call(finish_kernel, grid_spec=pltpu.PrefetchScalarGridSpec(num_...  8.26 us
  transfers between devices with their start and end apart: 30, of which 12 were waited for; matrix products, arithmetic and copies ran while one was open for 44% of the time, Pallas kernels for 1%

profile of v5, /device:TPU:0, one launch (start us, length us, event | category | flops | bytes accessed | tf_op | source)
XLA Modules:
  0.0 245.6 jit_solution(4406753743195558911)
XLA Ops:
  0.0 1.7 slice_bitcast_fusion
  1.7 1.6 collective-permute-start
  3.4 3.0 %collective-permute-start.1 = (bf16[64,8192]{1,0:T(8,128)(2,1)S(1)}, bf16[64,8192]{1,0:T(8,128)(2,1)}, u32[]{:S(2)}, u32[]{:S(2)}) collective-permute-start(bf16[64,8192]{1,0:T(8,128)(2,1)S(1)} %get-tuple-element.73), channel_id=1, source_target_pairs={{0,2},{4,6},{8,10},{12,14},{2,0},{6,4},{10,8},{14,12},{1,3},{5,7},... | collective-permute-start | bytes 3145736 | tf_op jit(solution)/shard_map/ppermute | solution.py:108
  6.3 3.5 %collective-permute-start.2 = (bf16[64,8192]{1,0:T(8,128)(2,1)S(1)}, bf16[64,8192]{1,0:T(8,128)(2,1)}, u32[]{:S(2)}, u32[]{:S(2)}) collective-permute-start(bf16[64,8192]{1,0:T(8,128)(2,1)S(1)} %get-tuple-element.73), channel_id=1, source_target_pairs={{0,4},{2,6},{8,12},{10,14},{4,0},{6,2},{12,8},{14,10},{1,5},{3,7},... | collective-permute-start | bytes 3145736 | tf_op jit(solution)/shard_map/ppermute | solution.py:108
  16.1 2.2 copy-done
  18.3 1.6 pack.1
  20.6 1.8 dynamic-slice_bitcast_fusion.1
  22.4 8.0 %collective-permute-done.1 = bf16[64,8192]{1,0:T(8,128)(2,1)} collective-permute-done((bf16[64,8192]{1,0:T(8,128)(2,1)S(1)}, bf16[64,8192]{1,0:T(8,128)(2,1)}, u32[]{:S(2)}, u32[]{:S(2)}) %collective-permute-start.1) | collective-permute-done | bytes 1048608 | tf_op jit(solution)/shard_map/ppermute | solution.py:108
  30.4 3.6 %collective-permute-done.2 = bf16[64,8192]{1,0:T(8,128)(2,1)} collective-permute-done((bf16[64,8192]{1,0:T(8,128)(2,1)S(1)}, bf16[64,8192]{1,0:T(8,128)(2,1)}, u32[]{:S(2)}, u32[]{:S(2)}) %collective-permute-start.2) | collective-permute-done | bytes 1048608 | tf_op jit(solution)/shard_map/ppermute | solution.py:108
  34.1 1.6 collective-permute-start.3
  39.9 4.7 %fusion.83 = (bf16[1,1,64,64]{3,2,1,0:T(8,128)(2,1)S(1)}, bf16[1,1,64,64]{3,2,1,0:T(8,128)(2,1)S(1)}, bf16[1,1,64,64]{3,2,1,0:T(8,128)(2,1)S(1)}, bf16[1,1,64,64]{3,2,1,0:T(8,128)(2,1)S(1)}) fusion(bf16[128,256]{1,0:T(8,128)(2,1)S(1)} %fusion.108, pred[]{:T(512)} %bitcast.27, pred[]{:T(512)} %bitcast.26, pred[]{:T(512)} %bitcast.21, pred[]{:T(512)} %bitcast.20, ...), kind=kLoop, calls=%fused_computation.113 | loop fusion | flops 32768 | bytes 98312 | tf_op jit(solution)/shard_map/broadcast_in_dim | solution.py:298
  47.3 9.5 %fusion.114.refs_0_ = f32[256,1024]{1,0:T(8,128)S(1)} fusion(bf16[256,8192]{1,0:T(8,128)(2,1)} %copy-done.7, bf16[8192,1024]{1,0:T(8,128)(2,1)} %param.8), kind=kOutput, calls=%fused_computation.165 | convolution fusion | flops 4294967296 | bytes 22020096 | tf_op jit(solution)/shard_map/dot_general | solution.py:304
  60.2 2.6 %fusion.24 = bf16[128,128]{1,0:T(8,128)(2,1)S(1)} fusion(bf16[64,8192]{1,0:T(8,128)(2,1)} %collective-permute-done.4, bf16[64,8192]{1,0:T(8,128)(2,1)} %collective-permute-done.5, bf16[64,8192]{1,0:T(8,128)(2,1)} %copy-done.11, bf16[64,8192]{1,0:T(8,128)(2,1)S(1)} %get-tuple-element.139), kind=kOutput, calls=%fused_computation.25 | convolution fusion | flops 276824064 | bytes 4227072 | tf_op jit(solution)/shard_map/dot_general | solution.py:288
  62.8 2.6 %fusion.85 = (bf16[1,1,64,64]{3,2,1,0:T(8,128)(2,1)S(1)}, bf16[1,1,64,64]{3,2,1,0:T(8,128)(2,1)S(1)}) fusion(bf16[128,128]{1,0:T(8,128)(2,1)S(1)} %fusion.24, pred[]{:T(512)} %bitcast.33, pred[]{:T(512)} %bitcast.32, pred[]{:T(512)} %bitcast.30, pred[]{:T(512)} %bitcast.29), kind=kLoop, calls=%fused_computation.115 | loop fusion | flops 16384 | bytes 49156 | tf_op jit(solution)/shard_map/broadcast_in_dim | solution.py:298
  67.2 11.7 %collective-permute-done.9 = bf16[64,8192]{1,0:T(8,128)(2,1)} collective-permute-done((bf16[64,8192]{1,0:T(8,128)(2,1)}, bf16[64,8192]{1,0:T(8,128)(2,1)}, u32[]{:S(2)}, u32[]{:S(2)}) %collective-permute-start.9) | collective-permute-done | bytes 1048608 | tf_op jit(solution)/shard_map/ppermute | solution.py:108
  78.9 5.0 %collective-permute-done.8 = bf16[64,8192]{1,0:T(8,128)(2,1)} collective-permute-done((bf16[64,8192]{1,0:T(8,128)(2,1)}, bf16[64,8192]{1,0:T(8,128)(2,1)}, u32[]{:S(2)}, u32[]{:S(2)}) %collective-permute-start.8) | collective-permute-done | bytes 1048608 | tf_op jit(solution)/shard_map/ppermute | solution.py:108
  84.0 2.3 broadcast_select_fusion.4
  86.8 2.6 %fusion.28 = bf16[128,128]{1,0:T(8,128)(2,1)S(1)} fusion(bf16[64,8192]{1,0:T(8,128)(2,1)} %collective-permute-done.8, bf16[64,8192]{1,0:T(8,128)(2,1)} %broadcast_select_fusion.4, bf16[64,8192]{1,0:T(8,128)(2,1)} %copy-done.11, bf16[64,8192]{1,0:T(8,128)(2,1)S(1)} %get-tuple-element.139), kind=kOutput, calls=%fused_computation.29 | convolution fusion | flops 276824064 | bytes 4227072 | tf_op jit(solution)/shard_map/dot_general | solution.py:288
  89.4 2.7 %fusion.87 = (bf16[1,1,64,64]{3,2,1,0:T(8,128)(2,1)S(1)}, bf16[1,1,64,64]{3,2,1,0:T(8,128)(2,1)S(1)}) fusion(bf16[128,128]{1,0:T(8,128)(2,1)S(1)} %fusion.28, pred[]{:T(512)} %bitcast.39, pred[]{:T(512)} %bitcast.38, pred[]{:T(512)} %bitcast.36, pred[]{:T(512)} %bitcast.35), kind=kLoop, calls=%fused_computation.117 | loop fusion | flops 16384 | bytes 49156 | tf_op jit(solution)/shard_map/broadcast_in_dim | solution.py:298
  92.1 1.6 collective-permute-start.10
  95.6 12.6 %fusion.refs_1_ = f32[256,1024]{1,0:T(8,128)} fusion(bf16[8192,1024]{1,0:T(8,128)(2,1)} %param.8, bf16[64,8192]{1,0:T(8,128)(2,1)} %collective-permute-done.8, bf16[64,8192]{1,0:T(8,128)(2,1)} %broadcast_select_fusion.4, bf16[64,8192]{1,0:T(8,128)(2,1)} %collective-permute-done.4, bf16[64,8192]{1,0:T(8,128)(2,1)} %collective-permute-done.5), kind=kOutput, calls=%fused_computation | convolution fusion | flops 4311744512 | bytes 22020096 | tf_op jit(solution)/shard_map/dot_general | solution.py:304
  108.2 1.7 collective-permute-start.15
  109.8 2.4 broadcast_select_fusion.3
  113.7 2.3 fusion.32
  116.0 2.7 %fusion.89 = (bf16[1,1,64,64]{3,2,1,0:T(8,128)(2,1)S(1)}, bf16[1,1,64,64]{3,2,1,0:T(8,128)(2,1)S(1)}) fusion(bf16[128,128]{1,0:T(8,128)(2,1)S(1)} %fusion.32, pred[]{:T(512)} %bitcast.45, pred[]{:T(512)} %bitcast.44, pred[]{:T(512)} %bitcast.42, pred[]{:T(512)} %bitcast.41), kind=kLoop, calls=%fused_computation.119 | loop fusion | flops 16384 | bytes 49156 | tf_op jit(solution)/shard_map/broadcast_in_dim | solution.py:298
  120.6 8.4 %collective-permute-done.16 = bf16[64,8192]{1,0:T(8,128)(2,1)} collective-permute-done((bf16[64,8192]{1,0:T(8,128)(2,1)}, bf16[64,8192]{1,0:T(8,128)(2,1)}, u32[]{:S(2)}, u32[]{:S(2)}) %collective-permute-start.16) | collective-permute-done | bytes 1048608 | tf_op jit(solution)/shard_map/ppermute | solution.py:108
  128.9 2.3 broadcast_select_fusion.2
  131.8 2.6 %fusion.36 = bf16[128,128]{1,0:T(8,128)(2,1)S(1)} fusion(bf16[64,8192]{1,0:T(8,128)(2,1)} %collective-permute-done.16, bf16[64,8192]{1,0:T(8,128)(2,1)} %broadcast_select_fusion.2, bf16[64,8192]{1,0:T(8,128)(2,1)} %copy-done.11, bf16[64,8192]{1,0:T(8,128)(2,1)S(1)} %get-tuple-element.139), kind=kOutput, calls=%fused_computation.37 | convolution fusion | flops 276824064 | bytes 4227072 | tf_op jit(solution)/shard_map/dot_general | solution.py:288
  134.3 2.4 fusion.91
  138.6 12.6 %fusion.8.refs_2_ = f32[256,1024]{1,0:T(8,128)} fusion(bf16[8192,1024]{1,0:T(8,128)(2,1)} %param.8, bf16[64,8192]{1,0:T(8,128)(2,1)} %collective-permute-done.16, bf16[64,8192]{1,0:T(8,128)(2,1)} %broadcast_select_fusion.2, bf16[64,8192]{1,0:T(8,128)(2,1)} %collective-permute-done.11, bf16[64,8192]{1,0:T(8,128)(2,1)} %broadcast_select_fusion.3), kind=kOutput, calls=%fused_computation.8 | convolution fusion | flops 4311744512 | bytes 22020096 | tf_op jit(solution)/shard_map/dot_general | solution.py:304
  151.4 4.0 %collective-permute-done.14 = bf16[64,8192]{1,0:T(8,128)(2,1)} collective-permute-done((bf16[64,8192]{1,0:T(8,128)(2,1)}, bf16[64,8192]{1,0:T(8,128)(2,1)}, u32[]{:S(2)}, u32[]{:S(2)}) %collective-permute-start.14) | collective-permute-done | bytes 1048608 | tf_op jit(solution)/shard_map/ppermute | solution.py:108
  155.4 10.4 %all-to-all-start = ((bf16[16,64,512]{2,1,0:T(8,128)(2,1)}), bf16[16,64,512]{2,1,0:T(8,128)(2,1)S(1)}, u32[]{:S(2)}, u32[]{:S(2)}) async-start(bf16[16,64,512]{2,1,0:T(8,128)(2,1)} %bitcast.59), calls=%async_computation | async-start | bytes 2097152 | tf_op jit(solution)/shard_map/all_to_all | solution.py:332
  168.2 2.3 fusion.40
  170.4 2.6 %fusion.93 = (bf16[1,1,64,64]{3,2,1,0:T(8,128)(2,1)S(1)}, bf16[1,1,64,64]{3,2,1,0:T(8,128)(2,1)S(1)}) fusion(bf16[128,128]{1,0:T(8,128)(2,1)S(1)} %fusion.40, pred[]{:T(512)} %bitcast.57, pred[]{:T(512)} %bitcast.56, pred[]{:T(512)} %bitcast.54, pred[]{:T(512)} %bitcast.53), kind=kLoop, calls=%fused_computation.123 | loop fusion | flops 16384 | bytes 49156 | tf_op jit(solution)/shard_map/broadcast_in_dim | solution.py:298
  173.7 2.0 collective-permute-start.18
  176.3 6.4 %collective-permute-done.18 = bf16[4,2,64,64]{3,1,2,0:T(2,128)(2,1)} collective-permute-done((bf16[4,2,64,64]{3,1,2,0:T(2,128)(2,1)S(1)}, bf16[4,2,64,64]{3,1,2,0:T(2,128)(2,1)}, u32[]{:S(2)}, u32[]{:S(2)}) %collective-permute-start.18) | collective-permute-done | bytes 65568 | tf_op jit(solution)/shard_map/ppermute | solution.py:108
  182.8 6.0 %all-to-all-done.got = bf16[16,64,512]{2,1,0:T(8,128)(2,1)S(1)} async-done(((bf16[16,64,512]{2,1,0:T(8,128)(2,1)}), bf16[16,64,512]{2,1,0:T(8,128)(2,1)S(1)}, u32[]{:S(2)}, u32[]{:S(2)}) %all-to-all-start) | async-done | bytes 1048608 | tf_op jit(solution)/shard_map/all_to_all | solution.py:332
  189.9 3.2 %collective-permute-start.27 = (bf16[4,2,64,64]{3,1,2,0:T(2,128)(2,1)S(1)}, bf16[4,2,64,64]{3,1,2,0:T(2,128)(2,1)}, u32[]{:S(2)}, u32[]{:S(2)}) collective-permute-start(bf16[4,2,64,64]{3,1,2,0:T(2,128)(2,1)S(1)} %add.162), channel_id=1, source_target_pairs={{0,12},{2,14},{4,0},{6,2},{8,4},{10,6},{12,8},{14,10},{1,13},{3,15... | collective-permute-start | bytes 196616 | tf_op jit(solution)/shard_map/ppermute | solution.py:108
  193.1 1.9 collective-permute-start.26
  195.1 1.9 collective-permute-start.25
  198.4 2.6 %fusion.44 = bf16[128,128]{1,0:T(8,128)(2,1)S(1)} fusion(bf16[64,8192]{1,0:T(8,128)(2,1)} %collective-permute-done.19, bf16[64,8192]{1,0:T(8,128)(2,1)S(1)} %broadcast_select_fusion, bf16[64,8192]{1,0:T(8,128)(2,1)} %copy-done.11, bf16[64,8192]{1,0:T(8,128)(2,1)S(1)} %get-tuple-element.139), kind=kOutput, calls=%fused_computation.45 | convolution fusion | flops 276824064 | bytes 4227072 | tf_op jit(solution)/shard_map/dot_general | solution.py:288
  201.0 2.4 fusion.95
  205.4 1.6 collective-permute-start.28
  206.9 12.5 %fusion.16.refs_3_ = f32[256,1024]{1,0:T(8,128)} fusion(bf16[8192,1024]{1,0:T(8,128)(2,1)} %param.8, bf16[64,8192]{1,0:T(8,128)(2,1)} %collective-permute-done.19, bf16[64,8192]{1,0:T(8,128)(2,1)} %copy-done.5, bf16[64,8192]{1,0:T(8,128)(2,1)} %collective-permute-done.13, bf16[64,8192]{1,0:T(8,128)(2,1)} %copy-done.4), kind=kOutput, calls=%fused_computation.16 | convolution fusion | flops 4311744512 | bytes 22020096 | tf_op jit(solution)/shard_map/dot_general | solution.py:304
  219.7 2.5 %collective-permute-start.22 = (bf16[4,2,64,64]{3,1,2,0:T(2,128)(2,1)S(1)}, bf16[4,2,64,64]{3,1,2,0:T(2,128)(2,1)S(1)}, u32[]{:S(2)}, u32[]{:S(2)}) collective-permute-start(bf16[4,2,64,64]{3,1,2,0:T(2,128)(2,1)S(1)} %fusion.107), channel_id=1, source_target_pairs={{0,4},{2,6},{4,8},{6,10},{8,12},{10,14},{12,0},{14,2},{1,5},{3,7},... | collective-permute-start | bytes 196616 | tf_op jit(solution)/shard_map/ppermute | solution.py:108
  224.8 3.2 %collective-permute-done.22 = bf16[4,2,64,64]{3,1,2,0:T(2,128)(2,1)S(1)} collective-permute-done((bf16[4,2,64,64]{3,1,2,0:T(2,128)(2,1)S(1)}, bf16[4,2,64,64]{3,1,2,0:T(2,128)(2,1)S(1)}, u32[]{:S(2)}, u32[]{:S(2)}) %collective-permute-start.22) | collective-permute-done | bytes 65568 | tf_op jit(solution)/shard_map/ppermute | solution.py:108
  228.6 5.6 %collective-permute-done.23 = bf16[4,2,64,64]{3,1,2,0:T(2,128)(2,1)S(1)} collective-permute-done((bf16[4,2,64,64]{3,1,2,0:T(2,128)(2,1)S(1)}, bf16[4,2,64,64]{3,1,2,0:T(2,128)(2,1)S(1)}, u32[]{:S(2)}, u32[]{:S(2)}) %collective-permute-start.23) | collective-permute-done | bytes 65568 | tf_op jit(solution)/shard_map/ppermute | solution.py:108
  237.4 8.3 %finish.1 = bf16[1024,1024]{1,0:T(8,128)(2,1)} custom-call(s32[3,16]{1,0:T(4,128)S(1)} %add_add_fusion.2.table, f32[256,1024]{1,0:T(8,128)S(1)} %fusion.114.refs_0_, f32[256,1024]{1,0:T(8,128)S(1)} %copy-done.1, f32[256,1024]{1,0:T(8,128)S(1)} %copy-done.2, f32[256,1024]{1,0:T(8,128)S(1)} %copy-done.3, bf16[8,64,128]{2,1,0:T(8,128)(2,1)S(1)} %reshape.12.refs_4_, ...), custom_call_target="tpu_custom_call" | custom-call | tf_op jit(solution)/shard_map/finish/pallas_call | solution.py:189
  (125 shorter events, 38.1 us)
Async XLA Ops:
  0.0 10.3 %copy-start.9 = (s32[64]{0:T(128)S(1)}, s32[64]{0:T(128)}, u32[]{:S(2)}) copy-start(s32[64]{0:T(128)} %param.11) | copy-start | bytes 772
  0.0 10.3 %copy-start.8 = (s32[2,8]{1,0:T(2,128)S(1)}, s32[2,8]{1,0:T(2,128)}, u32[]{:S(2)}) copy-start(s32[2,8]{1,0:T(2,128)} %param.12) | copy-start | bytes 196
  1.7 20.6 %collective-permute-start = (bf16[64,8192]{1,0:T(8,128)(2,1)S(1)}, bf16[64,8192]{1,0:T(8,128)(2,1)}, u32[]{:S(2)}, u32[]{:S(2)}) collective-permute-start(bf16[64,8192]{1,0:T(8,128)(2,1)S(1)} %get-tuple-element.73), channel_id=1, source_target_pairs={{4,8},{6,10},{8,4},{10,6},{5,9},{7,11},{9,5},{11,7},{20,24},{22,26... | collective-permute-start | bytes 3145736 | tf_op jit(solution)/shard_map/ppermute | solution.py:108
  3.4 27.1 %collective-permute-start.1 = (bf16[64,8192]{1,0:T(8,128)(2,1)S(1)}, bf16[64,8192]{1,0:T(8,128)(2,1)}, u32[]{:S(2)}, u32[]{:S(2)}) collective-permute-start(bf16[64,8192]{1,0:T(8,128)(2,1)S(1)} %get-tuple-element.73), channel_id=1, source_target_pairs={{0,2},{4,6},{8,10},{12,14},{2,0},{6,4},{10,8},{14,12},{1,3},{5,7},... | collective-permute-start | bytes 3145736 | tf_op jit(solution)/shard_map/ppermute | solution.py:108
  6.3 27.7 %collective-permute-start.2 = (bf16[64,8192]{1,0:T(8,128)(2,1)S(1)}, bf16[64,8192]{1,0:T(8,128)(2,1)}, u32[]{:S(2)}, u32[]{:S(2)}) collective-permute-start(bf16[64,8192]{1,0:T(8,128)(2,1)S(1)} %get-tuple-element.73), channel_id=1, source_target_pairs={{0,4},{2,6},{8,12},{10,14},{4,0},{6,2},{12,8},{14,10},{1,5},{3,7},... | collective-permute-start | bytes 3145736 | tf_op jit(solution)/shard_map/ppermute | solution.py:108
  9.8 46.9 %collective-permute-start.4 = (bf16[64,8192]{1,0:T(8,128)(2,1)S(1)}, bf16[64,8192]{1,0:T(8,128)(2,1)}, u32[]{:S(2)}, u32[]{:S(2)}) collective-permute-start(bf16[64,8192]{1,0:T(8,128)(2,1)S(1)} %get-tuple-element.71), channel_id=1, source_target_pairs={{0,2},{4,6},{8,10},{12,14},{2,0},{6,4},{10,8},{14,12},{1,3},{5,7},... | collective-permute-start | bytes 3145736 | tf_op jit(solution)/shard_map/ppermute | solution.py:108
  10.3 46.4 %collective-permute-start.5 = (bf16[64,8192]{1,0:T(8,128)(2,1)S(1)}, bf16[64,8192]{1,0:T(8,128)(2,1)}, u32[]{:S(2)}, u32[]{:S(2)}) collective-permute-start(bf16[64,8192]{1,0:T(8,128)(2,1)S(1)} %get-tuple-element.71), channel_id=1, source_target_pairs={{0,4},{2,6},{8,12},{10,14},{4,0},{6,2},{12,8},{14,10},{1,5},{3,7},... | collective-permute-start | bytes 3145736 | tf_op jit(solution)/shard_map/ppermute | solution.py:108
  16.1 2.2 copy-start
  22.4 16.0 %collective-permute-start.6 = (bf16[64,8192]{1,0:T(8,128)(2,1)S(1)}, bf16[64,8192]{1,0:T(8,128)(2,1)S(1)}, u32[]{:S(2)}, u32[]{:S(2)}) collective-permute-start(bf16[64,8192]{1,0:T(8,128)(2,1)S(1)} %get-tuple-element.140), channel_id=1, source_target_pairs={{0,1},{1,0},{2,3},{3,2},{4,5},{5,4},{6,7},{7,6},{8,9},{9,8},{10,11... | collective-permute-start | bytes 3145736 | tf_op jit(solution)/shard_map/ppermute | solution.py:112
  34.1 22.7 %collective-permute-start.3 = (bf16[64,8192]{1,0:T(8,128)(2,1)S(1)}, bf16[64,8192]{1,0:T(8,128)(2,1)}, u32[]{:S(2)}, u32[]{:S(2)}) collective-permute-start(bf16[64,8192]{1,0:T(8,128)(2,1)S(1)} %get-tuple-element.71), channel_id=1, source_target_pairs={{4,8},{6,10},{8,4},{10,6},{5,9},{7,11},{9,5},{11,7},{20,24},{22,26... | collective-permute-start | bytes 3145736 | tf_op jit(solution)/shard_map/ppermute | solution.py:108
  38.4 7.7 %copy-start.7 = (bf16[256,8192]{1,0:T(8,128)(2,1)}, bf16[256,8192]{1,0:T(8,128)(2,1)S(1)}, u32[]{:S(2)}) copy-start(bf16[256,8192]{1,0:T(8,128)(2,1)S(1)} %constant_dynamic-update-slice_fusion) | copy-start | bytes 12582916
  38.4 7.7 %copy-start.11 = (bf16[64,8192]{1,0:T(8,128)(2,1)}, bf16[64,8192]{1,0:T(8,128)(2,1)S(1)}, u32[]{:S(2)}) copy-start(bf16[64,8192]{1,0:T(8,128)(2,1)S(1)} %collective-permute-done.6) | copy-start | bytes 3145732
  44.8 34.1 %collective-permute-start.9 = (bf16[64,8192]{1,0:T(8,128)(2,1)}, bf16[64,8192]{1,0:T(8,128)(2,1)}, u32[]{:S(2)}, u32[]{:S(2)}) collective-permute-start(bf16[64,8192]{1,0:T(8,128)(2,1)} %collective-permute-done), channel_id=1, source_target_pairs={{4,0},{6,2},{8,12},{10,14},{5,1},{7,3},{9,13},{11,15},{20,16},{22,... | collective-permute-start | bytes 3145736 | tf_op jit(solution)/shard_map/ppermute | solution.py:108
  56.8 22.2 %collective-permute-start.7 = (bf16[64,8192]{1,0:T(8,128)(2,1)}, bf16[64,8192]{1,0:T(8,128)(2,1)S(1)}, u32[]{:S(2)}, u32[]{:S(2)}) collective-permute-start(bf16[64,8192]{1,0:T(8,128)(2,1)} %collective-permute-done.2), channel_id=1, source_target_pairs={{4,8},{6,10},{8,4},{10,6},{5,9},{7,11},{9,5},{11,7},{20,24},{22,26... | collective-permute-start | bytes 3145736 | tf_op jit(solution)/shard_map/ppermute | solution.py:108
  57.5 26.5 %collective-permute-start.8 = (bf16[64,8192]{1,0:T(8,128)(2,1)}, bf16[64,8192]{1,0:T(8,128)(2,1)}, u32[]{:S(2)}, u32[]{:S(2)}) collective-permute-start(bf16[64,8192]{1,0:T(8,128)(2,1)} %collective-permute-done.5), channel_id=1, source_target_pairs={{0,2},{4,6},{8,10},{12,14},{2,0},{6,4},{10,8},{14,12},{1,3},{5,7},... | collective-permute-start | bytes 3145736 | tf_op jit(solution)/shard_map/ppermute | solution.py:108
  58.7 49.5 %collective-permute-start.11 = (bf16[64,8192]{1,0:T(8,128)(2,1)}, bf16[64,8192]{1,0:T(8,128)(2,1)}, u32[]{:S(2)}, u32[]{:S(2)}) collective-permute-start(bf16[64,8192]{1,0:T(8,128)(2,1)} %collective-permute-done.2), channel_id=1, source_target_pairs={{0,2},{4,6},{8,10},{12,14},{2,0},{6,4},{10,8},{14,12},{1,3},{5,7},... | collective-permute-start | bytes 3145736 | tf_op jit(solution)/shard_map/ppermute | solution.py:108
  65.4 42.7 %collective-permute-start.12 = (bf16[64,8192]{1,0:T(8,128)(2,1)}, bf16[64,8192]{1,0:T(8,128)(2,1)}, u32[]{:S(2)}, u32[]{:S(2)}) collective-permute-start(bf16[64,8192]{1,0:T(8,128)(2,1)} %collective-permute-done.3), channel_id=1, source_target_pairs={{4,0},{6,2},{8,12},{10,14},{5,1},{7,3},{9,13},{11,15},{20,16},{22,... | collective-permute-start | bytes 3145736 | tf_op jit(solution)/shard_map/ppermute | solution.py:108
  86.3 42.6 %collective-permute-start.16 = (bf16[64,8192]{1,0:T(8,128)(2,1)}, bf16[64,8192]{1,0:T(8,128)(2,1)}, u32[]{:S(2)}, u32[]{:S(2)}) collective-permute-start(bf16[64,8192]{1,0:T(8,128)(2,1)} %broadcast_select_fusion.4), channel_id=1, source_target_pairs={{0,2},{4,6},{8,10},{12,14},{2,0},{6,4},{10,8},{14,12},{1,3},{5,7},... | collective-permute-start | bytes 3145736 | tf_op jit(solution)/shard_map/ppermute | solution.py:108
  92.1 16.0 %collective-permute-start.10 = (bf16[64,8192]{1,0:T(8,128)(2,1)}, bf16[64,8192]{1,0:T(8,128)(2,1)}, u32[]{:S(2)}, u32[]{:S(2)}) collective-permute-start(bf16[64,8192]{1,0:T(8,128)(2,1)} %collective-permute-done.5), channel_id=1, source_target_pairs={{4,8},{6,10},{8,4},{10,6},{5,9},{7,11},{9,5},{11,7},{20,24},{22,26... | collective-permute-start | bytes 3145736 | tf_op jit(solution)/shard_map/ppermute | solution.py:108
  93.8 35.1 %collective-permute-start.17 = (bf16[64,8192]{1,0:T(8,128)(2,1)S(1)}, bf16[64,8192]{1,0:T(8,128)(2,1)}, u32[]{:S(2)}, u32[]{:S(2)}) collective-permute-start(bf16[64,8192]{1,0:T(8,128)(2,1)S(1)} %collective-permute-done.7), channel_id=1, source_target_pairs={{4,0},{6,2},{8,12},{10,14},{5,1},{7,3},{9,13},{11,15},{20,16},{22,... | collective-permute-start | bytes 3145736 | tf_op jit(solution)/shard_map/ppermute | solution.py:108
  95.6 18.1 %copy-start.12 = (bf16[64,8192]{1,0:T(8,128)(2,1)S(1)}, bf16[64,8192]{1,0:T(8,128)(2,1)}, u32[]{:S(2)}) copy-start(bf16[64,8192]{1,0:T(8,128)(2,1)} %copy-done.11) | copy-start | bytes 3145732
  108.2 20.8 %collective-permute-start.15 = (bf16[64,8192]{1,0:T(8,128)(2,1)}, bf16[64,8192]{1,0:T(8,128)(2,1)}, u32[]{:S(2)}, u32[]{:S(2)}) collective-permute-start(bf16[64,8192]{1,0:T(8,128)(2,1)} %collective-permute-done.8), channel_id=1, source_target_pairs={{4,8},{6,10},{8,4},{10,6},{5,9},{7,11},{9,5},{11,7},{20,24},{22,26... | collective-permute-start | bytes 3145736 | tf_op jit(solution)/shard_map/ppermute | solution.py:108
  112.2 39.2 %collective-permute-start.13 = (bf16[64,8192]{1,0:T(8,128)(2,1)}, bf16[64,8192]{1,0:T(8,128)(2,1)}, u32[]{:S(2)}, u32[]{:S(2)}) collective-permute-start(bf16[64,8192]{1,0:T(8,128)(2,1)} %broadcast_select_fusion.3), channel_id=1, source_target_pairs={{0,2},{4,6},{8,10},{12,14},{2,0},{6,4},{10,8},{14,12},{1,3},{5,7},... | collective-permute-start | bytes 3145736 | tf_op jit(solution)/shard_map/ppermute | solution.py:108
  118.8 36.6 %collective-permute-start.14 = (bf16[64,8192]{1,0:T(8,128)(2,1)}, bf16[64,8192]{1,0:T(8,128)(2,1)}, u32[]{:S(2)}, u32[]{:S(2)}) collective-permute-start(bf16[64,8192]{1,0:T(8,128)(2,1)} %collective-permute-done.10), channel_id=1, source_target_pairs={{4,0},{6,2},{8,12},{10,14},{5,1},{7,3},{9,13},{11,15},{20,16},{22,... | collective-permute-start | bytes 3145736 | tf_op jit(solution)/shard_map/ppermute | solution.py:108
  131.2 51.5 %collective-permute-start.19 = (bf16[64,8192]{1,0:T(8,128)(2,1)}, bf16[64,8192]{1,0:T(8,128)(2,1)}, u32[]{:S(2)}, u32[]{:S(2)}) collective-permute-start(bf16[64,8192]{1,0:T(8,128)(2,1)} %broadcast_select_fusion.2), channel_id=1, source_target_pairs={{0,2},{4,6},{8,10},{12,14},{2,0},{6,4},{10,8},{14,12},{1,3},{5,7},... | collective-permute-start | bytes 3145736 | tf_op jit(solution)/shard_map/ppermute | solution.py:108
  136.8 46.0 %collective-permute-start.20 = (bf16[64,8192]{1,0:T(8,128)(2,1)}, bf16[64,8192]{1,0:T(8,128)(2,1)}, u32[]{:S(2)}, u32[]{:S(2)}) collective-permute-start(bf16[64,8192]{1,0:T(8,128)(2,1)} %collective-permute-done.15), channel_id=1, source_target_pairs={{4,0},{6,2},{8,12},{10,14},{5,1},{7,3},{9,13},{11,15},{20,16},{22,... | collective-permute-start | bytes 3145736 | tf_op jit(solution)/shard_map/ppermute | solution.py:108
  155.4 33.4 %all-to-all-start = ((bf16[16,64,512]{2,1,0:T(8,128)(2,1)}), bf16[16,64,512]{2,1,0:T(8,128)(2,1)S(1)}, u32[]{:S(2)}, u32[]{:S(2)}) async-start(bf16[16,64,512]{2,1,0:T(8,128)(2,1)} %bitcast.59), calls=%async_computation | async-start | bytes 2097152 | tf_op jit(solution)/shard_map/all_to_all | solution.py:332
  167.2 1.0 copy-start.4
  168.2 7.5 %copy-start.10 = (s32[1,16]{1,0:T(1,128)S(1)}, s32[1,16]{1,0:T(1,128)}, u32[]{:S(2)}) copy-start(s32[1,16]{1,0:T(1,128)} %constant.98) | copy-start | bytes 196
  173.7 9.1 %copy-start.6 = (bf16[4,2,64,64]{3,1,2,0:T(2,128)(2,1)}, bf16[4,2,64,64]{3,1,2,0:T(2,128)(2,1)S(1)}, u32[]{:S(2)}) copy-start(bf16[4,2,64,64]{3,1,2,0:T(2,128)(2,1)S(1)} %slice.320) | copy-start | bytes 196612
  173.7 9.1 %collective-permute-start.18 = (bf16[4,2,64,64]{3,1,2,0:T(2,128)(2,1)S(1)}, bf16[4,2,64,64]{3,1,2,0:T(2,128)(2,1)}, u32[]{:S(2)}, u32[]{:S(2)}) collective-permute-start(bf16[4,2,64,64]{3,1,2,0:T(2,128)(2,1)S(1)} %slice.320), channel_id=1, source_target_pairs={{0,2},{4,6},{8,10},{12,14},{2,0},{6,4},{10,8},{14,12},{1,3},{5,7},... | collective-permute-start | bytes 196616 | tf_op jit(solution)/shard_map/ppermute | solution.py:108
  189.9 32.3 %collective-permute-start.27 = (bf16[4,2,64,64]{3,1,2,0:T(2,128)(2,1)S(1)}, bf16[4,2,64,64]{3,1,2,0:T(2,128)(2,1)}, u32[]{:S(2)}, u32[]{:S(2)}) collective-permute-start(bf16[4,2,64,64]{3,1,2,0:T(2,128)(2,1)S(1)} %add.162), channel_id=1, source_target_pairs={{0,12},{2,14},{4,0},{6,2},{8,4},{10,6},{12,8},{14,10},{1,13},{3,15... | collective-permute-start | bytes 196616 | tf_op jit(solution)/shard_map/ppermute | solution.py:108
  193.1 30.4 %collective-permute-start.26 = (bf16[4,2,64,64]{3,1,2,0:T(2,128)(2,1)S(1)}, bf16[4,2,64,64]{3,1,2,0:T(2,128)(2,1)}, u32[]{:S(2)}, u32[]{:S(2)}) collective-permute-start(bf16[4,2,64,64]{3,1,2,0:T(2,128)(2,1)S(1)} %add.162), channel_id=1, source_target_pairs={{0,8},{2,10},{4,12},{6,14},{8,0},{10,2},{12,4},{14,6},{1,9},{3,11}... | collective-permute-start | bytes 196616 | tf_op jit(solution)/shard_map/ppermute | solution.py:108
  195.1 28.7 %collective-permute-start.25 = (bf16[4,2,64,64]{3,1,2,0:T(2,128)(2,1)S(1)}, bf16[4,2,64,64]{3,1,2,0:T(2,128)(2,1)}, u32[]{:S(2)}, u32[]{:S(2)}) collective-permute-start(bf16[4,2,64,64]{3,1,2,0:T(2,128)(2,1)S(1)} %add.162), channel_id=1, source_target_pairs={{0,4},{2,6},{4,8},{6,10},{8,12},{10,14},{12,0},{14,2},{1,5},{3,7},... | collective-permute-start | bytes 196616 | tf_op jit(solution)/shard_map/ppermute | solution.py:108
  198.3 2.7 %copy-start.5 = (bf16[64,8192]{1,0:T(8,128)(2,1)}, bf16[64,8192]{1,0:T(8,128)(2,1)S(1)}, u32[]{:S(2)}) copy-start(bf16[64,8192]{1,0:T(8,128)(2,1)S(1)} %broadcast_select_fusion) | copy-start | bytes 3145732
  204.6 14.9 %collective-permute-start.21 = (bf16[4,2,64,64]{3,1,2,0:T(2,128)(2,1)S(1)}, bf16[4,2,64,64]{3,1,2,0:T(2,128)(2,1)S(1)}, u32[]{:S(2)}, u32[]{:S(2)}) collective-permute-start(bf16[4,2,64,64]{3,1,2,0:T(2,128)(2,1)S(1)} %pad_maximum_fusion.1), channel_id=1, source_target_pairs={{0,2},{4,6},{8,10},{12,14},{2,0},{6,4},{10,8},{14,12},{1,3},{5,7},... | collective-permute-start | bytes 196616 | tf_op jit(solution)/shard_map/ppermute | solution.py:108
  205.3 29.6 %copy-start.1 = (f32[256,1024]{1,0:T(8,128)S(1)}, f32[256,1024]{1,0:T(8,128)}, u32[]{:S(2)}) copy-start(f32[256,1024]{1,0:T(8,128)} %fusion.refs_1_) | copy-start | bytes 3145732
  205.4 29.5 %collective-permute-start.28 = (bf16[8,64,512]{2,1,0:T(8,128)(2,1)S(1)}, bf16[8,64,512]{2,1,0:T(8,128)(2,1)S(1)}, u32[]{:S(2)}, u32[]{:S(2)}) collective-permute-start(bf16[8,64,512]{2,1,0:T(8,128)(2,1)S(1)} %take.1.refs_5_), channel_id=1, source_target_pairs={{0,16},{16,0},{1,17},{17,1},{2,18},{18,2},{3,19},{19,3},{4,20},{20... | collective-permute-start | bytes 1572872 | tf_op jit(solution)/shard_map/ppermute | solution.py:112
  219.7 8.4 %collective-permute-start.22 = (bf16[4,2,64,64]{3,1,2,0:T(2,128)(2,1)S(1)}, bf16[4,2,64,64]{3,1,2,0:T(2,128)(2,1)S(1)}, u32[]{:S(2)}, u32[]{:S(2)}) collective-permute-start(bf16[4,2,64,64]{3,1,2,0:T(2,128)(2,1)S(1)} %fusion.107), channel_id=1, source_target_pairs={{0,4},{2,6},{4,8},{6,10},{8,12},{10,14},{12,0},{14,2},{1,5},{3,7},... | collective-permute-start | bytes 196616 | tf_op jit(solution)/shard_map/ppermute | solution.py:108
  222.2 6.4 %collective-permute-start.24 = (bf16[4,2,64,64]{3,1,2,0:T(2,128)(2,1)S(1)}, bf16[4,2,64,64]{3,1,2,0:T(2,128)(2,1)S(1)}, u32[]{:S(2)}, u32[]{:S(2)}) collective-permute-start(bf16[4,2,64,64]{3,1,2,0:T(2,128)(2,1)S(1)} %fusion.107), channel_id=1, source_target_pairs={{0,12},{2,14},{4,0},{6,2},{8,4},{10,6},{12,8},{14,10},{1,13},{3,15... | collective-permute-start | bytes 196616 | tf_op jit(solution)/shard_map/ppermute | solution.py:108
  223.6 10.6 %collective-permute-start.23 = (bf16[4,2,64,64]{3,1,2,0:T(2,128)(2,1)S(1)}, bf16[4,2,64,64]{3,1,2,0:T(2,128)(2,1)S(1)}, u32[]{:S(2)}, u32[]{:S(2)}) collective-permute-start(bf16[4,2,64,64]{3,1,2,0:T(2,128)(2,1)S(1)} %fusion.107), channel_id=1, source_target_pairs={{0,8},{2,10},{4,12},{6,14},{8,0},{10,2},{12,4},{14,6},{1,9},{3,11}... | collective-permute-start | bytes 196616 | tf_op jit(solution)/shard_map/ppermute | solution.py:108
  234.9 1.2 copy-start.2
  236.1 1.2 copy-start.3

commit v6 on v1

--- a/solution.py
+++ b/solution.py
@@ -1,6 +1,11 @@
+import functools
+
 import jax
 import jax.numpy as jnp
+import numpy as np
 from jax import lax
+from jax.experimental import pallas as pl
+from jax.experimental.pallas import tpu as pltpu
 from jax.sharding import PartitionSpec as P
 
 BLOCK = 128
@@ -90,92 +95,312 @@
     return pairs + [(b, a) for a, b in pairs]
 
 
-ACROSS = both_ways([(0, 1), (2, 3), (4, 5), (6, 7)])
-NEAR = both_ways([(0, 2), (1, 3), (4, 6), (5, 7)])
-FAR = both_ways([(0, 4), (1, 5), (2, 6), (3, 7)])
-CHUNKS = 4
+ACROSS = [(i, i ^ 1) for i in range(8)]
+ALONG = {"x%d" % d: [(i, i ^ (2 * d)) for i in range(8)] for d in (1, 2, 3)}
+HALF = BLOCK // 2
+DEPTH = 1024
+VMEM_LIMIT = 16 * 1024 * 1024
+
+
+def send(value, pairs):
+    return lax.ppermute(value, "tensor", pairs)
 
 
 def swap(value, axis):
     return lax.ppermute(value, axis, [(0, 1), (1, 0)])
+
+
+def settings():
+    return dict(
+        compiler_params=pltpu.CompilerParams(vmem_limit_bytes=VMEM_LIMIT),
+        cost_estimate=pl.CostEstimate(flops=1, bytes_accessed=1, transcendentals=0),
+    )
+
+
+def in_vmem(count):
+    return [pl.BlockSpec(memory_space=pltpu.VMEM)] * count
+
+
+def pin_kernel(weight, own, swapped, out, sem):
+    columns = weight.shape[1]
+    copy = pltpu.make_async_copy(weight, out.at[:, pl.ds(0, columns)], sem)
+    copy.start()
+    for at in range(0, weight.shape[0], DEPTH):
+        cut = pl.ds(at, DEPTH)
+        out[cut, columns:] = jnp.concatenate([own[:, cut], swapped[:, cut]], axis=0).T
+    copy.wait()
+
+
+def pin_call(weight, own, swapped):
+    width, columns = weight.shape
+    return pl.pallas_call(
+        pin_kernel,
+        in_specs=[pl.BlockSpec(memory_space=pltpu.HBM)] + in_vmem(2),
+        out_specs=in_vmem(1)[0],
+        out_shape=pltpu.VMEM((width, columns + 2 * own.shape[0]), weight.dtype),
+        scratch_shapes=[pltpu.SemaphoreType.DMA],
+        name="pin",
+        **settings(),
+    )(pltpu.with_memory_space_constraint(weight, pltpu.HBM), own, swapped)
+
+
+def rows_kernel(first, table, weights, *refs):
+    *pieces, base, small = refs
+    columns = base.shape[1]
+    total = None
+    for at in range(0, weights.shape[0], DEPTH):
+        cut = pl.ds(at, DEPTH)
+        x = [p[:, cut] for p in pieces]
+        x = x[0] if len(x) == 1 else jnp.concatenate(x, axis=0)
+        part = jnp.dot(x, weights[cut, :], preferred_element_type=jnp.float32)
+        total = part if total is None else total + part
+    base[...] = total[:, :columns]
+    lane = lax.broadcasted_iota(jnp.int32, small.shape, 1)
+    row = lax.broadcasted_iota(jnp.int32, small.shape, 0)
+    use = jnp.where(
+        row < HALF,
+        jnp.where(lane < 64, table[0, first], table[1, first]),
+        jnp.where(lane < 64, table[0, first + 1], table[1, first + 1]),
+    )
+    small[...] = jnp.where(use > 0, total[:, columns:], 0.0).astype(jnp.bfloat16)
+
+
+def rows_call(first, table, weights, pieces):
+    columns = weights.shape[1] - 128
+    operands = [pltpu.with_memory_space_constraint(weights, pltpu.VMEM)] + pieces
+    return pl.pallas_call(
+        functools.partial(rows_kernel, first),
+        in_specs=[pl.BlockSpec(memory_space=pltpu.SMEM)] + in_vmem(len(operands)),
+        out_specs=in_vmem(2),
+        out_shape=[
+            jax.ShapeDtypeStruct((BLOCK, columns), jnp.float32),
+            jax.ShapeDtypeStruct((BLOCK, 128), jnp.bfloat16),
+        ],
+        name="rows",
+        **settings(),
+    )(table, *operands)
+
+
+def pack_kernel(table, up, out):
+    part = out.shape[3]
+    for t in range(8):
+        at = pl.multiple_of((2 * t + table[2]) * part, part)
+        out[t, 0] = up[0, :, pl.ds(at, part)]
+
+
+def pack_call(table, up_maps):
+    _, rank, width = up_maps.shape
+    part = width // 16
+    return pl.pallas_call(
+        pack_kernel,
+        grid_spec=pltpu.PrefetchScalarGridSpec(
+            num_scalar_prefetch=1,
+            grid=(2,),
+            in_specs=[pl.BlockSpec((1, rank, width), lambda s, t: (t[s], 0, 0))],
+            out_specs=pl.BlockSpec((8, 1, rank, part), lambda s, t: (0, s, 0, 0)),
+        ),
+        out_shape=jax.ShapeDtypeStruct((8, 2, rank, part), jnp.bfloat16),
+        name="pack",
+        **settings(),
+    )(table, up_maps)
+
+
+def take_kernel(table, got, out):
+    out[...] = got[...]
+
+
+def take_call(table, got):
+    _, rank, part = got.shape
+    return pl.pallas_call(
+        take_kernel,
+        grid_spec=pltpu.PrefetchScalarGridSpec(
+            num_scalar_prefetch=1,
+            grid=(8,),
+            in_specs=[pl.BlockSpec((1, rank, part), lambda b, t: (t[b], 0, 0))],
+            out_specs=pl.BlockSpec((1, rank, part), lambda b, t: (b, 0, 0)),
+        ),
+        out_shape=jax.ShapeDtypeStruct((8, rank, part), jnp.bfloat16),
+        name="take",
+        **settings(),
+    )(table, got)
+
+
+def finish_kernel(sources, table, *refs):
+    bases = refs[: max(sources) + 1]
+    shrunk, up_mine, up_other, out = refs[len(bases)], refs[len(bases) + 1], refs[len(bases) + 2], refs[-1]
+    at = pl.program_id(0)
+    part = up_mine.shape[2]
+    both = shrunk[...].astype(jnp.float32)
+    both = (both[:, :64] + both[:, 64:]).astype(jnp.bfloat16)
+    group = table[8]
+    for g, base in enumerate(bases):
+        steps = [i for i, source in enumerate(sources) if source == g]
+
+        @pl.when((at >= steps[0]) & (at <= steps[-1]))
+        def _():
+            for up, side in ((up_mine, group), (up_other, 1 - group)):
+                cut = pl.ds(pl.multiple_of(side * part, part), part)
+                grown = jnp.dot(both, up[0], preferred_element_type=jnp.float32)
+                out[:, cut] = (base[:, cut] + 0.5 * grown).astype(out.dtype)
+
+
+def finish_call(table, half, bases, shrunk, up_mine, up_other, into):
+    columns = bases[0].shape[1]
+    _, rank, part = up_mine.shape
+    sources = [0, 1, 2, 2, 3, 3, 4, 4]
+
+    def base_spec(g):
+        if g < 2:
+            return pl.BlockSpec((HALF, columns), lambda i, t: (half, 0))
+        return pl.BlockSpec((HALF, columns), lambda i, t: (jnp.clip(i - 2 * g + 2, 0, 1), 0))
+
+    up = pl.BlockSpec((1, rank, part), lambda i, t: (t[i], 0, 0))
+    specs = [base_spec(g) for g in range(5)]
+    specs += [pl.BlockSpec((HALF, 2 * rank), lambda i, t: (t[i], 0)), up, up]
+    operands = [*bases, shrunk, up_mine, up_other]
+    aliases = {}
+    if into is not None:
+        aliases = {1 + len(operands): 0}
+        operands.append(into)
+        specs.append(pl.BlockSpec(memory_space=pltpu.HBM))
+    return pl.pallas_call(
+        functools.partial(finish_kernel, sources),
+        grid_spec=pltpu.PrefetchScalarGridSpec(
+            num_scalar_prefetch=1,
+            grid=(8,),
+            in_specs=specs,
+            out_specs=pl.BlockSpec((HALF, columns), lambda i, t: (2 * t[i] + half, 0)),
+        ),
+        out_shape=jax.ShapeDtypeStruct((8 * BLOCK, columns), jnp.bfloat16),
+        input_output_aliases=aliases,
+        name="finish",
+        **settings(),
+    )(table, *operands)
+
+
+CUTS = {"": (0, 128), "0": (0, 64), "1": (64, 128), "1a": (64, 96), "1b": (96, 128)}
+GROUPS = [
+    [("own", "")],
+    [("own_y", "")],
+    [("x1", "0"), ("x2", "0")],
+    [("x1", "1"), ("x2", "1")],
+    [("x1_y", "0"), ("x2_y", "0")],
+    [("x1_y", "1"), ("x2_y", "1")],
+    [("x3", "0"), ("x3_y", "0")],
+    [("x3", "1a"), ("x3", "1b"), ("x3_y", "1a"), ("x3_y", "1b")],
+]
+HALVES = [
+    ("own", 0), ("own", 1), ("own_y", 0), ("own_y", 1), ("x1", 0), ("x2", 0), ("x1", 1), ("x2", 1),
+    ("x1_y", 0), ("x2_y", 0), ("x1_y", 1), ("x2_y", 1), ("x3", 0), ("x3_y", 0), ("x3", 1), ("x3_y", 1),
+]
+EVENTS = [
+    ([], [("x1", "0"), ("x2", "0")], [("own", "")], []),
+    ([("x1", "0")], [("x2", "1")], [("x1", "0")], [0]),
+    ([("x2", "0")], [("x1", "1")], [("x2", "0")], [2]),
+    ([("own_y", "")], [], [], [1]),
+    ([("x2", "1")], [("x3", "0")], [("x2", "1")], []),
+    ([("x1_y", "0"), ("x2_y", "0"), ("x1", "1")], [("x3", "1a")], [("x1", "1")], [3, 4]),
+    ([("x3", "0"), ("x2_y", "1")], [("x3", "1b")], [("x3", "0")], []),
+    ([("x1_y", "1"), ("x3", "1a")], [], [("x3", "1a")], [5]),
+    ([("x3", "1b")], [], [("x3", "1b")], []),
+    ([("x3_y", "0")], [], [], [6]),
+    ([("x3_y", "1a"), ("x3_y", "1b")], [], [], [7]),
+]
 
 
 def chain_body(
     tokens, query_weight, adapter_down_maps, adapter_up_maps, adapter_home_slot, adapter_per_block
 ):
     me = lax.axis_index("tensor")
+    z, y = me // 2, me % 2
     store = lax.axis_index("store")
     group = lax.axis_index("groups")
     myself = me * 2 + store
     held, rank, width = adapter_down_maps.shape
     columns = query_weight.shape[1]
-    part = columns // 2
     rows = tokens[0]
-    step = BLOCK // CHUNKS
+    have = {("own", name): rows[slice(*cut)] for name, cut in CUTS.items()}
+    flight = {}
+
+    def issue(along, across):
+        for name, piece in along:
+            flight[name, piece] = send(have["own", piece], ALONG[name])
+        for name, piece in across:
+            flight[name + "_y", piece] = send(have[name, piece], ACROSS)
+
+    issue(*EVENTS[0][1:3])
 
     store_slots = find_slots(adapter_home_slot, adapter_per_block)
     owner = store_slots // held
     inside = store_slots % held
     picked = jnp.max(jnp.where(owner == myself, inside, 0), axis=1)
-    owner_row = lax.dynamic_index_in_dim(owner, store, 0, keepdims=False)
-
-    gathered = [
-        lax.all_gather(rows[c * step : (c + 1) * step], "tensor", axis=0) for c in range(CHUNKS)
-    ]
-
-    def pick(maps, index):
-        local = lax.dynamic_index_in_dim(picked, index, 0, keepdims=False)
-        return lax.dynamic_index_in_dim(maps, local, 0, keepdims=False)
-
-    down_own = pick(adapter_down_maps, store)
-    down_swapped = swap(pick(adapter_down_maps, 1 - store), "store")
-    candidates = jnp.concatenate([down_own, down_swapped])
-    use_own = (owner_row == myself)[:, None, None]
-    use_swapped = (owner_row == me * 2 + 1 - store)[:, None, None]
-
-    def shrink(chunk):
-        value = lax.dot_general(
-            candidates,
-            chunk.reshape(8 * step, width),
-            (((1,), (1,)), ((), ())),
-            preferred_element_type=jnp.float32,
+    owner_row = lax.dynamic_index_in_dim(owner, store, 0, keepdims=False).astype(jnp.int32)
+    pick_own = lax.dynamic_index_in_dim(picked, store, 0, keepdims=False)
+    pick_lent = lax.dynamic_index_in_dim(picked, 1 - store, 0, keepdims=False)
+
+    down_own = lax.dynamic_index_in_dim(adapter_down_maps, pick_own, 0, keepdims=False)
+    down_lent = lax.dynamic_index_in_dim(adapter_down_maps, pick_lent, 0, keepdims=False)
+    weights = pin_call(query_weight, down_own, swap(down_lent, "store"))
+    up_sent = pack_call(jnp.concatenate([picked, group[None]]).astype(jnp.int32), adapter_up_maps)
+
+    blocks = jnp.stack(
+        [
+            (z if name[0] == "o" else z ^ int(name[1])) * 2 + (1 - y if name.endswith("_y") else y)
+            for name, _ in HALVES
+        ]
+    ).astype(jnp.int32)
+    hit = blocks[:, None] == jnp.arange(8, dtype=jnp.int32)[None, :]
+    owners = jnp.sum(jnp.where(hit, owner_row[None, :], 0), axis=1)
+    table = jnp.stack([owners == myself, owners == me * 2 + 1 - store]).astype(jnp.int32)
+
+    bases = [None] * 8
+    shrunk = [jnp.zeros((8, HALF, 2 * rank), jnp.bfloat16) for _ in range(2)]
+    extra = {"up": up_sent}
+    for at, (waits, along, across, groups) in enumerate(EVENTS[1:], 1):
+        got = {key: flight.pop(key) for key in waits}
+        if at >= len(EVENTS) - 2:
+            extra.update(flight.pop("late"))
+        got, have, bases, shrunk, extra = lax.optimization_barrier(
+            (got, have, bases, shrunk, extra)
         )
-        value = value.reshape(2, rank, 8, step).transpose(0, 2, 1, 3)
-        value = jnp.where(use_own, value[0], jnp.where(use_swapped, value[1], 0))
-        value = value.astype(jnp.bfloat16)
-        for pairs in (ACROSS, NEAR, FAR):
-            value = value + lax.ppermute(value, "tensor", pairs)
-        return value
-
-    def columns_of(up):
-        halves = up.reshape(rank, 8, 2, part)
-        half = lax.dynamic_index_in_dim(halves, group, 2, keepdims=False)
-        return half.transpose(1, 0, 2)
-
-    up_sent = jnp.stack(
-        [columns_of(pick(adapter_up_maps, 0)), columns_of(pick(adapter_up_maps, 1))], axis=1
-    )
-    up_got = lax.all_to_all(
-        up_sent.reshape(16, rank, part), ("tensor", "store"), split_axis=0, concat_axis=0, tiled=True
-    )
-    up_half = jnp.stack(
-        [lax.dynamic_index_in_dim(up_got, owner_row[b], 0, keepdims=False) for b in range(8)]
-    )
-    up_other = swap(up_half, "groups")
-    up = jnp.concatenate(
-        [jnp.where(group == 0, up_half, up_other), jnp.where(group == 0, up_other, up_half)], axis=2
-    )
-
-    outputs = []
-    for chunk in gathered:
-        base = jnp.dot(
-            chunk.reshape(8 * step, width), query_weight, preferred_element_type=jnp.float32
+        have.update({key: got[key] for key in waits})
+        issue(along, across)
+        if at == 6:
+            sent = extra.pop("up").reshape(16, rank, -1)
+            flight["late"] = {
+                "up": lax.all_to_all(
+                    sent, ("tensor", "store"), split_axis=0, concat_axis=0, tiled=True
+                )
+            }
+        for g in groups:
+            base, small = rows_call(2 * g, table, weights, [have[key] for key in GROUPS[g]])
+            bases[g] = base
+            for i in range(2):
+                half = HALVES[2 * g + i][1]
+                shrunk[half] = lax.dynamic_update_slice(
+                    shrunk[half], small[None, i * HALF : (i + 1) * HALF], (blocks[2 * g + i], 0, 0)
+                )
+        if at == len(EVENTS) - 2:
+            flight["late"] = {"first": send(shrunk[0], ACROSS)}
+
+    up_mine = take_call(owner_row, extra["up"])
+    up_other = swap(up_mine, "groups")
+
+    def total(value):
+        arrived = [send(value, pairs) for pairs in ALONG.values()]
+        return (value + arrived[0] + arrived[1] + arrived[2]).reshape(8 * HALF, 2 * rank)
+
+    first = total(shrunk[0] + extra["first"])
+    second = total(shrunk[1] + send(shrunk[1], ACROSS))
+    query = None
+    for half, value in enumerate((first, second)):
+        chosen = [0, 1] + [g for g in range(2, 8) if HALVES[2 * g][1] == half]
+        places = [2 * g + half for g in (0, 1)] + [2 * g + i for g in chosen[2:] for i in range(2)]
+        order = jnp.concatenate([blocks[np.array(places)], group[None]]).astype(jnp.int32)
+        query = finish_call(
+            order, half, [bases[g] for g in chosen], value, up_mine, up_other, query
         )
-        grown = jnp.einsum("brn,brf->bnf", shrink(chunk), up, preferred_element_type=jnp.float32)
-        value = base.reshape(8, step, columns) + 0.5 * grown
-        outputs.append(value.astype(jnp.bfloat16))
-    query = jnp.concatenate(outputs, axis=1)
-    return query.reshape(1, 8 * BLOCK, columns)
+    return query[None]
 
 
 def body(tokens, *rest):

time: 382 us -> 293 us (0.77)
  waiting for transfers between devices: 259 us -> 128 us
  Pallas kernels: 0 us -> 52.7 us
  matrix products: 44.3 us -> 0 us
  local copies, waits for them, and re-layouts: 13.9 us -> 46.7 us
  between operations: 35.7 us -> 4.17 us
  starting transfers between devices: 24.1 us -> 55.4 us
    all_gather x4 -> x0, waiting for transfers between devices: 231 us -> none  [chain_body(): lax.all_gather(rows[c * step:(c + 1) * step], 'tensor', axis=0)]
    ppermute x12 -> x23, waiting for transfers between devices: 3.8 us -> 128 us  [send(): return lax.ppermute(value, 'tensor', pairs)]
    pallas_call x0 -> x13, Pallas kernels: none -> 52.7 us  [the longest x8 34.5 us: rows_call(): pl.pallas_call(functools.partial(rows_kernel, first), in_specs=[pl.BlockS...]
    dot_general x12 -> x0, matrix products: 44.3 us -> none  [the longest x4 29.3 us: chain_body(): jnp.dot(chunk.reshape(8 * step, width), query_weight, preferred_element_t...]
    unnamed x21 -> x47, local copies, waits for them, and re-layouts: 0.56 us -> 36.6 us
    ppermute x12 -> x23, starting transfers between devices: 14.6 us -> 50.2 us  [send(): return lax.ppermute(value, 'tensor', pairs)]
    all_to_all x1, waiting for transfers between devices: 11.6 us -> 0.01 us  [chain_body(): lax.all_to_all(sent, ('tensor', 'store'), split_axis=0, concat_axis=0, ti...]
    ppermute x2, waiting for transfers between devices: 11.5 us -> 0.01 us  [swap(): return lax.ppermute(value, axis, [(0, 1), (1, 0)])]
  transfers between devices with their start and end apart: 19 -> 26, of which waited for: 9 -> 10; matrix products, arithmetic and copies ran while one was open for 14% -> 4% of each run, Pallas kernels for 0% -> 15%
where the time goes in v6:
time: 293 us; the launch traced here: 292 us
  waiting for transfers between devices  128 us (44%)
  starting transfers between devices  55.4 us (19%)
  Pallas kernels  52.7 us (18%)
  local copies, waits for them, and re-layouts  46.7 us (16%)
  other arithmetic  5.5 us (2%)
  between operations  4.17 us (1%)
    ppermute x23, waiting for transfers between devices, send(): return lax.ppermute(value, 'tensor', pairs)  128 us
    ppermute x23, starting transfers between devices, send(): return lax.ppermute(value, 'tensor', pairs)  50.2 us
    unnamed x47, local copies, waits for them, and re-layouts  36.6 us
    pallas_call x8, Pallas kernels, rows_call(): pl.pallas_call(functools.partial(rows_kernel, first), in_specs=[pl.BlockS...  34.5 us
    pallas_call x2, Pallas kernels, finish_call(): pl.pallas_call(functools.partial(finish_kernel, sources), grid_spec=pltpu...  8.91 us
    pallas_call x1, Pallas kernels, pin_call(): pl.pallas_call(pin_kernel, in_specs=[pl.BlockSpec(memory_space=pltpu.HBM)...  7 us
  transfers between devices with their start and end apart: 26, of which 10 were waited for; matrix products, arithmetic and copies ran while one was open for 4% of the time, Pallas kernels for 15%

profile of v6, /device:TPU:0, one launch (start us, length us, event | category | flops | bytes accessed | tf_op | source)
XLA Modules:
  0.0 292.2 jit_solution(9234569499819796467)
XLA Ops:
  0.0 3.1 %slice_bitcast_fusion = (bf16[64,8192]{1,0:T(8,128)(2,1)}, bf16[64,8192]{1,0:T(8,128)(2,1)}) fusion(bf16[1,128,8192]{2,1,0:T(8,128)(2,1)} %param.10), kind=kLoop, calls=%fused_computation.4 | loop fusion | bytes 4194304 | tf_op jit(solution)/shard_map/slice | solution.py:322
  3.1 3.0 %collective-permute-start.1 = (bf16[64,8192]{1,0:T(8,128)(2,1)}, bf16[64,8192]{1,0:T(8,128)(2,1)}, u32[]{:S(2)}, u32[]{:S(2)}) collective-permute-start(bf16[64,8192]{1,0:T(8,128)(2,1)} %get-tuple-element.166), channel_id=1, source_target_pairs={{0,4},{2,6},{4,0},{6,2},{8,12},{10,14},{12,8},{14,10},{1,5},{3,7},... | collective-permute-start | bytes 3145736 | tf_op jit(solution)/shard_map/ppermute | solution.py:106
  6.1 2.6 collective-permute-start
  13.5 2.8 dynamic-slice_bitcast_fusion
  16.4 1.5 collective-permute-start.7
  19.0 2.2 copy-done.6
  21.2 1.6 pack.1
  23.0 28.9 %collective-permute-done.1.refs_0_ = bf16[64,8192]{1,0:T(8,128)(2,1)} collective-permute-done((bf16[64,8192]{1,0:T(8,128)(2,1)}, bf16[64,8192]{1,0:T(8,128)(2,1)}, u32[]{:S(2)}, u32[]{:S(2)}) %collective-permute-start.1) | collective-permute-done | bytes 1048608 | tf_op jit(solution)/shard_map/ppermute | solution.py:106
  52.7 1.6 collective-permute-start.4
  54.3 7.0 %pin.1.weights = bf16[8192,1152]{1,0:T(8,128)(2,1)S(1)} custom-call(bf16[8192,1024]{1,0:T(8,128)(2,1)} %weight.1, bf16[64,8192]{1,0:T(8,128)(2,1)S(1)} %get-tuple-element.262.own, bf16[64,8192]{1,0:T(8,128)(2,1)} %collective-permute-done.2.swapped), custom_call_target="tpu_custom_call" | custom-call | flops 1 | bytes 1 | tf_op jit(solution)/shard_map/pin/pallas_call | solution.py:136
  61.3 3.5 %rows.8 = (f32[128,1024]{1,0:T(8,128)S(1)}, bf16[128,128]{1,0:T(8,128)(2,1)S(1)}) custom-call(s32[2,16]{1,0:T(2,128)S(1)} %add_convert_fusion.table, bf16[8192,1152]{1,0:T(8,128)(2,1)S(1)} %pin.1.weights, bf16[128,8192]{1,0:T(8,128)(2,1)S(1)} %bitcast.67), custom_call_target="tpu_custom_call" | custom-call | flops 1 | bytes 1 | tf_op jit(solution)/shard_map/rows/pallas_call | solution.py:171
  64.9 10.6 %collective-permute-start.3 = (bf16[64,8192]{1,0:T(8,128)(2,1)}, bf16[64,8192]{1,0:T(8,128)(2,1)}, u32[]{:S(2)}, u32[]{:S(2)}) collective-permute-start(bf16[64,8192]{1,0:T(8,128)(2,1)} %get-tuple-element.143), channel_id=1, source_target_pairs={{0,4},{2,6},{4,0},{6,2},{8,12},{10,14},{12,8},{14,10},{1,5},{3,7},... | collective-permute-start | bytes 3145736 | tf_op jit(solution)/shard_map/ppermute | solution.py:106
  75.5 1.5 collective-permute-start.5
  77.0 4.5 %rows.9 = (f32[128,1024]{1,0:T(8,128)S(1)}, bf16[128,128]{1,0:T(8,128)(2,1)S(1)}) custom-call(s32[2,16]{1,0:T(2,128)S(1)} %add_convert_fusion.table, bf16[8192,1152]{1,0:T(8,128)(2,1)S(1)} %pin.1.weights, bf16[64,8192]{1,0:T(8,128)(2,1)} %collective-permute-done.1.refs_0_, bf16[64,8192]{1,0:T(8,128)(2,1)} %collective-permute-done.refs_1_), custom_call_target="tpu_custom_call" | custom-call | flops 1 | bytes 1 | tf_op jit(solution)/shard_map/rows/pallas_call | solution.py:171
  81.5 4.6 %rows.10 = (f32[128,1024]{1,0:T(8,128)S(1)}, bf16[128,128]{1,0:T(8,128)(2,1)S(1)}) custom-call(s32[2,16]{1,0:T(2,128)S(1)} %add_convert_fusion.table, bf16[8192,1152]{1,0:T(8,128)(2,1)S(1)} %pin.1.weights, bf16[128,8192]{1,0:T(8,128)(2,1)} %collective-permute-done.7.refs_0_), custom_call_target="tpu_custom_call" | custom-call | flops 1 | bytes 1 | tf_op jit(solution)/shard_map/rows/pallas_call | solution.py:171
  86.1 13.6 %collective-permute-done.6.refs_1_ = bf16[64,8192]{1,0:T(8,128)(2,1)} collective-permute-done((bf16[64,8192]{1,0:T(8,128)(2,1)}, bf16[64,8192]{1,0:T(8,128)(2,1)}, u32[]{:S(2)}, u32[]{:S(2)}) %collective-permute-start.6) | collective-permute-done | bytes 1048608 | tf_op jit(solution)/shard_map/ppermute | solution.py:106
  99.8 1.5 collective-permute-start.10
  101.3 2.2 collective-permute-start.11
  103.5 30.9 %collective-permute-done.3.refs_0_ = bf16[64,8192]{1,0:T(8,128)(2,1)} collective-permute-done((bf16[64,8192]{1,0:T(8,128)(2,1)}, bf16[64,8192]{1,0:T(8,128)(2,1)}, u32[]{:S(2)}, u32[]{:S(2)}) %collective-permute-start.3) | collective-permute-done | bytes 1048608 | tf_op jit(solution)/shard_map/ppermute | solution.py:106
  134.4 6.4 %copy-done.1 = bf16[8192,1152]{1,0:T(8,128)(2,1)S(1)} copy-done((bf16[8192,1152]{1,0:T(8,128)(2,1)S(1)}, bf16[8192,1152]{1,0:T(8,128)(2,1)}, u32[]{:S(2)}) %copy-start.1) | copy-done | bytes 18874392
  140.8 4.4 %rows.12 = (f32[128,1024]{1,0:T(8,128)S(1)}, bf16[128,128]{1,0:T(8,128)(2,1)S(1)}) custom-call(s32[2,16]{1,0:T(2,128)S(1)} %add_convert_fusion.table, bf16[8192,1152]{1,0:T(8,128)(2,1)S(1)} %copy-done.1, bf16[64,8192]{1,0:T(8,128)(2,1)} %collective-permute-done.4.refs_0_, bf16[64,8192]{1,0:T(8,128)(2,1)} %collective-permute-done.5.refs_1_), custom_call_target="tpu_custom_call" | custom-call | flops 1 | bytes 1 | tf_op jit(solution)/shard_map/rows/pallas_call | solution.py:171
  146.1 4.6 %rows.11 = (f32[128,1024]{1,0:T(8,128)S(1)}, bf16[128,128]{1,0:T(8,128)(2,1)S(1)}) custom-call(s32[2,16]{1,0:T(2,128)S(1)} %add_convert_fusion.table, bf16[8192,1152]{1,0:T(8,128)(2,1)S(1)} %copy-done.1, bf16[64,8192]{1,0:T(8,128)(2,1)} %collective-permute-done.3.refs_0_, bf16[64,8192]{1,0:T(8,128)(2,1)} %collective-permute-done.6.refs_1_), custom_call_target="tpu_custom_call" | custom-call | flops 1 | bytes 1 | tf_op jit(solution)/shard_map/rows/pallas_call | solution.py:171
  152.6 3.7 %all-to-all-start = ((bf16[16,64,512]{2,1,0:T(8,128)(2,1)}), bf16[16,64,512]{2,1,0:T(8,128)(2,1)S(1)}, u32[]{:S(2)}, u32[]{:S(2)}) async-start(bf16[16,64,512]{2,1,0:T(8,128)(2,1)} %bitcast.33), calls=%async_computation | async-start | bytes 2097152 | tf_op jit(solution)/shard_map/all_to_all | solution.py:371
  156.2 1.8 collective-permute-start.8
  158.3 3.6 %collective-permute-start.9 = (bf16[32,8192]{1,0:T(8,128)(2,1)}, bf16[32,8192]{1,0:T(8,128)(2,1)S(1)}, u32[]{:S(2)}, u32[]{:S(2)}) collective-permute-start(bf16[32,8192]{1,0:T(8,128)(2,1)} %get-tuple-element.177), channel_id=1, source_target_pairs={{0,12},{2,14},{4,8},{6,10},{8,4},{10,6},{12,0},{14,2},{1,13},{3,15... | collective-permute-start | bytes 1572872 | tf_op jit(solution)/shard_map/ppermute | solution.py:106
  162.1 27.8 %collective-permute-done.9.refs_0_ = bf16[32,8192]{1,0:T(8,128)(2,1)S(1)} collective-permute-done((bf16[32,8192]{1,0:T(8,128)(2,1)}, bf16[32,8192]{1,0:T(8,128)(2,1)S(1)}, u32[]{:S(2)}, u32[]{:S(2)}) %collective-permute-start.9) | collective-permute-done | bytes 524320 | tf_op jit(solution)/shard_map/ppermute | solution.py:106
  189.9 3.2 %collective-permute-done.8.refs_0_ = bf16[64,8192]{1,0:T(8,128)(2,1)} collective-permute-done((bf16[64,8192]{1,0:T(8,128)(2,1)}, bf16[64,8192]{1,0:T(8,128)(2,1)}, u32[]{:S(2)}, u32[]{:S(2)}) %collective-permute-start.8) | collective-permute-done | bytes 1048608 | tf_op jit(solution)/shard_map/ppermute | solution.py:106
  193.1 6.4 %copy-done.2 = bf16[8192,1152]{1,0:T(8,128)(2,1)S(1)} copy-done((bf16[8192,1152]{1,0:T(8,128)(2,1)S(1)}, bf16[8192,1152]{1,0:T(8,128)(2,1)}, u32[]{:S(2)}) %copy-start.2) | copy-done | bytes 18874392
  199.5 1.2 copy-done.8
  200.7 4.1 %rows.13 = (f32[128,1024]{1,0:T(8,128)S(1)}, bf16[128,128]{1,0:T(8,128)(2,1)S(1)}) custom-call(s32[2,16]{1,0:T(2,128)S(1)} %add_convert_fusion.table, bf16[8192,1152]{1,0:T(8,128)(2,1)S(1)} %copy-done.2, bf16[64,8192]{1,0:T(8,128)(2,1)} %collective-permute-done.8.refs_0_, bf16[64,8192]{1,0:T(8,128)(2,1)S(1)} %copy-done.8), custom_call_target="tpu_custom_call" | custom-call | flops 1 | bytes 1 | tf_op jit(solution)/shard_map/rows/pallas_call | solution.py:171
  205.7 2.1 collective-permute-start.14
  207.8 8.2 %collective-permute-done.15.refs_1_ = bf16[64,8192]{1,0:T(8,128)(2,1)} collective-permute-done((bf16[64,8192]{1,0:T(8,128)(2,1)}, bf16[64,8192]{1,0:T(8,128)(2,1)}, u32[]{:S(2)}, u32[]{:S(2)}) %collective-permute-start.15) | collective-permute-done | bytes 1048608 | tf_op jit(solution)/shard_map/ppermute | solution.py:106
  216.0 6.4 %copy-done.3 = bf16[8192,1152]{1,0:T(8,128)(2,1)S(1)} copy-done((bf16[8192,1152]{1,0:T(8,128)(2,1)S(1)}, bf16[8192,1152]{1,0:T(8,128)(2,1)}, u32[]{:S(2)}) %copy-start.3) | copy-done | bytes 18874392
  222.4 4.4 %rows.14 = (f32[128,1024]{1,0:T(8,128)S(1)}, bf16[128,128]{1,0:T(8,128)(2,1)S(1)}) custom-call(s32[2,16]{1,0:T(2,128)S(1)} %add_convert_fusion.table, bf16[8192,1152]{1,0:T(8,128)(2,1)S(1)} %copy-done.3, bf16[64,8192]{1,0:T(8,128)(2,1)} %collective-permute-done.11.refs_0_, bf16[64,8192]{1,0:T(8,128)(2,1)} %collective-permute-done.15.refs_1_), custom_call_target="tpu_custom_call" | custom-call | flops 1 | bytes 1 | tf_op jit(solution)/shard_map/rows/pallas_call | solution.py:171
  228.6 1.2 gather_fusion.1
  230.4 8.1 %collective-permute-done.14.refs_3_ = bf16[32,8192]{1,0:T(8,128)(2,1)} collective-permute-done((bf16[32,8192]{1,0:T(8,128)(2,1)}, bf16[32,8192]{1,0:T(8,128)(2,1)}, u32[]{:S(2)}, u32[]{:S(2)}) %collective-permute-start.14) | collective-permute-done | bytes 524320 | tf_op jit(solution)/shard_map/ppermute | solution.py:106
  238.5 2.2 collective-permute-done.16
  242.3 8.1 %collective-permute-start.22 = (bf16[8,64,128]{2,1,0:T(8,128)(2,1)S(1)}, bf16[8,64,128]{2,1,0:T(8,128)(2,1)S(1)}, u32[]{:S(2)}, u32[]{:S(2)}) collective-permute-start(bf16[8,64,128]{2,1,0:T(8,128)(2,1)S(1)} %add.159), channel_id=1, source_target_pairs={{0,4},{2,6},{4,0},{6,2},{8,12},{10,14},{12,8},{14,10},{1,5},{3,7},... | collective-permute-start | bytes 393224 | tf_op jit(solution)/shard_map/ppermute | solution.py:106
  250.5 2.4 collective-permute-start.24
  252.9 6.4 %copy-done.4 = bf16[8192,1152]{1,0:T(8,128)(2,1)S(1)} copy-done((bf16[8192,1152]{1,0:T(8,128)(2,1)S(1)}, bf16[8192,1152]{1,0:T(8,128)(2,1)}, u32[]{:S(2)}) %copy-start.4) | copy-done | bytes 18874392
  259.2 4.3 %rows.15 = (f32[128,1024]{1,0:T(8,128)S(1)}, bf16[128,128]{1,0:T(8,128)(2,1)S(1)}) custom-call(s32[2,16]{1,0:T(2,128)S(1)} %add_convert_fusion.table, bf16[8192,1152]{1,0:T(8,128)(2,1)S(1)} %copy-done.4, bf16[32,8192]{1,0:T(8,128)(2,1)S(1)} %collective-permute-done.9.refs_0_, bf16[32,8192]{1,0:T(8,128)(2,1)} %collective-permute-done.13.refs_1_, ...), custom_call_target="tpu_custom_call" | custom-call | flops 1 | bytes 1 | tf_op jit(solution)/shard_map/rows/pallas_call | solution.py:171
  264.3 1.6 collective-permute-start.17
  265.9 1.1 gather_fusion
  267.8 1.6 collective-permute-start.21
  273.0 2.4 collective-permute-start.20
  277.2 4.0 %collective-permute-done.19 = bf16[8,64,128]{2,1,0:T(8,128)(2,1)S(1)} collective-permute-done((bf16[8,64,128]{2,1,0:T(8,128)(2,1)S(1)}, bf16[8,64,128]{2,1,0:T(8,128)(2,1)S(1)}, u32[]{:S(2)}, u32[]{:S(2)}) %collective-permute-start.19) | collective-permute-done | bytes 131104 | tf_op jit(solution)/shard_map/ppermute | solution.py:106
  283.3 4.5 %finish.2.refs_8_ = bf16[1024,1024]{1,0:T(8,128)(2,1)} custom-call(s32[9]{0:T(128)S(1)} %pad_add_fusion.2.table, f32[128,1024]{1,0:T(8,128)S(1)} %get-tuple-element.242.refs_0_, f32[128,1024]{1,0:T(8,128)S(1)} %get-tuple-element.243.refs_1_, f32[128,1024]{1,0:T(8,128)S(1)} %get-tuple-element.254.refs_2_, f32[128,1024]{1,0:T(8,128)S(1)} %copy-done.12, ...), custom_call_target="tpu_custom_call" | custom-call | flops 1 | bytes 1 | tf_op jit(solution)/shard_map/finish/pallas_call | solution.py:266
  287.8 4.5 %finish.3 = bf16[1024,1024]{1,0:T(8,128)(2,1)} custom-call(s32[9]{0:T(128)S(1)} %pad_add_fusion.table, f32[128,1024]{1,0:T(8,128)S(1)} %get-tuple-element.242.refs_0_, f32[128,1024]{1,0:T(8,128)S(1)} %get-tuple-element.243.refs_1_, f32[128,1024]{1,0:T(8,128)S(1)} %copy-done.10, f32[128,1024]{1,0:T(8,128)S(1)} %copy-done.14, ...), custom_call_target="tpu_custom_call", output_to_operand_aliasing={{}: (9, {})} | custom-call | flops 1 | bytes 1 | tf_op jit(solution)/shard_map/finish/pallas_call | solution.py:266
  (100 shorter events, 20.3 us)
Async XLA Ops:
  0.0 8.7 %copy-start.21 = (s32[64]{0:T(128)S(1)}, s32[64]{0:T(128)}, u32[]{:S(2)}) copy-start(s32[64]{0:T(128)} %param.14) | copy-start | bytes 772
  0.0 8.7 %copy-start.20 = (s32[2,8]{1,0:T(2,128)S(1)}, s32[2,8]{1,0:T(2,128)}, u32[]{:S(2)}) copy-start(s32[2,8]{1,0:T(2,128)} %param.15) | copy-start | bytes 196
  3.1 48.8 %collective-permute-start.1 = (bf16[64,8192]{1,0:T(8,128)(2,1)}, bf16[64,8192]{1,0:T(8,128)(2,1)}, u32[]{:S(2)}, u32[]{:S(2)}) collective-permute-start(bf16[64,8192]{1,0:T(8,128)(2,1)} %get-tuple-element.166), channel_id=1, source_target_pairs={{0,4},{2,6},{4,0},{6,2},{8,12},{10,14},{12,8},{14,10},{1,5},{3,7},... | collective-permute-start | bytes 3145736 | tf_op jit(solution)/shard_map/ppermute | solution.py:106
  6.1 58.7 %collective-permute-start = (bf16[64,8192]{1,0:T(8,128)(2,1)}, bf16[64,8192]{1,0:T(8,128)(2,1)}, u32[]{:S(2)}, u32[]{:S(2)}) collective-permute-start(bf16[64,8192]{1,0:T(8,128)(2,1)} %get-tuple-element.166), channel_id=1, source_target_pairs={{0,8},{2,10},{4,12},{6,14},{8,0},{10,2},{12,4},{14,6},{1,9},{3,11}... | collective-permute-start | bytes 3145736 | tf_op jit(solution)/shard_map/ppermute | solution.py:106
  13.5 2.8 copy-start.5
  16.4 37.9 %collective-permute-start.2 = (bf16[64,8192]{1,0:T(8,128)(2,1)}, bf16[64,8192]{1,0:T(8,128)(2,1)}, u32[]{:S(2)}, u32[]{:S(2)}) collective-permute-start(bf16[64,8192]{1,0:T(8,128)(2,1)} %get-tuple-element.261), channel_id=1, source_target_pairs={{0,1},{1,0},{2,3},{3,2},{4,5},{5,4},{6,7},{7,6},{8,9},{9,8},{10,11... | collective-permute-start | bytes 3145736 | tf_op jit(solution)/shard_map/ppermute | solution.py:110
  16.4 65.1 %collective-permute-start.7 = (bf16[128,8192]{1,0:T(8,128)(2,1)S(1)}, bf16[128,8192]{1,0:T(8,128)(2,1)}, u32[]{:S(2)}, u32[]{:S(2)}) collective-permute-start(bf16[128,8192]{1,0:T(8,128)(2,1)S(1)} %bitcast.66), channel_id=1, source_target_pairs={{0,2},{2,0},{4,6},{6,4},{8,10},{10,8},{12,14},{14,12},{1,3},{3,1},... | collective-permute-start | bytes 6291464 | tf_op jit(solution)/shard_map/ppermute | solution.py:106
  19.0 2.2 copy-start.6
  51.9 47.8 %collective-permute-start.6 = (bf16[64,8192]{1,0:T(8,128)(2,1)}, bf16[64,8192]{1,0:T(8,128)(2,1)}, u32[]{:S(2)}, u32[]{:S(2)}) collective-permute-start(bf16[64,8192]{1,0:T(8,128)(2,1)} %get-tuple-element.143), channel_id=1, source_target_pairs={{0,8},{2,10},{4,12},{6,14},{8,0},{10,2},{12,4},{14,6},{1,9},{3,11}... | collective-permute-start | bytes 3145736 | tf_op jit(solution)/shard_map/ppermute | solution.py:106
  52.7 81.7 %collective-permute-start.4 = (bf16[64,8192]{1,0:T(8,128)(2,1)}, bf16[64,8192]{1,0:T(8,128)(2,1)}, u32[]{:S(2)}, u32[]{:S(2)}) collective-permute-start(bf16[64,8192]{1,0:T(8,128)(2,1)} %collective-permute-done.1.refs_0_), channel_id=1, source_target_pairs={{0,2},{2,0},{4,6},{6,4},{8,10},{10,8},{12,14},{14,12},{1,3},{3,1},... | collective-permute-start | bytes 3145736 | tf_op jit(solution)/shard_map/ppermute | solution.py:106
  61.3 20.2 %copy-start = (bf16[8192,1152]{1,0:T(8,128)(2,1)}, bf16[8192,1152]{1,0:T(8,128)(2,1)S(1)}, u32[]{:S(2)}) copy-start(bf16[8192,1152]{1,0:T(8,128)(2,1)S(1)} %pin.1.weights) | copy-start | bytes 56623108
  64.9 69.5 %collective-permute-start.3 = (bf16[64,8192]{1,0:T(8,128)(2,1)}, bf16[64,8192]{1,0:T(8,128)(2,1)}, u32[]{:S(2)}, u32[]{:S(2)}) collective-permute-start(bf16[64,8192]{1,0:T(8,128)(2,1)} %get-tuple-element.143), channel_id=1, source_target_pairs={{0,4},{2,6},{4,0},{6,2},{8,12},{10,14},{12,8},{14,10},{1,5},{3,7},... | collective-permute-start | bytes 3145736 | tf_op jit(solution)/shard_map/ppermute | solution.py:106
  75.5 58.9 %collective-permute-start.5 = (bf16[64,8192]{1,0:T(8,128)(2,1)}, bf16[64,8192]{1,0:T(8,128)(2,1)}, u32[]{:S(2)}, u32[]{:S(2)}) collective-permute-start(bf16[64,8192]{1,0:T(8,128)(2,1)} %collective-permute-done.refs_1_), channel_id=1, source_target_pairs={{0,2},{2,0},{4,6},{6,4},{8,10},{10,8},{12,14},{14,12},{1,3},{3,1},... | collective-permute-start | bytes 3145736 | tf_op jit(solution)/shard_map/ppermute | solution.py:106
  99.8 51.8 %collective-permute-start.10 = (bf16[64,8192]{1,0:T(8,128)(2,1)}, bf16[64,8192]{1,0:T(8,128)(2,1)S(1)}, u32[]{:S(2)}, u32[]{:S(2)}) collective-permute-start(bf16[64,8192]{1,0:T(8,128)(2,1)} %collective-permute-done.6.refs_1_), channel_id=1, source_target_pairs={{0,2},{2,0},{4,6},{6,4},{8,10},{10,8},{12,14},{14,12},{1,3},{3,1},... | collective-permute-start | bytes 3145736 | tf_op jit(solution)/shard_map/ppermute | solution.py:106
  101.3 51.3 %collective-permute-start.11 = (bf16[64,8192]{1,0:T(8,128)(2,1)}, bf16[64,8192]{1,0:T(8,128)(2,1)}, u32[]{:S(2)}, u32[]{:S(2)}) collective-permute-start(bf16[64,8192]{1,0:T(8,128)(2,1)} %get-tuple-element.166), channel_id=1, source_target_pairs={{0,12},{2,14},{4,8},{6,10},{8,4},{10,6},{12,0},{14,2},{1,13},{3,15... | collective-permute-start | bytes 3145736 | tf_op jit(solution)/shard_map/ppermute | solution.py:106
  134.4 6.4 %copy-start.1 = (bf16[8192,1152]{1,0:T(8,128)(2,1)S(1)}, bf16[8192,1152]{1,0:T(8,128)(2,1)}, u32[]{:S(2)}) copy-start(bf16[8192,1152]{1,0:T(8,128)(2,1)} %copy-done) | copy-start | bytes 56623108
  145.2 0.9 copy-start.11
  150.7 0.8 copy-start.9
  151.6 1.0 copy-start.7
  152.6 63.4 %all-to-all-start = ((bf16[16,64,512]{2,1,0:T(8,128)(2,1)}), bf16[16,64,512]{2,1,0:T(8,128)(2,1)S(1)}, u32[]{:S(2)}, u32[]{:S(2)}) async-start(bf16[16,64,512]{2,1,0:T(8,128)(2,1)} %bitcast.33), calls=%async_computation | async-start | bytes 2097152 | tf_op jit(solution)/shard_map/all_to_all | solution.py:371
  156.2 36.9 %collective-permute-start.8 = (bf16[64,8192]{1,0:T(8,128)(2,1)}, bf16[64,8192]{1,0:T(8,128)(2,1)}, u32[]{:S(2)}, u32[]{:S(2)}) collective-permute-start(bf16[64,8192]{1,0:T(8,128)(2,1)} %collective-permute-done.3.refs_0_), channel_id=1, source_target_pairs={{0,2},{2,0},{4,6},{6,4},{8,10},{10,8},{12,14},{14,12},{1,3},{3,1},... | collective-permute-start | bytes 3145736 | tf_op jit(solution)/shard_map/ppermute | solution.py:106
  158.0 58.0 %collective-permute-start.15 = (bf16[64,8192]{1,0:T(8,128)(2,1)}, bf16[64,8192]{1,0:T(8,128)(2,1)}, u32[]{:S(2)}, u32[]{:S(2)}) collective-permute-start(bf16[64,8192]{1,0:T(8,128)(2,1)} %collective-permute-done.11.refs_0_), channel_id=1, source_target_pairs={{0,2},{2,0},{4,6},{6,4},{8,10},{10,8},{12,14},{14,12},{1,3},{3,1},... | collective-permute-start | bytes 3145736 | tf_op jit(solution)/shard_map/ppermute | solution.py:106
  158.3 31.6 %collective-permute-start.9 = (bf16[32,8192]{1,0:T(8,128)(2,1)}, bf16[32,8192]{1,0:T(8,128)(2,1)S(1)}, u32[]{:S(2)}, u32[]{:S(2)}) collective-permute-start(bf16[32,8192]{1,0:T(8,128)(2,1)} %get-tuple-element.177), channel_id=1, source_target_pairs={{0,12},{2,14},{4,8},{6,10},{8,4},{10,6},{12,0},{14,2},{1,13},{3,15... | collective-permute-start | bytes 1572872 | tf_op jit(solution)/shard_map/ppermute | solution.py:106
  161.9 43.8 %collective-permute-start.13 = (bf16[32,8192]{1,0:T(8,128)(2,1)}, bf16[32,8192]{1,0:T(8,128)(2,1)}, u32[]{:S(2)}, u32[]{:S(2)}) collective-permute-start(bf16[32,8192]{1,0:T(8,128)(2,1)} %get-tuple-element.192), channel_id=1, source_target_pairs={{0,12},{2,14},{4,8},{6,10},{8,4},{10,6},{12,0},{14,2},{1,13},{3,15... | collective-permute-start | bytes 1572872 | tf_op jit(solution)/shard_map/ppermute | solution.py:106
  193.1 37.2 %collective-permute-start.12 = (bf16[32,8192]{1,0:T(8,128)(2,1)S(1)}, bf16[32,8192]{1,0:T(8,128)(2,1)}, u32[]{:S(2)}, u32[]{:S(2)}) collective-permute-start(bf16[32,8192]{1,0:T(8,128)(2,1)S(1)} %collective-permute-done.9.refs_0_), channel_id=1, source_target_pairs={{0,2},{2,0},{4,6},{6,4},{8,10},{10,8},{12,14},{14,12},{1,3},{3,1},... | collective-permute-start | bytes 1572872 | tf_op jit(solution)/shard_map/ppermute | solution.py:106
  193.1 6.4 %copy-start.2 = (bf16[8192,1152]{1,0:T(8,128)(2,1)S(1)}, bf16[8192,1152]{1,0:T(8,128)(2,1)}, u32[]{:S(2)}) copy-start(bf16[8192,1152]{1,0:T(8,128)(2,1)} %copy-done) | copy-start | bytes 56623108
  199.5 1.2 copy-start.8
  204.9 0.8 copy-start.13
  205.7 32.8 %collective-permute-start.14 = (bf16[32,8192]{1,0:T(8,128)(2,1)}, bf16[32,8192]{1,0:T(8,128)(2,1)}, u32[]{:S(2)}, u32[]{:S(2)}) collective-permute-start(bf16[32,8192]{1,0:T(8,128)(2,1)} %collective-permute-done.13.refs_1_), channel_id=1, source_target_pairs={{0,2},{2,0},{4,6},{6,4},{8,10},{10,8},{12,14},{14,12},{1,3},{3,1},... | collective-permute-start | bytes 1572872 | tf_op jit(solution)/shard_map/ppermute | solution.py:106
  216.0 6.4 %copy-start.3 = (bf16[8192,1152]{1,0:T(8,128)(2,1)S(1)}, bf16[8192,1152]{1,0:T(8,128)(2,1)}, u32[]{:S(2)}) copy-start(bf16[8192,1152]{1,0:T(8,128)(2,1)} %copy-done) | copy-start | bytes 56623108
  226.8 0.8 copy-start.15
  227.6 13.1 %collective-permute-start.16 = (bf16[8,64,128]{2,1,0:T(8,128)(2,1)S(1)}, bf16[8,64,128]{2,1,0:T(8,128)(2,1)S(1)}, u32[]{:S(2)}, u32[]{:S(2)}) collective-permute-start(bf16[8,64,128]{2,1,0:T(8,128)(2,1)S(1)} %bitcast_dynamic-update-slice_fusion.2), channel_id=1, source_target_pairs={{0,2},{2,0},{4,6},{6,4},{8,10},{10,8},{12,14},{14,12},{1,3},{3,1},... | collective-permute-start | bytes 393224 | tf_op jit(solution)/shard_map/ppermute | solution.py:106
  241.3 24.5 %copy-start.22 = (s32[8]{0:T(128)S(1)}, s32[8]{0:T(128)}, u32[]{:S(2)}) copy-start(s32[8]{0:T(128)} %gather_fusion.1) | copy-start | bytes 100
  242.3 29.8 %collective-permute-start.22 = (bf16[8,64,128]{2,1,0:T(8,128)(2,1)S(1)}, bf16[8,64,128]{2,1,0:T(8,128)(2,1)S(1)}, u32[]{:S(2)}, u32[]{:S(2)}) collective-permute-start(bf16[8,64,128]{2,1,0:T(8,128)(2,1)S(1)} %add.159), channel_id=1, source_target_pairs={{0,4},{2,6},{4,0},{6,2},{8,12},{10,14},{12,8},{14,10},{1,5},{3,7},... | collective-permute-start | bytes 393224 | tf_op jit(solution)/shard_map/ppermute | solution.py:106
  250.4 22.6 %collective-permute-start.23 = (bf16[8,64,128]{2,1,0:T(8,128)(2,1)S(1)}, bf16[8,64,128]{2,1,0:T(8,128)(2,1)}, u32[]{:S(2)}, u32[]{:S(2)}) collective-permute-start(bf16[8,64,128]{2,1,0:T(8,128)(2,1)S(1)} %add.159), channel_id=1, source_target_pairs={{0,8},{2,10},{4,12},{6,14},{8,0},{10,2},{12,4},{14,6},{1,9},{3,11}... | collective-permute-start | bytes 393224 | tf_op jit(solution)/shard_map/ppermute | solution.py:106
  250.5 25.0 %collective-permute-start.24 = (bf16[8,64,128]{2,1,0:T(8,128)(2,1)S(1)}, bf16[8,64,128]{2,1,0:T(8,128)(2,1)}, u32[]{:S(2)}, u32[]{:S(2)}) collective-permute-start(bf16[8,64,128]{2,1,0:T(8,128)(2,1)S(1)} %add.159), channel_id=1, source_target_pairs={{0,12},{2,14},{4,8},{6,10},{8,4},{10,6},{12,0},{14,2},{1,13},{3,15... | collective-permute-start | bytes 393224 | tf_op jit(solution)/shard_map/ppermute | solution.py:106
  252.9 6.4 %copy-start.4 = (bf16[8192,1152]{1,0:T(8,128)(2,1)S(1)}, bf16[8192,1152]{1,0:T(8,128)(2,1)}, u32[]{:S(2)}) copy-start(bf16[8192,1152]{1,0:T(8,128)(2,1)} %copy-done) | copy-start | bytes 56623108
  263.5 0.8 copy-start.17
  264.3 5.7 %collective-permute-start.17 = (bf16[8,64,128]{2,1,0:T(8,128)(2,1)S(1)}, bf16[8,64,128]{2,1,0:T(8,128)(2,1)}, u32[]{:S(2)}, u32[]{:S(2)}) collective-permute-start(bf16[8,64,128]{2,1,0:T(8,128)(2,1)S(1)} %bitcast_dynamic-update-slice_fusion), channel_id=1, source_target_pairs={{0,2},{2,0},{4,6},{6,4},{8,10},{10,8},{12,14},{14,12},{1,3},{3,1},... | collective-permute-start | bytes 393224 | tf_op jit(solution)/shard_map/ppermute | solution.py:106
  267.8 13.4 %collective-permute-start.21 = (bf16[8,64,512]{2,1,0:T(8,128)(2,1)S(1)}, bf16[8,64,512]{2,1,0:T(8,128)(2,1)S(1)}, u32[]{:S(2)}, u32[]{:S(2)}) collective-permute-start(bf16[8,64,512]{2,1,0:T(8,128)(2,1)S(1)} %take.1.refs_6_), channel_id=1, source_target_pairs={{0,16},{16,0},{1,17},{17,1},{2,18},{18,2},{3,19},{19,3},{4,20},{20... | collective-permute-start | bytes 1572872 | tf_op jit(solution)/shard_map/ppermute | solution.py:110
  271.0 6.2 %collective-permute-start.18 = (bf16[8,64,128]{2,1,0:T(8,128)(2,1)S(1)}, bf16[8,64,128]{2,1,0:T(8,128)(2,1)S(1)}, u32[]{:S(2)}, u32[]{:S(2)}) collective-permute-start(bf16[8,64,128]{2,1,0:T(8,128)(2,1)S(1)} %add.154), channel_id=1, source_target_pairs={{0,4},{2,6},{4,0},{6,2},{8,12},{10,14},{12,8},{14,10},{1,5},{3,7},... | collective-permute-start | bytes 393224 | tf_op jit(solution)/shard_map/ppermute | solution.py:106
  272.1 9.1 %collective-permute-start.19 = (bf16[8,64,128]{2,1,0:T(8,128)(2,1)S(1)}, bf16[8,64,128]{2,1,0:T(8,128)(2,1)S(1)}, u32[]{:S(2)}, u32[]{:S(2)}) collective-permute-start(bf16[8,64,128]{2,1,0:T(8,128)(2,1)S(1)} %add.154), channel_id=1, source_target_pairs={{0,8},{2,10},{4,12},{6,14},{8,0},{10,2},{12,4},{14,6},{1,9},{3,11}... | collective-permute-start | bytes 393224 | tf_op jit(solution)/shard_map/ppermute | solution.py:106
  273.0 8.2 %collective-permute-start.20 = (bf16[8,64,128]{2,1,0:T(8,128)(2,1)S(1)}, bf16[8,64,128]{2,1,0:T(8,128)(2,1)S(1)}, u32[]{:S(2)}, u32[]{:S(2)}) collective-permute-start(bf16[8,64,128]{2,1,0:T(8,128)(2,1)S(1)} %add.154), channel_id=1, source_target_pairs={{0,12},{2,14},{4,8},{6,10},{8,4},{10,6},{12,0},{14,2},{1,13},{3,15... | collective-permute-start | bytes 393224 | tf_op jit(solution)/shard_map/ppermute | solution.py:106
  281.2 1.0 copy-start.12
  282.3 1.0 copy-start.16
  283.3 4.5 %copy-start.10 = (f32[128,1024]{1,0:T(8,128)S(1)}, f32[128,1024]{1,0:T(8,128)}, u32[]{:S(2)}) copy-start(f32[128,1024]{1,0:T(8,128)} %copy-done.9) | copy-start | bytes 1572868
  283.3 4.5 %copy-start.14 = (f32[128,1024]{1,0:T(8,128)S(1)}, f32[128,1024]{1,0:T(8,128)}, u32[]{:S(2)}) copy-start(f32[128,1024]{1,0:T(8,128)} %copy-done.13) | copy-start | bytes 1572868
  283.3 4.5 %copy-start.18 = (f32[128,1024]{1,0:T(8,128)S(1)}, f32[128,1024]{1,0:T(8,128)}, u32[]{:S(2)}) copy-start(f32[128,1024]{1,0:T(8,128)} %copy-done.17) | copy-start | bytes 1572868
  (1 other events, 0.7 us)

commit v7 on v6

--- a/solution.py
+++ b/solution.py
@@ -2,7 +2,6 @@
 
 import jax
 import jax.numpy as jnp
-import numpy as np
 from jax import lax
 from jax.experimental import pallas as pl
 from jax.experimental.pallas import tpu as pltpu
@@ -95,8 +94,11 @@
     return pairs + [(b, a) for a, b in pairs]
 
 
+RING = [0, 2, 4, 6, 7, 5, 3, 1]
+AHEAD = [(RING[i], RING[(i + 1) % 8]) for i in range(8)]
+BACK = [(b, a) for a, b in AHEAD]
 ACROSS = [(i, i ^ 1) for i in range(8)]
-ALONG = {"x%d" % d: [(i, i ^ (2 * d)) for i in range(8)] for d in (1, 2, 3)}
+ALONG = [[(i, i ^ (2 * d)) for i in range(8)] for d in (1, 2, 3)]
 HALF = BLOCK // 2
 DEPTH = 1024
 VMEM_LIMIT = 16 * 1024 * 1024
@@ -141,11 +143,11 @@
         scratch_shapes=[pltpu.SemaphoreType.DMA],
         name="pin",
         **settings(),
-    )(pltpu.with_memory_space_constraint(weight, pltpu.HBM), own, swapped)
-
-
-def rows_kernel(first, table, weights, *refs):
-    *pieces, base, small = refs
+    )(weight, own, swapped)
+
+
+def rows_kernel(group, table, weights, *refs):
+    *pieces, shrunk, base, shrunk_out = refs
     columns = base.shape[1]
     total = None
     for at in range(0, weights.shape[0], DEPTH):
@@ -155,21 +157,23 @@
         part = jnp.dot(x, weights[cut, :], preferred_element_type=jnp.float32)
         total = part if total is None else total + part
     base[...] = total[:, :columns]
-    lane = lax.broadcasted_iota(jnp.int32, small.shape, 1)
-    row = lax.broadcasted_iota(jnp.int32, small.shape, 0)
+    lane = lax.broadcasted_iota(jnp.int32, shrunk.shape, 1)
+    row = lax.broadcasted_iota(jnp.int32, shrunk.shape, 0)
     use = jnp.where(
         row < HALF,
-        jnp.where(lane < 64, table[0, first], table[1, first]),
-        jnp.where(lane < 64, table[0, first + 1], table[1, first + 1]),
-    )
-    small[...] = jnp.where(use > 0, total[:, columns:], 0.0).astype(jnp.bfloat16)
-
-
-def rows_call(first, table, weights, pieces):
+        jnp.where(lane < 64, table[0, 2 * group], table[1, 2 * group]),
+        jnp.where(lane < 64, table[0, 2 * group + 1], table[1, 2 * group + 1]),
+    )
+    small = total[:, columns:].astype(jnp.bfloat16).astype(jnp.float32)
+    old = shrunk[...].astype(jnp.float32)
+    shrunk_out[...] = jnp.where(use > 0, small, old).astype(jnp.bfloat16)
+
+
+def rows_call(group, table, weights, pieces, shrunk):
     columns = weights.shape[1] - 128
-    operands = [pltpu.with_memory_space_constraint(weights, pltpu.VMEM)] + pieces
-    return pl.pallas_call(
-        functools.partial(rows_kernel, first),
+    operands = [pltpu.with_memory_space_constraint(weights, pltpu.VMEM)] + pieces + [shrunk]
+    return pl.pallas_call(
+        functools.partial(rows_kernel, group),
         in_specs=[pl.BlockSpec(memory_space=pltpu.SMEM)] + in_vmem(len(operands)),
         out_specs=in_vmem(2),
         out_shape=[
@@ -202,7 +206,7 @@
         out_shape=jax.ShapeDtypeStruct((8, 2, rank, part), jnp.bfloat16),
         name="pack",
         **settings(),
-    )(table, up_maps)
+    )(table, pltpu.with_memory_space_constraint(up_maps, pltpu.HBM))
 
 
 def take_kernel(table, got, out):
@@ -225,87 +229,44 @@
     )(table, got)
 
 
-def finish_kernel(sources, table, *refs):
-    bases = refs[: max(sources) + 1]
-    shrunk, up_mine, up_other, out = refs[len(bases)], refs[len(bases) + 1], refs[len(bases) + 2], refs[-1]
+def finish_kernel(table, *refs):
+    *bases, shrunk, up_mine, up_other, out = refs
     at = pl.program_id(0)
     part = up_mine.shape[2]
-    both = shrunk[...].astype(jnp.float32)
-    both = (both[:, :64] + both[:, 64:]).astype(jnp.bfloat16)
-    group = table[8]
+    both = shrunk[0].astype(jnp.float32)
+    value = jnp.where(table[2, at] > 0, both[:, 64:], both[:, :64]).astype(jnp.bfloat16)
+    group = table[3, at]
     for g, base in enumerate(bases):
-        steps = [i for i, source in enumerate(sources) if source == g]
-
-        @pl.when((at >= steps[0]) & (at <= steps[-1]))
+
+        @pl.when(at // 2 == g)
         def _():
             for up, side in ((up_mine, group), (up_other, 1 - group)):
                 cut = pl.ds(pl.multiple_of(side * part, part), part)
-                grown = jnp.dot(both, up[0], preferred_element_type=jnp.float32)
+                grown = jnp.dot(value, up[0], preferred_element_type=jnp.float32)
                 out[:, cut] = (base[:, cut] + 0.5 * grown).astype(out.dtype)
 
 
-def finish_call(table, half, bases, shrunk, up_mine, up_other, into):
+def finish_call(table, bases, shrunk, up_mine, up_other):
     columns = bases[0].shape[1]
     _, rank, part = up_mine.shape
-    sources = [0, 1, 2, 2, 3, 3, 4, 4]
 
     def base_spec(g):
-        if g < 2:
-            return pl.BlockSpec((HALF, columns), lambda i, t: (half, 0))
-        return pl.BlockSpec((HALF, columns), lambda i, t: (jnp.clip(i - 2 * g + 2, 0, 1), 0))
-
-    up = pl.BlockSpec((1, rank, part), lambda i, t: (t[i], 0, 0))
-    specs = [base_spec(g) for g in range(5)]
-    specs += [pl.BlockSpec((HALF, 2 * rank), lambda i, t: (t[i], 0)), up, up]
-    operands = [*bases, shrunk, up_mine, up_other]
-    aliases = {}
-    if into is not None:
-        aliases = {1 + len(operands): 0}
-        operands.append(into)
-        specs.append(pl.BlockSpec(memory_space=pltpu.HBM))
-    return pl.pallas_call(
-        functools.partial(finish_kernel, sources),
+        return pl.BlockSpec((HALF, columns), lambda i, t: (jnp.clip(i - 2 * g, 0, 1), 0))
+
+    up = pl.BlockSpec((1, rank, part), lambda i, t: (t[0, i], 0, 0))
+    return pl.pallas_call(
+        finish_kernel,
         grid_spec=pltpu.PrefetchScalarGridSpec(
             num_scalar_prefetch=1,
-            grid=(8,),
-            in_specs=specs,
-            out_specs=pl.BlockSpec((HALF, columns), lambda i, t: (2 * t[i] + half, 0)),
+            grid=(16,),
+            in_specs=[base_spec(g) for g in range(8)]
+            + [pl.BlockSpec((1, HALF, 2 * rank), lambda i, t: (t[1, i], i % 2, 0)), up, up],
+            out_specs=pl.BlockSpec((HALF, columns), lambda i, t: (2 * t[0, i] + i % 2, 0)),
         ),
         out_shape=jax.ShapeDtypeStruct((8 * BLOCK, columns), jnp.bfloat16),
-        input_output_aliases=aliases,
         name="finish",
         **settings(),
-    )(table, *operands)
-
-
-CUTS = {"": (0, 128), "0": (0, 64), "1": (64, 128), "1a": (64, 96), "1b": (96, 128)}
-GROUPS = [
-    [("own", "")],
-    [("own_y", "")],
-    [("x1", "0"), ("x2", "0")],
-    [("x1", "1"), ("x2", "1")],
-    [("x1_y", "0"), ("x2_y", "0")],
-    [("x1_y", "1"), ("x2_y", "1")],
-    [("x3", "0"), ("x3_y", "0")],
-    [("x3", "1a"), ("x3", "1b"), ("x3_y", "1a"), ("x3_y", "1b")],
-]
-HALVES = [
-    ("own", 0), ("own", 1), ("own_y", 0), ("own_y", 1), ("x1", 0), ("x2", 0), ("x1", 1), ("x2", 1),
-    ("x1_y", 0), ("x2_y", 0), ("x1_y", 1), ("x2_y", 1), ("x3", 0), ("x3_y", 0), ("x3", 1), ("x3_y", 1),
-]
-EVENTS = [
-    ([], [("x1", "0"), ("x2", "0")], [("own", "")], []),
-    ([("x1", "0")], [("x2", "1")], [("x1", "0")], [0]),
-    ([("x2", "0")], [("x1", "1")], [("x2", "0")], [2]),
-    ([("own_y", "")], [], [], [1]),
-    ([("x2", "1")], [("x3", "0")], [("x2", "1")], []),
-    ([("x1_y", "0"), ("x2_y", "0"), ("x1", "1")], [("x3", "1a")], [("x1", "1")], [3, 4]),
-    ([("x3", "0"), ("x2_y", "1")], [("x3", "1b")], [("x3", "0")], []),
-    ([("x1_y", "1"), ("x3", "1a")], [], [("x3", "1a")], [5]),
-    ([("x3", "1b")], [], [("x3", "1b")], []),
-    ([("x3_y", "0")], [], [], [6]),
-    ([("x3_y", "1a"), ("x3_y", "1b")], [], [], [7]),
-]
+    )(table, *bases, shrunk, up_mine, up_other)
 
 
 def chain_body(
@@ -317,18 +278,11 @@
     group = lax.axis_index("groups")
     myself = me * 2 + store
     held, rank, width = adapter_down_maps.shape
-    columns = query_weight.shape[1]
     rows = tokens[0]
-    have = {("own", name): rows[slice(*cut)] for name, cut in CUTS.items()}
-    flight = {}
-
-    def issue(along, across):
-        for name, piece in along:
-            flight[name, piece] = send(have["own", piece], ALONG[name])
-        for name, piece in across:
-            flight[name + "_y", piece] = send(have[name, piece], ACROSS)
-
-    issue(*EVENTS[0][1:3])
+    halves = [rows[:HALF], rows[HALF:]]
+
+    ahead, back = list(halves), list(halves[::-1])
+    flight = [(send(ahead[k], AHEAD), send(back[k], BACK)) for k in range(2)]
 
     store_slots = find_slots(adapter_home_slot, adapter_per_block)
     owner = store_slots // held
@@ -343,64 +297,53 @@
     weights = pin_call(query_weight, down_own, swap(down_lent, "store"))
     up_sent = pack_call(jnp.concatenate([picked, group[None]]).astype(jnp.int32), adapter_up_maps)
 
-    blocks = jnp.stack(
-        [
-            (z if name[0] == "o" else z ^ int(name[1])) * 2 + (1 - y if name.endswith("_y") else y)
-            for name, _ in HALVES
-        ]
-    ).astype(jnp.int32)
+    position = jnp.where(y == 0, z, 7 - z)
+    places = []
+    for k in range(8):
+        step = (k + 1) // 2
+        places += [position - step, position + step] if k % 2 else [position + step, position - step]
+    places = jnp.stack(places) % 8
+    blocks = jnp.where(places < 4, 2 * places, 15 - 2 * places).astype(jnp.int32)
     hit = blocks[:, None] == jnp.arange(8, dtype=jnp.int32)[None, :]
     owners = jnp.sum(jnp.where(hit, owner_row[None, :], 0), axis=1)
     table = jnp.stack([owners == myself, owners == me * 2 + 1 - store]).astype(jnp.int32)
 
-    bases = [None] * 8
-    shrunk = [jnp.zeros((8, HALF, 2 * rank), jnp.bfloat16) for _ in range(2)]
+    bases = []
+    shrunk = jnp.zeros((BLOCK, 2 * rank), jnp.bfloat16)
+    pieces = [rows]
     extra = {"up": up_sent}
-    for at, (waits, along, across, groups) in enumerate(EVENTS[1:], 1):
-        got = {key: flight.pop(key) for key in waits}
-        if at >= len(EVENTS) - 2:
-            extra.update(flight.pop("late"))
-        got, have, bases, shrunk, extra = lax.optimization_barrier(
-            (got, have, bases, shrunk, extra)
+    for k in range(7):
+        base, shrunk = rows_call(k, table, weights, pieces, shrunk)
+        bases.append(base)
+        if k == 6:
+            extra["up"] = up_got
+        (got_ahead, got_back), ahead, back, bases, shrunk, extra = lax.optimization_barrier(
+            (flight[k], ahead, back, bases, shrunk, extra)
         )
-        have.update({key: got[key] for key in waits})
-        issue(along, across)
-        if at == 6:
-            sent = extra.pop("up").reshape(16, rank, -1)
-            flight["late"] = {
-                "up": lax.all_to_all(
-                    sent, ("tensor", "store"), split_axis=0, concat_axis=0, tiled=True
-                )
-            }
-        for g in groups:
-            base, small = rows_call(2 * g, table, weights, [have[key] for key in GROUPS[g]])
-            bases[g] = base
-            for i in range(2):
-                half = HALVES[2 * g + i][1]
-                shrunk[half] = lax.dynamic_update_slice(
-                    shrunk[half], small[None, i * HALF : (i + 1) * HALF], (blocks[2 * g + i], 0, 0)
-                )
-        if at == len(EVENTS) - 2:
-            flight["late"] = {"first": send(shrunk[0], ACROSS)}
+        ahead.append(got_ahead)
+        back.append(got_back)
+        if k < 5:
+            flight.append((send(ahead[k + 2], AHEAD), send(back[k + 2], BACK)))
+        if k == 4:
+            up_got = lax.all_to_all(
+                extra["up"].reshape(16, rank, -1),
+                ("tensor", "store"),
+                split_axis=0,
+                concat_axis=0,
+                tiled=True,
+            )
+        pieces = [got_ahead, got_back] if k % 2 == 0 else [got_back, got_ahead]
+    base, shrunk = rows_call(7, table, weights, pieces, shrunk)
+    bases.append(base)
 
     up_mine = take_call(owner_row, extra["up"])
     up_other = swap(up_mine, "groups")
-
-    def total(value):
-        arrived = [send(value, pairs) for pairs in ALONG.values()]
-        return (value + arrived[0] + arrived[1] + arrived[2]).reshape(8 * HALF, 2 * rank)
-
-    first = total(shrunk[0] + extra["first"])
-    second = total(shrunk[1] + send(shrunk[1], ACROSS))
-    query = None
-    for half, value in enumerate((first, second)):
-        chosen = [0, 1] + [g for g in range(2, 8) if HALVES[2 * g][1] == half]
-        places = [2 * g + half for g in (0, 1)] + [2 * g + i for g in chosen[2:] for i in range(2)]
-        order = jnp.concatenate([blocks[np.array(places)], group[None]]).astype(jnp.int32)
-        query = finish_call(
-            order, half, [bases[g] for g in chosen], value, up_mine, up_other, query
-        )
-    return query[None]
+    pair = jnp.stack([shrunk, send(shrunk, ACROSS)])
+    everyone = jnp.concatenate([pair] + [send(pair, pairs) for pairs in ALONG])
+    home, core = owners // 2, owners % 2
+    where = 2 * ((home // 2) ^ z) + ((home % 2) ^ y)
+    table = jnp.stack([blocks, where, core != store, jnp.broadcast_to(group, (16,))])
+    return finish_call(table.astype(jnp.int32), bases, everyone, up_mine, up_other)[None]
 
 
 def body(tokens, *rest):

time: 293 us -> 238 us (0.81)
  starting transfers between devices: 55.4 us -> 33.1 us
  local copies, waits for them, and re-layouts: 46.7 us -> 28.4 us
  waiting for transfers between devices: 128 us -> 120 us
  other arithmetic: 5.5 us -> 1.48 us
  Pallas kernels: 52.7 us -> 49.1 us
    ppermute x23 -> x18, starting transfers between devices: 50.2 us -> 26.1 us  [send(): return lax.ppermute(value, 'tensor', pairs)]
    unnamed x47 -> x38, local copies, waits for them, and re-layouts: 36.6 us -> 23.3 us
    ppermute x23 -> x18, waiting for transfers between devices: 128 us -> 120 us  [send(): return lax.ppermute(value, 'tensor', pairs)]
    pallas_call x1, Pallas kernels: 7 us -> 3.99 us  [pin_call(): pl.pallas_call(pin_kernel, in_specs=[pl.BlockSpec(memory_space=pltpu.HBM)...]
    pallas_call x10 -> x9, Pallas kernels: 43.4 us -> 41.5 us  [the longest x8 32.7 us: rows_call(): pl.pallas_call(functools.partial(rows_kernel, group), in_specs=[pl.BlockS...]
  transfers between devices with their start and end apart: 26 -> 21, of which waited for: 10 -> 15; matrix products, arithmetic and copies ran while one was open for 4% -> 1% of each run, Pallas kernels for 15% -> 15%
where the time goes in v7:
time: 238 us; the launch traced here: 236 us
  waiting for transfers between devices  120 us (50%)
  Pallas kernels  49.1 us (21%)
  starting transfers between devices  33.1 us (14%)
  local copies, waits for them, and re-layouts  28.4 us (12%)
  between operations  4.12 us (2%)
    ppermute x18, waiting for transfers between devices, send(): return lax.ppermute(value, 'tensor', pairs)  120 us
    pallas_call x8, Pallas kernels, rows_call(): pl.pallas_call(functools.partial(rows_kernel, group), in_specs=[pl.BlockS...  32.7 us
    ppermute x18, starting transfers between devices, send(): return lax.ppermute(value, 'tensor', pairs)  26.1 us
    unnamed x38, local copies, waits for them, and re-layouts  23.3 us
    pallas_call x1, Pallas kernels, finish_call(): pl.pallas_call(finish_kernel, grid_spec=pltpu.PrefetchScalarGridSpec(num_...  8.79 us
    all_to_all x1, starting transfers between devices, chain_body(): lax.all_to_all(extra['up'].reshape(16, rank, -1), ('tensor', 'store'), sp...  5.01 us
  transfers between devices with their start and end apart: 21, of which 15 were waited for; matrix products, arithmetic and copies ran while one was open for 1% of the time, Pallas kernels for 15%

profile of v7, /device:TPU:0, one launch (start us, length us, event | category | flops | bytes accessed | tf_op | source)
XLA Modules:
  0.0 236.3 jit_solution(5294899104088658808)
XLA Ops:
  0.0 1.1 select_reduce_fusion
  5.6 2.7 %dynamic-slice_bitcast_fusion = (bf16[64,8192]{1,0:T(8,128)(2,1)}, bf16[64,8192]{1,0:T(8,128)(2,1)S(1)}) fusion(bf16[4,64,8192]{2,1,0:T(8,128)(2,1)} %param.8, s32[]{:T(128)S(6)} %select_n.151, s32[]{:T(128)S(6)} %select_n.149), kind=kLoop, calls=%fused_computation | loop fusion | bytes 4194312 | tf_op jit(solution)/shard_map/jit(dynamic_index_in_dim)/squeeze | solution.py:296
  8.7 1.5 slice_bitcast_fusion
  10.2 2.6 %collective-permute-start = (bf16[64,8192]{1,0:T(8,128)(2,1)}, bf16[64,8192]{1,0:T(8,128)(2,1)}, u32[]{:S(2)}, u32[]{:S(2)}) collective-permute-start(bf16[64,8192]{1,0:T(8,128)(2,1)} %get-tuple-element.152), channel_id=1, source_target_pairs={{0,4},{4,8},{8,12},{12,14},{14,10},{10,6},{6,2},{2,0},{1,5},{5,9},... | collective-permute-start | bytes 3145736 | tf_op jit(solution)/shard_map/ppermute | solution.py:108
  12.8 2.0 collective-permute-start.5
  14.9 3.0 %pack.1 = bf16[8,2,64,512]{3,2,1,0:T(8,128)(2,1)} custom-call(s32[3]{0:T(128)S(1)} %pad_add_fusion.table, bf16[4,64,8192]{2,1,0:T(8,128)(2,1)} %up.1), custom_call_target="tpu_custom_call" | custom-call | flops 1 | bytes 1 | tf_op jit(solution)/shard_map/pack/pallas_call | solution.py:198
  18.1 5.8 %copy-done.3 = bf16[8192,1024]{1,0:T(8,128)(2,1)S(1)} copy-done((bf16[8192,1024]{1,0:T(8,128)(2,1)S(1)}, bf16[8192,1024]{1,0:T(8,128)(2,1)}, u32[]{:S(2)}) %copy-start.3) | copy-done | bytes 16777240
  23.9 4.0 %pin.1.weights = bf16[8192,1152]{1,0:T(8,128)(2,1)S(1)} custom-call(bf16[8192,1024]{1,0:T(8,128)(2,1)S(1)} %copy-done.3, bf16[64,8192]{1,0:T(8,128)(2,1)S(1)} %get-tuple-element.150.own, bf16[64,8192]{1,0:T(8,128)(2,1)} %collective-permute-done.2.swapped), custom_call_target="tpu_custom_call" | custom-call | flops 1 | bytes 1 | tf_op jit(solution)/shard_map/pin/pallas_call | solution.py:138
  27.9 3.4 %rows.8 = (f32[128,1024]{1,0:T(8,128)S(1)}, bf16[128,128]{1,0:T(8,128)(2,1)S(1)}) custom-call(s32[2,16]{1,0:T(2,128)S(1)} %add_convert_fusion.table, bf16[8192,1152]{1,0:T(8,128)(2,1)S(1)} %pin.1.weights, bf16[128,8192]{1,0:T(8,128)(2,1)S(1)} %bitcast.58, bf16[128,128]{1,0:T(8,128)(2,1)S(1)} %broadcast_in_dim.48.refs_1_), custom_call_target="tpu_custom_call" | custom-call | flops 1 | bytes 1 | tf_op jit(solution)/shard_map/rows/pallas_call | solution.py:175
  31.4 1.6 copy-done.5
  32.9 4.2 %collective-permute-done.refs_0_ = bf16[64,8192]{1,0:T(8,128)(2,1)} collective-permute-done((bf16[64,8192]{1,0:T(8,128)(2,1)}, bf16[64,8192]{1,0:T(8,128)(2,1)}, u32[]{:S(2)}, u32[]{:S(2)}) %collective-permute-start) | collective-permute-done | bytes 1048608 | tf_op jit(solution)/shard_map/ppermute | solution.py:108
  37.1 2.0 collective-permute-done.1.refs_1_
  39.1 1.6 collective-permute-start.3
  41.1 4.4 %rows.9 = (f32[128,1024]{1,0:T(8,128)S(1)}, bf16[128,128]{1,0:T(8,128)(2,1)S(1)}) custom-call(s32[2,16]{1,0:T(2,128)S(1)} %add_convert_fusion.table, bf16[8192,1152]{1,0:T(8,128)(2,1)S(1)} %pin.1.weights, bf16[64,8192]{1,0:T(8,128)(2,1)} %collective-permute-done.refs_0_, bf16[64,8192]{1,0:T(8,128)(2,1)} %collective-permute-done.1.refs_1_, ...), custom_call_target="tpu_custom_call" | custom-call | flops 1 | bytes 1 | tf_op jit(solution)/shard_map/rows/pallas_call | solution.py:175
  45.6 0.8 copy-done.7
  46.4 13.2 %collective-permute-done.5.refs_1_ = bf16[64,8192]{1,0:T(8,128)(2,1)} collective-permute-done((bf16[64,8192]{1,0:T(8,128)(2,1)}, bf16[64,8192]{1,0:T(8,128)(2,1)}, u32[]{:S(2)}, u32[]{:S(2)}) %collective-permute-start.5) | collective-permute-done | bytes 1048608 | tf_op jit(solution)/shard_map/ppermute | solution.py:108
  59.6 2.0 collective-permute-done.6.refs_0_
  61.6 2.0 collective-permute-start.9
  63.6 4.4 %rows.10 = (f32[128,1024]{1,0:T(8,128)S(1)}, bf16[128,128]{1,0:T(8,128)(2,1)S(1)}) custom-call(s32[2,16]{1,0:T(2,128)S(1)} %add_convert_fusion.table, bf16[8192,1152]{1,0:T(8,128)(2,1)S(1)} %pin.1.weights, bf16[64,8192]{1,0:T(8,128)(2,1)} %collective-permute-done.6.refs_0_, bf16[64,8192]{1,0:T(8,128)(2,1)} %collective-permute-done.5.refs_1_, ...), custom_call_target="tpu_custom_call" | custom-call | flops 1 | bytes 1 | tf_op jit(solution)/shard_map/rows/pallas_call | solution.py:175
  68.0 0.8 copy-done.9
  68.8 13.1 %collective-permute-done.3.refs_0_ = bf16[64,8192]{1,0:T(8,128)(2,1)S(1)} collective-permute-done((bf16[64,8192]{1,0:T(8,128)(2,1)}, bf16[64,8192]{1,0:T(8,128)(2,1)S(1)}, u32[]{:S(2)}, u32[]{:S(2)}) %collective-permute-start.3) | collective-permute-done | bytes 1048608 | tf_op jit(solution)/shard_map/ppermute | solution.py:108
  82.0 2.0 collective-permute-done.4.refs_1_
  83.9 1.6 collective-permute-start.7
  85.9 3.5 %rows.11 = (f32[128,1024]{1,0:T(8,128)S(1)}, bf16[128,128]{1,0:T(8,128)(2,1)S(1)}) custom-call(s32[2,16]{1,0:T(2,128)S(1)} %add_convert_fusion.table, bf16[8192,1152]{1,0:T(8,128)(2,1)S(1)} %pin.1.weights, bf16[64,8192]{1,0:T(8,128)(2,1)S(1)} %collective-permute-done.3.refs_0_, bf16[64,8192]{1,0:T(8,128)(2,1)S(1)} %collective-permute-done.4.refs_1_, ...), custom_call_target="tpu_custom_call" | custom-call | flops 1 | bytes 1 | tf_op jit(solution)/shard_map/rows/pallas_call | solution.py:175
  89.4 17.0 %collective-permute-done.10.refs_0_ = bf16[64,8192]{1,0:T(8,128)(2,1)S(1)} collective-permute-done((bf16[64,8192]{1,0:T(8,128)(2,1)}, bf16[64,8192]{1,0:T(8,128)(2,1)S(1)}, u32[]{:S(2)}, u32[]{:S(2)}) %collective-permute-start.10) | collective-permute-done | bytes 1048608 | tf_op jit(solution)/shard_map/ppermute | solution.py:108
  106.4 3.4 %rows.12 = (f32[128,1024]{1,0:T(8,128)S(1)}, bf16[128,128]{1,0:T(8,128)(2,1)S(1)}) custom-call(s32[2,16]{1,0:T(2,128)S(1)} %add_convert_fusion.table, bf16[8192,1152]{1,0:T(8,128)(2,1)S(1)} %pin.1.weights, bf16[64,8192]{1,0:T(8,128)(2,1)S(1)} %collective-permute-done.10.refs_0_, bf16[64,8192]{1,0:T(8,128)(2,1)S(1)} %collective-permute-done.9.refs_1_, ...), custom_call_target="tpu_custom_call" | custom-call | flops 1 | bytes 1 | tf_op jit(solution)/shard_map/rows/pallas_call | solution.py:175
  109.9 0.8 copy-done.13
  110.6 16.2 %collective-permute-done.7.refs_0_ = bf16[64,8192]{1,0:T(8,128)(2,1)} collective-permute-done((bf16[64,8192]{1,0:T(8,128)(2,1)S(1)}, bf16[64,8192]{1,0:T(8,128)(2,1)}, u32[]{:S(2)}, u32[]{:S(2)}) %collective-permute-start.7) | collective-permute-done | bytes 1048608 | tf_op jit(solution)/shard_map/ppermute | solution.py:108
  126.8 1.4 collective-permute-done.8.refs_1_
  128.3 5.0 %all-to-all-start = ((bf16[16,64,512]{2,1,0:T(8,128)(2,1)}), bf16[16,64,512]{2,1,0:T(8,128)(2,1)S(1)}, u32[]{:S(2)}, u32[]{:S(2)}) async-start(bf16[16,64,512]{2,1,0:T(8,128)(2,1)} %bitcast.28), calls=%async_computation | async-start | bytes 2097152 | tf_op jit(solution)/shard_map/all_to_all | solution.py:328
  133.3 1.9 collective-permute-start.13
  135.4 1.9 collective-permute-start.11
  137.7 6.4 %copy-done.1 = bf16[8192,1152]{1,0:T(8,128)(2,1)S(1)} copy-done((bf16[8192,1152]{1,0:T(8,128)(2,1)S(1)}, bf16[8192,1152]{1,0:T(8,128)(2,1)}, u32[]{:S(2)}) %copy-start.1) | copy-done | bytes 18874392
  144.1 4.4 %rows.13 = (f32[128,1024]{1,0:T(8,128)S(1)}, bf16[128,128]{1,0:T(8,128)(2,1)S(1)}) custom-call(s32[2,16]{1,0:T(2,128)S(1)} %add_convert_fusion.table, bf16[8192,1152]{1,0:T(8,128)(2,1)S(1)} %copy-done.1, bf16[64,8192]{1,0:T(8,128)(2,1)} %collective-permute-done.7.refs_0_, bf16[64,8192]{1,0:T(8,128)(2,1)} %collective-permute-done.8.refs_1_, ...), custom_call_target="tpu_custom_call" | custom-call | flops 1 | bytes 1 | tf_op jit(solution)/shard_map/rows/pallas_call | solution.py:175
  148.5 0.8 copy-done.15
  149.3 24.7 %collective-permute-done.13.refs_1_ = bf16[64,8192]{1,0:T(8,128)(2,1)} collective-permute-done((bf16[64,8192]{1,0:T(8,128)(2,1)S(1)}, bf16[64,8192]{1,0:T(8,128)(2,1)}, u32[]{:S(2)}, u32[]{:S(2)}) %collective-permute-start.13) | collective-permute-done | bytes 1048608 | tf_op jit(solution)/shard_map/ppermute | solution.py:108
  174.0 2.3 collective-permute-done.14.refs_0_
  176.3 4.4 %rows.14 = (f32[128,1024]{1,0:T(8,128)S(1)}, bf16[128,128]{1,0:T(8,128)(2,1)S(1)}) custom-call(s32[2,16]{1,0:T(2,128)S(1)} %add_convert_fusion.table, bf16[8192,1152]{1,0:T(8,128)(2,1)S(1)} %copy-done.1, bf16[64,8192]{1,0:T(8,128)(2,1)} %collective-permute-done.14.refs_0_, bf16[64,8192]{1,0:T(8,128)(2,1)} %collective-permute-done.13.refs_1_, ...), custom_call_target="tpu_custom_call" | custom-call | flops 1 | bytes 1 | tf_op jit(solution)/shard_map/rows/pallas_call | solution.py:175
  180.8 15.7 %collective-permute-done.11.refs_0_ = bf16[64,8192]{1,0:T(8,128)(2,1)} collective-permute-done((bf16[64,8192]{1,0:T(8,128)(2,1)}, bf16[64,8192]{1,0:T(8,128)(2,1)}, u32[]{:S(2)}, u32[]{:S(2)}) %collective-permute-start.11) | collective-permute-done | bytes 1048608 | tf_op jit(solution)/shard_map/ppermute | solution.py:108
  196.4 1.9 collective-permute-done.12.refs_1_
  198.3 6.4 %copy-done.2 = bf16[8192,1152]{1,0:T(8,128)(2,1)S(1)} copy-done((bf16[8192,1152]{1,0:T(8,128)(2,1)S(1)}, bf16[8192,1152]{1,0:T(8,128)(2,1)}, u32[]{:S(2)}) %copy-start.2) | copy-done | bytes 18874392
  204.7 4.6 %rows.15 = (f32[128,1024]{1,0:T(8,128)S(1)}, bf16[128,128]{1,0:T(8,128)(2,1)S(1)}) custom-call(s32[2,16]{1,0:T(2,128)S(1)} %add_convert_fusion.table, bf16[8192,1152]{1,0:T(8,128)(2,1)S(1)} %copy-done.2, bf16[64,8192]{1,0:T(8,128)(2,1)} %collective-permute-done.11.refs_0_, bf16[64,8192]{1,0:T(8,128)(2,1)} %collective-permute-done.12.refs_1_, ...), custom_call_target="tpu_custom_call" | custom-call | flops 1 | bytes 1 | tf_op jit(solution)/shard_map/rows/pallas_call | solution.py:175
  209.3 1.6 collective-permute-start.15
  211.6 1.6 collective-permute-start.19
  213.3 7.2 %collective-permute-start.16 = (bf16[2,128,128]{2,1,0:T(8,128)(2,1)S(1)}, bf16[2,128,128]{2,1,0:T(8,128)(2,1)S(1)}, u32[]{:S(2)}, u32[]{:S(2)}) collective-permute-start(bf16[2,128,128]{2,1,0:T(8,128)(2,1)S(1)} %pad_maximum_fusion), channel_id=1, source_target_pairs={{0,4},{2,6},{4,0},{6,2},{8,12},{10,14},{12,8},{14,10},{1,5},{3,7},... | collective-permute-start | bytes 196616 | tf_op jit(solution)/shard_map/ppermute | solution.py:108
  220.7 2.3 collective-permute-start.18
  223.0 4.4 %collective-permute-done.17 = bf16[2,128,128]{2,1,0:T(8,128)(2,1)S(1)} collective-permute-done((bf16[2,128,128]{2,1,0:T(8,128)(2,1)S(1)}, bf16[2,128,128]{2,1,0:T(8,128)(2,1)S(1)}, u32[]{:S(2)}, u32[]{:S(2)}) %collective-permute-start.17) | collective-permute-done | bytes 65568 | tf_op jit(solution)/shard_map/ppermute | solution.py:108
  227.5 8.8 %finish.1 = bf16[1024,1024]{1,0:T(8,128)(2,1)} custom-call(s32[4,16]{1,0:T(4,128)S(1)} %add_add_fusion.table, f32[128,1024]{1,0:T(8,128)S(1)} %copy-done.6, f32[128,1024]{1,0:T(8,128)S(1)} %copy-done.8, f32[128,1024]{1,0:T(8,128)S(1)} %copy-done.10, f32[128,1024]{1,0:T(8,128)S(1)} %copy-done.12, f32[128,1024]{1,0:T(8,128)S(1)} %copy-done.14, ...), custom_call_target="tpu_custom_call" | custom-call | flops 1 | bytes 1 | tf_op jit(solution)/shard_map/finish/pallas_call | solution.py:257
  (63 shorter events, 4.2 us)
Async XLA Ops:
  0.0 8.7 %copy-start.4 = (bf16[1,128,8192]{2,1,0:T(8,128)(2,1)S(1)}, bf16[1,128,8192]{2,1,0:T(8,128)(2,1)}, u32[]{:S(2)}) copy-start(bf16[1,128,8192]{2,1,0:T(8,128)(2,1)} %param.6) | copy-start | bytes 6291460
  8.2 9.9 %collective-permute-start.2 = (bf16[64,8192]{1,0:T(8,128)(2,1)}, bf16[64,8192]{1,0:T(8,128)(2,1)}, u32[]{:S(2)}, u32[]{:S(2)}) collective-permute-start(bf16[64,8192]{1,0:T(8,128)(2,1)} %get-tuple-element.149), channel_id=1, source_target_pairs={{0,1},{1,0},{2,3},{3,2},{4,5},{5,4},{6,7},{7,6},{8,9},{9,8},{10,11... | collective-permute-start | bytes 3145736 | tf_op jit(solution)/shard_map/ppermute | solution.py:112
  10.2 26.9 %collective-permute-start = (bf16[64,8192]{1,0:T(8,128)(2,1)}, bf16[64,8192]{1,0:T(8,128)(2,1)}, u32[]{:S(2)}, u32[]{:S(2)}) collective-permute-start(bf16[64,8192]{1,0:T(8,128)(2,1)} %get-tuple-element.152), channel_id=1, source_target_pairs={{0,4},{4,8},{8,12},{12,14},{14,10},{10,6},{6,2},{2,0},{1,5},{5,9},... | collective-permute-start | bytes 3145736 | tf_op jit(solution)/shard_map/ppermute | solution.py:108
  12.8 26.3 %collective-permute-start.1 = (bf16[64,8192]{1,0:T(8,128)(2,1)}, bf16[64,8192]{1,0:T(8,128)(2,1)}, u32[]{:S(2)}, u32[]{:S(2)}) collective-permute-start(bf16[64,8192]{1,0:T(8,128)(2,1)} %get-tuple-element.151), channel_id=1, source_target_pairs={{4,0},{8,4},{12,8},{14,12},{10,14},{6,10},{2,6},{0,2},{5,1},{9,5},... | collective-permute-start | bytes 3145736 | tf_op jit(solution)/shard_map/ppermute | solution.py:108
  12.8 46.8 %collective-permute-start.5 = (bf16[64,8192]{1,0:T(8,128)(2,1)}, bf16[64,8192]{1,0:T(8,128)(2,1)}, u32[]{:S(2)}, u32[]{:S(2)}) collective-permute-start(bf16[64,8192]{1,0:T(8,128)(2,1)} %get-tuple-element.151), channel_id=1, source_target_pairs={{0,4},{4,8},{8,12},{12,14},{14,10},{10,6},{6,2},{2,0},{1,5},{5,9},... | collective-permute-start | bytes 3145736 | tf_op jit(solution)/shard_map/ppermute | solution.py:108
  14.8 46.8 %collective-permute-start.6 = (bf16[64,8192]{1,0:T(8,128)(2,1)}, bf16[64,8192]{1,0:T(8,128)(2,1)}, u32[]{:S(2)}, u32[]{:S(2)}) collective-permute-start(bf16[64,8192]{1,0:T(8,128)(2,1)} %get-tuple-element.152), channel_id=1, source_target_pairs={{4,0},{8,4},{12,8},{14,12},{10,14},{6,10},{2,6},{0,2},{5,1},{9,5},... | collective-permute-start | bytes 3145736 | tf_op jit(solution)/shard_map/ppermute | solution.py:108
  18.1 5.8 %copy-start.3 = (bf16[8192,1024]{1,0:T(8,128)(2,1)S(1)}, bf16[8192,1024]{1,0:T(8,128)(2,1)}, u32[]{:S(2)}) copy-start(bf16[8192,1024]{1,0:T(8,128)(2,1)} %weight.1) | copy-start | bytes 50331652
  27.9 78.5 %copy-start = (bf16[8192,1152]{1,0:T(8,128)(2,1)}, bf16[8192,1152]{1,0:T(8,128)(2,1)S(1)}, u32[]{:S(2)}) copy-start(bf16[8192,1152]{1,0:T(8,128)(2,1)S(1)} %pin.1.weights) | copy-start | bytes 56623108
  31.4 1.6 copy-start.5
  39.1 42.9 %collective-permute-start.3 = (bf16[64,8192]{1,0:T(8,128)(2,1)}, bf16[64,8192]{1,0:T(8,128)(2,1)S(1)}, u32[]{:S(2)}, u32[]{:S(2)}) collective-permute-start(bf16[64,8192]{1,0:T(8,128)(2,1)} %collective-permute-done.refs_0_), channel_id=1, source_target_pairs={{0,4},{4,8},{8,12},{12,14},{14,10},{10,6},{6,2},{2,0},{1,5},{5,9},... | collective-permute-start | bytes 3145736 | tf_op jit(solution)/shard_map/ppermute | solution.py:108
  40.7 43.3 %collective-permute-start.4 = (bf16[64,8192]{1,0:T(8,128)(2,1)}, bf16[64,8192]{1,0:T(8,128)(2,1)S(1)}, u32[]{:S(2)}, u32[]{:S(2)}) collective-permute-start(bf16[64,8192]{1,0:T(8,128)(2,1)} %collective-permute-done.1.refs_1_), channel_id=1, source_target_pairs={{4,0},{8,4},{12,8},{14,12},{10,14},{6,10},{2,6},{0,2},{5,1},{9,5},... | collective-permute-start | bytes 3145736 | tf_op jit(solution)/shard_map/ppermute | solution.py:108
  45.6 0.8 copy-start.7
  61.6 44.8 %collective-permute-start.10 = (bf16[64,8192]{1,0:T(8,128)(2,1)}, bf16[64,8192]{1,0:T(8,128)(2,1)S(1)}, u32[]{:S(2)}, u32[]{:S(2)}) collective-permute-start(bf16[64,8192]{1,0:T(8,128)(2,1)} %collective-permute-done.6.refs_0_), channel_id=1, source_target_pairs={{4,0},{8,4},{12,8},{14,12},{10,14},{6,10},{2,6},{0,2},{5,1},{9,5},... | collective-permute-start | bytes 3145736 | tf_op jit(solution)/shard_map/ppermute | solution.py:108
  61.6 44.8 %collective-permute-start.9 = (bf16[64,8192]{1,0:T(8,128)(2,1)}, bf16[64,8192]{1,0:T(8,128)(2,1)S(1)}, u32[]{:S(2)}, u32[]{:S(2)}) collective-permute-start(bf16[64,8192]{1,0:T(8,128)(2,1)} %collective-permute-done.5.refs_1_), channel_id=1, source_target_pairs={{0,4},{4,8},{8,12},{12,14},{14,10},{10,6},{6,2},{2,0},{1,5},{5,9},... | collective-permute-start | bytes 3145736 | tf_op jit(solution)/shard_map/ppermute | solution.py:108
  68.0 0.8 copy-start.9
  83.9 42.9 %collective-permute-start.7 = (bf16[64,8192]{1,0:T(8,128)(2,1)S(1)}, bf16[64,8192]{1,0:T(8,128)(2,1)}, u32[]{:S(2)}, u32[]{:S(2)}) collective-permute-start(bf16[64,8192]{1,0:T(8,128)(2,1)S(1)} %collective-permute-done.3.refs_0_), channel_id=1, source_target_pairs={{0,4},{4,8},{8,12},{12,14},{14,10},{10,6},{6,2},{2,0},{1,5},{5,9},... | collective-permute-start | bytes 3145736 | tf_op jit(solution)/shard_map/ppermute | solution.py:108
  85.5 42.8 %collective-permute-start.8 = (bf16[64,8192]{1,0:T(8,128)(2,1)S(1)}, bf16[64,8192]{1,0:T(8,128)(2,1)}, u32[]{:S(2)}, u32[]{:S(2)}) collective-permute-start(bf16[64,8192]{1,0:T(8,128)(2,1)S(1)} %collective-permute-done.4.refs_1_), channel_id=1, source_target_pairs={{4,0},{8,4},{12,8},{14,12},{10,14},{6,10},{2,6},{0,2},{5,1},{9,5},... | collective-permute-start | bytes 3145736 | tf_op jit(solution)/shard_map/ppermute | solution.py:108
  89.4 20.4 %copy-start.11 = (f32[128,1024]{1,0:T(8,128)}, f32[128,1024]{1,0:T(8,128)S(1)}, u32[]{:S(2)}) copy-start(f32[128,1024]{1,0:T(8,128)S(1)} %get-tuple-element.137.refs_3_) | copy-start | bytes 1572868
  109.9 0.8 copy-start.13
  128.3 70.1 %all-to-all-start = ((bf16[16,64,512]{2,1,0:T(8,128)(2,1)}), bf16[16,64,512]{2,1,0:T(8,128)(2,1)S(1)}, u32[]{:S(2)}, u32[]{:S(2)}) async-start(bf16[16,64,512]{2,1,0:T(8,128)(2,1)} %bitcast.28), calls=%async_computation | async-start | bytes 2097152 | tf_op jit(solution)/shard_map/all_to_all | solution.py:328
  133.3 40.7 %collective-permute-start.13 = (bf16[64,8192]{1,0:T(8,128)(2,1)S(1)}, bf16[64,8192]{1,0:T(8,128)(2,1)}, u32[]{:S(2)}, u32[]{:S(2)}) collective-permute-start(bf16[64,8192]{1,0:T(8,128)(2,1)S(1)} %collective-permute-done.9.refs_1_), channel_id=1, source_target_pairs={{0,4},{4,8},{8,12},{12,14},{14,10},{10,6},{6,2},{2,0},{1,5},{5,9},... | collective-permute-start | bytes 3145736 | tf_op jit(solution)/shard_map/ppermute | solution.py:108
  135.2 41.1 %collective-permute-start.14 = (bf16[64,8192]{1,0:T(8,128)(2,1)S(1)}, bf16[64,8192]{1,0:T(8,128)(2,1)}, u32[]{:S(2)}, u32[]{:S(2)}) collective-permute-start(bf16[64,8192]{1,0:T(8,128)(2,1)S(1)} %collective-permute-done.10.refs_0_), channel_id=1, source_target_pairs={{4,0},{8,4},{12,8},{14,12},{10,14},{6,10},{2,6},{0,2},{5,1},{9,5},... | collective-permute-start | bytes 3145736 | tf_op jit(solution)/shard_map/ppermute | solution.py:108
  135.4 61.0 %collective-permute-start.11 = (bf16[64,8192]{1,0:T(8,128)(2,1)}, bf16[64,8192]{1,0:T(8,128)(2,1)}, u32[]{:S(2)}, u32[]{:S(2)}) collective-permute-start(bf16[64,8192]{1,0:T(8,128)(2,1)} %collective-permute-done.7.refs_0_), channel_id=1, source_target_pairs={{0,4},{4,8},{8,12},{12,14},{14,10},{10,6},{6,2},{2,0},{1,5},{5,9},... | collective-permute-start | bytes 3145736 | tf_op jit(solution)/shard_map/ppermute | solution.py:108
  137.2 61.1 %collective-permute-start.12 = (bf16[64,8192]{1,0:T(8,128)(2,1)}, bf16[64,8192]{1,0:T(8,128)(2,1)}, u32[]{:S(2)}, u32[]{:S(2)}) collective-permute-start(bf16[64,8192]{1,0:T(8,128)(2,1)} %collective-permute-done.8.refs_1_), channel_id=1, source_target_pairs={{4,0},{8,4},{12,8},{14,12},{10,14},{6,10},{2,6},{0,2},{5,1},{9,5},... | collective-permute-start | bytes 3145736 | tf_op jit(solution)/shard_map/ppermute | solution.py:108
  137.7 6.4 %copy-start.1 = (bf16[8192,1152]{1,0:T(8,128)(2,1)S(1)}, bf16[8192,1152]{1,0:T(8,128)(2,1)}, u32[]{:S(2)}) copy-start(bf16[8192,1152]{1,0:T(8,128)(2,1)} %copy-done) | copy-start | bytes 56623108
  148.5 0.8 copy-start.15
  198.3 6.4 %copy-start.2 = (bf16[8192,1152]{1,0:T(8,128)(2,1)S(1)}, bf16[8192,1152]{1,0:T(8,128)(2,1)}, u32[]{:S(2)}) copy-start(bf16[8192,1152]{1,0:T(8,128)(2,1)} %copy-done) | copy-start | bytes 56623108
  204.7 22.8 %copy-start.6 = (f32[128,1024]{1,0:T(8,128)S(1)}, f32[128,1024]{1,0:T(8,128)}, u32[]{:S(2)}) copy-start(f32[128,1024]{1,0:T(8,128)} %copy-done.5) | copy-start | bytes 1572868
  204.7 22.8 %copy-start.8 = (f32[128,1024]{1,0:T(8,128)S(1)}, f32[128,1024]{1,0:T(8,128)}, u32[]{:S(2)}) copy-start(f32[128,1024]{1,0:T(8,128)} %copy-done.7) | copy-start | bytes 1572868
  204.7 22.8 %copy-start.10 = (f32[128,1024]{1,0:T(8,128)S(1)}, f32[128,1024]{1,0:T(8,128)}, u32[]{:S(2)}) copy-start(f32[128,1024]{1,0:T(8,128)} %copy-done.9) | copy-start | bytes 1572868
  204.7 22.8 %copy-start.12 = (f32[128,1024]{1,0:T(8,128)S(1)}, f32[128,1024]{1,0:T(8,128)}, u32[]{:S(2)}) copy-start(f32[128,1024]{1,0:T(8,128)} %copy-done.11) | copy-start | bytes 1572868
  204.7 22.8 %copy-start.14 = (f32[128,1024]{1,0:T(8,128)S(1)}, f32[128,1024]{1,0:T(8,128)}, u32[]{:S(2)}) copy-start(f32[128,1024]{1,0:T(8,128)} %copy-done.13) | copy-start | bytes 1572868
  204.7 22.8 %copy-start.16 = (f32[128,1024]{1,0:T(8,128)S(1)}, f32[128,1024]{1,0:T(8,128)}, u32[]{:S(2)}) copy-start(f32[128,1024]{1,0:T(8,128)} %copy-done.15) | copy-start | bytes 1572868
  209.3 4.0 %collective-permute-start.15 = (bf16[128,128]{1,0:T(8,128)(2,1)S(1)}, bf16[128,128]{1,0:T(8,128)(2,1)S(1)}, u32[]{:S(2)}, u32[]{:S(2)}) collective-permute-start(bf16[128,128]{1,0:T(8,128)(2,1)S(1)} %get-tuple-element.145), channel_id=1, source_target_pairs={{0,2},{2,0},{4,6},{6,4},{8,10},{10,8},{12,14},{14,12},{1,3},{3,1},... | collective-permute-start | bytes 98312 | tf_op jit(solution)/shard_map/ppermute | solution.py:108
  211.6 15.9 %collective-permute-start.19 = (bf16[8,64,512]{2,1,0:T(8,128)(2,1)S(1)}, bf16[8,64,512]{2,1,0:T(8,128)(2,1)S(1)}, u32[]{:S(2)}, u32[]{:S(2)}) collective-permute-start(bf16[8,64,512]{2,1,0:T(8,128)(2,1)S(1)} %take.1.refs_9_), channel_id=1, source_target_pairs={{0,16},{16,0},{1,17},{17,1},{2,18},{18,2},{3,19},{19,3},{4,20},{20... | collective-permute-start | bytes 1572872 | tf_op jit(solution)/shard_map/ppermute | solution.py:112
  213.3 9.7 %collective-permute-start.16 = (bf16[2,128,128]{2,1,0:T(8,128)(2,1)S(1)}, bf16[2,128,128]{2,1,0:T(8,128)(2,1)S(1)}, u32[]{:S(2)}, u32[]{:S(2)}) collective-permute-start(bf16[2,128,128]{2,1,0:T(8,128)(2,1)S(1)} %pad_maximum_fusion), channel_id=1, source_target_pairs={{0,4},{2,6},{4,0},{6,2},{8,12},{10,14},{12,8},{14,10},{1,5},{3,7},... | collective-permute-start | bytes 196616 | tf_op jit(solution)/shard_map/ppermute | solution.py:108
  220.5 6.9 %collective-permute-start.17 = (bf16[2,128,128]{2,1,0:T(8,128)(2,1)S(1)}, bf16[2,128,128]{2,1,0:T(8,128)(2,1)S(1)}, u32[]{:S(2)}, u32[]{:S(2)}) collective-permute-start(bf16[2,128,128]{2,1,0:T(8,128)(2,1)S(1)} %pad_maximum_fusion), channel_id=1, source_target_pairs={{0,8},{2,10},{4,12},{6,14},{8,0},{10,2},{12,4},{14,6},{1,9},{3,11}... | collective-permute-start | bytes 196616 | tf_op jit(solution)/shard_map/ppermute | solution.py:108
  220.7 6.8 %collective-permute-start.18 = (bf16[2,128,128]{2,1,0:T(8,128)(2,1)S(1)}, bf16[2,128,128]{2,1,0:T(8,128)(2,1)S(1)}, u32[]{:S(2)}, u32[]{:S(2)}) collective-permute-start(bf16[2,128,128]{2,1,0:T(8,128)(2,1)S(1)} %pad_maximum_fusion), channel_id=1, source_target_pairs={{0,12},{2,14},{4,8},{6,10},{8,4},{10,6},{12,0},{14,2},{1,13},{3,15... | collective-permute-start | bytes 196616 | tf_op jit(solution)/shard_map/ppermute | solution.py:108

commit v8 on v7

--- a/solution.py
+++ b/solution.py
@@ -230,40 +230,37 @@
 
 
 def finish_kernel(table, *refs):
-    *bases, shrunk, up_mine, up_other, out = refs
-    at = pl.program_id(0)
+    *bases, shrunk, up_mine, up_other, out, rows, sems = refs
     part = up_mine.shape[2]
-    both = shrunk[0].astype(jnp.float32)
-    value = jnp.where(table[2, at] > 0, both[:, 64:], both[:, :64]).astype(jnp.bfloat16)
-    group = table[3, at]
-    for g, base in enumerate(bases):
-
-        @pl.when(at // 2 == g)
-        def _():
-            for up, side in ((up_mine, group), (up_other, 1 - group)):
-                cut = pl.ds(pl.multiple_of(side * part, part), part)
-                grown = jnp.dot(value, up[0], preferred_element_type=jnp.float32)
-                out[:, cut] = (base[:, cut] + 0.5 * grown).astype(out.dtype)
+    group = table[3, 0]
+    copies = []
+    for i in range(16):
+        block, half = table[0, i], i % 2
+        own = pl.ds(half * HALF, HALF)
+        both = shrunk[table[1, i], own, :].astype(jnp.float32)
+        value = jnp.where(table[2, i] > 0, both[:, 64:], both[:, :64]).astype(jnp.bfloat16)
+        for up, side in ((up_mine, group), (up_other, 1 - group)):
+            cut = pl.ds(pl.multiple_of(side * part, part), part)
+            grown = jnp.dot(value, up[block], preferred_element_type=jnp.float32)
+            rows[i, :, cut] = (bases[i // 2][own, cut] + 0.5 * grown).astype(rows.dtype)
+        to = pl.ds(pl.multiple_of((2 * block + half) * HALF, HALF), HALF)
+        copies.append(pltpu.make_async_copy(rows.at[i], out.at[to], sems.at[i]))
+        copies[-1].start()
+    for copy in copies:
+        copy.wait()
 
 
 def finish_call(table, bases, shrunk, up_mine, up_other):
     columns = bases[0].shape[1]
-    _, rank, part = up_mine.shape
-
-    def base_spec(g):
-        return pl.BlockSpec((HALF, columns), lambda i, t: (jnp.clip(i - 2 * g, 0, 1), 0))
-
-    up = pl.BlockSpec((1, rank, part), lambda i, t: (t[0, i], 0, 0))
     return pl.pallas_call(
         finish_kernel,
-        grid_spec=pltpu.PrefetchScalarGridSpec(
-            num_scalar_prefetch=1,
-            grid=(16,),
-            in_specs=[base_spec(g) for g in range(8)]
-            + [pl.BlockSpec((1, HALF, 2 * rank), lambda i, t: (t[1, i], i % 2, 0)), up, up],
-            out_specs=pl.BlockSpec((HALF, columns), lambda i, t: (2 * t[0, i] + i % 2, 0)),
-        ),
+        in_specs=[pl.BlockSpec(memory_space=pltpu.SMEM)] + in_vmem(11),
+        out_specs=pl.BlockSpec(memory_space=pltpu.HBM),
         out_shape=jax.ShapeDtypeStruct((8 * BLOCK, columns), jnp.bfloat16),
+        scratch_shapes=[
+            pltpu.VMEM((16, HALF, columns), jnp.bfloat16),
+            pltpu.SemaphoreType.DMA((16,)),
+        ],
         name="finish",
         **settings(),
     )(table, *bases, shrunk, up_mine, up_other)
@@ -283,6 +280,12 @@
 
     ahead, back = list(halves), list(halves[::-1])
     flight = [(send(ahead[k], AHEAD), send(back[k], BACK)) for k in range(2)]
+    got, ahead, back, adapter_home_slot, adapter_per_block = lax.optimization_barrier(
+        (flight[0], ahead, back, adapter_home_slot, adapter_per_block)
+    )
+    ahead.append(got[0])
+    back.append(got[1])
+    flight.append((send(ahead[2], AHEAD), send(back[2], BACK)))
 
     store_slots = find_slots(adapter_home_slot, adapter_per_block)
     owner = store_slots // held
@@ -294,7 +297,8 @@
 
     down_own = lax.dynamic_index_in_dim(adapter_down_maps, pick_own, 0, keepdims=False)
     down_lent = lax.dynamic_index_in_dim(adapter_down_maps, pick_lent, 0, keepdims=False)
-    weights = pin_call(query_weight, down_own, swap(down_lent, "store"))
+    down_swapped = swap(down_lent, "store")
+    weights = pin_call(query_weight, down_own, down_swapped)
     up_sent = pack_call(jnp.concatenate([picked, group[None]]).astype(jnp.int32), adapter_up_maps)
 
     position = jnp.where(y == 0, z, 7 - z)
@@ -310,33 +314,25 @@
 
     bases = []
     shrunk = jnp.zeros((BLOCK, 2 * rank), jnp.bfloat16)
-    pieces = [rows]
-    extra = {"up": up_sent}
-    for k in range(7):
-        base, shrunk = rows_call(k, table, weights, pieces, shrunk)
-        bases.append(base)
-        if k == 6:
-            extra["up"] = up_got
-        (got_ahead, got_back), ahead, back, bases, shrunk, extra = lax.optimization_barrier(
-            (flight[k], ahead, back, bases, shrunk, extra)
+    groups = [[rows], [ahead[2], back[2]]]
+    for k in range(1, 7):
+        (got_ahead, got_back), ahead, back, bases, shrunk, up_sent = lax.optimization_barrier(
+            (flight[k], ahead, back, bases, shrunk, up_sent)
         )
         ahead.append(got_ahead)
         back.append(got_back)
         if k < 5:
             flight.append((send(ahead[k + 2], AHEAD), send(back[k + 2], BACK)))
-        if k == 4:
-            up_got = lax.all_to_all(
-                extra["up"].reshape(16, rank, -1),
-                ("tensor", "store"),
-                split_axis=0,
-                concat_axis=0,
-                tiled=True,
-            )
-        pieces = [got_ahead, got_back] if k % 2 == 0 else [got_back, got_ahead]
-    base, shrunk = rows_call(7, table, weights, pieces, shrunk)
-    bases.append(base)
-
-    up_mine = take_call(owner_row, extra["up"])
+        groups.append([got_ahead, got_back] if k % 2 == 0 else [got_back, got_ahead])
+        for g in range(len(bases), min(len(bases) + 2, k + 2)):
+            base, shrunk = rows_call(g, table, weights, groups[g], shrunk)
+            bases.append(base)
+    shrunk, up_sent = lax.optimization_barrier((shrunk, up_sent))
+    up_got = lax.all_to_all(
+        up_sent.reshape(16, rank, -1), ("tensor", "store"), split_axis=0, concat_axis=0, tiled=True
+    )
+
+    up_mine = take_call(owner_row, up_got)
     up_other = swap(up_mine, "groups")
     pair = jnp.stack([shrunk, send(shrunk, ACROSS)])
     everyone = jnp.concatenate([pair] + [send(pair, pairs) for pairs in ALONG])

time: 238 us -> 224 us (0.941)
  the two profiles are of different devices: /device:TPU:0 before, /device:TPU:13 now
where the time goes in v8:
time: 224 us
  waiting for transfers between devices  130 us (58%)
  Pallas kernels  39.3 us (18%)
  starting transfers between devices  25.8 us (12%)
  local copies, waits for them, and re-layouts  24 us (11%)
  between operations  4.25 us (2%)
    ppermute x18, waiting for transfers between devices, send(): return lax.ppermute(value, 'tensor', pairs)  101 us
    pallas_call x8, Pallas kernels, rows_call(): pl.pallas_call(functools.partial(rows_kernel, group), in_specs=[pl.BlockS...  30.6 us
    all_to_all x1, waiting for transfers between devices, chain_body(): lax.all_to_all(up_sent.reshape(16, rank, -1), ('tensor', 'store'), split_...  19.1 us
    unnamed x36, local copies, waits for them, and re-layouts  16.4 us
    ppermute x18, starting transfers between devices, send(): return lax.ppermute(value, 'tensor', pairs)  13.5 us
    ppermute x2, waiting for transfers between devices, swap(): return lax.ppermute(value, axis, [(0, 1), (1, 0)])  9.94 us
    all_to_all x1, starting transfers between devices, chain_body(): lax.all_to_all(up_sent.reshape(16, rank, -1), ('tensor', 'store'), split_...  7.84 us
  transfers between devices with their start and end apart: 21, of which 11 were waited for; matrix products, arithmetic and copies ran while one was open for 3% of the time, Pallas kernels for 15%

profile of v8, /device:TPU:13, one launch (start us, length us, event | category | flops | bytes accessed | tf_op | source)
XLA Modules:
  0.0 223.6 jit_solution(15861771824180984270)
XLA Ops:
  0.0 3.1 %slice_bitcast_fusion = (bf16[64,8192]{1,0:T(8,128)(2,1)}, bf16[64,8192]{1,0:T(8,128)(2,1)}) fusion(bf16[1,128,8192]{2,1,0:T(8,128)(2,1)} %param.6), kind=kLoop, calls=%fused_computation.2 | loop fusion | bytes 4194304 | tf_op jit(solution)/shard_map/slice | solution.py:279
  3.3 1.3 collective-permute-start.1
  4.7 1.3 collective-permute-start.5
  6.0 21.4 %collective-permute-done.refs_0_ = bf16[64,8192]{1,0:T(8,128)(2,1)} collective-permute-done((bf16[64,8192]{1,0:T(8,128)(2,1)}, bf16[64,8192]{1,0:T(8,128)(2,1)}, u32[]{:S(2)}, u32[]{:S(2)}) %collective-permute-start) | collective-permute-done | bytes 1048608 | tf_op jit(solution)/shard_map/ppermute | solution.py:108
  32.2 2.7 %dynamic-slice_bitcast_fusion = (bf16[64,8192]{1,0:T(8,128)(2,1)}, bf16[64,8192]{1,0:T(8,128)(2,1)S(1)}) fusion(bf16[4,64,8192]{2,1,0:T(8,128)(2,1)} %param.8, s32[]{:T(128)S(6)} %select_n.151, s32[]{:T(128)S(6)} %select_n.149), kind=kLoop, calls=%fused_computation | loop fusion | bytes 4194312 | tf_op jit(solution)/shard_map/jit(dynamic_index_in_dim)/squeeze | solution.py:299
  34.9 3.2 %collective-permute-start.6 = (bf16[64,8192]{1,0:T(8,128)(2,1)}, bf16[64,8192]{1,0:T(8,128)(2,1)S(1)}, u32[]{:S(2)}, u32[]{:S(2)}) collective-permute-start(bf16[64,8192]{1,0:T(8,128)(2,1)} %get-tuple-element.147), channel_id=1, source_target_pairs={{0,1},{1,0},{2,3},{3,2},{4,5},{5,4},{6,7},{7,6},{8,9},{9,8},{10,11... | collective-permute-start | bytes 3145736 | tf_op jit(solution)/shard_map/ppermute | solution.py:112
  38.1 1.5 collective-permute-start.3
  39.8 2.9 %pack.1 = bf16[8,2,64,512]{3,2,1,0:T(8,128)(2,1)} custom-call(s32[3]{0:T(128)S(1)} %pad_add_fusion.table, bf16[4,64,8192]{2,1,0:T(8,128)(2,1)} %up.1), custom_call_target="tpu_custom_call" | custom-call | flops 1 | bytes 1 | tf_op jit(solution)/shard_map/pack/pallas_call | solution.py:198
  42.7 7.2 %collective-permute-done.4.refs_1_ = bf16[64,8192]{1,0:T(8,128)(2,1)S(1)} collective-permute-done((bf16[64,8192]{1,0:T(8,128)(2,1)}, bf16[64,8192]{1,0:T(8,128)(2,1)S(1)}, u32[]{:S(2)}, u32[]{:S(2)}) %collective-permute-start.4) | collective-permute-done | bytes 1048608 | tf_op jit(solution)/shard_map/ppermute | solution.py:108
  49.9 1.3 collective-permute-start.10
  51.5 5.8 %copy-done = bf16[8192,1024]{1,0:T(8,128)(2,1)S(1)} copy-done((bf16[8192,1024]{1,0:T(8,128)(2,1)S(1)}, bf16[8192,1024]{1,0:T(8,128)(2,1)}, u32[]{:S(2)}) %copy-start) | copy-done | bytes 16777240
  57.3 2.8 %pin.1.weights = bf16[8192,1152]{1,0:T(8,128)(2,1)S(1)} custom-call(bf16[8192,1024]{1,0:T(8,128)(2,1)S(1)} %copy-done, bf16[64,8192]{1,0:T(8,128)(2,1)S(1)} %get-tuple-element.148.own, bf16[64,8192]{1,0:T(8,128)(2,1)S(1)} %collective-permute-done.6.swapped), custom_call_target="tpu_custom_call" | custom-call | flops 1 | bytes 1 | tf_op jit(solution)/shard_map/pin/pallas_call | solution.py:138
  60.1 3.5 %rows.8 = (f32[128,1024]{1,0:T(8,128)S(1)}, bf16[128,128]{1,0:T(8,128)(2,1)S(1)}) custom-call(s32[2,16]{1,0:T(2,128)S(1)} %add_convert_fusion.table, bf16[8192,1152]{1,0:T(8,128)(2,1)S(1)} %pin.1.weights, bf16[128,8192]{1,0:T(8,128)(2,1)S(1)} %bitcast.58, bf16[128,128]{1,0:T(8,128)(2,1)S(1)} %broadcast_in_dim.48.refs_1_), custom_call_target="tpu_custom_call" | custom-call | flops 1 | bytes 1 | tf_op jit(solution)/shard_map/rows/pallas_call | solution.py:175
  63.5 4.5 %rows.9 = (f32[128,1024]{1,0:T(8,128)S(1)}, bf16[128,128]{1,0:T(8,128)(2,1)S(1)}) custom-call(s32[2,16]{1,0:T(2,128)S(1)} %add_convert_fusion.table, bf16[8192,1152]{1,0:T(8,128)(2,1)S(1)} %pin.1.weights, bf16[64,8192]{1,0:T(8,128)(2,1)} %collective-permute-done.refs_0_, bf16[64,8192]{1,0:T(8,128)(2,1)} %collective-permute-done.1.refs_1_, ...), custom_call_target="tpu_custom_call" | custom-call | flops 1 | bytes 1 | tf_op jit(solution)/shard_map/rows/pallas_call | solution.py:175
  68.0 4.3 %collective-permute-done.2.refs_0_ = bf16[64,8192]{1,0:T(8,128)(2,1)} collective-permute-done((bf16[64,8192]{1,0:T(8,128)(2,1)}, bf16[64,8192]{1,0:T(8,128)(2,1)}, u32[]{:S(2)}, u32[]{:S(2)}) %collective-permute-start.2) | collective-permute-done | bytes 1048608 | tf_op jit(solution)/shard_map/ppermute | solution.py:108
  72.6 1.2 collective-permute-start.8
  73.8 4.2 %rows.10 = (f32[128,1024]{1,0:T(8,128)S(1)}, bf16[128,128]{1,0:T(8,128)(2,1)S(1)}) custom-call(s32[2,16]{1,0:T(2,128)S(1)} %add_convert_fusion.table, bf16[8192,1152]{1,0:T(8,128)(2,1)S(1)} %pin.1.weights, bf16[64,8192]{1,0:T(8,128)(2,1)} %collective-permute-done.5.refs_0_, bf16[64,8192]{1,0:T(8,128)(2,1)S(1)} %collective-permute-done.4.refs_1_, ...), custom_call_target="tpu_custom_call" | custom-call | flops 1 | bytes 1 | tf_op jit(solution)/shard_map/rows/pallas_call | solution.py:175
  78.0 0.8 copy-done.2
  78.8 4.5 %rows.11 = (f32[128,1024]{1,0:T(8,128)S(1)}, bf16[128,128]{1,0:T(8,128)(2,1)S(1)}) custom-call(s32[2,16]{1,0:T(2,128)S(1)} %add_convert_fusion.table, bf16[8192,1152]{1,0:T(8,128)(2,1)S(1)} %pin.1.weights, bf16[64,8192]{1,0:T(8,128)(2,1)} %collective-permute-done.2.refs_0_, bf16[64,8192]{1,0:T(8,128)(2,1)} %collective-permute-done.3.refs_1_, ...), custom_call_target="tpu_custom_call" | custom-call | flops 1 | bytes 1 | tf_op jit(solution)/shard_map/rows/pallas_call | solution.py:175
  83.3 0.8 copy-done.4
  84.1 10.4 %collective-permute-done.10.refs_0_ = bf16[64,8192]{1,0:T(8,128)(2,1)S(1)} collective-permute-done((bf16[64,8192]{1,0:T(8,128)(2,1)}, bf16[64,8192]{1,0:T(8,128)(2,1)S(1)}, u32[]{:S(2)}, u32[]{:S(2)}) %collective-permute-start.10) | collective-permute-done | bytes 1048608 | tf_op jit(solution)/shard_map/ppermute | solution.py:108
  95.0 1.2 collective-permute-start.14
  96.2 3.5 %rows.12 = (f32[128,1024]{1,0:T(8,128)S(1)}, bf16[128,128]{1,0:T(8,128)(2,1)S(1)}) custom-call(s32[2,16]{1,0:T(2,128)S(1)} %add_convert_fusion.table, bf16[8192,1152]{1,0:T(8,128)(2,1)S(1)} %pin.1.weights, bf16[64,8192]{1,0:T(8,128)(2,1)S(1)} %collective-permute-done.10.refs_0_, bf16[64,8192]{1,0:T(8,128)(2,1)S(1)} %collective-permute-done.9.refs_1_, ...), custom_call_target="tpu_custom_call" | custom-call | flops 1 | bytes 1 | tf_op jit(solution)/shard_map/rows/pallas_call | solution.py:175
  99.7 0.8 copy-done.6
  100.5 16.7 %collective-permute-done.7.refs_0_ = bf16[64,8192]{1,0:T(8,128)(2,1)S(1)} collective-permute-done((bf16[64,8192]{1,0:T(8,128)(2,1)}, bf16[64,8192]{1,0:T(8,128)(2,1)S(1)}, u32[]{:S(2)}, u32[]{:S(2)}) %collective-permute-start.7) | collective-permute-done | bytes 1048608 | tf_op jit(solution)/shard_map/ppermute | solution.py:108
  117.4 1.2 collective-permute-start.12
  118.7 3.5 %rows.13 = (f32[128,1024]{1,0:T(8,128)S(1)}, bf16[128,128]{1,0:T(8,128)(2,1)S(1)}) custom-call(s32[2,16]{1,0:T(2,128)S(1)} %add_convert_fusion.table, bf16[8192,1152]{1,0:T(8,128)(2,1)S(1)} %pin.1.weights, bf16[64,8192]{1,0:T(8,128)(2,1)S(1)} %collective-permute-done.7.refs_0_, bf16[64,8192]{1,0:T(8,128)(2,1)S(1)} %collective-permute-done.8.refs_1_, ...), custom_call_target="tpu_custom_call" | custom-call | flops 1 | bytes 1 | tf_op jit(solution)/shard_map/rows/pallas_call | solution.py:175
  122.1 0.8 copy-done.8
  122.9 16.7 %collective-permute-done.13.refs_1_ = bf16[64,8192]{1,0:T(8,128)(2,1)S(1)} collective-permute-done((bf16[64,8192]{1,0:T(8,128)(2,1)S(1)}, bf16[64,8192]{1,0:T(8,128)(2,1)S(1)}, u32[]{:S(2)}, u32[]{:S(2)}) %collective-permute-start.13) | collective-permute-done | bytes 1048608 | tf_op jit(solution)/shard_map/ppermute | solution.py:108
  139.7 3.5 %rows.14 = (f32[128,1024]{1,0:T(8,128)S(1)}, bf16[128,128]{1,0:T(8,128)(2,1)S(1)}) custom-call(s32[2,16]{1,0:T(2,128)S(1)} %add_convert_fusion.table, bf16[8192,1152]{1,0:T(8,128)(2,1)S(1)} %pin.1.weights, bf16[64,8192]{1,0:T(8,128)(2,1)S(1)} %collective-permute-done.14.refs_0_, bf16[64,8192]{1,0:T(8,128)(2,1)S(1)} %collective-permute-done.13.refs_1_, ...), custom_call_target="tpu_custom_call" | custom-call | flops 1 | bytes 1 | tf_op jit(solution)/shard_map/rows/pallas_call | solution.py:175
  143.2 0.8 copy-done.10
  144.0 18.2 %collective-permute-done.11.refs_0_ = bf16[64,8192]{1,0:T(8,128)(2,1)S(1)} collective-permute-done((bf16[64,8192]{1,0:T(8,128)(2,1)S(1)}, bf16[64,8192]{1,0:T(8,128)(2,1)S(1)}, u32[]{:S(2)}, u32[]{:S(2)}) %collective-permute-start.11) | collective-permute-done | bytes 1048608 | tf_op jit(solution)/shard_map/ppermute | solution.py:108
  162.1 3.5 %rows.15 = (f32[128,1024]{1,0:T(8,128)S(1)}, bf16[128,128]{1,0:T(8,128)(2,1)S(1)}) custom-call(s32[2,16]{1,0:T(2,128)S(1)} %add_convert_fusion.table, bf16[8192,1152]{1,0:T(8,128)(2,1)S(1)} %pin.1.weights, bf16[64,8192]{1,0:T(8,128)(2,1)S(1)} %collective-permute-done.11.refs_0_, bf16[64,8192]{1,0:T(8,128)(2,1)S(1)} %collective-permute-done.12.refs_1_, ...), custom_call_target="tpu_custom_call" | custom-call | flops 1 | bytes 1 | tf_op jit(solution)/shard_map/rows/pallas_call | solution.py:175
  165.6 0.8 copy-done.12
  166.4 7.8 %all-to-all-start = ((bf16[16,64,512]{2,1,0:T(8,128)(2,1)}), bf16[16,64,512]{2,1,0:T(8,128)(2,1)S(1)}, u32[]{:S(2)}, u32[]{:S(2)}) async-start(bf16[16,64,512]{2,1,0:T(8,128)(2,1)} %bitcast.30), calls=%async_computation | async-start | bytes 2097152 | tf_op jit(solution)/shard_map/all_to_all | solution.py:331
  174.9 5.6 %collective-permute-done.15 = bf16[128,128]{1,0:T(8,128)(2,1)S(1)} collective-permute-done((bf16[128,128]{1,0:T(8,128)(2,1)S(1)}, bf16[128,128]{1,0:T(8,128)(2,1)S(1)}, u32[]{:S(2)}, u32[]{:S(2)}) %collective-permute-start.15) | collective-permute-done | bytes 32800 | tf_op jit(solution)/shard_map/ppermute | solution.py:108
  180.5 2.6 %collective-permute-start.17 = (bf16[2,128,128]{2,1,0:T(8,128)(2,1)S(1)}, bf16[2,128,128]{2,1,0:T(8,128)(2,1)}, u32[]{:S(2)}, u32[]{:S(2)}) collective-permute-start(bf16[2,128,128]{2,1,0:T(8,128)(2,1)S(1)} %pad_maximum_fusion), channel_id=1, source_target_pairs={{0,8},{2,10},{4,12},{6,14},{8,0},{10,2},{12,4},{14,6},{1,9},{3,11}... | collective-permute-start | bytes 196616 | tf_op jit(solution)/shard_map/ppermute | solution.py:108
  183.4 19.1 %all-to-all-done.got = bf16[16,64,512]{2,1,0:T(8,128)(2,1)S(1)} async-done(((bf16[16,64,512]{2,1,0:T(8,128)(2,1)}), bf16[16,64,512]{2,1,0:T(8,128)(2,1)S(1)}, u32[]{:S(2)}, u32[]{:S(2)}) %all-to-all-start) | async-done | bytes 1048608 | tf_op jit(solution)/shard_map/all_to_all | solution.py:331
  203.1 1.3 collective-permute-start.19
  204.4 0.9 constant_dynamic-update-slice_fusion.2
  205.3 0.9 constant_dynamic-update-slice_fusion.1
  206.2 0.9 constant_dynamic-update-slice_fusion.refs_8_
  207.0 9.9 %collective-permute-done.19.refs_10_ = bf16[8,64,512]{2,1,0:T(8,128)(2,1)S(1)} collective-permute-done((bf16[8,64,512]{2,1,0:T(8,128)(2,1)S(1)}, bf16[8,64,512]{2,1,0:T(8,128)(2,1)S(1)}, u32[]{:S(2)}, u32[]{:S(2)}) %collective-permute-start.19) | collective-permute-done | bytes 524320 | tf_op jit(solution)/shard_map/ppermute | solution.py:112
  217.0 1.0 copy-done.7
  218.0 1.0 copy-done.9
  219.0 1.0 copy-done.11
  220.1 1.0 copy-done.13
  221.1 2.3 %finish.1 = bf16[1024,1024]{1,0:T(8,128)(2,1)} custom-call(s32[4,16]{1,0:T(4,128)S(1)} %add_add_fusion.table, f32[128,1024]{1,0:T(8,128)S(1)} %get-tuple-element.130.refs_0_, f32[128,1024]{1,0:T(8,128)S(1)} %get-tuple-element.131.refs_1_, f32[128,1024]{1,0:T(8,128)S(1)} %copy-done.3, f32[128,1024]{1,0:T(8,128)S(1)} %copy-done.5, f32[128,1024]{1,0:T(8,128)S(1)} %copy-done.7, ...), custom_call_target="tpu_custom_call" | custom-call | flops 1 | bytes 1 | tf_op jit(solution)/shard_map/finish/pallas_call | solution.py:255
  (61 shorter events, 4.3 us)
Async XLA Ops:
  0.0 27.4 %copy-start.15 = (s32[64]{0:T(128)S(1)}, s32[64]{0:T(128)}, u32[]{:S(2)}) copy-start(s32[64]{0:T(128)} %param.10) | copy-start | bytes 772
  0.0 27.4 %copy-start.14 = (s32[2,8]{1,0:T(2,128)S(1)}, s32[2,8]{1,0:T(2,128)}, u32[]{:S(2)}) copy-start(s32[2,8]{1,0:T(2,128)} %param.11) | copy-start | bytes 196
  3.1 24.3 %collective-permute-start = (bf16[64,8192]{1,0:T(8,128)(2,1)}, bf16[64,8192]{1,0:T(8,128)(2,1)}, u32[]{:S(2)}, u32[]{:S(2)}) collective-permute-start(bf16[64,8192]{1,0:T(8,128)(2,1)} %get-tuple-element.150), channel_id=1, source_target_pairs={{0,4},{4,8},{8,12},{12,14},{14,10},{10,6},{6,2},{2,0},{1,5},{5,9},... | collective-permute-start | bytes 3145736 | tf_op jit(solution)/shard_map/ppermute | solution.py:108
  3.3 24.2 %collective-permute-start.1 = (bf16[64,8192]{1,0:T(8,128)(2,1)}, bf16[64,8192]{1,0:T(8,128)(2,1)}, u32[]{:S(2)}, u32[]{:S(2)}) collective-permute-start(bf16[64,8192]{1,0:T(8,128)(2,1)} %get-tuple-element.149), channel_id=1, source_target_pairs={{4,0},{8,4},{12,8},{14,12},{10,14},{6,10},{2,6},{0,2},{5,1},{9,5},... | collective-permute-start | bytes 3145736 | tf_op jit(solution)/shard_map/ppermute | solution.py:108
  4.5 45.3 %collective-permute-start.4 = (bf16[64,8192]{1,0:T(8,128)(2,1)}, bf16[64,8192]{1,0:T(8,128)(2,1)S(1)}, u32[]{:S(2)}, u32[]{:S(2)}) collective-permute-start(bf16[64,8192]{1,0:T(8,128)(2,1)} %get-tuple-element.149), channel_id=1, source_target_pairs={{0,4},{4,8},{8,12},{12,14},{14,10},{10,6},{6,2},{2,0},{1,5},{5,9},... | collective-permute-start | bytes 3145736 | tf_op jit(solution)/shard_map/ppermute | solution.py:108
  4.7 45.2 %collective-permute-start.5 = (bf16[64,8192]{1,0:T(8,128)(2,1)}, bf16[64,8192]{1,0:T(8,128)(2,1)}, u32[]{:S(2)}, u32[]{:S(2)}) collective-permute-start(bf16[64,8192]{1,0:T(8,128)(2,1)} %get-tuple-element.150), channel_id=1, source_target_pairs={{4,0},{8,4},{12,8},{14,12},{10,14},{6,10},{2,6},{0,2},{5,1},{9,5},... | collective-permute-start | bytes 3145736 | tf_op jit(solution)/shard_map/ppermute | solution.py:108
  34.9 16.6 %collective-permute-start.6 = (bf16[64,8192]{1,0:T(8,128)(2,1)}, bf16[64,8192]{1,0:T(8,128)(2,1)S(1)}, u32[]{:S(2)}, u32[]{:S(2)}) collective-permute-start(bf16[64,8192]{1,0:T(8,128)(2,1)} %get-tuple-element.147), channel_id=1, source_target_pairs={{0,1},{1,0},{2,3},{3,2},{4,5},{5,4},{6,7},{7,6},{8,9},{9,8},{10,11... | collective-permute-start | bytes 3145736 | tf_op jit(solution)/shard_map/ppermute | solution.py:112
  38.1 34.2 %collective-permute-start.2 = (bf16[64,8192]{1,0:T(8,128)(2,1)}, bf16[64,8192]{1,0:T(8,128)(2,1)}, u32[]{:S(2)}, u32[]{:S(2)}) collective-permute-start(bf16[64,8192]{1,0:T(8,128)(2,1)} %collective-permute-done.refs_0_), channel_id=1, source_target_pairs={{0,4},{4,8},{8,12},{12,14},{14,10},{10,6},{6,2},{2,0},{1,5},{5,9},... | collective-permute-start | bytes 3145736 | tf_op jit(solution)/shard_map/ppermute | solution.py:108
  38.1 34.2 %collective-permute-start.3 = (bf16[64,8192]{1,0:T(8,128)(2,1)}, bf16[64,8192]{1,0:T(8,128)(2,1)}, u32[]{:S(2)}, u32[]{:S(2)}) collective-permute-start(bf16[64,8192]{1,0:T(8,128)(2,1)} %collective-permute-done.1.refs_1_), channel_id=1, source_target_pairs={{4,0},{8,4},{12,8},{14,12},{10,14},{6,10},{2,6},{0,2},{5,1},{9,5},... | collective-permute-start | bytes 3145736 | tf_op jit(solution)/shard_map/ppermute | solution.py:108
  49.9 44.7 %collective-permute-start.10 = (bf16[64,8192]{1,0:T(8,128)(2,1)}, bf16[64,8192]{1,0:T(8,128)(2,1)S(1)}, u32[]{:S(2)}, u32[]{:S(2)}) collective-permute-start(bf16[64,8192]{1,0:T(8,128)(2,1)} %collective-permute-done.5.refs_0_), channel_id=1, source_target_pairs={{4,0},{8,4},{12,8},{14,12},{10,14},{6,10},{2,6},{0,2},{5,1},{9,5},... | collective-permute-start | bytes 3145736 | tf_op jit(solution)/shard_map/ppermute | solution.py:108
  51.2 43.5 %collective-permute-start.9 = (bf16[64,8192]{1,0:T(8,128)(2,1)S(1)}, bf16[64,8192]{1,0:T(8,128)(2,1)S(1)}, u32[]{:S(2)}, u32[]{:S(2)}) collective-permute-start(bf16[64,8192]{1,0:T(8,128)(2,1)S(1)} %collective-permute-done.4.refs_1_), channel_id=1, source_target_pairs={{0,4},{4,8},{8,12},{12,14},{14,10},{10,6},{6,2},{2,0},{1,5},{5,9},... | collective-permute-start | bytes 3145736 | tf_op jit(solution)/shard_map/ppermute | solution.py:108
  51.5 5.8 %copy-start = (bf16[8192,1024]{1,0:T(8,128)(2,1)S(1)}, bf16[8192,1024]{1,0:T(8,128)(2,1)}, u32[]{:S(2)}) copy-start(bf16[8192,1024]{1,0:T(8,128)(2,1)} %weight.1) | copy-start | bytes 50331652
  57.3 2.8 %copy-start.1 = (bf16[1,128,8192]{2,1,0:T(8,128)(2,1)S(1)}, bf16[1,128,8192]{2,1,0:T(8,128)(2,1)}, u32[]{:S(2)}) copy-start(bf16[1,128,8192]{2,1,0:T(8,128)(2,1)} %param.6) | copy-start | bytes 6291460
  72.4 44.8 %collective-permute-start.7 = (bf16[64,8192]{1,0:T(8,128)(2,1)}, bf16[64,8192]{1,0:T(8,128)(2,1)S(1)}, u32[]{:S(2)}, u32[]{:S(2)}) collective-permute-start(bf16[64,8192]{1,0:T(8,128)(2,1)} %collective-permute-done.2.refs_0_), channel_id=1, source_target_pairs={{0,4},{4,8},{8,12},{12,14},{14,10},{10,6},{6,2},{2,0},{1,5},{5,9},... | collective-permute-start | bytes 3145736 | tf_op jit(solution)/shard_map/ppermute | solution.py:108
  72.6 44.6 %collective-permute-start.8 = (bf16[64,8192]{1,0:T(8,128)(2,1)}, bf16[64,8192]{1,0:T(8,128)(2,1)S(1)}, u32[]{:S(2)}, u32[]{:S(2)}) collective-permute-start(bf16[64,8192]{1,0:T(8,128)(2,1)} %collective-permute-done.3.refs_1_), channel_id=1, source_target_pairs={{4,0},{8,4},{12,8},{14,12},{10,14},{6,10},{2,6},{0,2},{5,1},{9,5},... | collective-permute-start | bytes 3145736 | tf_op jit(solution)/shard_map/ppermute | solution.py:108
  78.0 0.8 copy-start.2
  83.3 0.8 copy-start.4
  94.7 44.9 %collective-permute-start.13 = (bf16[64,8192]{1,0:T(8,128)(2,1)S(1)}, bf16[64,8192]{1,0:T(8,128)(2,1)S(1)}, u32[]{:S(2)}, u32[]{:S(2)}) collective-permute-start(bf16[64,8192]{1,0:T(8,128)(2,1)S(1)} %collective-permute-done.9.refs_1_), channel_id=1, source_target_pairs={{0,4},{4,8},{8,12},{12,14},{14,10},{10,6},{6,2},{2,0},{1,5},{5,9},... | collective-permute-start | bytes 3145736 | tf_op jit(solution)/shard_map/ppermute | solution.py:108
  95.0 44.7 %collective-permute-start.14 = (bf16[64,8192]{1,0:T(8,128)(2,1)S(1)}, bf16[64,8192]{1,0:T(8,128)(2,1)S(1)}, u32[]{:S(2)}, u32[]{:S(2)}) collective-permute-start(bf16[64,8192]{1,0:T(8,128)(2,1)S(1)} %collective-permute-done.10.refs_0_), channel_id=1, source_target_pairs={{4,0},{8,4},{12,8},{14,12},{10,14},{6,10},{2,6},{0,2},{5,1},{9,5},... | collective-permute-start | bytes 3145736 | tf_op jit(solution)/shard_map/ppermute | solution.py:108
  99.7 0.8 copy-start.6
  117.2 44.9 %collective-permute-start.11 = (bf16[64,8192]{1,0:T(8,128)(2,1)S(1)}, bf16[64,8192]{1,0:T(8,128)(2,1)S(1)}, u32[]{:S(2)}, u32[]{:S(2)}) collective-permute-start(bf16[64,8192]{1,0:T(8,128)(2,1)S(1)} %collective-permute-done.7.refs_0_), channel_id=1, source_target_pairs={{0,4},{4,8},{8,12},{12,14},{14,10},{10,6},{6,2},{2,0},{1,5},{5,9},... | collective-permute-start | bytes 3145736 | tf_op jit(solution)/shard_map/ppermute | solution.py:108
  117.4 44.7 %collective-permute-start.12 = (bf16[64,8192]{1,0:T(8,128)(2,1)S(1)}, bf16[64,8192]{1,0:T(8,128)(2,1)S(1)}, u32[]{:S(2)}, u32[]{:S(2)}) collective-permute-start(bf16[64,8192]{1,0:T(8,128)(2,1)S(1)} %collective-permute-done.8.refs_1_), channel_id=1, source_target_pairs={{4,0},{8,4},{12,8},{14,12},{10,14},{6,10},{2,6},{0,2},{5,1},{9,5},... | collective-permute-start | bytes 3145736 | tf_op jit(solution)/shard_map/ppermute | solution.py:108
  122.1 0.8 copy-start.8
  143.2 0.8 copy-start.10
  165.6 0.8 copy-start.12
  166.4 50.5 %copy-start.3 = (f32[128,1024]{1,0:T(8,128)S(1)}, f32[128,1024]{1,0:T(8,128)}, u32[]{:S(2)}) copy-start(f32[128,1024]{1,0:T(8,128)} %copy-done.2) | copy-start | bytes 1572868
  166.4 50.5 %copy-start.5 = (f32[128,1024]{1,0:T(8,128)S(1)}, f32[128,1024]{1,0:T(8,128)}, u32[]{:S(2)}) copy-start(f32[128,1024]{1,0:T(8,128)} %copy-done.4) | copy-start | bytes 1572868
  166.4 36.0 %all-to-all-start = ((bf16[16,64,512]{2,1,0:T(8,128)(2,1)}), bf16[16,64,512]{2,1,0:T(8,128)(2,1)S(1)}, u32[]{:S(2)}, u32[]{:S(2)}) async-start(bf16[16,64,512]{2,1,0:T(8,128)(2,1)} %bitcast.30), calls=%async_computation | async-start | bytes 2097152 | tf_op jit(solution)/shard_map/all_to_all | solution.py:331
  174.6 5.9 %collective-permute-start.15 = (bf16[128,128]{1,0:T(8,128)(2,1)S(1)}, bf16[128,128]{1,0:T(8,128)(2,1)S(1)}, u32[]{:S(2)}, u32[]{:S(2)}) collective-permute-start(bf16[128,128]{1,0:T(8,128)(2,1)S(1)} %get-tuple-element.143), channel_id=1, source_target_pairs={{0,2},{2,0},{4,6},{6,4},{8,10},{10,8},{12,14},{14,12},{1,3},{3,1},... | collective-permute-start | bytes 98312 | tf_op jit(solution)/shard_map/ppermute | solution.py:108
  180.4 24.0 %collective-permute-start.16 = (bf16[2,128,128]{2,1,0:T(8,128)(2,1)S(1)}, bf16[2,128,128]{2,1,0:T(8,128)(2,1)}, u32[]{:S(2)}, u32[]{:S(2)}) collective-permute-start(bf16[2,128,128]{2,1,0:T(8,128)(2,1)S(1)} %pad_maximum_fusion), channel_id=1, source_target_pairs={{0,4},{2,6},{4,0},{6,2},{8,12},{10,14},{12,8},{14,10},{1,5},{3,7},... | collective-permute-start | bytes 196616 | tf_op jit(solution)/shard_map/ppermute | solution.py:108
  180.5 24.8 %collective-permute-start.17 = (bf16[2,128,128]{2,1,0:T(8,128)(2,1)S(1)}, bf16[2,128,128]{2,1,0:T(8,128)(2,1)}, u32[]{:S(2)}, u32[]{:S(2)}) collective-permute-start(bf16[2,128,128]{2,1,0:T(8,128)(2,1)S(1)} %pad_maximum_fusion), channel_id=1, source_target_pairs={{0,8},{2,10},{4,12},{6,14},{8,0},{10,2},{12,4},{14,6},{1,9},{3,11}... | collective-permute-start | bytes 196616 | tf_op jit(solution)/shard_map/ppermute | solution.py:108
  183.2 23.0 %collective-permute-start.18 = (bf16[2,128,128]{2,1,0:T(8,128)(2,1)S(1)}, bf16[2,128,128]{2,1,0:T(8,128)(2,1)}, u32[]{:S(2)}, u32[]{:S(2)}) collective-permute-start(bf16[2,128,128]{2,1,0:T(8,128)(2,1)S(1)} %pad_maximum_fusion), channel_id=1, source_target_pairs={{0,12},{2,14},{4,8},{6,10},{8,4},{10,6},{12,0},{14,2},{1,13},{3,15... | collective-permute-start | bytes 196616 | tf_op jit(solution)/shard_map/ppermute | solution.py:108
  203.1 13.8 %collective-permute-start.19 = (bf16[8,64,512]{2,1,0:T(8,128)(2,1)S(1)}, bf16[8,64,512]{2,1,0:T(8,128)(2,1)S(1)}, u32[]{:S(2)}, u32[]{:S(2)}) collective-permute-start(bf16[8,64,512]{2,1,0:T(8,128)(2,1)S(1)} %take.1.refs_9_), channel_id=1, source_target_pairs={{0,16},{16,0},{1,17},{17,1},{2,18},{18,2},{3,19},{19,3},{4,20},{20... | collective-permute-start | bytes 1572872 | tf_op jit(solution)/shard_map/ppermute | solution.py:112
  217.0 1.0 copy-start.7
  218.0 1.0 copy-start.9
  219.0 1.0 copy-start.11
  220.1 1.0 copy-start.13

commit v9 on v8

--- a/solution.py
+++ b/solution.py
@@ -230,19 +230,27 @@
 
 
 def finish_kernel(table, *refs):
-    *bases, shrunk, up_mine, up_other, out, rows, sems = refs
+    bases, gathered, refs = refs[:8], refs[8:12], refs[12:]
+    up_mine, up_other, out, base, shrunk, rows, base_sems, sems = refs
     part = up_mine.shape[2]
     group = table[3, 0]
+    fetches = [pltpu.make_async_copy(bases[g], base.at[g], base_sems.at[g]) for g in range(8)]
+    for fetch in fetches:
+        fetch.start()
+    for i, pair in enumerate(gathered):
+        shrunk[pl.ds(2 * i, 2)] = pair[...]
     copies = []
     for i in range(16):
         block, half = table[0, i], i % 2
+        if half == 0:
+            fetches[i // 2].wait()
         own = pl.ds(half * HALF, HALF)
         both = shrunk[table[1, i], own, :].astype(jnp.float32)
         value = jnp.where(table[2, i] > 0, both[:, 64:], both[:, :64]).astype(jnp.bfloat16)
         for up, side in ((up_mine, group), (up_other, 1 - group)):
             cut = pl.ds(pl.multiple_of(side * part, part), part)
             grown = jnp.dot(value, up[block], preferred_element_type=jnp.float32)
-            rows[i, :, cut] = (bases[i // 2][own, cut] + 0.5 * grown).astype(rows.dtype)
+            rows[i, :, cut] = (base[i // 2, own, cut] + 0.5 * grown).astype(rows.dtype)
         to = pl.ds(pl.multiple_of((2 * block + half) * HALF, HALF), HALF)
         copies.append(pltpu.make_async_copy(rows.at[i], out.at[to], sems.at[i]))
         copies[-1].start()
@@ -250,20 +258,25 @@
         copy.wait()
 
 
-def finish_call(table, bases, shrunk, up_mine, up_other):
+def finish_call(table, bases, gathered, up_mine, up_other):
     columns = bases[0].shape[1]
     return pl.pallas_call(
         finish_kernel,
-        in_specs=[pl.BlockSpec(memory_space=pltpu.SMEM)] + in_vmem(11),
+        in_specs=[pl.BlockSpec(memory_space=pltpu.SMEM)]
+        + [pl.BlockSpec(memory_space=pl.ANY)] * 8
+        + in_vmem(6),
         out_specs=pl.BlockSpec(memory_space=pltpu.HBM),
         out_shape=jax.ShapeDtypeStruct((8 * BLOCK, columns), jnp.bfloat16),
         scratch_shapes=[
+            pltpu.VMEM((8, BLOCK, columns), jnp.float32),
+            pltpu.VMEM((8,) + gathered[0].shape[1:], jnp.bfloat16),
             pltpu.VMEM((16, HALF, columns), jnp.bfloat16),
+            pltpu.SemaphoreType.DMA((8,)),
             pltpu.SemaphoreType.DMA((16,)),
         ],
         name="finish",
         **settings(),
-    )(table, *bases, shrunk, up_mine, up_other)
+    )(table, *bases, *gathered, up_mine, up_other)
 
 
 def chain_body(
@@ -315,27 +328,34 @@
     bases = []
     shrunk = jnp.zeros((BLOCK, 2 * rank), jnp.bfloat16)
     groups = [[rows], [ahead[2], back[2]]]
-    for k in range(1, 7):
+    for k in range(1, 6):
         (got_ahead, got_back), ahead, back, bases, shrunk, up_sent = lax.optimization_barrier(
             (flight[k], ahead, back, bases, shrunk, up_sent)
         )
         ahead.append(got_ahead)
         back.append(got_back)
-        if k < 5:
+        if k < 4:
             flight.append((send(ahead[k + 2], AHEAD), send(back[k + 2], BACK)))
+        else:
+            cut = slice(0, HALF // 2) if k == 4 else slice(HALF // 2, HALF)
+            flight.append((send(ahead[6][cut], AHEAD), send(back[6][cut], BACK)))
         groups.append([got_ahead, got_back] if k % 2 == 0 else [got_back, got_ahead])
         for g in range(len(bases), min(len(bases) + 2, k + 2)):
             base, shrunk = rows_call(g, table, weights, groups[g], shrunk)
             bases.append(base)
-    shrunk, up_sent = lax.optimization_barrier((shrunk, up_sent))
+    first, bases, shrunk, up_sent = lax.optimization_barrier((flight[6], bases, shrunk, up_sent))
     up_got = lax.all_to_all(
         up_sent.reshape(16, rank, -1), ("tensor", "store"), split_axis=0, concat_axis=0, tiled=True
     )
-
+    first, second, bases, shrunk = lax.optimization_barrier((first, flight[7], bases, shrunk))
+    base, shrunk = rows_call(7, table, weights, [first[0], second[0], first[1], second[1]], shrunk)
+    bases.append(base)
+
+    across, up_got = lax.optimization_barrier((send(shrunk, ACROSS), up_got))
+    pair = jnp.stack([shrunk, across])
+    everyone = [pair] + [send(pair, pairs) for pairs in ALONG]
     up_mine = take_call(owner_row, up_got)
     up_other = swap(up_mine, "groups")
-    pair = jnp.stack([shrunk, send(shrunk, ACROSS)])
-    everyone = jnp.concatenate([pair] + [send(pair, pairs) for pairs in ALONG])
     home, core = owners // 2, owners % 2
     where = 2 * ((home // 2) ^ z) + ((home % 2) ^ y)
     table = jnp.stack([blocks, where, core != store, jnp.broadcast_to(group, (16,))])

time: 224 us -> 236 us (1.054)
  the two profiles are of different devices: /device:TPU:13 before, /device:TPU:0 now
where the time goes in v9:
time: 236 us; the launch traced here: 233 us
  waiting for transfers between devices  117 us (50%)
  Pallas kernels  41.8 us (18%)
  starting transfers between devices  35.8 us (15%)
  local copies, waits for them, and re-layouts  34.1 us (14%)
  between operations  4.31 us (2%)
    ppermute x20, waiting for transfers between devices, send(): return lax.ppermute(value, 'tensor', pairs)  117 us
    pallas_call x8, Pallas kernels, rows_call(): pl.pallas_call(functools.partial(rows_kernel, group), in_specs=[pl.BlockS...  31 us
    ppermute x20, starting transfers between devices, send(): return lax.ppermute(value, 'tensor', pairs)  28.8 us
    unnamed x52, local copies, waits for them, and re-layouts  27.2 us
    all_to_all x1, starting transfers between devices, chain_body(): lax.all_to_all(up_sent.reshape(16, rank, -1), ('tensor', 'store'), split_...  5.44 us
  transfers between devices with their start and end apart: 23, of which 18 were waited for; matrix products, arithmetic and copies ran while one was open for 2% of the time, Pallas kernels for 16%

profile of v9, /device:TPU:0, one launch (start us, length us, event | category | flops | bytes accessed | tf_op | source)
XLA Modules:
  0.0 233.4 jit_solution(14848216263151311424)
XLA Ops:
  0.0 3.1 %slice_bitcast_fusion = (bf16[64,8192]{1,0:T(8,128)(2,1)}, bf16[64,8192]{1,0:T(8,128)(2,1)}) fusion(bf16[1,128,8192]{2,1,0:T(8,128)(2,1)} %param.6), kind=kLoop, calls=%fused_computation.2 | loop fusion | bytes 4194304 | tf_op jit(solution)/shard_map/slice | solution.py:292
  3.1 3.0 %collective-permute-start = (bf16[64,8192]{1,0:T(8,128)(2,1)}, bf16[64,8192]{1,0:T(8,128)(2,1)S(1)}, u32[]{:S(2)}, u32[]{:S(2)}) collective-permute-start(bf16[64,8192]{1,0:T(8,128)(2,1)} %get-tuple-element.178), channel_id=1, source_target_pairs={{0,4},{4,8},{8,12},{12,14},{14,10},{10,6},{6,2},{2,0},{1,5},{5,9},... | collective-permute-start | bytes 3145736 | tf_op jit(solution)/shard_map/ppermute | solution.py:108
  6.1 2.0 collective-permute-start.4
  8.2 22.1 %collective-permute-done.refs_0_ = bf16[64,8192]{1,0:T(8,128)(2,1)S(1)} collective-permute-done((bf16[64,8192]{1,0:T(8,128)(2,1)}, bf16[64,8192]{1,0:T(8,128)(2,1)S(1)}, u32[]{:S(2)}, u32[]{:S(2)}) %collective-permute-start) | collective-permute-done | bytes 1048608 | tf_op jit(solution)/shard_map/ppermute | solution.py:108
  30.3 2.3 collective-permute-done.1.refs_1_
  37.3 2.8 %dynamic-slice_bitcast_fusion = (bf16[64,8192]{1,0:T(8,128)(2,1)}, bf16[64,8192]{1,0:T(8,128)(2,1)S(1)}) fusion(bf16[4,64,8192]{2,1,0:T(8,128)(2,1)} %param.8, s32[]{:T(128)S(6)} %select_n.151, s32[]{:T(128)S(6)} %select_n.149), kind=kLoop, calls=%fused_computation | loop fusion | bytes 4194312 | tf_op jit(solution)/shard_map/jit(dynamic_index_in_dim)/squeeze | solution.py:312
  40.1 1.6 collective-permute-start.2
  42.3 2.8 %pack.1 = bf16[8,2,64,512]{3,2,1,0:T(8,128)(2,1)} custom-call(s32[3]{0:T(128)S(1)} %pad_add_fusion.table, bf16[4,64,8192]{2,1,0:T(8,128)(2,1)} %up.1), custom_call_target="tpu_custom_call" | custom-call | flops 1 | bytes 1 | tf_op jit(solution)/shard_map/pack/pallas_call | solution.py:198
  45.1 7.7 %collective-permute-done.4.refs_1_ = bf16[64,8192]{1,0:T(8,128)(2,1)} collective-permute-done((bf16[64,8192]{1,0:T(8,128)(2,1)}, bf16[64,8192]{1,0:T(8,128)(2,1)}, u32[]{:S(2)}, u32[]{:S(2)}) %collective-permute-start.4) | collective-permute-done | bytes 1048608 | tf_op jit(solution)/shard_map/ppermute | solution.py:108
  52.8 2.2 collective-permute-done.5.refs_0_
  55.0 2.0 collective-permute-start.9
  57.2 5.8 %copy-done.2 = bf16[8192,1024]{1,0:T(8,128)(2,1)S(1)} copy-done((bf16[8192,1024]{1,0:T(8,128)(2,1)S(1)}, bf16[8192,1024]{1,0:T(8,128)(2,1)}, u32[]{:S(2)}) %copy-start.2) | copy-done | bytes 16777240
  62.9 2.8 %pin.1.weights = bf16[8192,1152]{1,0:T(8,128)(2,1)S(1)} custom-call(bf16[8192,1024]{1,0:T(8,128)(2,1)S(1)} %copy-done.2, bf16[64,8192]{1,0:T(8,128)(2,1)S(1)} %get-tuple-element.176.own, bf16[64,8192]{1,0:T(8,128)(2,1)S(1)} %collective-permute-done.6.swapped), custom_call_target="tpu_custom_call" | custom-call | flops 1 | bytes 1 | tf_op jit(solution)/shard_map/pin/pallas_call | solution.py:138
  65.7 3.4 %rows.8 = (f32[128,1024]{1,0:T(8,128)S(1)}, bf16[128,128]{1,0:T(8,128)(2,1)S(1)}) custom-call(s32[2,16]{1,0:T(2,128)S(1)} %add_convert_fusion.table, bf16[8192,1152]{1,0:T(8,128)(2,1)S(1)} %pin.1.weights, bf16[128,8192]{1,0:T(8,128)(2,1)S(1)} %bitcast.56, bf16[128,128]{1,0:T(8,128)(2,1)S(1)} %broadcast_in_dim.48.refs_1_), custom_call_target="tpu_custom_call" | custom-call | flops 1 | bytes 1 | tf_op jit(solution)/shard_map/rows/pallas_call | solution.py:175
  69.2 1.6 copy-done.4
  70.8 4.9 %rows.9 = (f32[128,1024]{1,0:T(8,128)S(1)}, bf16[128,128]{1,0:T(8,128)(2,1)S(1)}) custom-call(s32[2,16]{1,0:T(2,128)S(1)} %add_convert_fusion.table, bf16[8192,1152]{1,0:T(8,128)(2,1)S(1)} %pin.1.weights, bf16[64,8192]{1,0:T(8,128)(2,1)S(1)} %collective-permute-done.refs_0_, bf16[64,8192]{1,0:T(8,128)(2,1)} %collective-permute-done.1.refs_1_, ...), custom_call_target="tpu_custom_call" | custom-call | flops 1 | bytes 1 | tf_op jit(solution)/shard_map/rows/pallas_call | solution.py:175
  77.5 1.6 collective-permute-start.7
  79.5 4.4 %rows.10 = (f32[128,1024]{1,0:T(8,128)S(1)}, bf16[128,128]{1,0:T(8,128)(2,1)S(1)}) custom-call(s32[2,16]{1,0:T(2,128)S(1)} %add_convert_fusion.table, bf16[8192,1152]{1,0:T(8,128)(2,1)S(1)} %pin.1.weights, bf16[64,8192]{1,0:T(8,128)(2,1)} %collective-permute-done.5.refs_0_, bf16[64,8192]{1,0:T(8,128)(2,1)} %collective-permute-done.4.refs_1_, ...), custom_call_target="tpu_custom_call" | custom-call | flops 1 | bytes 1 | tf_op jit(solution)/shard_map/rows/pallas_call | solution.py:175
  84.8 4.4 %rows.11 = (f32[128,1024]{1,0:T(8,128)S(1)}, bf16[128,128]{1,0:T(8,128)(2,1)S(1)}) custom-call(s32[2,16]{1,0:T(2,128)S(1)} %add_convert_fusion.table, bf16[8192,1152]{1,0:T(8,128)(2,1)S(1)} %pin.1.weights, bf16[64,8192]{1,0:T(8,128)(2,1)} %collective-permute-done.2.refs_0_, bf16[64,8192]{1,0:T(8,128)(2,1)} %collective-permute-done.3.refs_1_, ...), custom_call_target="tpu_custom_call" | custom-call | flops 1 | bytes 1 | tf_op jit(solution)/shard_map/rows/pallas_call | solution.py:175
  90.1 9.7 %collective-permute-done.10.refs_0_ = bf16[64,8192]{1,0:T(8,128)(2,1)S(1)} collective-permute-done((bf16[64,8192]{1,0:T(8,128)(2,1)}, bf16[64,8192]{1,0:T(8,128)(2,1)S(1)}, u32[]{:S(2)}, u32[]{:S(2)}) %collective-permute-start.10) | collective-permute-done | bytes 1048608 | tf_op jit(solution)/shard_map/ppermute | solution.py:108
  99.8 1.6 collective-permute-start.13
  101.9 3.4 %rows.12 = (f32[128,1024]{1,0:T(8,128)S(1)}, bf16[128,128]{1,0:T(8,128)(2,1)S(1)}) custom-call(s32[2,16]{1,0:T(2,128)S(1)} %add_convert_fusion.table, bf16[8192,1152]{1,0:T(8,128)(2,1)S(1)} %pin.1.weights, bf16[64,8192]{1,0:T(8,128)(2,1)S(1)} %collective-permute-done.10.refs_0_, bf16[64,8192]{1,0:T(8,128)(2,1)S(1)} %collective-permute-done.9.refs_1_, ...), custom_call_target="tpu_custom_call" | custom-call | flops 1 | bytes 1 | tf_op jit(solution)/shard_map/rows/pallas_call | solution.py:175
  106.1 14.0 %collective-permute-done.7.refs_0_ = bf16[64,8192]{1,0:T(8,128)(2,1)S(1)} collective-permute-done((bf16[64,8192]{1,0:T(8,128)(2,1)}, bf16[64,8192]{1,0:T(8,128)(2,1)S(1)}, u32[]{:S(2)}, u32[]{:S(2)}) %collective-permute-start.7) | collective-permute-done | bytes 1048608 | tf_op jit(solution)/shard_map/ppermute | solution.py:108
  120.1 2.2 collective-permute-done.8.refs_1_
  122.3 1.6 collective-permute-start.11
  124.7 3.5 %rows.13 = (f32[128,1024]{1,0:T(8,128)S(1)}, bf16[128,128]{1,0:T(8,128)(2,1)S(1)}) custom-call(s32[2,16]{1,0:T(2,128)S(1)} %add_convert_fusion.table, bf16[8192,1152]{1,0:T(8,128)(2,1)S(1)} %pin.1.weights, bf16[64,8192]{1,0:T(8,128)(2,1)S(1)} %collective-permute-done.7.refs_0_, bf16[64,8192]{1,0:T(8,128)(2,1)S(1)} %collective-permute-done.8.refs_1_, ...), custom_call_target="tpu_custom_call" | custom-call | flops 1 | bytes 1 | tf_op jit(solution)/shard_map/rows/pallas_call | solution.py:175
  129.0 13.6 %collective-permute-done.13.refs_1_ = bf16[64,8192]{1,0:T(8,128)(2,1)S(1)} collective-permute-done((bf16[64,8192]{1,0:T(8,128)(2,1)S(1)}, bf16[64,8192]{1,0:T(8,128)(2,1)S(1)}, u32[]{:S(2)}, u32[]{:S(2)}) %collective-permute-start.13) | collective-permute-done | bytes 1048608 | tf_op jit(solution)/shard_map/ppermute | solution.py:108
  142.6 2.2 collective-permute-done.14.refs_0_
  144.8 3.5 %rows.14 = (f32[128,1024]{1,0:T(8,128)S(1)}, bf16[128,128]{1,0:T(8,128)(2,1)S(1)}) custom-call(s32[2,16]{1,0:T(2,128)S(1)} %add_convert_fusion.table, bf16[8192,1152]{1,0:T(8,128)(2,1)S(1)} %pin.1.weights, bf16[64,8192]{1,0:T(8,128)(2,1)S(1)} %collective-permute-done.14.refs_0_, bf16[64,8192]{1,0:T(8,128)(2,1)S(1)} %collective-permute-done.13.refs_1_, ...), custom_call_target="tpu_custom_call" | custom-call | flops 1 | bytes 1 | tf_op jit(solution)/shard_map/rows/pallas_call | solution.py:175
  149.0 4.0 %collective-permute-done.11.refs_0_ = bf16[32,8192]{1,0:T(8,128)(2,1)S(1)} collective-permute-done((bf16[32,8192]{1,0:T(8,128)(2,1)S(1)}, bf16[32,8192]{1,0:T(8,128)(2,1)S(1)}, u32[]{:S(2)}, u32[]{:S(2)}) %collective-permute-start.11) | collective-permute-done | bytes 524320 | tf_op jit(solution)/shard_map/ppermute | solution.py:108
  155.4 5.4 %all-to-all-start = ((bf16[16,64,512]{2,1,0:T(8,128)(2,1)}), bf16[16,64,512]{2,1,0:T(8,128)(2,1)S(1)}, u32[]{:S(2)}, u32[]{:S(2)}) async-start(bf16[16,64,512]{2,1,0:T(8,128)(2,1)} %bitcast.29), calls=%async_computation | async-start | bytes 2097152 | tf_op jit(solution)/shard_map/all_to_all | solution.py:347
  160.9 2.0 collective-permute-start.15
  163.0 27.1 %collective-permute-done.15.refs_1_ = bf16[32,8192]{1,0:T(8,128)(2,1)S(1)} collective-permute-done((bf16[32,8192]{1,0:T(8,128)(2,1)S(1)}, bf16[32,8192]{1,0:T(8,128)(2,1)S(1)}, u32[]{:S(2)}, u32[]{:S(2)}) %collective-permute-start.15) | collective-permute-done | bytes 524320 | tf_op jit(solution)/shard_map/ppermute | solution.py:108
  190.1 1.9 collective-permute-done.16.refs_3_
  192.0 6.4 %copy-done.1 = bf16[8192,1152]{1,0:T(8,128)(2,1)S(1)} copy-done((bf16[8192,1152]{1,0:T(8,128)(2,1)S(1)}, bf16[8192,1152]{1,0:T(8,128)(2,1)}, u32[]{:S(2)}) %copy-start.1) | copy-done | bytes 18874392
  198.4 1.0 copy-done.21
  199.4 1.0 copy-done.23
  200.5 3.4 %rows.15 = (f32[128,1024]{1,0:T(8,128)S(1)}, bf16[128,128]{1,0:T(8,128)(2,1)S(1)}) custom-call(s32[2,16]{1,0:T(2,128)S(1)} %add_convert_fusion.table, bf16[8192,1152]{1,0:T(8,128)(2,1)S(1)} %copy-done.1, bf16[32,8192]{1,0:T(8,128)(2,1)S(1)} %copy-done.21, bf16[32,8192]{1,0:T(8,128)(2,1)S(1)} %collective-permute-done.15.refs_1_, ...), custom_call_target="tpu_custom_call" | custom-call | flops 1 | bytes 1 | tf_op jit(solution)/shard_map/rows/pallas_call | solution.py:175
  204.7 1.5 collective-permute-start.17
  206.4 2.2 collective-permute-done.17
  209.4 1.6 collective-permute-start.21
  211.0 7.2 %collective-permute-start.18 = (bf16[2,128,128]{2,1,0:T(8,128)(2,1)S(1)}, bf16[2,128,128]{2,1,0:T(8,128)(2,1)S(1)}, u32[]{:S(2)}, u32[]{:S(2)}) collective-permute-start(bf16[2,128,128]{2,1,0:T(8,128)(2,1)S(1)} %pad_maximum_fusion.refs_8_), channel_id=1, source_target_pairs={{0,4},{2,6},{4,0},{6,2},{8,12},{10,14},{12,8},{14,10},{1,5},{3,7},... | collective-permute-start | bytes 196616 | tf_op jit(solution)/shard_map/ppermute | solution.py:108
  218.3 2.3 collective-permute-start.20
  220.7 1.1 collective-permute-done.18.refs_9_
  221.8 1.8 collective-permute-done.19.refs_10_
  226.6 1.0 copy-done.17
  227.6 1.0 copy-done.19
  228.7 4.5 %finish.1 = bf16[1024,1024]{1,0:T(8,128)(2,1)} custom-call(s32[4,16]{1,0:T(4,128)S(1)} %add_add_fusion.table, f32[128,1024]{1,0:T(8,128)S(1)} %copy-done.5, f32[128,1024]{1,0:T(8,128)S(1)} %copy-done.7, f32[128,1024]{1,0:T(8,128)S(1)} %copy-done.9, f32[128,1024]{1,0:T(8,128)S(1)} %copy-done.11, f32[128,1024]{1,0:T(8,128)S(1)} %copy-done.13, ...), custom_call_target="tpu_custom_call" | custom-call | flops 1 | bytes 1 | tf_op jit(solution)/shard_map/finish/pallas_call | solution.py:263
  (84 shorter events, 16.6 us)
Async XLA Ops:
  0.0 32.5 %copy-start.25 = (s32[64]{0:T(128)S(1)}, s32[64]{0:T(128)}, u32[]{:S(2)}) copy-start(s32[64]{0:T(128)} %param.10) | copy-start | bytes 772
  0.0 32.5 %copy-start.24 = (s32[2,8]{1,0:T(2,128)S(1)}, s32[2,8]{1,0:T(2,128)}, u32[]{:S(2)}) copy-start(s32[2,8]{1,0:T(2,128)} %param.11) | copy-start | bytes 196
  3.1 27.2 %collective-permute-start = (bf16[64,8192]{1,0:T(8,128)(2,1)}, bf16[64,8192]{1,0:T(8,128)(2,1)S(1)}, u32[]{:S(2)}, u32[]{:S(2)}) collective-permute-start(bf16[64,8192]{1,0:T(8,128)(2,1)} %get-tuple-element.178), channel_id=1, source_target_pairs={{0,4},{4,8},{8,12},{12,14},{14,10},{10,6},{6,2},{2,0},{1,5},{5,9},... | collective-permute-start | bytes 3145736 | tf_op jit(solution)/shard_map/ppermute | solution.py:108
  6.1 26.4 %collective-permute-start.1 = (bf16[64,8192]{1,0:T(8,128)(2,1)}, bf16[64,8192]{1,0:T(8,128)(2,1)}, u32[]{:S(2)}, u32[]{:S(2)}) collective-permute-start(bf16[64,8192]{1,0:T(8,128)(2,1)} %get-tuple-element.177), channel_id=1, source_target_pairs={{4,0},{8,4},{12,8},{14,12},{10,14},{6,10},{2,6},{0,2},{5,1},{9,5},... | collective-permute-start | bytes 3145736 | tf_op jit(solution)/shard_map/ppermute | solution.py:108
  6.1 46.7 %collective-permute-start.4 = (bf16[64,8192]{1,0:T(8,128)(2,1)}, bf16[64,8192]{1,0:T(8,128)(2,1)}, u32[]{:S(2)}, u32[]{:S(2)}) collective-permute-start(bf16[64,8192]{1,0:T(8,128)(2,1)} %get-tuple-element.177), channel_id=1, source_target_pairs={{0,4},{4,8},{8,12},{12,14},{14,10},{10,6},{6,2},{2,0},{1,5},{5,9},... | collective-permute-start | bytes 3145736 | tf_op jit(solution)/shard_map/ppermute | solution.py:108
  8.1 46.8 %collective-permute-start.5 = (bf16[64,8192]{1,0:T(8,128)(2,1)}, bf16[64,8192]{1,0:T(8,128)(2,1)}, u32[]{:S(2)}, u32[]{:S(2)}) collective-permute-start(bf16[64,8192]{1,0:T(8,128)(2,1)} %get-tuple-element.178), channel_id=1, source_target_pairs={{4,0},{8,4},{12,8},{14,12},{10,14},{6,10},{2,6},{0,2},{5,1},{9,5},... | collective-permute-start | bytes 3145736 | tf_op jit(solution)/shard_map/ppermute | solution.py:108
  40.1 17.0 %collective-permute-start.6 = (bf16[64,8192]{1,0:T(8,128)(2,1)}, bf16[64,8192]{1,0:T(8,128)(2,1)S(1)}, u32[]{:S(2)}, u32[]{:S(2)}) collective-permute-start(bf16[64,8192]{1,0:T(8,128)(2,1)} %get-tuple-element.175), channel_id=1, source_target_pairs={{0,1},{1,0},{2,3},{3,2},{4,5},{5,4},{6,7},{7,6},{8,9},{9,8},{10,11... | collective-permute-start | bytes 3145736 | tf_op jit(solution)/shard_map/ppermute | solution.py:112
  40.1 36.4 %collective-permute-start.2 = (bf16[64,8192]{1,0:T(8,128)(2,1)S(1)}, bf16[64,8192]{1,0:T(8,128)(2,1)}, u32[]{:S(2)}, u32[]{:S(2)}) collective-permute-start(bf16[64,8192]{1,0:T(8,128)(2,1)S(1)} %collective-permute-done.refs_0_), channel_id=1, source_target_pairs={{0,4},{4,8},{8,12},{12,14},{14,10},{10,6},{6,2},{2,0},{1,5},{5,9},... | collective-permute-start | bytes 3145736 | tf_op jit(solution)/shard_map/ppermute | solution.py:108
  41.7 35.8 %collective-permute-start.3 = (bf16[64,8192]{1,0:T(8,128)(2,1)}, bf16[64,8192]{1,0:T(8,128)(2,1)}, u32[]{:S(2)}, u32[]{:S(2)}) collective-permute-start(bf16[64,8192]{1,0:T(8,128)(2,1)} %collective-permute-done.1.refs_1_), channel_id=1, source_target_pairs={{4,0},{8,4},{12,8},{14,12},{10,14},{6,10},{2,6},{0,2},{5,1},{9,5},... | collective-permute-start | bytes 3145736 | tf_op jit(solution)/shard_map/ppermute | solution.py:108
  55.0 44.8 %collective-permute-start.10 = (bf16[64,8192]{1,0:T(8,128)(2,1)}, bf16[64,8192]{1,0:T(8,128)(2,1)S(1)}, u32[]{:S(2)}, u32[]{:S(2)}) collective-permute-start(bf16[64,8192]{1,0:T(8,128)(2,1)} %collective-permute-done.5.refs_0_), channel_id=1, source_target_pairs={{4,0},{8,4},{12,8},{14,12},{10,14},{6,10},{2,6},{0,2},{5,1},{9,5},... | collective-permute-start | bytes 3145736 | tf_op jit(solution)/shard_map/ppermute | solution.py:108
  55.0 44.8 %collective-permute-start.9 = (bf16[64,8192]{1,0:T(8,128)(2,1)}, bf16[64,8192]{1,0:T(8,128)(2,1)S(1)}, u32[]{:S(2)}, u32[]{:S(2)}) collective-permute-start(bf16[64,8192]{1,0:T(8,128)(2,1)} %collective-permute-done.4.refs_1_), channel_id=1, source_target_pairs={{0,4},{4,8},{8,12},{12,14},{14,10},{10,6},{6,2},{2,0},{1,5},{5,9},... | collective-permute-start | bytes 3145736 | tf_op jit(solution)/shard_map/ppermute | solution.py:108
  57.1 5.8 %copy-start.2 = (bf16[8192,1024]{1,0:T(8,128)(2,1)S(1)}, bf16[8192,1024]{1,0:T(8,128)(2,1)}, u32[]{:S(2)}) copy-start(bf16[8192,1024]{1,0:T(8,128)(2,1)} %weight.1) | copy-start | bytes 50331652
  62.9 2.8 %copy-start.3 = (bf16[1,128,8192]{2,1,0:T(8,128)(2,1)S(1)}, bf16[1,128,8192]{2,1,0:T(8,128)(2,1)}, u32[]{:S(2)}) copy-start(bf16[1,128,8192]{2,1,0:T(8,128)(2,1)} %param.6) | copy-start | bytes 6291460
  65.7 79.1 %copy-start = (bf16[8192,1152]{1,0:T(8,128)(2,1)}, bf16[8192,1152]{1,0:T(8,128)(2,1)S(1)}, u32[]{:S(2)}) copy-start(bf16[8192,1152]{1,0:T(8,128)(2,1)S(1)} %pin.1.weights) | copy-start | bytes 56623108
  69.2 1.6 copy-start.4
  75.7 0.8 copy-start.6
  77.5 42.7 %collective-permute-start.7 = (bf16[64,8192]{1,0:T(8,128)(2,1)}, bf16[64,8192]{1,0:T(8,128)(2,1)S(1)}, u32[]{:S(2)}, u32[]{:S(2)}) collective-permute-start(bf16[64,8192]{1,0:T(8,128)(2,1)} %collective-permute-done.2.refs_0_), channel_id=1, source_target_pairs={{0,4},{4,8},{8,12},{12,14},{14,10},{10,6},{6,2},{2,0},{1,5},{5,9},... | collective-permute-start | bytes 3145736 | tf_op jit(solution)/shard_map/ppermute | solution.py:108
  79.0 43.3 %collective-permute-start.8 = (bf16[64,8192]{1,0:T(8,128)(2,1)}, bf16[64,8192]{1,0:T(8,128)(2,1)S(1)}, u32[]{:S(2)}, u32[]{:S(2)}) collective-permute-start(bf16[64,8192]{1,0:T(8,128)(2,1)} %collective-permute-done.3.refs_1_), channel_id=1, source_target_pairs={{4,0},{8,4},{12,8},{14,12},{10,14},{6,10},{2,6},{0,2},{5,1},{9,5},... | collective-permute-start | bytes 3145736 | tf_op jit(solution)/shard_map/ppermute | solution.py:108
  83.9 0.8 copy-start.8
  89.2 0.9 copy-start.10
  99.8 42.8 %collective-permute-start.13 = (bf16[64,8192]{1,0:T(8,128)(2,1)S(1)}, bf16[64,8192]{1,0:T(8,128)(2,1)S(1)}, u32[]{:S(2)}, u32[]{:S(2)}) collective-permute-start(bf16[64,8192]{1,0:T(8,128)(2,1)S(1)} %collective-permute-done.9.refs_1_), channel_id=1, source_target_pairs={{0,4},{4,8},{8,12},{12,14},{14,10},{10,6},{6,2},{2,0},{1,5},{5,9},... | collective-permute-start | bytes 3145736 | tf_op jit(solution)/shard_map/ppermute | solution.py:108
  101.4 43.4 %collective-permute-start.14 = (bf16[64,8192]{1,0:T(8,128)(2,1)S(1)}, bf16[64,8192]{1,0:T(8,128)(2,1)S(1)}, u32[]{:S(2)}, u32[]{:S(2)}) collective-permute-start(bf16[64,8192]{1,0:T(8,128)(2,1)S(1)} %collective-permute-done.10.refs_0_), channel_id=1, source_target_pairs={{4,0},{8,4},{12,8},{14,12},{10,14},{6,10},{2,6},{0,2},{5,1},{9,5},... | collective-permute-start | bytes 3145736 | tf_op jit(solution)/shard_map/ppermute | solution.py:108
  105.3 0.8 copy-start.12
  122.3 30.7 %collective-permute-start.11 = (bf16[32,8192]{1,0:T(8,128)(2,1)S(1)}, bf16[32,8192]{1,0:T(8,128)(2,1)S(1)}, u32[]{:S(2)}, u32[]{:S(2)}) collective-permute-start(bf16[32,8192]{1,0:T(8,128)(2,1)S(1)} %slice.28), channel_id=1, source_target_pairs={{0,4},{4,8},{8,12},{12,14},{14,10},{10,6},{6,2},{2,0},{1,5},{5,9},... | collective-permute-start | bytes 1572872 | tf_op jit(solution)/shard_map/ppermute | solution.py:108
  124.0 30.5 %collective-permute-start.12 = (bf16[32,8192]{1,0:T(8,128)(2,1)S(1)}, bf16[32,8192]{1,0:T(8,128)(2,1)S(1)}, u32[]{:S(2)}, u32[]{:S(2)}) collective-permute-start(bf16[32,8192]{1,0:T(8,128)(2,1)S(1)} %slice.29), channel_id=1, source_target_pairs={{4,0},{8,4},{12,8},{14,12},{10,14},{6,10},{2,6},{0,2},{5,1},{9,5},... | collective-permute-start | bytes 1572872 | tf_op jit(solution)/shard_map/ppermute | solution.py:108
  128.2 0.8 copy-start.14
  153.0 0.8 copy-start.20
  154.5 0.8 copy-start.22
  155.4 53.3 %all-to-all-start = ((bf16[16,64,512]{2,1,0:T(8,128)(2,1)}), bf16[16,64,512]{2,1,0:T(8,128)(2,1)S(1)}, u32[]{:S(2)}, u32[]{:S(2)}) async-start(bf16[16,64,512]{2,1,0:T(8,128)(2,1)} %bitcast.29), calls=%async_computation | async-start | bytes 2097152 | tf_op jit(solution)/shard_map/all_to_all | solution.py:347
  160.9 29.3 %collective-permute-start.15 = (bf16[32,8192]{1,0:T(8,128)(2,1)S(1)}, bf16[32,8192]{1,0:T(8,128)(2,1)S(1)}, u32[]{:S(2)}, u32[]{:S(2)}) collective-permute-start(bf16[32,8192]{1,0:T(8,128)(2,1)S(1)} %slice.30), channel_id=1, source_target_pairs={{0,4},{4,8},{8,12},{12,14},{14,10},{10,6},{6,2},{2,0},{1,5},{5,9},... | collective-permute-start | bytes 1572872 | tf_op jit(solution)/shard_map/ppermute | solution.py:108
  162.8 61.7 %copy-start.5 = (f32[128,1024]{1,0:T(8,128)S(1)}, f32[128,1024]{1,0:T(8,128)}, u32[]{:S(2)}) copy-start(f32[128,1024]{1,0:T(8,128)} %copy-done.4) | copy-start | bytes 1572868
  162.8 61.7 %copy-start.7 = (f32[128,1024]{1,0:T(8,128)S(1)}, f32[128,1024]{1,0:T(8,128)}, u32[]{:S(2)}) copy-start(f32[128,1024]{1,0:T(8,128)} %copy-done.6) | copy-start | bytes 1572868
  162.9 29.2 %collective-permute-start.16 = (bf16[32,8192]{1,0:T(8,128)(2,1)S(1)}, bf16[32,8192]{1,0:T(8,128)(2,1)S(1)}, u32[]{:S(2)}, u32[]{:S(2)}) collective-permute-start(bf16[32,8192]{1,0:T(8,128)(2,1)S(1)} %slice.31), channel_id=1, source_target_pairs={{4,0},{8,4},{12,8},{14,12},{10,14},{6,10},{2,6},{0,2},{5,1},{9,5},... | collective-permute-start | bytes 1572872 | tf_op jit(solution)/shard_map/ppermute | solution.py:108
  192.0 6.4 %copy-start.1 = (bf16[8192,1152]{1,0:T(8,128)(2,1)S(1)}, bf16[8192,1152]{1,0:T(8,128)(2,1)}, u32[]{:S(2)}) copy-start(bf16[8192,1152]{1,0:T(8,128)(2,1)} %copy-done) | copy-start | bytes 56623108
  198.4 1.0 copy-start.21
  199.4 1.0 copy-start.23
  200.5 24.0 %copy-start.9 = (f32[128,1024]{1,0:T(8,128)S(1)}, f32[128,1024]{1,0:T(8,128)}, u32[]{:S(2)}) copy-start(f32[128,1024]{1,0:T(8,128)} %copy-done.8) | copy-start | bytes 1572868
  200.5 24.0 %copy-start.11 = (f32[128,1024]{1,0:T(8,128)S(1)}, f32[128,1024]{1,0:T(8,128)}, u32[]{:S(2)}) copy-start(f32[128,1024]{1,0:T(8,128)} %copy-done.10) | copy-start | bytes 1572868
  203.9 0.8 copy-start.18
  204.7 3.9 %collective-permute-start.17 = (bf16[128,128]{1,0:T(8,128)(2,1)S(1)}, bf16[128,128]{1,0:T(8,128)(2,1)S(1)}, u32[]{:S(2)}, u32[]{:S(2)}) collective-permute-start(bf16[128,128]{1,0:T(8,128)(2,1)S(1)} %get-tuple-element.169), channel_id=1, source_target_pairs={{0,2},{2,0},{4,6},{6,4},{8,10},{10,8},{12,14},{14,12},{1,3},{3,1},... | collective-permute-start | bytes 98312 | tf_op jit(solution)/shard_map/ppermute | solution.py:108
  209.4 15.1 %collective-permute-start.21 = (bf16[8,64,512]{2,1,0:T(8,128)(2,1)S(1)}, bf16[8,64,512]{2,1,0:T(8,128)(2,1)S(1)}, u32[]{:S(2)}, u32[]{:S(2)}) collective-permute-start(bf16[8,64,512]{2,1,0:T(8,128)(2,1)S(1)} %take.1.refs_12_), channel_id=1, source_target_pairs={{0,16},{16,0},{1,17},{17,1},{2,18},{18,2},{3,19},{19,3},{4,20},{20... | collective-permute-start | bytes 1572872 | tf_op jit(solution)/shard_map/ppermute | solution.py:112
  211.0 10.9 %collective-permute-start.18 = (bf16[2,128,128]{2,1,0:T(8,128)(2,1)S(1)}, bf16[2,128,128]{2,1,0:T(8,128)(2,1)S(1)}, u32[]{:S(2)}, u32[]{:S(2)}) collective-permute-start(bf16[2,128,128]{2,1,0:T(8,128)(2,1)S(1)} %pad_maximum_fusion.refs_8_), channel_id=1, source_target_pairs={{0,4},{2,6},{4,0},{6,2},{8,12},{10,14},{12,8},{14,10},{1,5},{3,7},... | collective-permute-start | bytes 196616 | tf_op jit(solution)/shard_map/ppermute | solution.py:108
  218.2 5.5 %collective-permute-start.19 = (bf16[2,128,128]{2,1,0:T(8,128)(2,1)S(1)}, bf16[2,128,128]{2,1,0:T(8,128)(2,1)S(1)}, u32[]{:S(2)}, u32[]{:S(2)}) collective-permute-start(bf16[2,128,128]{2,1,0:T(8,128)(2,1)S(1)} %pad_maximum_fusion.refs_8_), channel_id=1, source_target_pairs={{0,8},{2,10},{4,12},{6,14},{8,0},{10,2},{12,4},{14,6},{1,9},{3,11}... | collective-permute-start | bytes 196616 | tf_op jit(solution)/shard_map/ppermute | solution.py:108
  218.3 6.2 %collective-permute-start.20 = (bf16[2,128,128]{2,1,0:T(8,128)(2,1)S(1)}, bf16[2,128,128]{2,1,0:T(8,128)(2,1)S(1)}, u32[]{:S(2)}, u32[]{:S(2)}) collective-permute-start(bf16[2,128,128]{2,1,0:T(8,128)(2,1)S(1)} %pad_maximum_fusion.refs_8_), channel_id=1, source_target_pairs={{0,12},{2,14},{4,8},{6,10},{8,4},{10,6},{12,0},{14,2},{1,13},{3,15... | collective-permute-start | bytes 196616 | tf_op jit(solution)/shard_map/ppermute | solution.py:108
  224.5 1.0 copy-start.13
  225.6 1.0 copy-start.15
  226.6 1.0 copy-start.17
  227.6 1.0 copy-start.19
  (1 other events, 0.8 us)

commit v10 on v8

--- a/solution.py
+++ b/solution.py
@@ -99,7 +99,9 @@
 BACK = [(b, a) for a, b in AHEAD]
 ACROSS = [(i, i ^ 1) for i in range(8)]
 ALONG = [[(i, i ^ (2 * d)) for i in range(8)] for d in (1, 2, 3)]
-HALF = BLOCK // 2
+SHARED = 32
+HALF = (BLOCK - SHARED) // 2
+STARTS = [SHARED, SHARED + HALF]
 DEPTH = 1024
 VMEM_LIMIT = 16 * 1024 * 1024
 
@@ -146,7 +148,7 @@
     )(weight, own, swapped)
 
 
-def rows_kernel(group, table, weights, *refs):
+def rows_kernel(sections, table, weights, *refs):
     *pieces, shrunk, base, shrunk_out = refs
     columns = base.shape[1]
     total = None
@@ -157,27 +159,30 @@
         part = jnp.dot(x, weights[cut, :], preferred_element_type=jnp.float32)
         total = part if total is None else total + part
     base[...] = total[:, :columns]
-    lane = lax.broadcasted_iota(jnp.int32, shrunk.shape, 1)
-    row = lax.broadcasted_iota(jnp.int32, shrunk.shape, 0)
-    use = jnp.where(
-        row < HALF,
-        jnp.where(lane < 64, table[0, 2 * group], table[1, 2 * group]),
-        jnp.where(lane < 64, table[0, 2 * group + 1], table[1, 2 * group + 1]),
-    )
     small = total[:, columns:].astype(jnp.bfloat16).astype(jnp.float32)
-    old = shrunk[...].astype(jnp.float32)
-    shrunk_out[...] = jnp.where(use > 0, small, old).astype(jnp.bfloat16)
-
-
-def rows_call(group, table, weights, pieces, shrunk):
+    values = {}
+    for at, rows, start, entry in sections:
+        lane = lax.broadcasted_iota(jnp.int32, (rows, 128), 1)
+        use = jnp.where(lane < 64, table[0, entry], table[1, entry])
+        old = values.get(start)
+        if old is None:
+            old = shrunk[start : start + rows].astype(jnp.float32)
+        values[start] = jnp.where(use > 0, small[at : at + rows], old)
+    shrunk_out[...] = shrunk[...]
+    for start, value in values.items():
+        shrunk_out[start : start + value.shape[0]] = value.astype(jnp.bfloat16)
+
+
+def rows_call(sections, table, weights, pieces, shrunk):
     columns = weights.shape[1] - 128
+    count = sum(rows for _, rows, _, _ in sections)
     operands = [pltpu.with_memory_space_constraint(weights, pltpu.VMEM)] + pieces + [shrunk]
     return pl.pallas_call(
-        functools.partial(rows_kernel, group),
+        functools.partial(rows_kernel, sections),
         in_specs=[pl.BlockSpec(memory_space=pltpu.SMEM)] + in_vmem(len(operands)),
         out_specs=in_vmem(2),
         out_shape=[
-            jax.ShapeDtypeStruct((BLOCK, columns), jnp.float32),
+            jax.ShapeDtypeStruct((count, columns), jnp.float32),
             jax.ShapeDtypeStruct((BLOCK, 128), jnp.bfloat16),
         ],
         name="rows",
@@ -229,41 +234,61 @@
     )(table, got)
 
 
-def finish_kernel(table, *refs):
-    *bases, shrunk, up_mine, up_other, out, rows, sems = refs
+def finish_kernel(jobs, table, *refs):
+    count = len(refs) - 12
+    bases, gathered, refs = refs[:count], refs[count : count + 4], refs[count + 4 :]
+    up_mine, up_other, out, base, shrunk, rows, base_sems, sems = refs
     part = up_mine.shape[2]
     group = table[3, 0]
-    copies = []
-    for i in range(16):
-        block, half = table[0, i], i % 2
-        own = pl.ds(half * HALF, HALF)
-        both = shrunk[table[1, i], own, :].astype(jnp.float32)
-        value = jnp.where(table[2, i] > 0, both[:, 64:], both[:, :64]).astype(jnp.bfloat16)
+    fetches = []
+    for g, source in enumerate(bases):
+        to = base.at[g, pl.ds(0, source.shape[0])]
+        fetches.append(pltpu.make_async_copy(source, to, base_sems.at[g]))
+        fetches[-1].start()
+    for i, pair in enumerate(gathered):
+        shrunk[pl.ds(2 * i, 2)] = pair[...]
+    copies, fetched = [], set()
+    for entry, (g, at, count, start) in enumerate(jobs):
+        block = table[0, entry]
+        if g not in fetched:
+            fetches[g].wait()
+            fetched.add(g)
+        own = pl.ds(at, count)
+        both = shrunk[table[1, entry], start : start + count, :].astype(jnp.float32)
+        value = jnp.where(table[2, entry] > 0, both[:, 64:], both[:, :64]).astype(jnp.bfloat16)
         for up, side in ((up_mine, group), (up_other, 1 - group)):
             cut = pl.ds(pl.multiple_of(side * part, part), part)
             grown = jnp.dot(value, up[block], preferred_element_type=jnp.float32)
-            rows[i, :, cut] = (bases[i // 2][own, cut] + 0.5 * grown).astype(rows.dtype)
-        to = pl.ds(pl.multiple_of((2 * block + half) * HALF, HALF), HALF)
-        copies.append(pltpu.make_async_copy(rows.at[i], out.at[to], sems.at[i]))
+            rows[entry, :count, cut] = (base[g, own, cut] + 0.5 * grown).astype(rows.dtype)
+        to = pl.ds(pl.multiple_of(block * BLOCK + start, 16), count)
+        copies.append(
+            pltpu.make_async_copy(rows.at[entry, pl.ds(0, count)], out.at[to], sems.at[entry])
+        )
         copies[-1].start()
     for copy in copies:
         copy.wait()
 
 
-def finish_call(table, bases, shrunk, up_mine, up_other):
+def finish_call(jobs, table, bases, gathered, up_mine, up_other):
     columns = bases[0].shape[1]
     return pl.pallas_call(
-        finish_kernel,
-        in_specs=[pl.BlockSpec(memory_space=pltpu.SMEM)] + in_vmem(11),
+        functools.partial(finish_kernel, jobs),
+        in_specs=[pl.BlockSpec(memory_space=pltpu.SMEM)]
+        + [pl.BlockSpec(memory_space=pl.ANY)] * len(bases)
+        + in_vmem(6),
         out_specs=pl.BlockSpec(memory_space=pltpu.HBM),
         out_shape=jax.ShapeDtypeStruct((8 * BLOCK, columns), jnp.bfloat16),
         scratch_shapes=[
-            pltpu.VMEM((16, HALF, columns), jnp.bfloat16),
-            pltpu.SemaphoreType.DMA((16,)),
+            pltpu.VMEM((len(bases), BLOCK, columns), jnp.float32),
+            pltpu.VMEM((8,) + gathered[0].shape[1:], jnp.bfloat16),
+            pltpu.VMEM((len(jobs), HALF, columns), jnp.bfloat16),
+            pltpu.SemaphoreType.DMA((len(bases),)),
+            pltpu.SemaphoreType.DMA((len(jobs),)),
         ],
         name="finish",
-        **settings(),
-    )(table, *bases, shrunk, up_mine, up_other)
+        compiler_params=pltpu.CompilerParams(vmem_limit_bytes=48 * 1024 * 1024),
+        cost_estimate=pl.CostEstimate(flops=1, bytes_accessed=1, transcendentals=0),
+    )(table, *bases, *gathered, up_mine, up_other)
 
 
 def chain_body(
@@ -276,7 +301,8 @@
     myself = me * 2 + store
     held, rank, width = adapter_down_maps.shape
     rows = tokens[0]
-    halves = [rows[:HALF], rows[HALF:]]
+    shared = lax.all_gather(rows[:SHARED], "tensor", axis=0)
+    halves = [rows[start : start + HALF] for start in STARTS]
 
     ahead, back = list(halves), list(halves[::-1])
     flight = [(send(ahead[k], AHEAD), send(back[k], BACK)) for k in range(2)]
@@ -310,11 +336,21 @@
     blocks = jnp.where(places < 4, 2 * places, 15 - 2 * places).astype(jnp.int32)
     hit = blocks[:, None] == jnp.arange(8, dtype=jnp.int32)[None, :]
     owners = jnp.sum(jnp.where(hit, owner_row[None, :], 0), axis=1)
+    blocks = jnp.concatenate([blocks, jnp.arange(8, dtype=jnp.int32)])
+    owners = jnp.concatenate([owners, owner_row])
     table = jnp.stack([owners == myself, owners == me * 2 + 1 - store]).astype(jnp.int32)
 
-    bases = []
+    sections = [
+        [(0, HALF, STARTS[0], 2 * g), (HALF, HALF, STARTS[1], 2 * g + 1)] for g in range(8)
+    ] + [[(SHARED * i, SHARED, 0, 16 + 4 * g + i) for i in range(4)] for g in range(2)]
+    bases = [None] * 10
     shrunk = jnp.zeros((BLOCK, 2 * rank), jnp.bfloat16)
-    groups = [[rows], [ahead[2], back[2]]]
+
+    def work(g, pieces):
+        bases[g], value = rows_call(sections[g], table, weights, pieces, shrunk)
+        return value
+
+    groups = [halves, [ahead[2], back[2]]]
     for k in range(1, 7):
         (got_ahead, got_back), ahead, back, bases, shrunk, up_sent = lax.optimization_barrier(
             (flight[k], ahead, back, bases, shrunk, up_sent)
@@ -324,22 +360,26 @@
         if k < 5:
             flight.append((send(ahead[k + 2], AHEAD), send(back[k + 2], BACK)))
         groups.append([got_ahead, got_back] if k % 2 == 0 else [got_back, got_ahead])
-        for g in range(len(bases), min(len(bases) + 2, k + 2)):
-            base, shrunk = rows_call(g, table, weights, groups[g], shrunk)
-            bases.append(base)
+        for g in {1: (0, 1), 2: (2, 3)}.get(k, (k + 1,)):
+            shrunk = work(g, groups[g])
+        if k == 4:
+            shared = shared.reshape(2, 4 * SHARED, width)
+            for g in range(2):
+                shrunk = work(8 + g, [shared[g]])
     shrunk, up_sent = lax.optimization_barrier((shrunk, up_sent))
     up_got = lax.all_to_all(
         up_sent.reshape(16, rank, -1), ("tensor", "store"), split_axis=0, concat_axis=0, tiled=True
     )
-
+    across, up_got = lax.optimization_barrier((send(shrunk, ACROSS), up_got))
+    pair = jnp.stack([shrunk, across])
+    everyone = [pair] + [send(pair, pairs) for pairs in ALONG]
     up_mine = take_call(owner_row, up_got)
     up_other = swap(up_mine, "groups")
-    pair = jnp.stack([shrunk, send(shrunk, ACROSS)])
-    everyone = jnp.concatenate([pair] + [send(pair, pairs) for pairs in ALONG])
     home, core = owners // 2, owners % 2
     where = 2 * ((home // 2) ^ z) + ((home % 2) ^ y)
-    table = jnp.stack([blocks, where, core != store, jnp.broadcast_to(group, (16,))])
-    return finish_call(table.astype(jnp.int32), bases, everyone, up_mine, up_other)[None]
+    table = jnp.stack([blocks, where, core != store, jnp.broadcast_to(group, blocks.shape)])
+    jobs = [(g, at, count, start) for g in range(10) for at, count, start, _ in sections[g]]
+    return finish_call(jobs, table.astype(jnp.int32), bases, everyone, up_mine, up_other)[None]
 
 
 def body(tokens, *rest):

time: 224 us -> 252 us (1.12)
  the two profiles are of different devices: /device:TPU:13 before, /device:TPU:0 now
where the time goes in v10:
time: 252 us; the launch traced here: 251 us
  waiting for transfers between devices  116 us (46%)
  Pallas kernels  54.3 us (22%)
  local copies, waits for them, and re-layouts  31.8 us (13%)
  starting transfers between devices  30.2 us (12%)
  between operations  17.6 us (7%)
    ppermute x18, waiting for transfers between devices, send(): return lax.ppermute(value, 'tensor', pairs)  101 us
    pallas_call x10, Pallas kernels, rows_call(): pl.pallas_call(functools.partial(rows_kernel, sections), in_specs=[pl.Blo...  41.5 us
    ppermute x18, starting transfers between devices, send(): return lax.ppermute(value, 'tensor', pairs)  23.8 us
    unnamed x54, local copies, waits for them, and re-layouts  23.2 us
    all_to_all x1, waiting for transfers between devices, chain_body(): lax.all_to_all(up_sent.reshape(16, rank, -1), ('tensor', 'store'), split_...  13.7 us
    pallas_call x1, Pallas kernels, finish_call(): pl.pallas_call(functools.partial(finish_kernel, jobs), in_specs=[pl.Block...  6.44 us
  transfers between devices with their start and end apart: 22, of which 15 were waited for; matrix products, arithmetic and copies ran while one was open for 3% of the time, Pallas kernels for 17%

profile of v10, /device:TPU:0, one launch (start us, length us, event | category | flops | bytes accessed | tf_op | source)
XLA Modules:
  0.0 250.9 jit_solution(9235165657815460601)
XLA Ops:
  6.5 1.9 slice.28
  8.5 1.5 slice_bitcast_fusion
  10.0 3.1 %collective-permute-start = (bf16[48,8192]{1,0:T(8,128)(2,1)S(1)}, bf16[48,8192]{1,0:T(8,128)(2,1)}, u32[]{:S(2)}, u32[]{:S(2)}) collective-permute-start(bf16[48,8192]{1,0:T(8,128)(2,1)S(1)} %get-tuple-element.174.refs_0_), channel_id=1, source_target_pairs={{0,4},{4,8},{8,12},{12,14},{14,10},{10,6},{6,2},{2,0},{1,5},{5,9},... | collective-permute-start | bytes 2359304 | tf_op jit(solution)/shard_map/ppermute | solution.py:110
  13.1 2.0 collective-permute-start.4
  15.2 25.6 %collective-permute-done.refs_0_ = bf16[48,8192]{1,0:T(8,128)(2,1)} collective-permute-done((bf16[48,8192]{1,0:T(8,128)(2,1)S(1)}, bf16[48,8192]{1,0:T(8,128)(2,1)}, u32[]{:S(2)}, u32[]{:S(2)}) %collective-permute-start) | collective-permute-done | bytes 786464 | tf_op jit(solution)/shard_map/ppermute | solution.py:110
  40.7 8.8 %collective-permute-done.1.refs_1_ = bf16[48,8192]{1,0:T(8,128)(2,1)} collective-permute-done((bf16[48,8192]{1,0:T(8,128)(2,1)S(1)}, bf16[48,8192]{1,0:T(8,128)(2,1)}, u32[]{:S(2)}, u32[]{:S(2)}) %collective-permute-start.1) | collective-permute-done | bytes 786464 | tf_op jit(solution)/shard_map/ppermute | solution.py:110
  54.3 1.7 dynamic-slice_bitcast_fusion
  56.2 2.0 collective-permute-start.3
  58.3 2.9 %pack.1 = bf16[8,2,64,512]{3,2,1,0:T(8,128)(2,1)} custom-call(s32[3]{0:T(128)S(1)} %pad_add_fusion.1.table, bf16[4,64,8192]{2,1,0:T(8,128)(2,1)} %up.1), custom_call_target="tpu_custom_call" | custom-call | flops 1 | bytes 1 | tf_op jit(solution)/shard_map/pack/pallas_call | solution.py:203
  61.2 5.3 %collective-permute-done.4.refs_1_ = bf16[48,8192]{1,0:T(8,128)(2,1)S(1)} collective-permute-done((bf16[48,8192]{1,0:T(8,128)(2,1)S(1)}, bf16[48,8192]{1,0:T(8,128)(2,1)S(1)}, u32[]{:S(2)}, u32[]{:S(2)}) %collective-permute-start.4) | collective-permute-done | bytes 786464 | tf_op jit(solution)/shard_map/ppermute | solution.py:110
  66.5 4.8 %collective-permute-done.5.refs_0_ = bf16[48,8192]{1,0:T(8,128)(2,1)S(1)} collective-permute-done((bf16[48,8192]{1,0:T(8,128)(2,1)S(1)}, bf16[48,8192]{1,0:T(8,128)(2,1)S(1)}, u32[]{:S(2)}, u32[]{:S(2)}) %collective-permute-start.5) | collective-permute-done | bytes 786464 | tf_op jit(solution)/shard_map/ppermute | solution.py:110
  71.4 2.0 collective-permute-start.9
  73.6 5.8 %copy-done.2 = bf16[8192,1024]{1,0:T(8,128)(2,1)S(1)} copy-done((bf16[8192,1024]{1,0:T(8,128)(2,1)S(1)}, bf16[8192,1024]{1,0:T(8,128)(2,1)}, u32[]{:S(2)}) %copy-start.2) | copy-done | bytes 16777240
  79.4 2.8 %pin.1.weights = bf16[8192,1152]{1,0:T(8,128)(2,1)S(1)} custom-call(bf16[8192,1024]{1,0:T(8,128)(2,1)S(1)} %copy-done.2, bf16[64,8192]{1,0:T(8,128)(2,1)S(1)} %get-tuple-element.172.own, bf16[64,8192]{1,0:T(8,128)(2,1)S(1)} %collective-permute-done.6.swapped), custom_call_target="tpu_custom_call" | custom-call | flops 1 | bytes 1 | tf_op jit(solution)/shard_map/pin/pallas_call | solution.py:140
  82.2 3.8 %rows.10 = (f32[96,1024]{1,0:T(8,128)S(1)}, bf16[128,128]{1,0:T(8,128)(2,1)S(1)}) custom-call(s32[2,24]{1,0:T(2,128)S(1)} %add_convert_fusion.table, bf16[8192,1152]{1,0:T(8,128)(2,1)S(1)} %pin.1.weights, bf16[48,8192]{1,0:T(8,128)(2,1)S(1)} %get-tuple-element.174.refs_0_, bf16[48,8192]{1,0:T(8,128)(2,1)S(1)} %get-tuple-element.173.refs_1_, ...), custom_call_target="tpu_custom_call" | custom-call | flops 1 | bytes 1 | tf_op jit(solution)/shard_map/rows/pallas_call | solution.py:180
  86.0 5.8 %rows.11 = (f32[96,1024]{1,0:T(8,128)S(1)}, bf16[128,128]{1,0:T(8,128)(2,1)S(1)}) custom-call(s32[2,24]{1,0:T(2,128)S(1)} %add_convert_fusion.table, bf16[8192,1152]{1,0:T(8,128)(2,1)S(1)} %pin.1.weights, bf16[48,8192]{1,0:T(8,128)(2,1)} %collective-permute-done.refs_0_, bf16[48,8192]{1,0:T(8,128)(2,1)} %collective-permute-done.1.refs_1_, ...), custom_call_target="tpu_custom_call" | custom-call | flops 1 | bytes 1 | tf_op jit(solution)/shard_map/rows/pallas_call | solution.py:180
  92.6 7.7 %collective-permute-done.2.refs_0_ = bf16[48,8192]{1,0:T(8,128)(2,1)S(1)} collective-permute-done((bf16[48,8192]{1,0:T(8,128)(2,1)}, bf16[48,8192]{1,0:T(8,128)(2,1)S(1)}, u32[]{:S(2)}, u32[]{:S(2)}) %collective-permute-start.2) | collective-permute-done | bytes 786464 | tf_op jit(solution)/shard_map/ppermute | solution.py:110
  100.3 17.2 %collective-permute-done.3.refs_1_ = bf16[48,8192]{1,0:T(8,128)(2,1)S(1)} collective-permute-done((bf16[48,8192]{1,0:T(8,128)(2,1)}, bf16[48,8192]{1,0:T(8,128)(2,1)S(1)}, u32[]{:S(2)}, u32[]{:S(2)}) %collective-permute-start.3) | collective-permute-done | bytes 786464 | tf_op jit(solution)/shard_map/ppermute | solution.py:110
  117.5 2.0 collective-permute-start.8
  119.5 3.8 %rows.12 = (f32[96,1024]{1,0:T(8,128)S(1)}, bf16[128,128]{1,0:T(8,128)(2,1)S(1)}) custom-call(s32[2,24]{1,0:T(2,128)S(1)} %add_convert_fusion.table, bf16[8192,1152]{1,0:T(8,128)(2,1)S(1)} %pin.1.weights, bf16[48,8192]{1,0:T(8,128)(2,1)S(1)} %collective-permute-done.5.refs_0_, bf16[48,8192]{1,0:T(8,128)(2,1)S(1)} %collective-permute-done.4.refs_1_, ...), custom_call_target="tpu_custom_call" | custom-call | flops 1 | bytes 1 | tf_op jit(solution)/shard_map/rows/pallas_call | solution.py:180
  123.4 3.8 %rows.13 = (f32[96,1024]{1,0:T(8,128)S(1)}, bf16[128,128]{1,0:T(8,128)(2,1)S(1)}) custom-call(s32[2,24]{1,0:T(2,128)S(1)} %add_convert_fusion.table, bf16[8192,1152]{1,0:T(8,128)(2,1)S(1)} %pin.1.weights, bf16[48,8192]{1,0:T(8,128)(2,1)S(1)} %collective-permute-done.2.refs_0_, bf16[48,8192]{1,0:T(8,128)(2,1)S(1)} %collective-permute-done.3.refs_1_, ...), custom_call_target="tpu_custom_call" | custom-call | flops 1 | bytes 1 | tf_op jit(solution)/shard_map/rows/pallas_call | solution.py:180
  127.9 6.8 %collective-permute-done.10.refs_0_ = bf16[48,8192]{1,0:T(8,128)(2,1)} collective-permute-done((bf16[48,8192]{1,0:T(8,128)(2,1)S(1)}, bf16[48,8192]{1,0:T(8,128)(2,1)}, u32[]{:S(2)}, u32[]{:S(2)}) %collective-permute-start.10) | collective-permute-done | bytes 786464 | tf_op jit(solution)/shard_map/ppermute | solution.py:110
  134.7 1.6 collective-permute-start.13
  136.8 4.6 %rows.14 = (f32[96,1024]{1,0:T(8,128)S(1)}, bf16[128,128]{1,0:T(8,128)(2,1)S(1)}) custom-call(s32[2,24]{1,0:T(2,128)S(1)} %add_convert_fusion.table, bf16[8192,1152]{1,0:T(8,128)(2,1)S(1)} %pin.1.weights, bf16[48,8192]{1,0:T(8,128)(2,1)} %collective-permute-done.10.refs_0_, bf16[48,8192]{1,0:T(8,128)(2,1)} %collective-permute-done.9.refs_1_, ...), custom_call_target="tpu_custom_call" | custom-call | flops 1 | bytes 1 | tf_op jit(solution)/shard_map/rows/pallas_call | solution.py:180
  142.2 6.8 %collective-permute-done.7.refs_0_ = bf16[48,8192]{1,0:T(8,128)(2,1)S(1)} collective-permute-done((bf16[48,8192]{1,0:T(8,128)(2,1)S(1)}, bf16[48,8192]{1,0:T(8,128)(2,1)S(1)}, u32[]{:S(2)}, u32[]{:S(2)}) %collective-permute-start.7) | collective-permute-done | bytes 786464 | tf_op jit(solution)/shard_map/ppermute | solution.py:110
  149.0 2.5 %collective-permute-done.8.refs_1_ = bf16[48,8192]{1,0:T(8,128)(2,1)S(1)} collective-permute-done((bf16[48,8192]{1,0:T(8,128)(2,1)S(1)}, bf16[48,8192]{1,0:T(8,128)(2,1)S(1)}, u32[]{:S(2)}, u32[]{:S(2)}) %collective-permute-start.8) | collective-permute-done | bytes 786464 | tf_op jit(solution)/shard_map/ppermute | solution.py:110
  151.5 1.6 collective-permute-start.11
  153.5 3.8 %rows.15 = (f32[96,1024]{1,0:T(8,128)S(1)}, bf16[128,128]{1,0:T(8,128)(2,1)S(1)}) custom-call(s32[2,24]{1,0:T(2,128)S(1)} %add_convert_fusion.table, bf16[8192,1152]{1,0:T(8,128)(2,1)S(1)} %pin.1.weights, bf16[48,8192]{1,0:T(8,128)(2,1)S(1)} %collective-permute-done.7.refs_0_, bf16[48,8192]{1,0:T(8,128)(2,1)S(1)} %collective-permute-done.8.refs_1_, ...), custom_call_target="tpu_custom_call" | custom-call | flops 1 | bytes 1 | tf_op jit(solution)/shard_map/rows/pallas_call | solution.py:180
  158.7 2.7 %fusion.4 = (bf16[4,32,8192]{2,1,0:T(8,128)(2,1)S(1)}, bf16[4,32,8192]{2,1,0:T(8,128)(2,1)S(1)}) fusion(bf16[8,32,8192]{2,1,0:T(8,128)(2,1)} %all-gather.2.cloned.1.call-done), kind=kLoop, calls=%fused_computation.44 | loop fusion | bytes 8388608 | tf_op jit(solution)/shard_map/slice | solution.py:368
  161.4 6.4 %copy-done.1 = bf16[8192,1152]{1,0:T(8,128)(2,1)S(1)} copy-done((bf16[8192,1152]{1,0:T(8,128)(2,1)S(1)}, bf16[8192,1152]{1,0:T(8,128)(2,1)}, u32[]{:S(2)}) %copy-start.1) | copy-done | bytes 18874392
  167.8 3.5 %rows.16 = (f32[128,1024]{1,0:T(8,128)S(1)}, bf16[128,128]{1,0:T(8,128)(2,1)S(1)}) custom-call(s32[2,24]{1,0:T(2,128)S(1)} %add_convert_fusion.table, bf16[8192,1152]{1,0:T(8,128)(2,1)S(1)} %copy-done.1, bf16[128,8192]{1,0:T(8,128)(2,1)S(1)} %bitcast.33, bf16[128,128]{1,0:T(8,128)(2,1)S(1)} %copy-done.22), custom_call_target="tpu_custom_call" | custom-call | flops 1 | bytes 1 | tf_op jit(solution)/shard_map/rows/pallas_call | solution.py:180
  172.1 3.5 %rows.17 = (f32[128,1024]{1,0:T(8,128)S(1)}, bf16[128,128]{1,0:T(8,128)(2,1)S(1)}) custom-call(s32[2,24]{1,0:T(2,128)S(1)} %add_convert_fusion.table, bf16[8192,1152]{1,0:T(8,128)(2,1)S(1)} %copy-done.1, bf16[128,8192]{1,0:T(8,128)(2,1)S(1)} %bitcast.32, bf16[128,128]{1,0:T(8,128)(2,1)S(1)} %get-tuple-element.128.refs_1_), custom_call_target="tpu_custom_call" | custom-call | flops 1 | bytes 1 | tf_op jit(solution)/shard_map/rows/pallas_call | solution.py:180
  175.6 3.8 %rows.18 = (f32[96,1024]{1,0:T(8,128)S(1)}, bf16[128,128]{1,0:T(8,128)(2,1)S(1)}) custom-call(s32[2,24]{1,0:T(2,128)S(1)} %add_convert_fusion.table, bf16[8192,1152]{1,0:T(8,128)(2,1)S(1)} %copy-done.1, bf16[48,8192]{1,0:T(8,128)(2,1)S(1)} %collective-permute-done.14.refs_0_, bf16[48,8192]{1,0:T(8,128)(2,1)S(1)} %collective-permute-done.13.refs_1_, ...), custom_call_target="tpu_custom_call" | custom-call | flops 1 | bytes 1 | tf_op jit(solution)/shard_map/rows/pallas_call | solution.py:180
  180.2 1.3 collective-permute-done.11.refs_0_
  181.5 2.3 collective-permute-done.12.refs_1_
  183.8 5.0 %rows.19 = (f32[96,1024]{1,0:T(8,128)S(1)}, bf16[128,128]{1,0:T(8,128)(2,1)S(1)}) custom-call(s32[2,24]{1,0:T(2,128)S(1)} %add_convert_fusion.table, bf16[8192,1152]{1,0:T(8,128)(2,1)S(1)} %copy-done.1, bf16[48,8192]{1,0:T(8,128)(2,1)} %collective-permute-done.11.refs_0_, bf16[48,8192]{1,0:T(8,128)(2,1)} %collective-permute-done.12.refs_1_, ...), custom_call_target="tpu_custom_call" | custom-call | flops 1 | bytes 1 | tf_op jit(solution)/shard_map/rows/pallas_call | solution.py:180
  189.7 4.8 %all-to-all-start = ((bf16[16,64,512]{2,1,0:T(8,128)(2,1)}), bf16[16,64,512]{2,1,0:T(8,128)(2,1)S(1)}, u32[]{:S(2)}, u32[]{:S(2)}) async-start(bf16[16,64,512]{2,1,0:T(8,128)(2,1)} %bitcast.22), calls=%async_computation | async-start | bytes 2097152 | tf_op jit(solution)/shard_map/all_to_all | solution.py:370
  194.5 1.9 collective-permute-start.15
  196.6 7.1 %collective-permute-done.15 = bf16[128,128]{1,0:T(8,128)(2,1)S(1)} collective-permute-done((bf16[128,128]{1,0:T(8,128)(2,1)S(1)}, bf16[128,128]{1,0:T(8,128)(2,1)S(1)}, u32[]{:S(2)}, u32[]{:S(2)}) %collective-permute-start.15) | collective-permute-done | bytes 32800 | tf_op jit(solution)/shard_map/ppermute | solution.py:110
  203.7 13.7 %all-to-all-done.got = bf16[16,64,512]{2,1,0:T(8,128)(2,1)S(1)} async-done(((bf16[16,64,512]{2,1,0:T(8,128)(2,1)}), bf16[16,64,512]{2,1,0:T(8,128)(2,1)S(1)}, u32[]{:S(2)}, u32[]{:S(2)}) %all-to-all-start) | async-done | bytes 1048608 | tf_op jit(solution)/shard_map/all_to_all | solution.py:370
  218.1 1.5 collective-permute-start.19
  219.7 3.3 %collective-permute-start.16 = (bf16[2,128,128]{2,1,0:T(8,128)(2,1)S(1)}, bf16[2,128,128]{2,1,0:T(8,128)(2,1)S(1)}, u32[]{:S(2)}, u32[]{:S(2)}) collective-permute-start(bf16[2,128,128]{2,1,0:T(8,128)(2,1)S(1)} %pad_maximum_fusion.refs_10_), channel_id=1, source_target_pairs={{0,4},{2,6},{4,0},{6,2},{8,12},{10,14},{12,8},{14,10},{1,5},{3,7},... | collective-permute-start | bytes 196616 | tf_op jit(solution)/shard_map/ppermute | solution.py:110
  223.0 1.9 collective-permute-start.17
  224.9 1.4 collective-permute-start.18
  226.4 4.9 %collective-permute-done.17.refs_12_ = bf16[2,128,128]{2,1,0:T(8,128)(2,1)S(1)} collective-permute-done((bf16[2,128,128]{2,1,0:T(8,128)(2,1)S(1)}, bf16[2,128,128]{2,1,0:T(8,128)(2,1)S(1)}, u32[]{:S(2)}, u32[]{:S(2)}) %collective-permute-start.17) | collective-permute-done | bytes 65568 | tf_op jit(solution)/shard_map/ppermute | solution.py:110
  231.3 1.4 collective-permute-done.19.refs_15_
  235.7 1.0 copy-done.18
  237.6 6.4 %finish.1 = bf16[1024,1024]{1,0:T(8,128)(2,1)} custom-call(s32[4,24]{1,0:T(4,128)S(1)} %add_add_fusion.table, f32[96,1024]{1,0:T(8,128)S(1)} %get-tuple-element.146.refs_0_, f32[96,1024]{1,0:T(8,128)S(1)} %copy-done.8, f32[96,1024]{1,0:T(8,128)S(1)} %copy-done.10, f32[96,1024]{1,0:T(8,128)S(1)} %copy-done.12, f32[96,1024]{1,0:T(8,128)S(1)} %copy-done.14, ...), custom_call_target="tpu_custom_call" | custom-call | flops 1 | bytes 1 | tf_op jit(solution)/shard_map/finish/pallas_call | solution.py:274
  (88 shorter events, 13.4 us)
Async XLA Ops:
  6.5 43.0 %copy-start.24 = (s32[64]{0:T(128)S(1)}, s32[64]{0:T(128)}, u32[]{:S(2)}) copy-start(s32[64]{0:T(128)} %param.10) | copy-start | bytes 772
  6.5 43.0 %copy-start.23 = (s32[2,8]{1,0:T(2,128)S(1)}, s32[2,8]{1,0:T(2,128)}, u32[]{:S(2)}) copy-start(s32[2,8]{1,0:T(2,128)} %param.11) | copy-start | bytes 196
  6.5 152.2 %all-gather.2.cloned.1.call-start = ((), (), s32[]{:S(2)}) async-start(), calls=%async_computation.1 | async-start | bytes 4718592 | tf_op jit(solution)/shard_map/all_gather | solution.py:304
  10.0 30.8 %collective-permute-start = (bf16[48,8192]{1,0:T(8,128)(2,1)S(1)}, bf16[48,8192]{1,0:T(8,128)(2,1)}, u32[]{:S(2)}, u32[]{:S(2)}) collective-permute-start(bf16[48,8192]{1,0:T(8,128)(2,1)S(1)} %get-tuple-element.174.refs_0_), channel_id=1, source_target_pairs={{0,4},{4,8},{8,12},{12,14},{14,10},{10,6},{6,2},{2,0},{1,5},{5,9},... | collective-permute-start | bytes 2359304 | tf_op jit(solution)/shard_map/ppermute | solution.py:110
  13.0 36.5 %collective-permute-start.1 = (bf16[48,8192]{1,0:T(8,128)(2,1)S(1)}, bf16[48,8192]{1,0:T(8,128)(2,1)}, u32[]{:S(2)}, u32[]{:S(2)}) collective-permute-start(bf16[48,8192]{1,0:T(8,128)(2,1)S(1)} %get-tuple-element.173.refs_1_), channel_id=1, source_target_pairs={{4,0},{8,4},{12,8},{14,12},{10,14},{6,10},{2,6},{0,2},{5,1},{9,5},... | collective-permute-start | bytes 2359304 | tf_op jit(solution)/shard_map/ppermute | solution.py:110
  13.1 53.5 %collective-permute-start.4 = (bf16[48,8192]{1,0:T(8,128)(2,1)S(1)}, bf16[48,8192]{1,0:T(8,128)(2,1)S(1)}, u32[]{:S(2)}, u32[]{:S(2)}) collective-permute-start(bf16[48,8192]{1,0:T(8,128)(2,1)S(1)} %get-tuple-element.173.refs_1_), channel_id=1, source_target_pairs={{0,4},{4,8},{8,12},{12,14},{14,10},{10,6},{6,2},{2,0},{1,5},{5,9},... | collective-permute-start | bytes 2359304 | tf_op jit(solution)/shard_map/ppermute | solution.py:110
  15.1 56.3 %collective-permute-start.5 = (bf16[48,8192]{1,0:T(8,128)(2,1)S(1)}, bf16[48,8192]{1,0:T(8,128)(2,1)S(1)}, u32[]{:S(2)}, u32[]{:S(2)}) collective-permute-start(bf16[48,8192]{1,0:T(8,128)(2,1)S(1)} %get-tuple-element.174.refs_0_), channel_id=1, source_target_pairs={{4,0},{8,4},{12,8},{14,12},{10,14},{6,10},{2,6},{0,2},{5,1},{9,5},... | collective-permute-start | bytes 2359304 | tf_op jit(solution)/shard_map/ppermute | solution.py:110
  56.0 17.6 %collective-permute-start.6 = (bf16[64,8192]{1,0:T(8,128)(2,1)S(1)}, bf16[64,8192]{1,0:T(8,128)(2,1)S(1)}, u32[]{:S(2)}, u32[]{:S(2)}) collective-permute-start(bf16[64,8192]{1,0:T(8,128)(2,1)S(1)} %get-tuple-element.171), channel_id=1, source_target_pairs={{0,1},{1,0},{2,3},{3,2},{4,5},{5,4},{6,7},{7,6},{8,9},{9,8},{10,11... | collective-permute-start | bytes 3145736 | tf_op jit(solution)/shard_map/ppermute | solution.py:114
  56.1 17.4 %copy-start.25 = (s32[16]{0:T(128)}, s32[16]{0:T(128)S(1)}, u32[]{:S(2)}) copy-start(s32[16]{0:T(128)S(1)} %compare_select_fusion.3) | copy-start | bytes 196
  56.1 44.2 %collective-permute-start.2 = (bf16[48,8192]{1,0:T(8,128)(2,1)}, bf16[48,8192]{1,0:T(8,128)(2,1)S(1)}, u32[]{:S(2)}, u32[]{:S(2)}) collective-permute-start(bf16[48,8192]{1,0:T(8,128)(2,1)} %collective-permute-done.refs_0_), channel_id=1, source_target_pairs={{0,4},{4,8},{8,12},{12,14},{14,10},{10,6},{6,2},{2,0},{1,5},{5,9},... | collective-permute-start | bytes 2359304 | tf_op jit(solution)/shard_map/ppermute | solution.py:110
  56.2 61.3 %collective-permute-start.3 = (bf16[48,8192]{1,0:T(8,128)(2,1)}, bf16[48,8192]{1,0:T(8,128)(2,1)S(1)}, u32[]{:S(2)}, u32[]{:S(2)}) collective-permute-start(bf16[48,8192]{1,0:T(8,128)(2,1)} %collective-permute-done.1.refs_1_), channel_id=1, source_target_pairs={{4,0},{8,4},{12,8},{14,12},{10,14},{6,10},{2,6},{0,2},{5,1},{9,5},... | collective-permute-start | bytes 2359304 | tf_op jit(solution)/shard_map/ppermute | solution.py:110
  71.4 63.4 %collective-permute-start.10 = (bf16[48,8192]{1,0:T(8,128)(2,1)S(1)}, bf16[48,8192]{1,0:T(8,128)(2,1)}, u32[]{:S(2)}, u32[]{:S(2)}) collective-permute-start(bf16[48,8192]{1,0:T(8,128)(2,1)S(1)} %collective-permute-done.5.refs_0_), channel_id=1, source_target_pairs={{4,0},{8,4},{12,8},{14,12},{10,14},{6,10},{2,6},{0,2},{5,1},{9,5},... | collective-permute-start | bytes 2359304 | tf_op jit(solution)/shard_map/ppermute | solution.py:110
  71.4 63.4 %collective-permute-start.9 = (bf16[48,8192]{1,0:T(8,128)(2,1)S(1)}, bf16[48,8192]{1,0:T(8,128)(2,1)}, u32[]{:S(2)}, u32[]{:S(2)}) collective-permute-start(bf16[48,8192]{1,0:T(8,128)(2,1)S(1)} %collective-permute-done.4.refs_1_), channel_id=1, source_target_pairs={{0,4},{4,8},{8,12},{12,14},{14,10},{10,6},{6,2},{2,0},{1,5},{5,9},... | collective-permute-start | bytes 2359304 | tf_op jit(solution)/shard_map/ppermute | solution.py:110
  73.6 5.8 %copy-start.2 = (bf16[8192,1024]{1,0:T(8,128)(2,1)S(1)}, bf16[8192,1024]{1,0:T(8,128)(2,1)}, u32[]{:S(2)}) copy-start(bf16[8192,1024]{1,0:T(8,128)(2,1)} %weight.1) | copy-start | bytes 50331652
  82.2 71.3 %copy-start = (bf16[8192,1152]{1,0:T(8,128)(2,1)}, bf16[8192,1152]{1,0:T(8,128)(2,1)S(1)}, u32[]{:S(2)}) copy-start(bf16[8192,1152]{1,0:T(8,128)(2,1)S(1)} %pin.1.weights) | copy-start | bytes 56623108
  91.9 0.8 copy-start.7
  117.5 31.4 %collective-permute-start.7 = (bf16[48,8192]{1,0:T(8,128)(2,1)S(1)}, bf16[48,8192]{1,0:T(8,128)(2,1)S(1)}, u32[]{:S(2)}, u32[]{:S(2)}) collective-permute-start(bf16[48,8192]{1,0:T(8,128)(2,1)S(1)} %collective-permute-done.2.refs_0_), channel_id=1, source_target_pairs={{0,4},{4,8},{8,12},{12,14},{14,10},{10,6},{6,2},{2,0},{1,5},{5,9},... | collective-permute-start | bytes 2359304 | tf_op jit(solution)/shard_map/ppermute | solution.py:110
  117.5 34.0 %collective-permute-start.8 = (bf16[48,8192]{1,0:T(8,128)(2,1)S(1)}, bf16[48,8192]{1,0:T(8,128)(2,1)S(1)}, u32[]{:S(2)}, u32[]{:S(2)}) collective-permute-start(bf16[48,8192]{1,0:T(8,128)(2,1)S(1)} %collective-permute-done.3.refs_1_), channel_id=1, source_target_pairs={{4,0},{8,4},{12,8},{14,12},{10,14},{6,10},{2,6},{0,2},{5,1},{9,5},... | collective-permute-start | bytes 2359304 | tf_op jit(solution)/shard_map/ppermute | solution.py:110
  123.4 3.8 %copy-start.9 = (f32[96,1024]{1,0:T(8,128)}, f32[96,1024]{1,0:T(8,128)S(1)}, u32[]{:S(2)}) copy-start(f32[96,1024]{1,0:T(8,128)S(1)} %get-tuple-element.148.refs_2_) | copy-start | bytes 1179652
  127.2 0.7 copy-start.11
  134.7 40.8 %collective-permute-start.13 = (bf16[48,8192]{1,0:T(8,128)(2,1)}, bf16[48,8192]{1,0:T(8,128)(2,1)S(1)}, u32[]{:S(2)}, u32[]{:S(2)}) collective-permute-start(bf16[48,8192]{1,0:T(8,128)(2,1)} %collective-permute-done.9.refs_1_), channel_id=1, source_target_pairs={{0,4},{4,8},{8,12},{12,14},{14,10},{10,6},{6,2},{2,0},{1,5},{5,9},... | collective-permute-start | bytes 2359304 | tf_op jit(solution)/shard_map/ppermute | solution.py:110
  136.3 39.3 %collective-permute-start.14 = (bf16[48,8192]{1,0:T(8,128)(2,1)}, bf16[48,8192]{1,0:T(8,128)(2,1)S(1)}, u32[]{:S(2)}, u32[]{:S(2)}) collective-permute-start(bf16[48,8192]{1,0:T(8,128)(2,1)} %collective-permute-done.10.refs_0_), channel_id=1, source_target_pairs={{4,0},{8,4},{12,8},{14,12},{10,14},{6,10},{2,6},{0,2},{5,1},{9,5},... | collective-permute-start | bytes 2359304 | tf_op jit(solution)/shard_map/ppermute | solution.py:110
  141.4 0.8 copy-start.13
  151.5 30.0 %collective-permute-start.11 = (bf16[48,8192]{1,0:T(8,128)(2,1)S(1)}, bf16[48,8192]{1,0:T(8,128)(2,1)}, u32[]{:S(2)}, u32[]{:S(2)}) collective-permute-start(bf16[48,8192]{1,0:T(8,128)(2,1)S(1)} %collective-permute-done.7.refs_0_), channel_id=1, source_target_pairs={{0,4},{4,8},{8,12},{12,14},{14,10},{10,6},{6,2},{2,0},{1,5},{5,9},... | collective-permute-start | bytes 2359304 | tf_op jit(solution)/shard_map/ppermute | solution.py:110
  153.1 30.8 %collective-permute-start.12 = (bf16[48,8192]{1,0:T(8,128)(2,1)S(1)}, bf16[48,8192]{1,0:T(8,128)(2,1)}, u32[]{:S(2)}, u32[]{:S(2)}) collective-permute-start(bf16[48,8192]{1,0:T(8,128)(2,1)S(1)} %collective-permute-done.8.refs_1_), channel_id=1, source_target_pairs={{4,0},{8,4},{12,8},{14,12},{10,14},{6,10},{2,6},{0,2},{5,1},{9,5},... | collective-permute-start | bytes 2359304 | tf_op jit(solution)/shard_map/ppermute | solution.py:110
  157.3 0.8 copy-start.15
  158.7 2.7 %copy-start.22 = (bf16[128,128]{1,0:T(8,128)(2,1)S(1)}, bf16[128,128]{1,0:T(8,128)(2,1)}, u32[]{:S(2)}) copy-start(bf16[128,128]{1,0:T(8,128)(2,1)} %copy-done.21) | copy-start | bytes 98308
  161.4 6.4 %copy-start.1 = (bf16[8192,1152]{1,0:T(8,128)(2,1)S(1)}, bf16[8192,1152]{1,0:T(8,128)(2,1)}, u32[]{:S(2)}) copy-start(bf16[8192,1152]{1,0:T(8,128)(2,1)} %copy-done) | copy-start | bytes 56623108
  171.3 0.8 copy-start.3
  175.6 3.8 %copy-start.5 = (f32[128,1024]{1,0:T(8,128)}, f32[128,1024]{1,0:T(8,128)S(1)}, u32[]{:S(2)}) copy-start(f32[128,1024]{1,0:T(8,128)S(1)} %get-tuple-element.158.refs_9_) | copy-start | bytes 1572868
  179.4 0.8 copy-start.17
  183.8 12.6 %copy-start.26 = (s32[16]{0:T(128)S(1)}, s32[16]{0:T(128)}, u32[]{:S(2)}) copy-start(s32[16]{0:T(128)} %copy-done.25) | copy-start | bytes 196
  183.8 48.8 %copy-start.4 = (f32[128,1024]{1,0:T(8,128)S(1)}, f32[128,1024]{1,0:T(8,128)}, u32[]{:S(2)}) copy-start(f32[128,1024]{1,0:T(8,128)} %copy-done.3) | copy-start | bytes 1572868
  183.8 48.8 %copy-start.6 = (f32[128,1024]{1,0:T(8,128)S(1)}, f32[128,1024]{1,0:T(8,128)}, u32[]{:S(2)}) copy-start(f32[128,1024]{1,0:T(8,128)} %copy-done.5) | copy-start | bytes 1572868
  183.8 48.8 %copy-start.8 = (f32[96,1024]{1,0:T(8,128)S(1)}, f32[96,1024]{1,0:T(8,128)}, u32[]{:S(2)}) copy-start(f32[96,1024]{1,0:T(8,128)} %copy-done.7) | copy-start | bytes 1179652
  183.8 48.8 %copy-start.10 = (f32[96,1024]{1,0:T(8,128)S(1)}, f32[96,1024]{1,0:T(8,128)}, u32[]{:S(2)}) copy-start(f32[96,1024]{1,0:T(8,128)} %copy-done.9) | copy-start | bytes 1179652
  188.9 0.8 copy-start.19
  189.7 27.8 %all-to-all-start = ((bf16[16,64,512]{2,1,0:T(8,128)(2,1)}), bf16[16,64,512]{2,1,0:T(8,128)(2,1)S(1)}, u32[]{:S(2)}, u32[]{:S(2)}) async-start(bf16[16,64,512]{2,1,0:T(8,128)(2,1)} %bitcast.22), calls=%async_computation | async-start | bytes 2097152 | tf_op jit(solution)/shard_map/all_to_all | solution.py:370
  194.5 9.2 %collective-permute-start.15 = (bf16[128,128]{1,0:T(8,128)(2,1)S(1)}, bf16[128,128]{1,0:T(8,128)(2,1)S(1)}, u32[]{:S(2)}, u32[]{:S(2)}) collective-permute-start(bf16[128,128]{1,0:T(8,128)(2,1)S(1)} %get-tuple-element.161), channel_id=1, source_target_pairs={{0,2},{2,0},{4,6},{6,4},{8,10},{10,8},{12,14},{14,12},{1,3},{3,1},... | collective-permute-start | bytes 98312 | tf_op jit(solution)/shard_map/ppermute | solution.py:110
  218.1 14.5 %collective-permute-start.19 = (bf16[8,64,512]{2,1,0:T(8,128)(2,1)S(1)}, bf16[8,64,512]{2,1,0:T(8,128)(2,1)S(1)}, u32[]{:S(2)}, u32[]{:S(2)}) collective-permute-start(bf16[8,64,512]{2,1,0:T(8,128)(2,1)S(1)} %take.1.refs_14_), channel_id=1, source_target_pairs={{0,16},{16,0},{1,17},{17,1},{2,18},{18,2},{3,19},{19,3},{4,20},{20... | collective-permute-start | bytes 1572872 | tf_op jit(solution)/shard_map/ppermute | solution.py:114
  219.7 6.7 %collective-permute-start.16 = (bf16[2,128,128]{2,1,0:T(8,128)(2,1)S(1)}, bf16[2,128,128]{2,1,0:T(8,128)(2,1)S(1)}, u32[]{:S(2)}, u32[]{:S(2)}) collective-permute-start(bf16[2,128,128]{2,1,0:T(8,128)(2,1)S(1)} %pad_maximum_fusion.refs_10_), channel_id=1, source_target_pairs={{0,4},{2,6},{4,0},{6,2},{8,12},{10,14},{12,8},{14,10},{1,5},{3,7},... | collective-permute-start | bytes 196616 | tf_op jit(solution)/shard_map/ppermute | solution.py:110
  223.0 8.3 %collective-permute-start.17 = (bf16[2,128,128]{2,1,0:T(8,128)(2,1)S(1)}, bf16[2,128,128]{2,1,0:T(8,128)(2,1)S(1)}, u32[]{:S(2)}, u32[]{:S(2)}) collective-permute-start(bf16[2,128,128]{2,1,0:T(8,128)(2,1)S(1)} %pad_maximum_fusion.refs_10_), channel_id=1, source_target_pairs={{0,8},{2,10},{4,12},{6,14},{8,0},{10,2},{12,4},{14,6},{1,9},{3,11}... | collective-permute-start | bytes 196616 | tf_op jit(solution)/shard_map/ppermute | solution.py:110
  224.9 6.3 %collective-permute-start.18 = (bf16[2,128,128]{2,1,0:T(8,128)(2,1)S(1)}, bf16[2,128,128]{2,1,0:T(8,128)(2,1)S(1)}, u32[]{:S(2)}, u32[]{:S(2)}) collective-permute-start(bf16[2,128,128]{2,1,0:T(8,128)(2,1)S(1)} %pad_maximum_fusion.refs_10_), channel_id=1, source_target_pairs={{0,12},{2,14},{4,8},{6,10},{8,4},{10,6},{12,0},{14,2},{1,13},{3,15... | collective-permute-start | bytes 196616 | tf_op jit(solution)/shard_map/ppermute | solution.py:110
  232.7 1.0 copy-start.12
  233.7 1.0 copy-start.14
  234.7 1.0 copy-start.16
  235.7 1.0 copy-start.18
  236.7 1.0 copy-start.20
  (1 other events, 0.6 us)
Sparse Core Ops, SparseCore 0:
  9.5 124.0 all-gather.1

commit v11 on v9

--- a/solution.py
+++ b/solution.py
@@ -137,7 +137,7 @@
     width, columns = weight.shape
     return pl.pallas_call(
         pin_kernel,
-        in_specs=[pl.BlockSpec(memory_space=pltpu.HBM)] + in_vmem(2),
+        in_specs=[pl.BlockSpec(memory_space=pl.ANY)] + in_vmem(2),
         out_specs=in_vmem(1)[0],
         out_shape=pltpu.VMEM((width, columns + 2 * own.shape[0]), weight.dtype),
         scratch_shapes=[pltpu.SemaphoreType.DMA],
@@ -276,7 +276,13 @@
         ],
         name="finish",
         **settings(),
-    )(table, *bases, *gathered, up_mine, up_other)
+    )(
+        table,
+        *[pltpu.with_memory_space_constraint(base, pltpu.HBM) for base in bases],
+        *gathered,
+        up_mine,
+        up_other,
+    )
 
 
 def chain_body(
@@ -328,32 +334,28 @@
     bases = []
     shrunk = jnp.zeros((BLOCK, 2 * rank), jnp.bfloat16)
     groups = [[rows], [ahead[2], back[2]]]
-    for k in range(1, 6):
+    for k in range(1, 7):
         (got_ahead, got_back), ahead, back, bases, shrunk, up_sent = lax.optimization_barrier(
             (flight[k], ahead, back, bases, shrunk, up_sent)
         )
         ahead.append(got_ahead)
         back.append(got_back)
-        if k < 4:
+        if k < 5:
             flight.append((send(ahead[k + 2], AHEAD), send(back[k + 2], BACK)))
-        else:
-            cut = slice(0, HALF // 2) if k == 4 else slice(HALF // 2, HALF)
-            flight.append((send(ahead[6][cut], AHEAD), send(back[6][cut], BACK)))
         groups.append([got_ahead, got_back] if k % 2 == 0 else [got_back, got_ahead])
-        for g in range(len(bases), min(len(bases) + 2, k + 2)):
+        for g in range(len(bases), min(len(bases) + 2, k + 2, 7)):
             base, shrunk = rows_call(g, table, weights, groups[g], shrunk)
             bases.append(base)
-    first, bases, shrunk, up_sent = lax.optimization_barrier((flight[6], bases, shrunk, up_sent))
     up_got = lax.all_to_all(
         up_sent.reshape(16, rank, -1), ("tensor", "store"), split_axis=0, concat_axis=0, tiled=True
     )
-    first, second, bases, shrunk = lax.optimization_barrier((first, flight[7], bases, shrunk))
-    base, shrunk = rows_call(7, table, weights, [first[0], second[0], first[1], second[1]], shrunk)
+    base, shrunk = rows_call(7, table, weights, groups[7], shrunk)
     bases.append(base)
 
-    across, up_got = lax.optimization_barrier((send(shrunk, ACROSS), up_got))
+    across = send(shrunk, ACROSS)
     pair = jnp.stack([shrunk, across])
     everyone = [pair] + [send(pair, pairs) for pairs in ALONG]
+    up_got, _ = lax.optimization_barrier((up_got, across))
     up_mine = take_call(owner_row, up_got)
     up_other = swap(up_mine, "groups")
     home, core = owners // 2, owners % 2

time: 236 us -> 215 us (0.911)
  local copies, waits for them, and re-layouts: 34.1 us -> 26 us
  waiting for transfers between devices: 117 us -> 109 us
  starting transfers between devices: 35.8 us -> 30.2 us
    ppermute x20 -> x18, waiting for transfers between devices: 117 us -> 100 us  [send(): return lax.ppermute(value, 'tensor', pairs)]
    unnamed x52 -> x28, local copies, waits for them, and re-layouts: 27.2 us -> 19.2 us
    all_to_all x1, waiting for transfers between devices: 0.01 us -> 7.76 us  [chain_body(): lax.all_to_all(up_sent.reshape(16, rank, -1), ('tensor', 'store'), split_...]
    ppermute x20 -> x18, starting transfers between devices: 28.8 us -> 23.7 us  [send(): return lax.ppermute(value, 'tensor', pairs)]
  transfers between devices with their start and end apart: 23 -> 21, of which waited for: 18 -> 15; matrix products, arithmetic and copies ran while one was open for 2% -> 2% of each run, Pallas kernels for 16% -> 18%
where the time goes in v11:
time: 215 us; the launch traced here: 214 us
  waiting for transfers between devices  109 us (51%)
  Pallas kernels  43.7 us (20%)
  starting transfers between devices  30.2 us (14%)
  local copies, waits for them, and re-layouts  26 us (12%)
  between operations  4.38 us (2%)
    ppermute x18, waiting for transfers between devices, send(): return lax.ppermute(value, 'tensor', pairs)  100 us
    pallas_call x8, Pallas kernels, rows_call(): pl.pallas_call(functools.partial(rows_kernel, group), in_specs=[pl.BlockS...  32 us
    ppermute x18, starting transfers between devices, send(): return lax.ppermute(value, 'tensor', pairs)  23.7 us
    unnamed x28, local copies, waits for them, and re-layouts  19.2 us
    all_to_all x1, waiting for transfers between devices, chain_body(): lax.all_to_all(up_sent.reshape(16, rank, -1), ('tensor', 'store'), split_...  7.76 us
    pallas_call x1, Pallas kernels, finish_call(): pl.pallas_call(finish_kernel, in_specs=[pl.BlockSpec(memory_space=pltpu.S...  5.24 us
    all_to_all x1, starting transfers between devices, chain_body(): lax.all_to_all(up_sent.reshape(16, rank, -1), ('tensor', 'store'), split_...  4.93 us
  transfers between devices with their start and end apart: 21, of which 15 were waited for; matrix products, arithmetic and copies ran while one was open for 2% of the time, Pallas kernels for 18%

profile of v11, /device:TPU:0, one launch (start us, length us, event | category | flops | bytes accessed | tf_op | source)
XLA Modules:
  0.0 214.3 jit_solution(17136000063785776543)
XLA Ops:
  0.0 3.1 %slice_bitcast_fusion = (bf16[64,8192]{1,0:T(8,128)(2,1)}, bf16[64,8192]{1,0:T(8,128)(2,1)}) fusion(bf16[1,128,8192]{2,1,0:T(8,128)(2,1)} %param.6), kind=kLoop, calls=%fused_computation.2 | loop fusion | bytes 4194304 | tf_op jit(solution)/shard_map/slice | solution.py:298
  3.1 3.0 %collective-permute-start = (bf16[64,8192]{1,0:T(8,128)(2,1)}, bf16[64,8192]{1,0:T(8,128)(2,1)}, u32[]{:S(2)}, u32[]{:S(2)}) collective-permute-start(bf16[64,8192]{1,0:T(8,128)(2,1)} %get-tuple-element.148), channel_id=1, source_target_pairs={{0,4},{4,8},{8,12},{12,14},{14,10},{10,6},{6,2},{2,0},{1,5},{5,9},... | collective-permute-start | bytes 3145736 | tf_op jit(solution)/shard_map/ppermute | solution.py:108
  6.1 2.0 collective-permute-start.4
  8.2 22.2 %collective-permute-done.refs_0_ = bf16[64,8192]{1,0:T(8,128)(2,1)} collective-permute-done((bf16[64,8192]{1,0:T(8,128)(2,1)}, bf16[64,8192]{1,0:T(8,128)(2,1)}, u32[]{:S(2)}, u32[]{:S(2)}) %collective-permute-start) | collective-permute-done | bytes 1048608 | tf_op jit(solution)/shard_map/ppermute | solution.py:108
  30.4 2.2 %collective-permute-done.1.refs_1_ = bf16[64,8192]{1,0:T(8,128)(2,1)} collective-permute-done((bf16[64,8192]{1,0:T(8,128)(2,1)}, bf16[64,8192]{1,0:T(8,128)(2,1)}, u32[]{:S(2)}, u32[]{:S(2)}) %collective-permute-start.1) | collective-permute-done | bytes 1048608 | tf_op jit(solution)/shard_map/ppermute | solution.py:108
  37.5 2.7 %dynamic-slice_bitcast_fusion = (bf16[64,8192]{1,0:T(8,128)(2,1)}, bf16[64,8192]{1,0:T(8,128)(2,1)S(1)}) fusion(bf16[4,64,8192]{2,1,0:T(8,128)(2,1)} %param.8, s32[]{:T(128)S(6)} %select_n.151, s32[]{:T(128)S(6)} %select_n.149), kind=kLoop, calls=%fused_computation | loop fusion | bytes 4194312 | tf_op jit(solution)/shard_map/jit(dynamic_index_in_dim)/squeeze | solution.py:318
  40.2 1.7 collective-permute-start.2
  42.4 2.9 %pack.1 = bf16[8,2,64,512]{3,2,1,0:T(8,128)(2,1)} custom-call(s32[3]{0:T(128)S(1)} %pad_add_fusion.table, bf16[4,64,8192]{2,1,0:T(8,128)(2,1)} %up.1), custom_call_target="tpu_custom_call" | custom-call | flops 1 | bytes 1 | tf_op jit(solution)/shard_map/pack/pallas_call | solution.py:198
  45.3 7.4 %collective-permute-done.4.refs_1_ = bf16[64,8192]{1,0:T(8,128)(2,1)S(1)} collective-permute-done((bf16[64,8192]{1,0:T(8,128)(2,1)}, bf16[64,8192]{1,0:T(8,128)(2,1)S(1)}, u32[]{:S(2)}, u32[]{:S(2)}) %collective-permute-start.4) | collective-permute-done | bytes 1048608 | tf_op jit(solution)/shard_map/ppermute | solution.py:108
  52.7 2.3 %collective-permute-done.5.refs_0_ = bf16[64,8192]{1,0:T(8,128)(2,1)} collective-permute-done((bf16[64,8192]{1,0:T(8,128)(2,1)}, bf16[64,8192]{1,0:T(8,128)(2,1)}, u32[]{:S(2)}, u32[]{:S(2)}) %collective-permute-start.5) | collective-permute-done | bytes 1048608 | tf_op jit(solution)/shard_map/ppermute | solution.py:108
  55.0 2.0 collective-permute-start.9
  57.2 5.8 %copy-done.2 = bf16[8192,1024]{1,0:T(8,128)(2,1)S(1)} copy-done((bf16[8192,1024]{1,0:T(8,128)(2,1)S(1)}, bf16[8192,1024]{1,0:T(8,128)(2,1)}, u32[]{:S(2)}) %copy-start.2) | copy-done | bytes 16777240
  62.9 2.8 %pin.1.weights = bf16[8192,1152]{1,0:T(8,128)(2,1)S(1)} custom-call(bf16[8192,1024]{1,0:T(8,128)(2,1)S(1)} %copy-done.2, bf16[64,8192]{1,0:T(8,128)(2,1)S(1)} %get-tuple-element.146.own, bf16[64,8192]{1,0:T(8,128)(2,1)S(1)} %collective-permute-done.6.swapped), custom_call_target="tpu_custom_call" | custom-call | flops 1 | bytes 1 | tf_op jit(solution)/shard_map/pin/pallas_call | solution.py:138
  65.7 3.5 %rows.8 = (f32[128,1024]{1,0:T(8,128)S(1)}, bf16[128,128]{1,0:T(8,128)(2,1)S(1)}) custom-call(s32[2,16]{1,0:T(2,128)S(1)} %add_convert_fusion.table, bf16[8192,1152]{1,0:T(8,128)(2,1)S(1)} %pin.1.weights, bf16[128,8192]{1,0:T(8,128)(2,1)S(1)} %bitcast.56, bf16[128,128]{1,0:T(8,128)(2,1)S(1)} %broadcast_in_dim.48.refs_1_), custom_call_target="tpu_custom_call" | custom-call | flops 1 | bytes 1 | tf_op jit(solution)/shard_map/rows/pallas_call | solution.py:175
  69.2 1.5 copy-done.4
  70.7 6.0 %rows.9 = (f32[128,1024]{1,0:T(8,128)S(1)}, bf16[128,128]{1,0:T(8,128)(2,1)S(1)}) custom-call(s32[2,16]{1,0:T(2,128)S(1)} %add_convert_fusion.table, bf16[8192,1152]{1,0:T(8,128)(2,1)S(1)} %pin.1.weights, bf16[64,8192]{1,0:T(8,128)(2,1)} %collective-permute-done.refs_0_, bf16[64,8192]{1,0:T(8,128)(2,1)} %collective-permute-done.1.refs_1_, ...), custom_call_target="tpu_custom_call" | custom-call | flops 1 | bytes 1 | tf_op jit(solution)/shard_map/rows/pallas_call | solution.py:175
  77.5 1.6 collective-permute-start.7
  79.6 4.2 %rows.10 = (f32[128,1024]{1,0:T(8,128)S(1)}, bf16[128,128]{1,0:T(8,128)(2,1)S(1)}) custom-call(s32[2,16]{1,0:T(2,128)S(1)} %add_convert_fusion.table, bf16[8192,1152]{1,0:T(8,128)(2,1)S(1)} %pin.1.weights, bf16[64,8192]{1,0:T(8,128)(2,1)} %collective-permute-done.5.refs_0_, bf16[64,8192]{1,0:T(8,128)(2,1)S(1)} %collective-permute-done.4.refs_1_, ...), custom_call_target="tpu_custom_call" | custom-call | flops 1 | bytes 1 | tf_op jit(solution)/shard_map/rows/pallas_call | solution.py:175
  83.8 0.8 copy-done.6
  84.6 4.5 %rows.11 = (f32[128,1024]{1,0:T(8,128)S(1)}, bf16[128,128]{1,0:T(8,128)(2,1)S(1)}) custom-call(s32[2,16]{1,0:T(2,128)S(1)} %add_convert_fusion.table, bf16[8192,1152]{1,0:T(8,128)(2,1)S(1)} %pin.1.weights, bf16[64,8192]{1,0:T(8,128)(2,1)} %collective-permute-done.2.refs_0_, bf16[64,8192]{1,0:T(8,128)(2,1)} %collective-permute-done.3.refs_1_, ...), custom_call_target="tpu_custom_call" | custom-call | flops 1 | bytes 1 | tf_op jit(solution)/shard_map/rows/pallas_call | solution.py:175
  89.9 10.0 %collective-permute-done.10.refs_0_ = bf16[64,8192]{1,0:T(8,128)(2,1)S(1)} collective-permute-done((bf16[64,8192]{1,0:T(8,128)(2,1)}, bf16[64,8192]{1,0:T(8,128)(2,1)S(1)}, u32[]{:S(2)}, u32[]{:S(2)}) %collective-permute-start.10) | collective-permute-done | bytes 1048608 | tf_op jit(solution)/shard_map/ppermute | solution.py:108
  99.8 1.6 collective-permute-start.13
  101.9 3.5 %rows.12 = (f32[128,1024]{1,0:T(8,128)S(1)}, bf16[128,128]{1,0:T(8,128)(2,1)S(1)}) custom-call(s32[2,16]{1,0:T(2,128)S(1)} %add_convert_fusion.table, bf16[8192,1152]{1,0:T(8,128)(2,1)S(1)} %pin.1.weights, bf16[64,8192]{1,0:T(8,128)(2,1)S(1)} %collective-permute-done.10.refs_0_, bf16[64,8192]{1,0:T(8,128)(2,1)S(1)} %collective-permute-done.9.refs_1_, ...), custom_call_target="tpu_custom_call" | custom-call | flops 1 | bytes 1 | tf_op jit(solution)/shard_map/rows/pallas_call | solution.py:175
  106.2 14.0 %collective-permute-done.7.refs_0_ = bf16[64,8192]{1,0:T(8,128)(2,1)S(1)} collective-permute-done((bf16[64,8192]{1,0:T(8,128)(2,1)}, bf16[64,8192]{1,0:T(8,128)(2,1)S(1)}, u32[]{:S(2)}, u32[]{:S(2)}) %collective-permute-start.7) | collective-permute-done | bytes 1048608 | tf_op jit(solution)/shard_map/ppermute | solution.py:108
  120.2 2.2 %collective-permute-done.8.refs_1_ = bf16[64,8192]{1,0:T(8,128)(2,1)S(1)} collective-permute-done((bf16[64,8192]{1,0:T(8,128)(2,1)}, bf16[64,8192]{1,0:T(8,128)(2,1)S(1)}, u32[]{:S(2)}, u32[]{:S(2)}) %collective-permute-start.8) | collective-permute-done | bytes 1048608 | tf_op jit(solution)/shard_map/ppermute | solution.py:108
  122.3 1.6 collective-permute-start.11
  124.3 3.5 %rows.13 = (f32[128,1024]{1,0:T(8,128)S(1)}, bf16[128,128]{1,0:T(8,128)(2,1)S(1)}) custom-call(s32[2,16]{1,0:T(2,128)S(1)} %add_convert_fusion.table, bf16[8192,1152]{1,0:T(8,128)(2,1)S(1)} %pin.1.weights, bf16[64,8192]{1,0:T(8,128)(2,1)S(1)} %collective-permute-done.7.refs_0_, bf16[64,8192]{1,0:T(8,128)(2,1)S(1)} %collective-permute-done.8.refs_1_, ...), custom_call_target="tpu_custom_call" | custom-call | flops 1 | bytes 1 | tf_op jit(solution)/shard_map/rows/pallas_call | solution.py:175
  127.8 0.8 copy-done.9
  128.7 14.0 %collective-permute-done.13.refs_1_ = bf16[64,8192]{1,0:T(8,128)(2,1)S(1)} collective-permute-done((bf16[64,8192]{1,0:T(8,128)(2,1)S(1)}, bf16[64,8192]{1,0:T(8,128)(2,1)S(1)}, u32[]{:S(2)}, u32[]{:S(2)}) %collective-permute-start.13) | collective-permute-done | bytes 1048608 | tf_op jit(solution)/shard_map/ppermute | solution.py:108
  142.6 2.2 %collective-permute-done.14.refs_0_ = bf16[64,8192]{1,0:T(8,128)(2,1)S(1)} collective-permute-done((bf16[64,8192]{1,0:T(8,128)(2,1)S(1)}, bf16[64,8192]{1,0:T(8,128)(2,1)S(1)}, u32[]{:S(2)}, u32[]{:S(2)}) %collective-permute-start.14) | collective-permute-done | bytes 1048608 | tf_op jit(solution)/shard_map/ppermute | solution.py:108
  144.8 3.5 %rows.14 = (f32[128,1024]{1,0:T(8,128)S(1)}, bf16[128,128]{1,0:T(8,128)(2,1)S(1)}) custom-call(s32[2,16]{1,0:T(2,128)S(1)} %add_convert_fusion.table, bf16[8192,1152]{1,0:T(8,128)(2,1)S(1)} %pin.1.weights, bf16[64,8192]{1,0:T(8,128)(2,1)S(1)} %collective-permute-done.14.refs_0_, bf16[64,8192]{1,0:T(8,128)(2,1)S(1)} %collective-permute-done.13.refs_1_, ...), custom_call_target="tpu_custom_call" | custom-call | flops 1 | bytes 1 | tf_op jit(solution)/shard_map/rows/pallas_call | solution.py:175
  148.3 0.8 copy-done.10
  149.1 15.2 %collective-permute-done.11.refs_0_ = bf16[64,8192]{1,0:T(8,128)(2,1)S(1)} collective-permute-done((bf16[64,8192]{1,0:T(8,128)(2,1)S(1)}, bf16[64,8192]{1,0:T(8,128)(2,1)S(1)}, u32[]{:S(2)}, u32[]{:S(2)}) %collective-permute-start.11) | collective-permute-done | bytes 1048608 | tf_op jit(solution)/shard_map/ppermute | solution.py:108
  164.3 1.5 collective-permute-done.12.refs_1_
  165.8 4.9 %all-to-all-start = ((bf16[16,64,512]{2,1,0:T(8,128)(2,1)}), bf16[16,64,512]{2,1,0:T(8,128)(2,1)S(1)}, u32[]{:S(2)}, u32[]{:S(2)}) async-start(bf16[16,64,512]{2,1,0:T(8,128)(2,1)} %bitcast.30), calls=%async_computation | async-start | bytes 2097152 | tf_op jit(solution)/shard_map/all_to_all | solution.py:349
  170.7 6.4 %copy-done.1 = bf16[8192,1152]{1,0:T(8,128)(2,1)S(1)} copy-done((bf16[8192,1152]{1,0:T(8,128)(2,1)S(1)}, bf16[8192,1152]{1,0:T(8,128)(2,1)}, u32[]{:S(2)}) %copy-start.1) | copy-done | bytes 18874392
  177.1 3.4 %rows.15 = (f32[128,1024]{1,0:T(8,128)S(1)}, bf16[128,128]{1,0:T(8,128)(2,1)S(1)}) custom-call(s32[2,16]{1,0:T(2,128)S(1)} %add_convert_fusion.table, bf16[8192,1152]{1,0:T(8,128)(2,1)S(1)} %copy-done.1, bf16[64,8192]{1,0:T(8,128)(2,1)S(1)} %collective-permute-done.11.refs_0_, bf16[64,8192]{1,0:T(8,128)(2,1)S(1)} %collective-permute-done.12.refs_1_, ...), custom_call_target="tpu_custom_call" | custom-call | flops 1 | bytes 1 | tf_op jit(solution)/shard_map/rows/pallas_call | solution.py:175
  180.5 0.8 copy-done.11
  181.3 1.9 collective-permute-start.15
  183.5 2.4 %collective-permute-done.15 = bf16[128,128]{1,0:T(8,128)(2,1)S(1)} collective-permute-done((bf16[128,128]{1,0:T(8,128)(2,1)S(1)}, bf16[128,128]{1,0:T(8,128)(2,1)S(1)}, u32[]{:S(2)}, u32[]{:S(2)}) %collective-permute-start.15) | collective-permute-done | bytes 32800 | tf_op jit(solution)/shard_map/ppermute | solution.py:108
  185.9 7.8 %all-to-all-done.got = bf16[16,64,512]{2,1,0:T(8,128)(2,1)S(1)} async-done(((bf16[16,64,512]{2,1,0:T(8,128)(2,1)}), bf16[16,64,512]{2,1,0:T(8,128)(2,1)S(1)}, u32[]{:S(2)}, u32[]{:S(2)}) %all-to-all-start) | async-done | bytes 1048608 | tf_op jit(solution)/shard_map/all_to_all | solution.py:349
  194.4 1.6 collective-permute-start.19
  196.0 3.3 %collective-permute-start.16 = (bf16[2,128,128]{2,1,0:T(8,128)(2,1)S(1)}, bf16[2,128,128]{2,1,0:T(8,128)(2,1)S(1)}, u32[]{:S(2)}, u32[]{:S(2)}) collective-permute-start(bf16[2,128,128]{2,1,0:T(8,128)(2,1)S(1)} %pad_maximum_fusion.refs_8_), channel_id=1, source_target_pairs={{0,4},{2,6},{4,0},{6,2},{8,12},{10,14},{12,8},{14,10},{1,5},{3,7},... | collective-permute-start | bytes 196616 | tf_op jit(solution)/shard_map/ppermute | solution.py:108
  199.2 1.9 collective-permute-start.17
  201.2 1.4 collective-permute-start.18
  202.6 4.9 %collective-permute-done.17.refs_10_ = bf16[2,128,128]{2,1,0:T(8,128)(2,1)S(1)} collective-permute-done((bf16[2,128,128]{2,1,0:T(8,128)(2,1)S(1)}, bf16[2,128,128]{2,1,0:T(8,128)(2,1)S(1)}, u32[]{:S(2)}, u32[]{:S(2)}) %collective-permute-start.17) | collective-permute-done | bytes 65568 | tf_op jit(solution)/shard_map/ppermute | solution.py:108
  207.5 1.4 collective-permute-done.19.refs_13_
  208.9 5.2 %finish.1 = bf16[1024,1024]{1,0:T(8,128)(2,1)} custom-call(s32[4,16]{1,0:T(4,128)S(1)} %add_add_fusion.table, f32[128,1024]{1,0:T(8,128)} %copy-done.4, f32[128,1024]{1,0:T(8,128)} %copy-done.5, f32[128,1024]{1,0:T(8,128)} %copy-done.6, f32[128,1024]{1,0:T(8,128)} %copy-done.7, f32[128,1024]{1,0:T(8,128)} %copy-done.8, f32[128,1024]{1,0:T(8,128)} %copy-done.9, ...), custom_call_target="tpu_custom_call" | custom-call | flops 1 | bytes 1 | tf_op jit(solution)/shard_map/finish/pallas_call | solution.py:263
  (52 shorter events, 6.4 us)
Async XLA Ops:
  0.0 32.5 %copy-start.13 = (s32[64]{0:T(128)S(1)}, s32[64]{0:T(128)}, u32[]{:S(2)}) copy-start(s32[64]{0:T(128)} %param.10) | copy-start | bytes 772
  0.0 32.5 %copy-start.12 = (s32[2,8]{1,0:T(2,128)S(1)}, s32[2,8]{1,0:T(2,128)}, u32[]{:S(2)}) copy-start(s32[2,8]{1,0:T(2,128)} %param.11) | copy-start | bytes 196
  3.1 27.3 %collective-permute-start = (bf16[64,8192]{1,0:T(8,128)(2,1)}, bf16[64,8192]{1,0:T(8,128)(2,1)}, u32[]{:S(2)}, u32[]{:S(2)}) collective-permute-start(bf16[64,8192]{1,0:T(8,128)(2,1)} %get-tuple-element.148), channel_id=1, source_target_pairs={{0,4},{4,8},{8,12},{12,14},{14,10},{10,6},{6,2},{2,0},{1,5},{5,9},... | collective-permute-start | bytes 3145736 | tf_op jit(solution)/shard_map/ppermute | solution.py:108
  6.1 26.4 %collective-permute-start.1 = (bf16[64,8192]{1,0:T(8,128)(2,1)}, bf16[64,8192]{1,0:T(8,128)(2,1)}, u32[]{:S(2)}, u32[]{:S(2)}) collective-permute-start(bf16[64,8192]{1,0:T(8,128)(2,1)} %get-tuple-element.147), channel_id=1, source_target_pairs={{4,0},{8,4},{12,8},{14,12},{10,14},{6,10},{2,6},{0,2},{5,1},{9,5},... | collective-permute-start | bytes 3145736 | tf_op jit(solution)/shard_map/ppermute | solution.py:108
  6.1 46.6 %collective-permute-start.4 = (bf16[64,8192]{1,0:T(8,128)(2,1)}, bf16[64,8192]{1,0:T(8,128)(2,1)S(1)}, u32[]{:S(2)}, u32[]{:S(2)}) collective-permute-start(bf16[64,8192]{1,0:T(8,128)(2,1)} %get-tuple-element.147), channel_id=1, source_target_pairs={{0,4},{4,8},{8,12},{12,14},{14,10},{10,6},{6,2},{2,0},{1,5},{5,9},... | collective-permute-start | bytes 3145736 | tf_op jit(solution)/shard_map/ppermute | solution.py:108
  8.2 46.8 %collective-permute-start.5 = (bf16[64,8192]{1,0:T(8,128)(2,1)}, bf16[64,8192]{1,0:T(8,128)(2,1)}, u32[]{:S(2)}, u32[]{:S(2)}) collective-permute-start(bf16[64,8192]{1,0:T(8,128)(2,1)} %get-tuple-element.148), channel_id=1, source_target_pairs={{4,0},{8,4},{12,8},{14,12},{10,14},{6,10},{2,6},{0,2},{5,1},{9,5},... | collective-permute-start | bytes 3145736 | tf_op jit(solution)/shard_map/ppermute | solution.py:108
  40.2 17.0 %collective-permute-start.6 = (bf16[64,8192]{1,0:T(8,128)(2,1)}, bf16[64,8192]{1,0:T(8,128)(2,1)S(1)}, u32[]{:S(2)}, u32[]{:S(2)}) collective-permute-start(bf16[64,8192]{1,0:T(8,128)(2,1)} %get-tuple-element.145), channel_id=1, source_target_pairs={{0,1},{1,0},{2,3},{3,2},{4,5},{5,4},{6,7},{7,6},{8,9},{9,8},{10,11... | collective-permute-start | bytes 3145736 | tf_op jit(solution)/shard_map/ppermute | solution.py:112
  40.2 37.3 %collective-permute-start.2 = (bf16[64,8192]{1,0:T(8,128)(2,1)}, bf16[64,8192]{1,0:T(8,128)(2,1)}, u32[]{:S(2)}, u32[]{:S(2)}) collective-permute-start(bf16[64,8192]{1,0:T(8,128)(2,1)} %collective-permute-done.refs_0_), channel_id=1, source_target_pairs={{0,4},{4,8},{8,12},{12,14},{14,10},{10,6},{6,2},{2,0},{1,5},{5,9},... | collective-permute-start | bytes 3145736 | tf_op jit(solution)/shard_map/ppermute | solution.py:108
  41.9 35.7 %collective-permute-start.3 = (bf16[64,8192]{1,0:T(8,128)(2,1)}, bf16[64,8192]{1,0:T(8,128)(2,1)}, u32[]{:S(2)}, u32[]{:S(2)}) collective-permute-start(bf16[64,8192]{1,0:T(8,128)(2,1)} %collective-permute-done.1.refs_1_), channel_id=1, source_target_pairs={{4,0},{8,4},{12,8},{14,12},{10,14},{6,10},{2,6},{0,2},{5,1},{9,5},... | collective-permute-start | bytes 3145736 | tf_op jit(solution)/shard_map/ppermute | solution.py:108
  55.0 44.8 %collective-permute-start.10 = (bf16[64,8192]{1,0:T(8,128)(2,1)}, bf16[64,8192]{1,0:T(8,128)(2,1)S(1)}, u32[]{:S(2)}, u32[]{:S(2)}) collective-permute-start(bf16[64,8192]{1,0:T(8,128)(2,1)} %collective-permute-done.5.refs_0_), channel_id=1, source_target_pairs={{4,0},{8,4},{12,8},{14,12},{10,14},{6,10},{2,6},{0,2},{5,1},{9,5},... | collective-permute-start | bytes 3145736 | tf_op jit(solution)/shard_map/ppermute | solution.py:108
  55.0 44.8 %collective-permute-start.9 = (bf16[64,8192]{1,0:T(8,128)(2,1)S(1)}, bf16[64,8192]{1,0:T(8,128)(2,1)S(1)}, u32[]{:S(2)}, u32[]{:S(2)}) collective-permute-start(bf16[64,8192]{1,0:T(8,128)(2,1)S(1)} %collective-permute-done.4.refs_1_), channel_id=1, source_target_pairs={{0,4},{4,8},{8,12},{12,14},{14,10},{10,6},{6,2},{2,0},{1,5},{5,9},... | collective-permute-start | bytes 3145736 | tf_op jit(solution)/shard_map/ppermute | solution.py:108
  57.2 5.8 %copy-start.2 = (bf16[8192,1024]{1,0:T(8,128)(2,1)S(1)}, bf16[8192,1024]{1,0:T(8,128)(2,1)}, u32[]{:S(2)}) copy-start(bf16[8192,1024]{1,0:T(8,128)(2,1)} %weight.1) | copy-start | bytes 50331652
  62.9 2.8 %copy-start.3 = (bf16[1,128,8192]{2,1,0:T(8,128)(2,1)S(1)}, bf16[1,128,8192]{2,1,0:T(8,128)(2,1)}, u32[]{:S(2)}) copy-start(bf16[1,128,8192]{2,1,0:T(8,128)(2,1)} %param.6) | copy-start | bytes 6291460
  65.7 79.1 %copy-start = (bf16[8192,1152]{1,0:T(8,128)(2,1)}, bf16[8192,1152]{1,0:T(8,128)(2,1)S(1)}, u32[]{:S(2)}) copy-start(bf16[8192,1152]{1,0:T(8,128)(2,1)S(1)} %pin.1.weights) | copy-start | bytes 56623108
  69.2 1.5 copy-start.4
  76.7 0.8 copy-start.5
  77.5 42.6 %collective-permute-start.7 = (bf16[64,8192]{1,0:T(8,128)(2,1)}, bf16[64,8192]{1,0:T(8,128)(2,1)S(1)}, u32[]{:S(2)}, u32[]{:S(2)}) collective-permute-start(bf16[64,8192]{1,0:T(8,128)(2,1)} %collective-permute-done.2.refs_0_), channel_id=1, source_target_pairs={{0,4},{4,8},{8,12},{12,14},{14,10},{10,6},{6,2},{2,0},{1,5},{5,9},... | collective-permute-start | bytes 3145736 | tf_op jit(solution)/shard_map/ppermute | solution.py:108
  79.1 43.2 %collective-permute-start.8 = (bf16[64,8192]{1,0:T(8,128)(2,1)}, bf16[64,8192]{1,0:T(8,128)(2,1)S(1)}, u32[]{:S(2)}, u32[]{:S(2)}) collective-permute-start(bf16[64,8192]{1,0:T(8,128)(2,1)} %collective-permute-done.3.refs_1_), channel_id=1, source_target_pairs={{4,0},{8,4},{12,8},{14,12},{10,14},{6,10},{2,6},{0,2},{5,1},{9,5},... | collective-permute-start | bytes 3145736 | tf_op jit(solution)/shard_map/ppermute | solution.py:108
  83.8 0.8 copy-start.6
  89.1 0.8 copy-start.7
  99.8 42.8 %collective-permute-start.13 = (bf16[64,8192]{1,0:T(8,128)(2,1)S(1)}, bf16[64,8192]{1,0:T(8,128)(2,1)S(1)}, u32[]{:S(2)}, u32[]{:S(2)}) collective-permute-start(bf16[64,8192]{1,0:T(8,128)(2,1)S(1)} %collective-permute-done.9.refs_1_), channel_id=1, source_target_pairs={{0,4},{4,8},{8,12},{12,14},{14,10},{10,6},{6,2},{2,0},{1,5},{5,9},... | collective-permute-start | bytes 3145736 | tf_op jit(solution)/shard_map/ppermute | solution.py:108
  101.4 43.4 %collective-permute-start.14 = (bf16[64,8192]{1,0:T(8,128)(2,1)S(1)}, bf16[64,8192]{1,0:T(8,128)(2,1)S(1)}, u32[]{:S(2)}, u32[]{:S(2)}) collective-permute-start(bf16[64,8192]{1,0:T(8,128)(2,1)S(1)} %collective-permute-done.10.refs_0_), channel_id=1, source_target_pairs={{4,0},{8,4},{12,8},{14,12},{10,14},{6,10},{2,6},{0,2},{5,1},{9,5},... | collective-permute-start | bytes 3145736 | tf_op jit(solution)/shard_map/ppermute | solution.py:108
  105.4 0.8 copy-start.8
  122.3 42.0 %collective-permute-start.11 = (bf16[64,8192]{1,0:T(8,128)(2,1)S(1)}, bf16[64,8192]{1,0:T(8,128)(2,1)S(1)}, u32[]{:S(2)}, u32[]{:S(2)}) collective-permute-start(bf16[64,8192]{1,0:T(8,128)(2,1)S(1)} %collective-permute-done.7.refs_0_), channel_id=1, source_target_pairs={{0,4},{4,8},{8,12},{12,14},{14,10},{10,6},{6,2},{2,0},{1,5},{5,9},... | collective-permute-start | bytes 3145736 | tf_op jit(solution)/shard_map/ppermute | solution.py:108
  123.9 41.9 %collective-permute-start.12 = (bf16[64,8192]{1,0:T(8,128)(2,1)S(1)}, bf16[64,8192]{1,0:T(8,128)(2,1)S(1)}, u32[]{:S(2)}, u32[]{:S(2)}) collective-permute-start(bf16[64,8192]{1,0:T(8,128)(2,1)S(1)} %collective-permute-done.8.refs_1_), channel_id=1, source_target_pairs={{4,0},{8,4},{12,8},{14,12},{10,14},{6,10},{2,6},{0,2},{5,1},{9,5},... | collective-permute-start | bytes 3145736 | tf_op jit(solution)/shard_map/ppermute | solution.py:108
  127.8 0.8 copy-start.9
  148.3 0.8 copy-start.10
  165.8 27.9 %all-to-all-start = ((bf16[16,64,512]{2,1,0:T(8,128)(2,1)}), bf16[16,64,512]{2,1,0:T(8,128)(2,1)S(1)}, u32[]{:S(2)}, u32[]{:S(2)}) async-start(bf16[16,64,512]{2,1,0:T(8,128)(2,1)} %bitcast.30), calls=%async_computation | async-start | bytes 2097152 | tf_op jit(solution)/shard_map/all_to_all | solution.py:349
  170.7 6.4 %copy-start.1 = (bf16[8192,1152]{1,0:T(8,128)(2,1)S(1)}, bf16[8192,1152]{1,0:T(8,128)(2,1)}, u32[]{:S(2)}) copy-start(bf16[8192,1152]{1,0:T(8,128)(2,1)} %copy-done) | copy-start | bytes 56623108
  180.5 0.8 copy-start.11
  181.3 4.6 %collective-permute-start.15 = (bf16[128,128]{1,0:T(8,128)(2,1)S(1)}, bf16[128,128]{1,0:T(8,128)(2,1)S(1)}, u32[]{:S(2)}, u32[]{:S(2)}) collective-permute-start(bf16[128,128]{1,0:T(8,128)(2,1)S(1)} %get-tuple-element.140), channel_id=1, source_target_pairs={{0,2},{2,0},{4,6},{6,4},{8,10},{10,8},{12,14},{14,12},{1,3},{3,1},... | collective-permute-start | bytes 98312 | tf_op jit(solution)/shard_map/ppermute | solution.py:108
  194.4 14.5 %collective-permute-start.19 = (bf16[8,64,512]{2,1,0:T(8,128)(2,1)S(1)}, bf16[8,64,512]{2,1,0:T(8,128)(2,1)S(1)}, u32[]{:S(2)}, u32[]{:S(2)}) collective-permute-start(bf16[8,64,512]{2,1,0:T(8,128)(2,1)S(1)} %take.1.refs_12_), channel_id=1, source_target_pairs={{0,16},{16,0},{1,17},{17,1},{2,18},{18,2},{3,19},{19,3},{4,20},{20... | collective-permute-start | bytes 1572872 | tf_op jit(solution)/shard_map/ppermute | solution.py:112
  196.0 6.7 %collective-permute-start.16 = (bf16[2,128,128]{2,1,0:T(8,128)(2,1)S(1)}, bf16[2,128,128]{2,1,0:T(8,128)(2,1)S(1)}, u32[]{:S(2)}, u32[]{:S(2)}) collective-permute-start(bf16[2,128,128]{2,1,0:T(8,128)(2,1)S(1)} %pad_maximum_fusion.refs_8_), channel_id=1, source_target_pairs={{0,4},{2,6},{4,0},{6,2},{8,12},{10,14},{12,8},{14,10},{1,5},{3,7},... | collective-permute-start | bytes 196616 | tf_op jit(solution)/shard_map/ppermute | solution.py:108
  199.2 8.3 %collective-permute-start.17 = (bf16[2,128,128]{2,1,0:T(8,128)(2,1)S(1)}, bf16[2,128,128]{2,1,0:T(8,128)(2,1)S(1)}, u32[]{:S(2)}, u32[]{:S(2)}) collective-permute-start(bf16[2,128,128]{2,1,0:T(8,128)(2,1)S(1)} %pad_maximum_fusion.refs_8_), channel_id=1, source_target_pairs={{0,8},{2,10},{4,12},{6,14},{8,0},{10,2},{12,4},{14,6},{1,9},{3,11}... | collective-permute-start | bytes 196616 | tf_op jit(solution)/shard_map/ppermute | solution.py:108
  201.2 6.3 %collective-permute-start.18 = (bf16[2,128,128]{2,1,0:T(8,128)(2,1)S(1)}, bf16[2,128,128]{2,1,0:T(8,128)(2,1)S(1)}, u32[]{:S(2)}, u32[]{:S(2)}) collective-permute-start(bf16[2,128,128]{2,1,0:T(8,128)(2,1)S(1)} %pad_maximum_fusion.refs_8_), channel_id=1, source_target_pairs={{0,12},{2,14},{4,8},{6,10},{8,4},{10,6},{12,0},{14,2},{1,13},{3,15... | collective-permute-start | bytes 196616 | tf_op jit(solution)/shard_map/ppermute | solution.py:108

commit v12 on v11

--- a/solution.py
+++ b/solution.py
@@ -158,12 +158,7 @@
         total = part if total is None else total + part
     base[...] = total[:, :columns]
     lane = lax.broadcasted_iota(jnp.int32, shrunk.shape, 1)
-    row = lax.broadcasted_iota(jnp.int32, shrunk.shape, 0)
-    use = jnp.where(
-        row < HALF,
-        jnp.where(lane < 64, table[0, 2 * group], table[1, 2 * group]),
-        jnp.where(lane < 64, table[0, 2 * group + 1], table[1, 2 * group + 1]),
-    )
+    use = jnp.where(lane < 64, table[0, group], table[1, group])
     small = total[:, columns:].astype(jnp.bfloat16).astype(jnp.float32)
     old = shrunk[...].astype(jnp.float32)
     shrunk_out[...] = jnp.where(use > 0, small, old).astype(jnp.bfloat16)
@@ -240,18 +235,16 @@
     for i, pair in enumerate(gathered):
         shrunk[pl.ds(2 * i, 2)] = pair[...]
     copies = []
-    for i in range(16):
-        block, half = table[0, i], i % 2
-        if half == 0:
-            fetches[i // 2].wait()
-        own = pl.ds(half * HALF, HALF)
-        both = shrunk[table[1, i], own, :].astype(jnp.float32)
+    for i in range(8):
+        block = table[0, i]
+        both = shrunk[table[1, i]].astype(jnp.float32)
         value = jnp.where(table[2, i] > 0, both[:, 64:], both[:, :64]).astype(jnp.bfloat16)
+        fetches[i].wait()
         for up, side in ((up_mine, group), (up_other, 1 - group)):
             cut = pl.ds(pl.multiple_of(side * part, part), part)
             grown = jnp.dot(value, up[block], preferred_element_type=jnp.float32)
-            rows[i, :, cut] = (base[i // 2, own, cut] + 0.5 * grown).astype(rows.dtype)
-        to = pl.ds(pl.multiple_of((2 * block + half) * HALF, HALF), HALF)
+            rows[i, :, cut] = (base[i, :, cut] + 0.5 * grown).astype(rows.dtype)
+        to = pl.ds(pl.multiple_of(block * BLOCK, BLOCK), BLOCK)
         copies.append(pltpu.make_async_copy(rows.at[i], out.at[to], sems.at[i]))
         copies[-1].start()
     for copy in copies:
@@ -270,9 +263,9 @@
         scratch_shapes=[
             pltpu.VMEM((8, BLOCK, columns), jnp.float32),
             pltpu.VMEM((8,) + gathered[0].shape[1:], jnp.bfloat16),
-            pltpu.VMEM((16, HALF, columns), jnp.bfloat16),
+            pltpu.VMEM((8, BLOCK, columns), jnp.bfloat16),
             pltpu.SemaphoreType.DMA((8,)),
-            pltpu.SemaphoreType.DMA((16,)),
+            pltpu.SemaphoreType.DMA((8,)),
         ],
         name="finish",
         **settings(),
@@ -295,16 +288,8 @@
     myself = me * 2 + store
     held, rank, width = adapter_down_maps.shape
     rows = tokens[0]
-    halves = [rows[:HALF], rows[HALF:]]
-
-    ahead, back = list(halves), list(halves[::-1])
-    flight = [(send(ahead[k], AHEAD), send(back[k], BACK)) for k in range(2)]
-    got, ahead, back, adapter_home_slot, adapter_per_block = lax.optimization_barrier(
-        (flight[0], ahead, back, adapter_home_slot, adapter_per_block)
-    )
-    ahead.append(got[0])
-    back.append(got[1])
-    flight.append((send(ahead[2], AHEAD), send(back[2], BACK)))
+
+    flight = (send(rows, AHEAD), send(rows, BACK))
 
     store_slots = find_slots(adapter_home_slot, adapter_per_block)
     owner = store_slots // held
@@ -316,16 +301,10 @@
 
     down_own = lax.dynamic_index_in_dim(adapter_down_maps, pick_own, 0, keepdims=False)
     down_lent = lax.dynamic_index_in_dim(adapter_down_maps, pick_lent, 0, keepdims=False)
-    down_swapped = swap(down_lent, "store")
-    weights = pin_call(query_weight, down_own, down_swapped)
     up_sent = pack_call(jnp.concatenate([picked, group[None]]).astype(jnp.int32), adapter_up_maps)
 
     position = jnp.where(y == 0, z, 7 - z)
-    places = []
-    for k in range(8):
-        step = (k + 1) // 2
-        places += [position - step, position + step] if k % 2 else [position + step, position - step]
-    places = jnp.stack(places) % 8
+    places = jnp.stack([position + d for d in (0, -1, 1, -2, 2, -3, 3, 4)]) % 8
     blocks = jnp.where(places < 4, 2 * places, 15 - 2 * places).astype(jnp.int32)
     hit = blocks[:, None] == jnp.arange(8, dtype=jnp.int32)[None, :]
     owners = jnp.sum(jnp.where(hit, owner_row[None, :], 0), axis=1)
@@ -333,23 +312,28 @@
 
     bases = []
     shrunk = jnp.zeros((BLOCK, 2 * rank), jnp.bfloat16)
-    groups = [[rows], [ahead[2], back[2]]]
-    for k in range(1, 7):
-        (got_ahead, got_back), ahead, back, bases, shrunk, up_sent = lax.optimization_barrier(
-            (flight[k], ahead, back, bases, shrunk, up_sent)
+    groups = [[rows]]
+    extra = (down_own, down_lent, up_sent)
+    for k in range(4):
+        (ahead, back), bases, shrunk, extra = lax.optimization_barrier(
+            (flight, bases, shrunk, extra)
         )
-        ahead.append(got_ahead)
-        back.append(got_back)
-        if k < 5:
-            flight.append((send(ahead[k + 2], AHEAD), send(back[k + 2], BACK)))
-        groups.append([got_ahead, got_back] if k % 2 == 0 else [got_back, got_ahead])
-        for g in range(len(bases), min(len(bases) + 2, k + 2, 7)):
+        if k == 3:
+            break
+        cut = (slice(None), slice(None)) if k < 2 else (slice(0, HALF), slice(HALF, BLOCK))
+        flight = (send(ahead[cut[0]], AHEAD), send(back[cut[1]], BACK))
+        groups += [[ahead], [back]]
+        if k == 0:
+            down_swapped = swap(extra[1], "store")
+        if k == 1:
+            weights = pin_call(query_weight, extra[0], down_swapped)
+        for g in {0: (), 1: range(3), 2: range(3, 7)}[k]:
             base, shrunk = rows_call(g, table, weights, groups[g], shrunk)
             bases.append(base)
     up_got = lax.all_to_all(
-        up_sent.reshape(16, rank, -1), ("tensor", "store"), split_axis=0, concat_axis=0, tiled=True
-    )
-    base, shrunk = rows_call(7, table, weights, groups[7], shrunk)
+        extra[2].reshape(16, rank, -1), ("tensor", "store"), split_axis=0, concat_axis=0, tiled=True
+    )
+    base, shrunk = rows_call(7, table, weights, [ahead, back], shrunk)
     bases.append(base)
 
     across = send(shrunk, ACROSS)
@@ -360,7 +344,7 @@
     up_other = swap(up_mine, "groups")
     home, core = owners // 2, owners % 2
     where = 2 * ((home // 2) ^ z) + ((home % 2) ^ y)
-    table = jnp.stack([blocks, where, core != store, jnp.broadcast_to(group, (16,))])
+    table = jnp.stack([blocks, where, core != store, jnp.broadcast_to(group, (8,))])
     return finish_call(table.astype(jnp.int32), bases, everyone, up_mine, up_other)[None]
 
 

time: 215 us -> 218 us (1.014)
  starting transfers between devices: 30.2 us -> 23.1 us
  waiting for transfers between devices: 109 us -> 116 us
    ppermute x18 -> x12, starting transfers between devices: 23.7 us -> 17.5 us  [send(): return lax.ppermute(value, 'tensor', pairs)]
    ppermute x18 -> x12, waiting for transfers between devices: 100 us -> 105 us  [send(): return lax.ppermute(value, 'tensor', pairs)]
    ppermute x2, waiting for transfers between devices: 1.37 us -> 4.07 us  [swap(): return lax.ppermute(value, axis, [(0, 1), (1, 0)])]
    unnamed x28 -> x32, local copies, waits for them, and re-layouts: 19.2 us -> 20.8 us
  transfers between devices with their start and end apart: 21 -> 15, of which waited for: 15 -> 12; matrix products, arithmetic and copies ran while one was open for 2% -> 2% of each run, Pallas kernels for 18% -> 19%
where the time goes in v12:
time: 218 us; the launch traced here: 217 us
  waiting for transfers between devices  116 us (53%)
  Pallas kernels  45.7 us (21%)
  local copies, waits for them, and re-layouts  25.8 us (12%)
  starting transfers between devices  23.1 us (11%)
  between operations  4.06 us (2%)
    ppermute x12, waiting for transfers between devices, send(): return lax.ppermute(value, 'tensor', pairs)  105 us
    pallas_call x8, Pallas kernels, rows_call(): pl.pallas_call(functools.partial(rows_kernel, group), in_specs=[pl.BlockS...  33.5 us
    unnamed x32, local copies, waits for them, and re-layouts  20.8 us
    ppermute x12, starting transfers between devices, send(): return lax.ppermute(value, 'tensor', pairs)  17.5 us
    all_to_all x1, waiting for transfers between devices, chain_body(): lax.all_to_all(extra[2].reshape(16, rank, -1), ('tensor', 'store'), split...  7.77 us
    pallas_call x1, Pallas kernels, finish_call(): pl.pallas_call(finish_kernel, in_specs=[pl.BlockSpec(memory_space=pltpu.S...  4.59 us
  transfers between devices with their start and end apart: 15, of which 12 were waited for; matrix products, arithmetic and copies ran while one was open for 2% of the time, Pallas kernels for 19%

profile of v12, /device:TPU:0, one launch (start us, length us, event | category | flops | bytes accessed | tf_op | source)
XLA Modules:
  0.0 216.6 jit_solution(3566441987395141032)
XLA Ops:
  0.0 3.0 %collective-permute-start = (bf16[128,8192]{1,0:T(8,128)(2,1)}, bf16[128,8192]{1,0:T(8,128)(2,1)}, u32[]{:S(2)}, u32[]{:S(2)}) collective-permute-start(bf16[128,8192]{1,0:T(8,128)(2,1)} %bitcast.50), channel_id=1, source_target_pairs={{0,4},{4,8},{8,12},{12,14},{14,10},{10,6},{6,2},{2,0},{1,5},{5,9},... | collective-permute-start | bytes 6291464 | tf_op jit(solution)/shard_map/ppermute | solution.py:108
  3.0 0.9 select_reduce_fusion
  4.1 2.8 %pack.1 = bf16[8,2,64,512]{3,2,1,0:T(8,128)(2,1)} custom-call(s32[3]{0:T(128)S(1)} %pad_add_fusion.table, bf16[4,64,8192]{2,1,0:T(8,128)(2,1)} %up.1), custom_call_target="tpu_custom_call" | custom-call | flops 1 | bytes 1 | tf_op jit(solution)/shard_map/pack/pallas_call | solution.py:193
  11.2 2.8 %dynamic-slice_bitcast_fusion = (bf16[64,8192]{1,0:T(8,128)(2,1)}, bf16[64,8192]{1,0:T(8,128)(2,1)S(1)}) fusion(bf16[4,64,8192]{2,1,0:T(8,128)(2,1)} %param.8, s32[]{:T(128)S(6)} %select_n.151, s32[]{:T(128)S(6)} %select_n.149), kind=kLoop, calls=%fused_computation | loop fusion | bytes 4194312 | tf_op jit(solution)/shard_map/jit(dynamic_index_in_dim)/squeeze | solution.py:303
  13.9 35.0 %collective-permute-done.refs_0_ = bf16[128,8192]{1,0:T(8,128)(2,1)} collective-permute-done((bf16[128,8192]{1,0:T(8,128)(2,1)}, bf16[128,8192]{1,0:T(8,128)(2,1)}, u32[]{:S(2)}, u32[]{:S(2)}) %collective-permute-start) | collective-permute-done | bytes 2097184 | tf_op jit(solution)/shard_map/ppermute | solution.py:108
  48.9 1.4 collective-permute-done.1.refs_0_
  50.3 1.6 collective-permute-start.2
  52.4 1.3 copy-done.4
  53.7 43.2 %collective-permute-done.2.refs_0_ = bf16[128,8192]{1,0:T(8,128)(2,1)} collective-permute-done((bf16[128,8192]{1,0:T(8,128)(2,1)}, bf16[128,8192]{1,0:T(8,128)(2,1)}, u32[]{:S(2)}, u32[]{:S(2)}) %collective-permute-start.2) | collective-permute-done | bytes 2097184 | tf_op jit(solution)/shard_map/ppermute | solution.py:108
  96.9 1.1 collective-permute-done.3.refs_0_
  98.0 1.6 collective-permute-start.4
  100.4 2.7 %collective-permute-done.6.swapped = bf16[64,8192]{1,0:T(8,128)(2,1)} collective-permute-done((bf16[64,8192]{1,0:T(8,128)(2,1)}, bf16[64,8192]{1,0:T(8,128)(2,1)}, u32[]{:S(2)}, u32[]{:S(2)}) %collective-permute-start.6) | collective-permute-done | bytes 1048608 | tf_op jit(solution)/shard_map/ppermute | solution.py:112
  103.0 5.8 %copy-done.2 = bf16[8192,1024]{1,0:T(8,128)(2,1)S(1)} copy-done((bf16[8192,1024]{1,0:T(8,128)(2,1)S(1)}, bf16[8192,1024]{1,0:T(8,128)(2,1)}, u32[]{:S(2)}) %copy-start.2) | copy-done | bytes 16777240
  108.8 4.1 %pin.1.weights = bf16[8192,1152]{1,0:T(8,128)(2,1)S(1)} custom-call(bf16[8192,1024]{1,0:T(8,128)(2,1)S(1)} %copy-done.2, bf16[64,8192]{1,0:T(8,128)(2,1)S(1)} %get-tuple-element.59.own, bf16[64,8192]{1,0:T(8,128)(2,1)} %collective-permute-done.6.swapped), custom_call_target="tpu_custom_call" | custom-call | flops 1 | bytes 1 | tf_op jit(solution)/shard_map/pin/pallas_call | solution.py:138
  113.0 3.5 %rows.8 = (f32[128,1024]{1,0:T(8,128)S(1)}, bf16[128,128]{1,0:T(8,128)(2,1)S(1)}) custom-call(s32[2,8]{1,0:T(2,128)S(1)} %add_convert_fusion.table, bf16[8192,1152]{1,0:T(8,128)(2,1)S(1)} %pin.1.weights, bf16[128,8192]{1,0:T(8,128)(2,1)S(1)} %bitcast.52, bf16[128,128]{1,0:T(8,128)(2,1)S(1)} %broadcast_in_dim.48.refs_1_), custom_call_target="tpu_custom_call" | custom-call | flops 1 | bytes 1 | tf_op jit(solution)/shard_map/rows/pallas_call | solution.py:170
  116.5 1.6 copy-done.8
  118.1 6.0 %rows.9 = (f32[128,1024]{1,0:T(8,128)S(1)}, bf16[128,128]{1,0:T(8,128)(2,1)S(1)}) custom-call(s32[2,8]{1,0:T(2,128)S(1)} %add_convert_fusion.table, bf16[8192,1152]{1,0:T(8,128)(2,1)S(1)} %pin.1.weights, bf16[128,8192]{1,0:T(8,128)(2,1)} %collective-permute-done.refs_0_, bf16[128,128]{1,0:T(8,128)(2,1)S(1)} %get-tuple-element.62.refs_1_), custom_call_target="tpu_custom_call" | custom-call | flops 1 | bytes 1 | tf_op jit(solution)/shard_map/rows/pallas_call | solution.py:170
  124.1 0.8 copy-done.9
  124.9 3.5 %rows.10 = (f32[128,1024]{1,0:T(8,128)S(1)}, bf16[128,128]{1,0:T(8,128)(2,1)S(1)}) custom-call(s32[2,8]{1,0:T(2,128)S(1)} %add_convert_fusion.table, bf16[8192,1152]{1,0:T(8,128)(2,1)S(1)} %pin.1.weights, bf16[128,8192]{1,0:T(8,128)(2,1)S(1)} %copy-done.5, bf16[128,128]{1,0:T(8,128)(2,1)S(1)} %get-tuple-element.64.refs_1_), custom_call_target="tpu_custom_call" | custom-call | flops 1 | bytes 1 | tf_op jit(solution)/shard_map/rows/pallas_call | solution.py:170
  128.4 15.0 %collective-permute-done.4.refs_0_ = bf16[128,8192]{1,0:T(8,128)(2,1)} collective-permute-done((bf16[128,8192]{1,0:T(8,128)(2,1)}, bf16[128,8192]{1,0:T(8,128)(2,1)}, u32[]{:S(2)}, u32[]{:S(2)}) %collective-permute-start.4) | collective-permute-done | bytes 2097184 | tf_op jit(solution)/shard_map/ppermute | solution.py:108
  143.4 1.2 collective-permute-done.5.refs_0_
  144.6 1.3 slice.6
  145.9 1.6 collective-permute-start.7
  147.6 0.7 collective-permute-start.8
  148.3 4.6 %rows.11 = (f32[128,1024]{1,0:T(8,128)S(1)}, bf16[128,128]{1,0:T(8,128)(2,1)S(1)}) custom-call(s32[2,8]{1,0:T(2,128)S(1)} %add_convert_fusion.table, bf16[8192,1152]{1,0:T(8,128)(2,1)S(1)} %pin.1.weights, bf16[128,8192]{1,0:T(8,128)(2,1)} %collective-permute-done.2.refs_0_, bf16[128,128]{1,0:T(8,128)(2,1)S(1)} %get-tuple-element.73.refs_1_), custom_call_target="tpu_custom_call" | custom-call | flops 1 | bytes 1 | tf_op jit(solution)/shard_map/rows/pallas_call | solution.py:170
  152.9 0.8 copy-done.11
  153.7 4.5 %rows.12 = (f32[128,1024]{1,0:T(8,128)S(1)}, bf16[128,128]{1,0:T(8,128)(2,1)S(1)}) custom-call(s32[2,8]{1,0:T(2,128)S(1)} %add_convert_fusion.table, bf16[8192,1152]{1,0:T(8,128)(2,1)S(1)} %pin.1.weights, bf16[128,8192]{1,0:T(8,128)(2,1)} %collective-permute-done.3.refs_0_, bf16[128,128]{1,0:T(8,128)(2,1)S(1)} %get-tuple-element.75.refs_1_), custom_call_target="tpu_custom_call" | custom-call | flops 1 | bytes 1 | tf_op jit(solution)/shard_map/rows/pallas_call | solution.py:170
  158.2 0.8 copy-done.12
  159.0 4.6 %rows.13 = (f32[128,1024]{1,0:T(8,128)S(1)}, bf16[128,128]{1,0:T(8,128)(2,1)S(1)}) custom-call(s32[2,8]{1,0:T(2,128)S(1)} %add_convert_fusion.table, bf16[8192,1152]{1,0:T(8,128)(2,1)S(1)} %pin.1.weights, bf16[128,8192]{1,0:T(8,128)(2,1)} %collective-permute-done.4.refs_0_, bf16[128,128]{1,0:T(8,128)(2,1)S(1)} %get-tuple-element.77.refs_1_), custom_call_target="tpu_custom_call" | custom-call | flops 1 | bytes 1 | tf_op jit(solution)/shard_map/rows/pallas_call | solution.py:170
  163.6 0.8 copy-done.13
  164.4 3.5 %rows.14 = (f32[128,1024]{1,0:T(8,128)S(1)}, bf16[128,128]{1,0:T(8,128)(2,1)S(1)}) custom-call(s32[2,8]{1,0:T(2,128)S(1)} %add_convert_fusion.table, bf16[8192,1152]{1,0:T(8,128)(2,1)S(1)} %pin.1.weights, bf16[128,8192]{1,0:T(8,128)(2,1)S(1)} %collective-permute-done.5.refs_0_, bf16[128,128]{1,0:T(8,128)(2,1)S(1)} %get-tuple-element.79.refs_1_), custom_call_target="tpu_custom_call" | custom-call | flops 1 | bytes 1 | tf_op jit(solution)/shard_map/rows/pallas_call | solution.py:170
  167.9 0.8 copy-done.14
  169.0 1.0 copy-done.6
  170.0 4.0 %all-to-all-start = ((bf16[16,64,512]{2,1,0:T(8,128)(2,1)}), bf16[16,64,512]{2,1,0:T(8,128)(2,1)S(1)}, u32[]{:S(2)}, u32[]{:S(2)}) async-start(bf16[16,64,512]{2,1,0:T(8,128)(2,1)} %bitcast.26), calls=%async_computation | async-start | bytes 2097152 | tf_op jit(solution)/shard_map/all_to_all | solution.py:333
  174.0 6.4 %copy-done.1 = bf16[8192,1152]{1,0:T(8,128)(2,1)S(1)} copy-done((bf16[8192,1152]{1,0:T(8,128)(2,1)S(1)}, bf16[8192,1152]{1,0:T(8,128)(2,1)}, u32[]{:S(2)}) %copy-start.1) | copy-done | bytes 18874392
  180.4 3.4 %rows.15 = (f32[128,1024]{1,0:T(8,128)S(1)}, bf16[128,128]{1,0:T(8,128)(2,1)S(1)}) custom-call(s32[2,8]{1,0:T(2,128)S(1)} %add_convert_fusion.table, bf16[8192,1152]{1,0:T(8,128)(2,1)S(1)} %copy-done.1, bf16[64,8192]{1,0:T(8,128)(2,1)S(1)} %collective-permute-done.7.refs_0_, bf16[64,8192]{1,0:T(8,128)(2,1)S(1)} %copy-done.7, ...), custom_call_target="tpu_custom_call" | custom-call | flops 1 | bytes 1 | tf_op jit(solution)/shard_map/rows/pallas_call | solution.py:170
  183.8 0.8 copy-done.15
  184.6 1.6 collective-permute-start.9
  186.4 2.5 %collective-permute-done.9 = bf16[128,128]{1,0:T(8,128)(2,1)S(1)} collective-permute-done((bf16[128,128]{1,0:T(8,128)(2,1)S(1)}, bf16[128,128]{1,0:T(8,128)(2,1)S(1)}, u32[]{:S(2)}, u32[]{:S(2)}) %collective-permute-start.9) | collective-permute-done | bytes 32800 | tf_op jit(solution)/shard_map/ppermute | solution.py:108
  188.9 7.8 %all-to-all-done.got = bf16[16,64,512]{2,1,0:T(8,128)(2,1)S(1)} async-done(((bf16[16,64,512]{2,1,0:T(8,128)(2,1)}), bf16[16,64,512]{2,1,0:T(8,128)(2,1)S(1)}, u32[]{:S(2)}, u32[]{:S(2)}) %all-to-all-start) | async-done | bytes 1048608 | tf_op jit(solution)/shard_map/all_to_all | solution.py:333
  196.7 0.7 take.1.refs_12_
  197.4 1.6 collective-permute-start.13
  199.0 3.3 %collective-permute-start.10 = (bf16[2,128,128]{2,1,0:T(8,128)(2,1)S(1)}, bf16[2,128,128]{2,1,0:T(8,128)(2,1)S(1)}, u32[]{:S(2)}, u32[]{:S(2)}) collective-permute-start(bf16[2,128,128]{2,1,0:T(8,128)(2,1)S(1)} %pad_maximum_fusion.refs_8_), channel_id=1, source_target_pairs={{0,4},{2,6},{4,0},{6,2},{8,12},{10,14},{12,8},{14,10},{1,5},{3,7},... | collective-permute-start | bytes 196616 | tf_op jit(solution)/shard_map/ppermute | solution.py:108
  202.2 1.9 collective-permute-start.11
  204.2 1.4 collective-permute-start.12
  205.6 4.9 %collective-permute-done.11.refs_10_ = bf16[2,128,128]{2,1,0:T(8,128)(2,1)S(1)} collective-permute-done((bf16[2,128,128]{2,1,0:T(8,128)(2,1)S(1)}, bf16[2,128,128]{2,1,0:T(8,128)(2,1)S(1)}, u32[]{:S(2)}, u32[]{:S(2)}) %collective-permute-start.11) | collective-permute-done | bytes 65568 | tf_op jit(solution)/shard_map/ppermute | solution.py:108
  210.5 1.4 collective-permute-done.13.refs_13_
  211.9 4.6 %finish.1 = bf16[1024,1024]{1,0:T(8,128)(2,1)} custom-call(s32[4,8]{1,0:T(4,128)S(1)} %add_add_fusion.table, f32[128,1024]{1,0:T(8,128)} %copy-done.8, f32[128,1024]{1,0:T(8,128)} %copy-done.9, f32[128,1024]{1,0:T(8,128)} %copy-done.10, f32[128,1024]{1,0:T(8,128)} %copy-done.11, f32[128,1024]{1,0:T(8,128)} %copy-done.12, f32[128,1024]{1,0:T(8,128)} %copy-done.13, ...), custom_call_target="tpu_custom_call" | custom-call | flops 1 | bytes 1 | tf_op jit(solution)/shard_map/finish/pallas_call | solution.py:256
  (45 shorter events, 2.7 us)
Async XLA Ops:
  0.0 48.9 %collective-permute-start = (bf16[128,8192]{1,0:T(8,128)(2,1)}, bf16[128,8192]{1,0:T(8,128)(2,1)}, u32[]{:S(2)}, u32[]{:S(2)}) collective-permute-start(bf16[128,8192]{1,0:T(8,128)(2,1)} %bitcast.50), channel_id=1, source_target_pairs={{0,4},{4,8},{8,12},{12,14},{14,10},{10,6},{6,2},{2,0},{1,5},{5,9},... | collective-permute-start | bytes 6291464 | tf_op jit(solution)/shard_map/ppermute | solution.py:108
  3.0 47.3 %collective-permute-start.1 = (bf16[128,8192]{1,0:T(8,128)(2,1)}, bf16[128,8192]{1,0:T(8,128)(2,1)S(1)}, u32[]{:S(2)}, u32[]{:S(2)}) collective-permute-start(bf16[128,8192]{1,0:T(8,128)(2,1)} %bitcast.51), channel_id=1, source_target_pairs={{4,0},{8,4},{12,8},{14,12},{10,14},{6,10},{2,6},{0,2},{5,1},{9,5},... | collective-permute-start | bytes 6291464 | tf_op jit(solution)/shard_map/ppermute | solution.py:108
  50.3 46.6 %collective-permute-start.2 = (bf16[128,8192]{1,0:T(8,128)(2,1)}, bf16[128,8192]{1,0:T(8,128)(2,1)}, u32[]{:S(2)}, u32[]{:S(2)}) collective-permute-start(bf16[128,8192]{1,0:T(8,128)(2,1)} %collective-permute-done.refs_0_), channel_id=1, source_target_pairs={{0,4},{4,8},{8,12},{12,14},{14,10},{10,6},{6,2},{2,0},{1,5},{5,9},... | collective-permute-start | bytes 6291464 | tf_op jit(solution)/shard_map/ppermute | solution.py:108
  51.9 46.1 %collective-permute-start.3 = (bf16[128,8192]{1,0:T(8,128)(2,1)S(1)}, bf16[128,8192]{1,0:T(8,128)(2,1)}, u32[]{:S(2)}, u32[]{:S(2)}) collective-permute-start(bf16[128,8192]{1,0:T(8,128)(2,1)S(1)} %collective-permute-done.1.refs_0_), channel_id=1, source_target_pairs={{4,0},{8,4},{12,8},{14,12},{10,14},{6,10},{2,6},{0,2},{5,1},{9,5},... | collective-permute-start | bytes 6291464 | tf_op jit(solution)/shard_map/ppermute | solution.py:108
  52.4 1.3 copy-start.4
  98.0 45.4 %collective-permute-start.4 = (bf16[128,8192]{1,0:T(8,128)(2,1)}, bf16[128,8192]{1,0:T(8,128)(2,1)}, u32[]{:S(2)}, u32[]{:S(2)}) collective-permute-start(bf16[128,8192]{1,0:T(8,128)(2,1)} %collective-permute-done.2.refs_0_), channel_id=1, source_target_pairs={{0,4},{4,8},{8,12},{12,14},{14,10},{10,6},{6,2},{2,0},{1,5},{5,9},... | collective-permute-start | bytes 6291464 | tf_op jit(solution)/shard_map/ppermute | solution.py:108
  99.6 45.0 %collective-permute-start.5 = (bf16[128,8192]{1,0:T(8,128)(2,1)}, bf16[128,8192]{1,0:T(8,128)(2,1)S(1)}, u32[]{:S(2)}, u32[]{:S(2)}) collective-permute-start(bf16[128,8192]{1,0:T(8,128)(2,1)} %collective-permute-done.3.refs_0_), channel_id=1, source_target_pairs={{4,0},{8,4},{12,8},{14,12},{10,14},{6,10},{2,6},{0,2},{5,1},{9,5},... | collective-permute-start | bytes 6291464 | tf_op jit(solution)/shard_map/ppermute | solution.py:108
  100.0 3.0 %collective-permute-start.6 = (bf16[64,8192]{1,0:T(8,128)(2,1)}, bf16[64,8192]{1,0:T(8,128)(2,1)}, u32[]{:S(2)}, u32[]{:S(2)}) collective-permute-start(bf16[64,8192]{1,0:T(8,128)(2,1)} %get-tuple-element.55), channel_id=1, source_target_pairs={{0,1},{1,0},{2,3},{3,2},{4,5},{5,4},{6,7},{7,6},{8,9},{9,8},{10,11... | collective-permute-start | bytes 3145736 | tf_op jit(solution)/shard_map/ppermute | solution.py:112
  103.0 5.8 %copy-start.2 = (bf16[8192,1024]{1,0:T(8,128)(2,1)S(1)}, bf16[8192,1024]{1,0:T(8,128)(2,1)}, u32[]{:S(2)}) copy-start(bf16[8192,1024]{1,0:T(8,128)(2,1)} %weight.1) | copy-start | bytes 50331652
  108.8 4.2 %copy-start.3 = (bf16[1,128,8192]{2,1,0:T(8,128)(2,1)S(1)}, bf16[1,128,8192]{2,1,0:T(8,128)(2,1)}, u32[]{:S(2)}) copy-start(bf16[1,128,8192]{2,1,0:T(8,128)(2,1)} %param.6) | copy-start | bytes 6291460
  113.0 51.4 %copy-start = (bf16[8192,1152]{1,0:T(8,128)(2,1)}, bf16[8192,1152]{1,0:T(8,128)(2,1)S(1)}, u32[]{:S(2)}) copy-start(bf16[8192,1152]{1,0:T(8,128)(2,1)S(1)} %pin.1.weights) | copy-start | bytes 56623108
  116.5 1.6 copy-start.8
  118.1 6.8 %copy-start.5 = (bf16[128,8192]{1,0:T(8,128)(2,1)S(1)}, bf16[128,8192]{1,0:T(8,128)(2,1)}, u32[]{:S(2)}) copy-start(bf16[128,8192]{1,0:T(8,128)(2,1)} %copy-done.4) | copy-start | bytes 6291460
  124.1 0.8 copy-start.9
  128.4 19.2 %copy-start.10 = (f32[128,1024]{1,0:T(8,128)}, f32[128,1024]{1,0:T(8,128)S(1)}, u32[]{:S(2)}) copy-start(f32[128,1024]{1,0:T(8,128)S(1)} %get-tuple-element.85.refs_2_) | copy-start | bytes 1572868
  145.9 22.8 %collective-permute-start.7 = (bf16[64,8192]{1,0:T(8,128)(2,1)S(1)}, bf16[64,8192]{1,0:T(8,128)(2,1)S(1)}, u32[]{:S(2)}, u32[]{:S(2)}) collective-permute-start(bf16[64,8192]{1,0:T(8,128)(2,1)S(1)} %slice.6), channel_id=1, source_target_pairs={{0,4},{4,8},{8,12},{12,14},{14,10},{10,6},{6,2},{2,0},{1,5},{5,9},... | collective-permute-start | bytes 3145736 | tf_op jit(solution)/shard_map/ppermute | solution.py:108
  147.6 21.5 %collective-permute-start.8 = (bf16[64,8192]{1,0:T(8,128)(2,1)S(1)}, bf16[64,8192]{1,0:T(8,128)(2,1)S(1)}, u32[]{:S(2)}, u32[]{:S(2)}) collective-permute-start(bf16[64,8192]{1,0:T(8,128)(2,1)S(1)} %slice.7), channel_id=1, source_target_pairs={{4,0},{8,4},{12,8},{14,12},{10,14},{6,10},{2,6},{0,2},{5,1},{9,5},... | collective-permute-start | bytes 3145736 | tf_op jit(solution)/shard_map/ppermute | solution.py:108
  152.9 0.8 copy-start.11
  158.2 0.8 copy-start.12
  163.6 0.8 copy-start.13
  167.9 0.8 copy-start.14
  169.0 1.0 copy-start.6
  170.0 4.0 %copy-start.7 = (bf16[64,8192]{1,0:T(8,128)(2,1)S(1)}, bf16[64,8192]{1,0:T(8,128)(2,1)}, u32[]{:S(2)}) copy-start(bf16[64,8192]{1,0:T(8,128)(2,1)} %copy-done.6) | copy-start | bytes 3145732
  170.0 26.7 %all-to-all-start = ((bf16[16,64,512]{2,1,0:T(8,128)(2,1)}), bf16[16,64,512]{2,1,0:T(8,128)(2,1)S(1)}, u32[]{:S(2)}, u32[]{:S(2)}) async-start(bf16[16,64,512]{2,1,0:T(8,128)(2,1)} %bitcast.26), calls=%async_computation | async-start | bytes 2097152 | tf_op jit(solution)/shard_map/all_to_all | solution.py:333
  174.0 6.4 %copy-start.1 = (bf16[8192,1152]{1,0:T(8,128)(2,1)S(1)}, bf16[8192,1152]{1,0:T(8,128)(2,1)}, u32[]{:S(2)}) copy-start(bf16[8192,1152]{1,0:T(8,128)(2,1)} %copy-done) | copy-start | bytes 56623108
  183.8 0.8 copy-start.15
  184.6 4.3 %collective-permute-start.9 = (bf16[128,128]{1,0:T(8,128)(2,1)S(1)}, bf16[128,128]{1,0:T(8,128)(2,1)S(1)}, u32[]{:S(2)}, u32[]{:S(2)}) collective-permute-start(bf16[128,128]{1,0:T(8,128)(2,1)S(1)} %get-tuple-element.94), channel_id=1, source_target_pairs={{0,2},{2,0},{4,6},{6,4},{8,10},{10,8},{12,14},{14,12},{1,3},{3,1},... | collective-permute-start | bytes 98312 | tf_op jit(solution)/shard_map/ppermute | solution.py:108
  197.4 14.5 %collective-permute-start.13 = (bf16[8,64,512]{2,1,0:T(8,128)(2,1)S(1)}, bf16[8,64,512]{2,1,0:T(8,128)(2,1)S(1)}, u32[]{:S(2)}, u32[]{:S(2)}) collective-permute-start(bf16[8,64,512]{2,1,0:T(8,128)(2,1)S(1)} %take.1.refs_12_), channel_id=1, source_target_pairs={{0,16},{16,0},{1,17},{17,1},{2,18},{18,2},{3,19},{19,3},{4,20},{20... | collective-permute-start | bytes 1572872 | tf_op jit(solution)/shard_map/ppermute | solution.py:112
  199.0 6.6 %collective-permute-start.10 = (bf16[2,128,128]{2,1,0:T(8,128)(2,1)S(1)}, bf16[2,128,128]{2,1,0:T(8,128)(2,1)S(1)}, u32[]{:S(2)}, u32[]{:S(2)}) collective-permute-start(bf16[2,128,128]{2,1,0:T(8,128)(2,1)S(1)} %pad_maximum_fusion.refs_8_), channel_id=1, source_target_pairs={{0,4},{2,6},{4,0},{6,2},{8,12},{10,14},{12,8},{14,10},{1,5},{3,7},... | collective-permute-start | bytes 196616 | tf_op jit(solution)/shard_map/ppermute | solution.py:108
  202.2 8.2 %collective-permute-start.11 = (bf16[2,128,128]{2,1,0:T(8,128)(2,1)S(1)}, bf16[2,128,128]{2,1,0:T(8,128)(2,1)S(1)}, u32[]{:S(2)}, u32[]{:S(2)}) collective-permute-start(bf16[2,128,128]{2,1,0:T(8,128)(2,1)S(1)} %pad_maximum_fusion.refs_8_), channel_id=1, source_target_pairs={{0,8},{2,10},{4,12},{6,14},{8,0},{10,2},{12,4},{14,6},{1,9},{3,11}... | collective-permute-start | bytes 196616 | tf_op jit(solution)/shard_map/ppermute | solution.py:108
  204.2 6.3 %collective-permute-start.12 = (bf16[2,128,128]{2,1,0:T(8,128)(2,1)S(1)}, bf16[2,128,128]{2,1,0:T(8,128)(2,1)S(1)}, u32[]{:S(2)}, u32[]{:S(2)}) collective-permute-start(bf16[2,128,128]{2,1,0:T(8,128)(2,1)S(1)} %pad_maximum_fusion.refs_8_), channel_id=1, source_target_pairs={{0,12},{2,14},{4,8},{6,10},{8,4},{10,6},{12,0},{14,2},{1,13},{3,15... | collective-permute-start | bytes 196616 | tf_op jit(solution)/shard_map/ppermute | solution.py:108

commit v13 on v12

--- a/solution.py
+++ b/solution.py
@@ -184,7 +184,7 @@
     part = out.shape[3]
     for t in range(8):
         at = pl.multiple_of((2 * t + table[2]) * part, part)
-        out[t, 0] = up[0, :, pl.ds(at, part)]
+        out[0, t] = up[0, :, pl.ds(at, part)]
 
 
 def pack_call(table, up_maps):
@@ -196,9 +196,9 @@
             num_scalar_prefetch=1,
             grid=(2,),
             in_specs=[pl.BlockSpec((1, rank, width), lambda s, t: (t[s], 0, 0))],
-            out_specs=pl.BlockSpec((8, 1, rank, part), lambda s, t: (0, s, 0, 0)),
+            out_specs=pl.BlockSpec((1, 8, rank, part), lambda s, t: (s, 0, 0, 0)),
         ),
-        out_shape=jax.ShapeDtypeStruct((8, 2, rank, part), jnp.bfloat16),
+        out_shape=jax.ShapeDtypeStruct((2, 8, rank, part), jnp.bfloat16),
         name="pack",
         **settings(),
     )(table, pltpu.with_memory_space_constraint(up_maps, pltpu.HBM))
@@ -301,7 +301,8 @@
 
     down_own = lax.dynamic_index_in_dim(adapter_down_maps, pick_own, 0, keepdims=False)
     down_lent = lax.dynamic_index_in_dim(adapter_down_maps, pick_lent, 0, keepdims=False)
-    up_sent = pack_call(jnp.concatenate([picked, group[None]]).astype(jnp.int32), adapter_up_maps)
+    choice = jnp.stack([pick_own, pick_lent, group.astype(pick_own.dtype)]).astype(jnp.int32)
+    up_sent = pack_call(choice, adapter_up_maps)
 
     position = jnp.where(y == 0, z, 7 - z)
     places = jnp.stack([position + d for d in (0, -1, 1, -2, 2, -3, 3, 4)]) % 8
@@ -324,24 +325,34 @@
         flight = (send(ahead[cut[0]], AHEAD), send(back[cut[1]], BACK))
         groups += [[ahead], [back]]
         if k == 0:
-            down_swapped = swap(extra[1], "store")
+            down_own, down_lent, up_sent = extra
+            extra = (down_own, swap(down_lent, "store"), up_sent[0], swap(up_sent[1], "store"))
         if k == 1:
-            weights = pin_call(query_weight, extra[0], down_swapped)
+            weights = pin_call(query_weight, extra[0], extra[1])
+            pieces = jnp.stack([extra[2], extra[3]], axis=1)
+
+            def piece(other):
+                return lax.dynamic_index_in_dim(pieces, me ^ other, 0, keepdims=False)
+
+            extra = [piece(0)] + [
+                send(piece(d), [(i, i ^ d) for i in range(8)]) for d in (1, 2, 4, 6, 3, 5, 7)
+            ]
+        if k == 2:
+            found = [extra[n] for n in (0, 1, 2, 5, 3, 6, 4, 7)]
+            found = jnp.stack(found).reshape(16, rank, -1)
+            home, core = owner_row // 2, owner_row % 2
+            chosen = 2 * (home ^ me) + jnp.where(core == store, 0, 1)
+            up_mine = take_call(chosen.astype(jnp.int32), found)
+            extra = (up_mine, swap(up_mine, "groups"))
         for g in {0: (), 1: range(3), 2: range(3, 7)}[k]:
             base, shrunk = rows_call(g, table, weights, groups[g], shrunk)
             bases.append(base)
-    up_got = lax.all_to_all(
-        extra[2].reshape(16, rank, -1), ("tensor", "store"), split_axis=0, concat_axis=0, tiled=True
-    )
+    up_mine, up_other = extra
     base, shrunk = rows_call(7, table, weights, [ahead, back], shrunk)
     bases.append(base)
 
-    across = send(shrunk, ACROSS)
-    pair = jnp.stack([shrunk, across])
+    pair = jnp.stack([shrunk, send(shrunk, ACROSS)])
     everyone = [pair] + [send(pair, pairs) for pairs in ALONG]
-    up_got, _ = lax.optimization_barrier((up_got, across))
-    up_mine = take_call(owner_row, up_got)
-    up_other = swap(up_mine, "groups")
     home, core = owners // 2, owners % 2
     where = 2 * ((home // 2) ^ z) + ((home % 2) ^ y)
     table = jnp.stack([blocks, where, core != store, jnp.broadcast_to(group, (8,))])

time: 218 us -> 254 us (1.17)
  waiting for transfers between devices: 116 us -> 140 us
  local copies, waits for them, and re-layouts: 25.8 us -> 30.5 us
  other arithmetic: 1.43 us -> 5.61 us
  starting transfers between devices: 23.1 us -> 27 us
    ppermute x12 -> x19, waiting for transfers between devices: 105 us -> 138 us  [send(): return lax.ppermute(value, 'tensor', pairs)]
    all_to_all x1 -> x0, waiting for transfers between devices: 7.77 us -> none  [chain_body(): lax.all_to_all(extra[2].reshape(16, rank, -1), ('tensor', 'store'), split...]
    ppermute x12 -> x19, starting transfers between devices: 17.5 us -> 24.9 us  [send(): return lax.ppermute(value, 'tensor', pairs)]
    all_to_all x1 -> x0, starting transfers between devices: 4 us -> none  [chain_body(): lax.all_to_all(extra[2].reshape(16, rank, -1), ('tensor', 'store'), split...]
    squeeze x0 -> x2, other arithmetic: none -> 2.92 us  [piece(): return lax.dynamic_index_in_dim(pieces, me ^ other, 0, keepdims=False)]
    unnamed x32 -> x37, local copies, waits for them, and re-layouts: 20.8 us -> 22.7 us
  transfers between devices with their start and end apart: 15 -> 22, of which waited for: 12 -> 10; matrix products, arithmetic and copies ran while one was open for 2% -> 5% of each run, Pallas kernels for 19% -> 14%
where the time goes in v13:
time: 254 us; the launch traced here: 253 us
  waiting for transfers between devices  140 us (55%)
  Pallas kernels  45.5 us (18%)
  local copies, waits for them, and re-layouts  30.5 us (12%)
  starting transfers between devices  27 us (11%)
  other arithmetic  5.61 us (2%)
  between operations  4.32 us (2%)
    ppermute x19, waiting for transfers between devices, send(): return lax.ppermute(value, 'tensor', pairs)  138 us
    pallas_call x8, Pallas kernels, rows_call(): pl.pallas_call(functools.partial(rows_kernel, group), in_specs=[pl.BlockS...  35.4 us
    ppermute x19, starting transfers between devices, send(): return lax.ppermute(value, 'tensor', pairs)  24.9 us
    unnamed x37, local copies, waits for them, and re-layouts  22.7 us
  transfers between devices with their start and end apart: 22, of which 10 were waited for; matrix products, arithmetic and copies ran while one was open for 5% of the time, Pallas kernels for 14%

profile of v13, /device:TPU:0, one launch (start us, length us, event | category | flops | bytes accessed | tf_op | source)
XLA Modules:
  0.0 253.3 jit_solution(8239306331793480565)
XLA Ops:
  0.0 3.0 %collective-permute-start = (bf16[128,8192]{1,0:T(8,128)(2,1)}, bf16[128,8192]{1,0:T(8,128)(2,1)}, u32[]{:S(2)}, u32[]{:S(2)}) collective-permute-start(bf16[128,8192]{1,0:T(8,128)(2,1)} %bitcast.89), channel_id=1, source_target_pairs={{0,4},{4,8},{8,12},{12,14},{14,10},{10,6},{6,2},{2,0},{1,5},{5,9},... | collective-permute-start | bytes 6291464 | tf_op jit(solution)/shard_map/ppermute | solution.py:108
  3.0 0.9 select_reduce_fusion
  4.7 1.3 pad_add_fusion.table
  6.0 1.9 pack.1
  11.7 1.7 dynamic-slice_bitcast_fusion
  13.4 35.5 %collective-permute-done.refs_0_ = bf16[128,8192]{1,0:T(8,128)(2,1)} collective-permute-done((bf16[128,8192]{1,0:T(8,128)(2,1)}, bf16[128,8192]{1,0:T(8,128)(2,1)}, u32[]{:S(2)}, u32[]{:S(2)}) %collective-permute-start) | collective-permute-done | bytes 2097184 | tf_op jit(solution)/shard_map/ppermute | solution.py:108
  48.9 1.5 collective-permute-done.1.refs_0_
  50.4 1.6 collective-permute-start.2
  52.5 0.9 slice_bitcast_fusion
  53.9 2.0 collective-permute-done.5
  55.9 1.0 copy-done.4
  56.9 40.0 %collective-permute-done.2.refs_0_ = bf16[128,8192]{1,0:T(8,128)(2,1)} collective-permute-done((bf16[128,8192]{1,0:T(8,128)(2,1)}, bf16[128,8192]{1,0:T(8,128)(2,1)}, u32[]{:S(2)}, u32[]{:S(2)}) %collective-permute-start.2) | collective-permute-done | bytes 2097184 | tf_op jit(solution)/shard_map/ppermute | solution.py:108
  96.9 1.3 collective-permute-done.3.refs_0_
  98.2 1.6 collective-permute-start.6
  100.3 2.0 fusion.15
  102.3 2.5 collective-permute-start.10
  104.8 1.5 collective-permute-start.11
  106.3 1.3 collective-permute-start.14
  107.6 52.2 %collective-permute-done.10 = bf16[2,64,512]{2,1,0:T(8,128)(2,1)S(1)} collective-permute-done((bf16[2,64,512]{2,1,0:T(8,128)(2,1)S(1)}, bf16[2,64,512]{2,1,0:T(8,128)(2,1)S(1)}, u32[]{:S(2)}, u32[]{:S(2)}) %collective-permute-start.10) | collective-permute-done | bytes 131104 | tf_op jit(solution)/shard_map/ppermute | solution.py:108
  160.0 1.0 fusion.8
  161.8 3.5 %collective-permute-start.12 = (bf16[2,64,512]{2,1,0:T(8,128)(2,1)S(1)}, bf16[2,64,512]{2,1,0:T(8,128)(2,1)S(1)}, u32[]{:S(2)}, u32[]{:S(2)}) collective-permute-start(bf16[2,64,512]{2,1,0:T(8,128)(2,1)S(1)} %get-tuple-element.128), channel_id=1, source_target_pairs={{0,6},{2,4},{4,2},{6,0},{8,14},{10,12},{12,10},{14,8},{1,7},{3,5},... | collective-permute-start | bytes 393224 | tf_op jit(solution)/shard_map/ppermute | solution.py:108
  165.3 1.0 collective-permute-done.8
  166.3 1.7 collective-permute-start.13
  168.1 5.8 %copy-done.2 = bf16[8192,1024]{1,0:T(8,128)(2,1)S(1)} copy-done((bf16[8192,1024]{1,0:T(8,128)(2,1)S(1)}, bf16[8192,1024]{1,0:T(8,128)(2,1)}, u32[]{:S(2)}) %copy-start.2) | copy-done | bytes 16777240
  173.8 1.2 copy-done.5
  175.0 2.8 %pin.1.weights = bf16[8192,1152]{1,0:T(8,128)(2,1)S(1)} custom-call(bf16[8192,1024]{1,0:T(8,128)(2,1)S(1)} %copy-done.2, bf16[64,8192]{1,0:T(8,128)(2,1)S(1)} %get-tuple-element.68.own, bf16[64,8192]{1,0:T(8,128)(2,1)S(1)} %copy-done.5), custom_call_target="tpu_custom_call" | custom-call | flops 1 | bytes 1 | tf_op jit(solution)/shard_map/pin/pallas_call | solution.py:138
  177.9 3.4 %rows.8 = (f32[128,1024]{1,0:T(8,128)S(1)}, bf16[128,128]{1,0:T(8,128)(2,1)S(1)}) custom-call(s32[2,8]{1,0:T(2,128)S(1)} %add_convert_fusion.table, bf16[8192,1152]{1,0:T(8,128)(2,1)S(1)} %pin.1.weights, bf16[128,8192]{1,0:T(8,128)(2,1)S(1)} %bitcast.91, bf16[128,128]{1,0:T(8,128)(2,1)S(1)} %broadcast_in_dim.49.refs_1_), custom_call_target="tpu_custom_call" | custom-call | flops 1 | bytes 1 | tf_op jit(solution)/shard_map/rows/pallas_call | solution.py:170
  181.3 1.6 copy-done.6
  182.9 5.9 %rows.9 = (f32[128,1024]{1,0:T(8,128)S(1)}, bf16[128,128]{1,0:T(8,128)(2,1)S(1)}) custom-call(s32[2,8]{1,0:T(2,128)S(1)} %add_convert_fusion.table, bf16[8192,1152]{1,0:T(8,128)(2,1)S(1)} %pin.1.weights, bf16[128,8192]{1,0:T(8,128)(2,1)} %collective-permute-done.refs_0_, bf16[128,128]{1,0:T(8,128)(2,1)S(1)} %get-tuple-element.72.refs_1_), custom_call_target="tpu_custom_call" | custom-call | flops 1 | bytes 1 | tf_op jit(solution)/shard_map/rows/pallas_call | solution.py:170
  189.6 4.5 %rows.10 = (f32[128,1024]{1,0:T(8,128)S(1)}, bf16[128,128]{1,0:T(8,128)(2,1)S(1)}) custom-call(s32[2,8]{1,0:T(2,128)S(1)} %add_convert_fusion.table, bf16[8192,1152]{1,0:T(8,128)(2,1)S(1)} %pin.1.weights, bf16[128,8192]{1,0:T(8,128)(2,1)} %collective-permute-done.1.refs_0_, bf16[128,128]{1,0:T(8,128)(2,1)S(1)} %get-tuple-element.74.refs_1_), custom_call_target="tpu_custom_call" | custom-call | flops 1 | bytes 1 | tf_op jit(solution)/shard_map/rows/pallas_call | solution.py:170
  194.2 2.4 slice.14
  196.6 1.0 slice.15
  197.7 2.0 collective-permute-start.16
  199.7 0.9 bitcast_dynamic-update-slice_fusion.6
  200.7 0.9 bitcast_dynamic-update-slice_fusion.1
  201.6 0.9 bitcast_dynamic-update-slice_fusion
  202.5 0.9 take.1.refs_12_
  203.4 1.6 collective-permute-start.17
  205.1 6.4 %copy-done.1 = bf16[8192,1152]{1,0:T(8,128)(2,1)S(1)} copy-done((bf16[8192,1152]{1,0:T(8,128)(2,1)S(1)}, bf16[8192,1152]{1,0:T(8,128)(2,1)}, u32[]{:S(2)}) %copy-start.1) | copy-done | bytes 18874392
  211.4 4.5 %rows.11 = (f32[128,1024]{1,0:T(8,128)S(1)}, bf16[128,128]{1,0:T(8,128)(2,1)S(1)}) custom-call(s32[2,8]{1,0:T(2,128)S(1)} %add_convert_fusion.table, bf16[8192,1152]{1,0:T(8,128)(2,1)S(1)} %copy-done.1, bf16[128,8192]{1,0:T(8,128)(2,1)} %collective-permute-done.2.refs_0_, bf16[128,128]{1,0:T(8,128)(2,1)S(1)} %get-tuple-element.84.refs_1_), custom_call_target="tpu_custom_call" | custom-call | flops 1 | bytes 1 | tf_op jit(solution)/shard_map/rows/pallas_call | solution.py:170
  216.7 4.5 %rows.12 = (f32[128,1024]{1,0:T(8,128)S(1)}, bf16[128,128]{1,0:T(8,128)(2,1)S(1)}) custom-call(s32[2,8]{1,0:T(2,128)S(1)} %add_convert_fusion.table, bf16[8192,1152]{1,0:T(8,128)(2,1)S(1)} %copy-done.1, bf16[128,8192]{1,0:T(8,128)(2,1)} %collective-permute-done.3.refs_0_, bf16[128,128]{1,0:T(8,128)(2,1)S(1)} %get-tuple-element.86.refs_1_), custom_call_target="tpu_custom_call" | custom-call | flops 1 | bytes 1 | tf_op jit(solution)/shard_map/rows/pallas_call | solution.py:170
  222.1 4.5 %rows.13 = (f32[128,1024]{1,0:T(8,128)S(1)}, bf16[128,128]{1,0:T(8,128)(2,1)S(1)}) custom-call(s32[2,8]{1,0:T(2,128)S(1)} %add_convert_fusion.table, bf16[8192,1152]{1,0:T(8,128)(2,1)S(1)} %copy-done.1, bf16[128,8192]{1,0:T(8,128)(2,1)} %collective-permute-done.6.refs_0_, bf16[128,128]{1,0:T(8,128)(2,1)S(1)} %get-tuple-element.88.refs_1_), custom_call_target="tpu_custom_call" | custom-call | flops 1 | bytes 1 | tf_op jit(solution)/shard_map/rows/pallas_call | solution.py:170
  227.4 3.4 %rows.14 = (f32[128,1024]{1,0:T(8,128)S(1)}, bf16[128,128]{1,0:T(8,128)(2,1)S(1)}) custom-call(s32[2,8]{1,0:T(2,128)S(1)} %add_convert_fusion.table, bf16[8192,1152]{1,0:T(8,128)(2,1)S(1)} %copy-done.1, bf16[128,8192]{1,0:T(8,128)(2,1)S(1)} %collective-permute-done.7.refs_0_, bf16[128,128]{1,0:T(8,128)(2,1)S(1)} %get-tuple-element.90.refs_1_), custom_call_target="tpu_custom_call" | custom-call | flops 1 | bytes 1 | tf_op jit(solution)/shard_map/rows/pallas_call | solution.py:170
  231.6 4.7 %rows.15 = (f32[128,1024]{1,0:T(8,128)S(1)}, bf16[128,128]{1,0:T(8,128)(2,1)S(1)}) custom-call(s32[2,8]{1,0:T(2,128)S(1)} %add_convert_fusion.table, bf16[8192,1152]{1,0:T(8,128)(2,1)S(1)} %copy-done.1, bf16[64,8192]{1,0:T(8,128)(2,1)} %collective-permute-done.15.refs_0_, bf16[64,8192]{1,0:T(8,128)(2,1)} %collective-permute-done.16.refs_1_, ...), custom_call_target="tpu_custom_call" | custom-call | flops 1 | bytes 1 | tf_op jit(solution)/shard_map/rows/pallas_call | solution.py:170
  237.2 3.8 %collective-permute-done.18 = bf16[128,128]{1,0:T(8,128)(2,1)S(1)} collective-permute-done((bf16[128,128]{1,0:T(8,128)(2,1)S(1)}, bf16[128,128]{1,0:T(8,128)(2,1)S(1)}, u32[]{:S(2)}, u32[]{:S(2)}) %collective-permute-start.18) | collective-permute-done | bytes 32800 | tf_op jit(solution)/shard_map/ppermute | solution.py:108
  241.8 3.7 %collective-permute-start.21 = (bf16[2,128,128]{2,1,0:T(8,128)(2,1)S(1)}, bf16[2,128,128]{2,1,0:T(8,128)(2,1)S(1)}, u32[]{:S(2)}, u32[]{:S(2)}) collective-permute-start(bf16[2,128,128]{2,1,0:T(8,128)(2,1)S(1)} %pad_maximum_fusion.refs_8_), channel_id=1, source_target_pairs={{0,12},{2,14},{4,8},{6,10},{8,4},{10,6},{12,0},{14,2},{1,13},{3,15... | collective-permute-start | bytes 196616 | tf_op jit(solution)/shard_map/ppermute | solution.py:108
  246.3 2.2 collective-permute-done.21.refs_11_
  248.5 4.6 %finish.1 = bf16[1024,1024]{1,0:T(8,128)(2,1)} custom-call(s32[4,8]{1,0:T(4,128)S(1)} %add_add_fusion.table, f32[128,1024]{1,0:T(8,128)} %copy-done.6, f32[128,1024]{1,0:T(8,128)} %copy-done.7, f32[128,1024]{1,0:T(8,128)} %copy-done.8, f32[128,1024]{1,0:T(8,128)} %copy-done.9, f32[128,1024]{1,0:T(8,128)} %copy-done.10, f32[128,1024]{1,0:T(8,128)} %copy-done.11, ...), custom_call_target="tpu_custom_call" | custom-call | flops 1 | bytes 1 | tf_op jit(solution)/shard_map/finish/pallas_call | solution.py:256
  (68 shorter events, 10.1 us)
Async XLA Ops:
  0.0 48.9 %collective-permute-start = (bf16[128,8192]{1,0:T(8,128)(2,1)}, bf16[128,8192]{1,0:T(8,128)(2,1)}, u32[]{:S(2)}, u32[]{:S(2)}) collective-permute-start(bf16[128,8192]{1,0:T(8,128)(2,1)} %bitcast.89), channel_id=1, source_target_pairs={{0,4},{4,8},{8,12},{12,14},{14,10},{10,6},{6,2},{2,0},{1,5},{5,9},... | collective-permute-start | bytes 6291464 | tf_op jit(solution)/shard_map/ppermute | solution.py:108
  3.0 47.4 %collective-permute-start.1 = (bf16[128,8192]{1,0:T(8,128)(2,1)}, bf16[128,8192]{1,0:T(8,128)(2,1)}, u32[]{:S(2)}, u32[]{:S(2)}) collective-permute-start(bf16[128,8192]{1,0:T(8,128)(2,1)} %bitcast.90), channel_id=1, source_target_pairs={{4,0},{8,4},{12,8},{14,12},{10,14},{6,10},{2,6},{0,2},{5,1},{9,5},... | collective-permute-start | bytes 6291464 | tf_op jit(solution)/shard_map/ppermute | solution.py:108
  50.4 46.5 %collective-permute-start.2 = (bf16[128,8192]{1,0:T(8,128)(2,1)}, bf16[128,8192]{1,0:T(8,128)(2,1)}, u32[]{:S(2)}, u32[]{:S(2)}) collective-permute-start(bf16[128,8192]{1,0:T(8,128)(2,1)} %collective-permute-done.refs_0_), channel_id=1, source_target_pairs={{0,4},{4,8},{8,12},{12,14},{14,10},{10,6},{6,2},{2,0},{1,5},{5,9},... | collective-permute-start | bytes 6291464 | tf_op jit(solution)/shard_map/ppermute | solution.py:108
  52.0 46.2 %collective-permute-start.3 = (bf16[128,8192]{1,0:T(8,128)(2,1)}, bf16[128,8192]{1,0:T(8,128)(2,1)}, u32[]{:S(2)}, u32[]{:S(2)}) collective-permute-start(bf16[128,8192]{1,0:T(8,128)(2,1)} %collective-permute-done.1.refs_0_), channel_id=1, source_target_pairs={{4,0},{8,4},{12,8},{14,12},{10,14},{6,10},{2,6},{0,2},{5,1},{9,5},... | collective-permute-start | bytes 6291464 | tf_op jit(solution)/shard_map/ppermute | solution.py:108
  52.5 3.4 %collective-permute-start.4 = (bf16[64,8192]{1,0:T(8,128)(2,1)S(1)}, bf16[64,8192]{1,0:T(8,128)(2,1)S(1)}, u32[]{:S(2)}, u32[]{:S(2)}) collective-permute-start(bf16[64,8192]{1,0:T(8,128)(2,1)S(1)} %get-tuple-element.64), channel_id=1, source_target_pairs={{0,1},{1,0},{2,3},{3,2},{4,5},{5,4},{6,7},{7,6},{8,9},{9,8},{10,11... | collective-permute-start | bytes 3145736 | tf_op jit(solution)/shard_map/ppermute | solution.py:112
  53.4 2.5 collective-permute-start.5
  55.9 42.4 %copy-start.14 = (bf16[8,64,512]{2,1,0:T(8,128)(2,1)}, bf16[8,64,512]{2,1,0:T(8,128)(2,1)S(1)}, u32[]{:S(2)}) copy-start(bf16[8,64,512]{2,1,0:T(8,128)(2,1)S(1)} %collective-permute-done.5) | copy-start | bytes 1572868
  55.9 1.0 copy-start.4
  98.2 96.0 %collective-permute-start.6 = (bf16[128,8192]{1,0:T(8,128)(2,1)}, bf16[128,8192]{1,0:T(8,128)(2,1)}, u32[]{:S(2)}, u32[]{:S(2)}) collective-permute-start(bf16[128,8192]{1,0:T(8,128)(2,1)} %collective-permute-done.2.refs_0_), channel_id=1, source_target_pairs={{0,4},{4,8},{8,12},{12,14},{14,10},{10,6},{6,2},{2,0},{1,5},{5,9},... | collective-permute-start | bytes 6291464 | tf_op jit(solution)/shard_map/ppermute | solution.py:108
  99.8 94.4 %collective-permute-start.7 = (bf16[128,8192]{1,0:T(8,128)(2,1)}, bf16[128,8192]{1,0:T(8,128)(2,1)S(1)}, u32[]{:S(2)}, u32[]{:S(2)}) collective-permute-start(bf16[128,8192]{1,0:T(8,128)(2,1)} %collective-permute-done.3.refs_0_), channel_id=1, source_target_pairs={{4,0},{8,4},{12,8},{14,12},{10,14},{6,10},{2,6},{0,2},{5,1},{9,5},... | collective-permute-start | bytes 6291464 | tf_op jit(solution)/shard_map/ppermute | solution.py:108
  102.3 57.5 %collective-permute-start.10 = (bf16[2,64,512]{2,1,0:T(8,128)(2,1)S(1)}, bf16[2,64,512]{2,1,0:T(8,128)(2,1)S(1)}, u32[]{:S(2)}, u32[]{:S(2)}) collective-permute-start(bf16[2,64,512]{2,1,0:T(8,128)(2,1)S(1)} %get-tuple-element.125), channel_id=1, source_target_pairs={{0,8},{2,10},{4,12},{6,14},{8,0},{10,2},{12,4},{14,6},{1,9},{3,11}... | collective-permute-start | bytes 393224 | tf_op jit(solution)/shard_map/ppermute | solution.py:108
  104.8 56.1 %collective-permute-start.11 = (bf16[2,64,512]{2,1,0:T(8,128)(2,1)}, bf16[2,64,512]{2,1,0:T(8,128)(2,1)}, u32[]{:S(2)}, u32[]{:S(2)}) collective-permute-start(bf16[2,64,512]{2,1,0:T(8,128)(2,1)} %get-tuple-element.126), channel_id=1, source_target_pairs={{0,12},{2,14},{4,8},{6,10},{8,4},{10,6},{12,0},{14,2},{1,13},{3,15... | collective-permute-start | bytes 393224 | tf_op jit(solution)/shard_map/ppermute | solution.py:108
  106.3 55.5 %collective-permute-start.14 = (bf16[2,64,512]{2,1,0:T(8,128)(2,1)}, bf16[2,64,512]{2,1,0:T(8,128)(2,1)}, u32[]{:S(2)}, u32[]{:S(2)}) collective-permute-start(bf16[2,64,512]{2,1,0:T(8,128)(2,1)} %get-tuple-element.121), channel_id=1, source_target_pairs={{0,14},{2,12},{4,10},{6,8},{8,6},{10,4},{12,2},{14,0},{1,15},{3,13... | collective-permute-start | bytes 393224 | tf_op jit(solution)/shard_map/ppermute | solution.py:108
  159.8 6.5 %collective-permute-start.8 = (bf16[2,64,512]{2,1,0:T(8,128)(2,1)S(1)}, bf16[2,64,512]{2,1,0:T(8,128)(2,1)}, u32[]{:S(2)}, u32[]{:S(2)}) collective-permute-start(bf16[2,64,512]{2,1,0:T(8,128)(2,1)S(1)} %get-tuple-element.123), channel_id=1, source_target_pairs={{0,2},{2,0},{4,6},{6,4},{8,10},{10,8},{12,14},{14,12},{1,3},{3,1},... | collective-permute-start | bytes 393224 | tf_op jit(solution)/shard_map/ppermute | solution.py:108
  161.0 33.2 %collective-permute-start.9 = (bf16[2,64,512]{2,1,0:T(8,128)(2,1)}, bf16[2,64,512]{2,1,0:T(8,128)(2,1)S(1)}, u32[]{:S(2)}, u32[]{:S(2)}) collective-permute-start(bf16[2,64,512]{2,1,0:T(8,128)(2,1)} %get-tuple-element.124), channel_id=1, source_target_pairs={{0,4},{2,6},{4,0},{6,2},{8,12},{10,14},{12,8},{14,10},{1,5},{3,7},... | collective-permute-start | bytes 393224 | tf_op jit(solution)/shard_map/ppermute | solution.py:108
  161.8 32.3 %collective-permute-start.12 = (bf16[2,64,512]{2,1,0:T(8,128)(2,1)S(1)}, bf16[2,64,512]{2,1,0:T(8,128)(2,1)S(1)}, u32[]{:S(2)}, u32[]{:S(2)}) collective-permute-start(bf16[2,64,512]{2,1,0:T(8,128)(2,1)S(1)} %get-tuple-element.128), channel_id=1, source_target_pairs={{0,6},{2,4},{4,2},{6,0},{8,14},{10,12},{12,10},{14,8},{1,7},{3,5},... | collective-permute-start | bytes 393224 | tf_op jit(solution)/shard_map/ppermute | solution.py:108
  166.3 27.9 %collective-permute-start.13 = (bf16[2,64,512]{2,1,0:T(8,128)(2,1)S(1)}, bf16[2,64,512]{2,1,0:T(8,128)(2,1)S(1)}, u32[]{:S(2)}, u32[]{:S(2)}) collective-permute-start(bf16[2,64,512]{2,1,0:T(8,128)(2,1)S(1)} %get-tuple-element.127), channel_id=1, source_target_pairs={{0,10},{2,8},{4,14},{6,12},{8,2},{10,0},{12,6},{14,4},{1,11},{3,9}... | collective-permute-start | bytes 393224 | tf_op jit(solution)/shard_map/ppermute | solution.py:108
  168.0 5.8 %copy-start.2 = (bf16[8192,1024]{1,0:T(8,128)(2,1)S(1)}, bf16[8192,1024]{1,0:T(8,128)(2,1)}, u32[]{:S(2)}) copy-start(bf16[8192,1024]{1,0:T(8,128)(2,1)} %weight.1) | copy-start | bytes 50331652
  173.8 1.2 copy-start.5
  175.0 2.8 %copy-start.3 = (bf16[1,128,8192]{2,1,0:T(8,128)(2,1)S(1)}, bf16[1,128,8192]{2,1,0:T(8,128)(2,1)}, u32[]{:S(2)}) copy-start(bf16[1,128,8192]{2,1,0:T(8,128)(2,1)} %param.6) | copy-start | bytes 6291460
  177.8 11.8 %copy-start = (bf16[8192,1152]{1,0:T(8,128)(2,1)}, bf16[8192,1152]{1,0:T(8,128)(2,1)S(1)}, u32[]{:S(2)}) copy-start(bf16[8192,1152]{1,0:T(8,128)(2,1)S(1)} %pin.1.weights) | copy-start | bytes 56623108
  181.3 1.6 copy-start.6
  188.8 0.8 copy-start.7
  194.1 3.5 %copy-start.8 = (f32[128,1024]{1,0:T(8,128)}, f32[128,1024]{1,0:T(8,128)S(1)}, u32[]{:S(2)}) copy-start(f32[128,1024]{1,0:T(8,128)S(1)} %get-tuple-element.103.refs_2_) | copy-start | bytes 1572868
  196.6 35.0 %collective-permute-start.15 = (bf16[64,8192]{1,0:T(8,128)(2,1)}, bf16[64,8192]{1,0:T(8,128)(2,1)}, u32[]{:S(2)}, u32[]{:S(2)}) collective-permute-start(bf16[64,8192]{1,0:T(8,128)(2,1)} %slice.14), channel_id=1, source_target_pairs={{0,4},{4,8},{8,12},{12,14},{14,10},{10,6},{6,2},{2,0},{1,5},{5,9},... | collective-permute-start | bytes 3145736 | tf_op jit(solution)/shard_map/ppermute | solution.py:108
  197.7 34.0 %collective-permute-start.16 = (bf16[64,8192]{1,0:T(8,128)(2,1)}, bf16[64,8192]{1,0:T(8,128)(2,1)}, u32[]{:S(2)}, u32[]{:S(2)}) collective-permute-start(bf16[64,8192]{1,0:T(8,128)(2,1)} %slice.15), channel_id=1, source_target_pairs={{4,0},{8,4},{12,8},{14,12},{10,14},{6,10},{2,6},{0,2},{5,1},{9,5},... | collective-permute-start | bytes 3145736 | tf_op jit(solution)/shard_map/ppermute | solution.py:108
  203.4 28.2 %collective-permute-start.17 = (bf16[8,64,512]{2,1,0:T(8,128)(2,1)S(1)}, bf16[8,64,512]{2,1,0:T(8,128)(2,1)S(1)}, u32[]{:S(2)}, u32[]{:S(2)}) collective-permute-start(bf16[8,64,512]{2,1,0:T(8,128)(2,1)S(1)} %take.1.refs_12_), channel_id=1, source_target_pairs={{0,16},{16,0},{1,17},{17,1},{2,18},{18,2},{3,19},{19,3},{4,20},{20... | collective-permute-start | bytes 1572872 | tf_op jit(solution)/shard_map/ppermute | solution.py:112
  205.1 6.4 %copy-start.1 = (bf16[8192,1152]{1,0:T(8,128)(2,1)S(1)}, bf16[8192,1152]{1,0:T(8,128)(2,1)}, u32[]{:S(2)}) copy-start(bf16[8192,1152]{1,0:T(8,128)(2,1)} %copy-done) | copy-start | bytes 56623108
  215.9 0.8 copy-start.9
  221.2 0.8 copy-start.10
  226.6 0.8 copy-start.11
  230.8 0.8 copy-start.12
  236.3 0.8 copy-start.13
  237.1 3.9 %collective-permute-start.18 = (bf16[128,128]{1,0:T(8,128)(2,1)S(1)}, bf16[128,128]{1,0:T(8,128)(2,1)S(1)}, u32[]{:S(2)}, u32[]{:S(2)}) collective-permute-start(bf16[128,128]{1,0:T(8,128)(2,1)S(1)} %get-tuple-element.112), channel_id=1, source_target_pairs={{0,2},{2,0},{4,6},{6,4},{8,10},{10,8},{12,14},{14,12},{1,3},{3,1},... | collective-permute-start | bytes 98312 | tf_op jit(solution)/shard_map/ppermute | solution.py:108
  241.0 4.5 %collective-permute-start.19 = (bf16[2,128,128]{2,1,0:T(8,128)(2,1)S(1)}, bf16[2,128,128]{2,1,0:T(8,128)(2,1)S(1)}, u32[]{:S(2)}, u32[]{:S(2)}) collective-permute-start(bf16[2,128,128]{2,1,0:T(8,128)(2,1)S(1)} %pad_maximum_fusion.refs_8_), channel_id=1, source_target_pairs={{0,4},{2,6},{4,0},{6,2},{8,12},{10,14},{12,8},{14,10},{1,5},{3,7},... | collective-permute-start | bytes 196616 | tf_op jit(solution)/shard_map/ppermute | solution.py:108
  241.1 5.2 %collective-permute-start.20 = (bf16[2,128,128]{2,1,0:T(8,128)(2,1)S(1)}, bf16[2,128,128]{2,1,0:T(8,128)(2,1)S(1)}, u32[]{:S(2)}, u32[]{:S(2)}) collective-permute-start(bf16[2,128,128]{2,1,0:T(8,128)(2,1)S(1)} %pad_maximum_fusion.refs_8_), channel_id=1, source_target_pairs={{0,8},{2,10},{4,12},{6,14},{8,0},{10,2},{12,4},{14,6},{1,9},{3,11}... | collective-permute-start | bytes 196616 | tf_op jit(solution)/shard_map/ppermute | solution.py:108
  241.8 6.7 %collective-permute-start.21 = (bf16[2,128,128]{2,1,0:T(8,128)(2,1)S(1)}, bf16[2,128,128]{2,1,0:T(8,128)(2,1)S(1)}, u32[]{:S(2)}, u32[]{:S(2)}) collective-permute-start(bf16[2,128,128]{2,1,0:T(8,128)(2,1)S(1)} %pad_maximum_fusion.refs_8_), channel_id=1, source_target_pairs={{0,12},{2,14},{4,8},{6,10},{8,4},{10,6},{12,0},{14,2},{1,13},{3,15... | collective-permute-start | bytes 196616 | tf_op jit(solution)/shard_map/ppermute | solution.py:108

commit v14 on v11

--- a/solution.py
+++ b/solution.py
@@ -189,7 +189,7 @@
     part = out.shape[3]
     for t in range(8):
         at = pl.multiple_of((2 * t + table[2]) * part, part)
-        out[t, 0] = up[0, :, pl.ds(at, part)]
+        out[0, t] = up[0, :, pl.ds(at, part)]
 
 
 def pack_call(table, up_maps):
@@ -201,9 +201,9 @@
             num_scalar_prefetch=1,
             grid=(2,),
             in_specs=[pl.BlockSpec((1, rank, width), lambda s, t: (t[s], 0, 0))],
-            out_specs=pl.BlockSpec((8, 1, rank, part), lambda s, t: (0, s, 0, 0)),
+            out_specs=pl.BlockSpec((1, 8, rank, part), lambda s, t: (s, 0, 0, 0)),
         ),
-        out_shape=jax.ShapeDtypeStruct((8, 2, rank, part), jnp.bfloat16),
+        out_shape=jax.ShapeDtypeStruct((2, 8, rank, part), jnp.bfloat16),
         name="pack",
         **settings(),
     )(table, pltpu.with_memory_space_constraint(up_maps, pltpu.HBM))
@@ -298,13 +298,11 @@
     halves = [rows[:HALF], rows[HALF:]]
 
     ahead, back = list(halves), list(halves[::-1])
-    flight = [(send(ahead[k], AHEAD), send(back[k], BACK)) for k in range(2)]
-    got, ahead, back, adapter_home_slot, adapter_per_block = lax.optimization_barrier(
-        (flight[0], ahead, back, adapter_home_slot, adapter_per_block)
-    )
-    ahead.append(got[0])
-    back.append(got[1])
-    flight.append((send(ahead[2], AHEAD), send(back[2], BACK)))
+
+    def ring(k):
+        return send(ahead[k], AHEAD), send(back[k], BACK)
+
+    flight = {0: ring(0), 1: ring(1)}
 
     store_slots = find_slots(adapter_home_slot, adapter_per_block)
     owner = store_slots // held
@@ -316,9 +314,8 @@
 
     down_own = lax.dynamic_index_in_dim(adapter_down_maps, pick_own, 0, keepdims=False)
     down_lent = lax.dynamic_index_in_dim(adapter_down_maps, pick_lent, 0, keepdims=False)
-    down_swapped = swap(down_lent, "store")
-    weights = pin_call(query_weight, down_own, down_swapped)
-    up_sent = pack_call(jnp.concatenate([picked, group[None]]).astype(jnp.int32), adapter_up_maps)
+    choice = jnp.stack([pick_own, pick_lent, group.astype(pick_own.dtype)]).astype(jnp.int32)
+    up_sent = pack_call(choice, adapter_up_maps)
 
     position = jnp.where(y == 0, z, 7 - z)
     places = []
@@ -331,33 +328,67 @@
     owners = jnp.sum(jnp.where(hit, owner_row[None, :], 0), axis=1)
     table = jnp.stack([owners == myself, owners == me * 2 + 1 - store]).astype(jnp.int32)
 
+    def piece(other):
+        return lax.dynamic_index_in_dim(pieces, me ^ other, 0, keepdims=False)
+
+    def to_chip(other):
+        return send(piece(other), [(i, i ^ other) for i in range(8)])
+
+    def arrive(got):
+        ahead.append(got[0])
+        back.append(got[1])
+        step = len(ahead) - 2
+        groups.append(list(got) if step % 2 else list(got[::-1]))
+
+    groups = [[rows]]
+    got, ahead, back, down_own, down_lent, up_sent = lax.optimization_barrier(
+        (flight.pop(0), ahead, back, down_own, down_lent, up_sent)
+    )
+    arrive(got)
+    down_swapped = swap(down_lent, "store")
+    pieces = jnp.stack([up_sent[0], swap(up_sent[1], "store")], axis=1)
+    ups = {0: piece(0), 7: to_chip(7), 6: to_chip(6), 5: to_chip(5)}
+    got, ahead, back, down_own, down_swapped, pieces = lax.optimization_barrier(
+        (flight.pop(1), ahead, back, down_own, down_swapped, pieces)
+    )
+    arrive(got)
+    far, pieces = lax.optimization_barrier(({d: ups[d] for d in (0, 5, 6, 7)}, pieces))
+    ups = far | {d: to_chip(d) for d in (4, 3, 2, 1)}
+    ups, ahead, back, down_own, down_swapped = lax.optimization_barrier(
+        (ups, ahead, back, down_own, down_swapped)
+    )
+    flight.update({2: ring(2), 3: ring(3)})
+    weights = pin_call(query_weight, down_own, down_swapped)
+
     bases = []
     shrunk = jnp.zeros((BLOCK, 2 * rank), jnp.bfloat16)
-    groups = [[rows], [ahead[2], back[2]]]
-    for k in range(1, 7):
-        (got_ahead, got_back), ahead, back, bases, shrunk, up_sent = lax.optimization_barrier(
-            (flight[k], ahead, back, bases, shrunk, up_sent)
-        )
-        ahead.append(got_ahead)
-        back.append(got_back)
-        if k < 5:
-            flight.append((send(ahead[k + 2], AHEAD), send(back[k + 2], BACK)))
-        groups.append([got_ahead, got_back] if k % 2 == 0 else [got_back, got_ahead])
-        for g in range(len(bases), min(len(bases) + 2, k + 2, 7)):
+
+    def work(shrunk, count):
+        for g in range(len(bases), min(len(bases) + count, len(groups), 7)):
             base, shrunk = rows_call(g, table, weights, groups[g], shrunk)
             bases.append(base)
-    up_got = lax.all_to_all(
-        up_sent.reshape(16, rank, -1), ("tensor", "store"), split_axis=0, concat_axis=0, tiled=True
-    )
+        return shrunk
+
+    shrunk = work(shrunk, 2)
+    for k in range(2, 7):
+        got, ahead, back, bases, shrunk = lax.optimization_barrier(
+            (flight.pop(k), ahead, back, bases, shrunk)
+        )
+        arrive(got)
+        if k + 2 < 7:
+            flight[k + 2] = ring(k + 2)
+        if k == 4:
+            found = jnp.stack([ups[d] for d in range(8)]).reshape(16, rank, -1)
+            home, core = owner_row // 2, owner_row % 2
+            chosen = 2 * (home ^ me) + jnp.where(core == store, 0, 1)
+            up_mine = take_call(chosen.astype(jnp.int32), found)
+            up_other = swap(up_mine, "groups")
+        shrunk = work(shrunk, 2)
     base, shrunk = rows_call(7, table, weights, groups[7], shrunk)
     bases.append(base)
 
-    across = send(shrunk, ACROSS)
-    pair = jnp.stack([shrunk, across])
+    pair = jnp.stack([shrunk, send(shrunk, ACROSS)])
     everyone = [pair] + [send(pair, pairs) for pairs in ALONG]
-    up_got, _ = lax.optimization_barrier((up_got, across))
-    up_mine = take_call(owner_row, up_got)
-    up_other = swap(up_mine, "groups")
     home, core = owners // 2, owners % 2
     where = 2 * ((home // 2) ^ z) + ((home % 2) ^ y)
     table = jnp.stack([blocks, where, core != store, jnp.broadcast_to(group, (16,))])

time: 215 us -> 230 us (1.070)
  starting transfers between devices: 30.2 us -> 38.9 us
  local copies, waits for them, and re-layouts: 26 us -> 31.5 us
  other arithmetic: 0.64 us -> 4.37 us
    ppermute x18 -> x25, starting transfers between devices: 23.7 us -> 36.8 us  [send(): return lax.ppermute(value, 'tensor', pairs)]
    all_to_all x1 -> x0, waiting for transfers between devices: 7.76 us -> none  [chain_body(): lax.all_to_all(up_sent.reshape(16, rank, -1), ('tensor', 'store'), split_...]
    ppermute x18 -> x25, waiting for transfers between devices: 100 us -> 106 us  [send(): return lax.ppermute(value, 'tensor', pairs)]
    all_to_all x1 -> x0, starting transfers between devices: 4.93 us -> none  [chain_body(): lax.all_to_all(up_sent.reshape(16, rank, -1), ('tensor', 'store'), split_...]
    unnamed x28 -> x53, local copies, waits for them, and re-layouts: 19.2 us -> 23.6 us
    another operation x1 -> x3, other arithmetic: 0.01 us -> 2.69 us  [the longest x1 1.38 us: chain_body(): jnp.stack([pick_own, pick_lent, group.astype(pick_own.dtype)])]
  transfers between devices with their start and end apart: 21 -> 28, of which waited for: 15 -> 19; matrix products, arithmetic and copies ran while one was open for 2% -> 6% of each run, Pallas kernels for 18% -> 16%
where the time goes in v14:
time: 230 us; the launch traced here: 229 us
  waiting for transfers between devices  108 us (47%)
  Pallas kernels  41.9 us (18%)
  starting transfers between devices  38.9 us (17%)
  local copies, waits for them, and re-layouts  31.5 us (14%)
  between operations  4.5 us (2%)
  other arithmetic  4.37 us (2%)
    ppermute x25, waiting for transfers between devices, send(): return lax.ppermute(value, 'tensor', pairs)  106 us
    ppermute x25, starting transfers between devices, send(): return lax.ppermute(value, 'tensor', pairs)  36.8 us
    pallas_call x8, Pallas kernels, rows_call(): pl.pallas_call(functools.partial(rows_kernel, group), in_specs=[pl.BlockS...  31.3 us
    unnamed x53, local copies, waits for them, and re-layouts  23.6 us
    pallas_call x1, Pallas kernels, finish_call(): pl.pallas_call(finish_kernel, in_specs=[pl.BlockSpec(memory_space=pltpu.S...  5.23 us
  transfers between devices with their start and end apart: 28, of which 19 were waited for; matrix products, arithmetic and copies ran while one was open for 6% of the time, Pallas kernels for 16%

profile of v14, /device:TPU:0, one launch (start us, length us, event | category | flops | bytes accessed | tf_op | source)
XLA Modules:
  0.0 229.0 jit_solution(14307958219614148547)
XLA Ops:
  0.0 3.1 %slice_bitcast_fusion = (bf16[64,8192]{1,0:T(8,128)(2,1)}, bf16[64,8192]{1,0:T(8,128)(2,1)}) fusion(bf16[1,128,8192]{2,1,0:T(8,128)(2,1)} %param.6), kind=kLoop, calls=%fused_computation.11 | loop fusion | bytes 4194304 | tf_op jit(solution)/shard_map/slice | solution.py:298
  3.1 3.0 %collective-permute-start.1 = (bf16[64,8192]{1,0:T(8,128)(2,1)}, bf16[64,8192]{1,0:T(8,128)(2,1)}, u32[]{:S(2)}, u32[]{:S(2)}) collective-permute-start(bf16[64,8192]{1,0:T(8,128)(2,1)} %get-tuple-element.183), channel_id=1, source_target_pairs={{4,0},{8,4},{12,8},{14,12},{10,14},{6,10},{2,6},{0,2},{5,1},{9,5},... | collective-permute-start | bytes 3145736 | tf_op jit(solution)/shard_map/ppermute | solution.py:108
  6.1 2.0 collective-permute-start
  13.1 2.8 %dynamic-slice_bitcast_fusion = (bf16[64,8192]{1,0:T(8,128)(2,1)}, bf16[64,8192]{1,0:T(8,128)(2,1)S(1)}) fusion(bf16[4,64,8192]{2,1,0:T(8,128)(2,1)} %param.8, s32[]{:T(128)S(6)} %select_n.191, s32[]{:T(128)S(6)} %select_n.189), kind=kLoop, calls=%fused_computation.9 | loop fusion | bytes 4194312 | tf_op jit(solution)/shard_map/jit(dynamic_index_in_dim)/squeeze | solution.py:316
  15.9 1.4 pad_add_fusion.table
  17.3 1.9 pack.1
  19.2 34.3 %collective-permute-done.refs_0_ = bf16[64,8192]{1,0:T(8,128)(2,1)} collective-permute-done((bf16[64,8192]{1,0:T(8,128)(2,1)}, bf16[64,8192]{1,0:T(8,128)(2,1)}, u32[]{:S(2)}, u32[]{:S(2)}) %collective-permute-start) | collective-permute-done | bytes 1048608 | tf_op jit(solution)/shard_map/ppermute | solution.py:108
  55.1 2.2 collective-permute-done.2
  57.3 1.1 fusion.4
  58.4 3.7 %collective-permute-start.3 = (bf16[2,64,512]{2,1,0:T(8,128)(2,1)S(1)}, bf16[2,64,512]{2,1,0:T(8,128)(2,1)S(1)}, u32[]{:S(2)}, u32[]{:S(2)}) collective-permute-start(bf16[2,64,512]{2,1,0:T(8,128)(2,1)S(1)} %get-tuple-element.191), channel_id=1, source_target_pairs={{0,10},{2,8},{4,14},{6,12},{8,2},{10,0},{12,6},{14,4},{1,11},{3,9}... | collective-permute-start | bytes 393224 | tf_op jit(solution)/shard_map/ppermute | solution.py:108
  62.0 1.3 collective-permute-start.4
  63.4 1.3 collective-permute-start.5
  64.7 1.3 pad_maximum_fusion
  66.0 8.3 %collective-permute-done.3 = bf16[2,64,512]{2,1,0:T(8,128)(2,1)S(1)} collective-permute-done((bf16[2,64,512]{2,1,0:T(8,128)(2,1)S(1)}, bf16[2,64,512]{2,1,0:T(8,128)(2,1)S(1)}, u32[]{:S(2)}, u32[]{:S(2)}) %collective-permute-start.3) | collective-permute-done | bytes 131104 | tf_op jit(solution)/shard_map/ppermute | solution.py:108
  75.0 6.1 %collective-permute-start.10 = (bf16[2,64,512]{2,1,0:T(8,128)(2,1)S(1)}, bf16[2,64,512]{2,1,0:T(8,128)(2,1)}, u32[]{:S(2)}, u32[]{:S(2)}) collective-permute-start(bf16[2,64,512]{2,1,0:T(8,128)(2,1)S(1)} %get-tuple-element.187), channel_id=1, source_target_pairs={{0,4},{2,6},{4,0},{6,2},{8,12},{10,14},{12,8},{14,10},{1,5},{3,7},... | collective-permute-start | bytes 393224 | tf_op jit(solution)/shard_map/ppermute | solution.py:108
  82.0 3.1 %collective-permute-start.12 = (bf16[2,64,512]{2,1,0:T(8,128)(2,1)S(1)}, bf16[2,64,512]{2,1,0:T(8,128)(2,1)}, u32[]{:S(2)}, u32[]{:S(2)}) collective-permute-start(bf16[2,64,512]{2,1,0:T(8,128)(2,1)S(1)} %get-tuple-element.185), channel_id=1, source_target_pairs={{0,8},{2,10},{4,12},{6,14},{8,0},{10,2},{12,4},{14,6},{1,9},{3,11}... | collective-permute-start | bytes 393224 | tf_op jit(solution)/shard_map/ppermute | solution.py:108
  85.5 2.8 %collective-permute-done.10 = bf16[2,64,512]{2,1,0:T(8,128)(2,1)} collective-permute-done((bf16[2,64,512]{2,1,0:T(8,128)(2,1)S(1)}, bf16[2,64,512]{2,1,0:T(8,128)(2,1)}, u32[]{:S(2)}, u32[]{:S(2)}) %collective-permute-start.10) | collective-permute-done | bytes 131104 | tf_op jit(solution)/shard_map/ppermute | solution.py:108
  88.2 2.6 %collective-permute-done.11 = bf16[2,64,512]{2,1,0:T(8,128)(2,1)} collective-permute-done((bf16[2,64,512]{2,1,0:T(8,128)(2,1)S(1)}, bf16[2,64,512]{2,1,0:T(8,128)(2,1)}, u32[]{:S(2)}, u32[]{:S(2)}) %collective-permute-start.11) | collective-permute-done | bytes 131104 | tf_op jit(solution)/shard_map/ppermute | solution.py:108
  90.8 1.3 collective-permute-done.9
  94.4 1.1 collective-permute-start.17
  96.5 5.8 %copy-done.2 = bf16[8192,1024]{1,0:T(8,128)(2,1)S(1)} copy-done((bf16[8192,1024]{1,0:T(8,128)(2,1)S(1)}, bf16[8192,1024]{1,0:T(8,128)(2,1)}, u32[]{:S(2)}) %copy-start.2) | copy-done | bytes 16777240
  102.3 2.8 %pin.1.weights = bf16[8192,1152]{1,0:T(8,128)(2,1)S(1)} custom-call(bf16[8192,1024]{1,0:T(8,128)(2,1)S(1)} %copy-done.2, bf16[64,8192]{1,0:T(8,128)(2,1)S(1)} %get-tuple-element.112.own, bf16[64,8192]{1,0:T(8,128)(2,1)S(1)} %collective-permute-done.8.swapped), custom_call_target="tpu_custom_call" | custom-call | flops 1 | bytes 1 | tf_op jit(solution)/shard_map/pin/pallas_call | solution.py:138
  105.1 3.4 %rows.8 = (f32[128,1024]{1,0:T(8,128)S(1)}, bf16[128,128]{1,0:T(8,128)(2,1)S(1)}) custom-call(s32[2,16]{1,0:T(2,128)S(1)} %add_convert_fusion.table, bf16[8192,1152]{1,0:T(8,128)(2,1)S(1)} %pin.1.weights, bf16[128,8192]{1,0:T(8,128)(2,1)S(1)} %bitcast.96, bf16[128,128]{1,0:T(8,128)(2,1)S(1)} %broadcast_in_dim.49.refs_1_), custom_call_target="tpu_custom_call" | custom-call | flops 1 | bytes 1 | tf_op jit(solution)/shard_map/rows/pallas_call | solution.py:175
  108.5 1.6 copy-done.4
  110.1 1.5 copy-done
  111.6 4.4 %rows.9 = (f32[128,1024]{1,0:T(8,128)S(1)}, bf16[128,128]{1,0:T(8,128)(2,1)S(1)}) custom-call(s32[2,16]{1,0:T(2,128)S(1)} %add_convert_fusion.table, bf16[8192,1152]{1,0:T(8,128)(2,1)S(1)} %pin.1.weights, bf16[64,8192]{1,0:T(8,128)(2,1)} %collective-permute-done.refs_0_, bf16[64,8192]{1,0:T(8,128)(2,1)} %collective-permute-done.1.refs_1_, ...), custom_call_target="tpu_custom_call" | custom-call | flops 1 | bytes 1 | tf_op jit(solution)/shard_map/rows/pallas_call | solution.py:175
  116.9 1.7 collective-permute-done.13.refs_0_
  120.1 1.5 collective-permute-start.16
  123.6 6.4 %copy-done.1 = bf16[8192,1152]{1,0:T(8,128)(2,1)S(1)} copy-done((bf16[8192,1152]{1,0:T(8,128)(2,1)S(1)}, bf16[8192,1152]{1,0:T(8,128)(2,1)}, u32[]{:S(2)}) %copy-start.1) | copy-done | bytes 18874392
  129.9 4.1 %rows.10 = (f32[128,1024]{1,0:T(8,128)S(1)}, bf16[128,128]{1,0:T(8,128)(2,1)S(1)}) custom-call(s32[2,16]{1,0:T(2,128)S(1)} %add_convert_fusion.table, bf16[8192,1152]{1,0:T(8,128)(2,1)S(1)} %copy-done.1, bf16[64,8192]{1,0:T(8,128)(2,1)} %collective-permute-done.7.refs_0_, bf16[64,8192]{1,0:T(8,128)(2,1)S(1)} %collective-permute-done.6.refs_1_, ...), custom_call_target="tpu_custom_call" | custom-call | flops 1 | bytes 1 | tf_op jit(solution)/shard_map/rows/pallas_call | solution.py:175
  134.9 4.6 %rows.11 = (f32[128,1024]{1,0:T(8,128)S(1)}, bf16[128,128]{1,0:T(8,128)(2,1)S(1)}) custom-call(s32[2,16]{1,0:T(2,128)S(1)} %add_convert_fusion.table, bf16[8192,1152]{1,0:T(8,128)(2,1)S(1)} %copy-done.1, bf16[64,8192]{1,0:T(8,128)(2,1)} %collective-permute-done.13.refs_0_, bf16[64,8192]{1,0:T(8,128)(2,1)} %collective-permute-done.14.refs_1_, ...), custom_call_target="tpu_custom_call" | custom-call | flops 1 | bytes 1 | tf_op jit(solution)/shard_map/rows/pallas_call | solution.py:175
  142.7 1.5 collective-permute-start.22
  144.1 4.4 %rows.12 = (f32[128,1024]{1,0:T(8,128)S(1)}, bf16[128,128]{1,0:T(8,128)(2,1)S(1)}) custom-call(s32[2,16]{1,0:T(2,128)S(1)} %add_convert_fusion.table, bf16[8192,1152]{1,0:T(8,128)(2,1)S(1)} %copy-done.1, bf16[64,8192]{1,0:T(8,128)(2,1)} %collective-permute-done.18.refs_0_, bf16[64,8192]{1,0:T(8,128)(2,1)} %collective-permute-done.17.refs_1_, ...), custom_call_target="tpu_custom_call" | custom-call | flops 1 | bytes 1 | tf_op jit(solution)/shard_map/rows/pallas_call | solution.py:175
  148.6 14.8 %collective-permute-done.15.refs_0_ = bf16[64,8192]{1,0:T(8,128)(2,1)S(1)} collective-permute-done((bf16[64,8192]{1,0:T(8,128)(2,1)}, bf16[64,8192]{1,0:T(8,128)(2,1)S(1)}, u32[]{:S(2)}, u32[]{:S(2)}) %collective-permute-start.15) | collective-permute-done | bytes 1048608 | tf_op jit(solution)/shard_map/ppermute | solution.py:108
  165.0 1.5 collective-permute-start.20
  169.1 1.6 collective-permute-start.27
  170.7 3.4 %rows.13 = (f32[128,1024]{1,0:T(8,128)S(1)}, bf16[128,128]{1,0:T(8,128)(2,1)S(1)}) custom-call(s32[2,16]{1,0:T(2,128)S(1)} %add_convert_fusion.table, bf16[8192,1152]{1,0:T(8,128)(2,1)S(1)} %bitcast.95, bf16[64,8192]{1,0:T(8,128)(2,1)S(1)} %collective-permute-done.15.refs_0_, bf16[64,8192]{1,0:T(8,128)(2,1)S(1)} %collective-permute-done.16.refs_1_, ...), custom_call_target="tpu_custom_call" | custom-call | flops 1 | bytes 1 | tf_op jit(solution)/shard_map/rows/pallas_call | solution.py:175
  174.1 11.7 %collective-permute-done.21.refs_1_ = bf16[64,8192]{1,0:T(8,128)(2,1)S(1)} collective-permute-done((bf16[64,8192]{1,0:T(8,128)(2,1)}, bf16[64,8192]{1,0:T(8,128)(2,1)S(1)}, u32[]{:S(2)}, u32[]{:S(2)}) %collective-permute-start.21) | collective-permute-done | bytes 1048608 | tf_op jit(solution)/shard_map/ppermute | solution.py:108
  186.9 3.4 %rows.14 = (f32[128,1024]{1,0:T(8,128)S(1)}, bf16[128,128]{1,0:T(8,128)(2,1)S(1)}) custom-call(s32[2,16]{1,0:T(2,128)S(1)} %add_convert_fusion.table, bf16[8192,1152]{1,0:T(8,128)(2,1)S(1)} %bitcast.95, bf16[64,8192]{1,0:T(8,128)(2,1)S(1)} %collective-permute-done.22.refs_0_, bf16[64,8192]{1,0:T(8,128)(2,1)S(1)} %collective-permute-done.21.refs_1_, ...), custom_call_target="tpu_custom_call" | custom-call | flops 1 | bytes 1 | tf_op jit(solution)/shard_map/rows/pallas_call | solution.py:175
  191.2 14.1 %collective-permute-done.19.refs_0_ = bf16[64,8192]{1,0:T(8,128)(2,1)S(1)} collective-permute-done((bf16[64,8192]{1,0:T(8,128)(2,1)S(1)}, bf16[64,8192]{1,0:T(8,128)(2,1)S(1)}, u32[]{:S(2)}, u32[]{:S(2)}) %collective-permute-start.19) | collective-permute-done | bytes 1048608 | tf_op jit(solution)/shard_map/ppermute | solution.py:108
  205.2 2.0 collective-permute-done.20.refs_1_
  207.2 3.4 %rows.15 = (f32[128,1024]{1,0:T(8,128)S(1)}, bf16[128,128]{1,0:T(8,128)(2,1)S(1)}) custom-call(s32[2,16]{1,0:T(2,128)S(1)} %add_convert_fusion.table, bf16[8192,1152]{1,0:T(8,128)(2,1)S(1)} %bitcast.95, bf16[64,8192]{1,0:T(8,128)(2,1)S(1)} %collective-permute-done.19.refs_0_, bf16[64,8192]{1,0:T(8,128)(2,1)S(1)} %collective-permute-done.20.refs_1_, ...), custom_call_target="tpu_custom_call" | custom-call | flops 1 | bytes 1 | tf_op jit(solution)/shard_map/rows/pallas_call | solution.py:175
  211.9 3.5 %collective-permute-done.23 = bf16[128,128]{1,0:T(8,128)(2,1)S(1)} collective-permute-done((bf16[128,128]{1,0:T(8,128)(2,1)S(1)}, bf16[128,128]{1,0:T(8,128)(2,1)S(1)}, u32[]{:S(2)}, u32[]{:S(2)}) %collective-permute-start.23) | collective-permute-done | bytes 32800 | tf_op jit(solution)/shard_map/ppermute | solution.py:108
  216.0 1.5 collective-permute-start.25
  217.5 2.4 %collective-permute-start.26 = (bf16[2,128,128]{2,1,0:T(8,128)(2,1)S(1)}, bf16[2,128,128]{2,1,0:T(8,128)(2,1)S(1)}, u32[]{:S(2)}, u32[]{:S(2)}) collective-permute-start(bf16[2,128,128]{2,1,0:T(8,128)(2,1)S(1)} %pad_maximum_fusion.1.refs_8_), channel_id=1, source_target_pairs={{0,12},{2,14},{4,8},{6,10},{8,4},{10,6},{12,0},{14,2},{1,13},{3,15... | collective-permute-start | bytes 196616 | tf_op jit(solution)/shard_map/ppermute | solution.py:108
  219.9 1.2 collective-permute-done.25.refs_10_
  221.2 2.4 %collective-permute-done.26.refs_11_ = bf16[2,128,128]{2,1,0:T(8,128)(2,1)S(1)} collective-permute-done((bf16[2,128,128]{2,1,0:T(8,128)(2,1)S(1)}, bf16[2,128,128]{2,1,0:T(8,128)(2,1)S(1)}, u32[]{:S(2)}, u32[]{:S(2)}) %collective-permute-start.26) | collective-permute-done | bytes 65568 | tf_op jit(solution)/shard_map/ppermute | solution.py:108
  223.6 5.2 %finish.1 = bf16[1024,1024]{1,0:T(8,128)(2,1)} custom-call(s32[4,16]{1,0:T(4,128)S(1)} %add_add_fusion.table, f32[128,1024]{1,0:T(8,128)} %copy-done.4, f32[128,1024]{1,0:T(8,128)} %copy-done.5, f32[128,1024]{1,0:T(8,128)} %copy-done.6, f32[128,1024]{1,0:T(8,128)} %copy-done.7, f32[128,1024]{1,0:T(8,128)} %copy-done.8, f32[128,1024]{1,0:T(8,128)} %copy-done.9, ...), custom_call_target="tpu_custom_call" | custom-call | flops 1 | bytes 1 | tf_op jit(solution)/shard_map/finish/pallas_call | solution.py:263
  (97 shorter events, 24.1 us)
Async XLA Ops:
  0.0 8.2 %copy-start.17 = (s32[64]{0:T(128)S(1)}, s32[64]{0:T(128)}, u32[]{:S(2)}) copy-start(s32[64]{0:T(128)} %param.10) | copy-start | bytes 772
  0.0 8.2 %copy-start.16 = (s32[2,8]{1,0:T(2,128)S(1)}, s32[2,8]{1,0:T(2,128)}, u32[]{:S(2)}) copy-start(s32[2,8]{1,0:T(2,128)} %param.11) | copy-start | bytes 196
  3.1 50.4 %collective-permute-start.1 = (bf16[64,8192]{1,0:T(8,128)(2,1)}, bf16[64,8192]{1,0:T(8,128)(2,1)}, u32[]{:S(2)}, u32[]{:S(2)}) collective-permute-start(bf16[64,8192]{1,0:T(8,128)(2,1)} %get-tuple-element.183), channel_id=1, source_target_pairs={{4,0},{8,4},{12,8},{14,12},{10,14},{6,10},{2,6},{0,2},{5,1},{9,5},... | collective-permute-start | bytes 3145736 | tf_op jit(solution)/shard_map/ppermute | solution.py:108
  6.1 57.3 %collective-permute-start.6 = (bf16[64,8192]{1,0:T(8,128)(2,1)}, bf16[64,8192]{1,0:T(8,128)(2,1)S(1)}, u32[]{:S(2)}, u32[]{:S(2)}) collective-permute-start(bf16[64,8192]{1,0:T(8,128)(2,1)} %get-tuple-element.183), channel_id=1, source_target_pairs={{0,4},{4,8},{8,12},{12,14},{14,10},{10,6},{6,2},{2,0},{1,5},{5,9},... | collective-permute-start | bytes 3145736 | tf_op jit(solution)/shard_map/ppermute | solution.py:108
  6.1 47.3 %collective-permute-start = (bf16[64,8192]{1,0:T(8,128)(2,1)}, bf16[64,8192]{1,0:T(8,128)(2,1)}, u32[]{:S(2)}, u32[]{:S(2)}) collective-permute-start(bf16[64,8192]{1,0:T(8,128)(2,1)} %get-tuple-element.184), channel_id=1, source_target_pairs={{0,4},{4,8},{8,12},{12,14},{14,10},{10,6},{6,2},{2,0},{1,5},{5,9},... | collective-permute-start | bytes 3145736 | tf_op jit(solution)/shard_map/ppermute | solution.py:108
  8.2 57.8 %collective-permute-start.7 = (bf16[64,8192]{1,0:T(8,128)(2,1)}, bf16[64,8192]{1,0:T(8,128)(2,1)}, u32[]{:S(2)}, u32[]{:S(2)}) collective-permute-start(bf16[64,8192]{1,0:T(8,128)(2,1)} %get-tuple-element.184), channel_id=1, source_target_pairs={{4,0},{8,4},{12,8},{14,12},{10,14},{6,10},{2,6},{0,2},{5,1},{9,5},... | collective-permute-start | bytes 3145736 | tf_op jit(solution)/shard_map/ppermute | solution.py:108
  53.5 12.5 %collective-permute-start.8 = (bf16[64,8192]{1,0:T(8,128)(2,1)}, bf16[64,8192]{1,0:T(8,128)(2,1)S(1)}, u32[]{:S(2)}, u32[]{:S(2)}) collective-permute-start(bf16[64,8192]{1,0:T(8,128)(2,1)} %get-tuple-element.95), channel_id=1, source_target_pairs={{0,1},{1,0},{2,3},{3,2},{4,5},{5,4},{6,7},{7,6},{8,9},{9,8},{10,11... | collective-permute-start | bytes 3145736 | tf_op jit(solution)/shard_map/ppermute | solution.py:112
  54.6 2.7 %collective-permute-start.2 = (bf16[8,64,512]{2,1,0:T(8,128)(2,1)}, bf16[8,64,512]{2,1,0:T(8,128)(2,1)}, u32[]{:S(2)}, u32[]{:S(2)}) collective-permute-start(bf16[8,64,512]{2,1,0:T(8,128)(2,1)} %get-tuple-element.194), channel_id=1, source_target_pairs={{0,1},{1,0},{2,3},{3,2},{4,5},{5,4},{6,7},{7,6},{8,9},{9,8},{10,11... | collective-permute-start | bytes 1572872 | tf_op jit(solution)/shard_map/ppermute | solution.py:112
  58.4 15.9 %collective-permute-start.3 = (bf16[2,64,512]{2,1,0:T(8,128)(2,1)S(1)}, bf16[2,64,512]{2,1,0:T(8,128)(2,1)S(1)}, u32[]{:S(2)}, u32[]{:S(2)}) collective-permute-start(bf16[2,64,512]{2,1,0:T(8,128)(2,1)S(1)} %get-tuple-element.191), channel_id=1, source_target_pairs={{0,10},{2,8},{4,14},{6,12},{8,2},{10,0},{12,6},{14,4},{1,11},{3,9}... | collective-permute-start | bytes 393224 | tf_op jit(solution)/shard_map/ppermute | solution.py:108
  62.0 12.2 %collective-permute-start.4 = (bf16[2,64,512]{2,1,0:T(8,128)(2,1)S(1)}, bf16[2,64,512]{2,1,0:T(8,128)(2,1)S(1)}, u32[]{:S(2)}, u32[]{:S(2)}) collective-permute-start(bf16[2,64,512]{2,1,0:T(8,128)(2,1)S(1)} %get-tuple-element.192), channel_id=1, source_target_pairs={{0,12},{2,14},{4,8},{6,10},{8,4},{10,6},{12,0},{14,2},{1,13},{3,15... | collective-permute-start | bytes 393224 | tf_op jit(solution)/shard_map/ppermute | solution.py:108
  63.4 10.9 %collective-permute-start.5 = (bf16[2,64,512]{2,1,0:T(8,128)(2,1)S(1)}, bf16[2,64,512]{2,1,0:T(8,128)(2,1)S(1)}, u32[]{:S(2)}, u32[]{:S(2)}) collective-permute-start(bf16[2,64,512]{2,1,0:T(8,128)(2,1)S(1)} %get-tuple-element.189), channel_id=1, source_target_pairs={{0,14},{2,12},{4,10},{6,8},{8,6},{10,4},{12,2},{14,0},{1,15},{3,13... | collective-permute-start | bytes 393224 | tf_op jit(solution)/shard_map/ppermute | solution.py:108
  75.0 13.3 %collective-permute-start.10 = (bf16[2,64,512]{2,1,0:T(8,128)(2,1)S(1)}, bf16[2,64,512]{2,1,0:T(8,128)(2,1)}, u32[]{:S(2)}, u32[]{:S(2)}) collective-permute-start(bf16[2,64,512]{2,1,0:T(8,128)(2,1)S(1)} %get-tuple-element.187), channel_id=1, source_target_pairs={{0,4},{2,6},{4,0},{6,2},{8,12},{10,14},{12,8},{14,10},{1,5},{3,7},... | collective-permute-start | bytes 393224 | tf_op jit(solution)/shard_map/ppermute | solution.py:108
  81.0 9.8 %collective-permute-start.11 = (bf16[2,64,512]{2,1,0:T(8,128)(2,1)S(1)}, bf16[2,64,512]{2,1,0:T(8,128)(2,1)}, u32[]{:S(2)}, u32[]{:S(2)}) collective-permute-start(bf16[2,64,512]{2,1,0:T(8,128)(2,1)S(1)} %get-tuple-element.186), channel_id=1, source_target_pairs={{0,6},{2,4},{4,2},{6,0},{8,14},{10,12},{12,10},{14,8},{1,7},{3,5},... | collective-permute-start | bytes 393224 | tf_op jit(solution)/shard_map/ppermute | solution.py:108
  82.0 8.8 %collective-permute-start.12 = (bf16[2,64,512]{2,1,0:T(8,128)(2,1)S(1)}, bf16[2,64,512]{2,1,0:T(8,128)(2,1)}, u32[]{:S(2)}, u32[]{:S(2)}) collective-permute-start(bf16[2,64,512]{2,1,0:T(8,128)(2,1)S(1)} %get-tuple-element.185), channel_id=1, source_target_pairs={{0,8},{2,10},{4,12},{6,14},{8,0},{10,2},{12,4},{14,6},{1,9},{3,11}... | collective-permute-start | bytes 393224 | tf_op jit(solution)/shard_map/ppermute | solution.py:108
  85.1 7.0 %collective-permute-start.9 = (bf16[2,64,512]{2,1,0:T(8,128)(2,1)S(1)}, bf16[2,64,512]{2,1,0:T(8,128)(2,1)}, u32[]{:S(2)}, u32[]{:S(2)}) collective-permute-start(bf16[2,64,512]{2,1,0:T(8,128)(2,1)S(1)} %get-tuple-element.188), channel_id=1, source_target_pairs={{0,2},{2,0},{4,6},{6,4},{8,10},{10,8},{12,14},{14,12},{1,3},{3,1},... | collective-permute-start | bytes 393224 | tf_op jit(solution)/shard_map/ppermute | solution.py:108
  92.1 26.4 %collective-permute-start.13 = (bf16[64,8192]{1,0:T(8,128)(2,1)}, bf16[64,8192]{1,0:T(8,128)(2,1)}, u32[]{:S(2)}, u32[]{:S(2)}) collective-permute-start(bf16[64,8192]{1,0:T(8,128)(2,1)} %collective-permute-done.refs_0_), channel_id=1, source_target_pairs={{0,4},{4,8},{8,12},{12,14},{14,10},{10,6},{6,2},{2,0},{1,5},{5,9},... | collective-permute-start | bytes 3145736 | tf_op jit(solution)/shard_map/ppermute | solution.py:108
  93.2 26.4 %collective-permute-start.14 = (bf16[64,8192]{1,0:T(8,128)(2,1)}, bf16[64,8192]{1,0:T(8,128)(2,1)}, u32[]{:S(2)}, u32[]{:S(2)}) collective-permute-start(bf16[64,8192]{1,0:T(8,128)(2,1)} %collective-permute-done.1.refs_1_), channel_id=1, source_target_pairs={{4,0},{8,4},{12,8},{14,12},{10,14},{6,10},{2,6},{0,2},{5,1},{9,5},... | collective-permute-start | bytes 3145736 | tf_op jit(solution)/shard_map/ppermute | solution.py:108
  94.4 46.6 %collective-permute-start.17 = (bf16[64,8192]{1,0:T(8,128)(2,1)S(1)}, bf16[64,8192]{1,0:T(8,128)(2,1)}, u32[]{:S(2)}, u32[]{:S(2)}) collective-permute-start(bf16[64,8192]{1,0:T(8,128)(2,1)S(1)} %collective-permute-done.6.refs_1_), channel_id=1, source_target_pairs={{0,4},{4,8},{8,12},{12,14},{14,10},{10,6},{6,2},{2,0},{1,5},{5,9},... | collective-permute-start | bytes 3145736 | tf_op jit(solution)/shard_map/ppermute | solution.py:108
  95.5 46.6 %collective-permute-start.18 = (bf16[64,8192]{1,0:T(8,128)(2,1)}, bf16[64,8192]{1,0:T(8,128)(2,1)}, u32[]{:S(2)}, u32[]{:S(2)}) collective-permute-start(bf16[64,8192]{1,0:T(8,128)(2,1)} %collective-permute-done.7.refs_0_), channel_id=1, source_target_pairs={{4,0},{8,4},{12,8},{14,12},{10,14},{6,10},{2,6},{0,2},{5,1},{9,5},... | collective-permute-start | bytes 3145736 | tf_op jit(solution)/shard_map/ppermute | solution.py:108
  96.5 5.8 %copy-start.2 = (bf16[8192,1024]{1,0:T(8,128)(2,1)S(1)}, bf16[8192,1024]{1,0:T(8,128)(2,1)}, u32[]{:S(2)}) copy-start(bf16[8192,1024]{1,0:T(8,128)(2,1)} %weight.1) | copy-start | bytes 50331652
  102.2 2.8 %copy-start.3 = (bf16[1,128,8192]{2,1,0:T(8,128)(2,1)S(1)}, bf16[1,128,8192]{2,1,0:T(8,128)(2,1)}, u32[]{:S(2)}) copy-start(bf16[1,128,8192]{2,1,0:T(8,128)(2,1)} %param.6) | copy-start | bytes 6291460
  105.0 6.6 %copy-start = (bf16[8192,1152]{1,0:T(8,128)(2,1)}, bf16[8192,1152]{1,0:T(8,128)(2,1)S(1)}, u32[]{:S(2)}) copy-start(bf16[8192,1152]{1,0:T(8,128)(2,1)S(1)} %pin.1.weights) | copy-start | bytes 56623108
  108.5 1.6 copy-start.4
  116.1 0.8 copy-start.5
  119.6 43.8 %collective-permute-start.15 = (bf16[64,8192]{1,0:T(8,128)(2,1)}, bf16[64,8192]{1,0:T(8,128)(2,1)S(1)}, u32[]{:S(2)}, u32[]{:S(2)}) collective-permute-start(bf16[64,8192]{1,0:T(8,128)(2,1)} %collective-permute-done.13.refs_0_), channel_id=1, source_target_pairs={{0,4},{4,8},{8,12},{12,14},{14,10},{10,6},{6,2},{2,0},{1,5},{5,9},... | collective-permute-start | bytes 3145736 | tf_op jit(solution)/shard_map/ppermute | solution.py:108
  120.1 44.3 %collective-permute-start.16 = (bf16[64,8192]{1,0:T(8,128)(2,1)}, bf16[64,8192]{1,0:T(8,128)(2,1)S(1)}, u32[]{:S(2)}, u32[]{:S(2)}) collective-permute-start(bf16[64,8192]{1,0:T(8,128)(2,1)} %collective-permute-done.14.refs_1_), channel_id=1, source_target_pairs={{4,0},{8,4},{12,8},{14,12},{10,14},{6,10},{2,6},{0,2},{5,1},{9,5},... | collective-permute-start | bytes 3145736 | tf_op jit(solution)/shard_map/ppermute | solution.py:108
  123.6 6.4 %copy-start.1 = (bf16[8192,1152]{1,0:T(8,128)(2,1)S(1)}, bf16[8192,1152]{1,0:T(8,128)(2,1)}, u32[]{:S(2)}) copy-start(bf16[8192,1152]{1,0:T(8,128)(2,1)} %copy-done) | copy-start | bytes 56623108
  134.9 35.8 %slice-start = ((s8[18874368]{0:T(1024)(128)(4,1)}), s8[4194304]{0:T(1024)(128)(4,1)S(1)}, s32[]{:S(2)}) async-start(s8[18874368]{0:T(1024)(128)(4,1)} %bitcast.94), calls=%async_computation | async-start | bytes 8388608
  134.9 35.8 %slice-start.1 = ((s8[18874368]{0:T(1024)(128)(4,1)}), s8[4194304]{0:T(1024)(128)(4,1)S(1)}, s32[]{:S(2)}) async-start(s8[18874368]{0:T(1024)(128)(4,1)} %bitcast.94), calls=%async_computation.1 | async-start | bytes 8388608
  134.9 35.8 %slice-start.2 = ((s8[18874368]{0:T(1024)(128)(4,1)}), s8[4194304]{0:T(1024)(128)(4,1)S(1)}, s32[]{:S(2)}) async-start(s8[18874368]{0:T(1024)(128)(4,1)} %bitcast.94), calls=%async_computation.2 | async-start | bytes 8388608
  139.5 0.8 copy-start.7
  142.1 26.2 %copy-start.13 = (bf16[2,64,512]{2,1,0:T(8,128)(2,1)S(1)}, bf16[2,64,512]{2,1,0:T(8,128)(2,1)}, u32[]{:S(2)}) copy-start(bf16[2,64,512]{2,1,0:T(8,128)(2,1)} %copy-done.12) | copy-start | bytes 393220
  142.1 26.3 %copy-start.15 = (bf16[2,64,512]{2,1,0:T(8,128)(2,1)S(1)}, bf16[2,64,512]{2,1,0:T(8,128)(2,1)}, u32[]{:S(2)}) copy-start(bf16[2,64,512]{2,1,0:T(8,128)(2,1)} %copy-done.14) | copy-start | bytes 393220
  142.1 28.6 %slice-start.3 = ((s8[18874368]{0:T(1024)(128)(4,1)}), s8[4194304]{0:T(1024)(128)(4,1)S(1)}, s32[]{:S(2)}) async-start(s8[18874368]{0:T(1024)(128)(4,1)} %bitcast.94), calls=%async_computation.3 | async-start | bytes 8388608
  142.1 28.6 %slice-start.4 = ((s8[18874368]{0:T(1024)(128)(4,1)}), s8[2097152]{0:T(1024)(128)(4,1)S(1)}, s32[]{:S(2)}) async-start(s8[18874368]{0:T(1024)(128)(4,1)} %bitcast.94), calls=%async_computation.4 | async-start | bytes 4194304
  142.1 43.8 %collective-permute-start.21 = (bf16[64,8192]{1,0:T(8,128)(2,1)}, bf16[64,8192]{1,0:T(8,128)(2,1)S(1)}, u32[]{:S(2)}, u32[]{:S(2)}) collective-permute-start(bf16[64,8192]{1,0:T(8,128)(2,1)} %collective-permute-done.17.refs_1_), channel_id=1, source_target_pairs={{0,4},{4,8},{8,12},{12,14},{14,10},{10,6},{6,2},{2,0},{1,5},{5,9},... | collective-permute-start | bytes 3145736 | tf_op jit(solution)/shard_map/ppermute | solution.py:108
  142.7 44.2 %collective-permute-start.22 = (bf16[64,8192]{1,0:T(8,128)(2,1)}, bf16[64,8192]{1,0:T(8,128)(2,1)S(1)}, u32[]{:S(2)}, u32[]{:S(2)}) collective-permute-start(bf16[64,8192]{1,0:T(8,128)(2,1)} %collective-permute-done.18.refs_0_), channel_id=1, source_target_pairs={{4,0},{8,4},{12,8},{14,12},{10,14},{6,10},{2,6},{0,2},{5,1},{9,5},... | collective-permute-start | bytes 3145736 | tf_op jit(solution)/shard_map/ppermute | solution.py:108
  148.6 20.5 %copy-start.8 = (f32[128,1024]{1,0:T(8,128)}, f32[128,1024]{1,0:T(8,128)S(1)}, u32[]{:S(2)}) copy-start(f32[128,1024]{1,0:T(8,128)S(1)} %get-tuple-element.161.refs_4_) | copy-start | bytes 1572868
  164.4 40.8 %collective-permute-start.19 = (bf16[64,8192]{1,0:T(8,128)(2,1)S(1)}, bf16[64,8192]{1,0:T(8,128)(2,1)S(1)}, u32[]{:S(2)}, u32[]{:S(2)}) collective-permute-start(bf16[64,8192]{1,0:T(8,128)(2,1)S(1)} %collective-permute-done.15.refs_0_), channel_id=1, source_target_pairs={{0,4},{4,8},{8,12},{12,14},{14,10},{10,6},{6,2},{2,0},{1,5},{5,9},... | collective-permute-start | bytes 3145736 | tf_op jit(solution)/shard_map/ppermute | solution.py:108
  165.0 42.3 %collective-permute-start.20 = (bf16[64,8192]{1,0:T(8,128)(2,1)S(1)}, bf16[64,8192]{1,0:T(8,128)(2,1)S(1)}, u32[]{:S(2)}, u32[]{:S(2)}) collective-permute-start(bf16[64,8192]{1,0:T(8,128)(2,1)S(1)} %collective-permute-done.16.refs_1_), channel_id=1, source_target_pairs={{4,0},{8,4},{12,8},{14,12},{10,14},{6,10},{2,6},{0,2},{5,1},{9,5},... | collective-permute-start | bytes 3145736 | tf_op jit(solution)/shard_map/ppermute | solution.py:108
  169.1 50.9 %collective-permute-start.27 = (bf16[8,64,512]{2,1,0:T(8,128)(2,1)S(1)}, bf16[8,64,512]{2,1,0:T(8,128)(2,1)S(1)}, u32[]{:S(2)}, u32[]{:S(2)}) collective-permute-start(bf16[8,64,512]{2,1,0:T(8,128)(2,1)S(1)} %take.1.refs_12_), channel_id=1, source_target_pairs={{0,16},{16,0},{1,17},{17,1},{2,18},{18,2},{3,19},{19,3},{4,20},{20... | collective-permute-start | bytes 1572872 | tf_op jit(solution)/shard_map/ppermute | solution.py:112
  174.1 16.2 %copy-start.9 = (f32[128,1024]{1,0:T(8,128)}, f32[128,1024]{1,0:T(8,128)S(1)}, u32[]{:S(2)}) copy-start(f32[128,1024]{1,0:T(8,128)S(1)} %get-tuple-element.162.refs_5_) | copy-start | bytes 1572868
  190.3 0.8 copy-start.10
  210.7 0.8 copy-start.11
  211.5 3.9 %collective-permute-start.23 = (bf16[128,128]{1,0:T(8,128)(2,1)S(1)}, bf16[128,128]{1,0:T(8,128)(2,1)S(1)}, u32[]{:S(2)}, u32[]{:S(2)}) collective-permute-start(bf16[128,128]{1,0:T(8,128)(2,1)S(1)} %get-tuple-element.168), channel_id=1, source_target_pairs={{0,2},{2,0},{4,6},{6,4},{8,10},{10,8},{12,14},{14,12},{1,3},{3,1},... | collective-permute-start | bytes 98312 | tf_op jit(solution)/shard_map/ppermute | solution.py:108
  215.4 4.5 %collective-permute-start.24 = (bf16[2,128,128]{2,1,0:T(8,128)(2,1)S(1)}, bf16[2,128,128]{2,1,0:T(8,128)(2,1)S(1)}, u32[]{:S(2)}, u32[]{:S(2)}) collective-permute-start(bf16[2,128,128]{2,1,0:T(8,128)(2,1)S(1)} %pad_maximum_fusion.1.refs_8_), channel_id=1, source_target_pairs={{0,4},{2,6},{4,0},{6,2},{8,12},{10,14},{12,8},{14,10},{1,5},{3,7},... | collective-permute-start | bytes 196616 | tf_op jit(solution)/shard_map/ppermute | solution.py:108
  216.0 5.2 %collective-permute-start.25 = (bf16[2,128,128]{2,1,0:T(8,128)(2,1)S(1)}, bf16[2,128,128]{2,1,0:T(8,128)(2,1)S(1)}, u32[]{:S(2)}, u32[]{:S(2)}) collective-permute-start(bf16[2,128,128]{2,1,0:T(8,128)(2,1)S(1)} %pad_maximum_fusion.1.refs_8_), channel_id=1, source_target_pairs={{0,8},{2,10},{4,12},{6,14},{8,0},{10,2},{12,4},{14,6},{1,9},{3,11}... | collective-permute-start | bytes 196616 | tf_op jit(solution)/shard_map/ppermute | solution.py:108
  217.5 6.1 %collective-permute-start.26 = (bf16[2,128,128]{2,1,0:T(8,128)(2,1)S(1)}, bf16[2,128,128]{2,1,0:T(8,128)(2,1)S(1)}, u32[]{:S(2)}, u32[]{:S(2)}) collective-permute-start(bf16[2,128,128]{2,1,0:T(8,128)(2,1)S(1)} %pad_maximum_fusion.1.refs_8_), channel_id=1, source_target_pairs={{0,12},{2,14},{4,8},{6,10},{8,4},{10,6},{12,0},{14,2},{1,13},{3,15... | collective-permute-start | bytes 196616 | tf_op jit(solution)/shard_map/ppermute | solution.py:108
  (3 other events, 2.1 us)

commit v15 on v11

--- a/solution.py
+++ b/solution.py
@@ -189,7 +189,7 @@
     part = out.shape[3]
     for t in range(8):
         at = pl.multiple_of((2 * t + table[2]) * part, part)
-        out[t, 0] = up[0, :, pl.ds(at, part)]
+        out[0, t] = up[0, :, pl.ds(at, part)]
 
 
 def pack_call(table, up_maps):
@@ -201,9 +201,9 @@
             num_scalar_prefetch=1,
             grid=(2,),
             in_specs=[pl.BlockSpec((1, rank, width), lambda s, t: (t[s], 0, 0))],
-            out_specs=pl.BlockSpec((8, 1, rank, part), lambda s, t: (0, s, 0, 0)),
+            out_specs=pl.BlockSpec((1, 8, rank, part), lambda s, t: (s, 0, 0, 0)),
         ),
-        out_shape=jax.ShapeDtypeStruct((8, 2, rank, part), jnp.bfloat16),
+        out_shape=jax.ShapeDtypeStruct((2, 8, rank, part), jnp.bfloat16),
         name="pack",
         **settings(),
     )(table, pltpu.with_memory_space_constraint(up_maps, pltpu.HBM))
@@ -318,7 +318,9 @@
     down_lent = lax.dynamic_index_in_dim(adapter_down_maps, pick_lent, 0, keepdims=False)
     down_swapped = swap(down_lent, "store")
     weights = pin_call(query_weight, down_own, down_swapped)
-    up_sent = pack_call(jnp.concatenate([picked, group[None]]).astype(jnp.int32), adapter_up_maps)
+    choice = jnp.stack([pick_own, pick_lent, group.astype(pick_own.dtype)]).astype(jnp.int32)
+    up_sent = pack_call(choice, adapter_up_maps)
+    up_sent = jnp.stack([up_sent[0], swap(up_sent[1], "store")], axis=1)
 
     position = jnp.where(y == 0, z, 7 - z)
     places = []
@@ -342,13 +344,12 @@
         back.append(got_back)
         if k < 5:
             flight.append((send(ahead[k + 2], AHEAD), send(back[k + 2], BACK)))
+        if k == 5:
+            up_got = lax.all_to_all(up_sent, "tensor", split_axis=0, concat_axis=0, tiled=True)
         groups.append([got_ahead, got_back] if k % 2 == 0 else [got_back, got_ahead])
         for g in range(len(bases), min(len(bases) + 2, k + 2, 7)):
             base, shrunk = rows_call(g, table, weights, groups[g], shrunk)
             bases.append(base)
-    up_got = lax.all_to_all(
-        up_sent.reshape(16, rank, -1), ("tensor", "store"), split_axis=0, concat_axis=0, tiled=True
-    )
     base, shrunk = rows_call(7, table, weights, groups[7], shrunk)
     bases.append(base)
 
@@ -356,7 +357,9 @@
     pair = jnp.stack([shrunk, across])
     everyone = [pair] + [send(pair, pairs) for pairs in ALONG]
     up_got, _ = lax.optimization_barrier((up_got, across))
-    up_mine = take_call(owner_row, up_got)
+    home, core = owner_row // 2, owner_row % 2
+    chosen = 2 * home + jnp.where(core == store, 0, 1)
+    up_mine = take_call(chosen.astype(jnp.int32), up_got.reshape(16, rank, -1))
     up_other = swap(up_mine, "groups")
     home, core = owners // 2, owners % 2
     where = 2 * ((home // 2) ^ z) + ((home % 2) ^ y)

time: 215 us -> 223 us (1.037)
  local copies, waits for them, and re-layouts: 26 us -> 32.6 us
  waiting for transfers between devices: 109 us -> 103 us
  starting transfers between devices: 30.2 us -> 34.3 us
  other arithmetic: 0.64 us -> 3.99 us
    all_to_all x1, waiting for transfers between devices: 7.76 us -> 0.01 us  [chain_body(): lax.all_to_all(up_sent, 'tensor', split_axis=0, concat_axis=0, tiled=True)]
    unnamed x28 -> x44, local copies, waits for them, and re-layouts: 19.2 us -> 23.6 us
    another operation x0 -> x2, other arithmetic: none -> 3.41 us  [the longest x1 2.14 us: chain_body(): up_sent = jnp.stack([up_sent[0], swap(up_sent[1], 'store')], axis=1)]
    ppermute x18, starting transfers between devices: 23.7 us -> 26.7 us  [send(): return lax.ppermute(value, 'tensor', pairs)]
    ppermute x18, waiting for transfers between devices: 100 us -> 103 us  [send(): return lax.ppermute(value, 'tensor', pairs)]
  transfers between devices with their start and end apart: 21 -> 22, of which waited for: 15 -> 15; matrix products, arithmetic and copies ran while one was open for 2% -> 4% of each run, Pallas kernels for 18% -> 17%
where the time goes in v15:
time: 223 us; the launch traced here: 221 us
  waiting for transfers between devices  103 us (46%)
  Pallas kernels  43.6 us (20%)
  starting transfers between devices  34.3 us (15%)
  local copies, waits for them, and re-layouts  32.6 us (15%)
  between operations  4.03 us (2%)
  other arithmetic  3.99 us (2%)
    ppermute x18, waiting for transfers between devices, send(): return lax.ppermute(value, 'tensor', pairs)  103 us
    pallas_call x8, Pallas kernels, rows_call(): pl.pallas_call(functools.partial(rows_kernel, group), in_specs=[pl.BlockS...  32.8 us
    ppermute x18, starting transfers between devices, send(): return lax.ppermute(value, 'tensor', pairs)  26.7 us
    unnamed x44, local copies, waits for them, and re-layouts  23.6 us
    all_to_all x1, starting transfers between devices, chain_body(): lax.all_to_all(up_sent, 'tensor', split_axis=0, concat_axis=0, tiled=True)  5.52 us
    pallas_call x1, Pallas kernels, finish_call(): pl.pallas_call(finish_kernel, in_specs=[pl.BlockSpec(memory_space=pltpu.S...  5.24 us
  transfers between devices with their start and end apart: 22, of which 15 were waited for; matrix products, arithmetic and copies ran while one was open for 4% of the time, Pallas kernels for 17%

profile of v15, /device:TPU:0, one launch (start us, length us, event | category | flops | bytes accessed | tf_op | source)
XLA Modules:
  0.0 221.3 jit_solution(1190772340125290313)
XLA Ops:
  0.0 3.1 %slice_bitcast_fusion = (bf16[64,8192]{1,0:T(8,128)(2,1)}, bf16[64,8192]{1,0:T(8,128)(2,1)}) fusion(bf16[1,128,8192]{2,1,0:T(8,128)(2,1)} %param.6), kind=kLoop, calls=%fused_computation.3 | loop fusion | bytes 4194304 | tf_op jit(solution)/shard_map/slice | solution.py:298
  3.2 3.0 %collective-permute-start = (bf16[64,8192]{1,0:T(8,128)(2,1)}, bf16[64,8192]{1,0:T(8,128)(2,1)}, u32[]{:S(2)}, u32[]{:S(2)}) collective-permute-start(bf16[64,8192]{1,0:T(8,128)(2,1)} %get-tuple-element.148), channel_id=1, source_target_pairs={{0,4},{4,8},{8,12},{12,14},{14,10},{10,6},{6,2},{2,0},{1,5},{5,9},... | collective-permute-start | bytes 3145736 | tf_op jit(solution)/shard_map/ppermute | solution.py:108
  6.2 2.0 collective-permute-start.4
  8.2 22.2 %collective-permute-done.refs_0_ = bf16[64,8192]{1,0:T(8,128)(2,1)} collective-permute-done((bf16[64,8192]{1,0:T(8,128)(2,1)}, bf16[64,8192]{1,0:T(8,128)(2,1)}, u32[]{:S(2)}, u32[]{:S(2)}) %collective-permute-start) | collective-permute-done | bytes 1048608 | tf_op jit(solution)/shard_map/ppermute | solution.py:108
  30.4 2.2 collective-permute-done.1.refs_1_
  35.9 1.3 pad_add_fusion.table
  37.2 2.2 pack.1
  39.3 1.1 slice_bitcast_fusion.3
  41.6 2.7 %dynamic-slice_bitcast_fusion = (bf16[64,8192]{1,0:T(8,128)(2,1)}, bf16[64,8192]{1,0:T(8,128)(2,1)S(1)}) fusion(bf16[4,64,8192]{2,1,0:T(8,128)(2,1)} %param.8, s32[]{:T(128)S(6)} %select_n.166, s32[]{:T(128)S(6)} %select_n.165), kind=kLoop, calls=%fused_computation.1 | loop fusion | bytes 4194312 | tf_op jit(solution)/shard_map/jit(dynamic_index_in_dim)/squeeze | solution.py:318
  44.9 1.3 collective-permute-start.2
  47.0 2.1 pad_maximum_fusion
  49.1 3.7 %collective-permute-done.4.refs_1_ = bf16[64,8192]{1,0:T(8,128)(2,1)S(1)} collective-permute-done((bf16[64,8192]{1,0:T(8,128)(2,1)}, bf16[64,8192]{1,0:T(8,128)(2,1)S(1)}, u32[]{:S(2)}, u32[]{:S(2)}) %collective-permute-start.4) | collective-permute-done | bytes 1048608 | tf_op jit(solution)/shard_map/ppermute | solution.py:108
  52.8 2.3 %collective-permute-done.5.refs_0_ = bf16[64,8192]{1,0:T(8,128)(2,1)} collective-permute-done((bf16[64,8192]{1,0:T(8,128)(2,1)}, bf16[64,8192]{1,0:T(8,128)(2,1)}, u32[]{:S(2)}, u32[]{:S(2)}) %collective-permute-start.5) | collective-permute-done | bytes 1048608 | tf_op jit(solution)/shard_map/ppermute | solution.py:108
  55.0 1.6 collective-permute-start.10
  57.3 5.8 %copy-done.2 = bf16[8192,1024]{1,0:T(8,128)(2,1)S(1)} copy-done((bf16[8192,1024]{1,0:T(8,128)(2,1)S(1)}, bf16[8192,1024]{1,0:T(8,128)(2,1)}, u32[]{:S(2)}) %copy-start.2) | copy-done | bytes 16777240
  63.1 2.8 %pin.1.weights = bf16[8192,1152]{1,0:T(8,128)(2,1)S(1)} custom-call(bf16[8192,1024]{1,0:T(8,128)(2,1)S(1)} %copy-done.2, bf16[64,8192]{1,0:T(8,128)(2,1)S(1)} %get-tuple-element.146.own, bf16[64,8192]{1,0:T(8,128)(2,1)S(1)} %collective-permute-done.7.swapped), custom_call_target="tpu_custom_call" | custom-call | flops 1 | bytes 1 | tf_op jit(solution)/shard_map/pin/pallas_call | solution.py:138
  65.9 3.4 %rows.8 = (f32[128,1024]{1,0:T(8,128)S(1)}, bf16[128,128]{1,0:T(8,128)(2,1)S(1)}) custom-call(s32[2,16]{1,0:T(2,128)S(1)} %add_convert_fusion.table, bf16[8192,1152]{1,0:T(8,128)(2,1)S(1)} %pin.1.weights, bf16[128,8192]{1,0:T(8,128)(2,1)S(1)} %bitcast.62, bf16[128,128]{1,0:T(8,128)(2,1)S(1)} %broadcast_in_dim.49.refs_1_), custom_call_target="tpu_custom_call" | custom-call | flops 1 | bytes 1 | tf_op jit(solution)/shard_map/rows/pallas_call | solution.py:175
  69.4 1.5 copy-done.10
  70.9 6.0 %rows.9 = (f32[128,1024]{1,0:T(8,128)S(1)}, bf16[128,128]{1,0:T(8,128)(2,1)S(1)}) custom-call(s32[2,16]{1,0:T(2,128)S(1)} %add_convert_fusion.table, bf16[8192,1152]{1,0:T(8,128)(2,1)S(1)} %pin.1.weights, bf16[64,8192]{1,0:T(8,128)(2,1)} %collective-permute-done.refs_0_, bf16[64,8192]{1,0:T(8,128)(2,1)} %collective-permute-done.1.refs_1_, ...), custom_call_target="tpu_custom_call" | custom-call | flops 1 | bytes 1 | tf_op jit(solution)/shard_map/rows/pallas_call | solution.py:175
  77.6 1.6 collective-permute-start.8
  79.7 4.1 %rows.10 = (f32[128,1024]{1,0:T(8,128)S(1)}, bf16[128,128]{1,0:T(8,128)(2,1)S(1)}) custom-call(s32[2,16]{1,0:T(2,128)S(1)} %add_convert_fusion.table, bf16[8192,1152]{1,0:T(8,128)(2,1)S(1)} %pin.1.weights, bf16[64,8192]{1,0:T(8,128)(2,1)} %collective-permute-done.5.refs_0_, bf16[64,8192]{1,0:T(8,128)(2,1)S(1)} %collective-permute-done.4.refs_1_, ...), custom_call_target="tpu_custom_call" | custom-call | flops 1 | bytes 1 | tf_op jit(solution)/shard_map/rows/pallas_call | solution.py:175
  84.6 4.4 %rows.11 = (f32[128,1024]{1,0:T(8,128)S(1)}, bf16[128,128]{1,0:T(8,128)(2,1)S(1)}) custom-call(s32[2,16]{1,0:T(2,128)S(1)} %add_convert_fusion.table, bf16[8192,1152]{1,0:T(8,128)(2,1)S(1)} %pin.1.weights, bf16[64,8192]{1,0:T(8,128)(2,1)} %collective-permute-done.2.refs_0_, bf16[64,8192]{1,0:T(8,128)(2,1)} %collective-permute-done.3.refs_1_, ...), custom_call_target="tpu_custom_call" | custom-call | flops 1 | bytes 1 | tf_op jit(solution)/shard_map/rows/pallas_call | solution.py:175
  89.9 8.0 %collective-permute-done.10.refs_1_ = bf16[64,8192]{1,0:T(8,128)(2,1)} collective-permute-done((bf16[64,8192]{1,0:T(8,128)(2,1)S(1)}, bf16[64,8192]{1,0:T(8,128)(2,1)}, u32[]{:S(2)}, u32[]{:S(2)}) %collective-permute-start.10) | collective-permute-done | bytes 1048608 | tf_op jit(solution)/shard_map/ppermute | solution.py:108
  97.8 2.2 collective-permute-done.11.refs_0_
  100.0 1.6 collective-permute-start.14
  102.0 4.4 %rows.12 = (f32[128,1024]{1,0:T(8,128)S(1)}, bf16[128,128]{1,0:T(8,128)(2,1)S(1)}) custom-call(s32[2,16]{1,0:T(2,128)S(1)} %add_convert_fusion.table, bf16[8192,1152]{1,0:T(8,128)(2,1)S(1)} %pin.1.weights, bf16[64,8192]{1,0:T(8,128)(2,1)} %collective-permute-done.11.refs_0_, bf16[64,8192]{1,0:T(8,128)(2,1)} %collective-permute-done.10.refs_1_, ...), custom_call_target="tpu_custom_call" | custom-call | flops 1 | bytes 1 | tf_op jit(solution)/shard_map/rows/pallas_call | solution.py:175
  107.2 12.9 %collective-permute-done.8.refs_0_ = bf16[64,8192]{1,0:T(8,128)(2,1)S(1)} collective-permute-done((bf16[64,8192]{1,0:T(8,128)(2,1)}, bf16[64,8192]{1,0:T(8,128)(2,1)S(1)}, u32[]{:S(2)}, u32[]{:S(2)}) %collective-permute-start.8) | collective-permute-done | bytes 1048608 | tf_op jit(solution)/shard_map/ppermute | solution.py:108
  120.2 2.2 collective-permute-done.9.refs_1_
  122.4 3.5 %rows.13 = (f32[128,1024]{1,0:T(8,128)S(1)}, bf16[128,128]{1,0:T(8,128)(2,1)S(1)}) custom-call(s32[2,16]{1,0:T(2,128)S(1)} %add_convert_fusion.table, bf16[8192,1152]{1,0:T(8,128)(2,1)S(1)} %pin.1.weights, bf16[64,8192]{1,0:T(8,128)(2,1)S(1)} %collective-permute-done.8.refs_0_, bf16[64,8192]{1,0:T(8,128)(2,1)S(1)} %collective-permute-done.9.refs_1_, ...), custom_call_target="tpu_custom_call" | custom-call | flops 1 | bytes 1 | tf_op jit(solution)/shard_map/rows/pallas_call | solution.py:175
  126.7 15.2 %collective-permute-done.14.refs_1_ = bf16[64,8192]{1,0:T(8,128)(2,1)S(1)} collective-permute-done((bf16[64,8192]{1,0:T(8,128)(2,1)}, bf16[64,8192]{1,0:T(8,128)(2,1)S(1)}, u32[]{:S(2)}, u32[]{:S(2)}) %collective-permute-start.14) | collective-permute-done | bytes 1048608 | tf_op jit(solution)/shard_map/ppermute | solution.py:108
  141.8 1.0 copy-done.6
  144.3 1.1 copy.9
  145.4 5.5 %all-to-all-start = ((bf16[8,2,64,512]{3,2,1,0:T(8,128)(2,1)}), bf16[8,2,64,512]{3,2,1,0:T(8,128)(2,1)S(1)}, u32[]{:S(2)}, u32[]{:S(2)}) async-start(bf16[8,2,64,512]{3,2,1,0:T(8,128)(2,1)} %copy.9), calls=%async_computation | async-start | bytes 2097152 | tf_op jit(solution)/shard_map/all_to_all | solution.py:348
  151.0 2.0 collective-permute-start.12
  153.3 6.4 %copy-done.1 = bf16[8192,1152]{1,0:T(8,128)(2,1)S(1)} copy-done((bf16[8192,1152]{1,0:T(8,128)(2,1)S(1)}, bf16[8192,1152]{1,0:T(8,128)(2,1)}, u32[]{:S(2)}) %copy-start.1) | copy-done | bytes 18874392
  159.6 1.2 copy-done.7
  160.9 1.2 copy-done.9
  162.1 3.4 %rows.14 = (f32[128,1024]{1,0:T(8,128)S(1)}, bf16[128,128]{1,0:T(8,128)(2,1)S(1)}) custom-call(s32[2,16]{1,0:T(2,128)S(1)} %add_convert_fusion.table, bf16[8192,1152]{1,0:T(8,128)(2,1)S(1)} %copy-done.1, bf16[64,8192]{1,0:T(8,128)(2,1)S(1)} %copy-done.9, bf16[64,8192]{1,0:T(8,128)(2,1)S(1)} %copy-done.7, bf16[128,128]{1,0:T(8,128)(2,1)S(1)} %get-tuple-element.124.refs_2_), custom_call_target="tpu_custom_call" | custom-call | flops 1 | bytes 1 | tf_op jit(solution)/shard_map/rows/pallas_call | solution.py:175
  166.3 23.3 %collective-permute-done.12.refs_0_ = bf16[64,8192]{1,0:T(8,128)(2,1)S(1)} collective-permute-done((bf16[64,8192]{1,0:T(8,128)(2,1)S(1)}, bf16[64,8192]{1,0:T(8,128)(2,1)S(1)}, u32[]{:S(2)}, u32[]{:S(2)}) %collective-permute-start.12) | collective-permute-done | bytes 1048608 | tf_op jit(solution)/shard_map/ppermute | solution.py:108
  189.7 2.2 collective-permute-done.13.refs_1_
  191.8 3.4 %rows.15 = (f32[128,1024]{1,0:T(8,128)S(1)}, bf16[128,128]{1,0:T(8,128)(2,1)S(1)}) custom-call(s32[2,16]{1,0:T(2,128)S(1)} %add_convert_fusion.table, bf16[8192,1152]{1,0:T(8,128)(2,1)S(1)} %copy-done.1, bf16[64,8192]{1,0:T(8,128)(2,1)S(1)} %collective-permute-done.12.refs_0_, bf16[64,8192]{1,0:T(8,128)(2,1)S(1)} %collective-permute-done.13.refs_1_, ...), custom_call_target="tpu_custom_call" | custom-call | flops 1 | bytes 1 | tf_op jit(solution)/shard_map/rows/pallas_call | solution.py:175
  196.1 1.4 collective-permute-start.16
  197.7 2.3 %collective-permute-done.16 = bf16[128,128]{1,0:T(8,128)(2,1)S(1)} collective-permute-done((bf16[128,128]{1,0:T(8,128)(2,1)S(1)}, bf16[128,128]{1,0:T(8,128)(2,1)S(1)}, u32[]{:S(2)}, u32[]{:S(2)}) %collective-permute-start.16) | collective-permute-done | bytes 32800 | tf_op jit(solution)/shard_map/ppermute | solution.py:108
  200.7 1.6 collective-permute-start.20
  202.3 7.4 %collective-permute-start.17 = (bf16[2,128,128]{2,1,0:T(8,128)(2,1)S(1)}, bf16[2,128,128]{2,1,0:T(8,128)(2,1)S(1)}, u32[]{:S(2)}, u32[]{:S(2)}) collective-permute-start(bf16[2,128,128]{2,1,0:T(8,128)(2,1)S(1)} %pad_maximum_fusion.1.refs_8_), channel_id=1, source_target_pairs={{0,4},{2,6},{4,0},{6,2},{8,12},{10,14},{12,8},{14,10},{1,5},{3,7},... | collective-permute-start | bytes 196616 | tf_op jit(solution)/shard_map/ppermute | solution.py:108
  209.7 2.4 %collective-permute-start.19 = (bf16[2,128,128]{2,1,0:T(8,128)(2,1)S(1)}, bf16[2,128,128]{2,1,0:T(8,128)(2,1)S(1)}, u32[]{:S(2)}, u32[]{:S(2)}) collective-permute-start(bf16[2,128,128]{2,1,0:T(8,128)(2,1)S(1)} %pad_maximum_fusion.1.refs_8_), channel_id=1, source_target_pairs={{0,12},{2,14},{4,8},{6,10},{8,4},{10,6},{12,0},{14,2},{1,13},{3,15... | collective-permute-start | bytes 196616 | tf_op jit(solution)/shard_map/ppermute | solution.py:108
  212.2 2.9 %collective-permute-done.18.refs_10_ = bf16[2,128,128]{2,1,0:T(8,128)(2,1)S(1)} collective-permute-done((bf16[2,128,128]{2,1,0:T(8,128)(2,1)S(1)}, bf16[2,128,128]{2,1,0:T(8,128)(2,1)S(1)}, u32[]{:S(2)}, u32[]{:S(2)}) %collective-permute-start.18) | collective-permute-done | bytes 65568 | tf_op jit(solution)/shard_map/ppermute | solution.py:108
  215.8 5.2 %finish.1 = bf16[1024,1024]{1,0:T(8,128)(2,1)} custom-call(s32[4,16]{1,0:T(4,128)S(1)} %add_add_fusion.table, f32[128,1024]{1,0:T(8,128)} %copy-done.10, f32[128,1024]{1,0:T(8,128)} %copy-done.11, f32[128,1024]{1,0:T(8,128)} %copy-done.12, f32[128,1024]{1,0:T(8,128)} %copy-done.13, f32[128,1024]{1,0:T(8,128)} %copy-done.14, f32[128,1024]{1,0:T(8,128)} %copy-done.15, ...), custom_call_target="tpu_custom_call" | custom-call | flops 1 | bytes 1 | tf_op jit(solution)/shard_map/finish/pallas_call | solution.py:263
  (73 shorter events, 13.0 us)
Async XLA Ops:
  0.0 32.6 %copy-start.21 = (s32[64]{0:T(128)S(1)}, s32[64]{0:T(128)}, u32[]{:S(2)}) copy-start(s32[64]{0:T(128)} %param.10) | copy-start | bytes 772
  0.0 32.6 %copy-start.20 = (s32[2,8]{1,0:T(2,128)S(1)}, s32[2,8]{1,0:T(2,128)}, u32[]{:S(2)}) copy-start(s32[2,8]{1,0:T(2,128)} %param.11) | copy-start | bytes 196
  3.2 27.3 %collective-permute-start = (bf16[64,8192]{1,0:T(8,128)(2,1)}, bf16[64,8192]{1,0:T(8,128)(2,1)}, u32[]{:S(2)}, u32[]{:S(2)}) collective-permute-start(bf16[64,8192]{1,0:T(8,128)(2,1)} %get-tuple-element.148), channel_id=1, source_target_pairs={{0,4},{4,8},{8,12},{12,14},{14,10},{10,6},{6,2},{2,0},{1,5},{5,9},... | collective-permute-start | bytes 3145736 | tf_op jit(solution)/shard_map/ppermute | solution.py:108
  6.2 26.4 %collective-permute-start.1 = (bf16[64,8192]{1,0:T(8,128)(2,1)}, bf16[64,8192]{1,0:T(8,128)(2,1)}, u32[]{:S(2)}, u32[]{:S(2)}) collective-permute-start(bf16[64,8192]{1,0:T(8,128)(2,1)} %get-tuple-element.147), channel_id=1, source_target_pairs={{4,0},{8,4},{12,8},{14,12},{10,14},{6,10},{2,6},{0,2},{5,1},{9,5},... | collective-permute-start | bytes 3145736 | tf_op jit(solution)/shard_map/ppermute | solution.py:108
  6.2 46.6 %collective-permute-start.4 = (bf16[64,8192]{1,0:T(8,128)(2,1)}, bf16[64,8192]{1,0:T(8,128)(2,1)S(1)}, u32[]{:S(2)}, u32[]{:S(2)}) collective-permute-start(bf16[64,8192]{1,0:T(8,128)(2,1)} %get-tuple-element.147), channel_id=1, source_target_pairs={{0,4},{4,8},{8,12},{12,14},{14,10},{10,6},{6,2},{2,0},{1,5},{5,9},... | collective-permute-start | bytes 3145736 | tf_op jit(solution)/shard_map/ppermute | solution.py:108
  8.2 46.8 %collective-permute-start.5 = (bf16[64,8192]{1,0:T(8,128)(2,1)}, bf16[64,8192]{1,0:T(8,128)(2,1)}, u32[]{:S(2)}, u32[]{:S(2)}) collective-permute-start(bf16[64,8192]{1,0:T(8,128)(2,1)} %get-tuple-element.148), channel_id=1, source_target_pairs={{4,0},{8,4},{12,8},{14,12},{10,14},{6,10},{2,6},{0,2},{5,1},{9,5},... | collective-permute-start | bytes 3145736 | tf_op jit(solution)/shard_map/ppermute | solution.py:108
  40.4 5.8 %collective-permute-start.6 = (bf16[8,64,512]{2,1,0:T(8,128)(2,1)}, bf16[8,64,512]{2,1,0:T(8,128)(2,1)}, u32[]{:S(2)}, u32[]{:S(2)}) collective-permute-start(bf16[8,64,512]{2,1,0:T(8,128)(2,1)} %get-tuple-element.150), channel_id=1, source_target_pairs={{0,1},{1,0},{2,3},{3,2},{4,5},{5,4},{6,7},{7,6},{8,9},{9,8},{10,11... | collective-permute-start | bytes 1572872 | tf_op jit(solution)/shard_map/ppermute | solution.py:112
  41.6 5.3 %copy-start.19 = (bf16[8,1,64,512]{3,2,0,1:T(8,128)(2,1)S(1)}, bf16[8,1,64,512]{3,2,0,1:T(8,128)(2,1)}, u32[]{:S(2)}) copy-start(bf16[8,1,64,512]{3,2,0,1:T(8,128)(2,1)} %get-tuple-element.149) | copy-start | bytes 1572868
  44.4 12.9 %collective-permute-start.7 = (bf16[64,8192]{1,0:T(8,128)(2,1)}, bf16[64,8192]{1,0:T(8,128)(2,1)S(1)}, u32[]{:S(2)}, u32[]{:S(2)}) collective-permute-start(bf16[64,8192]{1,0:T(8,128)(2,1)} %get-tuple-element.145), channel_id=1, source_target_pairs={{0,1},{1,0},{2,3},{3,2},{4,5},{5,4},{6,7},{7,6},{8,9},{9,8},{10,11... | collective-permute-start | bytes 3145736 | tf_op jit(solution)/shard_map/ppermute | solution.py:112
  44.9 32.7 %collective-permute-start.2 = (bf16[64,8192]{1,0:T(8,128)(2,1)}, bf16[64,8192]{1,0:T(8,128)(2,1)}, u32[]{:S(2)}, u32[]{:S(2)}) collective-permute-start(bf16[64,8192]{1,0:T(8,128)(2,1)} %collective-permute-done.refs_0_), channel_id=1, source_target_pairs={{0,4},{4,8},{8,12},{12,14},{14,10},{10,6},{6,2},{2,0},{1,5},{5,9},... | collective-permute-start | bytes 3145736 | tf_op jit(solution)/shard_map/ppermute | solution.py:108
  46.3 31.4 %collective-permute-start.3 = (bf16[64,8192]{1,0:T(8,128)(2,1)}, bf16[64,8192]{1,0:T(8,128)(2,1)}, u32[]{:S(2)}, u32[]{:S(2)}) collective-permute-start(bf16[64,8192]{1,0:T(8,128)(2,1)} %collective-permute-done.1.refs_1_), channel_id=1, source_target_pairs={{4,0},{8,4},{12,8},{14,12},{10,14},{6,10},{2,6},{0,2},{5,1},{9,5},... | collective-permute-start | bytes 3145736 | tf_op jit(solution)/shard_map/ppermute | solution.py:108
  55.0 42.8 %collective-permute-start.10 = (bf16[64,8192]{1,0:T(8,128)(2,1)S(1)}, bf16[64,8192]{1,0:T(8,128)(2,1)}, u32[]{:S(2)}, u32[]{:S(2)}) collective-permute-start(bf16[64,8192]{1,0:T(8,128)(2,1)S(1)} %collective-permute-done.4.refs_1_), channel_id=1, source_target_pairs={{0,4},{4,8},{8,12},{12,14},{14,10},{10,6},{6,2},{2,0},{1,5},{5,9},... | collective-permute-start | bytes 3145736 | tf_op jit(solution)/shard_map/ppermute | solution.py:108
  56.6 43.4 %collective-permute-start.11 = (bf16[64,8192]{1,0:T(8,128)(2,1)}, bf16[64,8192]{1,0:T(8,128)(2,1)}, u32[]{:S(2)}, u32[]{:S(2)}) collective-permute-start(bf16[64,8192]{1,0:T(8,128)(2,1)} %collective-permute-done.5.refs_0_), channel_id=1, source_target_pairs={{4,0},{8,4},{12,8},{14,12},{10,14},{6,10},{2,6},{0,2},{5,1},{9,5},... | collective-permute-start | bytes 3145736 | tf_op jit(solution)/shard_map/ppermute | solution.py:108
  57.3 5.8 %copy-start.2 = (bf16[8192,1024]{1,0:T(8,128)(2,1)S(1)}, bf16[8192,1024]{1,0:T(8,128)(2,1)}, u32[]{:S(2)}) copy-start(bf16[8192,1024]{1,0:T(8,128)(2,1)} %weight.1) | copy-start | bytes 50331652
  63.1 2.8 %copy-start.3 = (bf16[1,128,8192]{2,1,0:T(8,128)(2,1)S(1)}, bf16[1,128,8192]{2,1,0:T(8,128)(2,1)}, u32[]{:S(2)}) copy-start(bf16[1,128,8192]{2,1,0:T(8,128)(2,1)} %param.6) | copy-start | bytes 6291460
  65.9 56.5 %copy-start = (bf16[8192,1152]{1,0:T(8,128)(2,1)}, bf16[8192,1152]{1,0:T(8,128)(2,1)S(1)}, u32[]{:S(2)}) copy-start(bf16[8192,1152]{1,0:T(8,128)(2,1)S(1)} %pin.1.weights) | copy-start | bytes 56623108
  69.4 1.5 copy-start.10
  76.8 0.8 copy-start.11
  77.6 42.6 %collective-permute-start.8 = (bf16[64,8192]{1,0:T(8,128)(2,1)}, bf16[64,8192]{1,0:T(8,128)(2,1)S(1)}, u32[]{:S(2)}, u32[]{:S(2)}) collective-permute-start(bf16[64,8192]{1,0:T(8,128)(2,1)} %collective-permute-done.2.refs_0_), channel_id=1, source_target_pairs={{0,4},{4,8},{8,12},{12,14},{14,10},{10,6},{6,2},{2,0},{1,5},{5,9},... | collective-permute-start | bytes 3145736 | tf_op jit(solution)/shard_map/ppermute | solution.py:108
  79.2 43.1 %collective-permute-start.9 = (bf16[64,8192]{1,0:T(8,128)(2,1)}, bf16[64,8192]{1,0:T(8,128)(2,1)S(1)}, u32[]{:S(2)}, u32[]{:S(2)}) collective-permute-start(bf16[64,8192]{1,0:T(8,128)(2,1)} %collective-permute-done.3.refs_1_), channel_id=1, source_target_pairs={{4,0},{8,4},{12,8},{14,12},{10,14},{6,10},{2,6},{0,2},{5,1},{9,5},... | collective-permute-start | bytes 3145736 | tf_op jit(solution)/shard_map/ppermute | solution.py:108
  83.8 0.8 copy-start.12
  89.0 0.8 copy-start.13
  100.0 41.9 %collective-permute-start.14 = (bf16[64,8192]{1,0:T(8,128)(2,1)}, bf16[64,8192]{1,0:T(8,128)(2,1)S(1)}, u32[]{:S(2)}, u32[]{:S(2)}) collective-permute-start(bf16[64,8192]{1,0:T(8,128)(2,1)} %collective-permute-done.10.refs_1_), channel_id=1, source_target_pairs={{0,4},{4,8},{8,12},{12,14},{14,10},{10,6},{6,2},{2,0},{1,5},{5,9},... | collective-permute-start | bytes 3145736 | tf_op jit(solution)/shard_map/ppermute | solution.py:108
  101.6 41.8 %collective-permute-start.15 = (bf16[64,8192]{1,0:T(8,128)(2,1)}, bf16[64,8192]{1,0:T(8,128)(2,1)S(1)}, u32[]{:S(2)}, u32[]{:S(2)}) collective-permute-start(bf16[64,8192]{1,0:T(8,128)(2,1)} %collective-permute-done.11.refs_0_), channel_id=1, source_target_pairs={{4,0},{8,4},{12,8},{14,12},{10,14},{6,10},{2,6},{0,2},{5,1},{9,5},... | collective-permute-start | bytes 3145736 | tf_op jit(solution)/shard_map/ppermute | solution.py:108
  106.5 0.8 copy-start.14
  122.4 3.5 %copy-start.4 = (bf16[64,8192]{1,0:T(8,128)(2,1)}, bf16[64,8192]{1,0:T(8,128)(2,1)S(1)}, u32[]{:S(2)}) copy-start(bf16[64,8192]{1,0:T(8,128)(2,1)S(1)} %collective-permute-done.9.refs_1_) | copy-start | bytes 3145732
  122.4 22.0 %copy-start.18 = (bf16[8,2,64,512]{3,2,0,1:T(8,128)(2,1)S(1)}, bf16[8,2,64,512]{3,2,0,1:T(8,128)(2,1)}, u32[]{:S(2)}) copy-start(bf16[8,2,64,512]{3,2,0,1:T(8,128)(2,1)} %pad_maximum_fusion) | copy-start | bytes 3145732
  125.9 0.8 copy-start.15
  141.8 1.0 copy-start.6
  142.8 10.2 %copy-start.5 = (bf16[64,8192]{1,0:T(8,128)(2,1)S(1)}, bf16[64,8192]{1,0:T(8,128)(2,1)}, u32[]{:S(2)}) copy-start(bf16[64,8192]{1,0:T(8,128)(2,1)} %copy-done.4) | copy-start | bytes 3145732
  143.4 1.0 copy-start.8
  145.4 54.6 %all-to-all-start = ((bf16[8,2,64,512]{3,2,1,0:T(8,128)(2,1)}), bf16[8,2,64,512]{3,2,1,0:T(8,128)(2,1)S(1)}, u32[]{:S(2)}, u32[]{:S(2)}) async-start(bf16[8,2,64,512]{3,2,1,0:T(8,128)(2,1)} %copy.9), calls=%async_computation | async-start | bytes 2097152 | tf_op jit(solution)/shard_map/all_to_all | solution.py:348
  151.0 38.7 %collective-permute-start.12 = (bf16[64,8192]{1,0:T(8,128)(2,1)S(1)}, bf16[64,8192]{1,0:T(8,128)(2,1)S(1)}, u32[]{:S(2)}, u32[]{:S(2)}) collective-permute-start(bf16[64,8192]{1,0:T(8,128)(2,1)S(1)} %collective-permute-done.8.refs_0_), channel_id=1, source_target_pairs={{0,4},{4,8},{8,12},{12,14},{14,10},{10,6},{6,2},{2,0},{1,5},{5,9},... | collective-permute-start | bytes 3145736 | tf_op jit(solution)/shard_map/ppermute | solution.py:108
  153.0 38.8 %collective-permute-start.13 = (bf16[64,8192]{1,0:T(8,128)(2,1)S(1)}, bf16[64,8192]{1,0:T(8,128)(2,1)S(1)}, u32[]{:S(2)}, u32[]{:S(2)}) collective-permute-start(bf16[64,8192]{1,0:T(8,128)(2,1)S(1)} %copy-done.5), channel_id=1, source_target_pairs={{4,0},{8,4},{12,8},{14,12},{10,14},{6,10},{2,6},{0,2},{5,1},{9,5},... | collective-permute-start | bytes 3145736 | tf_op jit(solution)/shard_map/ppermute | solution.py:108
  153.3 6.4 %copy-start.1 = (bf16[8192,1152]{1,0:T(8,128)(2,1)S(1)}, bf16[8192,1152]{1,0:T(8,128)(2,1)}, u32[]{:S(2)}) copy-start(bf16[8192,1152]{1,0:T(8,128)(2,1)} %copy-done) | copy-start | bytes 56623108
  159.6 1.2 copy-start.7
  160.9 1.2 copy-start.9
  165.5 0.8 copy-start.16
  195.2 0.8 copy-start.17
  196.1 3.9 %collective-permute-start.16 = (bf16[128,128]{1,0:T(8,128)(2,1)S(1)}, bf16[128,128]{1,0:T(8,128)(2,1)S(1)}, u32[]{:S(2)}, u32[]{:S(2)}) collective-permute-start(bf16[128,128]{1,0:T(8,128)(2,1)S(1)} %get-tuple-element.139), channel_id=1, source_target_pairs={{0,2},{2,0},{4,6},{6,4},{8,10},{10,8},{12,14},{14,12},{1,3},{3,1},... | collective-permute-start | bytes 98312 | tf_op jit(solution)/shard_map/ppermute | solution.py:108
  200.7 15.1 %collective-permute-start.20 = (bf16[8,64,512]{2,1,0:T(8,128)(2,1)S(1)}, bf16[8,64,512]{2,1,0:T(8,128)(2,1)S(1)}, u32[]{:S(2)}, u32[]{:S(2)}) collective-permute-start(bf16[8,64,512]{2,1,0:T(8,128)(2,1)S(1)} %take.1.refs_12_), channel_id=1, source_target_pairs={{0,16},{16,0},{1,17},{17,1},{2,18},{18,2},{3,19},{19,3},{4,20},{20... | collective-permute-start | bytes 1572872 | tf_op jit(solution)/shard_map/ppermute | solution.py:112
  202.3 9.9 %collective-permute-start.17 = (bf16[2,128,128]{2,1,0:T(8,128)(2,1)S(1)}, bf16[2,128,128]{2,1,0:T(8,128)(2,1)S(1)}, u32[]{:S(2)}, u32[]{:S(2)}) collective-permute-start(bf16[2,128,128]{2,1,0:T(8,128)(2,1)S(1)} %pad_maximum_fusion.1.refs_8_), channel_id=1, source_target_pairs={{0,4},{2,6},{4,0},{6,2},{8,12},{10,14},{12,8},{14,10},{1,5},{3,7},... | collective-permute-start | bytes 196616 | tf_op jit(solution)/shard_map/ppermute | solution.py:108
  209.7 5.4 %collective-permute-start.18 = (bf16[2,128,128]{2,1,0:T(8,128)(2,1)S(1)}, bf16[2,128,128]{2,1,0:T(8,128)(2,1)S(1)}, u32[]{:S(2)}, u32[]{:S(2)}) collective-permute-start(bf16[2,128,128]{2,1,0:T(8,128)(2,1)S(1)} %pad_maximum_fusion.1.refs_8_), channel_id=1, source_target_pairs={{0,8},{2,10},{4,12},{6,14},{8,0},{10,2},{12,4},{14,6},{1,9},{3,11}... | collective-permute-start | bytes 196616 | tf_op jit(solution)/shard_map/ppermute | solution.py:108
  209.7 6.2 %collective-permute-start.19 = (bf16[2,128,128]{2,1,0:T(8,128)(2,1)S(1)}, bf16[2,128,128]{2,1,0:T(8,128)(2,1)S(1)}, u32[]{:S(2)}, u32[]{:S(2)}) collective-permute-start(bf16[2,128,128]{2,1,0:T(8,128)(2,1)S(1)} %pad_maximum_fusion.1.refs_8_), channel_id=1, source_target_pairs={{0,12},{2,14},{4,8},{6,10},{8,4},{10,6},{12,0},{14,2},{1,13},{3,15... | collective-permute-start | bytes 196616 | tf_op jit(solution)/shard_map/ppermute | solution.py:108

commit v16 on v15

--- a/solution.py
+++ b/solution.py
@@ -112,10 +112,10 @@
     return lax.ppermute(value, axis, [(0, 1), (1, 0)])
 
 
-def settings():
+def settings(flops=1):
     return dict(
         compiler_params=pltpu.CompilerParams(vmem_limit_bytes=VMEM_LIMIT),
-        cost_estimate=pl.CostEstimate(flops=1, bytes_accessed=1, transcendentals=0),
+        cost_estimate=pl.CostEstimate(flops=flops, bytes_accessed=1, transcendentals=0),
     )
 
 
@@ -181,7 +181,7 @@
             jax.ShapeDtypeStruct((BLOCK, 128), jnp.bfloat16),
         ],
         name="rows",
-        **settings(),
+        **settings(flops=10**11 if group == 7 else 1),
     )(table, *operands)
 
 

time: 223 us -> 208 us (0.933)
  starting transfers between devices: 34.3 us -> 28 us
  waiting for transfers between devices: 103 us -> 96.7 us
    ppermute x18, waiting for transfers between devices: 103 us -> 81.2 us  [send(): return lax.ppermute(value, 'tensor', pairs)]
    all_to_all x1, waiting for transfers between devices: 0.01 us -> 12.7 us  [chain_body(): lax.all_to_all(up_sent, 'tensor', split_axis=0, concat_axis=0, tiled=True)]
    ppermute x18, starting transfers between devices: 26.7 us -> 21 us  [send(): return lax.ppermute(value, 'tensor', pairs)]
    ppermute x3, waiting for transfers between devices: 0.01 us -> 2.78 us  [swap(): return lax.ppermute(value, axis, [(0, 1), (1, 0)])]
    unnamed x44 -> x38, local copies, waits for them, and re-layouts: 23.6 us -> 21.5 us
  transfers between devices with their start and end apart: 22 -> 22, of which waited for: 15 -> 18; matrix products, arithmetic and copies ran while one was open for 4% -> 5% of each run, Pallas kernels for 17% -> 18%
where the time goes in v16:
time: 208 us
  waiting for transfers between devices  96.7 us (46%)
  Pallas kernels  44.3 us (21%)
  local copies, waits for them, and re-layouts  30.4 us (15%)
  starting transfers between devices  28 us (13%)
  between operations  4.45 us (2%)
  other arithmetic  3.82 us (2%)
    ppermute x18, waiting for transfers between devices, send(): return lax.ppermute(value, 'tensor', pairs)  81.2 us
    pallas_call x8, Pallas kernels, rows_call(): pl.pallas_call(functools.partial(rows_kernel, group), in_specs=[pl.BlockS...  33.4 us
    unnamed x38, local copies, waits for them, and re-layouts  21.5 us
    ppermute x18, starting transfers between devices, send(): return lax.ppermute(value, 'tensor', pairs)  21 us
    all_to_all x1, waiting for transfers between devices, chain_body(): lax.all_to_all(up_sent, 'tensor', split_axis=0, concat_axis=0, tiled=True)  12.7 us
    pallas_call x1, Pallas kernels, finish_call(): pl.pallas_call(finish_kernel, in_specs=[pl.BlockSpec(memory_space=pltpu.S...  5.23 us
    all_to_all x1, starting transfers between devices, chain_body(): lax.all_to_all(up_sent, 'tensor', split_axis=0, concat_axis=0, tiled=True)  4.82 us
  transfers between devices with their start and end apart: 22, of which 18 were waited for; matrix products, arithmetic and copies ran while one was open for 5% of the time, Pallas kernels for 18%

profile of v16, /device:TPU:0, one launch (start us, length us, event | category | flops | bytes accessed | tf_op | source)
XLA Modules:
  0.0 207.6 jit_solution(10627256950942126780)
XLA Ops:
  0.0 3.1 %slice_bitcast_fusion = (bf16[64,8192]{1,0:T(8,128)(2,1)}, bf16[64,8192]{1,0:T(8,128)(2,1)}) fusion(bf16[1,128,8192]{2,1,0:T(8,128)(2,1)} %param.6), kind=kLoop, calls=%fused_computation.3 | loop fusion | bytes 4194304 | tf_op jit(solution)/shard_map/slice | solution.py:298
  3.1 3.0 %collective-permute-start = (bf16[64,8192]{1,0:T(8,128)(2,1)}, bf16[64,8192]{1,0:T(8,128)(2,1)}, u32[]{:S(2)}, u32[]{:S(2)}) collective-permute-start(bf16[64,8192]{1,0:T(8,128)(2,1)} %get-tuple-element.148), channel_id=1, source_target_pairs={{0,4},{4,8},{8,12},{12,14},{14,10},{10,6},{6,2},{2,0},{1,5},{5,9},... | collective-permute-start | bytes 3145736 | tf_op jit(solution)/shard_map/ppermute | solution.py:108
  6.1 2.0 collective-permute-start.4
  8.1 22.2 %collective-permute-done.refs_0_ = bf16[64,8192]{1,0:T(8,128)(2,1)} collective-permute-done((bf16[64,8192]{1,0:T(8,128)(2,1)}, bf16[64,8192]{1,0:T(8,128)(2,1)}, u32[]{:S(2)}, u32[]{:S(2)}) %collective-permute-start) | collective-permute-done | bytes 1048608 | tf_op jit(solution)/shard_map/ppermute | solution.py:108
  30.4 2.2 %collective-permute-done.1.refs_1_ = bf16[64,8192]{1,0:T(8,128)(2,1)} collective-permute-done((bf16[64,8192]{1,0:T(8,128)(2,1)}, bf16[64,8192]{1,0:T(8,128)(2,1)}, u32[]{:S(2)}, u32[]{:S(2)}) %collective-permute-start.1) | collective-permute-done | bytes 1048608 | tf_op jit(solution)/shard_map/ppermute | solution.py:108
  36.2 1.4 pad_add_fusion.table
  37.6 2.2 %pack.1 = bf16[2,8,64,512]{3,2,1,0:T(8,128)(2,1)S(1)} custom-call(s32[3]{0:T(128)S(1)} %pad_add_fusion.table, bf16[4,64,8192]{2,1,0:T(8,128)(2,1)} %up.1), custom_call_target="tpu_custom_call" | custom-call | flops 1 | bytes 1 | tf_op jit(solution)/shard_map/pack/pallas_call | solution.py:198
  42.2 2.7 %dynamic-slice_bitcast_fusion = (bf16[64,8192]{1,0:T(8,128)(2,1)}, bf16[64,8192]{1,0:T(8,128)(2,1)S(1)}) fusion(bf16[4,64,8192]{2,1,0:T(8,128)(2,1)} %param.8, s32[]{:T(128)S(6)} %select_n.166, s32[]{:T(128)S(6)} %select_n.165), kind=kLoop, calls=%fused_computation.1 | loop fusion | bytes 4194312 | tf_op jit(solution)/shard_map/jit(dynamic_index_in_dim)/squeeze | solution.py:318
  45.5 1.5 collective-permute-start.2
  48.3 1.3 pad_maximum_fusion
  49.6 3.1 %collective-permute-done.4.refs_1_ = bf16[64,8192]{1,0:T(8,128)(2,1)S(1)} collective-permute-done((bf16[64,8192]{1,0:T(8,128)(2,1)}, bf16[64,8192]{1,0:T(8,128)(2,1)S(1)}, u32[]{:S(2)}, u32[]{:S(2)}) %collective-permute-start.4) | collective-permute-done | bytes 1048608 | tf_op jit(solution)/shard_map/ppermute | solution.py:108
  52.7 2.3 %collective-permute-done.5.refs_0_ = bf16[64,8192]{1,0:T(8,128)(2,1)} collective-permute-done((bf16[64,8192]{1,0:T(8,128)(2,1)}, bf16[64,8192]{1,0:T(8,128)(2,1)}, u32[]{:S(2)}, u32[]{:S(2)}) %collective-permute-start.5) | collective-permute-done | bytes 1048608 | tf_op jit(solution)/shard_map/ppermute | solution.py:108
  55.0 1.6 collective-permute-start.10
  57.0 5.8 %copy-done.2 = bf16[8192,1024]{1,0:T(8,128)(2,1)S(1)} copy-done((bf16[8192,1024]{1,0:T(8,128)(2,1)S(1)}, bf16[8192,1024]{1,0:T(8,128)(2,1)}, u32[]{:S(2)}) %copy-start.2) | copy-done | bytes 16777240
  62.8 2.8 %pin.1.weights = bf16[8192,1152]{1,0:T(8,128)(2,1)S(1)} custom-call(bf16[8192,1024]{1,0:T(8,128)(2,1)S(1)} %copy-done.2, bf16[64,8192]{1,0:T(8,128)(2,1)S(1)} %get-tuple-element.146.own, bf16[64,8192]{1,0:T(8,128)(2,1)S(1)} %collective-permute-done.7.swapped), custom_call_target="tpu_custom_call" | custom-call | flops 1 | bytes 1 | tf_op jit(solution)/shard_map/pin/pallas_call | solution.py:138
  65.6 3.4 %rows.8 = (f32[128,1024]{1,0:T(8,128)S(1)}, bf16[128,128]{1,0:T(8,128)(2,1)S(1)}) custom-call(s32[2,16]{1,0:T(2,128)S(1)} %add_convert_fusion.table, bf16[8192,1152]{1,0:T(8,128)(2,1)S(1)} %pin.1.weights, bf16[128,8192]{1,0:T(8,128)(2,1)S(1)} %bitcast.62, bf16[128,128]{1,0:T(8,128)(2,1)S(1)} %broadcast_in_dim.49.refs_1_), custom_call_target="tpu_custom_call" | custom-call | flops 1 | bytes 1 | tf_op jit(solution)/shard_map/rows/pallas_call | solution.py:175
  69.0 1.6 copy-done.6
  70.6 5.9 %rows.9 = (f32[128,1024]{1,0:T(8,128)S(1)}, bf16[128,128]{1,0:T(8,128)(2,1)S(1)}) custom-call(s32[2,16]{1,0:T(2,128)S(1)} %add_convert_fusion.table, bf16[8192,1152]{1,0:T(8,128)(2,1)S(1)} %pin.1.weights, bf16[64,8192]{1,0:T(8,128)(2,1)} %collective-permute-done.refs_0_, bf16[64,8192]{1,0:T(8,128)(2,1)} %collective-permute-done.1.refs_1_, ...), custom_call_target="tpu_custom_call" | custom-call | flops 1 | bytes 1 | tf_op jit(solution)/shard_map/rows/pallas_call | solution.py:175
  77.5 1.6 collective-permute-start.8
  79.5 4.1 %rows.10 = (f32[128,1024]{1,0:T(8,128)S(1)}, bf16[128,128]{1,0:T(8,128)(2,1)S(1)}) custom-call(s32[2,16]{1,0:T(2,128)S(1)} %add_convert_fusion.table, bf16[8192,1152]{1,0:T(8,128)(2,1)S(1)} %pin.1.weights, bf16[64,8192]{1,0:T(8,128)(2,1)} %collective-permute-done.5.refs_0_, bf16[64,8192]{1,0:T(8,128)(2,1)S(1)} %collective-permute-done.4.refs_1_, ...), custom_call_target="tpu_custom_call" | custom-call | flops 1 | bytes 1 | tf_op jit(solution)/shard_map/rows/pallas_call | solution.py:175
  84.4 4.4 %rows.11 = (f32[128,1024]{1,0:T(8,128)S(1)}, bf16[128,128]{1,0:T(8,128)(2,1)S(1)}) custom-call(s32[2,16]{1,0:T(2,128)S(1)} %add_convert_fusion.table, bf16[8192,1152]{1,0:T(8,128)(2,1)S(1)} %pin.1.weights, bf16[64,8192]{1,0:T(8,128)(2,1)} %collective-permute-done.2.refs_0_, bf16[64,8192]{1,0:T(8,128)(2,1)} %collective-permute-done.3.refs_1_, ...), custom_call_target="tpu_custom_call" | custom-call | flops 1 | bytes 1 | tf_op jit(solution)/shard_map/rows/pallas_call | solution.py:175
  89.7 8.0 %collective-permute-done.10.refs_1_ = bf16[64,8192]{1,0:T(8,128)(2,1)S(1)} collective-permute-done((bf16[64,8192]{1,0:T(8,128)(2,1)S(1)}, bf16[64,8192]{1,0:T(8,128)(2,1)S(1)}, u32[]{:S(2)}, u32[]{:S(2)}) %collective-permute-start.10) | collective-permute-done | bytes 1048608 | tf_op jit(solution)/shard_map/ppermute | solution.py:108
  97.7 2.2 %collective-permute-done.11.refs_0_ = bf16[64,8192]{1,0:T(8,128)(2,1)S(1)} collective-permute-done((bf16[64,8192]{1,0:T(8,128)(2,1)}, bf16[64,8192]{1,0:T(8,128)(2,1)S(1)}, u32[]{:S(2)}, u32[]{:S(2)}) %collective-permute-start.11) | collective-permute-done | bytes 1048608 | tf_op jit(solution)/shard_map/ppermute | solution.py:108
  99.8 1.6 collective-permute-start.14
  101.8 3.4 %rows.12 = (f32[128,1024]{1,0:T(8,128)S(1)}, bf16[128,128]{1,0:T(8,128)(2,1)S(1)}) custom-call(s32[2,16]{1,0:T(2,128)S(1)} %add_convert_fusion.table, bf16[8192,1152]{1,0:T(8,128)(2,1)S(1)} %pin.1.weights, bf16[64,8192]{1,0:T(8,128)(2,1)S(1)} %collective-permute-done.11.refs_0_, bf16[64,8192]{1,0:T(8,128)(2,1)S(1)} %collective-permute-done.10.refs_1_, ...), custom_call_target="tpu_custom_call" | custom-call | flops 1 | bytes 1 | tf_op jit(solution)/shard_map/rows/pallas_call | solution.py:175
  106.1 14.0 %collective-permute-done.8.refs_0_ = bf16[64,8192]{1,0:T(8,128)(2,1)S(1)} collective-permute-done((bf16[64,8192]{1,0:T(8,128)(2,1)}, bf16[64,8192]{1,0:T(8,128)(2,1)S(1)}, u32[]{:S(2)}, u32[]{:S(2)}) %collective-permute-start.8) | collective-permute-done | bytes 1048608 | tf_op jit(solution)/shard_map/ppermute | solution.py:108
  120.1 2.3 %collective-permute-done.9.refs_1_ = bf16[64,8192]{1,0:T(8,128)(2,1)} collective-permute-done((bf16[64,8192]{1,0:T(8,128)(2,1)}, bf16[64,8192]{1,0:T(8,128)(2,1)}, u32[]{:S(2)}, u32[]{:S(2)}) %collective-permute-start.9) | collective-permute-done | bytes 1048608 | tf_op jit(solution)/shard_map/ppermute | solution.py:108
  122.4 1.6 collective-permute-start.12
  124.4 4.2 %rows.13 = (f32[128,1024]{1,0:T(8,128)S(1)}, bf16[128,128]{1,0:T(8,128)(2,1)S(1)}) custom-call(s32[2,16]{1,0:T(2,128)S(1)} %add_convert_fusion.table, bf16[8192,1152]{1,0:T(8,128)(2,1)S(1)} %pin.1.weights, bf16[64,8192]{1,0:T(8,128)(2,1)S(1)} %collective-permute-done.8.refs_0_, bf16[64,8192]{1,0:T(8,128)(2,1)} %collective-permute-done.9.refs_1_, ...), custom_call_target="tpu_custom_call" | custom-call | flops 1 | bytes 1 | tf_op jit(solution)/shard_map/rows/pallas_call | solution.py:175
  129.4 13.2 %collective-permute-done.14.refs_1_ = bf16[64,8192]{1,0:T(8,128)(2,1)S(1)} collective-permute-done((bf16[64,8192]{1,0:T(8,128)(2,1)S(1)}, bf16[64,8192]{1,0:T(8,128)(2,1)S(1)}, u32[]{:S(2)}, u32[]{:S(2)}) %collective-permute-start.14) | collective-permute-done | bytes 1048608 | tf_op jit(solution)/shard_map/ppermute | solution.py:108
  142.6 2.2 %collective-permute-done.15.refs_0_ = bf16[64,8192]{1,0:T(8,128)(2,1)S(1)} collective-permute-done((bf16[64,8192]{1,0:T(8,128)(2,1)S(1)}, bf16[64,8192]{1,0:T(8,128)(2,1)S(1)}, u32[]{:S(2)}, u32[]{:S(2)}) %collective-permute-start.15) | collective-permute-done | bytes 1048608 | tf_op jit(solution)/shard_map/ppermute | solution.py:108
  146.8 4.8 %all-to-all-start = ((bf16[8,2,64,512]{3,2,1,0:T(8,128)(2,1)}), bf16[8,2,64,512]{3,2,1,0:T(8,128)(2,1)S(1)}, u32[]{:S(2)}, u32[]{:S(2)}) async-start(bf16[8,2,64,512]{3,2,1,0:T(8,128)(2,1)} %copy.9), calls=%async_computation | async-start | bytes 2097152 | tf_op jit(solution)/shard_map/all_to_all | solution.py:348
  151.6 6.4 %copy-done.1 = bf16[8192,1152]{1,0:T(8,128)(2,1)S(1)} copy-done((bf16[8192,1152]{1,0:T(8,128)(2,1)S(1)}, bf16[8192,1152]{1,0:T(8,128)(2,1)}, u32[]{:S(2)}) %copy-start.1) | copy-done | bytes 18874392
  158.0 1.2 copy-done.5
  159.2 3.5 %rows.14 = (f32[128,1024]{1,0:T(8,128)S(1)}, bf16[128,128]{1,0:T(8,128)(2,1)S(1)}) custom-call(s32[2,16]{1,0:T(2,128)S(1)} %add_convert_fusion.table, bf16[8192,1152]{1,0:T(8,128)(2,1)S(1)} %copy-done.1, bf16[64,8192]{1,0:T(8,128)(2,1)S(1)} %copy-done.5, bf16[64,8192]{1,0:T(8,128)(2,1)S(1)} %collective-permute-done.14.refs_1_, ...), custom_call_target="tpu_custom_call" | custom-call | flops 1 | bytes 1 | tf_op jit(solution)/shard_map/rows/pallas_call | solution.py:175
  163.5 1.7 collective-permute-done.12.refs_0_
  165.2 2.2 %collective-permute-done.13.refs_1_ = bf16[64,8192]{1,0:T(8,128)(2,1)} collective-permute-done((bf16[64,8192]{1,0:T(8,128)(2,1)}, bf16[64,8192]{1,0:T(8,128)(2,1)}, u32[]{:S(2)}, u32[]{:S(2)}) %collective-permute-start.13) | collective-permute-done | bytes 1048608 | tf_op jit(solution)/shard_map/ppermute | solution.py:108
  167.3 4.4 %rows.15 = (f32[128,1024]{1,0:T(8,128)S(1)}, bf16[128,128]{1,0:T(8,128)(2,1)S(1)}) custom-call(s32[2,16]{1,0:T(2,128)S(1)} %add_convert_fusion.table, bf16[8192,1152]{1,0:T(8,128)(2,1)S(1)} %copy-done.1, bf16[64,8192]{1,0:T(8,128)(2,1)} %collective-permute-done.12.refs_0_, bf16[64,8192]{1,0:T(8,128)(2,1)} %collective-permute-done.13.refs_1_, ...), custom_call_target="tpu_custom_call" | custom-call | flops 99999997952 | bytes 1 | tf_op jit(solution)/shard_map/rows/pallas_call | solution.py:175
  172.6 1.4 collective-permute-start.16
  174.1 2.4 %collective-permute-done.16 = bf16[128,128]{1,0:T(8,128)(2,1)S(1)} collective-permute-done((bf16[128,128]{1,0:T(8,128)(2,1)S(1)}, bf16[128,128]{1,0:T(8,128)(2,1)S(1)}, u32[]{:S(2)}, u32[]{:S(2)}) %collective-permute-start.16) | collective-permute-done | bytes 32800 | tf_op jit(solution)/shard_map/ppermute | solution.py:108
  176.6 12.7 %all-to-all-done = bf16[8,2,64,512]{3,2,1,0:T(8,128)(2,1)S(1)} async-done(((bf16[8,2,64,512]{3,2,1,0:T(8,128)(2,1)}), bf16[8,2,64,512]{3,2,1,0:T(8,128)(2,1)S(1)}, u32[]{:S(2)}, u32[]{:S(2)}) %all-to-all-start) | async-done | bytes 1048608 | tf_op jit(solution)/shard_map/all_to_all | solution.py:348
  190.0 1.6 collective-permute-start.20
  191.6 1.7 collective-permute-start.18
  193.4 2.6 %collective-permute-start.19 = (bf16[2,128,128]{2,1,0:T(8,128)(2,1)S(1)}, bf16[2,128,128]{2,1,0:T(8,128)(2,1)S(1)}, u32[]{:S(2)}, u32[]{:S(2)}) collective-permute-start(bf16[2,128,128]{2,1,0:T(8,128)(2,1)S(1)} %pad_maximum_fusion.1.refs_8_), channel_id=1, source_target_pairs={{0,12},{2,14},{4,8},{6,10},{8,4},{10,6},{12,0},{14,2},{1,13},{3,15... | collective-permute-start | bytes 196616 | tf_op jit(solution)/shard_map/ppermute | solution.py:108
  196.1 1.2 collective-permute-done.18.refs_10_
  197.3 2.1 %collective-permute-done.19.refs_11_ = bf16[2,128,128]{2,1,0:T(8,128)(2,1)S(1)} collective-permute-done((bf16[2,128,128]{2,1,0:T(8,128)(2,1)S(1)}, bf16[2,128,128]{2,1,0:T(8,128)(2,1)S(1)}, u32[]{:S(2)}, u32[]{:S(2)}) %collective-permute-start.19) | collective-permute-done | bytes 65568 | tf_op jit(solution)/shard_map/ppermute | solution.py:108
  199.4 2.8 %collective-permute-done.20.refs_13_ = bf16[8,64,512]{2,1,0:T(8,128)(2,1)S(1)} collective-permute-done((bf16[8,64,512]{2,1,0:T(8,128)(2,1)S(1)}, bf16[8,64,512]{2,1,0:T(8,128)(2,1)S(1)}, u32[]{:S(2)}, u32[]{:S(2)}) %collective-permute-start.20) | collective-permute-done | bytes 524320 | tf_op jit(solution)/shard_map/ppermute | solution.py:112
  202.2 5.2 %finish.1 = bf16[1024,1024]{1,0:T(8,128)(2,1)} custom-call(s32[4,16]{1,0:T(4,128)S(1)} %add_add_fusion.table, f32[128,1024]{1,0:T(8,128)} %copy-done.6, f32[128,1024]{1,0:T(8,128)} %copy-done.7, f32[128,1024]{1,0:T(8,128)} %copy-done.8, f32[128,1024]{1,0:T(8,128)} %copy-done.9, f32[128,1024]{1,0:T(8,128)} %copy-done.10, f32[128,1024]{1,0:T(8,128)} %copy-done.11, ...), custom_call_target="tpu_custom_call" | custom-call | flops 1 | bytes 1 | tf_op jit(solution)/shard_map/finish/pallas_call | solution.py:263
  (67 shorter events, 14.7 us)
Async XLA Ops:
  0.0 32.5 %copy-start.18 = (s32[64]{0:T(128)S(1)}, s32[64]{0:T(128)}, u32[]{:S(2)}) copy-start(s32[64]{0:T(128)} %param.10) | copy-start | bytes 772
  0.0 32.5 %copy-start.17 = (s32[2,8]{1,0:T(2,128)S(1)}, s32[2,8]{1,0:T(2,128)}, u32[]{:S(2)}) copy-start(s32[2,8]{1,0:T(2,128)} %param.11) | copy-start | bytes 196
  3.1 27.3 %collective-permute-start = (bf16[64,8192]{1,0:T(8,128)(2,1)}, bf16[64,8192]{1,0:T(8,128)(2,1)}, u32[]{:S(2)}, u32[]{:S(2)}) collective-permute-start(bf16[64,8192]{1,0:T(8,128)(2,1)} %get-tuple-element.148), channel_id=1, source_target_pairs={{0,4},{4,8},{8,12},{12,14},{14,10},{10,6},{6,2},{2,0},{1,5},{5,9},... | collective-permute-start | bytes 3145736 | tf_op jit(solution)/shard_map/ppermute | solution.py:108
  6.1 26.4 %collective-permute-start.1 = (bf16[64,8192]{1,0:T(8,128)(2,1)}, bf16[64,8192]{1,0:T(8,128)(2,1)}, u32[]{:S(2)}, u32[]{:S(2)}) collective-permute-start(bf16[64,8192]{1,0:T(8,128)(2,1)} %get-tuple-element.147), channel_id=1, source_target_pairs={{4,0},{8,4},{12,8},{14,12},{10,14},{6,10},{2,6},{0,2},{5,1},{9,5},... | collective-permute-start | bytes 3145736 | tf_op jit(solution)/shard_map/ppermute | solution.py:108
  6.1 46.6 %collective-permute-start.4 = (bf16[64,8192]{1,0:T(8,128)(2,1)}, bf16[64,8192]{1,0:T(8,128)(2,1)S(1)}, u32[]{:S(2)}, u32[]{:S(2)}) collective-permute-start(bf16[64,8192]{1,0:T(8,128)(2,1)} %get-tuple-element.147), channel_id=1, source_target_pairs={{0,4},{4,8},{8,12},{12,14},{14,10},{10,6},{6,2},{2,0},{1,5},{5,9},... | collective-permute-start | bytes 3145736 | tf_op jit(solution)/shard_map/ppermute | solution.py:108
  8.1 46.8 %collective-permute-start.5 = (bf16[64,8192]{1,0:T(8,128)(2,1)}, bf16[64,8192]{1,0:T(8,128)(2,1)}, u32[]{:S(2)}, u32[]{:S(2)}) collective-permute-start(bf16[64,8192]{1,0:T(8,128)(2,1)} %get-tuple-element.148), channel_id=1, source_target_pairs={{4,0},{8,4},{12,8},{14,12},{10,14},{6,10},{2,6},{0,2},{5,1},{9,5},... | collective-permute-start | bytes 3145736 | tf_op jit(solution)/shard_map/ppermute | solution.py:108
  40.9 6.1 %collective-permute-start.6 = (bf16[8,64,512]{2,1,0:T(8,128)(2,1)}, bf16[8,64,512]{2,1,0:T(8,128)(2,1)}, u32[]{:S(2)}, u32[]{:S(2)}) collective-permute-start(bf16[8,64,512]{2,1,0:T(8,128)(2,1)} %get-tuple-element.150), channel_id=1, source_target_pairs={{0,1},{1,0},{2,3},{3,2},{4,5},{5,4},{6,7},{7,6},{8,9},{9,8},{10,11... | collective-permute-start | bytes 1572872 | tf_op jit(solution)/shard_map/ppermute | solution.py:112
  44.9 12.1 %collective-permute-start.7 = (bf16[64,8192]{1,0:T(8,128)(2,1)}, bf16[64,8192]{1,0:T(8,128)(2,1)S(1)}, u32[]{:S(2)}, u32[]{:S(2)}) collective-permute-start(bf16[64,8192]{1,0:T(8,128)(2,1)} %get-tuple-element.145), channel_id=1, source_target_pairs={{0,1},{1,0},{2,3},{3,2},{4,5},{5,4},{6,7},{7,6},{8,9},{9,8},{10,11... | collective-permute-start | bytes 3145736 | tf_op jit(solution)/shard_map/ppermute | solution.py:112
  45.5 31.8 %collective-permute-start.2 = (bf16[64,8192]{1,0:T(8,128)(2,1)}, bf16[64,8192]{1,0:T(8,128)(2,1)}, u32[]{:S(2)}, u32[]{:S(2)}) collective-permute-start(bf16[64,8192]{1,0:T(8,128)(2,1)} %collective-permute-done.refs_0_), channel_id=1, source_target_pairs={{0,4},{4,8},{8,12},{12,14},{14,10},{10,6},{6,2},{2,0},{1,5},{5,9},... | collective-permute-start | bytes 3145736 | tf_op jit(solution)/shard_map/ppermute | solution.py:108
  47.0 30.4 %collective-permute-start.3 = (bf16[64,8192]{1,0:T(8,128)(2,1)}, bf16[64,8192]{1,0:T(8,128)(2,1)}, u32[]{:S(2)}, u32[]{:S(2)}) collective-permute-start(bf16[64,8192]{1,0:T(8,128)(2,1)} %collective-permute-done.1.refs_1_), channel_id=1, source_target_pairs={{4,0},{8,4},{12,8},{14,12},{10,14},{6,10},{2,6},{0,2},{5,1},{9,5},... | collective-permute-start | bytes 3145736 | tf_op jit(solution)/shard_map/ppermute | solution.py:108
  47.8 0.6 copy-start.14
  55.0 42.7 %collective-permute-start.10 = (bf16[64,8192]{1,0:T(8,128)(2,1)S(1)}, bf16[64,8192]{1,0:T(8,128)(2,1)S(1)}, u32[]{:S(2)}, u32[]{:S(2)}) collective-permute-start(bf16[64,8192]{1,0:T(8,128)(2,1)S(1)} %collective-permute-done.4.refs_1_), channel_id=1, source_target_pairs={{0,4},{4,8},{8,12},{12,14},{14,10},{10,6},{6,2},{2,0},{1,5},{5,9},... | collective-permute-start | bytes 3145736 | tf_op jit(solution)/shard_map/ppermute | solution.py:108
  56.6 43.3 %collective-permute-start.11 = (bf16[64,8192]{1,0:T(8,128)(2,1)}, bf16[64,8192]{1,0:T(8,128)(2,1)S(1)}, u32[]{:S(2)}, u32[]{:S(2)}) collective-permute-start(bf16[64,8192]{1,0:T(8,128)(2,1)} %collective-permute-done.5.refs_0_), channel_id=1, source_target_pairs={{4,0},{8,4},{12,8},{14,12},{10,14},{6,10},{2,6},{0,2},{5,1},{9,5},... | collective-permute-start | bytes 3145736 | tf_op jit(solution)/shard_map/ppermute | solution.py:108
  57.0 5.8 %copy-start.2 = (bf16[8192,1024]{1,0:T(8,128)(2,1)S(1)}, bf16[8192,1024]{1,0:T(8,128)(2,1)}, u32[]{:S(2)}) copy-start(bf16[8192,1024]{1,0:T(8,128)(2,1)} %weight.1) | copy-start | bytes 50331652
  62.8 2.8 %copy-start.3 = (bf16[1,128,8192]{2,1,0:T(8,128)(2,1)S(1)}, bf16[1,128,8192]{2,1,0:T(8,128)(2,1)}, u32[]{:S(2)}) copy-start(bf16[1,128,8192]{2,1,0:T(8,128)(2,1)} %param.6) | copy-start | bytes 6291460
  65.6 58.9 %copy-start = (bf16[8192,1152]{1,0:T(8,128)(2,1)}, bf16[8192,1152]{1,0:T(8,128)(2,1)S(1)}, u32[]{:S(2)}) copy-start(bf16[8192,1152]{1,0:T(8,128)(2,1)S(1)} %pin.1.weights) | copy-start | bytes 56623108
  69.0 1.6 copy-start.6
  76.5 0.8 copy-start.7
  77.5 42.7 %collective-permute-start.8 = (bf16[64,8192]{1,0:T(8,128)(2,1)}, bf16[64,8192]{1,0:T(8,128)(2,1)S(1)}, u32[]{:S(2)}, u32[]{:S(2)}) collective-permute-start(bf16[64,8192]{1,0:T(8,128)(2,1)} %collective-permute-done.2.refs_0_), channel_id=1, source_target_pairs={{0,4},{4,8},{8,12},{12,14},{14,10},{10,6},{6,2},{2,0},{1,5},{5,9},... | collective-permute-start | bytes 3145736 | tf_op jit(solution)/shard_map/ppermute | solution.py:108
  79.0 43.4 %collective-permute-start.9 = (bf16[64,8192]{1,0:T(8,128)(2,1)}, bf16[64,8192]{1,0:T(8,128)(2,1)}, u32[]{:S(2)}, u32[]{:S(2)}) collective-permute-start(bf16[64,8192]{1,0:T(8,128)(2,1)} %collective-permute-done.3.refs_1_), channel_id=1, source_target_pairs={{4,0},{8,4},{12,8},{14,12},{10,14},{6,10},{2,6},{0,2},{5,1},{9,5},... | collective-permute-start | bytes 3145736 | tf_op jit(solution)/shard_map/ppermute | solution.py:108
  83.6 0.8 copy-start.8
  88.9 0.8 copy-start.9
  99.8 42.8 %collective-permute-start.14 = (bf16[64,8192]{1,0:T(8,128)(2,1)S(1)}, bf16[64,8192]{1,0:T(8,128)(2,1)S(1)}, u32[]{:S(2)}, u32[]{:S(2)}) collective-permute-start(bf16[64,8192]{1,0:T(8,128)(2,1)S(1)} %collective-permute-done.10.refs_1_), channel_id=1, source_target_pairs={{0,4},{4,8},{8,12},{12,14},{14,10},{10,6},{6,2},{2,0},{1,5},{5,9},... | collective-permute-start | bytes 3145736 | tf_op jit(solution)/shard_map/ppermute | solution.py:108
  101.4 43.4 %collective-permute-start.15 = (bf16[64,8192]{1,0:T(8,128)(2,1)S(1)}, bf16[64,8192]{1,0:T(8,128)(2,1)S(1)}, u32[]{:S(2)}, u32[]{:S(2)}) collective-permute-start(bf16[64,8192]{1,0:T(8,128)(2,1)S(1)} %collective-permute-done.11.refs_0_), channel_id=1, source_target_pairs={{4,0},{8,4},{12,8},{14,12},{10,14},{6,10},{2,6},{0,2},{5,1},{9,5},... | collective-permute-start | bytes 3145736 | tf_op jit(solution)/shard_map/ppermute | solution.py:108
  105.3 0.8 copy-start.10
  122.4 42.8 %collective-permute-start.12 = (bf16[64,8192]{1,0:T(8,128)(2,1)S(1)}, bf16[64,8192]{1,0:T(8,128)(2,1)}, u32[]{:S(2)}, u32[]{:S(2)}) collective-permute-start(bf16[64,8192]{1,0:T(8,128)(2,1)S(1)} %collective-permute-done.8.refs_0_), channel_id=1, source_target_pairs={{0,4},{4,8},{8,12},{12,14},{14,10},{10,6},{6,2},{2,0},{1,5},{5,9},... | collective-permute-start | bytes 3145736 | tf_op jit(solution)/shard_map/ppermute | solution.py:108
  124.0 43.4 %collective-permute-start.13 = (bf16[64,8192]{1,0:T(8,128)(2,1)}, bf16[64,8192]{1,0:T(8,128)(2,1)}, u32[]{:S(2)}, u32[]{:S(2)}) collective-permute-start(bf16[64,8192]{1,0:T(8,128)(2,1)} %collective-permute-done.9.refs_1_), channel_id=1, source_target_pairs={{4,0},{8,4},{12,8},{14,12},{10,14},{6,10},{2,6},{0,2},{5,1},{9,5},... | collective-permute-start | bytes 3145736 | tf_op jit(solution)/shard_map/ppermute | solution.py:108
  128.6 0.8 copy-start.11
  144.8 1.0 copy-start.4
  146.8 42.5 %all-to-all-start = ((bf16[8,2,64,512]{3,2,1,0:T(8,128)(2,1)}), bf16[8,2,64,512]{3,2,1,0:T(8,128)(2,1)S(1)}, u32[]{:S(2)}, u32[]{:S(2)}) async-start(bf16[8,2,64,512]{3,2,1,0:T(8,128)(2,1)} %copy.9), calls=%async_computation | async-start | bytes 2097152 | tf_op jit(solution)/shard_map/all_to_all | solution.py:348
  151.6 6.4 %copy-start.1 = (bf16[8192,1152]{1,0:T(8,128)(2,1)S(1)}, bf16[8192,1152]{1,0:T(8,128)(2,1)}, u32[]{:S(2)}) copy-start(bf16[8192,1152]{1,0:T(8,128)(2,1)} %copy-done) | copy-start | bytes 56623108
  158.0 1.2 copy-start.5
  162.7 0.8 copy-start.12
  167.3 24.2 %copy-start.15 = (s32[16]{0:T(128)S(1)}, s32[16]{0:T(128)}, u32[]{:S(2)}) copy-start(s32[16]{0:T(128)} %copy-done.14) | copy-start | bytes 196
  167.3 28.7 %copy-start.16 = (s32[1,16]{1,0:T(1,128)S(1)}, s32[1,16]{1,0:T(1,128)}, u32[]{:S(2)}) copy-start(s32[1,16]{1,0:T(1,128)} %get-tuple-element.153) | copy-start | bytes 196
  171.8 0.8 copy-start.13
  172.6 4.0 %collective-permute-start.16 = (bf16[128,128]{1,0:T(8,128)(2,1)S(1)}, bf16[128,128]{1,0:T(8,128)(2,1)S(1)}, u32[]{:S(2)}, u32[]{:S(2)}) collective-permute-start(bf16[128,128]{1,0:T(8,128)(2,1)S(1)} %get-tuple-element.139), channel_id=1, source_target_pairs={{0,2},{2,0},{4,6},{6,4},{8,10},{10,8},{12,14},{14,12},{1,3},{3,1},... | collective-permute-start | bytes 98312 | tf_op jit(solution)/shard_map/ppermute | solution.py:108
  190.0 12.2 %collective-permute-start.20 = (bf16[8,64,512]{2,1,0:T(8,128)(2,1)S(1)}, bf16[8,64,512]{2,1,0:T(8,128)(2,1)S(1)}, u32[]{:S(2)}, u32[]{:S(2)}) collective-permute-start(bf16[8,64,512]{2,1,0:T(8,128)(2,1)S(1)} %take.1.refs_12_), channel_id=1, source_target_pairs={{0,16},{16,0},{1,17},{17,1},{2,18},{18,2},{3,19},{19,3},{4,20},{20... | collective-permute-start | bytes 1572872 | tf_op jit(solution)/shard_map/ppermute | solution.py:112
  191.6 4.5 %collective-permute-start.17 = (bf16[2,128,128]{2,1,0:T(8,128)(2,1)S(1)}, bf16[2,128,128]{2,1,0:T(8,128)(2,1)S(1)}, u32[]{:S(2)}, u32[]{:S(2)}) collective-permute-start(bf16[2,128,128]{2,1,0:T(8,128)(2,1)S(1)} %pad_maximum_fusion.1.refs_8_), channel_id=1, source_target_pairs={{0,4},{2,6},{4,0},{6,2},{8,12},{10,14},{12,8},{14,10},{1,5},{3,7},... | collective-permute-start | bytes 196616 | tf_op jit(solution)/shard_map/ppermute | solution.py:108
  191.6 5.7 %collective-permute-start.18 = (bf16[2,128,128]{2,1,0:T(8,128)(2,1)S(1)}, bf16[2,128,128]{2,1,0:T(8,128)(2,1)S(1)}, u32[]{:S(2)}, u32[]{:S(2)}) collective-permute-start(bf16[2,128,128]{2,1,0:T(8,128)(2,1)S(1)} %pad_maximum_fusion.1.refs_8_), channel_id=1, source_target_pairs={{0,8},{2,10},{4,12},{6,14},{8,0},{10,2},{12,4},{14,6},{1,9},{3,11}... | collective-permute-start | bytes 196616 | tf_op jit(solution)/shard_map/ppermute | solution.py:108
  193.4 6.1 %collective-permute-start.19 = (bf16[2,128,128]{2,1,0:T(8,128)(2,1)S(1)}, bf16[2,128,128]{2,1,0:T(8,128)(2,1)S(1)}, u32[]{:S(2)}, u32[]{:S(2)}) collective-permute-start(bf16[2,128,128]{2,1,0:T(8,128)(2,1)S(1)} %pad_maximum_fusion.1.refs_8_), channel_id=1, source_target_pairs={{0,12},{2,14},{4,8},{6,10},{8,4},{10,6},{12,0},{14,2},{1,13},{3,15... | collective-permute-start | bytes 196616 | tf_op jit(solution)/shard_map/ppermute | solution.py:108

commit v17 on v16

--- a/solution.py
+++ b/solution.py
@@ -229,27 +229,44 @@
     )(table, got)
 
 
-def finish_kernel(table, *refs):
-    bases, gathered, refs = refs[:8], refs[8:12], refs[12:]
-    up_mine, up_other, out, base, shrunk, rows, base_sems, sems = refs
-    part = up_mine.shape[2]
+def collect_kernel(*refs):
+    *bases, out, sems = refs
+    copies = [pltpu.make_async_copy(bases[g], out.at[g], sems.at[g]) for g in range(8)]
+    for copy in copies:
+        copy.start()
+    for copy in copies:
+        copy.wait()
+
+
+def collect_call(bases):
+    return pl.pallas_call(
+        collect_kernel,
+        in_specs=[pl.BlockSpec(memory_space=pl.ANY)] * 8,
+        out_specs=in_vmem(1)[0],
+        out_shape=pltpu.VMEM((8,) + bases[0].shape, jnp.float32),
+        scratch_shapes=[pltpu.SemaphoreType.DMA((8,))],
+        name="collect",
+        **settings(),
+    )(*[pltpu.with_memory_space_constraint(base, pltpu.HBM) for base in bases])
+
+
+def finish_kernel(table, base, *refs):
+    gathered, (mine_a, mine_b, other_a, other_b) = refs[:4], refs[4:8]
+    out, shrunk, rows, sems = refs[8:]
+    part = mine_a.shape[2]
     group = table[3, 0]
-    fetches = [pltpu.make_async_copy(bases[g], base.at[g], base_sems.at[g]) for g in range(8)]
-    for fetch in fetches:
-        fetch.start()
     for i, pair in enumerate(gathered):
         shrunk[pl.ds(2 * i, 2)] = pair[...]
     copies = []
     for i in range(16):
         block, half = table[0, i], i % 2
-        if half == 0:
-            fetches[i // 2].wait()
         own = pl.ds(half * HALF, HALF)
         both = shrunk[table[1, i], own, :].astype(jnp.float32)
         value = jnp.where(table[2, i] > 0, both[:, 64:], both[:, :64]).astype(jnp.bfloat16)
-        for up, side in ((up_mine, group), (up_other, 1 - group)):
+        for up, side in (((mine_a, mine_b), group), ((other_a, other_b), 1 - group)):
             cut = pl.ds(pl.multiple_of(side * part, part), part)
-            grown = jnp.dot(value, up[block], preferred_element_type=jnp.float32)
+            up = jnp.concatenate([up[0][block], up[1][block]], axis=0)
+            grown = jnp.dot(value, up, preferred_element_type=jnp.float32)
             rows[i, :, cut] = (base[i // 2, own, cut] + 0.5 * grown).astype(rows.dtype)
         to = pl.ds(pl.multiple_of((2 * block + half) * HALF, HALF), HALF)
         copies.append(pltpu.make_async_copy(rows.at[i], out.at[to], sems.at[i]))
@@ -258,31 +275,21 @@
         copy.wait()
 
 
-def finish_call(table, bases, gathered, up_mine, up_other):
-    columns = bases[0].shape[1]
+def finish_call(table, base, gathered, ups):
+    columns = base.shape[2]
     return pl.pallas_call(
         finish_kernel,
-        in_specs=[pl.BlockSpec(memory_space=pltpu.SMEM)]
-        + [pl.BlockSpec(memory_space=pl.ANY)] * 8
-        + in_vmem(6),
+        in_specs=[pl.BlockSpec(memory_space=pltpu.SMEM)] + in_vmem(9),
         out_specs=pl.BlockSpec(memory_space=pltpu.HBM),
         out_shape=jax.ShapeDtypeStruct((8 * BLOCK, columns), jnp.bfloat16),
         scratch_shapes=[
-            pltpu.VMEM((8, BLOCK, columns), jnp.float32),
             pltpu.VMEM((8,) + gathered[0].shape[1:], jnp.bfloat16),
             pltpu.VMEM((16, HALF, columns), jnp.bfloat16),
-            pltpu.SemaphoreType.DMA((8,)),
             pltpu.SemaphoreType.DMA((16,)),
         ],
         name="finish",
         **settings(),
-    )(
-        table,
-        *[pltpu.with_memory_space_constraint(base, pltpu.HBM) for base in bases],
-        *gathered,
-        up_mine,
-        up_other,
-    )
+    )(table, pltpu.with_memory_space_constraint(base, pltpu.VMEM), *gathered, *ups)
 
 
 def chain_body(
@@ -321,6 +328,7 @@
     choice = jnp.stack([pick_own, pick_lent, group.astype(pick_own.dtype)]).astype(jnp.int32)
     up_sent = pack_call(choice, adapter_up_maps)
     up_sent = jnp.stack([up_sent[0], swap(up_sent[1], "store")], axis=1)
+    up_sent = [up_sent[:, :, : rank // 2], up_sent[:, :, rank // 2 :]]
 
     position = jnp.where(y == 0, z, 7 - z)
     places = []
@@ -345,7 +353,10 @@
         if k < 5:
             flight.append((send(ahead[k + 2], AHEAD), send(back[k + 2], BACK)))
         if k == 5:
-            up_got = lax.all_to_all(up_sent, "tensor", split_axis=0, concat_axis=0, tiled=True)
+            up_got = [
+                lax.all_to_all(sent, "tensor", split_axis=0, concat_axis=0, tiled=True)
+                for sent in up_sent
+            ]
         groups.append([got_ahead, got_back] if k % 2 == 0 else [got_back, got_ahead])
         for g in range(len(bases), min(len(bases) + 2, k + 2, 7)):
             base, shrunk = rows_call(g, table, weights, groups[g], shrunk)
@@ -353,18 +364,25 @@
     base, shrunk = rows_call(7, table, weights, groups[7], shrunk)
     bases.append(base)
 
-    across = send(shrunk, ACROSS)
-    pair = jnp.stack([shrunk, across])
+    pair = jnp.stack([shrunk, send(shrunk, ACROSS)])
     everyone = [pair] + [send(pair, pairs) for pairs in ALONG]
-    up_got, _ = lax.optimization_barrier((up_got, across))
+    base = collect_call(bases)
+    up_got[0], everyone, base = lax.optimization_barrier((up_got[0], everyone, base))
     home, core = owner_row // 2, owner_row % 2
-    chosen = 2 * home + jnp.where(core == store, 0, 1)
-    up_mine = take_call(chosen.astype(jnp.int32), up_got.reshape(16, rank, -1))
-    up_other = swap(up_mine, "groups")
+    chosen = (2 * home + jnp.where(core == store, 0, 1)).astype(jnp.int32)
+
+    def take(got):
+        return take_call(chosen, got.reshape(16, rank // 2, -1))
+
+    mine = [take(up_got[0])]
+    other = [swap(mine[0], "groups")]
+    up_got[1], _ = lax.optimization_barrier((up_got[1], mine[0]))
+    mine.append(take(up_got[1]))
+    other.append(swap(mine[1], "groups"))
     home, core = owners // 2, owners % 2
     where = 2 * ((home // 2) ^ z) + ((home % 2) ^ y)
     table = jnp.stack([blocks, where, core != store, jnp.broadcast_to(group, (16,))])
-    return finish_call(table.astype(jnp.int32), bases, everyone, up_mine, up_other)[None]
+    return finish_call(table.astype(jnp.int32), base, everyone, mine + other)[None]
 
 
 def body(tokens, *rest):

time: 208 us -> 223 us (1.072)
  local copies, waits for them, and re-layouts: 30.4 us -> 39.9 us
  starting transfers between devices: 28 us -> 32.8 us
    unnamed x38 -> x50, local copies, waits for them, and re-layouts: 21.5 us -> 30.3 us
    all_to_all x1 -> x2, starting transfers between devices: 4.82 us -> 8.4 us  [chain_body(): lax.all_to_all(sent, 'tensor', split_axis=0, concat_axis=0, tiled=True)]
    ppermute x3 -> x4, waiting for transfers between devices: 2.78 us -> 6.29 us  [swap(): return lax.ppermute(value, axis, [(0, 1), (1, 0)])]
    pallas_call x1, Pallas kernels: 5.23 us -> 2.33 us  [finish_call(): pl.pallas_call(finish_kernel, in_specs=[pl.BlockSpec(memory_space=pltpu.S...]
    ppermute x18, waiting for transfers between devices: 81.2 us -> 78.5 us  [send(): return lax.ppermute(value, 'tensor', pairs)]
    all_to_all x1 -> x2, waiting for transfers between devices: 12.7 us -> 10.7 us  [chain_body(): lax.all_to_all(sent, 'tensor', split_axis=0, concat_axis=0, tiled=True)]
  transfers between devices with their start and end apart: 22 -> 24, of which waited for: 18 -> 16; matrix products, arithmetic and copies ran while one was open for 5% -> 5% of each run, Pallas kernels for 18% -> 19%
where the time goes in v17:
time: 223 us; the launch traced here: 222 us
  waiting for transfers between devices  95.6 us (43%)
  Pallas kernels  45.5 us (20%)
  local copies, waits for them, and re-layouts  39.9 us (18%)
  starting transfers between devices  32.8 us (15%)
  other arithmetic  4.46 us (2%)
  between operations  4.1 us (2%)
    ppermute x18, waiting for transfers between devices, send(): return lax.ppermute(value, 'tensor', pairs)  78.5 us
    pallas_call x8, Pallas kernels, rows_call(): pl.pallas_call(functools.partial(rows_kernel, group), in_specs=[pl.BlockS...  34.7 us
    unnamed x50, local copies, waits for them, and re-layouts  30.3 us
    ppermute x18, starting transfers between devices, send(): return lax.ppermute(value, 'tensor', pairs)  21.7 us
    all_to_all x2, waiting for transfers between devices, chain_body(): lax.all_to_all(sent, 'tensor', split_axis=0, concat_axis=0, tiled=True)  10.7 us
    all_to_all x2, starting transfers between devices, chain_body(): lax.all_to_all(sent, 'tensor', split_axis=0, concat_axis=0, tiled=True)  8.4 us
    ppermute x4, waiting for transfers between devices, swap(): return lax.ppermute(value, axis, [(0, 1), (1, 0)])  6.29 us
  transfers between devices with their start and end apart: 24, of which 16 were waited for; matrix products, arithmetic and copies ran while one was open for 5% of the time, Pallas kernels for 19%

profile of v17, /device:TPU:0, one launch (start us, length us, event | category | flops | bytes accessed | tf_op | source)
XLA Modules:
  0.0 222.3 jit_solution(15735075352589769780)
XLA Ops:
  0.0 3.1 %slice_bitcast_fusion = (bf16[64,8192]{1,0:T(8,128)(2,1)}, bf16[64,8192]{1,0:T(8,128)(2,1)}) fusion(bf16[1,128,8192]{2,1,0:T(8,128)(2,1)} %param.6), kind=kLoop, calls=%fused_computation.4 | loop fusion | bytes 4194304 | tf_op jit(solution)/shard_map/slice | solution.py:305
  3.1 3.0 %collective-permute-start = (bf16[64,8192]{1,0:T(8,128)(2,1)}, bf16[64,8192]{1,0:T(8,128)(2,1)}, u32[]{:S(2)}, u32[]{:S(2)}) collective-permute-start(bf16[64,8192]{1,0:T(8,128)(2,1)} %get-tuple-element.170), channel_id=1, source_target_pairs={{0,4},{4,8},{8,12},{12,14},{14,10},{10,6},{6,2},{2,0},{1,5},{5,9},... | collective-permute-start | bytes 3145736 | tf_op jit(solution)/shard_map/ppermute | solution.py:108
  6.1 2.0 collective-permute-start.2
  8.2 22.2 %collective-permute-done.refs_0_ = bf16[64,8192]{1,0:T(8,128)(2,1)} collective-permute-done((bf16[64,8192]{1,0:T(8,128)(2,1)}, bf16[64,8192]{1,0:T(8,128)(2,1)}, u32[]{:S(2)}, u32[]{:S(2)}) %collective-permute-start) | collective-permute-done | bytes 1048608 | tf_op jit(solution)/shard_map/ppermute | solution.py:108
  30.4 2.2 collective-permute-done.1.refs_1_
  37.2 2.2 pack.1
  41.6 2.7 %dynamic-slice_bitcast_fusion = (bf16[64,8192]{1,0:T(8,128)(2,1)}, bf16[64,8192]{1,0:T(8,128)(2,1)S(1)}) fusion(bf16[4,64,8192]{2,1,0:T(8,128)(2,1)} %param.8, s32[]{:T(128)S(6)} %select_n.166, s32[]{:T(128)S(6)} %select_n.165), kind=kLoop, calls=%fused_computation.2 | loop fusion | bytes 4194312 | tf_op jit(solution)/shard_map/jit(dynamic_index_in_dim)/squeeze | solution.py:325
  44.8 1.6 collective-permute-start.7
  46.9 2.1 pad_maximum_fusion
  49.0 3.8 %collective-permute-done.2.refs_1_ = bf16[64,8192]{1,0:T(8,128)(2,1)S(1)} collective-permute-done((bf16[64,8192]{1,0:T(8,128)(2,1)}, bf16[64,8192]{1,0:T(8,128)(2,1)S(1)}, u32[]{:S(2)}, u32[]{:S(2)}) %collective-permute-start.2) | collective-permute-done | bytes 1048608 | tf_op jit(solution)/shard_map/ppermute | solution.py:108
  52.8 2.3 %collective-permute-done.3.refs_0_ = bf16[64,8192]{1,0:T(8,128)(2,1)} collective-permute-done((bf16[64,8192]{1,0:T(8,128)(2,1)}, bf16[64,8192]{1,0:T(8,128)(2,1)}, u32[]{:S(2)}, u32[]{:S(2)}) %collective-permute-start.3) | collective-permute-done | bytes 1048608 | tf_op jit(solution)/shard_map/ppermute | solution.py:108
  55.0 1.6 collective-permute-start.5
  57.8 5.8 %copy-done.3 = bf16[8192,1024]{1,0:T(8,128)(2,1)S(1)} copy-done((bf16[8192,1024]{1,0:T(8,128)(2,1)S(1)}, bf16[8192,1024]{1,0:T(8,128)(2,1)}, u32[]{:S(2)}) %copy-start.3) | copy-done | bytes 16777240
  63.6 2.8 %pin.1.weights = bf16[8192,1152]{1,0:T(8,128)(2,1)S(1)} custom-call(bf16[8192,1024]{1,0:T(8,128)(2,1)S(1)} %copy-done.3, bf16[64,8192]{1,0:T(8,128)(2,1)S(1)} %get-tuple-element.168.own, bf16[64,8192]{1,0:T(8,128)(2,1)S(1)} %collective-permute-done.9.swapped), custom_call_target="tpu_custom_call" | custom-call | flops 1 | bytes 1 | tf_op jit(solution)/shard_map/pin/pallas_call | solution.py:138
  66.4 3.4 %rows.8 = (f32[128,1024]{1,0:T(8,128)S(1)}, bf16[128,128]{1,0:T(8,128)(2,1)S(1)}) custom-call(s32[2,16]{1,0:T(2,128)S(1)} %add_convert_fusion.table, bf16[8192,1152]{1,0:T(8,128)(2,1)S(1)} %pin.1.weights, bf16[128,8192]{1,0:T(8,128)(2,1)S(1)} %bitcast.63, bf16[128,128]{1,0:T(8,128)(2,1)S(1)} %broadcast_in_dim.49.refs_1_), custom_call_target="tpu_custom_call" | custom-call | flops 1 | bytes 1 | tf_op jit(solution)/shard_map/rows/pallas_call | solution.py:175
  71.3 6.0 %rows.9 = (f32[128,1024]{1,0:T(8,128)S(1)}, bf16[128,128]{1,0:T(8,128)(2,1)S(1)}) custom-call(s32[2,16]{1,0:T(2,128)S(1)} %add_convert_fusion.table, bf16[8192,1152]{1,0:T(8,128)(2,1)S(1)} %pin.1.weights, bf16[64,8192]{1,0:T(8,128)(2,1)} %collective-permute-done.refs_0_, bf16[64,8192]{1,0:T(8,128)(2,1)} %collective-permute-done.1.refs_1_, ...), custom_call_target="tpu_custom_call" | custom-call | flops 1 | bytes 1 | tf_op jit(solution)/shard_map/rows/pallas_call | solution.py:175
  78.1 1.6 collective-permute-start.12
  80.1 4.1 %rows.10 = (f32[128,1024]{1,0:T(8,128)S(1)}, bf16[128,128]{1,0:T(8,128)(2,1)S(1)}) custom-call(s32[2,16]{1,0:T(2,128)S(1)} %add_convert_fusion.table, bf16[8192,1152]{1,0:T(8,128)(2,1)S(1)} %pin.1.weights, bf16[64,8192]{1,0:T(8,128)(2,1)} %collective-permute-done.3.refs_0_, bf16[64,8192]{1,0:T(8,128)(2,1)S(1)} %collective-permute-done.2.refs_1_, ...), custom_call_target="tpu_custom_call" | custom-call | flops 1 | bytes 1 | tf_op jit(solution)/shard_map/rows/pallas_call | solution.py:175
  84.3 4.6 %rows.11 = (f32[128,1024]{1,0:T(8,128)S(1)}, bf16[128,128]{1,0:T(8,128)(2,1)S(1)}) custom-call(s32[2,16]{1,0:T(2,128)S(1)} %add_convert_fusion.table, bf16[8192,1152]{1,0:T(8,128)(2,1)S(1)} %pin.1.weights, bf16[64,8192]{1,0:T(8,128)(2,1)} %collective-permute-done.7.refs_0_, bf16[64,8192]{1,0:T(8,128)(2,1)} %collective-permute-done.8.refs_1_, ...), custom_call_target="tpu_custom_call" | custom-call | flops 1 | bytes 1 | tf_op jit(solution)/shard_map/rows/pallas_call | solution.py:175
  89.7 8.1 %collective-permute-done.5.refs_1_ = bf16[64,8192]{1,0:T(8,128)(2,1)} collective-permute-done((bf16[64,8192]{1,0:T(8,128)(2,1)S(1)}, bf16[64,8192]{1,0:T(8,128)(2,1)}, u32[]{:S(2)}, u32[]{:S(2)}) %collective-permute-start.5) | collective-permute-done | bytes 1048608 | tf_op jit(solution)/shard_map/ppermute | solution.py:108
  97.8 2.2 collective-permute-done.6.refs_0_
  100.0 1.6 collective-permute-start.10
  102.0 4.4 %rows.12 = (f32[128,1024]{1,0:T(8,128)S(1)}, bf16[128,128]{1,0:T(8,128)(2,1)S(1)}) custom-call(s32[2,16]{1,0:T(2,128)S(1)} %add_convert_fusion.table, bf16[8192,1152]{1,0:T(8,128)(2,1)S(1)} %pin.1.weights, bf16[64,8192]{1,0:T(8,128)(2,1)} %collective-permute-done.6.refs_0_, bf16[64,8192]{1,0:T(8,128)(2,1)} %collective-permute-done.5.refs_1_, ...), custom_call_target="tpu_custom_call" | custom-call | flops 1 | bytes 1 | tf_op jit(solution)/shard_map/rows/pallas_call | solution.py:175
  107.2 12.9 %collective-permute-done.12.refs_0_ = bf16[64,8192]{1,0:T(8,128)(2,1)S(1)} collective-permute-done((bf16[64,8192]{1,0:T(8,128)(2,1)}, bf16[64,8192]{1,0:T(8,128)(2,1)S(1)}, u32[]{:S(2)}, u32[]{:S(2)}) %collective-permute-start.12) | collective-permute-done | bytes 1048608 | tf_op jit(solution)/shard_map/ppermute | solution.py:108
  120.2 2.3 %collective-permute-done.13.refs_1_ = bf16[64,8192]{1,0:T(8,128)(2,1)} collective-permute-done((bf16[64,8192]{1,0:T(8,128)(2,1)}, bf16[64,8192]{1,0:T(8,128)(2,1)}, u32[]{:S(2)}, u32[]{:S(2)}) %collective-permute-start.13) | collective-permute-done | bytes 1048608 | tf_op jit(solution)/shard_map/ppermute | solution.py:108
  122.4 1.6 collective-permute-start.14
  124.5 4.2 %rows.13 = (f32[128,1024]{1,0:T(8,128)S(1)}, bf16[128,128]{1,0:T(8,128)(2,1)S(1)}) custom-call(s32[2,16]{1,0:T(2,128)S(1)} %add_convert_fusion.table, bf16[8192,1152]{1,0:T(8,128)(2,1)S(1)} %pin.1.weights, bf16[64,8192]{1,0:T(8,128)(2,1)S(1)} %collective-permute-done.12.refs_0_, bf16[64,8192]{1,0:T(8,128)(2,1)} %collective-permute-done.13.refs_1_, ...), custom_call_target="tpu_custom_call" | custom-call | flops 1 | bytes 1 | tf_op jit(solution)/shard_map/rows/pallas_call | solution.py:175
  129.4 13.2 %collective-permute-done.10.refs_1_ = bf16[64,8192]{1,0:T(8,128)(2,1)S(1)} collective-permute-done((bf16[64,8192]{1,0:T(8,128)(2,1)}, bf16[64,8192]{1,0:T(8,128)(2,1)S(1)}, u32[]{:S(2)}, u32[]{:S(2)}) %collective-permute-start.10) | collective-permute-done | bytes 1048608 | tf_op jit(solution)/shard_map/ppermute | solution.py:108
  142.6 2.2 collective-permute-done.11.refs_0_
  146.6 4.8 %all-to-all-start = ((bf16[8,2,32,512]{3,2,1,0:T(8,128)(2,1)}), bf16[8,2,32,512]{3,2,1,0:T(8,128)(2,1)S(1)}, u32[]{:S(2)}, u32[]{:S(2)}) async-start(bf16[8,2,32,512]{3,2,1,0:T(8,128)(2,1)} %copy.11), calls=%async_computation | async-start | bytes 1048576 | tf_op jit(solution)/shard_map/all_to_all | solution.py:357
  151.4 6.4 %copy-done.1 = bf16[8192,1152]{1,0:T(8,128)(2,1)S(1)} copy-done((bf16[8192,1152]{1,0:T(8,128)(2,1)S(1)}, bf16[8192,1152]{1,0:T(8,128)(2,1)}, u32[]{:S(2)}) %copy-start.1) | copy-done | bytes 18874392
  159.0 3.5 %rows.14 = (f32[128,1024]{1,0:T(8,128)S(1)}, bf16[128,128]{1,0:T(8,128)(2,1)S(1)}) custom-call(s32[2,16]{1,0:T(2,128)S(1)} %add_convert_fusion.table, bf16[8192,1152]{1,0:T(8,128)(2,1)S(1)} %copy-done.1, bf16[64,8192]{1,0:T(8,128)(2,1)S(1)} %copy-done.8, bf16[64,8192]{1,0:T(8,128)(2,1)S(1)} %collective-permute-done.10.refs_1_, ...), custom_call_target="tpu_custom_call" | custom-call | flops 1 | bytes 1 | tf_op jit(solution)/shard_map/rows/pallas_call | solution.py:175
  163.4 1.7 collective-permute-done.14.refs_0_
  165.1 2.2 collective-permute-done.15.refs_1_
  167.3 10.7 %all-to-all-done = bf16[8,2,32,512]{3,2,1,0:T(8,128)(2,1)S(1)} async-done(((bf16[8,2,32,512]{3,2,1,0:T(8,128)(2,1)}), bf16[8,2,32,512]{3,2,1,0:T(8,128)(2,1)S(1)}, u32[]{:S(2)}, u32[]{:S(2)}) %all-to-all-start) | async-done | bytes 524320 | tf_op jit(solution)/shard_map/all_to_all | solution.py:357
  178.0 3.6 %all-to-all-start.1 = ((bf16[8,2,32,512]{3,2,1,0:T(8,128)(2,1)}), bf16[8,2,32,512]{3,2,1,0:T(8,128)(2,1)S(1)}, u32[]{:S(2)}, u32[]{:S(2)}) async-start(bf16[8,2,32,512]{3,2,1,0:T(8,128)(2,1)} %copy.12), calls=%async_computation.1 | async-start | bytes 1048576 | tf_op jit(solution)/shard_map/all_to_all | solution.py:357
  181.6 6.4 %copy-done.2 = bf16[8192,1152]{1,0:T(8,128)(2,1)S(1)} copy-done((bf16[8192,1152]{1,0:T(8,128)(2,1)S(1)}, bf16[8192,1152]{1,0:T(8,128)(2,1)}, u32[]{:S(2)}) %copy-start.2) | copy-done | bytes 18874392
  188.0 4.4 %rows.15 = (f32[128,1024]{1,0:T(8,128)S(1)}, bf16[128,128]{1,0:T(8,128)(2,1)S(1)}) custom-call(s32[2,16]{1,0:T(2,128)S(1)} %add_convert_fusion.table, bf16[8192,1152]{1,0:T(8,128)(2,1)S(1)} %copy-done.2, bf16[64,8192]{1,0:T(8,128)(2,1)} %collective-permute-done.14.refs_0_, bf16[64,8192]{1,0:T(8,128)(2,1)} %collective-permute-done.15.refs_1_, ...), custom_call_target="tpu_custom_call" | custom-call | flops 99999997952 | bytes 1 | tf_op jit(solution)/shard_map/rows/pallas_call | solution.py:175
  193.2 2.0 collective-permute-start.16
  195.2 1.9 collective-permute-done.16
  197.1 2.1 collective-permute-start.17
  199.2 2.4 %collective-permute-start.18 = (bf16[2,128,128]{2,1,0:T(8,128)(2,1)S(1)}, bf16[2,128,128]{2,1,0:T(8,128)(2,1)S(1)}, u32[]{:S(2)}, u32[]{:S(2)}) collective-permute-start(bf16[2,128,128]{2,1,0:T(8,128)(2,1)S(1)} %pad_maximum_fusion.1.refs_0_), channel_id=1, source_target_pairs={{0,8},{2,10},{4,12},{6,14},{8,0},{10,2},{12,4},{14,6},{1,9},{3,11}... | collective-permute-start | bytes 196616 | tf_op jit(solution)/shard_map/ppermute | solution.py:108
  201.9 2.2 collect.1.base
  204.1 1.9 copy-done.4
  206.1 1.6 collective-permute-done.19.refs_3_
  211.3 6.3 %collective-permute-done.21.refs_7_ = bf16[8,32,512]{2,1,0:T(8,128)(2,1)S(1)} collective-permute-done((bf16[8,32,512]{2,1,0:T(8,128)(2,1)S(1)}, bf16[8,32,512]{2,1,0:T(8,128)(2,1)S(1)}, u32[]{:S(2)}, u32[]{:S(2)}) %collective-permute-start.21) | collective-permute-done | bytes 262176 | tf_op jit(solution)/shard_map/ppermute | solution.py:112
  217.6 2.2 copy-done.5
  219.8 2.3 %finish.1 = bf16[1024,1024]{1,0:T(8,128)(2,1)} custom-call(s32[4,16]{1,0:T(4,128)S(1)} %add_add_fusion.table, f32[8,128,1024]{2,1,0:T(8,128)S(1)} %copy-done.5, bf16[2,128,128]{2,1,0:T(8,128)(2,1)S(1)} %pad_maximum_fusion.1.refs_0_, bf16[2,128,128]{2,1,0:T(8,128)(2,1)S(1)} %collective-permute-done.17.refs_1_, ...), custom_call_target="tpu_custom_call" | custom-call | flops 1 | bytes 1 | tf_op jit(solution)/shard_map/finish/pallas_call | solution.py:280
  (86 shorter events, 20.1 us)
Async XLA Ops:
  0.0 32.5 %copy-start.24 = (s32[64]{0:T(128)S(1)}, s32[64]{0:T(128)}, u32[]{:S(2)}) copy-start(s32[64]{0:T(128)} %param.10) | copy-start | bytes 772
  0.0 32.5 %copy-start.23 = (s32[2,8]{1,0:T(2,128)S(1)}, s32[2,8]{1,0:T(2,128)}, u32[]{:S(2)}) copy-start(s32[2,8]{1,0:T(2,128)} %param.11) | copy-start | bytes 196
  3.1 27.3 %collective-permute-start = (bf16[64,8192]{1,0:T(8,128)(2,1)}, bf16[64,8192]{1,0:T(8,128)(2,1)}, u32[]{:S(2)}, u32[]{:S(2)}) collective-permute-start(bf16[64,8192]{1,0:T(8,128)(2,1)} %get-tuple-element.170), channel_id=1, source_target_pairs={{0,4},{4,8},{8,12},{12,14},{14,10},{10,6},{6,2},{2,0},{1,5},{5,9},... | collective-permute-start | bytes 3145736 | tf_op jit(solution)/shard_map/ppermute | solution.py:108
  6.1 26.4 %collective-permute-start.1 = (bf16[64,8192]{1,0:T(8,128)(2,1)}, bf16[64,8192]{1,0:T(8,128)(2,1)}, u32[]{:S(2)}, u32[]{:S(2)}) collective-permute-start(bf16[64,8192]{1,0:T(8,128)(2,1)} %get-tuple-element.169), channel_id=1, source_target_pairs={{4,0},{8,4},{12,8},{14,12},{10,14},{6,10},{2,6},{0,2},{5,1},{9,5},... | collective-permute-start | bytes 3145736 | tf_op jit(solution)/shard_map/ppermute | solution.py:108
  6.1 46.6 %collective-permute-start.2 = (bf16[64,8192]{1,0:T(8,128)(2,1)}, bf16[64,8192]{1,0:T(8,128)(2,1)S(1)}, u32[]{:S(2)}, u32[]{:S(2)}) collective-permute-start(bf16[64,8192]{1,0:T(8,128)(2,1)} %get-tuple-element.169), channel_id=1, source_target_pairs={{0,4},{4,8},{8,12},{12,14},{14,10},{10,6},{6,2},{2,0},{1,5},{5,9},... | collective-permute-start | bytes 3145736 | tf_op jit(solution)/shard_map/ppermute | solution.py:108
  8.2 46.8 %collective-permute-start.3 = (bf16[64,8192]{1,0:T(8,128)(2,1)}, bf16[64,8192]{1,0:T(8,128)(2,1)}, u32[]{:S(2)}, u32[]{:S(2)}) collective-permute-start(bf16[64,8192]{1,0:T(8,128)(2,1)} %get-tuple-element.170), channel_id=1, source_target_pairs={{4,0},{8,4},{12,8},{14,12},{10,14},{6,10},{2,6},{0,2},{5,1},{9,5},... | collective-permute-start | bytes 3145736 | tf_op jit(solution)/shard_map/ppermute | solution.py:108
  40.4 6.1 %collective-permute-start.4 = (bf16[8,64,512]{2,1,0:T(8,128)(2,1)}, bf16[8,64,512]{2,1,0:T(8,128)(2,1)}, u32[]{:S(2)}, u32[]{:S(2)}) collective-permute-start(bf16[8,64,512]{2,1,0:T(8,128)(2,1)} %get-tuple-element.173), channel_id=1, source_target_pairs={{0,1},{1,0},{2,3},{3,2},{4,5},{5,4},{6,7},{7,6},{8,9},{9,8},{10,11... | collective-permute-start | bytes 1572872 | tf_op jit(solution)/shard_map/ppermute | solution.py:112
  41.6 5.3 %copy-start.19 = (bf16[8,1,64,512]{3,2,0,1:T(8,128)(2,1)S(1)}, bf16[8,1,64,512]{3,2,0,1:T(8,128)(2,1)}, u32[]{:S(2)}) copy-start(bf16[8,1,64,512]{3,2,0,1:T(8,128)(2,1)} %get-tuple-element.174) | copy-start | bytes 1572868
  44.3 13.4 %collective-permute-start.9 = (bf16[64,8192]{1,0:T(8,128)(2,1)}, bf16[64,8192]{1,0:T(8,128)(2,1)S(1)}, u32[]{:S(2)}, u32[]{:S(2)}) collective-permute-start(bf16[64,8192]{1,0:T(8,128)(2,1)} %get-tuple-element.167), channel_id=1, source_target_pairs={{0,1},{1,0},{2,3},{3,2},{4,5},{5,4},{6,7},{7,6},{8,9},{9,8},{10,11... | collective-permute-start | bytes 3145736 | tf_op jit(solution)/shard_map/ppermute | solution.py:112
  44.8 33.3 %collective-permute-start.7 = (bf16[64,8192]{1,0:T(8,128)(2,1)}, bf16[64,8192]{1,0:T(8,128)(2,1)}, u32[]{:S(2)}, u32[]{:S(2)}) collective-permute-start(bf16[64,8192]{1,0:T(8,128)(2,1)} %collective-permute-done.refs_0_), channel_id=1, source_target_pairs={{0,4},{4,8},{8,12},{12,14},{14,10},{10,6},{6,2},{2,0},{1,5},{5,9},... | collective-permute-start | bytes 3145736 | tf_op jit(solution)/shard_map/ppermute | solution.py:108
  46.4 31.7 %collective-permute-start.8 = (bf16[64,8192]{1,0:T(8,128)(2,1)}, bf16[64,8192]{1,0:T(8,128)(2,1)}, u32[]{:S(2)}, u32[]{:S(2)}) collective-permute-start(bf16[64,8192]{1,0:T(8,128)(2,1)} %collective-permute-done.1.refs_1_), channel_id=1, source_target_pairs={{4,0},{8,4},{12,8},{14,12},{10,14},{6,10},{2,6},{0,2},{5,1},{9,5},... | collective-permute-start | bytes 3145736 | tf_op jit(solution)/shard_map/ppermute | solution.py:108
  55.0 42.8 %collective-permute-start.5 = (bf16[64,8192]{1,0:T(8,128)(2,1)S(1)}, bf16[64,8192]{1,0:T(8,128)(2,1)}, u32[]{:S(2)}, u32[]{:S(2)}) collective-permute-start(bf16[64,8192]{1,0:T(8,128)(2,1)S(1)} %collective-permute-done.2.refs_1_), channel_id=1, source_target_pairs={{0,4},{4,8},{8,12},{12,14},{14,10},{10,6},{6,2},{2,0},{1,5},{5,9},... | collective-permute-start | bytes 3145736 | tf_op jit(solution)/shard_map/ppermute | solution.py:108
  56.6 43.4 %collective-permute-start.6 = (bf16[64,8192]{1,0:T(8,128)(2,1)}, bf16[64,8192]{1,0:T(8,128)(2,1)}, u32[]{:S(2)}, u32[]{:S(2)}) collective-permute-start(bf16[64,8192]{1,0:T(8,128)(2,1)} %collective-permute-done.3.refs_0_), channel_id=1, source_target_pairs={{4,0},{8,4},{12,8},{14,12},{10,14},{6,10},{2,6},{0,2},{5,1},{9,5},... | collective-permute-start | bytes 3145736 | tf_op jit(solution)/shard_map/ppermute | solution.py:108
  57.8 5.8 %copy-start.3 = (bf16[8192,1024]{1,0:T(8,128)(2,1)S(1)}, bf16[8192,1024]{1,0:T(8,128)(2,1)}, u32[]{:S(2)}) copy-start(bf16[8192,1024]{1,0:T(8,128)(2,1)} %weight.1) | copy-start | bytes 50331652
  63.6 2.8 %copy-start.6 = (bf16[1,128,8192]{2,1,0:T(8,128)(2,1)S(1)}, bf16[1,128,8192]{2,1,0:T(8,128)(2,1)}, u32[]{:S(2)}) copy-start(bf16[1,128,8192]{2,1,0:T(8,128)(2,1)} %param.6) | copy-start | bytes 6291460
  66.3 58.1 %copy-start = (bf16[8192,1152]{1,0:T(8,128)(2,1)}, bf16[8192,1152]{1,0:T(8,128)(2,1)S(1)}, u32[]{:S(2)}) copy-start(bf16[8192,1152]{1,0:T(8,128)(2,1)S(1)} %pin.1.weights) | copy-start | bytes 56623108
  69.8 1.5 copy-start.9
  77.3 0.8 copy-start.10
  78.1 42.1 %collective-permute-start.12 = (bf16[64,8192]{1,0:T(8,128)(2,1)}, bf16[64,8192]{1,0:T(8,128)(2,1)S(1)}, u32[]{:S(2)}, u32[]{:S(2)}) collective-permute-start(bf16[64,8192]{1,0:T(8,128)(2,1)} %collective-permute-done.7.refs_0_), channel_id=1, source_target_pairs={{0,4},{4,8},{8,12},{12,14},{14,10},{10,6},{6,2},{2,0},{1,5},{5,9},... | collective-permute-start | bytes 3145736 | tf_op jit(solution)/shard_map/ppermute | solution.py:108
  79.7 42.7 %collective-permute-start.13 = (bf16[64,8192]{1,0:T(8,128)(2,1)}, bf16[64,8192]{1,0:T(8,128)(2,1)}, u32[]{:S(2)}, u32[]{:S(2)}) collective-permute-start(bf16[64,8192]{1,0:T(8,128)(2,1)} %collective-permute-done.8.refs_1_), channel_id=1, source_target_pairs={{4,0},{8,4},{12,8},{14,12},{10,14},{6,10},{2,6},{0,2},{5,1},{9,5},... | collective-permute-start | bytes 3145736 | tf_op jit(solution)/shard_map/ppermute | solution.py:108
  84.3 4.7 %copy-start.11 = (f32[128,1024]{1,0:T(8,128)}, f32[128,1024]{1,0:T(8,128)S(1)}, u32[]{:S(2)}) copy-start(f32[128,1024]{1,0:T(8,128)S(1)} %get-tuple-element.150.refs_2_) | copy-start | bytes 1572868
  88.9 0.8 copy-start.12
  100.0 42.7 %collective-permute-start.10 = (bf16[64,8192]{1,0:T(8,128)(2,1)}, bf16[64,8192]{1,0:T(8,128)(2,1)S(1)}, u32[]{:S(2)}, u32[]{:S(2)}) collective-permute-start(bf16[64,8192]{1,0:T(8,128)(2,1)} %collective-permute-done.5.refs_1_), channel_id=1, source_target_pairs={{0,4},{4,8},{8,12},{12,14},{14,10},{10,6},{6,2},{2,0},{1,5},{5,9},... | collective-permute-start | bytes 3145736 | tf_op jit(solution)/shard_map/ppermute | solution.py:108
  101.5 43.3 %collective-permute-start.11 = (bf16[64,8192]{1,0:T(8,128)(2,1)}, bf16[64,8192]{1,0:T(8,128)(2,1)S(1)}, u32[]{:S(2)}, u32[]{:S(2)}) collective-permute-start(bf16[64,8192]{1,0:T(8,128)(2,1)} %collective-permute-done.6.refs_0_), channel_id=1, source_target_pairs={{4,0},{8,4},{12,8},{14,12},{10,14},{6,10},{2,6},{0,2},{5,1},{9,5},... | collective-permute-start | bytes 3145736 | tf_op jit(solution)/shard_map/ppermute | solution.py:108
  106.4 0.8 copy-start.13
  122.4 23.3 %copy-start.18 = (bf16[8,2,32,512]{3,2,0,1:T(8,128)(2,1)S(1)}, bf16[8,2,32,512]{3,2,0,1:T(8,128)(2,1)}, u32[]{:S(2)}) copy-start(bf16[8,2,32,512]{3,2,0,1:T(8,128)(2,1)} %get-tuple-element.131) | copy-start | bytes 1572868
  122.4 42.7 %collective-permute-start.14 = (bf16[64,8192]{1,0:T(8,128)(2,1)S(1)}, bf16[64,8192]{1,0:T(8,128)(2,1)}, u32[]{:S(2)}, u32[]{:S(2)}) collective-permute-start(bf16[64,8192]{1,0:T(8,128)(2,1)S(1)} %collective-permute-done.12.refs_0_), channel_id=1, source_target_pairs={{0,4},{4,8},{8,12},{12,14},{14,10},{10,6},{6,2},{2,0},{1,5},{5,9},... | collective-permute-start | bytes 3145736 | tf_op jit(solution)/shard_map/ppermute | solution.py:108
  124.0 43.3 %collective-permute-start.15 = (bf16[64,8192]{1,0:T(8,128)(2,1)}, bf16[64,8192]{1,0:T(8,128)(2,1)}, u32[]{:S(2)}, u32[]{:S(2)}) collective-permute-start(bf16[64,8192]{1,0:T(8,128)(2,1)} %collective-permute-done.13.refs_1_), channel_id=1, source_target_pairs={{4,0},{8,4},{12,8},{14,12},{10,14},{6,10},{2,6},{0,2},{5,1},{9,5},... | collective-permute-start | bytes 3145736 | tf_op jit(solution)/shard_map/ppermute | solution.py:108
  128.6 0.8 copy-start.14
  144.8 1.0 copy-start.7
  146.6 31.4 %all-to-all-start = ((bf16[8,2,32,512]{3,2,1,0:T(8,128)(2,1)}), bf16[8,2,32,512]{3,2,1,0:T(8,128)(2,1)S(1)}, u32[]{:S(2)}, u32[]{:S(2)}) async-start(bf16[8,2,32,512]{3,2,1,0:T(8,128)(2,1)} %copy.11), calls=%async_computation | async-start | bytes 1048576 | tf_op jit(solution)/shard_map/all_to_all | solution.py:357
  151.4 6.4 %copy-start.1 = (bf16[8192,1152]{1,0:T(8,128)(2,1)S(1)}, bf16[8192,1152]{1,0:T(8,128)(2,1)}, u32[]{:S(2)}) copy-start(bf16[8192,1152]{1,0:T(8,128)(2,1)} %copy-done) | copy-start | bytes 56623108
  157.8 1.2 copy-start.8
  159.0 3.5 %copy-start.17 = (bf16[8,2,32,512]{3,2,0,1:T(8,128)(2,1)S(1)}, bf16[8,2,32,512]{3,2,0,1:T(8,128)(2,1)}, u32[]{:S(2)}) copy-start(bf16[8,2,32,512]{3,2,0,1:T(8,128)(2,1)} %get-tuple-element.143) | copy-start | bytes 1572868
  162.5 4.8 %copy-start.15 = (f32[128,1024]{1,0:T(8,128)}, f32[128,1024]{1,0:T(8,128)S(1)}, u32[]{:S(2)}) copy-start(f32[128,1024]{1,0:T(8,128)S(1)} %get-tuple-element.154.refs_6_) | copy-start | bytes 1572868
  178.0 31.9 %all-to-all-start.1 = ((bf16[8,2,32,512]{3,2,1,0:T(8,128)(2,1)}), bf16[8,2,32,512]{3,2,1,0:T(8,128)(2,1)S(1)}, u32[]{:S(2)}, u32[]{:S(2)}) async-start(bf16[8,2,32,512]{3,2,1,0:T(8,128)(2,1)} %copy.12), calls=%async_computation.1 | async-start | bytes 1048576 | tf_op jit(solution)/shard_map/all_to_all | solution.py:357
  181.6 6.4 %copy-start.2 = (bf16[8192,1152]{1,0:T(8,128)(2,1)S(1)}, bf16[8192,1152]{1,0:T(8,128)(2,1)}, u32[]{:S(2)}) copy-start(bf16[8192,1152]{1,0:T(8,128)(2,1)} %copy-done) | copy-start | bytes 56623108
  192.4 0.8 copy-start.16
  193.2 3.9 %collective-permute-start.16 = (bf16[128,128]{1,0:T(8,128)(2,1)S(1)}, bf16[128,128]{1,0:T(8,128)(2,1)S(1)}, u32[]{:S(2)}, u32[]{:S(2)}) collective-permute-start(bf16[128,128]{1,0:T(8,128)(2,1)S(1)} %get-tuple-element.147), channel_id=1, source_target_pairs={{0,2},{2,0},{4,6},{6,4},{8,10},{10,8},{12,14},{14,12},{1,3},{3,1},... | collective-permute-start | bytes 98312 | tf_op jit(solution)/shard_map/ppermute | solution.py:108
  197.1 8.9 %collective-permute-start.17 = (bf16[2,128,128]{2,1,0:T(8,128)(2,1)S(1)}, bf16[2,128,128]{2,1,0:T(8,128)(2,1)S(1)}, u32[]{:S(2)}, u32[]{:S(2)}) collective-permute-start(bf16[2,128,128]{2,1,0:T(8,128)(2,1)S(1)} %pad_maximum_fusion.1.refs_0_), channel_id=1, source_target_pairs={{0,4},{2,6},{4,0},{6,2},{8,12},{10,14},{12,8},{14,10},{1,5},{3,7},... | collective-permute-start | bytes 196616 | tf_op jit(solution)/shard_map/ppermute | solution.py:108
  199.2 6.8 %collective-permute-start.18 = (bf16[2,128,128]{2,1,0:T(8,128)(2,1)S(1)}, bf16[2,128,128]{2,1,0:T(8,128)(2,1)S(1)}, u32[]{:S(2)}, u32[]{:S(2)}) collective-permute-start(bf16[2,128,128]{2,1,0:T(8,128)(2,1)S(1)} %pad_maximum_fusion.1.refs_0_), channel_id=1, source_target_pairs={{0,8},{2,10},{4,12},{6,14},{8,0},{10,2},{12,4},{14,6},{1,9},{3,11}... | collective-permute-start | bytes 196616 | tf_op jit(solution)/shard_map/ppermute | solution.py:108
  201.6 6.1 %collective-permute-start.19 = (bf16[2,128,128]{2,1,0:T(8,128)(2,1)S(1)}, bf16[2,128,128]{2,1,0:T(8,128)(2,1)S(1)}, u32[]{:S(2)}, u32[]{:S(2)}) collective-permute-start(bf16[2,128,128]{2,1,0:T(8,128)(2,1)S(1)} %pad_maximum_fusion.1.refs_0_), channel_id=1, source_target_pairs={{0,12},{2,14},{4,8},{6,10},{8,4},{10,6},{12,0},{14,2},{1,13},{3,15... | collective-permute-start | bytes 196616 | tf_op jit(solution)/shard_map/ppermute | solution.py:108
  201.9 9.4 %copy-start.21 = (s32[16]{0:T(128)S(1)}, s32[16]{0:T(128)}, u32[]{:S(2)}) copy-start(s32[16]{0:T(128)} %copy-done.20) | copy-start | bytes 196
  201.9 9.4 %copy-start.22 = (s32[1,16]{1,0:T(1,128)S(1)}, s32[1,16]{1,0:T(1,128)}, u32[]{:S(2)}) copy-start(s32[1,16]{1,0:T(1,128)} %get-tuple-element.177) | copy-start | bytes 196
  204.1 2.0 copy-start.4
  208.4 9.2 %collective-permute-start.20 = (bf16[8,32,512]{2,1,0:T(8,128)(2,1)S(1)}, bf16[8,32,512]{2,1,0:T(8,128)(2,1)S(1)}, u32[]{:S(2)}, u32[]{:S(2)}) collective-permute-start(bf16[8,32,512]{2,1,0:T(8,128)(2,1)S(1)} %take.2.refs_4_), channel_id=1, source_target_pairs={{0,16},{16,0},{1,17},{17,1},{2,18},{18,2},{3,19},{19,3},{4,20},{20... | collective-permute-start | bytes 786440 | tf_op jit(solution)/shard_map/ppermute | solution.py:112
  210.6 7.0 %collective-permute-start.21 = (bf16[8,32,512]{2,1,0:T(8,128)(2,1)S(1)}, bf16[8,32,512]{2,1,0:T(8,128)(2,1)S(1)}, u32[]{:S(2)}, u32[]{:S(2)}) collective-permute-start(bf16[8,32,512]{2,1,0:T(8,128)(2,1)S(1)} %take.3.refs_5_), channel_id=1, source_target_pairs={{0,16},{16,0},{1,17},{17,1},{2,18},{18,2},{3,19},{19,3},{4,20},{20... | collective-permute-start | bytes 786440 | tf_op jit(solution)/shard_map/ppermute | solution.py:112
  217.6 2.2 copy-start.5
  (1 other events, 0.5 us)

commit v18 on v16

--- a/solution.py
+++ b/solution.py
@@ -356,7 +356,7 @@
     across = send(shrunk, ACROSS)
     pair = jnp.stack([shrunk, across])
     everyone = [pair] + [send(pair, pairs) for pairs in ALONG]
-    up_got, _ = lax.optimization_barrier((up_got, across))
+    up_got, everyone = lax.optimization_barrier((up_got, everyone))
     home, core = owner_row // 2, owner_row % 2
     chosen = 2 * home + jnp.where(core == store, 0, 1)
     up_mine = take_call(chosen.astype(jnp.int32), up_got.reshape(16, rank, -1))

time: 208 us -> 213 us (1.024)
  starting transfers between devices: 28 us -> 31.7 us
    all_to_all x1, waiting for transfers between devices: 12.7 us -> 0.01 us  [chain_body(): lax.all_to_all(up_sent, 'tensor', split_axis=0, concat_axis=0, tiled=True)]
    ppermute x3, waiting for transfers between devices: 2.78 us -> 9.98 us  [swap(): return lax.ppermute(value, axis, [(0, 1), (1, 0)])]
    ppermute x18, waiting for transfers between devices: 81.2 us -> 87.5 us  [send(): return lax.ppermute(value, 'tensor', pairs)]
    ppermute x18, starting transfers between devices: 21 us -> 24.8 us  [send(): return lax.ppermute(value, 'tensor', pairs)]
  transfers between devices with their start and end apart: 22 -> 22, of which waited for: 18 -> 16; matrix products, arithmetic and copies ran while one was open for 5% -> 5% of each run, Pallas kernels for 18% -> 18%
where the time goes in v18:
time: 213 us; the launch traced here: 212 us
  waiting for transfers between devices  97.5 us (46%)
  Pallas kernels  44.3 us (21%)
  starting transfers between devices  31.7 us (15%)
  local copies, waits for them, and re-layouts  30.4 us (14%)
  between operations  4.46 us (2%)
  other arithmetic  3.79 us (2%)
    ppermute x18, waiting for transfers between devices, send(): return lax.ppermute(value, 'tensor', pairs)  87.5 us
    pallas_call x8, Pallas kernels, rows_call(): pl.pallas_call(functools.partial(rows_kernel, group), in_specs=[pl.BlockS...  33.4 us
    ppermute x18, starting transfers between devices, send(): return lax.ppermute(value, 'tensor', pairs)  24.8 us
    unnamed x38, local copies, waits for them, and re-layouts  21.5 us
    ppermute x3, waiting for transfers between devices, swap(): return lax.ppermute(value, axis, [(0, 1), (1, 0)])  9.98 us
    pallas_call x1, Pallas kernels, finish_call(): pl.pallas_call(finish_kernel, in_specs=[pl.BlockSpec(memory_space=pltpu.S...  5.24 us
    all_to_all x1, starting transfers between devices, chain_body(): lax.all_to_all(up_sent, 'tensor', split_axis=0, concat_axis=0, tiled=True)  4.82 us
  transfers between devices with their start and end apart: 22, of which 16 were waited for; matrix products, arithmetic and copies ran while one was open for 5% of the time, Pallas kernels for 18%

profile of v18, /device:TPU:0, one launch (start us, length us, event | category | flops | bytes accessed | tf_op | source)
XLA Modules:
  0.0 212.1 jit_solution(9929051407054221861)
XLA Ops:
  0.0 3.1 %slice_bitcast_fusion = (bf16[64,8192]{1,0:T(8,128)(2,1)}, bf16[64,8192]{1,0:T(8,128)(2,1)}) fusion(bf16[1,128,8192]{2,1,0:T(8,128)(2,1)} %param.6), kind=kLoop, calls=%fused_computation.3 | loop fusion | bytes 4194304 | tf_op jit(solution)/shard_map/slice | solution.py:298
  3.1 3.0 %collective-permute-start = (bf16[64,8192]{1,0:T(8,128)(2,1)}, bf16[64,8192]{1,0:T(8,128)(2,1)}, u32[]{:S(2)}, u32[]{:S(2)}) collective-permute-start(bf16[64,8192]{1,0:T(8,128)(2,1)} %get-tuple-element.156), channel_id=1, source_target_pairs={{0,4},{4,8},{8,12},{12,14},{14,10},{10,6},{6,2},{2,0},{1,5},{5,9},... | collective-permute-start | bytes 3145736 | tf_op jit(solution)/shard_map/ppermute | solution.py:108
  6.1 2.0 collective-permute-start.4
  8.1 22.2 %collective-permute-done.refs_0_ = bf16[64,8192]{1,0:T(8,128)(2,1)} collective-permute-done((bf16[64,8192]{1,0:T(8,128)(2,1)}, bf16[64,8192]{1,0:T(8,128)(2,1)}, u32[]{:S(2)}, u32[]{:S(2)}) %collective-permute-start) | collective-permute-done | bytes 1048608 | tf_op jit(solution)/shard_map/ppermute | solution.py:108
  30.4 2.2 %collective-permute-done.1.refs_1_ = bf16[64,8192]{1,0:T(8,128)(2,1)} collective-permute-done((bf16[64,8192]{1,0:T(8,128)(2,1)}, bf16[64,8192]{1,0:T(8,128)(2,1)}, u32[]{:S(2)}, u32[]{:S(2)}) %collective-permute-start.1) | collective-permute-done | bytes 1048608 | tf_op jit(solution)/shard_map/ppermute | solution.py:108
  36.2 1.4 pad_add_fusion.table
  37.6 2.2 %pack.1 = bf16[2,8,64,512]{3,2,1,0:T(8,128)(2,1)S(1)} custom-call(s32[3]{0:T(128)S(1)} %pad_add_fusion.table, bf16[4,64,8192]{2,1,0:T(8,128)(2,1)} %up.1), custom_call_target="tpu_custom_call" | custom-call | flops 1 | bytes 1 | tf_op jit(solution)/shard_map/pack/pallas_call | solution.py:198
  39.8 1.1 slice_bitcast_fusion.3
  42.2 2.7 %dynamic-slice_bitcast_fusion = (bf16[64,8192]{1,0:T(8,128)(2,1)}, bf16[64,8192]{1,0:T(8,128)(2,1)S(1)}) fusion(bf16[4,64,8192]{2,1,0:T(8,128)(2,1)} %param.8, s32[]{:T(128)S(6)} %select_n.166, s32[]{:T(128)S(6)} %select_n.165), kind=kLoop, calls=%fused_computation.1 | loop fusion | bytes 4194312 | tf_op jit(solution)/shard_map/jit(dynamic_index_in_dim)/squeeze | solution.py:318
  45.4 1.4 collective-permute-start.2
  48.2 1.3 pad_maximum_fusion
  49.5 3.2 %collective-permute-done.4.refs_1_ = bf16[64,8192]{1,0:T(8,128)(2,1)S(1)} collective-permute-done((bf16[64,8192]{1,0:T(8,128)(2,1)}, bf16[64,8192]{1,0:T(8,128)(2,1)S(1)}, u32[]{:S(2)}, u32[]{:S(2)}) %collective-permute-start.4) | collective-permute-done | bytes 1048608 | tf_op jit(solution)/shard_map/ppermute | solution.py:108
  52.7 2.3 %collective-permute-done.5.refs_0_ = bf16[64,8192]{1,0:T(8,128)(2,1)} collective-permute-done((bf16[64,8192]{1,0:T(8,128)(2,1)}, bf16[64,8192]{1,0:T(8,128)(2,1)}, u32[]{:S(2)}, u32[]{:S(2)}) %collective-permute-start.5) | collective-permute-done | bytes 1048608 | tf_op jit(solution)/shard_map/ppermute | solution.py:108
  55.0 1.6 collective-permute-start.10
  57.0 5.8 %copy-done.2 = bf16[8192,1024]{1,0:T(8,128)(2,1)S(1)} copy-done((bf16[8192,1024]{1,0:T(8,128)(2,1)S(1)}, bf16[8192,1024]{1,0:T(8,128)(2,1)}, u32[]{:S(2)}) %copy-start.2) | copy-done | bytes 16777240
  62.8 2.8 %pin.1.weights = bf16[8192,1152]{1,0:T(8,128)(2,1)S(1)} custom-call(bf16[8192,1024]{1,0:T(8,128)(2,1)S(1)} %copy-done.2, bf16[64,8192]{1,0:T(8,128)(2,1)S(1)} %get-tuple-element.154.own, bf16[64,8192]{1,0:T(8,128)(2,1)S(1)} %collective-permute-done.7.swapped), custom_call_target="tpu_custom_call" | custom-call | flops 1 | bytes 1 | tf_op jit(solution)/shard_map/pin/pallas_call | solution.py:138
  65.6 3.4 %rows.8 = (f32[128,1024]{1,0:T(8,128)S(1)}, bf16[128,128]{1,0:T(8,128)(2,1)S(1)}) custom-call(s32[2,16]{1,0:T(2,128)S(1)} %add_convert_fusion.table, bf16[8192,1152]{1,0:T(8,128)(2,1)S(1)} %pin.1.weights, bf16[128,8192]{1,0:T(8,128)(2,1)S(1)} %bitcast.62, bf16[128,128]{1,0:T(8,128)(2,1)S(1)} %broadcast_in_dim.49.refs_1_), custom_call_target="tpu_custom_call" | custom-call | flops 1 | bytes 1 | tf_op jit(solution)/shard_map/rows/pallas_call | solution.py:175
  69.0 1.6 copy-done.6
  70.6 5.9 %rows.9 = (f32[128,1024]{1,0:T(8,128)S(1)}, bf16[128,128]{1,0:T(8,128)(2,1)S(1)}) custom-call(s32[2,16]{1,0:T(2,128)S(1)} %add_convert_fusion.table, bf16[8192,1152]{1,0:T(8,128)(2,1)S(1)} %pin.1.weights, bf16[64,8192]{1,0:T(8,128)(2,1)} %collective-permute-done.refs_0_, bf16[64,8192]{1,0:T(8,128)(2,1)} %collective-permute-done.1.refs_1_, ...), custom_call_target="tpu_custom_call" | custom-call | flops 1 | bytes 1 | tf_op jit(solution)/shard_map/rows/pallas_call | solution.py:175
  77.5 1.6 collective-permute-start.8
  79.5 4.1 %rows.10 = (f32[128,1024]{1,0:T(8,128)S(1)}, bf16[128,128]{1,0:T(8,128)(2,1)S(1)}) custom-call(s32[2,16]{1,0:T(2,128)S(1)} %add_convert_fusion.table, bf16[8192,1152]{1,0:T(8,128)(2,1)S(1)} %pin.1.weights, bf16[64,8192]{1,0:T(8,128)(2,1)} %collective-permute-done.5.refs_0_, bf16[64,8192]{1,0:T(8,128)(2,1)S(1)} %collective-permute-done.4.refs_1_, ...), custom_call_target="tpu_custom_call" | custom-call | flops 1 | bytes 1 | tf_op jit(solution)/shard_map/rows/pallas_call | solution.py:175
  84.4 4.4 %rows.11 = (f32[128,1024]{1,0:T(8,128)S(1)}, bf16[128,128]{1,0:T(8,128)(2,1)S(1)}) custom-call(s32[2,16]{1,0:T(2,128)S(1)} %add_convert_fusion.table, bf16[8192,1152]{1,0:T(8,128)(2,1)S(1)} %pin.1.weights, bf16[64,8192]{1,0:T(8,128)(2,1)} %collective-permute-done.2.refs_0_, bf16[64,8192]{1,0:T(8,128)(2,1)} %collective-permute-done.3.refs_1_, ...), custom_call_target="tpu_custom_call" | custom-call | flops 1 | bytes 1 | tf_op jit(solution)/shard_map/rows/pallas_call | solution.py:175
  89.7 8.0 %collective-permute-done.10.refs_1_ = bf16[64,8192]{1,0:T(8,128)(2,1)S(1)} collective-permute-done((bf16[64,8192]{1,0:T(8,128)(2,1)S(1)}, bf16[64,8192]{1,0:T(8,128)(2,1)S(1)}, u32[]{:S(2)}, u32[]{:S(2)}) %collective-permute-start.10) | collective-permute-done | bytes 1048608 | tf_op jit(solution)/shard_map/ppermute | solution.py:108
  97.7 2.2 %collective-permute-done.11.refs_0_ = bf16[64,8192]{1,0:T(8,128)(2,1)S(1)} collective-permute-done((bf16[64,8192]{1,0:T(8,128)(2,1)}, bf16[64,8192]{1,0:T(8,128)(2,1)S(1)}, u32[]{:S(2)}, u32[]{:S(2)}) %collective-permute-start.11) | collective-permute-done | bytes 1048608 | tf_op jit(solution)/shard_map/ppermute | solution.py:108
  99.8 1.6 collective-permute-start.14
  101.8 3.4 %rows.12 = (f32[128,1024]{1,0:T(8,128)S(1)}, bf16[128,128]{1,0:T(8,128)(2,1)S(1)}) custom-call(s32[2,16]{1,0:T(2,128)S(1)} %add_convert_fusion.table, bf16[8192,1152]{1,0:T(8,128)(2,1)S(1)} %pin.1.weights, bf16[64,8192]{1,0:T(8,128)(2,1)S(1)} %collective-permute-done.11.refs_0_, bf16[64,8192]{1,0:T(8,128)(2,1)S(1)} %collective-permute-done.10.refs_1_, ...), custom_call_target="tpu_custom_call" | custom-call | flops 1 | bytes 1 | tf_op jit(solution)/shard_map/rows/pallas_call | solution.py:175
  106.1 14.0 %collective-permute-done.8.refs_0_ = bf16[64,8192]{1,0:T(8,128)(2,1)S(1)} collective-permute-done((bf16[64,8192]{1,0:T(8,128)(2,1)}, bf16[64,8192]{1,0:T(8,128)(2,1)S(1)}, u32[]{:S(2)}, u32[]{:S(2)}) %collective-permute-start.8) | collective-permute-done | bytes 1048608 | tf_op jit(solution)/shard_map/ppermute | solution.py:108
  120.1 2.3 %collective-permute-done.9.refs_1_ = bf16[64,8192]{1,0:T(8,128)(2,1)} collective-permute-done((bf16[64,8192]{1,0:T(8,128)(2,1)}, bf16[64,8192]{1,0:T(8,128)(2,1)}, u32[]{:S(2)}, u32[]{:S(2)}) %collective-permute-start.9) | collective-permute-done | bytes 1048608 | tf_op jit(solution)/shard_map/ppermute | solution.py:108
  122.4 1.6 collective-permute-start.12
  124.4 4.2 %rows.13 = (f32[128,1024]{1,0:T(8,128)S(1)}, bf16[128,128]{1,0:T(8,128)(2,1)S(1)}) custom-call(s32[2,16]{1,0:T(2,128)S(1)} %add_convert_fusion.table, bf16[8192,1152]{1,0:T(8,128)(2,1)S(1)} %pin.1.weights, bf16[64,8192]{1,0:T(8,128)(2,1)S(1)} %collective-permute-done.8.refs_0_, bf16[64,8192]{1,0:T(8,128)(2,1)} %collective-permute-done.9.refs_1_, ...), custom_call_target="tpu_custom_call" | custom-call | flops 1 | bytes 1 | tf_op jit(solution)/shard_map/rows/pallas_call | solution.py:175
  129.4 13.2 %collective-permute-done.14.refs_1_ = bf16[64,8192]{1,0:T(8,128)(2,1)S(1)} collective-permute-done((bf16[64,8192]{1,0:T(8,128)(2,1)S(1)}, bf16[64,8192]{1,0:T(8,128)(2,1)S(1)}, u32[]{:S(2)}, u32[]{:S(2)}) %collective-permute-start.14) | collective-permute-done | bytes 1048608 | tf_op jit(solution)/shard_map/ppermute | solution.py:108
  142.6 2.2 %collective-permute-done.15.refs_0_ = bf16[64,8192]{1,0:T(8,128)(2,1)S(1)} collective-permute-done((bf16[64,8192]{1,0:T(8,128)(2,1)S(1)}, bf16[64,8192]{1,0:T(8,128)(2,1)S(1)}, u32[]{:S(2)}, u32[]{:S(2)}) %collective-permute-start.15) | collective-permute-done | bytes 1048608 | tf_op jit(solution)/shard_map/ppermute | solution.py:108
  146.8 4.8 %all-to-all-start = ((bf16[8,2,64,512]{3,2,1,0:T(8,128)(2,1)}), bf16[8,2,64,512]{3,2,1,0:T(8,128)(2,1)S(1)}, u32[]{:S(2)}, u32[]{:S(2)}) async-start(bf16[8,2,64,512]{3,2,1,0:T(8,128)(2,1)} %copy.9), calls=%async_computation | async-start | bytes 2097152 | tf_op jit(solution)/shard_map/all_to_all | solution.py:348
  151.6 6.4 %copy-done.1 = bf16[8192,1152]{1,0:T(8,128)(2,1)S(1)} copy-done((bf16[8192,1152]{1,0:T(8,128)(2,1)S(1)}, bf16[8192,1152]{1,0:T(8,128)(2,1)}, u32[]{:S(2)}) %copy-start.1) | copy-done | bytes 18874392
  158.0 1.2 copy-done.5
  159.2 3.4 %rows.14 = (f32[128,1024]{1,0:T(8,128)S(1)}, bf16[128,128]{1,0:T(8,128)(2,1)S(1)}) custom-call(s32[2,16]{1,0:T(2,128)S(1)} %add_convert_fusion.table, bf16[8192,1152]{1,0:T(8,128)(2,1)S(1)} %copy-done.1, bf16[64,8192]{1,0:T(8,128)(2,1)S(1)} %copy-done.5, bf16[64,8192]{1,0:T(8,128)(2,1)S(1)} %collective-permute-done.14.refs_1_, ...), custom_call_target="tpu_custom_call" | custom-call | flops 1 | bytes 1 | tf_op jit(solution)/shard_map/rows/pallas_call | solution.py:175
  163.5 1.7 collective-permute-done.12.refs_0_
  165.2 2.2 %collective-permute-done.13.refs_1_ = bf16[64,8192]{1,0:T(8,128)(2,1)} collective-permute-done((bf16[64,8192]{1,0:T(8,128)(2,1)}, bf16[64,8192]{1,0:T(8,128)(2,1)}, u32[]{:S(2)}, u32[]{:S(2)}) %collective-permute-start.13) | collective-permute-done | bytes 1048608 | tf_op jit(solution)/shard_map/ppermute | solution.py:108
  167.3 4.4 %rows.15 = (f32[128,1024]{1,0:T(8,128)S(1)}, bf16[128,128]{1,0:T(8,128)(2,1)S(1)}) custom-call(s32[2,16]{1,0:T(2,128)S(1)} %add_convert_fusion.table, bf16[8192,1152]{1,0:T(8,128)(2,1)S(1)} %copy-done.1, bf16[64,8192]{1,0:T(8,128)(2,1)} %collective-permute-done.12.refs_0_, bf16[64,8192]{1,0:T(8,128)(2,1)} %collective-permute-done.13.refs_1_, ...), custom_call_target="tpu_custom_call" | custom-call | flops 99999997952 | bytes 1 | tf_op jit(solution)/shard_map/rows/pallas_call | solution.py:175
  172.6 1.4 collective-permute-start.16
  174.0 2.7 %collective-permute-done.16 = bf16[128,128]{1,0:T(8,128)(2,1)S(1)} collective-permute-done((bf16[128,128]{1,0:T(8,128)(2,1)S(1)}, bf16[128,128]{1,0:T(8,128)(2,1)S(1)}, u32[]{:S(2)}, u32[]{:S(2)}) %collective-permute-start.16) | collective-permute-done | bytes 32800 | tf_op jit(solution)/shard_map/ppermute | solution.py:108
  176.6 4.6 %collective-permute-start.17 = (bf16[2,128,128]{2,1,0:T(8,128)(2,1)S(1)}, bf16[2,128,128]{2,1,0:T(8,128)(2,1)S(1)}, u32[]{:S(2)}, u32[]{:S(2)}) collective-permute-start(bf16[2,128,128]{2,1,0:T(8,128)(2,1)S(1)} %pad_maximum_fusion.1.refs_8_), channel_id=1, source_target_pairs={{0,4},{2,6},{4,0},{6,2},{8,12},{10,14},{12,8},{14,10},{1,5},{3,7},... | collective-permute-start | bytes 196616 | tf_op jit(solution)/shard_map/ppermute | solution.py:108
  181.3 2.5 %collective-permute-start.18 = (bf16[2,128,128]{2,1,0:T(8,128)(2,1)S(1)}, bf16[2,128,128]{2,1,0:T(8,128)(2,1)S(1)}, u32[]{:S(2)}, u32[]{:S(2)}) collective-permute-start(bf16[2,128,128]{2,1,0:T(8,128)(2,1)S(1)} %pad_maximum_fusion.1.refs_8_), channel_id=1, source_target_pairs={{0,8},{2,10},{4,12},{6,14},{8,0},{10,2},{12,4},{14,6},{1,9},{3,11}... | collective-permute-start | bytes 196616 | tf_op jit(solution)/shard_map/ppermute | solution.py:108
  183.8 1.2 collective-permute-start.19
  184.9 9.2 %collective-permute-done.18.refs_10_ = bf16[2,128,128]{2,1,0:T(8,128)(2,1)S(1)} collective-permute-done((bf16[2,128,128]{2,1,0:T(8,128)(2,1)S(1)}, bf16[2,128,128]{2,1,0:T(8,128)(2,1)S(1)}, u32[]{:S(2)}, u32[]{:S(2)}) %collective-permute-start.18) | collective-permute-done | bytes 65568 | tf_op jit(solution)/shard_map/ppermute | solution.py:108
  194.9 1.6 collective-permute-start.20
  196.7 10.0 %collective-permute-done.20.refs_13_ = bf16[8,64,512]{2,1,0:T(8,128)(2,1)S(1)} collective-permute-done((bf16[8,64,512]{2,1,0:T(8,128)(2,1)S(1)}, bf16[8,64,512]{2,1,0:T(8,128)(2,1)S(1)}, u32[]{:S(2)}, u32[]{:S(2)}) %collective-permute-start.20) | collective-permute-done | bytes 524320 | tf_op jit(solution)/shard_map/ppermute | solution.py:112
  206.7 5.2 %finish.1 = bf16[1024,1024]{1,0:T(8,128)(2,1)} custom-call(s32[4,16]{1,0:T(4,128)S(1)} %add_add_fusion.table, f32[128,1024]{1,0:T(8,128)} %copy-done.6, f32[128,1024]{1,0:T(8,128)} %copy-done.7, f32[128,1024]{1,0:T(8,128)} %copy-done.8, f32[128,1024]{1,0:T(8,128)} %copy-done.9, f32[128,1024]{1,0:T(8,128)} %copy-done.10, f32[128,1024]{1,0:T(8,128)} %copy-done.11, ...), custom_call_target="tpu_custom_call" | custom-call | flops 1 | bytes 1 | tf_op jit(solution)/shard_map/finish/pallas_call | solution.py:263
  (67 shorter events, 13.5 us)
Async XLA Ops:
  0.0 32.5 %copy-start.18 = (s32[64]{0:T(128)S(1)}, s32[64]{0:T(128)}, u32[]{:S(2)}) copy-start(s32[64]{0:T(128)} %param.10) | copy-start | bytes 772
  0.0 32.5 %copy-start.17 = (s32[2,8]{1,0:T(2,128)S(1)}, s32[2,8]{1,0:T(2,128)}, u32[]{:S(2)}) copy-start(s32[2,8]{1,0:T(2,128)} %param.11) | copy-start | bytes 196
  3.1 27.3 %collective-permute-start = (bf16[64,8192]{1,0:T(8,128)(2,1)}, bf16[64,8192]{1,0:T(8,128)(2,1)}, u32[]{:S(2)}, u32[]{:S(2)}) collective-permute-start(bf16[64,8192]{1,0:T(8,128)(2,1)} %get-tuple-element.156), channel_id=1, source_target_pairs={{0,4},{4,8},{8,12},{12,14},{14,10},{10,6},{6,2},{2,0},{1,5},{5,9},... | collective-permute-start | bytes 3145736 | tf_op jit(solution)/shard_map/ppermute | solution.py:108
  6.1 26.4 %collective-permute-start.1 = (bf16[64,8192]{1,0:T(8,128)(2,1)}, bf16[64,8192]{1,0:T(8,128)(2,1)}, u32[]{:S(2)}, u32[]{:S(2)}) collective-permute-start(bf16[64,8192]{1,0:T(8,128)(2,1)} %get-tuple-element.155), channel_id=1, source_target_pairs={{4,0},{8,4},{12,8},{14,12},{10,14},{6,10},{2,6},{0,2},{5,1},{9,5},... | collective-permute-start | bytes 3145736 | tf_op jit(solution)/shard_map/ppermute | solution.py:108
  6.1 46.6 %collective-permute-start.4 = (bf16[64,8192]{1,0:T(8,128)(2,1)}, bf16[64,8192]{1,0:T(8,128)(2,1)S(1)}, u32[]{:S(2)}, u32[]{:S(2)}) collective-permute-start(bf16[64,8192]{1,0:T(8,128)(2,1)} %get-tuple-element.155), channel_id=1, source_target_pairs={{0,4},{4,8},{8,12},{12,14},{14,10},{10,6},{6,2},{2,0},{1,5},{5,9},... | collective-permute-start | bytes 3145736 | tf_op jit(solution)/shard_map/ppermute | solution.py:108
  8.1 46.8 %collective-permute-start.5 = (bf16[64,8192]{1,0:T(8,128)(2,1)}, bf16[64,8192]{1,0:T(8,128)(2,1)}, u32[]{:S(2)}, u32[]{:S(2)}) collective-permute-start(bf16[64,8192]{1,0:T(8,128)(2,1)} %get-tuple-element.156), channel_id=1, source_target_pairs={{4,0},{8,4},{12,8},{14,12},{10,14},{6,10},{2,6},{0,2},{5,1},{9,5},... | collective-permute-start | bytes 3145736 | tf_op jit(solution)/shard_map/ppermute | solution.py:108
  40.9 5.9 %collective-permute-start.6 = (bf16[8,64,512]{2,1,0:T(8,128)(2,1)}, bf16[8,64,512]{2,1,0:T(8,128)(2,1)}, u32[]{:S(2)}, u32[]{:S(2)}) collective-permute-start(bf16[8,64,512]{2,1,0:T(8,128)(2,1)} %get-tuple-element.158), channel_id=1, source_target_pairs={{0,1},{1,0},{2,3},{3,2},{4,5},{5,4},{6,7},{7,6},{8,9},{9,8},{10,11... | collective-permute-start | bytes 1572872 | tf_op jit(solution)/shard_map/ppermute | solution.py:112
  44.9 12.1 %collective-permute-start.7 = (bf16[64,8192]{1,0:T(8,128)(2,1)}, bf16[64,8192]{1,0:T(8,128)(2,1)S(1)}, u32[]{:S(2)}, u32[]{:S(2)}) collective-permute-start(bf16[64,8192]{1,0:T(8,128)(2,1)} %get-tuple-element.153), channel_id=1, source_target_pairs={{0,1},{1,0},{2,3},{3,2},{4,5},{5,4},{6,7},{7,6},{8,9},{9,8},{10,11... | collective-permute-start | bytes 3145736 | tf_op jit(solution)/shard_map/ppermute | solution.py:112
  45.4 31.9 %collective-permute-start.2 = (bf16[64,8192]{1,0:T(8,128)(2,1)}, bf16[64,8192]{1,0:T(8,128)(2,1)}, u32[]{:S(2)}, u32[]{:S(2)}) collective-permute-start(bf16[64,8192]{1,0:T(8,128)(2,1)} %collective-permute-done.refs_0_), channel_id=1, source_target_pairs={{0,4},{4,8},{8,12},{12,14},{14,10},{10,6},{6,2},{2,0},{1,5},{5,9},... | collective-permute-start | bytes 3145736 | tf_op jit(solution)/shard_map/ppermute | solution.py:108
  46.8 30.6 %collective-permute-start.3 = (bf16[64,8192]{1,0:T(8,128)(2,1)}, bf16[64,8192]{1,0:T(8,128)(2,1)}, u32[]{:S(2)}, u32[]{:S(2)}) collective-permute-start(bf16[64,8192]{1,0:T(8,128)(2,1)} %collective-permute-done.1.refs_1_), channel_id=1, source_target_pairs={{4,0},{8,4},{12,8},{14,12},{10,14},{6,10},{2,6},{0,2},{5,1},{9,5},... | collective-permute-start | bytes 3145736 | tf_op jit(solution)/shard_map/ppermute | solution.py:108
  47.7 0.5 copy-start.14
  55.0 42.7 %collective-permute-start.10 = (bf16[64,8192]{1,0:T(8,128)(2,1)S(1)}, bf16[64,8192]{1,0:T(8,128)(2,1)S(1)}, u32[]{:S(2)}, u32[]{:S(2)}) collective-permute-start(bf16[64,8192]{1,0:T(8,128)(2,1)S(1)} %collective-permute-done.4.refs_1_), channel_id=1, source_target_pairs={{0,4},{4,8},{8,12},{12,14},{14,10},{10,6},{6,2},{2,0},{1,5},{5,9},... | collective-permute-start | bytes 3145736 | tf_op jit(solution)/shard_map/ppermute | solution.py:108
  56.6 43.3 %collective-permute-start.11 = (bf16[64,8192]{1,0:T(8,128)(2,1)}, bf16[64,8192]{1,0:T(8,128)(2,1)S(1)}, u32[]{:S(2)}, u32[]{:S(2)}) collective-permute-start(bf16[64,8192]{1,0:T(8,128)(2,1)} %collective-permute-done.5.refs_0_), channel_id=1, source_target_pairs={{4,0},{8,4},{12,8},{14,12},{10,14},{6,10},{2,6},{0,2},{5,1},{9,5},... | collective-permute-start | bytes 3145736 | tf_op jit(solution)/shard_map/ppermute | solution.py:108
  57.0 5.8 %copy-start.2 = (bf16[8192,1024]{1,0:T(8,128)(2,1)S(1)}, bf16[8192,1024]{1,0:T(8,128)(2,1)}, u32[]{:S(2)}) copy-start(bf16[8192,1024]{1,0:T(8,128)(2,1)} %weight.1) | copy-start | bytes 50331652
  62.8 2.8 %copy-start.3 = (bf16[1,128,8192]{2,1,0:T(8,128)(2,1)S(1)}, bf16[1,128,8192]{2,1,0:T(8,128)(2,1)}, u32[]{:S(2)}) copy-start(bf16[1,128,8192]{2,1,0:T(8,128)(2,1)} %param.6) | copy-start | bytes 6291460
  65.6 58.9 %copy-start = (bf16[8192,1152]{1,0:T(8,128)(2,1)}, bf16[8192,1152]{1,0:T(8,128)(2,1)S(1)}, u32[]{:S(2)}) copy-start(bf16[8192,1152]{1,0:T(8,128)(2,1)S(1)} %pin.1.weights) | copy-start | bytes 56623108
  69.0 1.6 copy-start.6
  76.5 0.8 copy-start.7
  77.5 42.7 %collective-permute-start.8 = (bf16[64,8192]{1,0:T(8,128)(2,1)}, bf16[64,8192]{1,0:T(8,128)(2,1)S(1)}, u32[]{:S(2)}, u32[]{:S(2)}) collective-permute-start(bf16[64,8192]{1,0:T(8,128)(2,1)} %collective-permute-done.2.refs_0_), channel_id=1, source_target_pairs={{0,4},{4,8},{8,12},{12,14},{14,10},{10,6},{6,2},{2,0},{1,5},{5,9},... | collective-permute-start | bytes 3145736 | tf_op jit(solution)/shard_map/ppermute | solution.py:108
  79.0 43.4 %collective-permute-start.9 = (bf16[64,8192]{1,0:T(8,128)(2,1)}, bf16[64,8192]{1,0:T(8,128)(2,1)}, u32[]{:S(2)}, u32[]{:S(2)}) collective-permute-start(bf16[64,8192]{1,0:T(8,128)(2,1)} %collective-permute-done.3.refs_1_), channel_id=1, source_target_pairs={{4,0},{8,4},{12,8},{14,12},{10,14},{6,10},{2,6},{0,2},{5,1},{9,5},... | collective-permute-start | bytes 3145736 | tf_op jit(solution)/shard_map/ppermute | solution.py:108
  83.6 0.8 copy-start.8
  88.9 0.8 copy-start.9
  99.8 42.8 %collective-permute-start.14 = (bf16[64,8192]{1,0:T(8,128)(2,1)S(1)}, bf16[64,8192]{1,0:T(8,128)(2,1)S(1)}, u32[]{:S(2)}, u32[]{:S(2)}) collective-permute-start(bf16[64,8192]{1,0:T(8,128)(2,1)S(1)} %collective-permute-done.10.refs_1_), channel_id=1, source_target_pairs={{0,4},{4,8},{8,12},{12,14},{14,10},{10,6},{6,2},{2,0},{1,5},{5,9},... | collective-permute-start | bytes 3145736 | tf_op jit(solution)/shard_map/ppermute | solution.py:108
  101.4 43.4 %collective-permute-start.15 = (bf16[64,8192]{1,0:T(8,128)(2,1)S(1)}, bf16[64,8192]{1,0:T(8,128)(2,1)S(1)}, u32[]{:S(2)}, u32[]{:S(2)}) collective-permute-start(bf16[64,8192]{1,0:T(8,128)(2,1)S(1)} %collective-permute-done.11.refs_0_), channel_id=1, source_target_pairs={{4,0},{8,4},{12,8},{14,12},{10,14},{6,10},{2,6},{0,2},{5,1},{9,5},... | collective-permute-start | bytes 3145736 | tf_op jit(solution)/shard_map/ppermute | solution.py:108
  105.3 0.8 copy-start.10
  122.4 42.8 %collective-permute-start.12 = (bf16[64,8192]{1,0:T(8,128)(2,1)S(1)}, bf16[64,8192]{1,0:T(8,128)(2,1)}, u32[]{:S(2)}, u32[]{:S(2)}) collective-permute-start(bf16[64,8192]{1,0:T(8,128)(2,1)S(1)} %collective-permute-done.8.refs_0_), channel_id=1, source_target_pairs={{0,4},{4,8},{8,12},{12,14},{14,10},{10,6},{6,2},{2,0},{1,5},{5,9},... | collective-permute-start | bytes 3145736 | tf_op jit(solution)/shard_map/ppermute | solution.py:108
  124.0 43.4 %collective-permute-start.13 = (bf16[64,8192]{1,0:T(8,128)(2,1)}, bf16[64,8192]{1,0:T(8,128)(2,1)}, u32[]{:S(2)}, u32[]{:S(2)}) collective-permute-start(bf16[64,8192]{1,0:T(8,128)(2,1)} %collective-permute-done.9.refs_1_), channel_id=1, source_target_pairs={{4,0},{8,4},{12,8},{14,12},{10,14},{6,10},{2,6},{0,2},{5,1},{9,5},... | collective-permute-start | bytes 3145736 | tf_op jit(solution)/shard_map/ppermute | solution.py:108
  128.6 0.8 copy-start.11
  144.8 1.0 copy-start.4
  146.8 47.4 %all-to-all-start = ((bf16[8,2,64,512]{3,2,1,0:T(8,128)(2,1)}), bf16[8,2,64,512]{3,2,1,0:T(8,128)(2,1)S(1)}, u32[]{:S(2)}, u32[]{:S(2)}) async-start(bf16[8,2,64,512]{3,2,1,0:T(8,128)(2,1)} %copy.9), calls=%async_computation | async-start | bytes 2097152 | tf_op jit(solution)/shard_map/all_to_all | solution.py:348
  151.6 6.4 %copy-start.1 = (bf16[8192,1152]{1,0:T(8,128)(2,1)S(1)}, bf16[8192,1152]{1,0:T(8,128)(2,1)}, u32[]{:S(2)}) copy-start(bf16[8192,1152]{1,0:T(8,128)(2,1)} %copy-done) | copy-start | bytes 56623108
  158.0 1.2 copy-start.5
  162.7 0.8 copy-start.12
  167.3 29.3 %copy-start.15 = (s32[16]{0:T(128)S(1)}, s32[16]{0:T(128)}, u32[]{:S(2)}) copy-start(s32[16]{0:T(128)} %copy-done.14) | copy-start | bytes 196
  167.3 29.3 %copy-start.16 = (s32[1,16]{1,0:T(1,128)S(1)}, s32[1,16]{1,0:T(1,128)}, u32[]{:S(2)}) copy-start(s32[1,16]{1,0:T(1,128)} %get-tuple-element.161) | copy-start | bytes 196
  171.8 0.8 copy-start.13
  172.6 4.0 %collective-permute-start.16 = (bf16[128,128]{1,0:T(8,128)(2,1)S(1)}, bf16[128,128]{1,0:T(8,128)(2,1)S(1)}, u32[]{:S(2)}, u32[]{:S(2)}) collective-permute-start(bf16[128,128]{1,0:T(8,128)(2,1)S(1)} %get-tuple-element.143), channel_id=1, source_target_pairs={{0,2},{2,0},{4,6},{6,4},{8,10},{10,8},{12,14},{14,12},{1,3},{3,1},... | collective-permute-start | bytes 98312 | tf_op jit(solution)/shard_map/ppermute | solution.py:108
  176.6 8.3 %collective-permute-start.17 = (bf16[2,128,128]{2,1,0:T(8,128)(2,1)S(1)}, bf16[2,128,128]{2,1,0:T(8,128)(2,1)S(1)}, u32[]{:S(2)}, u32[]{:S(2)}) collective-permute-start(bf16[2,128,128]{2,1,0:T(8,128)(2,1)S(1)} %pad_maximum_fusion.1.refs_8_), channel_id=1, source_target_pairs={{0,4},{2,6},{4,0},{6,2},{8,12},{10,14},{12,8},{14,10},{1,5},{3,7},... | collective-permute-start | bytes 196616 | tf_op jit(solution)/shard_map/ppermute | solution.py:108
  181.3 12.9 %collective-permute-start.18 = (bf16[2,128,128]{2,1,0:T(8,128)(2,1)S(1)}, bf16[2,128,128]{2,1,0:T(8,128)(2,1)S(1)}, u32[]{:S(2)}, u32[]{:S(2)}) collective-permute-start(bf16[2,128,128]{2,1,0:T(8,128)(2,1)S(1)} %pad_maximum_fusion.1.refs_8_), channel_id=1, source_target_pairs={{0,8},{2,10},{4,12},{6,14},{8,0},{10,2},{12,4},{14,6},{1,9},{3,11}... | collective-permute-start | bytes 196616 | tf_op jit(solution)/shard_map/ppermute | solution.py:108
  183.8 10.4 %collective-permute-start.19 = (bf16[2,128,128]{2,1,0:T(8,128)(2,1)S(1)}, bf16[2,128,128]{2,1,0:T(8,128)(2,1)S(1)}, u32[]{:S(2)}, u32[]{:S(2)}) collective-permute-start(bf16[2,128,128]{2,1,0:T(8,128)(2,1)S(1)} %pad_maximum_fusion.1.refs_8_), channel_id=1, source_target_pairs={{0,12},{2,14},{4,8},{6,10},{8,4},{10,6},{12,0},{14,2},{1,13},{3,15... | collective-permute-start | bytes 196616 | tf_op jit(solution)/shard_map/ppermute | solution.py:108
  194.9 11.8 %collective-permute-start.20 = (bf16[8,64,512]{2,1,0:T(8,128)(2,1)S(1)}, bf16[8,64,512]{2,1,0:T(8,128)(2,1)S(1)}, u32[]{:S(2)}, u32[]{:S(2)}) collective-permute-start(bf16[8,64,512]{2,1,0:T(8,128)(2,1)S(1)} %take.1.refs_12_), channel_id=1, source_target_pairs={{0,16},{16,0},{1,17},{17,1},{2,18},{18,2},{3,19},{19,3},{4,20},{20... | collective-permute-start | bytes 1572872 | tf_op jit(solution)/shard_map/ppermute | solution.py:112

commit v19 on v16

--- a/solution.py
+++ b/solution.py
@@ -229,12 +229,15 @@
     )(table, got)
 
 
-def finish_kernel(table, *refs):
-    bases, gathered, refs = refs[:8], refs[8:12], refs[12:]
-    up_mine, up_other, out, base, shrunk, rows, base_sems, sems = refs
-    part = up_mine.shape[2]
-    group = table[3, 0]
-    fetches = [pltpu.make_async_copy(bases[g], base.at[g], base_sems.at[g]) for g in range(8)]
+def finish_kernel(own_side, table, *refs):
+    bases, gathered, up, refs = refs[:8], refs[8:12], refs[12], refs[-6:]
+    out, base, shrunk, rows, base_sems, sems = refs
+    part = up.shape[2]
+    side = table[3, 0] if own_side else 1 - table[3, 0]
+    cut = pl.ds(pl.multiple_of(side * part, part), part)
+    fetches = [
+        pltpu.make_async_copy(bases[g].at[:, cut], base.at[g], base_sems.at[g]) for g in range(8)
+    ]
     for fetch in fetches:
         fetch.start()
     for i, pair in enumerate(gathered):
@@ -247,42 +250,42 @@
         own = pl.ds(half * HALF, HALF)
         both = shrunk[table[1, i], own, :].astype(jnp.float32)
         value = jnp.where(table[2, i] > 0, both[:, 64:], both[:, :64]).astype(jnp.bfloat16)
-        for up, side in ((up_mine, group), (up_other, 1 - group)):
-            cut = pl.ds(pl.multiple_of(side * part, part), part)
-            grown = jnp.dot(value, up[block], preferred_element_type=jnp.float32)
-            rows[i, :, cut] = (base[i // 2, own, cut] + 0.5 * grown).astype(rows.dtype)
+        grown = jnp.dot(value, up[block], preferred_element_type=jnp.float32)
+        rows[i] = (base[i // 2, own, :] + 0.5 * grown).astype(rows.dtype)
         to = pl.ds(pl.multiple_of((2 * block + half) * HALF, HALF), HALF)
-        copies.append(pltpu.make_async_copy(rows.at[i], out.at[to], sems.at[i]))
+        copies.append(pltpu.make_async_copy(rows.at[i], out.at[to, cut], sems.at[i]))
         copies[-1].start()
     for copy in copies:
         copy.wait()
 
 
-def finish_call(table, bases, gathered, up_mine, up_other):
+def finish_call(own_side, table, bases, gathered, up, into):
     columns = bases[0].shape[1]
-    return pl.pallas_call(
-        finish_kernel,
-        in_specs=[pl.BlockSpec(memory_space=pltpu.SMEM)]
-        + [pl.BlockSpec(memory_space=pl.ANY)] * 8
-        + in_vmem(6),
+    part = up.shape[2]
+    operands = [pltpu.with_memory_space_constraint(base, pltpu.HBM) for base in bases]
+    operands += [*gathered, up]
+    specs = [pl.BlockSpec(memory_space=pl.ANY)] * 8 + in_vmem(5)
+    aliases = {}
+    if into is not None:
+        aliases = {1 + len(operands): 0}
+        operands.append(pltpu.with_memory_space_constraint(into, pltpu.HBM))
+        specs.append(pl.BlockSpec(memory_space=pltpu.HBM))
+    return pl.pallas_call(
+        functools.partial(finish_kernel, own_side),
+        in_specs=[pl.BlockSpec(memory_space=pltpu.SMEM)] + specs,
         out_specs=pl.BlockSpec(memory_space=pltpu.HBM),
         out_shape=jax.ShapeDtypeStruct((8 * BLOCK, columns), jnp.bfloat16),
         scratch_shapes=[
-            pltpu.VMEM((8, BLOCK, columns), jnp.float32),
+            pltpu.VMEM((8, BLOCK, part), jnp.float32),
             pltpu.VMEM((8,) + gathered[0].shape[1:], jnp.bfloat16),
-            pltpu.VMEM((16, HALF, columns), jnp.bfloat16),
+            pltpu.VMEM((16, HALF, part), jnp.bfloat16),
             pltpu.SemaphoreType.DMA((8,)),
             pltpu.SemaphoreType.DMA((16,)),
         ],
+        input_output_aliases=aliases,
         name="finish",
         **settings(),
-    )(
-        table,
-        *[pltpu.with_memory_space_constraint(base, pltpu.HBM) for base in bases],
-        *gathered,
-        up_mine,
-        up_other,
-    )
+    )(table, *operands)
 
 
 def chain_body(
@@ -364,7 +367,9 @@
     home, core = owners // 2, owners % 2
     where = 2 * ((home // 2) ^ z) + ((home % 2) ^ y)
     table = jnp.stack([blocks, where, core != store, jnp.broadcast_to(group, (16,))])
-    return finish_call(table.astype(jnp.int32), bases, everyone, up_mine, up_other)[None]
+    table = table.astype(jnp.int32)
+    query = finish_call(True, table, bases, everyone, up_mine, None)
+    return finish_call(False, table, bases, everyone, up_other, query)[None]
 
 
 def body(tokens, *rest):

time: 208 us -> 210 us (level)
  Pallas kernels: 44.3 us -> 48.6 us
  waiting for transfers between devices: 96.7 us -> 93.9 us
    pallas_call x1 -> x2, Pallas kernels: 5.23 us -> 9.59 us  [finish_call(): pl.pallas_call(functools.partial(finish_kernel, own_side), in_specs=[pl.B...]
    ppermute x3, waiting for transfers between devices: 2.78 us -> 0.01 us  [swap(): return lax.ppermute(value, axis, [(0, 1), (1, 0)])]
  transfers between devices with their start and end apart: 22 -> 22, of which waited for: 18 -> 17; matrix products, arithmetic and copies ran while one was open for 5% -> 5% of each run, Pallas kernels for 18% -> 21%
where the time goes in v19:
time: 210 us; the launch traced here: 209 us
  waiting for transfers between devices  93.9 us (45%)
  Pallas kernels  48.6 us (23%)
  local copies, waits for them, and re-layouts  30.4 us (14%)
  starting transfers between devices  28 us (13%)
  between operations  4.47 us (2%)
  other arithmetic  3.82 us (2%)
    ppermute x18, waiting for transfers between devices, send(): return lax.ppermute(value, 'tensor', pairs)  81.2 us
    pallas_call x8, Pallas kernels, rows_call(): pl.pallas_call(functools.partial(rows_kernel, group), in_specs=[pl.BlockS...  33.4 us
    unnamed x38, local copies, waits for them, and re-layouts  21.5 us
    ppermute x18, starting transfers between devices, send(): return lax.ppermute(value, 'tensor', pairs)  21 us
    all_to_all x1, waiting for transfers between devices, chain_body(): lax.all_to_all(up_sent, 'tensor', split_axis=0, concat_axis=0, tiled=True)  12.7 us
    pallas_call x2, Pallas kernels, finish_call(): pl.pallas_call(functools.partial(finish_kernel, own_side), in_specs=[pl.B...  9.59 us
    all_to_all x1, starting transfers between devices, chain_body(): lax.all_to_all(up_sent, 'tensor', split_axis=0, concat_axis=0, tiled=True)  4.82 us
  transfers between devices with their start and end apart: 22, of which 17 were waited for; matrix products, arithmetic and copies ran while one was open for 5% of the time, Pallas kernels for 21%

profile of v19, /device:TPU:0, one launch (start us, length us, event | category | flops | bytes accessed | tf_op | source)
XLA Modules:
  0.0 209.2 jit_solution(6157908362049651856)
XLA Ops:
  0.0 3.1 %slice_bitcast_fusion = (bf16[64,8192]{1,0:T(8,128)(2,1)}, bf16[64,8192]{1,0:T(8,128)(2,1)}) fusion(bf16[1,128,8192]{2,1,0:T(8,128)(2,1)} %param.6), kind=kLoop, calls=%fused_computation.3 | loop fusion | bytes 4194304 | tf_op jit(solution)/shard_map/slice | solution.py:301
  3.1 3.0 %collective-permute-start = (bf16[64,8192]{1,0:T(8,128)(2,1)}, bf16[64,8192]{1,0:T(8,128)(2,1)}, u32[]{:S(2)}, u32[]{:S(2)}) collective-permute-start(bf16[64,8192]{1,0:T(8,128)(2,1)} %get-tuple-element.148), channel_id=1, source_target_pairs={{0,4},{4,8},{8,12},{12,14},{14,10},{10,6},{6,2},{2,0},{1,5},{5,9},... | collective-permute-start | bytes 3145736 | tf_op jit(solution)/shard_map/ppermute | solution.py:108
  6.1 2.0 collective-permute-start.4
  8.1 22.2 %collective-permute-done.refs_0_ = bf16[64,8192]{1,0:T(8,128)(2,1)} collective-permute-done((bf16[64,8192]{1,0:T(8,128)(2,1)}, bf16[64,8192]{1,0:T(8,128)(2,1)}, u32[]{:S(2)}, u32[]{:S(2)}) %collective-permute-start) | collective-permute-done | bytes 1048608 | tf_op jit(solution)/shard_map/ppermute | solution.py:108
  30.4 2.2 %collective-permute-done.1.refs_1_ = bf16[64,8192]{1,0:T(8,128)(2,1)} collective-permute-done((bf16[64,8192]{1,0:T(8,128)(2,1)}, bf16[64,8192]{1,0:T(8,128)(2,1)}, u32[]{:S(2)}, u32[]{:S(2)}) %collective-permute-start.1) | collective-permute-done | bytes 1048608 | tf_op jit(solution)/shard_map/ppermute | solution.py:108
  36.2 1.4 pad_add_fusion.table
  37.6 2.2 %pack.1 = bf16[2,8,64,512]{3,2,1,0:T(8,128)(2,1)S(1)} custom-call(s32[3]{0:T(128)S(1)} %pad_add_fusion.table, bf16[4,64,8192]{2,1,0:T(8,128)(2,1)} %up.1), custom_call_target="tpu_custom_call" | custom-call | flops 1 | bytes 1 | tf_op jit(solution)/shard_map/pack/pallas_call | solution.py:198
  42.2 2.7 %dynamic-slice_bitcast_fusion = (bf16[64,8192]{1,0:T(8,128)(2,1)}, bf16[64,8192]{1,0:T(8,128)(2,1)S(1)}) fusion(bf16[4,64,8192]{2,1,0:T(8,128)(2,1)} %param.8, s32[]{:T(128)S(6)} %select_n.166, s32[]{:T(128)S(6)} %select_n.165), kind=kLoop, calls=%fused_computation.1 | loop fusion | bytes 4194312 | tf_op jit(solution)/shard_map/jit(dynamic_index_in_dim)/squeeze | solution.py:321
  45.5 1.2 collective-permute-start.2
  48.3 1.3 pad_maximum_fusion
  49.6 3.1 %collective-permute-done.4.refs_1_ = bf16[64,8192]{1,0:T(8,128)(2,1)S(1)} collective-permute-done((bf16[64,8192]{1,0:T(8,128)(2,1)}, bf16[64,8192]{1,0:T(8,128)(2,1)S(1)}, u32[]{:S(2)}, u32[]{:S(2)}) %collective-permute-start.4) | collective-permute-done | bytes 1048608 | tf_op jit(solution)/shard_map/ppermute | solution.py:108
  52.7 2.3 %collective-permute-done.5.refs_0_ = bf16[64,8192]{1,0:T(8,128)(2,1)} collective-permute-done((bf16[64,8192]{1,0:T(8,128)(2,1)}, bf16[64,8192]{1,0:T(8,128)(2,1)}, u32[]{:S(2)}, u32[]{:S(2)}) %collective-permute-start.5) | collective-permute-done | bytes 1048608 | tf_op jit(solution)/shard_map/ppermute | solution.py:108
  55.0 1.6 collective-permute-start.10
  57.0 5.8 %copy-done.2 = bf16[8192,1024]{1,0:T(8,128)(2,1)S(1)} copy-done((bf16[8192,1024]{1,0:T(8,128)(2,1)S(1)}, bf16[8192,1024]{1,0:T(8,128)(2,1)}, u32[]{:S(2)}) %copy-start.2) | copy-done | bytes 16777240
  62.8 2.8 %pin.1.weights = bf16[8192,1152]{1,0:T(8,128)(2,1)S(1)} custom-call(bf16[8192,1024]{1,0:T(8,128)(2,1)S(1)} %copy-done.2, bf16[64,8192]{1,0:T(8,128)(2,1)S(1)} %get-tuple-element.146.own, bf16[64,8192]{1,0:T(8,128)(2,1)S(1)} %collective-permute-done.7.swapped), custom_call_target="tpu_custom_call" | custom-call | flops 1 | bytes 1 | tf_op jit(solution)/shard_map/pin/pallas_call | solution.py:138
  65.6 3.4 %rows.8 = (f32[128,1024]{1,0:T(8,128)S(1)}, bf16[128,128]{1,0:T(8,128)(2,1)S(1)}) custom-call(s32[2,16]{1,0:T(2,128)S(1)} %add_convert_fusion.table, bf16[8192,1152]{1,0:T(8,128)(2,1)S(1)} %pin.1.weights, bf16[128,8192]{1,0:T(8,128)(2,1)S(1)} %bitcast.62, bf16[128,128]{1,0:T(8,128)(2,1)S(1)} %broadcast_in_dim.49.refs_1_), custom_call_target="tpu_custom_call" | custom-call | flops 1 | bytes 1 | tf_op jit(solution)/shard_map/rows/pallas_call | solution.py:175
  69.0 1.6 copy-done.4
  70.6 5.9 %rows.9 = (f32[128,1024]{1,0:T(8,128)S(1)}, bf16[128,128]{1,0:T(8,128)(2,1)S(1)}) custom-call(s32[2,16]{1,0:T(2,128)S(1)} %add_convert_fusion.table, bf16[8192,1152]{1,0:T(8,128)(2,1)S(1)} %pin.1.weights, bf16[64,8192]{1,0:T(8,128)(2,1)} %collective-permute-done.refs_0_, bf16[64,8192]{1,0:T(8,128)(2,1)} %collective-permute-done.1.refs_1_, ...), custom_call_target="tpu_custom_call" | custom-call | flops 1 | bytes 1 | tf_op jit(solution)/shard_map/rows/pallas_call | solution.py:175
  77.5 1.6 collective-permute-start.8
  79.5 4.1 %rows.10 = (f32[128,1024]{1,0:T(8,128)S(1)}, bf16[128,128]{1,0:T(8,128)(2,1)S(1)}) custom-call(s32[2,16]{1,0:T(2,128)S(1)} %add_convert_fusion.table, bf16[8192,1152]{1,0:T(8,128)(2,1)S(1)} %pin.1.weights, bf16[64,8192]{1,0:T(8,128)(2,1)} %collective-permute-done.5.refs_0_, bf16[64,8192]{1,0:T(8,128)(2,1)S(1)} %collective-permute-done.4.refs_1_, ...), custom_call_target="tpu_custom_call" | custom-call | flops 1 | bytes 1 | tf_op jit(solution)/shard_map/rows/pallas_call | solution.py:175
  84.4 4.4 %rows.11 = (f32[128,1024]{1,0:T(8,128)S(1)}, bf16[128,128]{1,0:T(8,128)(2,1)S(1)}) custom-call(s32[2,16]{1,0:T(2,128)S(1)} %add_convert_fusion.table, bf16[8192,1152]{1,0:T(8,128)(2,1)S(1)} %pin.1.weights, bf16[64,8192]{1,0:T(8,128)(2,1)} %collective-permute-done.2.refs_0_, bf16[64,8192]{1,0:T(8,128)(2,1)} %collective-permute-done.3.refs_1_, ...), custom_call_target="tpu_custom_call" | custom-call | flops 1 | bytes 1 | tf_op jit(solution)/shard_map/rows/pallas_call | solution.py:175
  89.7 8.0 %collective-permute-done.10.refs_1_ = bf16[64,8192]{1,0:T(8,128)(2,1)S(1)} collective-permute-done((bf16[64,8192]{1,0:T(8,128)(2,1)S(1)}, bf16[64,8192]{1,0:T(8,128)(2,1)S(1)}, u32[]{:S(2)}, u32[]{:S(2)}) %collective-permute-start.10) | collective-permute-done | bytes 1048608 | tf_op jit(solution)/shard_map/ppermute | solution.py:108
  97.7 2.2 %collective-permute-done.11.refs_0_ = bf16[64,8192]{1,0:T(8,128)(2,1)S(1)} collective-permute-done((bf16[64,8192]{1,0:T(8,128)(2,1)}, bf16[64,8192]{1,0:T(8,128)(2,1)S(1)}, u32[]{:S(2)}, u32[]{:S(2)}) %collective-permute-start.11) | collective-permute-done | bytes 1048608 | tf_op jit(solution)/shard_map/ppermute | solution.py:108
  99.8 1.6 collective-permute-start.14
  101.8 3.4 %rows.12 = (f32[128,1024]{1,0:T(8,128)S(1)}, bf16[128,128]{1,0:T(8,128)(2,1)S(1)}) custom-call(s32[2,16]{1,0:T(2,128)S(1)} %add_convert_fusion.table, bf16[8192,1152]{1,0:T(8,128)(2,1)S(1)} %pin.1.weights, bf16[64,8192]{1,0:T(8,128)(2,1)S(1)} %collective-permute-done.11.refs_0_, bf16[64,8192]{1,0:T(8,128)(2,1)S(1)} %collective-permute-done.10.refs_1_, ...), custom_call_target="tpu_custom_call" | custom-call | flops 1 | bytes 1 | tf_op jit(solution)/shard_map/rows/pallas_call | solution.py:175
  106.1 14.0 %collective-permute-done.8.refs_0_ = bf16[64,8192]{1,0:T(8,128)(2,1)S(1)} collective-permute-done((bf16[64,8192]{1,0:T(8,128)(2,1)}, bf16[64,8192]{1,0:T(8,128)(2,1)S(1)}, u32[]{:S(2)}, u32[]{:S(2)}) %collective-permute-start.8) | collective-permute-done | bytes 1048608 | tf_op jit(solution)/shard_map/ppermute | solution.py:108
  120.1 2.3 %collective-permute-done.9.refs_1_ = bf16[64,8192]{1,0:T(8,128)(2,1)} collective-permute-done((bf16[64,8192]{1,0:T(8,128)(2,1)}, bf16[64,8192]{1,0:T(8,128)(2,1)}, u32[]{:S(2)}, u32[]{:S(2)}) %collective-permute-start.9) | collective-permute-done | bytes 1048608 | tf_op jit(solution)/shard_map/ppermute | solution.py:108
  122.4 1.6 collective-permute-start.12
  124.4 4.2 %rows.13 = (f32[128,1024]{1,0:T(8,128)S(1)}, bf16[128,128]{1,0:T(8,128)(2,1)S(1)}) custom-call(s32[2,16]{1,0:T(2,128)S(1)} %add_convert_fusion.table, bf16[8192,1152]{1,0:T(8,128)(2,1)S(1)} %pin.1.weights, bf16[64,8192]{1,0:T(8,128)(2,1)S(1)} %collective-permute-done.8.refs_0_, bf16[64,8192]{1,0:T(8,128)(2,1)} %collective-permute-done.9.refs_1_, ...), custom_call_target="tpu_custom_call" | custom-call | flops 1 | bytes 1 | tf_op jit(solution)/shard_map/rows/pallas_call | solution.py:175
  129.4 13.2 %collective-permute-done.14.refs_1_ = bf16[64,8192]{1,0:T(8,128)(2,1)S(1)} collective-permute-done((bf16[64,8192]{1,0:T(8,128)(2,1)S(1)}, bf16[64,8192]{1,0:T(8,128)(2,1)S(1)}, u32[]{:S(2)}, u32[]{:S(2)}) %collective-permute-start.14) | collective-permute-done | bytes 1048608 | tf_op jit(solution)/shard_map/ppermute | solution.py:108
  142.6 2.2 %collective-permute-done.15.refs_0_ = bf16[64,8192]{1,0:T(8,128)(2,1)S(1)} collective-permute-done((bf16[64,8192]{1,0:T(8,128)(2,1)S(1)}, bf16[64,8192]{1,0:T(8,128)(2,1)S(1)}, u32[]{:S(2)}, u32[]{:S(2)}) %collective-permute-start.15) | collective-permute-done | bytes 1048608 | tf_op jit(solution)/shard_map/ppermute | solution.py:108
  146.8 4.8 %all-to-all-start = ((bf16[8,2,64,512]{3,2,1,0:T(8,128)(2,1)}), bf16[8,2,64,512]{3,2,1,0:T(8,128)(2,1)S(1)}, u32[]{:S(2)}, u32[]{:S(2)}) async-start(bf16[8,2,64,512]{3,2,1,0:T(8,128)(2,1)} %copy.10), calls=%async_computation | async-start | bytes 2097152 | tf_op jit(solution)/shard_map/all_to_all | solution.py:351
  151.6 6.4 %copy-done.1 = bf16[8192,1152]{1,0:T(8,128)(2,1)S(1)} copy-done((bf16[8192,1152]{1,0:T(8,128)(2,1)S(1)}, bf16[8192,1152]{1,0:T(8,128)(2,1)}, u32[]{:S(2)}) %copy-start.1) | copy-done | bytes 18874392
  158.0 1.2 copy-done.13
  159.2 3.5 %rows.14 = (f32[128,1024]{1,0:T(8,128)S(1)}, bf16[128,128]{1,0:T(8,128)(2,1)S(1)}) custom-call(s32[2,16]{1,0:T(2,128)S(1)} %add_convert_fusion.table, bf16[8192,1152]{1,0:T(8,128)(2,1)S(1)} %copy-done.1, bf16[64,8192]{1,0:T(8,128)(2,1)S(1)} %copy-done.13, bf16[64,8192]{1,0:T(8,128)(2,1)S(1)} %collective-permute-done.14.refs_1_, ...), custom_call_target="tpu_custom_call" | custom-call | flops 1 | bytes 1 | tf_op jit(solution)/shard_map/rows/pallas_call | solution.py:175
  163.5 1.7 collective-permute-done.12.refs_0_
  165.2 2.2 %collective-permute-done.13.refs_1_ = bf16[64,8192]{1,0:T(8,128)(2,1)} collective-permute-done((bf16[64,8192]{1,0:T(8,128)(2,1)}, bf16[64,8192]{1,0:T(8,128)(2,1)}, u32[]{:S(2)}, u32[]{:S(2)}) %collective-permute-start.13) | collective-permute-done | bytes 1048608 | tf_op jit(solution)/shard_map/ppermute | solution.py:108
  167.3 4.4 %rows.15 = (f32[128,1024]{1,0:T(8,128)S(1)}, bf16[128,128]{1,0:T(8,128)(2,1)S(1)}) custom-call(s32[2,16]{1,0:T(2,128)S(1)} %add_convert_fusion.table, bf16[8192,1152]{1,0:T(8,128)(2,1)S(1)} %copy-done.1, bf16[64,8192]{1,0:T(8,128)(2,1)} %collective-permute-done.12.refs_0_, bf16[64,8192]{1,0:T(8,128)(2,1)} %collective-permute-done.13.refs_1_, ...), custom_call_target="tpu_custom_call" | custom-call | flops 99999997952 | bytes 1 | tf_op jit(solution)/shard_map/rows/pallas_call | solution.py:175
  172.6 1.4 collective-permute-start.16
  174.1 2.4 %collective-permute-done.16 = bf16[128,128]{1,0:T(8,128)(2,1)S(1)} collective-permute-done((bf16[128,128]{1,0:T(8,128)(2,1)S(1)}, bf16[128,128]{1,0:T(8,128)(2,1)S(1)}, u32[]{:S(2)}, u32[]{:S(2)}) %collective-permute-start.16) | collective-permute-done | bytes 32800 | tf_op jit(solution)/shard_map/ppermute | solution.py:108
  176.6 12.7 %all-to-all-done = bf16[8,2,64,512]{3,2,1,0:T(8,128)(2,1)S(1)} async-done(((bf16[8,2,64,512]{3,2,1,0:T(8,128)(2,1)}), bf16[8,2,64,512]{3,2,1,0:T(8,128)(2,1)S(1)}, u32[]{:S(2)}, u32[]{:S(2)}) %all-to-all-start) | async-done | bytes 1048608 | tf_op jit(solution)/shard_map/all_to_all | solution.py:351
  190.0 1.6 collective-permute-start.20
  191.6 1.7 collective-permute-start.18
  193.4 2.6 %collective-permute-start.19 = (bf16[2,128,128]{2,1,0:T(8,128)(2,1)S(1)}, bf16[2,128,128]{2,1,0:T(8,128)(2,1)S(1)}, u32[]{:S(2)}, u32[]{:S(2)}) collective-permute-start(bf16[2,128,128]{2,1,0:T(8,128)(2,1)S(1)} %pad_maximum_fusion.1.refs_8_), channel_id=1, source_target_pairs={{0,12},{2,14},{4,8},{6,10},{8,4},{10,6},{12,0},{14,2},{1,13},{3,15... | collective-permute-start | bytes 196616 | tf_op jit(solution)/shard_map/ppermute | solution.py:108
  196.1 1.2 collective-permute-done.18.refs_10_
  197.3 2.1 %collective-permute-done.19.refs_11_ = bf16[2,128,128]{2,1,0:T(8,128)(2,1)S(1)} collective-permute-done((bf16[2,128,128]{2,1,0:T(8,128)(2,1)S(1)}, bf16[2,128,128]{2,1,0:T(8,128)(2,1)S(1)}, u32[]{:S(2)}, u32[]{:S(2)}) %collective-permute-start.19) | collective-permute-done | bytes 65568 | tf_op jit(solution)/shard_map/ppermute | solution.py:108
  199.4 4.8 %finish.2.refs_13_ = bf16[1024,1024]{1,0:T(8,128)(2,1)} custom-call(s32[4,16]{1,0:T(4,128)S(1)} %add_add_fusion.table, f32[128,1024]{1,0:T(8,128)} %copy-done.4, f32[128,1024]{1,0:T(8,128)} %copy-done.5, f32[128,1024]{1,0:T(8,128)} %copy-done.6, f32[128,1024]{1,0:T(8,128)} %copy-done.7, f32[128,1024]{1,0:T(8,128)} %copy-done.8, f32[128,1024]{1,0:T(8,128)} %copy-done.9, ...), custom_call_target="tpu_custom_call" | custom-call | flops 1 | bytes 1 | tf_op jit(solution)/shard_map/finish/pallas_call | solution.py:273
  204.2 4.8 %finish.3 = bf16[1024,1024]{1,0:T(8,128)(2,1)} custom-call(s32[4,16]{1,0:T(4,128)S(1)} %add_add_fusion.table, f32[128,1024]{1,0:T(8,128)} %copy-done.4, f32[128,1024]{1,0:T(8,128)} %copy-done.5, f32[128,1024]{1,0:T(8,128)} %copy-done.6, f32[128,1024]{1,0:T(8,128)} %copy-done.7, f32[128,1024]{1,0:T(8,128)} %copy-done.8, ...), custom_call_target="tpu_custom_call", output_to_operand_aliasing={{}: (14, {})} | custom-call | flops 1 | bytes 1 | tf_op jit(solution)/shard_map/finish/pallas_call | solution.py:273
  (68 shorter events, 14.9 us)
Async XLA Ops:
  0.0 32.5 %copy-start.18 = (s32[64]{0:T(128)S(1)}, s32[64]{0:T(128)}, u32[]{:S(2)}) copy-start(s32[64]{0:T(128)} %param.10) | copy-start | bytes 772
  0.0 32.5 %copy-start.17 = (s32[2,8]{1,0:T(2,128)S(1)}, s32[2,8]{1,0:T(2,128)}, u32[]{:S(2)}) copy-start(s32[2,8]{1,0:T(2,128)} %param.11) | copy-start | bytes 196
  3.1 27.3 %collective-permute-start = (bf16[64,8192]{1,0:T(8,128)(2,1)}, bf16[64,8192]{1,0:T(8,128)(2,1)}, u32[]{:S(2)}, u32[]{:S(2)}) collective-permute-start(bf16[64,8192]{1,0:T(8,128)(2,1)} %get-tuple-element.148), channel_id=1, source_target_pairs={{0,4},{4,8},{8,12},{12,14},{14,10},{10,6},{6,2},{2,0},{1,5},{5,9},... | collective-permute-start | bytes 3145736 | tf_op jit(solution)/shard_map/ppermute | solution.py:108
  6.1 26.4 %collective-permute-start.1 = (bf16[64,8192]{1,0:T(8,128)(2,1)}, bf16[64,8192]{1,0:T(8,128)(2,1)}, u32[]{:S(2)}, u32[]{:S(2)}) collective-permute-start(bf16[64,8192]{1,0:T(8,128)(2,1)} %get-tuple-element.147), channel_id=1, source_target_pairs={{4,0},{8,4},{12,8},{14,12},{10,14},{6,10},{2,6},{0,2},{5,1},{9,5},... | collective-permute-start | bytes 3145736 | tf_op jit(solution)/shard_map/ppermute | solution.py:108
  6.1 46.6 %collective-permute-start.4 = (bf16[64,8192]{1,0:T(8,128)(2,1)}, bf16[64,8192]{1,0:T(8,128)(2,1)S(1)}, u32[]{:S(2)}, u32[]{:S(2)}) collective-permute-start(bf16[64,8192]{1,0:T(8,128)(2,1)} %get-tuple-element.147), channel_id=1, source_target_pairs={{0,4},{4,8},{8,12},{12,14},{14,10},{10,6},{6,2},{2,0},{1,5},{5,9},... | collective-permute-start | bytes 3145736 | tf_op jit(solution)/shard_map/ppermute | solution.py:108
  8.1 46.8 %collective-permute-start.5 = (bf16[64,8192]{1,0:T(8,128)(2,1)}, bf16[64,8192]{1,0:T(8,128)(2,1)}, u32[]{:S(2)}, u32[]{:S(2)}) collective-permute-start(bf16[64,8192]{1,0:T(8,128)(2,1)} %get-tuple-element.148), channel_id=1, source_target_pairs={{4,0},{8,4},{12,8},{14,12},{10,14},{6,10},{2,6},{0,2},{5,1},{9,5},... | collective-permute-start | bytes 3145736 | tf_op jit(solution)/shard_map/ppermute | solution.py:108
  40.9 5.9 %collective-permute-start.6 = (bf16[8,64,512]{2,1,0:T(8,128)(2,1)}, bf16[8,64,512]{2,1,0:T(8,128)(2,1)}, u32[]{:S(2)}, u32[]{:S(2)}) collective-permute-start(bf16[8,64,512]{2,1,0:T(8,128)(2,1)} %get-tuple-element.150), channel_id=1, source_target_pairs={{0,1},{1,0},{2,3},{3,2},{4,5},{5,4},{6,7},{7,6},{8,9},{9,8},{10,11... | collective-permute-start | bytes 1572872 | tf_op jit(solution)/shard_map/ppermute | solution.py:112
  44.9 12.1 %collective-permute-start.7 = (bf16[64,8192]{1,0:T(8,128)(2,1)}, bf16[64,8192]{1,0:T(8,128)(2,1)S(1)}, u32[]{:S(2)}, u32[]{:S(2)}) collective-permute-start(bf16[64,8192]{1,0:T(8,128)(2,1)} %get-tuple-element.145), channel_id=1, source_target_pairs={{0,1},{1,0},{2,3},{3,2},{4,5},{5,4},{6,7},{7,6},{8,9},{9,8},{10,11... | collective-permute-start | bytes 3145736 | tf_op jit(solution)/shard_map/ppermute | solution.py:112
  45.5 31.8 %collective-permute-start.2 = (bf16[64,8192]{1,0:T(8,128)(2,1)}, bf16[64,8192]{1,0:T(8,128)(2,1)}, u32[]{:S(2)}, u32[]{:S(2)}) collective-permute-start(bf16[64,8192]{1,0:T(8,128)(2,1)} %collective-permute-done.refs_0_), channel_id=1, source_target_pairs={{0,4},{4,8},{8,12},{12,14},{14,10},{10,6},{6,2},{2,0},{1,5},{5,9},... | collective-permute-start | bytes 3145736 | tf_op jit(solution)/shard_map/ppermute | solution.py:108
  46.8 30.7 %collective-permute-start.3 = (bf16[64,8192]{1,0:T(8,128)(2,1)}, bf16[64,8192]{1,0:T(8,128)(2,1)}, u32[]{:S(2)}, u32[]{:S(2)}) collective-permute-start(bf16[64,8192]{1,0:T(8,128)(2,1)} %collective-permute-done.1.refs_1_), channel_id=1, source_target_pairs={{4,0},{8,4},{12,8},{14,12},{10,14},{6,10},{2,6},{0,2},{5,1},{9,5},... | collective-permute-start | bytes 3145736 | tf_op jit(solution)/shard_map/ppermute | solution.py:108
  47.8 0.6 copy-start.14
  55.0 42.7 %collective-permute-start.10 = (bf16[64,8192]{1,0:T(8,128)(2,1)S(1)}, bf16[64,8192]{1,0:T(8,128)(2,1)S(1)}, u32[]{:S(2)}, u32[]{:S(2)}) collective-permute-start(bf16[64,8192]{1,0:T(8,128)(2,1)S(1)} %collective-permute-done.4.refs_1_), channel_id=1, source_target_pairs={{0,4},{4,8},{8,12},{12,14},{14,10},{10,6},{6,2},{2,0},{1,5},{5,9},... | collective-permute-start | bytes 3145736 | tf_op jit(solution)/shard_map/ppermute | solution.py:108
  56.6 43.3 %collective-permute-start.11 = (bf16[64,8192]{1,0:T(8,128)(2,1)}, bf16[64,8192]{1,0:T(8,128)(2,1)S(1)}, u32[]{:S(2)}, u32[]{:S(2)}) collective-permute-start(bf16[64,8192]{1,0:T(8,128)(2,1)} %collective-permute-done.5.refs_0_), channel_id=1, source_target_pairs={{4,0},{8,4},{12,8},{14,12},{10,14},{6,10},{2,6},{0,2},{5,1},{9,5},... | collective-permute-start | bytes 3145736 | tf_op jit(solution)/shard_map/ppermute | solution.py:108
  57.0 5.8 %copy-start.2 = (bf16[8192,1024]{1,0:T(8,128)(2,1)S(1)}, bf16[8192,1024]{1,0:T(8,128)(2,1)}, u32[]{:S(2)}) copy-start(bf16[8192,1024]{1,0:T(8,128)(2,1)} %weight.1) | copy-start | bytes 50331652
  62.8 2.8 %copy-start.3 = (bf16[1,128,8192]{2,1,0:T(8,128)(2,1)S(1)}, bf16[1,128,8192]{2,1,0:T(8,128)(2,1)}, u32[]{:S(2)}) copy-start(bf16[1,128,8192]{2,1,0:T(8,128)(2,1)} %param.6) | copy-start | bytes 6291460
  65.6 58.9 %copy-start = (bf16[8192,1152]{1,0:T(8,128)(2,1)}, bf16[8192,1152]{1,0:T(8,128)(2,1)S(1)}, u32[]{:S(2)}) copy-start(bf16[8192,1152]{1,0:T(8,128)(2,1)S(1)} %pin.1.weights) | copy-start | bytes 56623108
  69.0 1.6 copy-start.4
  76.5 0.8 copy-start.5
  77.5 42.7 %collective-permute-start.8 = (bf16[64,8192]{1,0:T(8,128)(2,1)}, bf16[64,8192]{1,0:T(8,128)(2,1)S(1)}, u32[]{:S(2)}, u32[]{:S(2)}) collective-permute-start(bf16[64,8192]{1,0:T(8,128)(2,1)} %collective-permute-done.2.refs_0_), channel_id=1, source_target_pairs={{0,4},{4,8},{8,12},{12,14},{14,10},{10,6},{6,2},{2,0},{1,5},{5,9},... | collective-permute-start | bytes 3145736 | tf_op jit(solution)/shard_map/ppermute | solution.py:108
  79.0 43.4 %collective-permute-start.9 = (bf16[64,8192]{1,0:T(8,128)(2,1)}, bf16[64,8192]{1,0:T(8,128)(2,1)}, u32[]{:S(2)}, u32[]{:S(2)}) collective-permute-start(bf16[64,8192]{1,0:T(8,128)(2,1)} %collective-permute-done.3.refs_1_), channel_id=1, source_target_pairs={{4,0},{8,4},{12,8},{14,12},{10,14},{6,10},{2,6},{0,2},{5,1},{9,5},... | collective-permute-start | bytes 3145736 | tf_op jit(solution)/shard_map/ppermute | solution.py:108
  83.6 0.8 copy-start.6
  88.9 0.8 copy-start.7
  99.8 42.8 %collective-permute-start.14 = (bf16[64,8192]{1,0:T(8,128)(2,1)S(1)}, bf16[64,8192]{1,0:T(8,128)(2,1)S(1)}, u32[]{:S(2)}, u32[]{:S(2)}) collective-permute-start(bf16[64,8192]{1,0:T(8,128)(2,1)S(1)} %collective-permute-done.10.refs_1_), channel_id=1, source_target_pairs={{0,4},{4,8},{8,12},{12,14},{14,10},{10,6},{6,2},{2,0},{1,5},{5,9},... | collective-permute-start | bytes 3145736 | tf_op jit(solution)/shard_map/ppermute | solution.py:108
  101.4 43.4 %collective-permute-start.15 = (bf16[64,8192]{1,0:T(8,128)(2,1)S(1)}, bf16[64,8192]{1,0:T(8,128)(2,1)S(1)}, u32[]{:S(2)}, u32[]{:S(2)}) collective-permute-start(bf16[64,8192]{1,0:T(8,128)(2,1)S(1)} %collective-permute-done.11.refs_0_), channel_id=1, source_target_pairs={{4,0},{8,4},{12,8},{14,12},{10,14},{6,10},{2,6},{0,2},{5,1},{9,5},... | collective-permute-start | bytes 3145736 | tf_op jit(solution)/shard_map/ppermute | solution.py:108
  105.3 0.8 copy-start.8
  122.4 42.8 %collective-permute-start.12 = (bf16[64,8192]{1,0:T(8,128)(2,1)S(1)}, bf16[64,8192]{1,0:T(8,128)(2,1)}, u32[]{:S(2)}, u32[]{:S(2)}) collective-permute-start(bf16[64,8192]{1,0:T(8,128)(2,1)S(1)} %collective-permute-done.8.refs_0_), channel_id=1, source_target_pairs={{0,4},{4,8},{8,12},{12,14},{14,10},{10,6},{6,2},{2,0},{1,5},{5,9},... | collective-permute-start | bytes 3145736 | tf_op jit(solution)/shard_map/ppermute | solution.py:108
  124.0 43.4 %collective-permute-start.13 = (bf16[64,8192]{1,0:T(8,128)(2,1)}, bf16[64,8192]{1,0:T(8,128)(2,1)}, u32[]{:S(2)}, u32[]{:S(2)}) collective-permute-start(bf16[64,8192]{1,0:T(8,128)(2,1)} %collective-permute-done.9.refs_1_), channel_id=1, source_target_pairs={{4,0},{8,4},{12,8},{14,12},{10,14},{6,10},{2,6},{0,2},{5,1},{9,5},... | collective-permute-start | bytes 3145736 | tf_op jit(solution)/shard_map/ppermute | solution.py:108
  128.6 0.8 copy-start.9
  144.8 1.0 copy-start.12
  146.8 42.5 %all-to-all-start = ((bf16[8,2,64,512]{3,2,1,0:T(8,128)(2,1)}), bf16[8,2,64,512]{3,2,1,0:T(8,128)(2,1)S(1)}, u32[]{:S(2)}, u32[]{:S(2)}) async-start(bf16[8,2,64,512]{3,2,1,0:T(8,128)(2,1)} %copy.10), calls=%async_computation | async-start | bytes 2097152 | tf_op jit(solution)/shard_map/all_to_all | solution.py:351
  151.6 6.4 %copy-start.1 = (bf16[8192,1152]{1,0:T(8,128)(2,1)S(1)}, bf16[8192,1152]{1,0:T(8,128)(2,1)}, u32[]{:S(2)}) copy-start(bf16[8192,1152]{1,0:T(8,128)(2,1)} %copy-done) | copy-start | bytes 56623108
  158.0 1.2 copy-start.13
  162.7 0.8 copy-start.10
  167.3 24.2 %copy-start.15 = (s32[16]{0:T(128)S(1)}, s32[16]{0:T(128)}, u32[]{:S(2)}) copy-start(s32[16]{0:T(128)} %copy-done.14) | copy-start | bytes 196
  167.3 28.7 %copy-start.16 = (s32[1,16]{1,0:T(1,128)S(1)}, s32[1,16]{1,0:T(1,128)}, u32[]{:S(2)}) copy-start(s32[1,16]{1,0:T(1,128)} %get-tuple-element.153) | copy-start | bytes 196
  171.8 0.8 copy-start.11
  172.6 4.0 %collective-permute-start.16 = (bf16[128,128]{1,0:T(8,128)(2,1)S(1)}, bf16[128,128]{1,0:T(8,128)(2,1)S(1)}, u32[]{:S(2)}, u32[]{:S(2)}) collective-permute-start(bf16[128,128]{1,0:T(8,128)(2,1)S(1)} %get-tuple-element.139), channel_id=1, source_target_pairs={{0,2},{2,0},{4,6},{6,4},{8,10},{10,8},{12,14},{14,12},{1,3},{3,1},... | collective-permute-start | bytes 98312 | tf_op jit(solution)/shard_map/ppermute | solution.py:108
  190.0 14.3 %collective-permute-start.20 = (bf16[8,64,512]{2,1,0:T(8,128)(2,1)S(1)}, bf16[8,64,512]{2,1,0:T(8,128)(2,1)S(1)}, u32[]{:S(2)}, u32[]{:S(2)}) collective-permute-start(bf16[8,64,512]{2,1,0:T(8,128)(2,1)S(1)} %take.1.refs_12_), channel_id=1, source_target_pairs={{0,16},{16,0},{1,17},{17,1},{2,18},{18,2},{3,19},{19,3},{4,20},{20... | collective-permute-start | bytes 1572872 | tf_op jit(solution)/shard_map/ppermute | solution.py:112
  191.6 4.5 %collective-permute-start.17 = (bf16[2,128,128]{2,1,0:T(8,128)(2,1)S(1)}, bf16[2,128,128]{2,1,0:T(8,128)(2,1)S(1)}, u32[]{:S(2)}, u32[]{:S(2)}) collective-permute-start(bf16[2,128,128]{2,1,0:T(8,128)(2,1)S(1)} %pad_maximum_fusion.1.refs_8_), channel_id=1, source_target_pairs={{0,4},{2,6},{4,0},{6,2},{8,12},{10,14},{12,8},{14,10},{1,5},{3,7},... | collective-permute-start | bytes 196616 | tf_op jit(solution)/shard_map/ppermute | solution.py:108
  191.6 5.7 %collective-permute-start.18 = (bf16[2,128,128]{2,1,0:T(8,128)(2,1)S(1)}, bf16[2,128,128]{2,1,0:T(8,128)(2,1)S(1)}, u32[]{:S(2)}, u32[]{:S(2)}) collective-permute-start(bf16[2,128,128]{2,1,0:T(8,128)(2,1)S(1)} %pad_maximum_fusion.1.refs_8_), channel_id=1, source_target_pairs={{0,8},{2,10},{4,12},{6,14},{8,0},{10,2},{12,4},{14,6},{1,9},{3,11}... | collective-permute-start | bytes 196616 | tf_op jit(solution)/shard_map/ppermute | solution.py:108
  193.4 6.1 %collective-permute-start.19 = (bf16[2,128,128]{2,1,0:T(8,128)(2,1)S(1)}, bf16[2,128,128]{2,1,0:T(8,128)(2,1)S(1)}, u32[]{:S(2)}, u32[]{:S(2)}) collective-permute-start(bf16[2,128,128]{2,1,0:T(8,128)(2,1)S(1)} %pad_maximum_fusion.1.refs_8_), channel_id=1, source_target_pairs={{0,12},{2,14},{4,8},{6,10},{8,4},{10,6},{12,0},{14,2},{1,13},{3,15... | collective-permute-start | bytes 196616 | tf_op jit(solution)/shard_map/ppermute | solution.py:108

commit v20 on v17

--- a/solution.py
+++ b/solution.py
@@ -251,9 +251,8 @@
 
 
 def finish_kernel(table, base, *refs):
-    gathered, (mine_a, mine_b, other_a, other_b) = refs[:4], refs[4:8]
-    out, shrunk, rows, sems = refs[8:]
-    part = mine_a.shape[2]
+    gathered, (mine, other, out, shrunk, rows, sems) = refs[:4], refs[4:]
+    part = mine.shape[2]
     group = table[3, 0]
     for i, pair in enumerate(gathered):
         shrunk[pl.ds(2 * i, 2)] = pair[...]
@@ -263,10 +262,9 @@
         own = pl.ds(half * HALF, HALF)
         both = shrunk[table[1, i], own, :].astype(jnp.float32)
         value = jnp.where(table[2, i] > 0, both[:, 64:], both[:, :64]).astype(jnp.bfloat16)
-        for up, side in (((mine_a, mine_b), group), ((other_a, other_b), 1 - group)):
+        for up, side in ((mine, group), (other, 1 - group)):
             cut = pl.ds(pl.multiple_of(side * part, part), part)
-            up = jnp.concatenate([up[0][block], up[1][block]], axis=0)
-            grown = jnp.dot(value, up, preferred_element_type=jnp.float32)
+            grown = jnp.dot(value, up[block], preferred_element_type=jnp.float32)
             rows[i, :, cut] = (base[i // 2, own, cut] + 0.5 * grown).astype(rows.dtype)
         to = pl.ds(pl.multiple_of((2 * block + half) * HALF, HALF), HALF)
         copies.append(pltpu.make_async_copy(rows.at[i], out.at[to], sems.at[i]))
@@ -279,7 +277,7 @@
     columns = base.shape[2]
     return pl.pallas_call(
         finish_kernel,
-        in_specs=[pl.BlockSpec(memory_space=pltpu.SMEM)] + in_vmem(9),
+        in_specs=[pl.BlockSpec(memory_space=pltpu.SMEM)] + in_vmem(7),
         out_specs=pl.BlockSpec(memory_space=pltpu.HBM),
         out_shape=jax.ShapeDtypeStruct((8 * BLOCK, columns), jnp.bfloat16),
         scratch_shapes=[
@@ -328,7 +326,6 @@
     choice = jnp.stack([pick_own, pick_lent, group.astype(pick_own.dtype)]).astype(jnp.int32)
     up_sent = pack_call(choice, adapter_up_maps)
     up_sent = jnp.stack([up_sent[0], swap(up_sent[1], "store")], axis=1)
-    up_sent = [up_sent[:, :, : rank // 2], up_sent[:, :, rank // 2 :]]
 
     position = jnp.where(y == 0, z, 7 - z)
     places = []
@@ -353,10 +350,7 @@
         if k < 5:
             flight.append((send(ahead[k + 2], AHEAD), send(back[k + 2], BACK)))
         if k == 5:
-            up_got = [
-                lax.all_to_all(sent, "tensor", split_axis=0, concat_axis=0, tiled=True)
-                for sent in up_sent
-            ]
+            up_got = lax.all_to_all(up_sent, "tensor", split_axis=0, concat_axis=0, tiled=True)
         groups.append([got_ahead, got_back] if k % 2 == 0 else [got_back, got_ahead])
         for g in range(len(bases), min(len(bases) + 2, k + 2, 7)):
             base, shrunk = rows_call(g, table, weights, groups[g], shrunk)
@@ -364,25 +358,19 @@
     base, shrunk = rows_call(7, table, weights, groups[7], shrunk)
     bases.append(base)
 
-    pair = jnp.stack([shrunk, send(shrunk, ACROSS)])
+    across = send(shrunk, ACROSS)
+    pair = jnp.stack([shrunk, across])
     everyone = [pair] + [send(pair, pairs) for pairs in ALONG]
-    base = collect_call(bases)
-    up_got[0], everyone, base = lax.optimization_barrier((up_got[0], everyone, base))
+    up_got, _ = lax.optimization_barrier((up_got, across))
     home, core = owner_row // 2, owner_row % 2
-    chosen = (2 * home + jnp.where(core == store, 0, 1)).astype(jnp.int32)
-
-    def take(got):
-        return take_call(chosen, got.reshape(16, rank // 2, -1))
-
-    mine = [take(up_got[0])]
-    other = [swap(mine[0], "groups")]
-    up_got[1], _ = lax.optimization_barrier((up_got[1], mine[0]))
-    mine.append(take(up_got[1]))
-    other.append(swap(mine[1], "groups"))
+    chosen = 2 * home + jnp.where(core == store, 0, 1)
+    up_mine = take_call(chosen.astype(jnp.int32), up_got.reshape(16, rank, -1))
+    up_other = swap(up_mine, "groups")
     home, core = owners // 2, owners % 2
     where = 2 * ((home // 2) ^ z) + ((home % 2) ^ y)
     table = jnp.stack([blocks, where, core != store, jnp.broadcast_to(group, (16,))])
-    return finish_call(table.astype(jnp.int32), base, everyone, mine + other)[None]
+    ups = [up_mine, up_other]
+    return finish_call(table.astype(jnp.int32), collect_call(bases), everyone, ups)[None]
 
 
 def body(tokens, *rest):

time: 223 us -> 205 us (0.919)
  local copies, waits for them, and re-layouts: 39.9 us -> 30.4 us
  starting transfers between devices: 32.8 us -> 27.9 us
    unnamed x50 -> x38, local copies, waits for them, and re-layouts: 30.3 us -> 21.5 us
    all_to_all x2 -> x1, starting transfers between devices: 8.4 us -> 4.82 us  [chain_body(): lax.all_to_all(up_sent, 'tensor', split_axis=0, concat_axis=0, tiled=True)]
    ppermute x4 -> x3, waiting for transfers between devices: 6.29 us -> 2.78 us  [swap(): return lax.ppermute(value, axis, [(0, 1), (1, 0)])]
    all_to_all x2 -> x1, waiting for transfers between devices: 10.7 us -> 12.7 us  [chain_body(): lax.all_to_all(up_sent, 'tensor', split_axis=0, concat_axis=0, tiled=True)]
  transfers between devices with their start and end apart: 24 -> 22, of which waited for: 16 -> 17; matrix products, arithmetic and copies ran while one was open for 5% -> 5% of each run, Pallas kernels for 19% -> 20%
where the time goes in v20:
time: 205 us
  waiting for transfers between devices  94.6 us (46%)
  Pallas kernels  43.6 us (21%)
  local copies, waits for them, and re-layouts  30.4 us (15%)
  starting transfers between devices  27.9 us (14%)
  between operations  4.47 us (2%)
  other arithmetic  3.82 us (2%)
    ppermute x18, waiting for transfers between devices, send(): return lax.ppermute(value, 'tensor', pairs)  79.1 us
    pallas_call x8, Pallas kernels, rows_call(): pl.pallas_call(functools.partial(rows_kernel, group), in_specs=[pl.BlockS...  33.4 us
    unnamed x38, local copies, waits for them, and re-layouts  21.5 us
    ppermute x18, starting transfers between devices, send(): return lax.ppermute(value, 'tensor', pairs)  21 us
    all_to_all x1, waiting for transfers between devices, chain_body(): lax.all_to_all(up_sent, 'tensor', split_axis=0, concat_axis=0, tiled=True)  12.7 us
    all_to_all x1, starting transfers between devices, chain_body(): lax.all_to_all(up_sent, 'tensor', split_axis=0, concat_axis=0, tiled=True)  4.82 us
  transfers between devices with their start and end apart: 22, of which 17 were waited for; matrix products, arithmetic and copies ran while one was open for 5% of the time, Pallas kernels for 20%

profile of v20, /device:TPU:0, one launch (start us, length us, event | category | flops | bytes accessed | tf_op | source)
XLA Modules:
  0.0 204.7 jit_solution(13508416911666577659)
XLA Ops:
  0.0 3.1 %slice_bitcast_fusion = (bf16[64,8192]{1,0:T(8,128)(2,1)}, bf16[64,8192]{1,0:T(8,128)(2,1)}) fusion(bf16[1,128,8192]{2,1,0:T(8,128)(2,1)} %param.6), kind=kLoop, calls=%fused_computation.3 | loop fusion | bytes 4194304 | tf_op jit(solution)/shard_map/slice | solution.py:303
  3.1 3.0 %collective-permute-start = (bf16[64,8192]{1,0:T(8,128)(2,1)}, bf16[64,8192]{1,0:T(8,128)(2,1)}, u32[]{:S(2)}, u32[]{:S(2)}) collective-permute-start(bf16[64,8192]{1,0:T(8,128)(2,1)} %get-tuple-element.148), channel_id=1, source_target_pairs={{0,4},{4,8},{8,12},{12,14},{14,10},{10,6},{6,2},{2,0},{1,5},{5,9},... | collective-permute-start | bytes 3145736 | tf_op jit(solution)/shard_map/ppermute | solution.py:108
  6.1 2.0 collective-permute-start.4
  8.1 22.2 %collective-permute-done.refs_0_ = bf16[64,8192]{1,0:T(8,128)(2,1)} collective-permute-done((bf16[64,8192]{1,0:T(8,128)(2,1)}, bf16[64,8192]{1,0:T(8,128)(2,1)}, u32[]{:S(2)}, u32[]{:S(2)}) %collective-permute-start) | collective-permute-done | bytes 1048608 | tf_op jit(solution)/shard_map/ppermute | solution.py:108
  30.4 2.2 %collective-permute-done.1.refs_1_ = bf16[64,8192]{1,0:T(8,128)(2,1)} collective-permute-done((bf16[64,8192]{1,0:T(8,128)(2,1)}, bf16[64,8192]{1,0:T(8,128)(2,1)}, u32[]{:S(2)}, u32[]{:S(2)}) %collective-permute-start.1) | collective-permute-done | bytes 1048608 | tf_op jit(solution)/shard_map/ppermute | solution.py:108
  36.2 1.4 pad_add_fusion.table
  37.6 2.2 %pack.1 = bf16[2,8,64,512]{3,2,1,0:T(8,128)(2,1)S(1)} custom-call(s32[3]{0:T(128)S(1)} %pad_add_fusion.table, bf16[4,64,8192]{2,1,0:T(8,128)(2,1)} %up.1), custom_call_target="tpu_custom_call" | custom-call | flops 1 | bytes 1 | tf_op jit(solution)/shard_map/pack/pallas_call | solution.py:198
  42.2 2.7 %dynamic-slice_bitcast_fusion = (bf16[64,8192]{1,0:T(8,128)(2,1)}, bf16[64,8192]{1,0:T(8,128)(2,1)S(1)}) fusion(bf16[4,64,8192]{2,1,0:T(8,128)(2,1)} %param.8, s32[]{:T(128)S(6)} %select_n.166, s32[]{:T(128)S(6)} %select_n.165), kind=kLoop, calls=%fused_computation.1 | loop fusion | bytes 4194312 | tf_op jit(solution)/shard_map/jit(dynamic_index_in_dim)/squeeze | solution.py:323
  45.4 1.6 collective-permute-start.2
  48.2 1.3 pad_maximum_fusion
  49.5 3.2 %collective-permute-done.4.refs_1_ = bf16[64,8192]{1,0:T(8,128)(2,1)S(1)} collective-permute-done((bf16[64,8192]{1,0:T(8,128)(2,1)}, bf16[64,8192]{1,0:T(8,128)(2,1)S(1)}, u32[]{:S(2)}, u32[]{:S(2)}) %collective-permute-start.4) | collective-permute-done | bytes 1048608 | tf_op jit(solution)/shard_map/ppermute | solution.py:108
  52.7 2.3 %collective-permute-done.5.refs_0_ = bf16[64,8192]{1,0:T(8,128)(2,1)} collective-permute-done((bf16[64,8192]{1,0:T(8,128)(2,1)}, bf16[64,8192]{1,0:T(8,128)(2,1)}, u32[]{:S(2)}, u32[]{:S(2)}) %collective-permute-start.5) | collective-permute-done | bytes 1048608 | tf_op jit(solution)/shard_map/ppermute | solution.py:108
  55.0 1.6 collective-permute-start.10
  57.0 5.8 %copy-done.2 = bf16[8192,1024]{1,0:T(8,128)(2,1)S(1)} copy-done((bf16[8192,1024]{1,0:T(8,128)(2,1)S(1)}, bf16[8192,1024]{1,0:T(8,128)(2,1)}, u32[]{:S(2)}) %copy-start.2) | copy-done | bytes 16777240
  62.8 2.8 %pin.1.weights = bf16[8192,1152]{1,0:T(8,128)(2,1)S(1)} custom-call(bf16[8192,1024]{1,0:T(8,128)(2,1)S(1)} %copy-done.2, bf16[64,8192]{1,0:T(8,128)(2,1)S(1)} %get-tuple-element.146.own, bf16[64,8192]{1,0:T(8,128)(2,1)S(1)} %collective-permute-done.7.swapped), custom_call_target="tpu_custom_call" | custom-call | flops 1 | bytes 1 | tf_op jit(solution)/shard_map/pin/pallas_call | solution.py:138
  65.6 3.4 %rows.8 = (f32[128,1024]{1,0:T(8,128)S(1)}, bf16[128,128]{1,0:T(8,128)(2,1)S(1)}) custom-call(s32[2,16]{1,0:T(2,128)S(1)} %add_convert_fusion.table, bf16[8192,1152]{1,0:T(8,128)(2,1)S(1)} %pin.1.weights, bf16[128,8192]{1,0:T(8,128)(2,1)S(1)} %bitcast.62, bf16[128,128]{1,0:T(8,128)(2,1)S(1)} %broadcast_in_dim.49.refs_1_), custom_call_target="tpu_custom_call" | custom-call | flops 1 | bytes 1 | tf_op jit(solution)/shard_map/rows/pallas_call | solution.py:175
  69.0 1.6 copy-done.6
  70.6 5.9 %rows.9 = (f32[128,1024]{1,0:T(8,128)S(1)}, bf16[128,128]{1,0:T(8,128)(2,1)S(1)}) custom-call(s32[2,16]{1,0:T(2,128)S(1)} %add_convert_fusion.table, bf16[8192,1152]{1,0:T(8,128)(2,1)S(1)} %pin.1.weights, bf16[64,8192]{1,0:T(8,128)(2,1)} %collective-permute-done.refs_0_, bf16[64,8192]{1,0:T(8,128)(2,1)} %collective-permute-done.1.refs_1_, ...), custom_call_target="tpu_custom_call" | custom-call | flops 1 | bytes 1 | tf_op jit(solution)/shard_map/rows/pallas_call | solution.py:175
  77.5 1.6 collective-permute-start.8
  79.5 4.1 %rows.10 = (f32[128,1024]{1,0:T(8,128)S(1)}, bf16[128,128]{1,0:T(8,128)(2,1)S(1)}) custom-call(s32[2,16]{1,0:T(2,128)S(1)} %add_convert_fusion.table, bf16[8192,1152]{1,0:T(8,128)(2,1)S(1)} %pin.1.weights, bf16[64,8192]{1,0:T(8,128)(2,1)} %collective-permute-done.5.refs_0_, bf16[64,8192]{1,0:T(8,128)(2,1)S(1)} %collective-permute-done.4.refs_1_, ...), custom_call_target="tpu_custom_call" | custom-call | flops 1 | bytes 1 | tf_op jit(solution)/shard_map/rows/pallas_call | solution.py:175
  84.4 4.4 %rows.11 = (f32[128,1024]{1,0:T(8,128)S(1)}, bf16[128,128]{1,0:T(8,128)(2,1)S(1)}) custom-call(s32[2,16]{1,0:T(2,128)S(1)} %add_convert_fusion.table, bf16[8192,1152]{1,0:T(8,128)(2,1)S(1)} %pin.1.weights, bf16[64,8192]{1,0:T(8,128)(2,1)} %collective-permute-done.2.refs_0_, bf16[64,8192]{1,0:T(8,128)(2,1)} %collective-permute-done.3.refs_1_, ...), custom_call_target="tpu_custom_call" | custom-call | flops 1 | bytes 1 | tf_op jit(solution)/shard_map/rows/pallas_call | solution.py:175
  89.7 8.0 %collective-permute-done.10.refs_1_ = bf16[64,8192]{1,0:T(8,128)(2,1)S(1)} collective-permute-done((bf16[64,8192]{1,0:T(8,128)(2,1)S(1)}, bf16[64,8192]{1,0:T(8,128)(2,1)S(1)}, u32[]{:S(2)}, u32[]{:S(2)}) %collective-permute-start.10) | collective-permute-done | bytes 1048608 | tf_op jit(solution)/shard_map/ppermute | solution.py:108
  97.7 2.2 %collective-permute-done.11.refs_0_ = bf16[64,8192]{1,0:T(8,128)(2,1)S(1)} collective-permute-done((bf16[64,8192]{1,0:T(8,128)(2,1)}, bf16[64,8192]{1,0:T(8,128)(2,1)S(1)}, u32[]{:S(2)}, u32[]{:S(2)}) %collective-permute-start.11) | collective-permute-done | bytes 1048608 | tf_op jit(solution)/shard_map/ppermute | solution.py:108
  99.8 1.6 collective-permute-start.14
  101.8 3.4 %rows.12 = (f32[128,1024]{1,0:T(8,128)S(1)}, bf16[128,128]{1,0:T(8,128)(2,1)S(1)}) custom-call(s32[2,16]{1,0:T(2,128)S(1)} %add_convert_fusion.table, bf16[8192,1152]{1,0:T(8,128)(2,1)S(1)} %pin.1.weights, bf16[64,8192]{1,0:T(8,128)(2,1)S(1)} %collective-permute-done.11.refs_0_, bf16[64,8192]{1,0:T(8,128)(2,1)S(1)} %collective-permute-done.10.refs_1_, ...), custom_call_target="tpu_custom_call" | custom-call | flops 1 | bytes 1 | tf_op jit(solution)/shard_map/rows/pallas_call | solution.py:175
  106.1 14.0 %collective-permute-done.8.refs_0_ = bf16[64,8192]{1,0:T(8,128)(2,1)S(1)} collective-permute-done((bf16[64,8192]{1,0:T(8,128)(2,1)}, bf16[64,8192]{1,0:T(8,128)(2,1)S(1)}, u32[]{:S(2)}, u32[]{:S(2)}) %collective-permute-start.8) | collective-permute-done | bytes 1048608 | tf_op jit(solution)/shard_map/ppermute | solution.py:108
  120.1 2.3 %collective-permute-done.9.refs_1_ = bf16[64,8192]{1,0:T(8,128)(2,1)} collective-permute-done((bf16[64,8192]{1,0:T(8,128)(2,1)}, bf16[64,8192]{1,0:T(8,128)(2,1)}, u32[]{:S(2)}, u32[]{:S(2)}) %collective-permute-start.9) | collective-permute-done | bytes 1048608 | tf_op jit(solution)/shard_map/ppermute | solution.py:108
  122.4 1.6 collective-permute-start.12
  124.4 4.2 %rows.13 = (f32[128,1024]{1,0:T(8,128)S(1)}, bf16[128,128]{1,0:T(8,128)(2,1)S(1)}) custom-call(s32[2,16]{1,0:T(2,128)S(1)} %add_convert_fusion.table, bf16[8192,1152]{1,0:T(8,128)(2,1)S(1)} %pin.1.weights, bf16[64,8192]{1,0:T(8,128)(2,1)S(1)} %collective-permute-done.8.refs_0_, bf16[64,8192]{1,0:T(8,128)(2,1)} %collective-permute-done.9.refs_1_, ...), custom_call_target="tpu_custom_call" | custom-call | flops 1 | bytes 1 | tf_op jit(solution)/shard_map/rows/pallas_call | solution.py:175
  129.4 13.2 %collective-permute-done.14.refs_1_ = bf16[64,8192]{1,0:T(8,128)(2,1)S(1)} collective-permute-done((bf16[64,8192]{1,0:T(8,128)(2,1)S(1)}, bf16[64,8192]{1,0:T(8,128)(2,1)S(1)}, u32[]{:S(2)}, u32[]{:S(2)}) %collective-permute-start.14) | collective-permute-done | bytes 1048608 | tf_op jit(solution)/shard_map/ppermute | solution.py:108
  142.6 2.2 %collective-permute-done.15.refs_0_ = bf16[64,8192]{1,0:T(8,128)(2,1)S(1)} collective-permute-done((bf16[64,8192]{1,0:T(8,128)(2,1)S(1)}, bf16[64,8192]{1,0:T(8,128)(2,1)S(1)}, u32[]{:S(2)}, u32[]{:S(2)}) %collective-permute-start.15) | collective-permute-done | bytes 1048608 | tf_op jit(solution)/shard_map/ppermute | solution.py:108
  146.8 4.8 %all-to-all-start = ((bf16[8,2,64,512]{3,2,1,0:T(8,128)(2,1)}), bf16[8,2,64,512]{3,2,1,0:T(8,128)(2,1)S(1)}, u32[]{:S(2)}, u32[]{:S(2)}) async-start(bf16[8,2,64,512]{3,2,1,0:T(8,128)(2,1)} %copy.9), calls=%async_computation | async-start | bytes 2097152 | tf_op jit(solution)/shard_map/all_to_all | solution.py:353
  151.6 6.4 %copy-done.1 = bf16[8192,1152]{1,0:T(8,128)(2,1)S(1)} copy-done((bf16[8192,1152]{1,0:T(8,128)(2,1)S(1)}, bf16[8192,1152]{1,0:T(8,128)(2,1)}, u32[]{:S(2)}) %copy-start.1) | copy-done | bytes 18874392
  158.0 1.2 copy-done.5
  159.2 3.5 %rows.14 = (f32[128,1024]{1,0:T(8,128)S(1)}, bf16[128,128]{1,0:T(8,128)(2,1)S(1)}) custom-call(s32[2,16]{1,0:T(2,128)S(1)} %add_convert_fusion.table, bf16[8192,1152]{1,0:T(8,128)(2,1)S(1)} %copy-done.1, bf16[64,8192]{1,0:T(8,128)(2,1)S(1)} %copy-done.5, bf16[64,8192]{1,0:T(8,128)(2,1)S(1)} %collective-permute-done.14.refs_1_, ...), custom_call_target="tpu_custom_call" | custom-call | flops 1 | bytes 1 | tf_op jit(solution)/shard_map/rows/pallas_call | solution.py:175
  163.5 1.7 collective-permute-done.12.refs_0_
  165.2 2.2 %collective-permute-done.13.refs_1_ = bf16[64,8192]{1,0:T(8,128)(2,1)} collective-permute-done((bf16[64,8192]{1,0:T(8,128)(2,1)}, bf16[64,8192]{1,0:T(8,128)(2,1)}, u32[]{:S(2)}, u32[]{:S(2)}) %collective-permute-start.13) | collective-permute-done | bytes 1048608 | tf_op jit(solution)/shard_map/ppermute | solution.py:108
  167.3 4.4 %rows.15 = (f32[128,1024]{1,0:T(8,128)S(1)}, bf16[128,128]{1,0:T(8,128)(2,1)S(1)}) custom-call(s32[2,16]{1,0:T(2,128)S(1)} %add_convert_fusion.table, bf16[8192,1152]{1,0:T(8,128)(2,1)S(1)} %copy-done.1, bf16[64,8192]{1,0:T(8,128)(2,1)} %collective-permute-done.12.refs_0_, bf16[64,8192]{1,0:T(8,128)(2,1)} %collective-permute-done.13.refs_1_, ...), custom_call_target="tpu_custom_call" | custom-call | flops 99999997952 | bytes 1 | tf_op jit(solution)/shard_map/rows/pallas_call | solution.py:175
  172.6 1.4 collective-permute-start.16
  174.1 2.4 %collective-permute-done.16 = bf16[128,128]{1,0:T(8,128)(2,1)S(1)} collective-permute-done((bf16[128,128]{1,0:T(8,128)(2,1)S(1)}, bf16[128,128]{1,0:T(8,128)(2,1)S(1)}, u32[]{:S(2)}, u32[]{:S(2)}) %collective-permute-start.16) | collective-permute-done | bytes 32800 | tf_op jit(solution)/shard_map/ppermute | solution.py:108
  176.6 12.7 %all-to-all-done = bf16[8,2,64,512]{3,2,1,0:T(8,128)(2,1)S(1)} async-done(((bf16[8,2,64,512]{3,2,1,0:T(8,128)(2,1)}), bf16[8,2,64,512]{3,2,1,0:T(8,128)(2,1)S(1)}, u32[]{:S(2)}, u32[]{:S(2)}) %all-to-all-start) | async-done | bytes 1048608 | tf_op jit(solution)/shard_map/all_to_all | solution.py:353
  190.0 1.6 collective-permute-start.20
  191.6 1.7 collective-permute-start.18
  193.4 2.6 %collective-permute-start.19 = (bf16[2,128,128]{2,1,0:T(8,128)(2,1)S(1)}, bf16[2,128,128]{2,1,0:T(8,128)(2,1)S(1)}, u32[]{:S(2)}, u32[]{:S(2)}) collective-permute-start(bf16[2,128,128]{2,1,0:T(8,128)(2,1)S(1)} %pad_maximum_fusion.1.refs_0_), channel_id=1, source_target_pairs={{0,12},{2,14},{4,8},{6,10},{8,4},{10,6},{12,0},{14,2},{1,13},{3,15... | collective-permute-start | bytes 196616 | tf_op jit(solution)/shard_map/ppermute | solution.py:108
  196.1 2.2 %collect.1.base = f32[8,128,1024]{2,1,0:T(8,128)S(1)} custom-call(f32[128,1024]{1,0:T(8,128)} %copy-done.6, f32[128,1024]{1,0:T(8,128)} %copy-done.7, f32[128,1024]{1,0:T(8,128)} %copy-done.8, f32[128,1024]{1,0:T(8,128)} %copy-done.9, f32[128,1024]{1,0:T(8,128)} %copy-done.10, f32[128,1024]{1,0:T(8,128)} %copy-done.11, f32[128,1024]{1,0:T(8,128)} %copy-done.12, ...), custom_call_target="tpu_custom_call" | custom-call | flops 1 | bytes 1 | tf_op jit(solution)/shard_map/collect/pallas_call | solution.py:242
  198.3 1.1 collective-permute-done.19.refs_3_
  199.4 2.8 %collective-permute-done.20.refs_5_ = bf16[8,64,512]{2,1,0:T(8,128)(2,1)S(1)} collective-permute-done((bf16[8,64,512]{2,1,0:T(8,128)(2,1)S(1)}, bf16[8,64,512]{2,1,0:T(8,128)(2,1)S(1)}, u32[]{:S(2)}, u32[]{:S(2)}) %collective-permute-start.20) | collective-permute-done | bytes 524320 | tf_op jit(solution)/shard_map/ppermute | solution.py:112
  202.2 2.3 %finish.1 = bf16[1024,1024]{1,0:T(8,128)(2,1)} custom-call(s32[4,16]{1,0:T(4,128)S(1)} %add_add_fusion.table, f32[8,128,1024]{2,1,0:T(8,128)S(1)} %collect.1.base, bf16[2,128,128]{2,1,0:T(8,128)(2,1)S(1)} %pad_maximum_fusion.1.refs_0_, bf16[2,128,128]{2,1,0:T(8,128)(2,1)S(1)} %collective-permute-done.17.refs_1_, ...), custom_call_target="tpu_custom_call" | custom-call | flops 1 | bytes 1 | tf_op jit(solution)/shard_map/finish/pallas_call | solution.py:278
  (68 shorter events, 14.5 us)
Async XLA Ops:
  0.0 32.5 %copy-start.18 = (s32[64]{0:T(128)S(1)}, s32[64]{0:T(128)}, u32[]{:S(2)}) copy-start(s32[64]{0:T(128)} %param.10) | copy-start | bytes 772
  0.0 32.5 %copy-start.17 = (s32[2,8]{1,0:T(2,128)S(1)}, s32[2,8]{1,0:T(2,128)}, u32[]{:S(2)}) copy-start(s32[2,8]{1,0:T(2,128)} %param.11) | copy-start | bytes 196
  3.1 27.3 %collective-permute-start = (bf16[64,8192]{1,0:T(8,128)(2,1)}, bf16[64,8192]{1,0:T(8,128)(2,1)}, u32[]{:S(2)}, u32[]{:S(2)}) collective-permute-start(bf16[64,8192]{1,0:T(8,128)(2,1)} %get-tuple-element.148), channel_id=1, source_target_pairs={{0,4},{4,8},{8,12},{12,14},{14,10},{10,6},{6,2},{2,0},{1,5},{5,9},... | collective-permute-start | bytes 3145736 | tf_op jit(solution)/shard_map/ppermute | solution.py:108
  6.1 26.4 %collective-permute-start.1 = (bf16[64,8192]{1,0:T(8,128)(2,1)}, bf16[64,8192]{1,0:T(8,128)(2,1)}, u32[]{:S(2)}, u32[]{:S(2)}) collective-permute-start(bf16[64,8192]{1,0:T(8,128)(2,1)} %get-tuple-element.147), channel_id=1, source_target_pairs={{4,0},{8,4},{12,8},{14,12},{10,14},{6,10},{2,6},{0,2},{5,1},{9,5},... | collective-permute-start | bytes 3145736 | tf_op jit(solution)/shard_map/ppermute | solution.py:108
  6.1 46.6 %collective-permute-start.4 = (bf16[64,8192]{1,0:T(8,128)(2,1)}, bf16[64,8192]{1,0:T(8,128)(2,1)S(1)}, u32[]{:S(2)}, u32[]{:S(2)}) collective-permute-start(bf16[64,8192]{1,0:T(8,128)(2,1)} %get-tuple-element.147), channel_id=1, source_target_pairs={{0,4},{4,8},{8,12},{12,14},{14,10},{10,6},{6,2},{2,0},{1,5},{5,9},... | collective-permute-start | bytes 3145736 | tf_op jit(solution)/shard_map/ppermute | solution.py:108
  8.1 46.8 %collective-permute-start.5 = (bf16[64,8192]{1,0:T(8,128)(2,1)}, bf16[64,8192]{1,0:T(8,128)(2,1)}, u32[]{:S(2)}, u32[]{:S(2)}) collective-permute-start(bf16[64,8192]{1,0:T(8,128)(2,1)} %get-tuple-element.148), channel_id=1, source_target_pairs={{4,0},{8,4},{12,8},{14,12},{10,14},{6,10},{2,6},{0,2},{5,1},{9,5},... | collective-permute-start | bytes 3145736 | tf_op jit(solution)/shard_map/ppermute | solution.py:108
  40.9 6.1 %collective-permute-start.6 = (bf16[8,64,512]{2,1,0:T(8,128)(2,1)}, bf16[8,64,512]{2,1,0:T(8,128)(2,1)}, u32[]{:S(2)}, u32[]{:S(2)}) collective-permute-start(bf16[8,64,512]{2,1,0:T(8,128)(2,1)} %get-tuple-element.150), channel_id=1, source_target_pairs={{0,1},{1,0},{2,3},{3,2},{4,5},{5,4},{6,7},{7,6},{8,9},{9,8},{10,11... | collective-permute-start | bytes 1572872 | tf_op jit(solution)/shard_map/ppermute | solution.py:112
  44.9 12.1 %collective-permute-start.7 = (bf16[64,8192]{1,0:T(8,128)(2,1)}, bf16[64,8192]{1,0:T(8,128)(2,1)S(1)}, u32[]{:S(2)}, u32[]{:S(2)}) collective-permute-start(bf16[64,8192]{1,0:T(8,128)(2,1)} %get-tuple-element.145), channel_id=1, source_target_pairs={{0,1},{1,0},{2,3},{3,2},{4,5},{5,4},{6,7},{7,6},{8,9},{9,8},{10,11... | collective-permute-start | bytes 3145736 | tf_op jit(solution)/shard_map/ppermute | solution.py:112
  45.4 31.9 %collective-permute-start.2 = (bf16[64,8192]{1,0:T(8,128)(2,1)}, bf16[64,8192]{1,0:T(8,128)(2,1)}, u32[]{:S(2)}, u32[]{:S(2)}) collective-permute-start(bf16[64,8192]{1,0:T(8,128)(2,1)} %collective-permute-done.refs_0_), channel_id=1, source_target_pairs={{0,4},{4,8},{8,12},{12,14},{14,10},{10,6},{6,2},{2,0},{1,5},{5,9},... | collective-permute-start | bytes 3145736 | tf_op jit(solution)/shard_map/ppermute | solution.py:108
  47.0 30.4 %collective-permute-start.3 = (bf16[64,8192]{1,0:T(8,128)(2,1)}, bf16[64,8192]{1,0:T(8,128)(2,1)}, u32[]{:S(2)}, u32[]{:S(2)}) collective-permute-start(bf16[64,8192]{1,0:T(8,128)(2,1)} %collective-permute-done.1.refs_1_), channel_id=1, source_target_pairs={{4,0},{8,4},{12,8},{14,12},{10,14},{6,10},{2,6},{0,2},{5,1},{9,5},... | collective-permute-start | bytes 3145736 | tf_op jit(solution)/shard_map/ppermute | solution.py:108
  47.7 0.6 copy-start.14
  55.0 42.7 %collective-permute-start.10 = (bf16[64,8192]{1,0:T(8,128)(2,1)S(1)}, bf16[64,8192]{1,0:T(8,128)(2,1)S(1)}, u32[]{:S(2)}, u32[]{:S(2)}) collective-permute-start(bf16[64,8192]{1,0:T(8,128)(2,1)S(1)} %collective-permute-done.4.refs_1_), channel_id=1, source_target_pairs={{0,4},{4,8},{8,12},{12,14},{14,10},{10,6},{6,2},{2,0},{1,5},{5,9},... | collective-permute-start | bytes 3145736 | tf_op jit(solution)/shard_map/ppermute | solution.py:108
  56.6 43.3 %collective-permute-start.11 = (bf16[64,8192]{1,0:T(8,128)(2,1)}, bf16[64,8192]{1,0:T(8,128)(2,1)S(1)}, u32[]{:S(2)}, u32[]{:S(2)}) collective-permute-start(bf16[64,8192]{1,0:T(8,128)(2,1)} %collective-permute-done.5.refs_0_), channel_id=1, source_target_pairs={{4,0},{8,4},{12,8},{14,12},{10,14},{6,10},{2,6},{0,2},{5,1},{9,5},... | collective-permute-start | bytes 3145736 | tf_op jit(solution)/shard_map/ppermute | solution.py:108
  57.0 5.8 %copy-start.2 = (bf16[8192,1024]{1,0:T(8,128)(2,1)S(1)}, bf16[8192,1024]{1,0:T(8,128)(2,1)}, u32[]{:S(2)}) copy-start(bf16[8192,1024]{1,0:T(8,128)(2,1)} %weight.1) | copy-start | bytes 50331652
  62.8 2.8 %copy-start.3 = (bf16[1,128,8192]{2,1,0:T(8,128)(2,1)S(1)}, bf16[1,128,8192]{2,1,0:T(8,128)(2,1)}, u32[]{:S(2)}) copy-start(bf16[1,128,8192]{2,1,0:T(8,128)(2,1)} %param.6) | copy-start | bytes 6291460
  65.6 58.9 %copy-start = (bf16[8192,1152]{1,0:T(8,128)(2,1)}, bf16[8192,1152]{1,0:T(8,128)(2,1)S(1)}, u32[]{:S(2)}) copy-start(bf16[8192,1152]{1,0:T(8,128)(2,1)S(1)} %pin.1.weights) | copy-start | bytes 56623108
  69.0 1.6 copy-start.6
  76.5 0.8 copy-start.7
  77.5 42.7 %collective-permute-start.8 = (bf16[64,8192]{1,0:T(8,128)(2,1)}, bf16[64,8192]{1,0:T(8,128)(2,1)S(1)}, u32[]{:S(2)}, u32[]{:S(2)}) collective-permute-start(bf16[64,8192]{1,0:T(8,128)(2,1)} %collective-permute-done.2.refs_0_), channel_id=1, source_target_pairs={{0,4},{4,8},{8,12},{12,14},{14,10},{10,6},{6,2},{2,0},{1,5},{5,9},... | collective-permute-start | bytes 3145736 | tf_op jit(solution)/shard_map/ppermute | solution.py:108
  79.0 43.4 %collective-permute-start.9 = (bf16[64,8192]{1,0:T(8,128)(2,1)}, bf16[64,8192]{1,0:T(8,128)(2,1)}, u32[]{:S(2)}, u32[]{:S(2)}) collective-permute-start(bf16[64,8192]{1,0:T(8,128)(2,1)} %collective-permute-done.3.refs_1_), channel_id=1, source_target_pairs={{4,0},{8,4},{12,8},{14,12},{10,14},{6,10},{2,6},{0,2},{5,1},{9,5},... | collective-permute-start | bytes 3145736 | tf_op jit(solution)/shard_map/ppermute | solution.py:108
  83.6 0.8 copy-start.8
  88.9 0.8 copy-start.9
  99.8 42.8 %collective-permute-start.14 = (bf16[64,8192]{1,0:T(8,128)(2,1)S(1)}, bf16[64,8192]{1,0:T(8,128)(2,1)S(1)}, u32[]{:S(2)}, u32[]{:S(2)}) collective-permute-start(bf16[64,8192]{1,0:T(8,128)(2,1)S(1)} %collective-permute-done.10.refs_1_), channel_id=1, source_target_pairs={{0,4},{4,8},{8,12},{12,14},{14,10},{10,6},{6,2},{2,0},{1,5},{5,9},... | collective-permute-start | bytes 3145736 | tf_op jit(solution)/shard_map/ppermute | solution.py:108
  101.4 43.4 %collective-permute-start.15 = (bf16[64,8192]{1,0:T(8,128)(2,1)S(1)}, bf16[64,8192]{1,0:T(8,128)(2,1)S(1)}, u32[]{:S(2)}, u32[]{:S(2)}) collective-permute-start(bf16[64,8192]{1,0:T(8,128)(2,1)S(1)} %collective-permute-done.11.refs_0_), channel_id=1, source_target_pairs={{4,0},{8,4},{12,8},{14,12},{10,14},{6,10},{2,6},{0,2},{5,1},{9,5},... | collective-permute-start | bytes 3145736 | tf_op jit(solution)/shard_map/ppermute | solution.py:108
  105.3 0.8 copy-start.10
  122.4 42.8 %collective-permute-start.12 = (bf16[64,8192]{1,0:T(8,128)(2,1)S(1)}, bf16[64,8192]{1,0:T(8,128)(2,1)}, u32[]{:S(2)}, u32[]{:S(2)}) collective-permute-start(bf16[64,8192]{1,0:T(8,128)(2,1)S(1)} %collective-permute-done.8.refs_0_), channel_id=1, source_target_pairs={{0,4},{4,8},{8,12},{12,14},{14,10},{10,6},{6,2},{2,0},{1,5},{5,9},... | collective-permute-start | bytes 3145736 | tf_op jit(solution)/shard_map/ppermute | solution.py:108
  124.0 43.4 %collective-permute-start.13 = (bf16[64,8192]{1,0:T(8,128)(2,1)}, bf16[64,8192]{1,0:T(8,128)(2,1)}, u32[]{:S(2)}, u32[]{:S(2)}) collective-permute-start(bf16[64,8192]{1,0:T(8,128)(2,1)} %collective-permute-done.9.refs_1_), channel_id=1, source_target_pairs={{4,0},{8,4},{12,8},{14,12},{10,14},{6,10},{2,6},{0,2},{5,1},{9,5},... | collective-permute-start | bytes 3145736 | tf_op jit(solution)/shard_map/ppermute | solution.py:108
  128.6 0.8 copy-start.11
  144.8 1.0 copy-start.4
  146.8 42.5 %all-to-all-start = ((bf16[8,2,64,512]{3,2,1,0:T(8,128)(2,1)}), bf16[8,2,64,512]{3,2,1,0:T(8,128)(2,1)S(1)}, u32[]{:S(2)}, u32[]{:S(2)}) async-start(bf16[8,2,64,512]{3,2,1,0:T(8,128)(2,1)} %copy.9), calls=%async_computation | async-start | bytes 2097152 | tf_op jit(solution)/shard_map/all_to_all | solution.py:353
  151.6 6.4 %copy-start.1 = (bf16[8192,1152]{1,0:T(8,128)(2,1)S(1)}, bf16[8192,1152]{1,0:T(8,128)(2,1)}, u32[]{:S(2)}) copy-start(bf16[8192,1152]{1,0:T(8,128)(2,1)} %copy-done) | copy-start | bytes 56623108
  158.0 1.2 copy-start.5
  162.7 0.8 copy-start.12
  167.3 24.2 %copy-start.15 = (s32[16]{0:T(128)S(1)}, s32[16]{0:T(128)}, u32[]{:S(2)}) copy-start(s32[16]{0:T(128)} %copy-done.14) | copy-start | bytes 196
  167.3 28.7 %copy-start.16 = (s32[1,16]{1,0:T(1,128)S(1)}, s32[1,16]{1,0:T(1,128)}, u32[]{:S(2)}) copy-start(s32[1,16]{1,0:T(1,128)} %get-tuple-element.153) | copy-start | bytes 196
  171.8 0.8 copy-start.13
  172.6 4.0 %collective-permute-start.16 = (bf16[128,128]{1,0:T(8,128)(2,1)S(1)}, bf16[128,128]{1,0:T(8,128)(2,1)S(1)}, u32[]{:S(2)}, u32[]{:S(2)}) collective-permute-start(bf16[128,128]{1,0:T(8,128)(2,1)S(1)} %get-tuple-element.139), channel_id=1, source_target_pairs={{0,2},{2,0},{4,6},{6,4},{8,10},{10,8},{12,14},{14,12},{1,3},{3,1},... | collective-permute-start | bytes 98312 | tf_op jit(solution)/shard_map/ppermute | solution.py:108
  190.0 12.2 %collective-permute-start.20 = (bf16[8,64,512]{2,1,0:T(8,128)(2,1)S(1)}, bf16[8,64,512]{2,1,0:T(8,128)(2,1)S(1)}, u32[]{:S(2)}, u32[]{:S(2)}) collective-permute-start(bf16[8,64,512]{2,1,0:T(8,128)(2,1)S(1)} %take.1.refs_4_), channel_id=1, source_target_pairs={{0,16},{16,0},{1,17},{17,1},{2,18},{18,2},{3,19},{19,3},{4,20},{20... | collective-permute-start | bytes 1572872 | tf_op jit(solution)/shard_map/ppermute | solution.py:112
  191.6 6.8 %collective-permute-start.17 = (bf16[2,128,128]{2,1,0:T(8,128)(2,1)S(1)}, bf16[2,128,128]{2,1,0:T(8,128)(2,1)S(1)}, u32[]{:S(2)}, u32[]{:S(2)}) collective-permute-start(bf16[2,128,128]{2,1,0:T(8,128)(2,1)S(1)} %pad_maximum_fusion.1.refs_0_), channel_id=1, source_target_pairs={{0,4},{2,6},{4,0},{6,2},{8,12},{10,14},{12,8},{14,10},{1,5},{3,7},... | collective-permute-start | bytes 196616 | tf_op jit(solution)/shard_map/ppermute | solution.py:108
  191.6 6.7 %collective-permute-start.18 = (bf16[2,128,128]{2,1,0:T(8,128)(2,1)S(1)}, bf16[2,128,128]{2,1,0:T(8,128)(2,1)S(1)}, u32[]{:S(2)}, u32[]{:S(2)}) collective-permute-start(bf16[2,128,128]{2,1,0:T(8,128)(2,1)S(1)} %pad_maximum_fusion.1.refs_0_), channel_id=1, source_target_pairs={{0,8},{2,10},{4,12},{6,14},{8,0},{10,2},{12,4},{14,6},{1,9},{3,11}... | collective-permute-start | bytes 196616 | tf_op jit(solution)/shard_map/ppermute | solution.py:108
  193.4 6.1 %collective-permute-start.19 = (bf16[2,128,128]{2,1,0:T(8,128)(2,1)S(1)}, bf16[2,128,128]{2,1,0:T(8,128)(2,1)S(1)}, u32[]{:S(2)}, u32[]{:S(2)}) collective-permute-start(bf16[2,128,128]{2,1,0:T(8,128)(2,1)S(1)} %pad_maximum_fusion.1.refs_0_), channel_id=1, source_target_pairs={{0,12},{2,14},{4,8},{6,10},{8,4},{10,6},{12,0},{14,2},{1,13},{3,15... | collective-permute-start | bytes 196616 | tf_op jit(solution)/shard_map/ppermute | solution.py:108

commit v21 on v17

--- a/solution.py
+++ b/solution.py
@@ -352,11 +352,10 @@
         back.append(got_back)
         if k < 5:
             flight.append((send(ahead[k + 2], AHEAD), send(back[k + 2], BACK)))
-        if k == 5:
-            up_got = [
-                lax.all_to_all(sent, "tensor", split_axis=0, concat_axis=0, tiled=True)
-                for sent in up_sent
-            ]
+        if k in (4, 5):
+            sent = up_sent[k - 4]
+            got = lax.all_to_all(sent, "tensor", split_axis=0, concat_axis=0, tiled=True)
+            up_sent = [got, up_sent[1]] if k == 4 else [up_sent[0], got]
         groups.append([got_ahead, got_back] if k % 2 == 0 else [got_back, got_ahead])
         for g in range(len(bases), min(len(bases) + 2, k + 2, 7)):
             base, shrunk = rows_call(g, table, weights, groups[g], shrunk)
@@ -364,25 +363,25 @@
     base, shrunk = rows_call(7, table, weights, groups[7], shrunk)
     bases.append(base)
 
-    pair = jnp.stack([shrunk, send(shrunk, ACROSS)])
+    across = send(shrunk, ACROSS)
+    pair = jnp.stack([shrunk, across])
     everyone = [pair] + [send(pair, pairs) for pairs in ALONG]
-    base = collect_call(bases)
-    up_got[0], everyone, base = lax.optimization_barrier((up_got[0], everyone, base))
     home, core = owner_row // 2, owner_row % 2
     chosen = (2 * home + jnp.where(core == store, 0, 1)).astype(jnp.int32)
 
     def take(got):
         return take_call(chosen, got.reshape(16, rank // 2, -1))
 
-    mine = [take(up_got[0])]
+    mine = [take(up_sent[0])]
     other = [swap(mine[0], "groups")]
-    up_got[1], _ = lax.optimization_barrier((up_got[1], mine[0]))
-    mine.append(take(up_got[1]))
+    got, _ = lax.optimization_barrier((up_sent[1], across))
+    mine.append(take(got))
     other.append(swap(mine[1], "groups"))
     home, core = owners // 2, owners % 2
     where = 2 * ((home // 2) ^ z) + ((home % 2) ^ y)
     table = jnp.stack([blocks, where, core != store, jnp.broadcast_to(group, (16,))])
-    return finish_call(table.astype(jnp.int32), base, everyone, mine + other)[None]
+    ups = mine + other
+    return finish_call(table.astype(jnp.int32), collect_call(bases), everyone, ups)[None]
 
 
 def body(tokens, *rest):

time: 223 us -> 218 us (0.978)
  waiting for transfers between devices: 95.6 us -> 86.9 us
    ppermute x18, waiting for transfers between devices: 78.5 us -> 61.2 us  [send(): return lax.ppermute(value, 'tensor', pairs)]
    all_to_all x2, waiting for transfers between devices: 10.7 us -> 25.7 us  [chain_body(): lax.all_to_all(sent, 'tensor', split_axis=0, concat_axis=0, tiled=True)]
    ppermute x4, waiting for transfers between devices: 6.29 us -> 0.01 us  [swap(): return lax.ppermute(value, axis, [(0, 1), (1, 0)])]
    unnamed x50 -> x38, local copies, waits for them, and re-layouts: 30.3 us -> 31.2 us
  transfers between devices with their start and end apart: 24 -> 24, of which waited for: 16 -> 15; matrix products, arithmetic and copies ran while one was open for 5% -> 6% of each run, Pallas kernels for 19% -> 18%
where the time goes in v21:
time: 218 us; the launch traced here: 217 us
  waiting for transfers between devices  86.9 us (40%)
  Pallas kernels  46.3 us (21%)
  local copies, waits for them, and re-layouts  41.8 us (19%)
  starting transfers between devices  32.7 us (15%)
  other arithmetic  4.63 us (2%)
  between operations  4.46 us (2%)
    ppermute x18, waiting for transfers between devices, send(): return lax.ppermute(value, 'tensor', pairs)  61.2 us
    pallas_call x8, Pallas kernels, rows_call(): pl.pallas_call(functools.partial(rows_kernel, group), in_specs=[pl.BlockS...  35.5 us
    unnamed x38, local copies, waits for them, and re-layouts  31.2 us
    all_to_all x2, waiting for transfers between devices, chain_body(): lax.all_to_all(sent, 'tensor', split_axis=0, concat_axis=0, tiled=True)  25.7 us
    ppermute x18, starting transfers between devices, send(): return lax.ppermute(value, 'tensor', pairs)  20.5 us
    all_to_all x2, starting transfers between devices, chain_body(): lax.all_to_all(sent, 'tensor', split_axis=0, concat_axis=0, tiled=True)  8.53 us
  transfers between devices with their start and end apart: 24, of which 15 were waited for; matrix products, arithmetic and copies ran while one was open for 6% of the time, Pallas kernels for 18%

profile of v21, /device:TPU:0, one launch (start us, length us, event | category | flops | bytes accessed | tf_op | source)
XLA Modules:
  0.0 216.8 jit_solution(5333872703896077860)
XLA Ops:
  0.0 3.1 %slice_bitcast_fusion = (bf16[64,8192]{1,0:T(8,128)(2,1)}, bf16[64,8192]{1,0:T(8,128)(2,1)}) fusion(bf16[1,128,8192]{2,1,0:T(8,128)(2,1)} %param.6), kind=kLoop, calls=%fused_computation.4 | loop fusion | bytes 4194304 | tf_op jit(solution)/shard_map/slice | solution.py:305
  3.1 3.0 %collective-permute-start = (bf16[64,8192]{1,0:T(8,128)(2,1)}, bf16[64,8192]{1,0:T(8,128)(2,1)}, u32[]{:S(2)}, u32[]{:S(2)}) collective-permute-start(bf16[64,8192]{1,0:T(8,128)(2,1)} %get-tuple-element.162), channel_id=1, source_target_pairs={{0,4},{4,8},{8,12},{12,14},{14,10},{10,6},{6,2},{2,0},{1,5},{5,9},... | collective-permute-start | bytes 3145736 | tf_op jit(solution)/shard_map/ppermute | solution.py:108
  6.1 2.0 collective-permute-start.4
  8.1 22.2 %collective-permute-done.refs_0_ = bf16[64,8192]{1,0:T(8,128)(2,1)} collective-permute-done((bf16[64,8192]{1,0:T(8,128)(2,1)}, bf16[64,8192]{1,0:T(8,128)(2,1)}, u32[]{:S(2)}, u32[]{:S(2)}) %collective-permute-start) | collective-permute-done | bytes 1048608 | tf_op jit(solution)/shard_map/ppermute | solution.py:108
  30.4 2.2 collective-permute-done.1.refs_1_
  36.2 1.4 pad_add_fusion.table
  37.6 2.2 pack.1
  42.2 2.7 %dynamic-slice_bitcast_fusion = (bf16[64,8192]{1,0:T(8,128)(2,1)}, bf16[64,8192]{1,0:T(8,128)(2,1)S(1)}) fusion(bf16[4,64,8192]{2,1,0:T(8,128)(2,1)} %param.8, s32[]{:T(128)S(6)} %select_n.166, s32[]{:T(128)S(6)} %select_n.165), kind=kLoop, calls=%fused_computation.2 | loop fusion | bytes 4194312 | tf_op jit(solution)/shard_map/jit(dynamic_index_in_dim)/squeeze | solution.py:325
  45.5 1.5 collective-permute-start.2
  47.7 2.1 pad_maximum_fusion
  49.9 2.9 %collective-permute-done.4.refs_1_ = bf16[64,8192]{1,0:T(8,128)(2,1)S(1)} collective-permute-done((bf16[64,8192]{1,0:T(8,128)(2,1)}, bf16[64,8192]{1,0:T(8,128)(2,1)S(1)}, u32[]{:S(2)}, u32[]{:S(2)}) %collective-permute-start.4) | collective-permute-done | bytes 1048608 | tf_op jit(solution)/shard_map/ppermute | solution.py:108
  52.7 2.3 %collective-permute-done.5.refs_0_ = bf16[64,8192]{1,0:T(8,128)(2,1)} collective-permute-done((bf16[64,8192]{1,0:T(8,128)(2,1)}, bf16[64,8192]{1,0:T(8,128)(2,1)}, u32[]{:S(2)}, u32[]{:S(2)}) %collective-permute-start.5) | collective-permute-done | bytes 1048608 | tf_op jit(solution)/shard_map/ppermute | solution.py:108
  55.0 1.6 collective-permute-start.10
  57.6 5.8 %copy-done.4 = bf16[8192,1024]{1,0:T(8,128)(2,1)S(1)} copy-done((bf16[8192,1024]{1,0:T(8,128)(2,1)S(1)}, bf16[8192,1024]{1,0:T(8,128)(2,1)}, u32[]{:S(2)}) %copy-start.4) | copy-done | bytes 16777240
  63.4 2.8 %pin.1.weights = bf16[8192,1152]{1,0:T(8,128)(2,1)S(1)} custom-call(bf16[8192,1024]{1,0:T(8,128)(2,1)S(1)} %copy-done.4, bf16[64,8192]{1,0:T(8,128)(2,1)S(1)} %get-tuple-element.160.own, bf16[64,8192]{1,0:T(8,128)(2,1)S(1)} %collective-permute-done.7.swapped), custom_call_target="tpu_custom_call" | custom-call | flops 1 | bytes 1 | tf_op jit(solution)/shard_map/pin/pallas_call | solution.py:138
  66.2 3.5 %rows.8 = (f32[128,1024]{1,0:T(8,128)S(1)}, bf16[128,128]{1,0:T(8,128)(2,1)S(1)}) custom-call(s32[2,16]{1,0:T(2,128)S(1)} %add_convert_fusion.table, bf16[8192,1152]{1,0:T(8,128)(2,1)S(1)} %pin.1.weights, bf16[128,8192]{1,0:T(8,128)(2,1)S(1)} %bitcast.63, bf16[128,128]{1,0:T(8,128)(2,1)S(1)} %broadcast_in_dim.49.refs_1_), custom_call_target="tpu_custom_call" | custom-call | flops 1 | bytes 1 | tf_op jit(solution)/shard_map/rows/pallas_call | solution.py:175
  69.7 1.6 copy-done.6
  71.2 5.9 %rows.9 = (f32[128,1024]{1,0:T(8,128)S(1)}, bf16[128,128]{1,0:T(8,128)(2,1)S(1)}) custom-call(s32[2,16]{1,0:T(2,128)S(1)} %add_convert_fusion.table, bf16[8192,1152]{1,0:T(8,128)(2,1)S(1)} %pin.1.weights, bf16[64,8192]{1,0:T(8,128)(2,1)} %collective-permute-done.refs_0_, bf16[64,8192]{1,0:T(8,128)(2,1)} %collective-permute-done.1.refs_1_, ...), custom_call_target="tpu_custom_call" | custom-call | flops 1 | bytes 1 | tf_op jit(solution)/shard_map/rows/pallas_call | solution.py:175
  78.0 1.6 collective-permute-start.8
  80.0 4.2 %rows.10 = (f32[128,1024]{1,0:T(8,128)S(1)}, bf16[128,128]{1,0:T(8,128)(2,1)S(1)}) custom-call(s32[2,16]{1,0:T(2,128)S(1)} %add_convert_fusion.table, bf16[8192,1152]{1,0:T(8,128)(2,1)S(1)} %pin.1.weights, bf16[64,8192]{1,0:T(8,128)(2,1)} %collective-permute-done.5.refs_0_, bf16[64,8192]{1,0:T(8,128)(2,1)S(1)} %collective-permute-done.4.refs_1_, ...), custom_call_target="tpu_custom_call" | custom-call | flops 1 | bytes 1 | tf_op jit(solution)/shard_map/rows/pallas_call | solution.py:175
  85.0 4.5 %rows.11 = (f32[128,1024]{1,0:T(8,128)S(1)}, bf16[128,128]{1,0:T(8,128)(2,1)S(1)}) custom-call(s32[2,16]{1,0:T(2,128)S(1)} %add_convert_fusion.table, bf16[8192,1152]{1,0:T(8,128)(2,1)S(1)} %pin.1.weights, bf16[64,8192]{1,0:T(8,128)(2,1)} %collective-permute-done.2.refs_0_, bf16[64,8192]{1,0:T(8,128)(2,1)} %collective-permute-done.3.refs_1_, ...), custom_call_target="tpu_custom_call" | custom-call | flops 1 | bytes 1 | tf_op jit(solution)/shard_map/rows/pallas_call | solution.py:175
  90.3 7.5 %collective-permute-done.10.refs_1_ = bf16[64,8192]{1,0:T(8,128)(2,1)} collective-permute-done((bf16[64,8192]{1,0:T(8,128)(2,1)S(1)}, bf16[64,8192]{1,0:T(8,128)(2,1)}, u32[]{:S(2)}, u32[]{:S(2)}) %collective-permute-start.10) | collective-permute-done | bytes 1048608 | tf_op jit(solution)/shard_map/ppermute | solution.py:108
  97.8 2.2 collective-permute-done.11.refs_0_
  99.9 1.6 collective-permute-start.14
  102.0 4.5 %rows.12 = (f32[128,1024]{1,0:T(8,128)S(1)}, bf16[128,128]{1,0:T(8,128)(2,1)S(1)}) custom-call(s32[2,16]{1,0:T(2,128)S(1)} %add_convert_fusion.table, bf16[8192,1152]{1,0:T(8,128)(2,1)S(1)} %pin.1.weights, bf16[64,8192]{1,0:T(8,128)(2,1)} %collective-permute-done.11.refs_0_, bf16[64,8192]{1,0:T(8,128)(2,1)} %collective-permute-done.10.refs_1_, ...), custom_call_target="tpu_custom_call" | custom-call | flops 1 | bytes 1 | tf_op jit(solution)/shard_map/rows/pallas_call | solution.py:175
  107.2 12.9 %collective-permute-done.8.refs_0_ = bf16[64,8192]{1,0:T(8,128)(2,1)S(1)} collective-permute-done((bf16[64,8192]{1,0:T(8,128)(2,1)}, bf16[64,8192]{1,0:T(8,128)(2,1)S(1)}, u32[]{:S(2)}, u32[]{:S(2)}) %collective-permute-start.8) | collective-permute-done | bytes 1048608 | tf_op jit(solution)/shard_map/ppermute | solution.py:108
  120.1 2.3 %collective-permute-done.9.refs_1_ = bf16[64,8192]{1,0:T(8,128)(2,1)} collective-permute-done((bf16[64,8192]{1,0:T(8,128)(2,1)}, bf16[64,8192]{1,0:T(8,128)(2,1)}, u32[]{:S(2)}, u32[]{:S(2)}) %collective-permute-start.9) | collective-permute-done | bytes 1048608 | tf_op jit(solution)/shard_map/ppermute | solution.py:108
  123.2 4.8 %all-to-all-start = ((bf16[8,2,32,512]{3,2,1,0:T(8,128)(2,1)}), bf16[8,2,32,512]{3,2,1,0:T(8,128)(2,1)S(1)}, u32[]{:S(2)}, u32[]{:S(2)}) async-start(bf16[8,2,32,512]{3,2,1,0:T(8,128)(2,1)} %copy.11), calls=%async_computation | async-start | bytes 1048576 | tf_op jit(solution)/shard_map/all_to_all | solution.py:357
  128.1 2.0 collective-permute-start.12
  130.1 6.4 %copy-done.1 = bf16[8192,1152]{1,0:T(8,128)(2,1)S(1)} copy-done((bf16[8192,1152]{1,0:T(8,128)(2,1)S(1)}, bf16[8192,1152]{1,0:T(8,128)(2,1)}, u32[]{:S(2)}) %copy-start.1) | copy-done | bytes 18874392
  136.5 4.2 %rows.13 = (f32[128,1024]{1,0:T(8,128)S(1)}, bf16[128,128]{1,0:T(8,128)(2,1)S(1)}) custom-call(s32[2,16]{1,0:T(2,128)S(1)} %add_convert_fusion.table, bf16[8192,1152]{1,0:T(8,128)(2,1)S(1)} %copy-done.1, bf16[64,8192]{1,0:T(8,128)(2,1)S(1)} %collective-permute-done.8.refs_0_, bf16[64,8192]{1,0:T(8,128)(2,1)} %collective-permute-done.9.refs_1_, ...), custom_call_target="tpu_custom_call" | custom-call | flops 1 | bytes 1 | tf_op jit(solution)/shard_map/rows/pallas_call | solution.py:175
  142.6 2.3 %collective-permute-done.15.refs_0_ = bf16[64,8192]{1,0:T(8,128)(2,1)} collective-permute-done((bf16[64,8192]{1,0:T(8,128)(2,1)}, bf16[64,8192]{1,0:T(8,128)(2,1)}, u32[]{:S(2)}, u32[]{:S(2)}) %collective-permute-start.15) | collective-permute-done | bytes 1048608 | tf_op jit(solution)/shard_map/ppermute | solution.py:108
  144.9 12.1 %all-to-all-done = bf16[8,2,32,512]{3,2,1,0:T(8,128)(2,1)S(1)} async-done(((bf16[8,2,32,512]{3,2,1,0:T(8,128)(2,1)}), bf16[8,2,32,512]{3,2,1,0:T(8,128)(2,1)S(1)}, u32[]{:S(2)}, u32[]{:S(2)}) %all-to-all-start) | async-done | bytes 524320 | tf_op jit(solution)/shard_map/all_to_all | solution.py:357
  157.0 1.9 copy.12
  158.9 3.7 %all-to-all-start.1 = ((bf16[8,2,32,512]{3,2,1,0:T(8,128)(2,1)}), bf16[8,2,32,512]{3,2,1,0:T(8,128)(2,1)S(1)}, u32[]{:S(2)}, u32[]{:S(2)}) async-start(bf16[8,2,32,512]{3,2,1,0:T(8,128)(2,1)} %copy.12), calls=%async_computation.1 | async-start | bytes 1048576 | tf_op jit(solution)/shard_map/all_to_all | solution.py:357
  162.8 6.4 %copy-done.2 = bf16[8192,1152]{1,0:T(8,128)(2,1)S(1)} copy-done((bf16[8192,1152]{1,0:T(8,128)(2,1)S(1)}, bf16[8192,1152]{1,0:T(8,128)(2,1)}, u32[]{:S(2)}) %copy-start.2) | copy-done | bytes 18874392
  169.2 4.2 %rows.14 = (f32[128,1024]{1,0:T(8,128)S(1)}, bf16[128,128]{1,0:T(8,128)(2,1)S(1)}) custom-call(s32[2,16]{1,0:T(2,128)S(1)} %add_convert_fusion.table, bf16[8192,1152]{1,0:T(8,128)(2,1)S(1)} %copy-done.2, bf16[64,8192]{1,0:T(8,128)(2,1)} %collective-permute-done.15.refs_0_, bf16[64,8192]{1,0:T(8,128)(2,1)S(1)} %collective-permute-done.14.refs_1_, ...), custom_call_target="tpu_custom_call" | custom-call | flops 1 | bytes 1 | tf_op jit(solution)/shard_map/rows/pallas_call | solution.py:175
  174.2 1.5 collective-permute-done.13.refs_1_
  175.7 13.5 %all-to-all-done.1 = bf16[8,2,32,512]{3,2,1,0:T(8,128)(2,1)S(1)} async-done(((bf16[8,2,32,512]{3,2,1,0:T(8,128)(2,1)}), bf16[8,2,32,512]{3,2,1,0:T(8,128)(2,1)S(1)}, u32[]{:S(2)}, u32[]{:S(2)}) %all-to-all-start.1) | async-done | bytes 524320 | tf_op jit(solution)/shard_map/all_to_all | solution.py:357
  189.3 6.4 %copy-done.3 = bf16[8192,1152]{1,0:T(8,128)(2,1)S(1)} copy-done((bf16[8192,1152]{1,0:T(8,128)(2,1)S(1)}, bf16[8192,1152]{1,0:T(8,128)(2,1)}, u32[]{:S(2)}) %copy-start.3) | copy-done | bytes 18874392
  195.6 4.5 %rows.15 = (f32[128,1024]{1,0:T(8,128)S(1)}, bf16[128,128]{1,0:T(8,128)(2,1)S(1)}) custom-call(s32[2,16]{1,0:T(2,128)S(1)} %add_convert_fusion.table, bf16[8192,1152]{1,0:T(8,128)(2,1)S(1)} %copy-done.3, bf16[64,8192]{1,0:T(8,128)(2,1)} %collective-permute-done.12.refs_0_, bf16[64,8192]{1,0:T(8,128)(2,1)} %collective-permute-done.13.refs_1_, ...), custom_call_target="tpu_custom_call" | custom-call | flops 99999997952 | bytes 1 | tf_op jit(solution)/shard_map/rows/pallas_call | solution.py:175
  201.7 1.6 collective-permute-start.20
  204.8 1.6 collective-permute-start.21
  206.5 1.7 collective-permute-start.18
  208.2 2.6 %collective-permute-start.19 = (bf16[2,128,128]{2,1,0:T(8,128)(2,1)S(1)}, bf16[2,128,128]{2,1,0:T(8,128)(2,1)S(1)}, u32[]{:S(2)}, u32[]{:S(2)}) collective-permute-start(bf16[2,128,128]{2,1,0:T(8,128)(2,1)S(1)} %pad_maximum_fusion.1.refs_0_), channel_id=1, source_target_pairs={{0,12},{2,14},{4,8},{6,10},{8,4},{10,6},{12,0},{14,2},{1,13},{3,15... | collective-permute-start | bytes 196616 | tf_op jit(solution)/shard_map/ppermute | solution.py:108
  210.9 2.2 %collect.1.base = f32[8,128,1024]{2,1,0:T(8,128)S(1)} custom-call(f32[128,1024]{1,0:T(8,128)} %copy-done.6, f32[128,1024]{1,0:T(8,128)} %copy-done.7, f32[128,1024]{1,0:T(8,128)} %copy-done.8, f32[128,1024]{1,0:T(8,128)} %copy-done.9, f32[128,1024]{1,0:T(8,128)} %copy-done.10, f32[128,1024]{1,0:T(8,128)} %copy-done.11, f32[128,1024]{1,0:T(8,128)} %copy-done.12, ...), custom_call_target="tpu_custom_call" | custom-call | flops 1 | bytes 1 | tf_op jit(solution)/shard_map/collect/pallas_call | solution.py:242
  213.2 1.1 collective-permute-done.19.refs_3_
  214.3 2.3 %finish.1 = bf16[1024,1024]{1,0:T(8,128)(2,1)} custom-call(s32[4,16]{1,0:T(4,128)S(1)} %add_add_fusion.table, f32[8,128,1024]{2,1,0:T(8,128)S(1)} %collect.1.base, bf16[2,128,128]{2,1,0:T(8,128)(2,1)S(1)} %pad_maximum_fusion.1.refs_0_, bf16[2,128,128]{2,1,0:T(8,128)(2,1)S(1)} %collective-permute-done.17.refs_1_, ...), custom_call_target="tpu_custom_call" | custom-call | flops 1 | bytes 1 | tf_op jit(solution)/shard_map/finish/pallas_call | solution.py:280
  (74 shorter events, 15.6 us)
Async XLA Ops:
  0.0 32.5 %copy-start.18 = (s32[64]{0:T(128)S(1)}, s32[64]{0:T(128)}, u32[]{:S(2)}) copy-start(s32[64]{0:T(128)} %param.10) | copy-start | bytes 772
  0.0 32.5 %copy-start.17 = (s32[2,8]{1,0:T(2,128)S(1)}, s32[2,8]{1,0:T(2,128)}, u32[]{:S(2)}) copy-start(s32[2,8]{1,0:T(2,128)} %param.11) | copy-start | bytes 196
  3.1 27.3 %collective-permute-start = (bf16[64,8192]{1,0:T(8,128)(2,1)}, bf16[64,8192]{1,0:T(8,128)(2,1)}, u32[]{:S(2)}, u32[]{:S(2)}) collective-permute-start(bf16[64,8192]{1,0:T(8,128)(2,1)} %get-tuple-element.162), channel_id=1, source_target_pairs={{0,4},{4,8},{8,12},{12,14},{14,10},{10,6},{6,2},{2,0},{1,5},{5,9},... | collective-permute-start | bytes 3145736 | tf_op jit(solution)/shard_map/ppermute | solution.py:108
  6.1 26.4 %collective-permute-start.1 = (bf16[64,8192]{1,0:T(8,128)(2,1)}, bf16[64,8192]{1,0:T(8,128)(2,1)}, u32[]{:S(2)}, u32[]{:S(2)}) collective-permute-start(bf16[64,8192]{1,0:T(8,128)(2,1)} %get-tuple-element.161), channel_id=1, source_target_pairs={{4,0},{8,4},{12,8},{14,12},{10,14},{6,10},{2,6},{0,2},{5,1},{9,5},... | collective-permute-start | bytes 3145736 | tf_op jit(solution)/shard_map/ppermute | solution.py:108
  6.1 46.6 %collective-permute-start.4 = (bf16[64,8192]{1,0:T(8,128)(2,1)}, bf16[64,8192]{1,0:T(8,128)(2,1)S(1)}, u32[]{:S(2)}, u32[]{:S(2)}) collective-permute-start(bf16[64,8192]{1,0:T(8,128)(2,1)} %get-tuple-element.161), channel_id=1, source_target_pairs={{0,4},{4,8},{8,12},{12,14},{14,10},{10,6},{6,2},{2,0},{1,5},{5,9},... | collective-permute-start | bytes 3145736 | tf_op jit(solution)/shard_map/ppermute | solution.py:108
  8.1 46.8 %collective-permute-start.5 = (bf16[64,8192]{1,0:T(8,128)(2,1)}, bf16[64,8192]{1,0:T(8,128)(2,1)}, u32[]{:S(2)}, u32[]{:S(2)}) collective-permute-start(bf16[64,8192]{1,0:T(8,128)(2,1)} %get-tuple-element.162), channel_id=1, source_target_pairs={{4,0},{8,4},{12,8},{14,12},{10,14},{6,10},{2,6},{0,2},{5,1},{9,5},... | collective-permute-start | bytes 3145736 | tf_op jit(solution)/shard_map/ppermute | solution.py:108
  40.9 6.1 %collective-permute-start.6 = (bf16[8,64,512]{2,1,0:T(8,128)(2,1)}, bf16[8,64,512]{2,1,0:T(8,128)(2,1)}, u32[]{:S(2)}, u32[]{:S(2)}) collective-permute-start(bf16[8,64,512]{2,1,0:T(8,128)(2,1)} %get-tuple-element.165), channel_id=1, source_target_pairs={{0,1},{1,0},{2,3},{3,2},{4,5},{5,4},{6,7},{7,6},{8,9},{9,8},{10,11... | collective-permute-start | bytes 1572872 | tf_op jit(solution)/shard_map/ppermute | solution.py:112
  44.9 12.7 %collective-permute-start.7 = (bf16[64,8192]{1,0:T(8,128)(2,1)}, bf16[64,8192]{1,0:T(8,128)(2,1)S(1)}, u32[]{:S(2)}, u32[]{:S(2)}) collective-permute-start(bf16[64,8192]{1,0:T(8,128)(2,1)} %get-tuple-element.159), channel_id=1, source_target_pairs={{0,1},{1,0},{2,3},{3,2},{4,5},{5,4},{6,7},{7,6},{8,9},{9,8},{10,11... | collective-permute-start | bytes 3145736 | tf_op jit(solution)/shard_map/ppermute | solution.py:112
  45.5 32.5 %collective-permute-start.2 = (bf16[64,8192]{1,0:T(8,128)(2,1)}, bf16[64,8192]{1,0:T(8,128)(2,1)}, u32[]{:S(2)}, u32[]{:S(2)}) collective-permute-start(bf16[64,8192]{1,0:T(8,128)(2,1)} %collective-permute-done.refs_0_), channel_id=1, source_target_pairs={{0,4},{4,8},{8,12},{12,14},{14,10},{10,6},{6,2},{2,0},{1,5},{5,9},... | collective-permute-start | bytes 3145736 | tf_op jit(solution)/shard_map/ppermute | solution.py:108
  47.0 31.0 %collective-permute-start.3 = (bf16[64,8192]{1,0:T(8,128)(2,1)}, bf16[64,8192]{1,0:T(8,128)(2,1)}, u32[]{:S(2)}, u32[]{:S(2)}) collective-permute-start(bf16[64,8192]{1,0:T(8,128)(2,1)} %collective-permute-done.1.refs_1_), channel_id=1, source_target_pairs={{4,0},{8,4},{12,8},{14,12},{10,14},{6,10},{2,6},{0,2},{5,1},{9,5},... | collective-permute-start | bytes 3145736 | tf_op jit(solution)/shard_map/ppermute | solution.py:108
  47.7 9.8 %copy-start.14 = (s32[16]{0:T(128)}, s32[16]{0:T(128)S(1)}, u32[]{:S(2)}) copy-start(s32[16]{0:T(128)S(1)} %select_reduce_fusion.1) | copy-start | bytes 196
  55.0 42.8 %collective-permute-start.10 = (bf16[64,8192]{1,0:T(8,128)(2,1)S(1)}, bf16[64,8192]{1,0:T(8,128)(2,1)}, u32[]{:S(2)}, u32[]{:S(2)}) collective-permute-start(bf16[64,8192]{1,0:T(8,128)(2,1)S(1)} %collective-permute-done.4.refs_1_), channel_id=1, source_target_pairs={{0,4},{4,8},{8,12},{12,14},{14,10},{10,6},{6,2},{2,0},{1,5},{5,9},... | collective-permute-start | bytes 3145736 | tf_op jit(solution)/shard_map/ppermute | solution.py:108
  56.6 43.4 %collective-permute-start.11 = (bf16[64,8192]{1,0:T(8,128)(2,1)}, bf16[64,8192]{1,0:T(8,128)(2,1)}, u32[]{:S(2)}, u32[]{:S(2)}) collective-permute-start(bf16[64,8192]{1,0:T(8,128)(2,1)} %collective-permute-done.5.refs_0_), channel_id=1, source_target_pairs={{4,0},{8,4},{12,8},{14,12},{10,14},{6,10},{2,6},{0,2},{5,1},{9,5},... | collective-permute-start | bytes 3145736 | tf_op jit(solution)/shard_map/ppermute | solution.py:108
  57.6 5.8 %copy-start.4 = (bf16[8192,1024]{1,0:T(8,128)(2,1)S(1)}, bf16[8192,1024]{1,0:T(8,128)(2,1)}, u32[]{:S(2)}) copy-start(bf16[8192,1024]{1,0:T(8,128)(2,1)} %weight.1) | copy-start | bytes 50331652
  63.4 2.8 %copy-start.5 = (bf16[1,128,8192]{2,1,0:T(8,128)(2,1)S(1)}, bf16[1,128,8192]{2,1,0:T(8,128)(2,1)}, u32[]{:S(2)}) copy-start(bf16[1,128,8192]{2,1,0:T(8,128)(2,1)} %param.6) | copy-start | bytes 6291460
  66.1 35.8 %copy-start = (bf16[8192,1152]{1,0:T(8,128)(2,1)}, bf16[8192,1152]{1,0:T(8,128)(2,1)S(1)}, u32[]{:S(2)}) copy-start(bf16[8192,1152]{1,0:T(8,128)(2,1)S(1)} %pin.1.weights) | copy-start | bytes 56623108
  69.6 1.6 copy-start.6
  77.2 0.8 copy-start.7
  78.0 42.2 %collective-permute-start.8 = (bf16[64,8192]{1,0:T(8,128)(2,1)}, bf16[64,8192]{1,0:T(8,128)(2,1)S(1)}, u32[]{:S(2)}, u32[]{:S(2)}) collective-permute-start(bf16[64,8192]{1,0:T(8,128)(2,1)} %collective-permute-done.2.refs_0_), channel_id=1, source_target_pairs={{0,4},{4,8},{8,12},{12,14},{14,10},{10,6},{6,2},{2,0},{1,5},{5,9},... | collective-permute-start | bytes 3145736 | tf_op jit(solution)/shard_map/ppermute | solution.py:108
  79.6 42.8 %collective-permute-start.9 = (bf16[64,8192]{1,0:T(8,128)(2,1)}, bf16[64,8192]{1,0:T(8,128)(2,1)}, u32[]{:S(2)}, u32[]{:S(2)}) collective-permute-start(bf16[64,8192]{1,0:T(8,128)(2,1)} %collective-permute-done.3.refs_1_), channel_id=1, source_target_pairs={{4,0},{8,4},{12,8},{14,12},{10,14},{6,10},{2,6},{0,2},{5,1},{9,5},... | collective-permute-start | bytes 3145736 | tf_op jit(solution)/shard_map/ppermute | solution.py:108
  84.2 0.8 copy-start.8
  89.5 0.8 copy-start.9
  99.9 42.7 %collective-permute-start.14 = (bf16[64,8192]{1,0:T(8,128)(2,1)}, bf16[64,8192]{1,0:T(8,128)(2,1)S(1)}, u32[]{:S(2)}, u32[]{:S(2)}) collective-permute-start(bf16[64,8192]{1,0:T(8,128)(2,1)} %collective-permute-done.10.refs_1_), channel_id=1, source_target_pairs={{0,4},{4,8},{8,12},{12,14},{14,10},{10,6},{6,2},{2,0},{1,5},{5,9},... | collective-permute-start | bytes 3145736 | tf_op jit(solution)/shard_map/ppermute | solution.py:108
  101.5 43.4 %collective-permute-start.15 = (bf16[64,8192]{1,0:T(8,128)(2,1)}, bf16[64,8192]{1,0:T(8,128)(2,1)}, u32[]{:S(2)}, u32[]{:S(2)}) collective-permute-start(bf16[64,8192]{1,0:T(8,128)(2,1)} %collective-permute-done.11.refs_0_), channel_id=1, source_target_pairs={{4,0},{8,4},{12,8},{14,12},{10,14},{6,10},{2,6},{0,2},{5,1},{9,5},... | collective-permute-start | bytes 3145736 | tf_op jit(solution)/shard_map/ppermute | solution.py:108
  106.5 0.8 copy-start.10
  123.2 33.8 %all-to-all-start = ((bf16[8,2,32,512]{3,2,1,0:T(8,128)(2,1)}), bf16[8,2,32,512]{3,2,1,0:T(8,128)(2,1)S(1)}, u32[]{:S(2)}, u32[]{:S(2)}) async-start(bf16[8,2,32,512]{3,2,1,0:T(8,128)(2,1)} %copy.11), calls=%async_computation | async-start | bytes 1048576 | tf_op jit(solution)/shard_map/all_to_all | solution.py:357
  128.1 46.1 %collective-permute-start.12 = (bf16[64,8192]{1,0:T(8,128)(2,1)S(1)}, bf16[64,8192]{1,0:T(8,128)(2,1)}, u32[]{:S(2)}, u32[]{:S(2)}) collective-permute-start(bf16[64,8192]{1,0:T(8,128)(2,1)S(1)} %collective-permute-done.8.refs_0_), channel_id=1, source_target_pairs={{0,4},{4,8},{8,12},{12,14},{14,10},{10,6},{6,2},{2,0},{1,5},{5,9},... | collective-permute-start | bytes 3145736 | tf_op jit(solution)/shard_map/ppermute | solution.py:108
  130.1 45.6 %collective-permute-start.13 = (bf16[64,8192]{1,0:T(8,128)(2,1)}, bf16[64,8192]{1,0:T(8,128)(2,1)}, u32[]{:S(2)}, u32[]{:S(2)}) collective-permute-start(bf16[64,8192]{1,0:T(8,128)(2,1)} %collective-permute-done.9.refs_1_), channel_id=1, source_target_pairs={{4,0},{8,4},{12,8},{14,12},{10,14},{6,10},{2,6},{0,2},{5,1},{9,5},... | collective-permute-start | bytes 3145736 | tf_op jit(solution)/shard_map/ppermute | solution.py:108
  130.1 6.4 %copy-start.1 = (bf16[8192,1152]{1,0:T(8,128)(2,1)S(1)}, bf16[8192,1152]{1,0:T(8,128)(2,1)}, u32[]{:S(2)}) copy-start(bf16[8192,1152]{1,0:T(8,128)(2,1)} %copy-done) | copy-start | bytes 56623108
  140.7 0.8 copy-start.11
  158.9 30.4 %all-to-all-start.1 = ((bf16[8,2,32,512]{3,2,1,0:T(8,128)(2,1)}), bf16[8,2,32,512]{3,2,1,0:T(8,128)(2,1)S(1)}, u32[]{:S(2)}, u32[]{:S(2)}) async-start(bf16[8,2,32,512]{3,2,1,0:T(8,128)(2,1)} %copy.12), calls=%async_computation.1 | async-start | bytes 1048576 | tf_op jit(solution)/shard_map/all_to_all | solution.py:357
  162.8 6.4 %copy-start.2 = (bf16[8192,1152]{1,0:T(8,128)(2,1)S(1)}, bf16[8192,1152]{1,0:T(8,128)(2,1)}, u32[]{:S(2)}) copy-start(bf16[8192,1152]{1,0:T(8,128)(2,1)} %copy-done) | copy-start | bytes 56623108
  173.4 0.8 copy-start.12
  189.2 6.4 %copy-start.3 = (bf16[8192,1152]{1,0:T(8,128)(2,1)S(1)}, bf16[8192,1152]{1,0:T(8,128)(2,1)}, u32[]{:S(2)}) copy-start(bf16[8192,1152]{1,0:T(8,128)(2,1)} %copy-done) | copy-start | bytes 56623108
  195.6 5.4 %copy-start.15 = (s32[16]{0:T(128)S(1)}, s32[16]{0:T(128)}, u32[]{:S(2)}) copy-start(s32[16]{0:T(128)} %copy-done.14) | copy-start | bytes 196
  195.6 15.2 %copy-start.16 = (s32[1,16]{1,0:T(1,128)S(1)}, s32[1,16]{1,0:T(1,128)}, u32[]{:S(2)}) copy-start(s32[1,16]{1,0:T(1,128)} %get-tuple-element.169) | copy-start | bytes 196
  200.1 10.8 %copy-start.13 = (f32[128,1024]{1,0:T(8,128)}, f32[128,1024]{1,0:T(8,128)S(1)}, u32[]{:S(2)}) copy-start(f32[128,1024]{1,0:T(8,128)S(1)} %get-tuple-element.150.refs_7_) | copy-start | bytes 1572868
  200.1 4.0 %collective-permute-start.16 = (bf16[128,128]{1,0:T(8,128)(2,1)S(1)}, bf16[128,128]{1,0:T(8,128)(2,1)S(1)}, u32[]{:S(2)}, u32[]{:S(2)}) collective-permute-start(bf16[128,128]{1,0:T(8,128)(2,1)S(1)} %get-tuple-element.151), channel_id=1, source_target_pairs={{0,2},{2,0},{4,6},{6,4},{8,10},{10,8},{12,14},{14,12},{1,3},{3,1},... | collective-permute-start | bytes 98312 | tf_op jit(solution)/shard_map/ppermute | solution.py:108
  201.7 12.6 %collective-permute-start.20 = (bf16[8,32,512]{2,1,0:T(8,128)(2,1)S(1)}, bf16[8,32,512]{2,1,0:T(8,128)(2,1)S(1)}, u32[]{:S(2)}, u32[]{:S(2)}) collective-permute-start(bf16[8,32,512]{2,1,0:T(8,128)(2,1)S(1)} %take.2.refs_4_), channel_id=1, source_target_pairs={{0,16},{16,0},{1,17},{17,1},{2,18},{18,2},{3,19},{19,3},{4,20},{20... | collective-permute-start | bytes 786440 | tf_op jit(solution)/shard_map/ppermute | solution.py:112
  204.8 9.5 %collective-permute-start.21 = (bf16[8,32,512]{2,1,0:T(8,128)(2,1)S(1)}, bf16[8,32,512]{2,1,0:T(8,128)(2,1)S(1)}, u32[]{:S(2)}, u32[]{:S(2)}) collective-permute-start(bf16[8,32,512]{2,1,0:T(8,128)(2,1)S(1)} %take.3.refs_5_), channel_id=1, source_target_pairs={{0,16},{16,0},{1,17},{17,1},{2,18},{18,2},{3,19},{19,3},{4,20},{20... | collective-permute-start | bytes 786440 | tf_op jit(solution)/shard_map/ppermute | solution.py:112
  206.4 6.8 %collective-permute-start.17 = (bf16[2,128,128]{2,1,0:T(8,128)(2,1)S(1)}, bf16[2,128,128]{2,1,0:T(8,128)(2,1)S(1)}, u32[]{:S(2)}, u32[]{:S(2)}) collective-permute-start(bf16[2,128,128]{2,1,0:T(8,128)(2,1)S(1)} %pad_maximum_fusion.1.refs_0_), channel_id=1, source_target_pairs={{0,4},{2,6},{4,0},{6,2},{8,12},{10,14},{12,8},{14,10},{1,5},{3,7},... | collective-permute-start | bytes 196616 | tf_op jit(solution)/shard_map/ppermute | solution.py:108
  206.5 6.7 %collective-permute-start.18 = (bf16[2,128,128]{2,1,0:T(8,128)(2,1)S(1)}, bf16[2,128,128]{2,1,0:T(8,128)(2,1)S(1)}, u32[]{:S(2)}, u32[]{:S(2)}) collective-permute-start(bf16[2,128,128]{2,1,0:T(8,128)(2,1)S(1)} %pad_maximum_fusion.1.refs_0_), channel_id=1, source_target_pairs={{0,8},{2,10},{4,12},{6,14},{8,0},{10,2},{12,4},{14,6},{1,9},{3,11}... | collective-permute-start | bytes 196616 | tf_op jit(solution)/shard_map/ppermute | solution.py:108
  208.2 6.1 %collective-permute-start.19 = (bf16[2,128,128]{2,1,0:T(8,128)(2,1)S(1)}, bf16[2,128,128]{2,1,0:T(8,128)(2,1)S(1)}, u32[]{:S(2)}, u32[]{:S(2)}) collective-permute-start(bf16[2,128,128]{2,1,0:T(8,128)(2,1)S(1)} %pad_maximum_fusion.1.refs_0_), channel_id=1, source_target_pairs={{0,12},{2,14},{4,8},{6,10},{8,4},{10,6},{12,0},{14,2},{1,13},{3,15... | collective-permute-start | bytes 196616 | tf_op jit(solution)/shard_map/ppermute | solution.py:108

commit v22 on v20

--- a/solution.py
+++ b/solution.py
@@ -121,6 +121,30 @@
 
 def in_vmem(count):
     return [pl.BlockSpec(memory_space=pltpu.VMEM)] * count
+
+
+def split_kernel(rows, first, second, sems):
+    copies = [
+        pltpu.make_async_copy(rows.at[pl.ds(i * HALF, HALF)], half, sems.at[i])
+        for i, half in enumerate((first, second))
+    ]
+    for copy in copies:
+        copy.start()
+    for copy in copies:
+        copy.wait()
+
+
+def split_call(rows):
+    half = pltpu.VMEM((HALF, rows.shape[1]), rows.dtype)
+    return pl.pallas_call(
+        split_kernel,
+        in_specs=[pl.BlockSpec(memory_space=pl.ANY)],
+        out_specs=in_vmem(2),
+        out_shape=[half, half],
+        scratch_shapes=[pltpu.SemaphoreType.DMA((2,))],
+        name="split",
+        **settings(),
+    )(pltpu.with_memory_space_constraint(rows, pltpu.HBM))
 
 
 def pin_kernel(weight, own, swapped, out, sem):
@@ -300,7 +324,7 @@
     myself = me * 2 + store
     held, rank, width = adapter_down_maps.shape
     rows = tokens[0]
-    halves = [rows[:HALF], rows[HALF:]]
+    halves = list(split_call(rows))
 
     ahead, back = list(halves), list(halves[::-1])
     flight = [(send(ahead[k], AHEAD), send(back[k], BACK)) for k in range(2)]

time: 205 us -> 205 us (level)
  local copies, waits for them, and re-layouts: 30.4 us -> 27.2 us
  Pallas kernels: 43.6 us -> 46.5 us
    slice x1 -> x0, local copies, waits for them, and re-layouts: 3.08 us -> none  [chain_body(): halves = [rows[:HALF], rows[HALF:]]]
    pallas_call x0 -> x1, Pallas kernels: none -> 2.9 us  [split_call(): pl.pallas_call(split_kernel, in_specs=[pl.BlockSpec(memory_space=pl.ANY)]...]
    unnamed x38 -> x34, local copies, waits for them, and re-layouts: 21.5 us -> 21.5 us
where the time goes in v22:
time: 205 us
  waiting for transfers between devices  94.1 us (46%)
  Pallas kernels  46.5 us (23%)
  starting transfers between devices  27.9 us (14%)
  local copies, waits for them, and re-layouts  27.2 us (13%)
  other arithmetic  4.49 us (2%)
  between operations  4.31 us (2%)
    ppermute x18, waiting for transfers between devices, send(): return lax.ppermute(value, 'tensor', pairs)  78.6 us
    pallas_call x8, Pallas kernels, rows_call(): pl.pallas_call(functools.partial(rows_kernel, group), in_specs=[pl.BlockS...  33.4 us
    unnamed x34, local copies, waits for them, and re-layouts  21.5 us
    ppermute x18, starting transfers between devices, send(): return lax.ppermute(value, 'tensor', pairs)  21.1 us
    all_to_all x1, waiting for transfers between devices, chain_body(): lax.all_to_all(up_sent, 'tensor', split_axis=0, concat_axis=0, tiled=True)  12.7 us
    all_to_all x1, starting transfers between devices, chain_body(): lax.all_to_all(up_sent, 'tensor', split_axis=0, concat_axis=0, tiled=True)  4.82 us
  transfers between devices with their start and end apart: 22, of which 17 were waited for; matrix products, arithmetic and copies ran while one was open for 5% of the time, Pallas kernels for 20%

profile of v22, /device:TPU:0, one launch (start us, length us, event | category | flops | bytes accessed | tf_op | source)
XLA Modules:
  0.0 204.6 jit_solution(730630512501581189)
XLA Ops:
  0.0 2.9 %split.1 = (bf16[64,8192]{1,0:T(8,128)(2,1)}, bf16[64,8192]{1,0:T(8,128)(2,1)}) custom-call(bf16[128,8192]{1,0:T(8,128)(2,1)} %bitcast.58), custom_call_target="tpu_custom_call" | custom-call | flops 1 | bytes 1 | tf_op jit(solution)/shard_map/split/pallas_call | solution.py:139
  2.9 3.1 %collective-permute-start = (bf16[64,8192]{1,0:T(8,128)(2,1)}, bf16[64,8192]{1,0:T(8,128)(2,1)}, u32[]{:S(2)}, u32[]{:S(2)}) collective-permute-start(bf16[64,8192]{1,0:T(8,128)(2,1)} %get-tuple-element.75), channel_id=1, source_target_pairs={{0,4},{4,8},{8,12},{12,14},{14,10},{10,6},{6,2},{2,0},{1,5},{5,9},... | collective-permute-start | bytes 3145736 | tf_op jit(solution)/shard_map/ppermute | solution.py:108
  6.0 2.0 collective-permute-start.4
  8.0 22.2 %collective-permute-done.refs_0_ = bf16[64,8192]{1,0:T(8,128)(2,1)} collective-permute-done((bf16[64,8192]{1,0:T(8,128)(2,1)}, bf16[64,8192]{1,0:T(8,128)(2,1)}, u32[]{:S(2)}, u32[]{:S(2)}) %collective-permute-start) | collective-permute-done | bytes 1048608 | tf_op jit(solution)/shard_map/ppermute | solution.py:108
  30.2 2.2 %collective-permute-done.1.refs_1_ = bf16[64,8192]{1,0:T(8,128)(2,1)} collective-permute-done((bf16[64,8192]{1,0:T(8,128)(2,1)}, bf16[64,8192]{1,0:T(8,128)(2,1)}, u32[]{:S(2)}, u32[]{:S(2)}) %collective-permute-start.1) | collective-permute-done | bytes 1048608 | tf_op jit(solution)/shard_map/ppermute | solution.py:108
  36.6 1.4 pad_add_fusion.table
  38.0 2.2 %pack.1 = bf16[2,8,64,512]{3,2,1,0:T(8,128)(2,1)S(1)} custom-call(s32[3]{0:T(128)S(1)} %pad_add_fusion.table, bf16[4,64,8192]{2,1,0:T(8,128)(2,1)} %up.1), custom_call_target="tpu_custom_call" | custom-call | flops 1 | bytes 1 | tf_op jit(solution)/shard_map/pack/pallas_call | solution.py:222
  40.1 1.1 slice_bitcast_fusion.1
  42.5 2.7 %dynamic-slice_bitcast_fusion = (bf16[64,8192]{1,0:T(8,128)(2,1)}, bf16[64,8192]{1,0:T(8,128)(2,1)S(1)}) fusion(bf16[4,64,8192]{2,1,0:T(8,128)(2,1)} %param.8, s32[]{:T(128)S(6)} %select_n.166, s32[]{:T(128)S(6)} %select_n.165), kind=kLoop, calls=%fused_computation.1 | loop fusion | bytes 4194312 | tf_op jit(solution)/shard_map/jit(dynamic_index_in_dim)/squeeze | solution.py:347
  45.7 1.6 collective-permute-start.2
  48.6 1.3 pad_maximum_fusion
  49.9 2.7 %collective-permute-done.4.refs_1_ = bf16[64,8192]{1,0:T(8,128)(2,1)S(1)} collective-permute-done((bf16[64,8192]{1,0:T(8,128)(2,1)}, bf16[64,8192]{1,0:T(8,128)(2,1)S(1)}, u32[]{:S(2)}, u32[]{:S(2)}) %collective-permute-start.4) | collective-permute-done | bytes 1048608 | tf_op jit(solution)/shard_map/ppermute | solution.py:108
  52.6 2.3 %collective-permute-done.5.refs_0_ = bf16[64,8192]{1,0:T(8,128)(2,1)} collective-permute-done((bf16[64,8192]{1,0:T(8,128)(2,1)}, bf16[64,8192]{1,0:T(8,128)(2,1)}, u32[]{:S(2)}, u32[]{:S(2)}) %collective-permute-start.5) | collective-permute-done | bytes 1048608 | tf_op jit(solution)/shard_map/ppermute | solution.py:108
  54.9 1.6 collective-permute-start.10
  56.9 5.8 %copy-done.2 = bf16[8192,1024]{1,0:T(8,128)(2,1)S(1)} copy-done((bf16[8192,1024]{1,0:T(8,128)(2,1)S(1)}, bf16[8192,1024]{1,0:T(8,128)(2,1)}, u32[]{:S(2)}) %copy-start.2) | copy-done | bytes 16777240
  62.7 2.8 %pin.1.weights = bf16[8192,1152]{1,0:T(8,128)(2,1)S(1)} custom-call(bf16[8192,1024]{1,0:T(8,128)(2,1)S(1)} %copy-done.2, bf16[64,8192]{1,0:T(8,128)(2,1)S(1)} %get-tuple-element.150.own, bf16[64,8192]{1,0:T(8,128)(2,1)S(1)} %collective-permute-done.7.swapped), custom_call_target="tpu_custom_call" | custom-call | flops 1 | bytes 1 | tf_op jit(solution)/shard_map/pin/pallas_call | solution.py:162
  65.5 3.4 %rows.8 = (f32[128,1024]{1,0:T(8,128)S(1)}, bf16[128,128]{1,0:T(8,128)(2,1)S(1)}) custom-call(s32[2,16]{1,0:T(2,128)S(1)} %add_convert_fusion.table, bf16[8192,1152]{1,0:T(8,128)(2,1)S(1)} %pin.1.weights, bf16[128,8192]{1,0:T(8,128)(2,1)S(1)} %bitcast.59, bf16[128,128]{1,0:T(8,128)(2,1)S(1)} %broadcast_in_dim.49.refs_1_), custom_call_target="tpu_custom_call" | custom-call | flops 1 | bytes 1 | tf_op jit(solution)/shard_map/rows/pallas_call | solution.py:199
  68.9 1.5 copy-done.6
  70.5 5.9 %rows.9 = (f32[128,1024]{1,0:T(8,128)S(1)}, bf16[128,128]{1,0:T(8,128)(2,1)S(1)}) custom-call(s32[2,16]{1,0:T(2,128)S(1)} %add_convert_fusion.table, bf16[8192,1152]{1,0:T(8,128)(2,1)S(1)} %pin.1.weights, bf16[64,8192]{1,0:T(8,128)(2,1)} %collective-permute-done.refs_0_, bf16[64,8192]{1,0:T(8,128)(2,1)} %collective-permute-done.1.refs_1_, ...), custom_call_target="tpu_custom_call" | custom-call | flops 1 | bytes 1 | tf_op jit(solution)/shard_map/rows/pallas_call | solution.py:199
  77.3 1.6 collective-permute-start.8
  79.4 4.1 %rows.10 = (f32[128,1024]{1,0:T(8,128)S(1)}, bf16[128,128]{1,0:T(8,128)(2,1)S(1)}) custom-call(s32[2,16]{1,0:T(2,128)S(1)} %add_convert_fusion.table, bf16[8192,1152]{1,0:T(8,128)(2,1)S(1)} %pin.1.weights, bf16[64,8192]{1,0:T(8,128)(2,1)} %collective-permute-done.5.refs_0_, bf16[64,8192]{1,0:T(8,128)(2,1)S(1)} %collective-permute-done.4.refs_1_, ...), custom_call_target="tpu_custom_call" | custom-call | flops 1 | bytes 1 | tf_op jit(solution)/shard_map/rows/pallas_call | solution.py:199
  84.3 4.4 %rows.11 = (f32[128,1024]{1,0:T(8,128)S(1)}, bf16[128,128]{1,0:T(8,128)(2,1)S(1)}) custom-call(s32[2,16]{1,0:T(2,128)S(1)} %add_convert_fusion.table, bf16[8192,1152]{1,0:T(8,128)(2,1)S(1)} %pin.1.weights, bf16[64,8192]{1,0:T(8,128)(2,1)} %collective-permute-done.2.refs_0_, bf16[64,8192]{1,0:T(8,128)(2,1)} %collective-permute-done.3.refs_1_, ...), custom_call_target="tpu_custom_call" | custom-call | flops 1 | bytes 1 | tf_op jit(solution)/shard_map/rows/pallas_call | solution.py:199
  89.5 8.0 %collective-permute-done.10.refs_1_ = bf16[64,8192]{1,0:T(8,128)(2,1)S(1)} collective-permute-done((bf16[64,8192]{1,0:T(8,128)(2,1)S(1)}, bf16[64,8192]{1,0:T(8,128)(2,1)S(1)}, u32[]{:S(2)}, u32[]{:S(2)}) %collective-permute-start.10) | collective-permute-done | bytes 1048608 | tf_op jit(solution)/shard_map/ppermute | solution.py:108
  97.5 2.2 %collective-permute-done.11.refs_0_ = bf16[64,8192]{1,0:T(8,128)(2,1)S(1)} collective-permute-done((bf16[64,8192]{1,0:T(8,128)(2,1)}, bf16[64,8192]{1,0:T(8,128)(2,1)S(1)}, u32[]{:S(2)}, u32[]{:S(2)}) %collective-permute-start.11) | collective-permute-done | bytes 1048608 | tf_op jit(solution)/shard_map/ppermute | solution.py:108
  99.7 1.6 collective-permute-start.14
  101.7 3.4 %rows.12 = (f32[128,1024]{1,0:T(8,128)S(1)}, bf16[128,128]{1,0:T(8,128)(2,1)S(1)}) custom-call(s32[2,16]{1,0:T(2,128)S(1)} %add_convert_fusion.table, bf16[8192,1152]{1,0:T(8,128)(2,1)S(1)} %pin.1.weights, bf16[64,8192]{1,0:T(8,128)(2,1)S(1)} %collective-permute-done.11.refs_0_, bf16[64,8192]{1,0:T(8,128)(2,1)S(1)} %collective-permute-done.10.refs_1_, ...), custom_call_target="tpu_custom_call" | custom-call | flops 1 | bytes 1 | tf_op jit(solution)/shard_map/rows/pallas_call | solution.py:199
  106.0 14.0 %collective-permute-done.8.refs_0_ = bf16[64,8192]{1,0:T(8,128)(2,1)S(1)} collective-permute-done((bf16[64,8192]{1,0:T(8,128)(2,1)}, bf16[64,8192]{1,0:T(8,128)(2,1)S(1)}, u32[]{:S(2)}, u32[]{:S(2)}) %collective-permute-start.8) | collective-permute-done | bytes 1048608 | tf_op jit(solution)/shard_map/ppermute | solution.py:108
  120.0 2.3 %collective-permute-done.9.refs_1_ = bf16[64,8192]{1,0:T(8,128)(2,1)} collective-permute-done((bf16[64,8192]{1,0:T(8,128)(2,1)}, bf16[64,8192]{1,0:T(8,128)(2,1)}, u32[]{:S(2)}, u32[]{:S(2)}) %collective-permute-start.9) | collective-permute-done | bytes 1048608 | tf_op jit(solution)/shard_map/ppermute | solution.py:108
  122.3 1.6 collective-permute-start.12
  124.3 4.2 %rows.13 = (f32[128,1024]{1,0:T(8,128)S(1)}, bf16[128,128]{1,0:T(8,128)(2,1)S(1)}) custom-call(s32[2,16]{1,0:T(2,128)S(1)} %add_convert_fusion.table, bf16[8192,1152]{1,0:T(8,128)(2,1)S(1)} %pin.1.weights, bf16[64,8192]{1,0:T(8,128)(2,1)S(1)} %collective-permute-done.8.refs_0_, bf16[64,8192]{1,0:T(8,128)(2,1)} %collective-permute-done.9.refs_1_, ...), custom_call_target="tpu_custom_call" | custom-call | flops 1 | bytes 1 | tf_op jit(solution)/shard_map/rows/pallas_call | solution.py:199
  129.3 13.2 %collective-permute-done.14.refs_1_ = bf16[64,8192]{1,0:T(8,128)(2,1)S(1)} collective-permute-done((bf16[64,8192]{1,0:T(8,128)(2,1)S(1)}, bf16[64,8192]{1,0:T(8,128)(2,1)S(1)}, u32[]{:S(2)}, u32[]{:S(2)}) %collective-permute-start.14) | collective-permute-done | bytes 1048608 | tf_op jit(solution)/shard_map/ppermute | solution.py:108
  142.5 2.2 %collective-permute-done.15.refs_0_ = bf16[64,8192]{1,0:T(8,128)(2,1)S(1)} collective-permute-done((bf16[64,8192]{1,0:T(8,128)(2,1)S(1)}, bf16[64,8192]{1,0:T(8,128)(2,1)S(1)}, u32[]{:S(2)}, u32[]{:S(2)}) %collective-permute-start.15) | collective-permute-done | bytes 1048608 | tf_op jit(solution)/shard_map/ppermute | solution.py:108
  146.7 4.8 %all-to-all-start = ((bf16[8,2,64,512]{3,2,1,0:T(8,128)(2,1)}), bf16[8,2,64,512]{3,2,1,0:T(8,128)(2,1)S(1)}, u32[]{:S(2)}, u32[]{:S(2)}) async-start(bf16[8,2,64,512]{3,2,1,0:T(8,128)(2,1)} %copy.9), calls=%async_computation | async-start | bytes 2097152 | tf_op jit(solution)/shard_map/all_to_all | solution.py:377
  151.5 6.4 %copy-done.1 = bf16[8192,1152]{1,0:T(8,128)(2,1)S(1)} copy-done((bf16[8192,1152]{1,0:T(8,128)(2,1)S(1)}, bf16[8192,1152]{1,0:T(8,128)(2,1)}, u32[]{:S(2)}) %copy-start.1) | copy-done | bytes 18874392
  157.9 1.2 copy-done.5
  159.1 3.5 %rows.14 = (f32[128,1024]{1,0:T(8,128)S(1)}, bf16[128,128]{1,0:T(8,128)(2,1)S(1)}) custom-call(s32[2,16]{1,0:T(2,128)S(1)} %add_convert_fusion.table, bf16[8192,1152]{1,0:T(8,128)(2,1)S(1)} %copy-done.1, bf16[64,8192]{1,0:T(8,128)(2,1)S(1)} %copy-done.5, bf16[64,8192]{1,0:T(8,128)(2,1)S(1)} %collective-permute-done.14.refs_1_, ...), custom_call_target="tpu_custom_call" | custom-call | flops 1 | bytes 1 | tf_op jit(solution)/shard_map/rows/pallas_call | solution.py:199
  163.3 1.7 collective-permute-done.12.refs_0_
  165.1 2.2 %collective-permute-done.13.refs_1_ = bf16[64,8192]{1,0:T(8,128)(2,1)} collective-permute-done((bf16[64,8192]{1,0:T(8,128)(2,1)}, bf16[64,8192]{1,0:T(8,128)(2,1)}, u32[]{:S(2)}, u32[]{:S(2)}) %collective-permute-start.13) | collective-permute-done | bytes 1048608 | tf_op jit(solution)/shard_map/ppermute | solution.py:108
  167.2 4.4 %rows.15 = (f32[128,1024]{1,0:T(8,128)S(1)}, bf16[128,128]{1,0:T(8,128)(2,1)S(1)}) custom-call(s32[2,16]{1,0:T(2,128)S(1)} %add_convert_fusion.table, bf16[8192,1152]{1,0:T(8,128)(2,1)S(1)} %copy-done.1, bf16[64,8192]{1,0:T(8,128)(2,1)} %collective-permute-done.12.refs_0_, bf16[64,8192]{1,0:T(8,128)(2,1)} %collective-permute-done.13.refs_1_, ...), custom_call_target="tpu_custom_call" | custom-call | flops 99999997952 | bytes 1 | tf_op jit(solution)/shard_map/rows/pallas_call | solution.py:199
  172.4 1.4 collective-permute-start.16
  174.0 2.4 %collective-permute-done.16 = bf16[128,128]{1,0:T(8,128)(2,1)S(1)} collective-permute-done((bf16[128,128]{1,0:T(8,128)(2,1)S(1)}, bf16[128,128]{1,0:T(8,128)(2,1)S(1)}, u32[]{:S(2)}, u32[]{:S(2)}) %collective-permute-start.16) | collective-permute-done | bytes 32800 | tf_op jit(solution)/shard_map/ppermute | solution.py:108
  176.4 12.7 %all-to-all-done = bf16[8,2,64,512]{3,2,1,0:T(8,128)(2,1)S(1)} async-done(((bf16[8,2,64,512]{3,2,1,0:T(8,128)(2,1)}), bf16[8,2,64,512]{3,2,1,0:T(8,128)(2,1)S(1)}, u32[]{:S(2)}, u32[]{:S(2)}) %all-to-all-start) | async-done | bytes 1048608 | tf_op jit(solution)/shard_map/all_to_all | solution.py:377
  189.8 1.6 collective-permute-start.20
  191.5 1.7 collective-permute-start.18
  193.2 2.6 %collective-permute-start.19 = (bf16[2,128,128]{2,1,0:T(8,128)(2,1)S(1)}, bf16[2,128,128]{2,1,0:T(8,128)(2,1)S(1)}, u32[]{:S(2)}, u32[]{:S(2)}) collective-permute-start(bf16[2,128,128]{2,1,0:T(8,128)(2,1)S(1)} %pad_maximum_fusion.1.refs_0_), channel_id=1, source_target_pairs={{0,12},{2,14},{4,8},{6,10},{8,4},{10,6},{12,0},{14,2},{1,13},{3,15... | collective-permute-start | bytes 196616 | tf_op jit(solution)/shard_map/ppermute | solution.py:108
  196.0 2.2 %collect.1.base = f32[8,128,1024]{2,1,0:T(8,128)S(1)} custom-call(f32[128,1024]{1,0:T(8,128)} %copy-done.6, f32[128,1024]{1,0:T(8,128)} %copy-done.7, f32[128,1024]{1,0:T(8,128)} %copy-done.8, f32[128,1024]{1,0:T(8,128)} %copy-done.9, f32[128,1024]{1,0:T(8,128)} %copy-done.10, f32[128,1024]{1,0:T(8,128)} %copy-done.11, f32[128,1024]{1,0:T(8,128)} %copy-done.12, ...), custom_call_target="tpu_custom_call" | custom-call | flops 1 | bytes 1 | tf_op jit(solution)/shard_map/collect/pallas_call | solution.py:266
  199.3 2.8 %collective-permute-done.20.refs_5_ = bf16[8,64,512]{2,1,0:T(8,128)(2,1)S(1)} collective-permute-done((bf16[8,64,512]{2,1,0:T(8,128)(2,1)S(1)}, bf16[8,64,512]{2,1,0:T(8,128)(2,1)S(1)}, u32[]{:S(2)}, u32[]{:S(2)}) %collective-permute-start.20) | collective-permute-done | bytes 524320 | tf_op jit(solution)/shard_map/ppermute | solution.py:112
  202.1 2.3 %finish.1 = bf16[1024,1024]{1,0:T(8,128)(2,1)} custom-call(s32[4,16]{1,0:T(4,128)S(1)} %add_add_fusion.table, f32[8,128,1024]{2,1,0:T(8,128)S(1)} %collect.1.base, bf16[2,128,128]{2,1,0:T(8,128)(2,1)S(1)} %pad_maximum_fusion.1.refs_0_, bf16[2,128,128]{2,1,0:T(8,128)(2,1)S(1)} %collective-permute-done.17.refs_1_, ...), custom_call_target="tpu_custom_call" | custom-call | flops 1 | bytes 1 | tf_op jit(solution)/shard_map/finish/pallas_call | solution.py:302
  (64 shorter events, 15.1 us)
Async XLA Ops:
  2.9 27.3 %collective-permute-start = (bf16[64,8192]{1,0:T(8,128)(2,1)}, bf16[64,8192]{1,0:T(8,128)(2,1)}, u32[]{:S(2)}, u32[]{:S(2)}) collective-permute-start(bf16[64,8192]{1,0:T(8,128)(2,1)} %get-tuple-element.75), channel_id=1, source_target_pairs={{0,4},{4,8},{8,12},{12,14},{14,10},{10,6},{6,2},{2,0},{1,5},{5,9},... | collective-permute-start | bytes 3145736 | tf_op jit(solution)/shard_map/ppermute | solution.py:108
  6.0 26.4 %collective-permute-start.1 = (bf16[64,8192]{1,0:T(8,128)(2,1)}, bf16[64,8192]{1,0:T(8,128)(2,1)}, u32[]{:S(2)}, u32[]{:S(2)}) collective-permute-start(bf16[64,8192]{1,0:T(8,128)(2,1)} %get-tuple-element.76), channel_id=1, source_target_pairs={{4,0},{8,4},{12,8},{14,12},{10,14},{6,10},{2,6},{0,2},{5,1},{9,5},... | collective-permute-start | bytes 3145736 | tf_op jit(solution)/shard_map/ppermute | solution.py:108
  6.0 46.6 %collective-permute-start.4 = (bf16[64,8192]{1,0:T(8,128)(2,1)}, bf16[64,8192]{1,0:T(8,128)(2,1)S(1)}, u32[]{:S(2)}, u32[]{:S(2)}) collective-permute-start(bf16[64,8192]{1,0:T(8,128)(2,1)} %get-tuple-element.76), channel_id=1, source_target_pairs={{0,4},{4,8},{8,12},{12,14},{14,10},{10,6},{6,2},{2,0},{1,5},{5,9},... | collective-permute-start | bytes 3145736 | tf_op jit(solution)/shard_map/ppermute | solution.py:108
  8.0 46.8 %collective-permute-start.5 = (bf16[64,8192]{1,0:T(8,128)(2,1)}, bf16[64,8192]{1,0:T(8,128)(2,1)}, u32[]{:S(2)}, u32[]{:S(2)}) collective-permute-start(bf16[64,8192]{1,0:T(8,128)(2,1)} %get-tuple-element.75), channel_id=1, source_target_pairs={{4,0},{8,4},{12,8},{14,12},{10,14},{6,10},{2,6},{0,2},{5,1},{9,5},... | collective-permute-start | bytes 3145736 | tf_op jit(solution)/shard_map/ppermute | solution.py:108
  41.2 6.1 %collective-permute-start.6 = (bf16[8,64,512]{2,1,0:T(8,128)(2,1)}, bf16[8,64,512]{2,1,0:T(8,128)(2,1)}, u32[]{:S(2)}, u32[]{:S(2)}) collective-permute-start(bf16[8,64,512]{2,1,0:T(8,128)(2,1)} %get-tuple-element.152), channel_id=1, source_target_pairs={{0,1},{1,0},{2,3},{3,2},{4,5},{5,4},{6,7},{7,6},{8,9},{9,8},{10,11... | collective-permute-start | bytes 1572872 | tf_op jit(solution)/shard_map/ppermute | solution.py:112
  45.2 11.7 %collective-permute-start.7 = (bf16[64,8192]{1,0:T(8,128)(2,1)}, bf16[64,8192]{1,0:T(8,128)(2,1)S(1)}, u32[]{:S(2)}, u32[]{:S(2)}) collective-permute-start(bf16[64,8192]{1,0:T(8,128)(2,1)} %get-tuple-element.149), channel_id=1, source_target_pairs={{0,1},{1,0},{2,3},{3,2},{4,5},{5,4},{6,7},{7,6},{8,9},{9,8},{10,11... | collective-permute-start | bytes 3145736 | tf_op jit(solution)/shard_map/ppermute | solution.py:112
  45.7 31.5 %collective-permute-start.2 = (bf16[64,8192]{1,0:T(8,128)(2,1)}, bf16[64,8192]{1,0:T(8,128)(2,1)}, u32[]{:S(2)}, u32[]{:S(2)}) collective-permute-start(bf16[64,8192]{1,0:T(8,128)(2,1)} %collective-permute-done.refs_0_), channel_id=1, source_target_pairs={{0,4},{4,8},{8,12},{12,14},{14,10},{10,6},{6,2},{2,0},{1,5},{5,9},... | collective-permute-start | bytes 3145736 | tf_op jit(solution)/shard_map/ppermute | solution.py:108
  47.3 30.0 %collective-permute-start.3 = (bf16[64,8192]{1,0:T(8,128)(2,1)}, bf16[64,8192]{1,0:T(8,128)(2,1)}, u32[]{:S(2)}, u32[]{:S(2)}) collective-permute-start(bf16[64,8192]{1,0:T(8,128)(2,1)} %collective-permute-done.1.refs_1_), channel_id=1, source_target_pairs={{4,0},{8,4},{12,8},{14,12},{10,14},{6,10},{2,6},{0,2},{5,1},{9,5},... | collective-permute-start | bytes 3145736 | tf_op jit(solution)/shard_map/ppermute | solution.py:108
  48.0 0.6 copy-start.14
  54.9 42.7 %collective-permute-start.10 = (bf16[64,8192]{1,0:T(8,128)(2,1)S(1)}, bf16[64,8192]{1,0:T(8,128)(2,1)S(1)}, u32[]{:S(2)}, u32[]{:S(2)}) collective-permute-start(bf16[64,8192]{1,0:T(8,128)(2,1)S(1)} %collective-permute-done.4.refs_1_), channel_id=1, source_target_pairs={{0,4},{4,8},{8,12},{12,14},{14,10},{10,6},{6,2},{2,0},{1,5},{5,9},... | collective-permute-start | bytes 3145736 | tf_op jit(solution)/shard_map/ppermute | solution.py:108
  56.4 43.3 %collective-permute-start.11 = (bf16[64,8192]{1,0:T(8,128)(2,1)}, bf16[64,8192]{1,0:T(8,128)(2,1)S(1)}, u32[]{:S(2)}, u32[]{:S(2)}) collective-permute-start(bf16[64,8192]{1,0:T(8,128)(2,1)} %collective-permute-done.5.refs_0_), channel_id=1, source_target_pairs={{4,0},{8,4},{12,8},{14,12},{10,14},{6,10},{2,6},{0,2},{5,1},{9,5},... | collective-permute-start | bytes 3145736 | tf_op jit(solution)/shard_map/ppermute | solution.py:108
  56.9 5.8 %copy-start.2 = (bf16[8192,1024]{1,0:T(8,128)(2,1)S(1)}, bf16[8192,1024]{1,0:T(8,128)(2,1)}, u32[]{:S(2)}) copy-start(bf16[8192,1024]{1,0:T(8,128)(2,1)} %weight.1) | copy-start | bytes 50331652
  62.7 2.8 %copy-start.3 = (bf16[1,128,8192]{2,1,0:T(8,128)(2,1)S(1)}, bf16[1,128,8192]{2,1,0:T(8,128)(2,1)}, u32[]{:S(2)}) copy-start(bf16[1,128,8192]{2,1,0:T(8,128)(2,1)} %param.6) | copy-start | bytes 6291460
  65.4 58.9 %copy-start = (bf16[8192,1152]{1,0:T(8,128)(2,1)}, bf16[8192,1152]{1,0:T(8,128)(2,1)S(1)}, u32[]{:S(2)}) copy-start(bf16[8192,1152]{1,0:T(8,128)(2,1)S(1)} %pin.1.weights) | copy-start | bytes 56623108
  68.9 1.6 copy-start.6
  76.4 0.8 copy-start.7
  77.3 42.7 %collective-permute-start.8 = (bf16[64,8192]{1,0:T(8,128)(2,1)}, bf16[64,8192]{1,0:T(8,128)(2,1)S(1)}, u32[]{:S(2)}, u32[]{:S(2)}) collective-permute-start(bf16[64,8192]{1,0:T(8,128)(2,1)} %collective-permute-done.2.refs_0_), channel_id=1, source_target_pairs={{0,4},{4,8},{8,12},{12,14},{14,10},{10,6},{6,2},{2,0},{1,5},{5,9},... | collective-permute-start | bytes 3145736 | tf_op jit(solution)/shard_map/ppermute | solution.py:108
  78.9 43.4 %collective-permute-start.9 = (bf16[64,8192]{1,0:T(8,128)(2,1)}, bf16[64,8192]{1,0:T(8,128)(2,1)}, u32[]{:S(2)}, u32[]{:S(2)}) collective-permute-start(bf16[64,8192]{1,0:T(8,128)(2,1)} %collective-permute-done.3.refs_1_), channel_id=1, source_target_pairs={{4,0},{8,4},{12,8},{14,12},{10,14},{6,10},{2,6},{0,2},{5,1},{9,5},... | collective-permute-start | bytes 3145736 | tf_op jit(solution)/shard_map/ppermute | solution.py:108
  83.5 0.8 copy-start.8
  88.7 0.8 copy-start.9
  99.7 42.8 %collective-permute-start.14 = (bf16[64,8192]{1,0:T(8,128)(2,1)S(1)}, bf16[64,8192]{1,0:T(8,128)(2,1)S(1)}, u32[]{:S(2)}, u32[]{:S(2)}) collective-permute-start(bf16[64,8192]{1,0:T(8,128)(2,1)S(1)} %collective-permute-done.10.refs_1_), channel_id=1, source_target_pairs={{0,4},{4,8},{8,12},{12,14},{14,10},{10,6},{6,2},{2,0},{1,5},{5,9},... | collective-permute-start | bytes 3145736 | tf_op jit(solution)/shard_map/ppermute | solution.py:108
  101.3 43.4 %collective-permute-start.15 = (bf16[64,8192]{1,0:T(8,128)(2,1)S(1)}, bf16[64,8192]{1,0:T(8,128)(2,1)S(1)}, u32[]{:S(2)}, u32[]{:S(2)}) collective-permute-start(bf16[64,8192]{1,0:T(8,128)(2,1)S(1)} %collective-permute-done.11.refs_0_), channel_id=1, source_target_pairs={{4,0},{8,4},{12,8},{14,12},{10,14},{6,10},{2,6},{0,2},{5,1},{9,5},... | collective-permute-start | bytes 3145736 | tf_op jit(solution)/shard_map/ppermute | solution.py:108
  105.2 0.8 copy-start.10
  122.3 42.8 %collective-permute-start.12 = (bf16[64,8192]{1,0:T(8,128)(2,1)S(1)}, bf16[64,8192]{1,0:T(8,128)(2,1)}, u32[]{:S(2)}, u32[]{:S(2)}) collective-permute-start(bf16[64,8192]{1,0:T(8,128)(2,1)S(1)} %collective-permute-done.8.refs_0_), channel_id=1, source_target_pairs={{0,4},{4,8},{8,12},{12,14},{14,10},{10,6},{6,2},{2,0},{1,5},{5,9},... | collective-permute-start | bytes 3145736 | tf_op jit(solution)/shard_map/ppermute | solution.py:108
  123.8 43.4 %collective-permute-start.13 = (bf16[64,8192]{1,0:T(8,128)(2,1)}, bf16[64,8192]{1,0:T(8,128)(2,1)}, u32[]{:S(2)}, u32[]{:S(2)}) collective-permute-start(bf16[64,8192]{1,0:T(8,128)(2,1)} %collective-permute-done.9.refs_1_), channel_id=1, source_target_pairs={{4,0},{8,4},{12,8},{14,12},{10,14},{6,10},{2,6},{0,2},{5,1},{9,5},... | collective-permute-start | bytes 3145736 | tf_op jit(solution)/shard_map/ppermute | solution.py:108
  128.5 0.8 copy-start.11
  144.6 1.0 copy-start.4
  146.7 42.5 %all-to-all-start = ((bf16[8,2,64,512]{3,2,1,0:T(8,128)(2,1)}), bf16[8,2,64,512]{3,2,1,0:T(8,128)(2,1)S(1)}, u32[]{:S(2)}, u32[]{:S(2)}) async-start(bf16[8,2,64,512]{3,2,1,0:T(8,128)(2,1)} %copy.9), calls=%async_computation | async-start | bytes 2097152 | tf_op jit(solution)/shard_map/all_to_all | solution.py:377
  151.5 6.4 %copy-start.1 = (bf16[8192,1152]{1,0:T(8,128)(2,1)S(1)}, bf16[8192,1152]{1,0:T(8,128)(2,1)}, u32[]{:S(2)}) copy-start(bf16[8192,1152]{1,0:T(8,128)(2,1)} %copy-done) | copy-start | bytes 56623108
  157.9 1.2 copy-start.5
  162.5 0.8 copy-start.12
  167.2 24.2 %copy-start.15 = (s32[16]{0:T(128)S(1)}, s32[16]{0:T(128)}, u32[]{:S(2)}) copy-start(s32[16]{0:T(128)} %copy-done.14) | copy-start | bytes 196
  167.2 28.7 %copy-start.16 = (s32[1,16]{1,0:T(1,128)S(1)}, s32[1,16]{1,0:T(1,128)}, u32[]{:S(2)}) copy-start(s32[1,16]{1,0:T(1,128)} %get-tuple-element.155) | copy-start | bytes 196
  171.7 0.8 copy-start.13
  172.4 4.0 %collective-permute-start.16 = (bf16[128,128]{1,0:T(8,128)(2,1)S(1)}, bf16[128,128]{1,0:T(8,128)(2,1)S(1)}, u32[]{:S(2)}, u32[]{:S(2)}) collective-permute-start(bf16[128,128]{1,0:T(8,128)(2,1)S(1)} %get-tuple-element.143), channel_id=1, source_target_pairs={{0,2},{2,0},{4,6},{6,4},{8,10},{10,8},{12,14},{14,12},{1,3},{3,1},... | collective-permute-start | bytes 98312 | tf_op jit(solution)/shard_map/ppermute | solution.py:108
  189.8 12.2 %collective-permute-start.20 = (bf16[8,64,512]{2,1,0:T(8,128)(2,1)S(1)}, bf16[8,64,512]{2,1,0:T(8,128)(2,1)S(1)}, u32[]{:S(2)}, u32[]{:S(2)}) collective-permute-start(bf16[8,64,512]{2,1,0:T(8,128)(2,1)S(1)} %take.1.refs_4_), channel_id=1, source_target_pairs={{0,16},{16,0},{1,17},{17,1},{2,18},{18,2},{3,19},{19,3},{4,20},{20... | collective-permute-start | bytes 1572872 | tf_op jit(solution)/shard_map/ppermute | solution.py:112
  191.4 6.8 %collective-permute-start.17 = (bf16[2,128,128]{2,1,0:T(8,128)(2,1)S(1)}, bf16[2,128,128]{2,1,0:T(8,128)(2,1)S(1)}, u32[]{:S(2)}, u32[]{:S(2)}) collective-permute-start(bf16[2,128,128]{2,1,0:T(8,128)(2,1)S(1)} %pad_maximum_fusion.1.refs_0_), channel_id=1, source_target_pairs={{0,4},{2,6},{4,0},{6,2},{8,12},{10,14},{12,8},{14,10},{1,5},{3,7},... | collective-permute-start | bytes 196616 | tf_op jit(solution)/shard_map/ppermute | solution.py:108
  191.5 6.7 %collective-permute-start.18 = (bf16[2,128,128]{2,1,0:T(8,128)(2,1)S(1)}, bf16[2,128,128]{2,1,0:T(8,128)(2,1)S(1)}, u32[]{:S(2)}, u32[]{:S(2)}) collective-permute-start(bf16[2,128,128]{2,1,0:T(8,128)(2,1)S(1)} %pad_maximum_fusion.1.refs_0_), channel_id=1, source_target_pairs={{0,8},{2,10},{4,12},{6,14},{8,0},{10,2},{12,4},{14,6},{1,9},{3,11}... | collective-permute-start | bytes 196616 | tf_op jit(solution)/shard_map/ppermute | solution.py:108
  193.2 6.1 %collective-permute-start.19 = (bf16[2,128,128]{2,1,0:T(8,128)(2,1)S(1)}, bf16[2,128,128]{2,1,0:T(8,128)(2,1)S(1)}, u32[]{:S(2)}, u32[]{:S(2)}) collective-permute-start(bf16[2,128,128]{2,1,0:T(8,128)(2,1)S(1)} %pad_maximum_fusion.1.refs_0_), channel_id=1, source_target_pairs={{0,12},{2,14},{4,8},{6,10},{8,4},{10,6},{12,0},{14,2},{1,13},{3,15... | collective-permute-start | bytes 196616 | tf_op jit(solution)/shard_map/ppermute | solution.py:108
